TPU v7x, 32 devices: a whole 2x2x4 slice. The times are simulated.
32 devices in a mesh: groups: 2 (over y), band: 4 (over z), dom: 2 (over x), lat: 2 (over core).
Axes of the slice: x: 2, y: 2, z: 4, core: 2. Of those that a mesh axis runs over, the one named last changes fastest.
Arguments:
- grid_in: bfloat16 [24, 1440, 227], P(('groups', 'band'), ('dom', 'lat')), parts along dimension 0, may hold values from -6 to 6
- w_grid: bfloat16 [227, 512], replicated, may hold values from -0.375 to 0.375
- w_gs: bfloat16 [512, 512], replicated, may hold values from -0.25 to 0.25
- w_gr: bfloat16 [512, 512], replicated, may hold values from -0.25 to 0.25
- w_gn: bfloat16 [512, 512], replicated, may hold values from -0.03125 to 0.03125
- w_ms: bfloat16 [512, 512], replicated, may hold values from -0.25 to 0.25
- w_mr: bfloat16 [512, 512], replicated, may hold values from -0.25 to 0.25
- w_mn: bfloat16 [512, 512], replicated, may hold values from -0.0625 to 0.0625
- mesh_in: bfloat16 [1024, 512], P(('groups', 'band', 'dom', 'lat')), parts along dimension 0, may hold values from -6 to 6
- d_out: bfloat16 [1024, 512], P(('groups', 'band', 'dom', 'lat')), parts along dimension 0, may hold values from -0.119628906 to 0.119628906
- g2m_send: int32 [8, 4, 1024], P(('groups', 'band'), ('dom', 'lat')), parts along dimension 0, may hold values from 0 to 3239, as said below
- g2m_recv: int32 [8, 4, 1024], P(('groups', 'band'), ('dom', 'lat')), parts along dimension 0, may hold values from 0 to 63, as said below
- g2m_count: int32 [8, 4], P(('groups', 'band'), ('dom', 'lat')), parts along dimension 0, may hold values from 1 to 1024, as said below
- mesh_send: int32 [8, 4, 512], P(('groups', 'band'), ('dom', 'lat')), parts along dimension 0, may hold values from 0 to 191, as said below
- mesh_recv: int32 [8, 4, 512], P(('groups', 'band'), ('dom', 'lat')), parts along dimension 0, may hold values from 0 to 31, as said below
- mesh_count: int32 [8, 4], P(('groups', 'band'), ('dom', 'lat')), parts along dimension 0, may hold values from 1 to 512, as said below
Outputs:
- mesh_out: bfloat16 [1024, 512], P(('groups', 'band', 'dom', 'lat')), parts along dimension 0
- grad_gs: float32 [1024, 512], P(('groups', 'band'), ('dom', 'lat')), parts along dimension 0
- grad_ms: float32 [1024, 512], P(('groups', 'band'), ('dom', 'lat')), parts along dimension 0
There are 2 independent parts, one for each index of `groups`. A program takes and returns all parts, laid end to end along the dimension named above; an argument that names none is the same for every part. Nothing has to cross between parts.
Inputs may be any that keep to these rules, and one draw needn't show every extreme that they name: `g2m_send`: row of the slot's grid_block; on the first band it is 1080 or more, on the last band under (6) * 360. `g2m_recv`: entry of the slot's cycle block. `g2m_count`: slots from this count on are padding. `mesh_send`: row of the slot's mesh_block; on the first band it is 64 or more, on the last band under 4 * 32. `mesh_recv`: one of the 32 nodes of the slot's band and sector. `mesh_count`: slots from this count on are padding.
All inputs are finite; a program needn't handle non-finite values.
Results may differ from a plain program's by a relative error of at most 0.009.
Values may be sent and summed in bfloat16 or wider, within the bound.
No kernel may reach another device: no remote copies, remote signals or barrier semaphores. Data moves between devices by JAX's collectives and lax.ppermute only.
A program may use at most 64 MiB of HBM per device.

v0:
```python
import jax
import jax.numpy as jnp
from jax import lax
from jax.sharding import PartitionSpec as P

H = 3


def with_halo(cells, sides, width, closed):
    for axis, dim in sides:
        count = lax.axis_size(axis)
        ends = count if closed else count - 1
        head = lax.slice_in_dim(cells, 0, width, axis=dim)
        tail = lax.slice_in_dim(cells, cells.shape[dim] - width, cells.shape[dim], axis=dim)
        cells = jnp.concatenate(
            [
                lax.ppermute(tail, axis, [(i, (i + 1) % count) for i in range(ends)]),
                cells,
                lax.ppermute(head, axis, [((i + 1) % count, i) for i in range(ends)]),
            ],
            axis=dim,
        )
    return cells


def silu_slope(inputs):
    logistic = jax.nn.sigmoid(inputs)
    return logistic * (1.0 + inputs * (1.0 - logistic))


def matmul(first_op, second_op):
    return jnp.dot(first_op, second_op, preferred_element_type=jnp.float32)


def matmul_back(first_op, second_op):
    return lax.dot_general(
        first_op, second_op, (((1,), (1,)), ((), ())), preferred_element_type=jnp.float32
    )


def outer_sum(rows, terms):
    return lax.dot_general(
        rows, terms, (((0,), (0,)), ((), ())), preferred_element_type=jnp.float32
    )


def exact_sum(table, values):
    return jnp.dot(
        table, values, precision=lax.Precision.HIGHEST, preferred_element_type=jnp.float32
    )


def hit_table(count, targets):
    return lax.iota(jnp.int32, count)[:, None] == targets[None, :]


def on_device(
    grid_in,
    w_grid,
    w_gs,
    w_gr,
    w_gn,
    w_ms,
    w_mr,
    w_mn,
    mesh_in,
    d_out,
    g2m_send,
    g2m_recv,
    g2m_count,
    mesh_send,
    mesh_recv,
    mesh_count,
):
    band_rows, cycle_cols, variables = grid_in.shape
    latent = w_grid.shape[1]
    node_count = mesh_in.shape[0]
    rim_rows = node_count // 2
    cycle_rows = 2 * node_count
    sectors = lax.axis_size(("dom", "lat"))
    band_count = lax.axis_size("band")
    grid_lat = jax.nn.silu(matmul(grid_in.reshape(-1, variables), w_grid)).astype(jnp.bfloat16)
    grid_rows = with_halo(
        grid_lat.reshape(band_rows, cycle_cols, latent), (("band", 0),), H, False
    ).reshape(-1, latent)
    grid_from = g2m_send.reshape(-1)
    grid_to = g2m_recv.reshape(-1)
    grid_flag = (lax.iota(jnp.int32, grid_from.shape[0]) < g2m_count.reshape(())).astype(
        jnp.float32
    )
    grid_live = grid_flag[:, None]
    senders = jnp.take(grid_rows, grid_from, axis=0)
    cycle_in = with_halo(mesh_in, ((("dom", "lat"), 0),), rim_rows, True)
    enc_pre = matmul(senders, w_gs) + jnp.take(matmul(cycle_in, w_gr), grid_to, axis=0)
    grid_hits = hit_table(cycle_rows, grid_to).astype(jnp.float32) * grid_flag[None, :]
    enc_part = exact_sum(grid_hits, jax.nn.silu(enc_pre))
    rim_parts = jnp.concatenate([enc_part[:rim_rows], enc_part[rim_rows + node_count :]], axis=0)
    returned = with_halo(rim_parts, ((("dom", "lat"), 0),), rim_rows, True)
    agg_one = enc_part[rim_rows : rim_rows + node_count] + jnp.concatenate(
        [returned[:rim_rows], returned[rim_rows + node_count :]], axis=0
    )
    enc_gate = matmul(agg_one.astype(jnp.bfloat16), w_gn)
    mesh_one = (mesh_in.astype(jnp.float32) + jax.nn.silu(enc_gate)).astype(jnp.bfloat16)
    cycle_one = with_halo(mesh_one, ((("dom", "lat"), 0),), rim_rows, True)
    mesh_block = with_halo(cycle_one[None], (("band", 0),), 1, False).reshape(-1, latent)
    mesh_from = mesh_send.reshape(-1)
    mesh_to = mesh_recv.reshape(-1)
    mesh_flag = (lax.iota(jnp.int32, mesh_from.shape[0]) < mesh_count.reshape(())).astype(
        jnp.float32
    )
    mesh_live = mesh_flag[:, None]
    proc_pre = jnp.take(matmul(mesh_block, w_ms), mesh_from, axis=0) + jnp.take(
        matmul(mesh_one, w_mr), mesh_to, axis=0
    )
    recv_hits = hit_table(node_count, mesh_to)
    agg_two = exact_sum(recv_hits.astype(jnp.float32) * mesh_flag[None, :], jax.nn.silu(proc_pre))
    proc_gate = matmul(agg_two.astype(jnp.bfloat16), w_mn)
    mesh_out = (mesh_one.astype(jnp.float32) + jax.nn.silu(proc_gate)).astype(jnp.bfloat16)
    cotangent = d_out.astype(jnp.float32)
    gate_two = (cotangent * silu_slope(proc_gate)).astype(jnp.bfloat16)
    back_two = matmul_back(gate_two, w_mn)
    proc_slope = (jnp.take(back_two, mesh_to, axis=0) * silu_slope(proc_pre) * mesh_live).astype(
        jnp.bfloat16
    )
    grad_proc = outer_sum(jnp.take(mesh_block, mesh_from, axis=0), proc_slope)
    send_sum = matmul(hit_table(3 * cycle_rows, mesh_from).astype(jnp.bfloat16), proc_slope)
    recv_sum = matmul(recv_hits.astype(jnp.bfloat16), proc_slope)
    by_band = send_sum.reshape(3, cycle_rows, latent)
    outward = jnp.concatenate([by_band[0], by_band[2]], axis=0)
    returned_band = with_halo(
        outward.astype(jnp.bfloat16), (("band", 0),), cycle_rows, False
    ).astype(outward.dtype)
    cycle_sum = by_band[1] + returned_band[:cycle_rows] + returned_band[3 * cycle_rows :]
    side_rows = jnp.concatenate([cycle_sum[:rim_rows], cycle_sum[rim_rows + node_count :]], axis=0)
    returned_cycle = with_halo(
        side_rows.astype(jnp.bfloat16), ((("dom", "lat"), 0),), rim_rows, True
    ).astype(side_rows.dtype)
    send_total = cycle_sum[rim_rows : rim_rows + node_count] + jnp.concatenate(
        [returned_cycle[:rim_rows], returned_cycle[rim_rows + node_count :]], axis=0
    )
    cot_one = (
        cotangent
        + matmul_back(send_total.astype(jnp.bfloat16), w_ms)
        + matmul_back(recv_sum.astype(jnp.bfloat16), w_mr)
    )
    gate_one = (cot_one * silu_slope(enc_gate)).astype(jnp.bfloat16)
    back_one = matmul_back(gate_one, w_gn)
    back_cycle = with_halo(back_one, ((("dom", "lat"), 0),), rim_rows, True)
    enc_slope = (jnp.take(back_cycle, grid_to, axis=0) * silu_slope(enc_pre) * grid_live).astype(
        jnp.bfloat16
    )
    grad_enc = outer_sum(senders, enc_slope)

    def as_tiles(gradient):
        split = gradient.reshape(band_count, latent // band_count, sectors, latent // sectors)
        return split.transpose(0, 2, 1, 3).reshape(
            band_count * sectors, latent // band_count, latent // sectors
        )

    grad_gs, grad_ms = (
        lax.psum_scatter(
            as_tiles(grad_enc), ("band", "dom", "lat"), scatter_dimension=0, tiled=True
        ),
        lax.psum_scatter(
            as_tiles(grad_proc), ("band", "dom", "lat"), scatter_dimension=0, tiled=True
        ),
    )
    return (mesh_out, grad_gs[0], grad_ms[0])


def solution(mesh):
    placed = (
        P(("groups", "band"), ("dom", "lat"), None),
        P(),
        P(),
        P(),
        P(),
        P(),
        P(),
        P(),
        P(("groups", "band", "dom", "lat"), None),
        P(("groups", "band", "dom", "lat"), None),
        P(("groups", "band"), ("dom", "lat"), None),
        P(("groups", "band"), ("dom", "lat"), None),
        P(("groups", "band"), ("dom", "lat")),
        P(("groups", "band"), ("dom", "lat"), None),
        P(("groups", "band"), ("dom", "lat"), None),
        P(("groups", "band"), ("dom", "lat")),
    )
    return jax.shard_map(
        on_device,
        mesh=mesh,
        in_specs=placed,
        out_specs=(
            P(("groups", "band", "dom", "lat"), None),
            P(("groups", "band"), ("dom", "lat")),
            P(("groups", "band"), ("dom", "lat")),
        ),
        check_vma=False,
    )
```

profile of v0, /device:TPU:0, one launch (start us, length us, event | category | flops | bytes accessed | tf_op | source)
XLA Modules:
  0.0 222.9 jit_solution(9332036034756648275)
XLA Ops:
  7.2 1.3 copy.21
  8.6 2.7 %multiply_convert_fusion = bf16[1080,512]{1,0:T(8,128)(2,1)} fusion(bf16[1080,227]{1,0:T(8,128)(2,1)S(1)} %bitcast.52, bf16[227,512]{1,0:T(8,128)(2,1)} %param.21), kind=kOutput, calls=%fused_computation.8 | convolution fusion | flops 253808640 | bytes 1828688 | tf_op jit(solution)/shard_map/dot_general | solution.py:32
  11.4 5.9 %collective-permute-start = (bf16[3,360,512]{2,1,0:T(8,128)(2,1)}, bf16[3,360,512]{2,1,0:T(8,128)(2,1)}, u32[]{:S(2)}, u32[]{:S(2)}) collective-permute-start(bf16[3,360,512]{2,1,0:T(8,128)(2,1)} %bitcast.4), channel_id=1, source_target_pairs={{0,4},{4,8},{8,12},{1,5},{5,9},{9,13},{2,6},{6,10},{10,14},{3,7},{... | collective-permute-start | bytes 3317768 | tf_op jit(solution)/shard_map/ppermute | solution.py:17
  18.7 1.7 collective-permute-start.3
  22.1 3.5 %gather_fusion.3 = f32[1024,512]{1,0:T(8,128)S(1)} fusion(f32[64,512]{1,0:T(8,128)S(1)} %fusion.28, s32[1024]{0:T(1024)S(1)} %fusion.48), kind=kCustom, calls=%fused_computation.clone | custom fusion | bytes 4198400 | tf_op jit(solution)/shard_map/jit(_take)/gather | solution.py:94
  25.6 14.6 %collective-permute-done = bf16[3,360,512]{2,1,0:T(8,128)(2,1)} collective-permute-done((bf16[3,360,512]{2,1,0:T(8,128)(2,1)}, bf16[3,360,512]{2,1,0:T(8,128)(2,1)}, u32[]{:S(2)}, u32[]{:S(2)}) %collective-permute-start) | collective-permute-done | bytes 1105952 | tf_op jit(solution)/shard_map/ppermute | solution.py:17
  40.2 5.1 %collective-permute-done.1 = bf16[3,360,512]{2,1,0:T(8,128)(2,1)} collective-permute-done((bf16[3,360,512]{2,1,0:T(8,128)(2,1)}, bf16[3,360,512]{2,1,0:T(8,128)(2,1)}, u32[]{:S(2)}, u32[]{:S(2)}) %collective-permute-start.1) | collective-permute-done | bytes 1105952 | tf_op jit(solution)/shard_map/ppermute | solution.py:19
  45.4 3.3 %pad_maximum_fusion = bf16[9,360,512]{2,1,0:T(8,128)(2,1)} fusion(bf16[3,360,512]{2,1,0:T(8,128)(2,1)} %collective-permute-done.1, bf16[3,360,512]{2,1,0:T(8,128)(2,1)} %bitcast.4, bf16[3,360,512]{2,1,0:T(8,128)(2,1)} %collective-permute-done), kind=kLoop, calls=%fused_computation.7 | loop fusion | flops 3317760 | bytes 6635520 | tf_op jit(solution)/shard_map/concatenate | solution.py:15
  48.7 7.5 %gather_fusion = bf16[1024,512]{1,0:T(8,128)(2,1)} fusion(bf16[3240,512]{1,0:T(8,128)(2,1)} %bitcast.47, s32[1024]{0:T(1024)S(1)} %broadcast_clamp_fusion), kind=kCustom, calls=%fused_computation.4 | custom fusion | bytes 2101248 | tf_op jit(solution)/shard_map/jit(_take)/gather | solution.py:92
  56.2 2.4 %select_add_fusion = f32[1024,512]{1,0:T(8,128)S(1)} fusion(f32[1024,512]{1,0:T(8,128)S(1)} %gather_fusion.3, pred[1024]{0:T(1024)(128)(4,1)S(1)} %get-tuple-element.27, bf16[512,512]{1,0:T(8,128)(2,1)S(1)} %copy-done, bf16[1024,512]{1,0:T(8,128)(2,1)} %gather_fusion, pred[1024]{0:T(1024)(128)(4,1)S(1)} %get-tuple-element.28), kind=kOutput, calls=%fused_computation.12 | convolution fusion | flops 538443776 | bytes 5769216 | tf_op jit(solution)/shard_map/dot_general | solution.py:32
  58.6 1.8 fusion.2
  60.5 1.7 collective-permute-start.5
  62.2 1.6 collective-permute-done.4
  64.1 1.7 collective-permute-start.6
  65.9 1.4 collective-permute-done.6
  67.4 2.5 %collective-permute-start.8 = (bf16[1,64,512]{2,1,0:T(8,128)(2,1)S(1)}, bf16[1,64,512]{2,1,0:T(8,128)(2,1)S(1)}, u32[]{:S(2)}, u32[]{:S(2)}) collective-permute-start(bf16[1,64,512]{2,1,0:T(8,128)(2,1)S(1)} %maximum_bitcast_fusion), channel_id=1, source_target_pairs={{0,4},{4,8},{8,12},{1,5},{5,9},{9,13},{2,6},{6,10},{10,14},{3,7},{... | collective-permute-start | bytes 196616 | tf_op jit(solution)/shard_map/ppermute | solution.py:17
  71.4 1.6 gather_fusion.4
  73.0 3.4 %collective-permute-done.9 = bf16[1,64,512]{2,1,0:T(8,128)(2,1)S(1)} collective-permute-done((bf16[1,64,512]{2,1,0:T(8,128)(2,1)S(1)}, bf16[1,64,512]{2,1,0:T(8,128)(2,1)S(1)}, u32[]{:S(2)}, u32[]{:S(2)}) %collective-permute-start.9) | collective-permute-done | bytes 65568 | tf_op jit(solution)/shard_map/ppermute | solution.py:19
  76.7 1.6 gather_fusion.1
  80.5 2.4 %gather_fusion.5 = f32[512,512]{1,0:T(8,128)} fusion(f32[32,512]{1,0:T(8,128)S(1)} %fusion.35, s32[1024]{0:T(1024)S(1)} %pad_clamp_fusion), kind=kCustom, calls=%fused_computation.3.clone | custom fusion | bytes 2099200 | tf_op jit(solution)/shard_map/jit(_take)/gather | solution.py:122
  82.9 1.8 fusion.7
  85.0 3.5 %collective-permute-start.10 = (bf16[64,512]{1,0:T(8,128)(2,1)S(1)}, bf16[64,512]{1,0:T(8,128)(2,1)S(1)}, u32[]{:S(2)}, u32[]{:S(2)}) collective-permute-start(bf16[64,512]{1,0:T(8,128)(2,1)S(1)} %get-tuple-element.7), channel_id=1, source_target_pairs={{0,4},{4,8},{8,12},{1,5},{5,9},{9,13},{2,6},{6,10},{10,14},{3,7},{... | collective-permute-start | bytes 196616 | tf_op jit(solution)/shard_map/ppermute | solution.py:17
  89.8 2.6 %gather_fusion.2 = bf16[512,512]{1,0:T(8,128)(2,1)} fusion(bf16[192,512]{1,0:T(8,128)(2,1)S(1)} %bitcast.46, s32[1024]{0:T(1024)S(1)} %pad_clamp_fusion.1), kind=kCustom, calls=%fused_computation.6 | custom fusion | bytes 1050624 | tf_op jit(solution)/shard_map/jit(_take)/gather | solution.py:125
  92.5 2.2 collective-permute-done.11
  94.8 1.7 collective-permute-start.13
  96.5 1.6 fusion.12
  101.0 1.7 collective-permute-start.15
  102.8 1.6 collective-permute-done.14
  104.4 4.9 %gather_fusion.6 = f32[1024,512]{1,0:T(8,128)} fusion(f32[64,512]{1,0:T(8,128)S(1)} %pad_maximum_fusion.2, s32[1024]{0:T(1024)S(1)} %fusion.48), kind=kCustom, calls=%fused_computation.2.clone | custom fusion | bytes 4198400 | tf_op jit(solution)/shard_map/jit(_take)/gather | solution.py:149
  109.3 3.7 %fusion.10 = f32[512,512]{1,0:T(8,128)S(1)} fusion(f32[1024,512]{1,0:T(8,128)} %gather_fusion.6, f32[1024,512]{1,0:T(8,128)} %copy-done.6, f32[1024]{0:T(1024)S(1)} %fusion.47, pred[1024]{0:T(1024)(128)(4,1)S(1)} %get-tuple-element.27, bf16[1024,512]{1,0:T(8,128)(2,1)S(1)} %copy-done.1, pred[1024]{0:T(1024)(128)(4,1)S(1)} %get-tuple-element.28), kind=kOutput, calls=%fused_computation.30 | convolution fusion | flops 543162368 | bytes 6297600 | tf_op jit(solution)/shard_map/dot_general | solution.py:42
  114.5 40.6 %reduce-scatter.5.cloned.1.call-done = f32[1,128,128]{2,1,0:T(8,128)} async-done(((f32[16,128,128]{2,1,0:T(8,128)}), f32[1,128,128]{2,1,0:T(8,128)}) %reduce-scatter.5.cloned.1.call-update) | async-done | bytes 65552 | tf_op jit(solution)/shard_map/reduce_scatter | solution.py:164
  155.1 61.0 %reduce-scatter.3.cloned.1.call-done = f32[1,128,128]{2,1,0:T(8,128)} async-done(((f32[16,128,128]{2,1,0:T(8,128)}), f32[1,128,128]{2,1,0:T(8,128)}) %reduce-scatter.3.cloned.1.call-update) | async-done | bytes 65552 | tf_op jit(solution)/shard_map/reduce_scatter | solution.py:161
  (92 shorter events, 12.2 us)
Async XLA Ops:
  7.2 49.0 %copy-start = (bf16[512,512]{1,0:T(8,128)(2,1)S(1)}, bf16[512,512]{1,0:T(8,128)(2,1)}, u32[]{:S(2)}) copy-start(bf16[512,512]{1,0:T(8,128)(2,1)} %param.22) | copy-start | bytes 1572868
  7.2 147.9 %reduce-scatter.5.cloned.1.call-start = ((), (), s32[]{:S(2)}) async-start(), calls=%async_computation.3 | async-start | bytes 1114112 | tf_op jit(solution)/shard_map/reduce_scatter | solution.py:164
  8.6 10.0 %copy-start.11 = (bf16[32,512]{1,0:T(8,128)(2,1)S(1)}, bf16[32,512]{1,0:T(8,128)(2,1)}, u32[]{:S(2)}) copy-start(bf16[32,512]{1,0:T(8,128)(2,1)} %param.28) | copy-start | bytes 98308
  8.6 11.9 %copy-start.15 = (s32[1,1,1024]{2,1,0:T(1,128)S(1)}, s32[1,1,1024]{2,1,0:T(1,128)}, u32[]{:S(2)}) copy-start(s32[1,1,1024]{2,1,0:T(1,128)} %param.30) | copy-start | bytes 12292
  8.6 11.9 %copy-start.13 = (s32[1,1,512]{2,1,0:T(1,128)S(1)}, s32[1,1,512]{2,1,0:T(1,128)}, u32[]{:S(2)}) copy-start(s32[1,1,512]{2,1,0:T(1,128)} %param.33) | copy-start | bytes 6148
  8.6 11.9 %copy-start.14 = (s32[1,1,512]{2,1,0:T(1,128)S(1)}, s32[1,1,512]{2,1,0:T(1,128)}, u32[]{:S(2)}) copy-start(s32[1,1,512]{2,1,0:T(1,128)} %param.34) | copy-start | bytes 6148
  8.6 13.2 %copy-start.16 = (s32[1,1,1024]{2,1,0:T(1,128)S(1)}, s32[1,1,1024]{2,1,0:T(1,128)}, u32[]{:S(2)}) copy-start(s32[1,1,1024]{2,1,0:T(1,128)} %param.31) | copy-start | bytes 12292
  8.6 13.3 %copy-start.10 = (bf16[512,512]{1,0:T(8,128)(2,1)S(1)}, bf16[512,512]{1,0:T(8,128)(2,1)}, u32[]{:S(2)}) copy-start(bf16[512,512]{1,0:T(8,128)(2,1)} %param.23) | copy-start | bytes 1572868
  11.4 28.9 %collective-permute-start = (bf16[3,360,512]{2,1,0:T(8,128)(2,1)}, bf16[3,360,512]{2,1,0:T(8,128)(2,1)}, u32[]{:S(2)}, u32[]{:S(2)}) collective-permute-start(bf16[3,360,512]{2,1,0:T(8,128)(2,1)} %bitcast.4), channel_id=1, source_target_pairs={{0,4},{4,8},{8,12},{1,5},{5,9},{9,13},{2,6},{6,10},{10,14},{3,7},{... | collective-permute-start | bytes 3317768 | tf_op jit(solution)/shard_map/ppermute | solution.py:17
  17.3 28.0 %collective-permute-start.1 = (bf16[3,360,512]{2,1,0:T(8,128)(2,1)}, bf16[3,360,512]{2,1,0:T(8,128)(2,1)}, u32[]{:S(2)}, u32[]{:S(2)}) collective-permute-start(bf16[3,360,512]{2,1,0:T(8,128)(2,1)} %bitcast.4), channel_id=1, source_target_pairs={{4,0},{8,4},{12,8},{5,1},{9,5},{13,9},{6,2},{10,6},{14,10},{7,3},{... | collective-permute-start | bytes 3317768 | tf_op jit(solution)/shard_map/ppermute | solution.py:19
  18.6 3.2 %collective-permute-start.2 = (bf16[16,512]{1,0:T(8,128)(2,1)S(1)}, bf16[16,512]{1,0:T(8,128)(2,1)S(1)}, u32[]{:S(2)}, u32[]{:S(2)}) collective-permute-start(bf16[16,512]{1,0:T(8,128)(2,1)S(1)} %get-tuple-element.19), channel_id=1, source_target_pairs={{0,1},{1,2},{2,3},{3,0},{4,5},{5,6},{6,7},{7,4},{8,9},{9,10},{10,1... | collective-permute-start | bytes 49160 | tf_op jit(solution)/shard_map/ppermute | solution.py:17
  18.7 3.2 %collective-permute-start.3 = (bf16[16,512]{1,0:T(8,128)(2,1)S(1)}, bf16[16,512]{1,0:T(8,128)(2,1)S(1)}, u32[]{:S(2)}, u32[]{:S(2)}) collective-permute-start(bf16[16,512]{1,0:T(8,128)(2,1)S(1)} %get-tuple-element.20), channel_id=1, source_target_pairs={{1,0},{2,1},{3,2},{0,3},{5,4},{6,5},{7,6},{4,7},{9,8},{10,9},{11,1... | collective-permute-start | bytes 49160 | tf_op jit(solution)/shard_map/ppermute | solution.py:19
  58.6 1.8 copy-start.6
  58.6 5.2 %copy-start.4 = (bf16[512,512]{1,0:T(8,128)(2,1)S(1)}, bf16[512,512]{1,0:T(8,128)(2,1)}, u32[]{:S(2)}) copy-start(bf16[512,512]{1,0:T(8,128)(2,1)} %param.24) | copy-start | bytes 1572868
  58.6 12.6 %copy-start.2 = (bf16[512,512]{1,0:T(8,128)(2,1)S(1)}, bf16[512,512]{1,0:T(8,128)(2,1)}, u32[]{:S(2)}) copy-start(bf16[512,512]{1,0:T(8,128)(2,1)} %param.26) | copy-start | bytes 1572868
  60.4 3.4 %collective-permute-start.4 = (f32[16,512]{1,0:T(8,128)S(1)}, f32[16,512]{1,0:T(8,128)S(1)}, u32[]{:S(2)}, u32[]{:S(2)}) collective-permute-start(f32[16,512]{1,0:T(8,128)S(1)} %get-tuple-element.9), channel_id=1, source_target_pairs={{0,1},{1,2},{2,3},{3,0},{4,5},{5,6},{6,7},{7,4},{8,9},{9,10},{10,1... | collective-permute-start | bytes 98312 | tf_op jit(solution)/shard_map/ppermute | solution.py:17
  60.5 3.3 %collective-permute-start.5 = (f32[16,512]{1,0:T(8,128)S(1)}, f32[16,512]{1,0:T(8,128)S(1)}, u32[]{:S(2)}, u32[]{:S(2)}) collective-permute-start(f32[16,512]{1,0:T(8,128)S(1)} %get-tuple-element.10), channel_id=1, source_target_pairs={{1,0},{2,1},{3,2},{0,3},{5,4},{6,5},{7,6},{4,7},{9,8},{10,9},{11,1... | collective-permute-start | bytes 98312 | tf_op jit(solution)/shard_map/ppermute | solution.py:19
  64.1 3.2 %collective-permute-start.6 = (bf16[16,512]{1,0:T(8,128)(2,1)S(1)}, bf16[16,512]{1,0:T(8,128)(2,1)S(1)}, u32[]{:S(2)}, u32[]{:S(2)}) collective-permute-start(bf16[16,512]{1,0:T(8,128)(2,1)S(1)} %get-tuple-element.17), channel_id=1, source_target_pairs={{0,1},{1,2},{2,3},{3,0},{4,5},{5,6},{6,7},{7,4},{8,9},{9,10},{10,1... | collective-permute-start | bytes 49160 | tf_op jit(solution)/shard_map/ppermute | solution.py:17
  65.7 1.6 collective-permute-start.7
  67.4 5.6 %collective-permute-start.8 = (bf16[1,64,512]{2,1,0:T(8,128)(2,1)S(1)}, bf16[1,64,512]{2,1,0:T(8,128)(2,1)S(1)}, u32[]{:S(2)}, u32[]{:S(2)}) collective-permute-start(bf16[1,64,512]{2,1,0:T(8,128)(2,1)S(1)} %maximum_bitcast_fusion), channel_id=1, source_target_pairs={{0,4},{4,8},{8,12},{1,5},{5,9},{9,13},{2,6},{6,10},{10,14},{3,7},{... | collective-permute-start | bytes 196616 | tf_op jit(solution)/shard_map/ppermute | solution.py:17
  69.9 6.5 %collective-permute-start.9 = (bf16[1,64,512]{2,1,0:T(8,128)(2,1)S(1)}, bf16[1,64,512]{2,1,0:T(8,128)(2,1)S(1)}, u32[]{:S(2)}, u32[]{:S(2)}) collective-permute-start(bf16[1,64,512]{2,1,0:T(8,128)(2,1)S(1)} %maximum_bitcast_fusion), channel_id=1, source_target_pairs={{4,0},{8,4},{12,8},{5,1},{9,5},{13,9},{6,2},{10,6},{14,10},{7,3},{... | collective-permute-start | bytes 196616 | tf_op jit(solution)/shard_map/ppermute | solution.py:19
  71.4 5.1 %copy-start.8 = (bf16[512,512]{1,0:T(8,128)(2,1)S(1)}, bf16[512,512]{1,0:T(8,128)(2,1)}, u32[]{:S(2)}) copy-start(bf16[512,512]{1,0:T(8,128)(2,1)} %param.25) | copy-start | bytes 1572868
  78.4 1.9 copy-start.12
  85.0 7.5 %collective-permute-start.10 = (bf16[64,512]{1,0:T(8,128)(2,1)S(1)}, bf16[64,512]{1,0:T(8,128)(2,1)S(1)}, u32[]{:S(2)}, u32[]{:S(2)}) collective-permute-start(bf16[64,512]{1,0:T(8,128)(2,1)S(1)} %get-tuple-element.7), channel_id=1, source_target_pairs={{0,4},{4,8},{8,12},{1,5},{5,9},{9,13},{2,6},{6,10},{10,14},{3,7},{... | collective-permute-start | bytes 196616 | tf_op jit(solution)/shard_map/ppermute | solution.py:17
  88.5 6.2 %collective-permute-start.11 = (bf16[64,512]{1,0:T(8,128)(2,1)S(1)}, bf16[64,512]{1,0:T(8,128)(2,1)S(1)}, u32[]{:S(2)}, u32[]{:S(2)}) collective-permute-start(bf16[64,512]{1,0:T(8,128)(2,1)S(1)} %get-tuple-element.8), channel_id=1, source_target_pairs={{4,0},{8,4},{12,8},{5,1},{9,5},{13,9},{6,2},{10,6},{14,10},{7,3},{... | collective-permute-start | bytes 196616 | tf_op jit(solution)/shard_map/ppermute | solution.py:19
  94.7 5.2 %collective-permute-start.12 = (bf16[16,512]{1,0:T(8,128)(2,1)S(1)}, bf16[16,512]{1,0:T(8,128)(2,1)S(1)}, u32[]{:S(2)}, u32[]{:S(2)}) collective-permute-start(bf16[16,512]{1,0:T(8,128)(2,1)S(1)} %get-tuple-element.15), channel_id=1, source_target_pairs={{0,1},{1,2},{2,3},{3,0},{4,5},{5,6},{6,7},{7,4},{8,9},{9,10},{10,1... | collective-permute-start | bytes 49160 | tf_op jit(solution)/shard_map/ppermute | solution.py:17
  94.8 5.1 %collective-permute-start.13 = (bf16[16,512]{1,0:T(8,128)(2,1)S(1)}, bf16[16,512]{1,0:T(8,128)(2,1)S(1)}, u32[]{:S(2)}, u32[]{:S(2)}) collective-permute-start(bf16[16,512]{1,0:T(8,128)(2,1)S(1)} %get-tuple-element.16), channel_id=1, source_target_pairs={{1,0},{2,1},{3,2},{0,3},{5,4},{6,5},{7,6},{4,7},{9,8},{10,9},{11,1... | collective-permute-start | bytes 49160 | tf_op jit(solution)/shard_map/ppermute | solution.py:19
  98.5 1.7 copy-start.3
  99.6 116.5 %reduce-scatter.3.cloned.1.call-start = ((), (), s32[]{:S(2)}) async-start(), calls=%async_computation.2 | async-start | bytes 1114112 | tf_op jit(solution)/shard_map/reduce_scatter | solution.py:161
  101.0 3.4 %collective-permute-start.14 = (f32[16,512]{1,0:T(8,128)S(1)}, f32[16,512]{1,0:T(8,128)S(1)}, u32[]{:S(2)}, u32[]{:S(2)}) collective-permute-start(f32[16,512]{1,0:T(8,128)S(1)} %get-tuple-element.11), channel_id=1, source_target_pairs={{0,1},{1,2},{2,3},{3,0},{4,5},{5,6},{6,7},{7,4},{8,9},{9,10},{10,1... | collective-permute-start | bytes 98312 | tf_op jit(solution)/shard_map/ppermute | solution.py:17
  101.0 3.3 %collective-permute-start.15 = (f32[16,512]{1,0:T(8,128)S(1)}, f32[16,512]{1,0:T(8,128)S(1)}, u32[]{:S(2)}, u32[]{:S(2)}) collective-permute-start(f32[16,512]{1,0:T(8,128)S(1)} %get-tuple-element.12), channel_id=1, source_target_pairs={{1,0},{2,1},{3,2},{0,3},{5,4},{6,5},{7,6},{4,7},{9,8},{10,9},{11,1... | collective-permute-start | bytes 98312 | tf_op jit(solution)/shard_map/ppermute | solution.py:19
  104.4 4.9 %copy-start.1 = (bf16[1024,512]{1,0:T(8,128)(2,1)S(1)}, bf16[1024,512]{1,0:T(8,128)(2,1)}, u32[]{:S(2)}) copy-start(bf16[1024,512]{1,0:T(8,128)(2,1)} %gather_fusion) | copy-start | bytes 3145732
  (3 other events, 3.6 us)
Sparse Core Ops, SparseCore 0:
  99.7 55.2 reduce-scatter.4
  159.7 56.3 reduce-scatter.2
where the time goes:
time: 223 us
  waiting for transfers between devices  132 us (59%)
  local copies, waits for them, and re-layouts  28.8 us (13%)
  starting transfers between devices  25.1 us (11%)
  matrix products  16.3 us (7%)
  between operations  15.9 us (7%)
  other arithmetic  5.25 us (2%)
    reduce_scatter x1, waiting for transfers between devices, on_device(): lax.psum_scatter(as_tiles(grad_enc), ('band', 'dom', 'lat'), scatter_dime...  61 us
    reduce_scatter x1, waiting for transfers between devices, on_device(): lax.psum_scatter(as_tiles(grad_proc), ('band', 'dom', 'lat'), scatter_dim...  40.6 us
    ppermute x8, waiting for transfers between devices, with_halo(): lax.ppermute(tail, axis, [(i, (i + 1) % count) for i in range(ends)])  19.2 us
    ppermute x8, starting transfers between devices, with_halo(): lax.ppermute(tail, axis, [(i, (i + 1) % count) for i in range(ends)])  13.8 us
    ppermute x8, starting transfers between devices, with_halo(): lax.ppermute(head, axis, [((i + 1) % count, i) for i in range(ends)])  11 us
    ppermute x8, waiting for transfers between devices, with_halo(): lax.ppermute(head, axis, [((i + 1) % count, i) for i in range(ends)])  10.8 us
    gather x1, local copies, waits for them, and re-layouts, on_device(): senders = jnp.take(grid_rows, grid_from, axis=0)  7.53 us
    dot_general x8, matrix products, matmul(): return jnp.dot(first_op, second_op, preferred_element_type=jnp.float32)  7.13 us
  transfers between devices with their start and end apart: 18, of which 10 were waited for; matrix products, arithmetic and copies ran while one was open for 10% of the time, Pallas kernels for 0%

commit v1 on v0

--- a/solution.py
+++ b/solution.py
@@ -79,17 +79,16 @@
     cycle_rows = 2 * node_count
     sectors = lax.axis_size(("dom", "lat"))
     band_count = lax.axis_size("band")
-    grid_lat = jax.nn.silu(matmul(grid_in.reshape(-1, variables), w_grid)).astype(jnp.bfloat16)
-    grid_rows = with_halo(
-        grid_lat.reshape(band_rows, cycle_cols, latent), (("band", 0),), H, False
-    ).reshape(-1, latent)
+    grid_raw = with_halo(grid_in, (("band", 0),), H, False).reshape(-1, variables)
     grid_from = g2m_send.reshape(-1)
     grid_to = g2m_recv.reshape(-1)
     grid_flag = (lax.iota(jnp.int32, grid_from.shape[0]) < g2m_count.reshape(())).astype(
         jnp.float32
     )
     grid_live = grid_flag[:, None]
-    senders = jnp.take(grid_rows, grid_from, axis=0)
+    senders = jax.nn.silu(matmul(jnp.take(grid_raw, grid_from, axis=0), w_grid)).astype(
+        jnp.bfloat16
+    )
     cycle_in = with_halo(mesh_in, ((("dom", "lat"), 0),), rim_rows, True)
     enc_pre = matmul(senders, w_gs) + jnp.take(matmul(cycle_in, w_gr), grid_to, axis=0)
     grid_hits = hit_table(cycle_rows, grid_to).astype(jnp.float32) * grid_flag[None, :]
@@ -157,15 +156,12 @@
             band_count * sectors, latent // band_count, latent // sectors
         )
 
-    grad_gs, grad_ms = (
-        lax.psum_scatter(
-            as_tiles(grad_enc), ("band", "dom", "lat"), scatter_dimension=0, tiled=True
-        ),
-        lax.psum_scatter(
-            as_tiles(grad_proc), ("band", "dom", "lat"), scatter_dimension=0, tiled=True
-        ),
-    )
-    return (mesh_out, grad_gs[0], grad_ms[0])
+    def summed_tile(gradient):
+        tiles = as_tiles(gradient).astype(jnp.bfloat16)
+        shares = lax.all_to_all(tiles, ("band", "dom", "lat"), 0, 0, tiled=True)
+        return jnp.sum(shares.astype(jnp.float32), axis=0)
+
+    return (mesh_out, summed_tile(grad_enc), summed_tile(grad_proc))
 
 
 def solution(mesh):

time: 223 us -> 121 us (0.54)
  waiting for transfers between devices: 132 us -> 23.5 us
  between operations: 15.9 us -> 2.53 us
  starting transfers between devices: 25.1 us -> 37.3 us
  other arithmetic: 5.25 us -> 11 us
    reduce_scatter x2 -> x0, waiting for transfers between devices: 102 us -> none  [the longest x1 61 us: on_device(): lax.psum_scatter(as_tiles(grad_enc), ('band', 'dom', 'lat'), scatter_dime...]
    ppermute x8, waiting for transfers between devices: 19.2 us -> 5.23 us  [with_halo(): lax.ppermute(tail, axis, [(i, (i + 1) % count) for i in range(ends)])]
    all_to_all x0 -> x2, waiting for transfers between devices: none -> 13.8 us  [summed_tile(): shares = lax.all_to_all(tiles, ('band', 'dom', 'lat'), 0, 0, tiled=True)]
    all_to_all x0 -> x2, starting transfers between devices: none -> 12.9 us  [summed_tile(): shares = lax.all_to_all(tiles, ('band', 'dom', 'lat'), 0, 0, tiled=True)]
    ppermute x8, waiting for transfers between devices: 10.8 us -> 4.48 us  [with_halo(): lax.ppermute(head, axis, [((i + 1) % count, i) for i in range(ends)])]
    convert_element_type x0 -> x4, local copies, waits for them, and re-layouts: none -> 4.26 us  [summed_tile(): tiles = as_tiles(gradient).astype(jnp.bfloat16)]
    gather x1, local copies, waits for them, and re-layouts: 7.53 us -> 3.94 us  [on_device(): jnp.take(grid_raw, grid_from, axis=0)]
    dot_general x8, matrix products: 7.13 us -> 4.53 us  [matmul(): return jnp.dot(first_op, second_op, preferred_element_type=jnp.float32)]
  transfers between devices with their start and end apart: 18 -> 18, of which waited for: 10 -> 7; matrix products, arithmetic and copies ran while one was open for 10% -> 28% of each run, Pallas kernels for 0% -> 0%
where the time goes in v1:
time: 121 us; the launch traced here: 120 us
  starting transfers between devices  37.3 us (31%)
  local copies, waits for them, and re-layouts  30.9 us (26%)
  waiting for transfers between devices  23.5 us (19%)
  matrix products  14.9 us (12%)
  other arithmetic  11 us (9%)
  between operations  2.53 us (2%)
    ppermute x8, starting transfers between devices, with_halo(): lax.ppermute(tail, axis, [(i, (i + 1) % count) for i in range(ends)])  16 us
    all_to_all x2, waiting for transfers between devices, summed_tile(): shares = lax.all_to_all(tiles, ('band', 'dom', 'lat'), 0, 0, tiled=True)  13.8 us
    all_to_all x2, starting transfers between devices, summed_tile(): shares = lax.all_to_all(tiles, ('band', 'dom', 'lat'), 0, 0, tiled=True)  12.9 us
    ppermute x8, starting transfers between devices, with_halo(): lax.ppermute(head, axis, [((i + 1) % count, i) for i in range(ends)])  8.44 us
    dot_general x2, matrix products, outer_sum(): lax.dot_general(rows, terms, (((0,), (0,)), ((), ())), preferred_element_...  6.24 us
    ppermute x8, waiting for transfers between devices, with_halo(): lax.ppermute(tail, axis, [(i, (i + 1) % count) for i in range(ends)])  5.23 us
    gather x1, local copies, waits for them, and re-layouts, on_device(): jnp.take(matmul(cycle_in, w_gr), grid_to, axis=0)  4.86 us
    gather x1, local copies, waits for them, and re-layouts, on_device(): jnp.take(back_cycle, grid_to, axis=0) * silu_slope(enc_pre) * grid_live  4.86 us
  transfers between devices with their start and end apart: 18, of which 7 were waited for; matrix products, arithmetic and copies ran while one was open for 28% of the time, Pallas kernels for 0%

profile of v1, /device:TPU:0, one launch (start us, length us, event | category | flops | bytes accessed | tf_op | source)
XLA Modules:
  0.0 120.2 jit_solution(6219754265725418656)
XLA Ops:
  0.6 1.4 %collective-permute-start.1 = (bf16[3,360,227]{1,2,0:T(8,128)(2,1)}, bf16[3,360,227]{1,2,0:T(8,128)(2,1)S(1)}, u32[]{:S(2)}, u32[]{:S(2)}) collective-permute-start(bf16[3,360,227]{1,2,0:T(8,128)(2,1)} %param.20), channel_id=1, source_target_pairs={{4,0},{8,4},{12,8},{5,1},{9,5},{13,9},{6,2},{10,6},{14,10},{7,3},{... | collective-permute-start | bytes 1470968 | tf_op jit(solution)/shard_map/ppermute | solution.py:19
  2.1 5.6 %collective-permute-start = (bf16[3,360,227]{1,2,0:T(8,128)(2,1)}, bf16[3,360,227]{1,2,0:T(8,128)(2,1)S(1)}, u32[]{:S(2)}, u32[]{:S(2)}) collective-permute-start(bf16[3,360,227]{1,2,0:T(8,128)(2,1)} %param.20), channel_id=1, source_target_pairs={{0,4},{4,8},{8,12},{1,5},{5,9},{9,13},{2,6},{6,10},{10,14},{3,7},{... | collective-permute-start | bytes 1470968 | tf_op jit(solution)/shard_map/ppermute | solution.py:17
  16.1 1.3 %fusion.28 = f32[64,512]{1,0:T(8,128)S(1)} fusion(bf16[512,512]{1,0:T(8,128)(2,1)} %param.23, bf16[16,512]{1,0:T(8,128)(2,1)S(1)} %collective-permute-done.3, bf16[32,512]{1,0:T(8,128)(2,1)} %param.28, bf16[16,512]{1,0:T(8,128)(2,1)S(1)} %collective-permute-done.2), kind=kOutput, calls=%fused_computation.61 | convolution fusion | flops 33751040 | bytes 720896 | tf_op jit(solution)/shard_map/dot_general | solution.py:32
  17.4 4.9 %gather_fusion.3 = f32[1024,512]{1,0:T(8,128)} fusion(f32[64,512]{1,0:T(8,128)S(1)} %fusion.28, s32[1024]{0:T(1024)S(1)} %fusion.48), kind=kCustom, calls=%fused_computation.clone | custom fusion | bytes 4198400 | tf_op jit(solution)/shard_map/jit(_take)/gather | solution.py:93
  22.3 1.4 %pad_maximum_fusion = bf16[9,360,227]{1,2,0:T(8,128)(2,1)} fusion(bf16[3,360,227]{1,2,0:T(8,128)(2,1)S(1)} %collective-permute-done.1, bf16[3,360,227]{1,2,0:T(8,128)(2,1)S(1)} %copy-done.12, bf16[3,360,227]{1,2,0:T(8,128)(2,1)S(1)} %collective-permute-done), kind=kLoop, calls=%fused_computation.15 | loop fusion | flops 1470960 | bytes 2941920 | tf_op jit(solution)/shard_map/concatenate | solution.py:15
  23.7 2.6 %copy.20 = bf16[9,360,227]{2,1,0:T(8,128)(2,1)S(1)} copy(bf16[9,360,227]{1,2,0:T(8,128)(2,1)} %pad_maximum_fusion) | data formatting | bytes 2941920 | tf_op jit(solution)/shard_map/concatenate | solution.py:15
  26.3 3.9 %gather_fusion = bf16[1024,227]{1,0:T(8,128)(2,1)S(1)} fusion(bf16[3240,227]{1,0:T(8,128)(2,1)S(1)} %bitcast.46, s32[1024]{0:T(1024)S(1)} %broadcast_clamp_fusion), kind=kCustom, calls=%fused_computation.4 | custom fusion | bytes 933888 | tf_op jit(solution)/shard_map/jit(_take)/gather | solution.py:89
  32.0 1.7 %copy-done.1 = f32[1024,512]{1,0:T(8,128)S(1)} copy-done((f32[1024,512]{1,0:T(8,128)S(1)}, f32[1024,512]{1,0:T(8,128)}, u32[]{:S(2)}) %copy-start.1) | copy-done | bytes 2097176
  33.7 2.0 %fusion.2 = f32[64,512]{1,0:T(8,128)S(1)} fusion(f32[1024,512]{1,0:T(8,128)S(1)} %fusion.72, f32[1024,512]{1,0:T(8,128)S(1)} %copy-done.1, pred[1024]{0:T(1024)(128)(4,1)S(1)} %get-tuple-element.28, f32[1024]{0:T(1024)S(1)} %get-tuple-element.27, s32[1024]{0:T(1024)S(1)} %bitcast.57), kind=kOutput, calls=%fused_computation.11 | convolution fusion | flops 405929984 | bytes 4334592 | tf_op jit(solution)/shard_map/dot_general | solution.py:48
  35.7 1.8 %collective-permute-start.5 = (f32[16,512]{1,0:T(8,128)S(1)}, f32[16,512]{1,0:T(8,128)S(1)}, u32[]{:S(2)}, u32[]{:S(2)}) collective-permute-start(f32[16,512]{1,0:T(8,128)S(1)} %get-tuple-element.10), channel_id=1, source_target_pairs={{1,0},{2,1},{3,2},{0,3},{5,4},{6,5},{7,6},{4,7},{9,8},{10,9},{11,1... | collective-permute-start | bytes 98312 | tf_op jit(solution)/shard_map/ppermute | solution.py:19
  37.5 1.6 %collective-permute-done.5 = f32[16,512]{1,0:T(8,128)S(1)} collective-permute-done((f32[16,512]{1,0:T(8,128)S(1)}, f32[16,512]{1,0:T(8,128)S(1)}, u32[]{:S(2)}, u32[]{:S(2)}) %collective-permute-start.5) | collective-permute-done | bytes 32800 | tf_op jit(solution)/shard_map/ppermute | solution.py:19
  39.1 1.8 %collective-permute-done.4 = f32[16,512]{1,0:T(8,128)S(1)} collective-permute-done((f32[16,512]{1,0:T(8,128)S(1)}, f32[16,512]{1,0:T(8,128)S(1)}, u32[]{:S(2)}, u32[]{:S(2)}) %collective-permute-start.4) | collective-permute-done | bytes 32800 | tf_op jit(solution)/shard_map/ppermute | solution.py:17
  42.6 1.9 %collective-permute-done.6 = bf16[16,512]{1,0:T(8,128)(2,1)S(1)} collective-permute-done((bf16[16,512]{1,0:T(8,128)(2,1)S(1)}, bf16[16,512]{1,0:T(8,128)(2,1)S(1)}, u32[]{:S(2)}, u32[]{:S(2)}) %collective-permute-start.6) | collective-permute-done | bytes 16416 | tf_op jit(solution)/shard_map/ppermute | solution.py:17
  44.5 1.3 %collective-permute-start.9 = (bf16[1,64,512]{2,1,0:T(8,128)(2,1)S(1)}, bf16[1,64,512]{2,1,0:T(8,128)(2,1)S(1)}, u32[]{:S(2)}, u32[]{:S(2)}) collective-permute-start(bf16[1,64,512]{2,1,0:T(8,128)(2,1)S(1)} %maximum_bitcast_fusion), channel_id=1, source_target_pairs={{4,0},{8,4},{12,8},{5,1},{9,5},{13,9},{6,2},{10,6},{14,10},{7,3},{... | collective-permute-start | bytes 196616 | tf_op jit(solution)/shard_map/ppermute | solution.py:19
  45.8 4.5 %collective-permute-start.8 = (bf16[1,64,512]{2,1,0:T(8,128)(2,1)S(1)}, bf16[1,64,512]{2,1,0:T(8,128)(2,1)S(1)}, u32[]{:S(2)}, u32[]{:S(2)}) collective-permute-start(bf16[1,64,512]{2,1,0:T(8,128)(2,1)S(1)} %maximum_bitcast_fusion), channel_id=1, source_target_pairs={{0,4},{4,8},{8,12},{1,5},{5,9},{9,13},{2,6},{6,10},{10,14},{3,7},{... | collective-permute-start | bytes 196616 | tf_op jit(solution)/shard_map/ppermute | solution.py:17
  50.5 1.6 %gather_fusion.4 = f32[512,512]{1,0:T(8,128)S(1)} fusion(f32[32,512]{1,0:T(8,128)S(1)} %fusion.74, s32[1024]{0:T(1024)S(1)} %pad_clamp_fusion), kind=kCustom, calls=%fused_computation.1.clone | custom fusion | bytes 2099200 | tf_op jit(solution)/shard_map/jit(_take)/gather | solution.py:111
  52.5 1.6 %gather_fusion.1 = f32[512,512]{1,0:T(8,128)S(1)} fusion(f32[192,512]{1,0:T(8,128)S(1)} %fusion.73, s32[1024]{0:T(1024)S(1)} %pad_clamp_fusion.1), kind=kCustom, calls=%fused_computation.5 | custom fusion | bytes 2099200 | tf_op jit(solution)/shard_map/jit(_take)/gather | solution.py:111
  56.4 2.3 %gather_fusion.5 = f32[512,512]{1,0:T(8,128)} fusion(f32[32,512]{1,0:T(8,128)S(1)} %fusion.35, s32[1024]{0:T(1024)S(1)} %pad_clamp_fusion), kind=kCustom, calls=%fused_computation.3.clone | custom fusion | bytes 2099200 | tf_op jit(solution)/shard_map/jit(_take)/gather | solution.py:121
  58.8 1.8 %fusion.7 = bf16[512,512]{1,0:T(8,128)(2,1)S(1)} fusion(f32[512,512]{1,0:T(8,128)} %gather_fusion.5, f32[512]{0:T(512)S(1)} %copy-done.19, pred[512]{0:T(512)(128)(4,1)S(1)} %copy-done.26, f32[512,512]{1,0:T(8,128)S(1)} %gather_fusion.4, f32[512,512]{1,0:T(8,128)S(1)} %gather_fusion.1, pred[512]{0:T(512)(128)(4,1)S(1)} %copy-done.23), kind=kLoop, calls=%fused_computation.26 | loop fusion | flops 3670016 | bytes 3673088 | tf_op jit(solution)/shard_map/convert_element_type | solution.py:121
  60.9 1.3 %collective-permute-start.11 = (bf16[64,512]{1,0:T(8,128)(2,1)S(1)}, bf16[64,512]{1,0:T(8,128)(2,1)S(1)}, u32[]{:S(2)}, u32[]{:S(2)}) collective-permute-start(bf16[64,512]{1,0:T(8,128)(2,1)S(1)} %get-tuple-element.8), channel_id=1, source_target_pairs={{4,0},{8,4},{12,8},{5,1},{9,5},{13,9},{6,2},{10,6},{14,10},{7,3},{... | collective-permute-start | bytes 196616 | tf_op jit(solution)/shard_map/ppermute | solution.py:19
  62.2 4.9 %collective-permute-start.10 = (bf16[64,512]{1,0:T(8,128)(2,1)S(1)}, bf16[64,512]{1,0:T(8,128)(2,1)S(1)}, u32[]{:S(2)}, u32[]{:S(2)}) collective-permute-start(bf16[64,512]{1,0:T(8,128)(2,1)S(1)} %get-tuple-element.7), channel_id=1, source_target_pairs={{0,4},{4,8},{8,12},{1,5},{5,9},{9,13},{2,6},{6,10},{10,14},{3,7},{... | collective-permute-start | bytes 196616 | tf_op jit(solution)/shard_map/ppermute | solution.py:17
  67.1 2.0 %gather_fusion.2 = bf16[512,512]{1,0:T(8,128)(2,1)S(1)} fusion(bf16[192,512]{1,0:T(8,128)(2,1)S(1)} %bitcast.45, s32[1024]{0:T(1024)S(1)} %pad_clamp_fusion.1), kind=kCustom, calls=%fused_computation.6 | custom fusion | bytes 1050624 | tf_op jit(solution)/shard_map/jit(_take)/gather | solution.py:124
  69.7 1.4 %convolution_convert_fusion = bf16[512,512]{1,0:T(8,128)(2,1)} fusion(bf16[512,512]{1,0:T(8,128)(2,1)S(1)} %fusion.7, bf16[512,512]{1,0:T(8,128)(2,1)S(1)} %gather_fusion.2, pred[512]{0:T(512)(128)(4,1)S(1)} %copy-done.24), kind=kOutput, calls=%fused_computation.16 | convolution fusion | flops 268959744 | bytes 1573376 | tf_op jit(solution)/shard_map/dot_general | solution.py:42
  71.1 1.3 %convert_element_type.130 = bf16[4,128,4,128]{3,2,1,0:T(4,128)(2,1)S(1)} reshape(bf16[512,512]{1,0:T(8,128)(2,1)} %convolution_convert_fusion) | data formatting | bytes 1048576 | tf_op jit(solution)/shard_map/convert_element_type | solution.py:160
  73.3 6.8 %all-to-all-start.1 = ((bf16[16,128,128]{2,1,0:T(8,128)(2,1)}), bf16[16,128,128]{2,1,0:T(8,128)(2,1)S(1)}, u32[]{:S(2)}, u32[]{:S(2)}) async-start(bf16[16,128,128]{2,1,0:T(8,128)(2,1)} %bitcast.47), calls=%async_computation.1 | async-start | bytes 1048576 | tf_op jit(solution)/shard_map/all_to_all | solution.py:161
  81.8 1.7 %collective-permute-start.15 = (f32[16,512]{1,0:T(8,128)S(1)}, f32[16,512]{1,0:T(8,128)S(1)}, u32[]{:S(2)}, u32[]{:S(2)}) collective-permute-start(f32[16,512]{1,0:T(8,128)S(1)} %get-tuple-element.12), channel_id=1, source_target_pairs={{1,0},{2,1},{3,2},{0,3},{5,4},{6,5},{7,6},{4,7},{9,8},{10,9},{11,1... | collective-permute-start | bytes 98312 | tf_op jit(solution)/shard_map/ppermute | solution.py:19
  83.6 2.0 %collective-permute-done.15 = f32[16,512]{1,0:T(8,128)S(1)} collective-permute-done((f32[16,512]{1,0:T(8,128)S(1)}, f32[16,512]{1,0:T(8,128)S(1)}, u32[]{:S(2)}, u32[]{:S(2)}) %collective-permute-start.15) | collective-permute-done | bytes 32800 | tf_op jit(solution)/shard_map/ppermute | solution.py:19
  85.5 1.6 %collective-permute-done.14 = f32[16,512]{1,0:T(8,128)S(1)} collective-permute-done((f32[16,512]{1,0:T(8,128)S(1)}, f32[16,512]{1,0:T(8,128)S(1)}, u32[]{:S(2)}, u32[]{:S(2)}) %collective-permute-start.14) | collective-permute-done | bytes 32800 | tf_op jit(solution)/shard_map/ppermute | solution.py:17
  87.1 4.9 %gather_fusion.6 = f32[1024,512]{1,0:T(8,128)} fusion(f32[64,512]{1,0:T(8,128)S(1)} %pad_maximum_fusion.2, s32[1024]{0:T(1024)S(1)} %fusion.48), kind=kCustom, calls=%fused_computation.2.clone | custom fusion | bytes 4198400 | tf_op jit(solution)/shard_map/jit(_take)/gather | solution.py:148
  92.0 4.9 %convolution_convert_fusion.1 = bf16[512,512]{1,0:T(8,128)(2,1)} fusion(bf16[1024,512]{1,0:T(8,128)(2,1)} %copy-done.11, f32[1024,512]{1,0:T(8,128)} %gather_fusion.6, f32[1024]{0:T(1024)S(1)} %copy-done.21, pred[1024]{0:T(1024)(128)(4,1)S(1)} %copy-done.28, f32[1024,512]{1,0:T(8,128)} %copy-done.3, f32[1024,512]{1,0:T(8,128)S(1)} %copy-done.2), kind=kOutput, calls=%fused_computation.17 | convolution fusion | flops 543948800 | bytes 7869440 | tf_op jit(solution)/shard_map/dot_general | solution.py:42
  98.9 6.1 %all-to-all-start = ((bf16[16,128,128]{2,1,0:T(8,128)(2,1)}), bf16[16,128,128]{2,1,0:T(8,128)(2,1)S(1)}, u32[]{:S(2)}, u32[]{:S(2)}) async-start(bf16[16,128,128]{2,1,0:T(8,128)(2,1)} %bitcast.14), calls=%async_computation | async-start | bytes 1048576 | tf_op jit(solution)/shard_map/all_to_all | solution.py:161
  105.7 13.8 %all-to-all-done = bf16[16,128,128]{2,1,0:T(8,128)(2,1)S(1)} async-done(((bf16[16,128,128]{2,1,0:T(8,128)(2,1)}), bf16[16,128,128]{2,1,0:T(8,128)(2,1)S(1)}, u32[]{:S(2)}, u32[]{:S(2)}) %all-to-all-start) | async-done | bytes 524320 | tf_op jit(solution)/shard_map/all_to_all | solution.py:161
  (118 shorter events, 20.3 us)
Async XLA Ops:
  0.6 30.4 %copy-start = (bf16[512,512]{1,0:T(8,128)(2,1)S(1)}, bf16[512,512]{1,0:T(8,128)(2,1)}, u32[]{:S(2)}) copy-start(bf16[512,512]{1,0:T(8,128)(2,1)} %param.22) | copy-start | bytes 1572868
  0.6 21.6 %collective-permute-start.1 = (bf16[3,360,227]{1,2,0:T(8,128)(2,1)}, bf16[3,360,227]{1,2,0:T(8,128)(2,1)S(1)}, u32[]{:S(2)}, u32[]{:S(2)}) collective-permute-start(bf16[3,360,227]{1,2,0:T(8,128)(2,1)} %param.20), channel_id=1, source_target_pairs={{4,0},{8,4},{12,8},{5,1},{9,5},{13,9},{6,2},{10,6},{14,10},{7,3},{... | collective-permute-start | bytes 1470968 | tf_op jit(solution)/shard_map/ppermute | solution.py:19
  2.1 20.2 %collective-permute-start = (bf16[3,360,227]{1,2,0:T(8,128)(2,1)}, bf16[3,360,227]{1,2,0:T(8,128)(2,1)S(1)}, u32[]{:S(2)}, u32[]{:S(2)}) collective-permute-start(bf16[3,360,227]{1,2,0:T(8,128)(2,1)} %param.20), channel_id=1, source_target_pairs={{0,4},{4,8},{8,12},{1,5},{5,9},{9,13},{2,6},{6,10},{10,14},{3,7},{... | collective-permute-start | bytes 1470968 | tf_op jit(solution)/shard_map/ppermute | solution.py:17
  8.4 7.7 %collective-permute-start.3 = (bf16[16,512]{1,0:T(8,128)(2,1)S(1)}, bf16[16,512]{1,0:T(8,128)(2,1)S(1)}, u32[]{:S(2)}, u32[]{:S(2)}) collective-permute-start(bf16[16,512]{1,0:T(8,128)(2,1)S(1)} %get-tuple-element.20), channel_id=1, source_target_pairs={{1,0},{2,1},{3,2},{0,3},{5,4},{6,5},{7,6},{4,7},{9,8},{10,9},{11,1... | collective-permute-start | bytes 49160 | tf_op jit(solution)/shard_map/ppermute | solution.py:19
  9.2 6.9 %collective-permute-start.2 = (bf16[16,512]{1,0:T(8,128)(2,1)S(1)}, bf16[16,512]{1,0:T(8,128)(2,1)S(1)}, u32[]{:S(2)}, u32[]{:S(2)}) collective-permute-start(bf16[16,512]{1,0:T(8,128)(2,1)S(1)} %get-tuple-element.19), channel_id=1, source_target_pairs={{0,1},{1,2},{2,3},{3,0},{4,5},{5,6},{6,7},{7,4},{8,9},{9,10},{10,1... | collective-permute-start | bytes 49160 | tf_op jit(solution)/shard_map/ppermute | solution.py:17
  12.7 19.4 %copy-start.20 = (f32[1024]{0:T(1024)}, f32[1024]{0:T(1024)S(1)}, u32[]{:S(2)}) copy-start(f32[1024]{0:T(1024)S(1)} %get-tuple-element.27) | copy-start | bytes 12292
  12.7 19.4 %copy-start.27 = (pred[1024]{0:T(1024)(128)(4,1)}, pred[1024]{0:T(1024)(128)(4,1)S(1)}, u32[]{:S(2)}) copy-start(pred[1024]{0:T(1024)(128)(4,1)S(1)} %get-tuple-element.28) | copy-start | bytes 3076
  14.7 39.4 %copy-start.18 = (f32[512]{0:T(512)}, f32[512]{0:T(512)S(1)}, u32[]{:S(2)}) copy-start(f32[512]{0:T(512)S(1)} %get-tuple-element.29) | copy-start | bytes 6148
  14.7 39.5 %copy-start.25 = (pred[512]{0:T(512)(128)(4,1)}, pred[512]{0:T(512)(128)(4,1)S(1)}, u32[]{:S(2)}) copy-start(pred[512]{0:T(512)(128)(4,1)S(1)} %get-tuple-element.30) | copy-start | bytes 1540
  16.1 38.1 %copy-start.22 = (pred[512]{0:T(512)(128)(4,1)}, pred[512]{0:T(512)(128)(4,1)S(1)}, u32[]{:S(2)}) copy-start(pred[512]{0:T(512)(128)(4,1)S(1)} %compare_and_fusion.3) | copy-start | bytes 1540
  33.7 7.2 %copy-start.6 = (bf16[512,512]{1,0:T(8,128)(2,1)S(1)}, bf16[512,512]{1,0:T(8,128)(2,1)}, u32[]{:S(2)}) copy-start(bf16[512,512]{1,0:T(8,128)(2,1)} %param.24) | copy-start | bytes 1572868
  33.7 7.2 %copy-start.13 = (bf16[32,512]{1,0:T(8,128)(2,1)S(1)}, bf16[32,512]{1,0:T(8,128)(2,1)}, u32[]{:S(2)}) copy-start(bf16[32,512]{1,0:T(8,128)(2,1)} %param.28) | copy-start | bytes 98308
  33.7 16.6 %copy-start.4 = (bf16[512,512]{1,0:T(8,128)(2,1)S(1)}, bf16[512,512]{1,0:T(8,128)(2,1)}, u32[]{:S(2)}) copy-start(bf16[512,512]{1,0:T(8,128)(2,1)} %param.26) | copy-start | bytes 1572868
  35.7 3.4 %collective-permute-start.5 = (f32[16,512]{1,0:T(8,128)S(1)}, f32[16,512]{1,0:T(8,128)S(1)}, u32[]{:S(2)}, u32[]{:S(2)}) collective-permute-start(f32[16,512]{1,0:T(8,128)S(1)} %get-tuple-element.10), channel_id=1, source_target_pairs={{1,0},{2,1},{3,2},{0,3},{5,4},{6,5},{7,6},{4,7},{9,8},{10,9},{11,1... | collective-permute-start | bytes 98312 | tf_op jit(solution)/shard_map/ppermute | solution.py:19
  37.5 3.4 %collective-permute-start.4 = (f32[16,512]{1,0:T(8,128)S(1)}, f32[16,512]{1,0:T(8,128)S(1)}, u32[]{:S(2)}, u32[]{:S(2)}) collective-permute-start(f32[16,512]{1,0:T(8,128)S(1)} %get-tuple-element.9), channel_id=1, source_target_pairs={{0,1},{1,2},{2,3},{3,0},{4,5},{5,6},{6,7},{7,4},{8,9},{9,10},{10,1... | collective-permute-start | bytes 98312 | tf_op jit(solution)/shard_map/ppermute | solution.py:17
  41.1 1.5 %collective-permute-start.7 = (bf16[16,512]{1,0:T(8,128)(2,1)S(1)}, bf16[16,512]{1,0:T(8,128)(2,1)S(1)}, u32[]{:S(2)}, u32[]{:S(2)}) collective-permute-start(bf16[16,512]{1,0:T(8,128)(2,1)S(1)} %get-tuple-element.18), channel_id=1, source_target_pairs={{1,0},{2,1},{3,2},{0,3},{5,4},{6,5},{7,6},{4,7},{9,8},{10,9},{11,1... | collective-permute-start | bytes 49160 | tf_op jit(solution)/shard_map/ppermute | solution.py:19
  41.2 3.3 %collective-permute-start.6 = (bf16[16,512]{1,0:T(8,128)(2,1)S(1)}, bf16[16,512]{1,0:T(8,128)(2,1)S(1)}, u32[]{:S(2)}, u32[]{:S(2)}) collective-permute-start(bf16[16,512]{1,0:T(8,128)(2,1)S(1)} %get-tuple-element.17), channel_id=1, source_target_pairs={{0,1},{1,2},{2,3},{3,0},{4,5},{5,6},{6,7},{7,4},{8,9},{9,10},{10,1... | collective-permute-start | bytes 49160 | tf_op jit(solution)/shard_map/ppermute | solution.py:17
  44.5 7.7 %collective-permute-start.9 = (bf16[1,64,512]{2,1,0:T(8,128)(2,1)S(1)}, bf16[1,64,512]{2,1,0:T(8,128)(2,1)S(1)}, u32[]{:S(2)}, u32[]{:S(2)}) collective-permute-start(bf16[1,64,512]{2,1,0:T(8,128)(2,1)S(1)} %maximum_bitcast_fusion), channel_id=1, source_target_pairs={{4,0},{8,4},{12,8},{5,1},{9,5},{13,9},{6,2},{10,6},{14,10},{7,3},{... | collective-permute-start | bytes 196616 | tf_op jit(solution)/shard_map/ppermute | solution.py:19
  45.8 6.4 %collective-permute-start.8 = (bf16[1,64,512]{2,1,0:T(8,128)(2,1)S(1)}, bf16[1,64,512]{2,1,0:T(8,128)(2,1)S(1)}, u32[]{:S(2)}, u32[]{:S(2)}) collective-permute-start(bf16[1,64,512]{2,1,0:T(8,128)(2,1)S(1)} %maximum_bitcast_fusion), channel_id=1, source_target_pairs={{0,4},{4,8},{8,12},{1,5},{5,9},{9,13},{2,6},{6,10},{10,14},{3,7},{... | collective-permute-start | bytes 196616 | tf_op jit(solution)/shard_map/ppermute | solution.py:17
  60.9 8.2 %collective-permute-start.11 = (bf16[64,512]{1,0:T(8,128)(2,1)S(1)}, bf16[64,512]{1,0:T(8,128)(2,1)S(1)}, u32[]{:S(2)}, u32[]{:S(2)}) collective-permute-start(bf16[64,512]{1,0:T(8,128)(2,1)S(1)} %get-tuple-element.8), channel_id=1, source_target_pairs={{4,0},{8,4},{12,8},{5,1},{9,5},{13,9},{6,2},{10,6},{14,10},{7,3},{... | collective-permute-start | bytes 196616 | tf_op jit(solution)/shard_map/ppermute | solution.py:19
  62.2 7.5 %copy-start.24 = (pred[512]{0:T(512)(128)(4,1)S(1)}, pred[512]{0:T(512)(128)(4,1)}, u32[]{:S(2)}) copy-start(pred[512]{0:T(512)(128)(4,1)} %copy-done.22) | copy-start | bytes 1540
  62.2 6.9 %collective-permute-start.10 = (bf16[64,512]{1,0:T(8,128)(2,1)S(1)}, bf16[64,512]{1,0:T(8,128)(2,1)S(1)}, u32[]{:S(2)}, u32[]{:S(2)}) collective-permute-start(bf16[64,512]{1,0:T(8,128)(2,1)S(1)} %get-tuple-element.7), channel_id=1, source_target_pairs={{0,4},{4,8},{8,12},{1,5},{5,9},{9,13},{2,6},{6,10},{10,14},{3,7},{... | collective-permute-start | bytes 196616 | tf_op jit(solution)/shard_map/ppermute | solution.py:17
  69.2 11.0 %collective-permute-start.13 = (bf16[16,512]{1,0:T(8,128)(2,1)S(1)}, bf16[16,512]{1,0:T(8,128)(2,1)}, u32[]{:S(2)}, u32[]{:S(2)}) collective-permute-start(bf16[16,512]{1,0:T(8,128)(2,1)S(1)} %get-tuple-element.16), channel_id=1, source_target_pairs={{1,0},{2,1},{3,2},{0,3},{5,4},{6,5},{7,6},{4,7},{9,8},{10,9},{11,1... | collective-permute-start | bytes 49160 | tf_op jit(solution)/shard_map/ppermute | solution.py:19
  69.2 10.9 %collective-permute-start.12 = (bf16[16,512]{1,0:T(8,128)(2,1)S(1)}, bf16[16,512]{1,0:T(8,128)(2,1)}, u32[]{:S(2)}, u32[]{:S(2)}) collective-permute-start(bf16[16,512]{1,0:T(8,128)(2,1)S(1)} %get-tuple-element.15), channel_id=1, source_target_pairs={{0,1},{1,2},{2,3},{3,0},{4,5},{5,6},{6,7},{7,4},{8,9},{9,10},{10,1... | collective-permute-start | bytes 49160 | tf_op jit(solution)/shard_map/ppermute | solution.py:17
  71.1 9.8 %copy-start.10 = (bf16[512,512]{1,0:T(8,128)(2,1)S(1)}, bf16[512,512]{1,0:T(8,128)(2,1)}, u32[]{:S(2)}) copy-start(bf16[512,512]{1,0:T(8,128)(2,1)} %param.25) | copy-start | bytes 1572868
  71.1 10.1 %copy-start.5 = (bf16[512,512]{1,0:T(8,128)(2,1)S(1)}, bf16[512,512]{1,0:T(8,128)(2,1)}, u32[]{:S(2)}) copy-start(bf16[512,512]{1,0:T(8,128)(2,1)} %param.26) | copy-start | bytes 1572868
  72.3 9.2 %copy-start.7 = (bf16[512,512]{1,0:T(8,128)(2,1)S(1)}, bf16[512,512]{1,0:T(8,128)(2,1)}, u32[]{:S(2)}) copy-start(bf16[512,512]{1,0:T(8,128)(2,1)} %param.24) | copy-start | bytes 1572868
  73.3 25.7 %all-to-all-start.1 = ((bf16[16,128,128]{2,1,0:T(8,128)(2,1)}), bf16[16,128,128]{2,1,0:T(8,128)(2,1)S(1)}, u32[]{:S(2)}, u32[]{:S(2)}) async-start(bf16[16,128,128]{2,1,0:T(8,128)(2,1)} %bitcast.47), calls=%async_computation.1 | async-start | bytes 1048576 | tf_op jit(solution)/shard_map/all_to_all | solution.py:161
  81.8 3.7 %collective-permute-start.15 = (f32[16,512]{1,0:T(8,128)S(1)}, f32[16,512]{1,0:T(8,128)S(1)}, u32[]{:S(2)}, u32[]{:S(2)}) collective-permute-start(f32[16,512]{1,0:T(8,128)S(1)} %get-tuple-element.12), channel_id=1, source_target_pairs={{1,0},{2,1},{3,2},{0,3},{5,4},{6,5},{7,6},{4,7},{9,8},{10,9},{11,1... | collective-permute-start | bytes 98312 | tf_op jit(solution)/shard_map/ppermute | solution.py:19
  83.6 3.5 %collective-permute-start.14 = (f32[16,512]{1,0:T(8,128)S(1)}, f32[16,512]{1,0:T(8,128)S(1)}, u32[]{:S(2)}, u32[]{:S(2)}) collective-permute-start(f32[16,512]{1,0:T(8,128)S(1)} %get-tuple-element.11), channel_id=1, source_target_pairs={{0,1},{1,2},{2,3},{3,0},{4,5},{5,6},{6,7},{7,4},{8,9},{9,10},{10,1... | collective-permute-start | bytes 98312 | tf_op jit(solution)/shard_map/ppermute | solution.py:17
  87.1 4.9 %copy-start.2 = (f32[1024,512]{1,0:T(8,128)S(1)}, f32[1024,512]{1,0:T(8,128)}, u32[]{:S(2)}) copy-start(f32[1024,512]{1,0:T(8,128)} %gather_fusion.3) | copy-start | bytes 6291460
  98.9 20.5 %all-to-all-start = ((bf16[16,128,128]{2,1,0:T(8,128)(2,1)}), bf16[16,128,128]{2,1,0:T(8,128)(2,1)S(1)}, u32[]{:S(2)}, u32[]{:S(2)}) async-start(bf16[16,128,128]{2,1,0:T(8,128)(2,1)} %bitcast.14), calls=%async_computation | async-start | bytes 1048576 | tf_op jit(solution)/shard_map/all_to_all | solution.py:161
  (16 other events, 44.1 us)

commit v2 on v1

v2 whole, which is shorter than its diff:
```python
import functools

import jax
import jax.numpy as jnp
from jax import lax
from jax.experimental import pallas as pl
from jax.experimental.pallas import tpu as pltpu
from jax.sharding import PartitionSpec as P

F32 = jnp.float32
BF16 = jnp.bfloat16
LANES = 128


def mm(a, b):
    return jnp.dot(a, b, preferred_element_type=F32)


def mm_nt(a, b):
    return lax.dot_general(a, b, (((1,), (1,)), ((), ())), preferred_element_type=F32)


def mm_tn(a, b):
    return lax.dot_general(a, b, (((0,), (0,)), ((), ())), preferred_element_type=F32)


def halves(x):
    high = x.astype(BF16)
    return high, (x - high.astype(F32)).astype(BF16)


def silu_parts(x):
    g = 1.0 / (1.0 + jnp.exp(-x))
    return x * g, g * (1.0 + x * (1.0 - g))


def ones_at(mask):
    return jnp.where(mask, 1.0, 0.0).astype(BF16)


def columns(row):
    count = row.shape[1]
    parts = [
        jnp.broadcast_to(row[:, i : i + LANES], (LANES, LANES)).T
        for i in range(0, count, LANES)
    ]
    return parts[0] if len(parts) == 1 else jnp.concatenate(parts, axis=0)


def hits_from(cols, width, period, start=0):
    parts = []
    for i in range(0, width, LANES):
        size = min(LANES, width - i)
        lane = lax.broadcasted_iota(jnp.int32, (cols.shape[0], size), 1) + i
        if period < width:
            lane = lax.rem(lane, period)
        parts.append(ones_at(cols[:, :size] == lane + start))
    return parts[0] if len(parts) == 1 else jnp.concatenate(parts, axis=1)


def hits_to(row, count):
    return ones_at(lax.broadcasted_iota(jnp.int32, (count, row.shape[1]), 0) == row)


def live_only(row, count, first=0):
    slot = lax.broadcasted_iota(jnp.int32, row.shape, 1) + first
    return jnp.where(slot < count, row, -1)


def even_on(axis):
    return lax.rem(lax.axis_index(axis), 2) == 0


def own_gather_kernel(send, grid, near, far, mesh_in, w_gr, rows_out, table_out):
    band_rows, cols, _ = grid.shape
    node_count = mesh_in.shape[0]
    rim = node_count // 2
    even = even_on("lat")
    left = jnp.where(even, far[...], near[...])[rim:]
    right = jnp.where(even, near[...], far[...])[:rim]
    cycle = jnp.concatenate([left, mesh_in[...], right], axis=0)
    high, low = halves(mm(cycle, w_gr[...]))
    table_out[: 2 * node_count] = high
    table_out[2 * node_count :] = low
    block = 256
    for first in range(0, send.shape[2], block):
        index = columns(send[0, :, first : first + block])
        total = None
        for k in range(band_rows):
            hit = hits_from(index, cols, cols, (band_rows + k) * cols)
            part = mm(hit, grid[k])
            total = part if total is None else total + part
        rows_out[first : first + block] = total.astype(BF16)


def encode_kernel(
    send, recv, count, near, far, own, table, w_grid, w_gs,
    senders_out, slope_out, part_out, near_out, far_out,
):
    band_rows, cols, _ = near.shape
    cycle = table.shape[0] // 2
    half = cycle // 2
    even_band = even_on("band")
    near_base = jnp.where(even_band, 2 * band_rows * cols, 0)
    far_base = jnp.where(even_band, 0, 2 * band_rows * cols)
    block = 256
    sums = None
    for first in range(0, send.shape[2], block):
        part_of = slice(first, first + block)
        index = columns(send[0, :, part_of])
        total = own[part_of].astype(F32)
        for base, halo in ((near_base, near), (far_base, far)):
            for k in range(band_rows):
                total = total + mm(hits_from(index, cols, cols, base + k * cols), halo[k])
        latent, _ = silu_parts(mm(total.astype(BF16), w_grid[...]))
        latent = latent.astype(BF16)
        senders_out[part_of] = latent
        target = live_only(recv[0, :, part_of], count[0, 0], first)
        pre = mm(latent, w_gs[...]) + mm(
            hits_from(columns(target), 2 * cycle, cycle), table[...]
        )
        value, slope = silu_parts(pre)
        slope_out[part_of] = slope.astype(BF16)
        part = mm(hits_to(target, cycle), value.astype(BF16))
        sums = part if sums is None else sums + part
    part_out[...] = sums
    even = even_on("lat")
    near_out[...] = jnp.where(even, sums[half:], sums[:half]).astype(BF16)
    far_out[...] = jnp.where(even, sums[:half], sums[half:]).astype(BF16)


def node_kernel(part, near, far, mesh_near, mesh_far, mesh_in, w_gn, mesh_out, slope_out):
    node_count = mesh_in.shape[0]
    rim = node_count // 2
    even = even_on("lat")
    left = jnp.where(even, far[...], near[...]).astype(F32)
    right = jnp.where(even, near[...], far[...]).astype(F32)
    total = part[...] + jnp.concatenate([left, right], axis=0)
    mesh_left = jnp.where(even, mesh_far[...], mesh_near[...])[rim:]
    mesh_right = jnp.where(even, mesh_near[...], mesh_far[...])[:rim]
    cycle = jnp.concatenate([mesh_left, mesh_in[...], mesh_right], axis=0)
    value, slope = silu_parts(mm(total.astype(BF16), w_gn[...]))
    mesh_out[...] = (cycle.astype(F32) + value).astype(BF16)
    slope_out[...] = slope


def process_kernel(
    send, recv, count, near, own, far, d_out, w_ms, w_mr, w_mn,
    mesh_out, sums_out, recv_out, near_out, far_out,
):
    cycle = own.shape[0]
    node_count = cycle // 2
    rim = node_count // 2
    even_band = even_on("band")
    raw = send[0]
    flipped = jnp.where(
        raw < cycle, raw + 2 * cycle, jnp.where(raw < 2 * cycle, raw, raw - 2 * cycle)
    )
    source = jnp.where(even_band, flipped, raw)
    target = live_only(recv[0], count[0, 0])
    home = own[rim : rim + node_count]
    block = jnp.concatenate([near[...], own[...], far[...]], axis=0)
    table = jnp.concatenate(
        [*halves(mm(block, w_ms[...])), *halves(mm(home, w_mr[...]))], axis=0
    )
    from_hits = hits_from(columns(source), 6 * cycle, 3 * cycle)
    to_hits = hits_from(columns(target), 2 * node_count, node_count)
    pre = mm(from_hits, table[: 6 * cycle]) + mm(to_hits, table[6 * cycle :])
    value, slope = silu_parts(pre)
    to_rows = hits_to(target, node_count)
    gate = mm(mm(to_rows, value.astype(BF16)).astype(BF16), w_mn[...])
    gate_value, gate_slope = silu_parts(gate)
    mesh_out[...] = (home.astype(F32) + gate_value).astype(BF16)
    gate_two = (d_out[...].astype(F32) * gate_slope).astype(BF16)
    back = jnp.concatenate(halves(mm_nt(gate_two, w_mn[...])), axis=0)
    edge_slope = (mm(to_hits, back) * slope).astype(BF16)
    sums = mm(hits_to(source, 3 * cycle), edge_slope)
    recv_out[...] = mm(to_rows, edge_slope).astype(BF16)
    sums_out[...] = sums
    near_out[...] = sums[:cycle].astype(BF16)
    far_out[...] = sums[2 * cycle :].astype(BF16)


def store_tiles(out, gradient):
    tiles, rows, cols = out.shape
    across = gradient.shape[1] // cols
    for i in range(tiles):
        r, c = (i // across) * rows, (i % across) * cols
        out[i] = gradient[r : r + rows, c : c + cols].astype(out.dtype)


def process_grad_kernel(near, own, far, sums, recv_sum, d_out, w_mr, tiles_out, home_out):
    block = jnp.concatenate([near[...], own[...], far[...]], axis=0)
    store_tiles(tiles_out, mm_tn(block, sums[...].astype(BF16)))
    home_out[...] = mm_nt(recv_sum[...], w_mr[...]) + d_out[...].astype(F32)


def cotangent_kernel(sums, near, far, home, w_ms, part_out, near_out, far_out):
    cycle = near.shape[0]
    half = cycle // 2
    rim = half // 2
    total = sums[cycle : 2 * cycle] + near[...].astype(F32) + far[...].astype(F32)
    back = mm_nt(total.astype(BF16), w_ms[...])
    back = jnp.concatenate(
        [back[:rim], back[rim : rim + half] + home[...], back[rim + half :]], axis=0
    )
    part_out[...] = back
    even = even_on("lat")
    near_out[...] = jnp.where(even, back[half:], back[:half]).astype(BF16)
    far_out[...] = jnp.where(even, back[:half], back[half:]).astype(BF16)


def encode_grad_kernel(
    recv, count, part, near, far, node_slope, w_gn, senders, edge_slope, tiles_out
):
    cycle = part.shape[0]
    even = even_on("lat")
    left = jnp.where(even, far[...], near[...]).astype(F32)
    right = jnp.where(even, near[...], far[...]).astype(F32)
    cot = part[...] + jnp.concatenate([left, right], axis=0)
    gate_one = (cot * node_slope[...]).astype(BF16)
    back = jnp.concatenate(halves(mm_nt(gate_one, w_gn[...])), axis=0)
    target = live_only(recv[0], count[0, 0])
    hits = hits_from(columns(target), 2 * cycle, cycle)
    slope = (mm(hits, back) * edge_slope[...].astype(F32)).astype(BF16)
    store_tiles(tiles_out, mm_tn(senders[...], slope))


def call(kernel, outs, *args, scalars=()):
    in_specs = [
        pl.BlockSpec(memory_space=pltpu.SMEM if i in scalars else pltpu.VMEM)
        for i in range(len(args))
    ]
    return pl.pallas_call(
        kernel,
        out_shape=[jax.ShapeDtypeStruct(shape, dtype) for shape, dtype in outs],
        in_specs=in_specs,
        out_specs=[pl.BlockSpec(memory_space=pltpu.VMEM)] * len(outs),
        compiler_params=pltpu.CompilerParams(vmem_limit_bytes=48 << 20),
    )(*args)


def pairings(count, closed):
    near = [(i, i ^ 1) for i in range(count)]
    far = []
    for i in range(count):
        j = i + 1 if i % 2 else i - 1
        if closed:
            j %= count
        far.append((i, j if 0 <= j < count else i))
    return near, far


def on_device(
    grid_in, w_grid, w_gs, w_gr, w_gn, w_ms, w_mr, w_mn, mesh_in, d_out,
    g2m_send, g2m_recv, g2m_count, mesh_send, mesh_recv, mesh_count,
):
    latent = w_grid.shape[1]
    variables = w_grid.shape[0]
    node_count = mesh_in.shape[0]
    cycle = 2 * node_count
    bands = lax.axis_size("band")
    sectors = lax.axis_size(("dom", "lat"))
    edges = g2m_send.shape[2]
    around = ("dom", "lat")
    band_near, band_far = pairings(bands, False)
    ring_near, ring_far = pairings(sectors, True)

    raw_near = lax.ppermute(grid_in, "band", band_near)
    raw_far = lax.ppermute(grid_in, "band", band_far)
    mesh_near = lax.ppermute(mesh_in, around, ring_near)
    mesh_far = lax.ppermute(mesh_in, around, ring_far)
    own_rows, table = call(
        own_gather_kernel,
        [((edges, variables), BF16), ((2 * cycle, latent), BF16)],
        g2m_send, grid_in, mesh_near, mesh_far, mesh_in, w_gr,
    )
    senders, edge_slope, part, to_near, to_far = call(
        encode_kernel,
        [
            ((edges, latent), BF16),
            ((edges, latent), BF16),
            ((cycle, latent), F32),
            ((node_count, latent), BF16),
            ((node_count, latent), BF16),
        ],
        g2m_send, g2m_recv, g2m_count, raw_near, raw_far, own_rows, table, w_grid, w_gs,
        scalars=(2,),
    )
    from_near = lax.ppermute(to_near, around, ring_near)
    from_far = lax.ppermute(to_far, around, ring_far)
    mesh_one, node_slope = call(
        node_kernel,
        [((cycle, latent), BF16), ((cycle, latent), F32)],
        part, from_near, from_far, mesh_near, mesh_far, mesh_in, w_gn,
    )
    one_near = lax.ppermute(mesh_one, "band", band_near)
    one_far = lax.ppermute(mesh_one, "band", band_far)
    mesh_out, sums, recv_sum, to_near, to_far = call(
        process_kernel,
        [
            ((node_count, latent), BF16),
            ((3 * cycle, latent), F32),
            ((node_count, latent), BF16),
            ((cycle, latent), BF16),
            ((cycle, latent), BF16),
        ],
        mesh_send, mesh_recv, mesh_count, one_near, mesh_one, one_far, d_out, w_ms, w_mr, w_mn,
        scalars=(2,),
    )
    from_near = lax.ppermute(to_near, "band", band_near)
    from_far = lax.ppermute(to_far, "band", band_far)
    tile_shape = (bands * sectors, latent // bands, latent // sectors)
    tiles_ms, home = call(
        process_grad_kernel,
        [(tile_shape, BF16), ((node_count, latent), F32)],
        one_near, mesh_one, one_far, sums, recv_sum, d_out, w_mr,
    )
    part, to_near, to_far = call(
        cotangent_kernel,
        [
            ((cycle, latent), F32),
            ((node_count, latent), BF16),
            ((node_count, latent), BF16),
        ],
        sums, from_near, from_far, home, w_ms,
    )
    from_near = lax.ppermute(to_near, around, ring_near)
    from_far = lax.ppermute(to_far, around, ring_far)
    (tiles_gs,) = call(
        encode_grad_kernel,
        [(tile_shape, BF16)],
        g2m_recv, g2m_count, part, from_near, from_far, node_slope, w_gn, senders, edge_slope,
        scalars=(1,),
    )

    def summed(tiles):
        shares = lax.all_to_all(tiles, ("band", "dom", "lat"), 0, 0, tiled=True)
        return jnp.sum(shares.astype(F32), axis=0)

    return mesh_out, summed(tiles_gs), summed(tiles_ms)


def solution(mesh):
    flat = P(("groups", "band", "dom", "lat"), None)
    grid = P(("groups", "band"), ("dom", "lat"), None)
    count = P(("groups", "band"), ("dom", "lat"))
    placed = (grid,) + (P(),) * 7 + (flat, flat) + (grid, grid, count) * 2
    return jax.shard_map(
        on_device,
        mesh=mesh,
        in_specs=placed,
        out_specs=(flat, count, count),
        check_vma=False,
    )
```

time: 121 us -> 89.9 us (0.74)
  local copies, waits for them, and re-layouts: 30.9 us -> 7.88 us
  matrix products: 14.9 us -> 0 us
  Pallas kernels: 0 us -> 13.2 us
  other arithmetic: 11 us -> 2.45 us
  waiting for transfers between devices: 23.5 us -> 31.7 us
  starting transfers between devices: 37.3 us -> 31.9 us
    gather x7 -> x0, local copies, waits for them, and re-layouts: 21.2 us -> none  [the longest x1 4.86 us: on_device(): jnp.take(matmul(cycle_in, w_gr), grid_to, axis=0)]
    dot_general x16 -> x0, matrix products: 14.9 us -> none  [the longest x2 6.24 us: outer_sum(): lax.dot_general(rows, terms, (((0,), (0,)), ((), ())), preferred_element_...]
    pallas_call x0 -> x7, Pallas kernels: none -> 13.2 us  [call(): pl.pallas_call(kernel, out_shape=[jax.ShapeDtypeStruct(shape, dtype) for...]
    ppermute x16 -> x12, waiting for transfers between devices: 9.71 us -> 18.9 us  [the longest x1 8.96 us: on_device(): from_near = lax.ppermute(to_near, 'band', band_near)]
    ppermute x16 -> x12, starting transfers between devices: 24.5 us -> 16.8 us  [the longest x1 4.29 us: on_device(): one_near = lax.ppermute(mesh_one, 'band', band_near)]
    unnamed x60 -> x39, local copies, waits for them, and re-layouts: 2.06 us -> 7.38 us
    convert_element_type x4 -> x0, local copies, waits for them, and re-layouts: 4.26 us -> none  [summed_tile(): tiles = as_tiles(gradient).astype(jnp.bfloat16)]
    convert_element_type x3 -> x0, other arithmetic: 3.19 us -> none  [the longest x1 1.81 us: on_device(): (jnp.take(back_two, mesh_to, axis=0) * silu_slope(proc_pre) * mesh_live)....]
  transfers between devices with their start and end apart: 18 -> 14, of which waited for: 7 -> 7; matrix products, arithmetic and copies ran while one was open for 28% -> 4% of each run, Pallas kernels for 0% -> 4%
where the time goes in v2:
time: 89.9 us; the launch traced here: 89.3 us
  starting transfers between devices  31.9 us (35%)
  waiting for transfers between devices  31.7 us (35%)
  Pallas kernels  13.2 us (15%)
  local copies, waits for them, and re-layouts  7.88 us (9%)
  other arithmetic  2.45 us (3%)
  between operations  2.18 us (2%)
    all_to_all x2, starting transfers between devices, summed(): shares = lax.all_to_all(tiles, ('band', 'dom', 'lat'), 0, 0, tiled=True)  15.1 us
    pallas_call x7, Pallas kernels, call(): pl.pallas_call(kernel, out_shape=[jax.ShapeDtypeStruct(shape, dtype) for...  13.2 us
    all_to_all x2, waiting for transfers between devices, summed(): shares = lax.all_to_all(tiles, ('band', 'dom', 'lat'), 0, 0, tiled=True)  12.7 us
    ppermute x1, waiting for transfers between devices, on_device(): from_near = lax.ppermute(to_near, 'band', band_near)  8.96 us
    unnamed x39, local copies, waits for them, and re-layouts  7.38 us
    ppermute x1, waiting for transfers between devices, on_device(): raw_near = lax.ppermute(grid_in, 'band', band_near)  4.55 us
    ppermute x1, starting transfers between devices, on_device(): one_near = lax.ppermute(mesh_one, 'band', band_near)  4.29 us
    ppermute x2, waiting for transfers between devices, on_device(): from_far = lax.ppermute(to_far, around, ring_far)  3.81 us
  transfers between devices with their start and end apart: 14, of which 7 were waited for; matrix products, arithmetic and copies ran while one was open for 4% of the time, Pallas kernels for 4%

profile of v2, /device:TPU:0, one launch (start us, length us, event | category | flops | bytes accessed | tf_op | source)
XLA Modules:
  0.0 89.3 jit_solution(13681002714488696339)
XLA Ops:
  0.7 3.1 %collective-permute-start = (bf16[3,360,227]{1,2,0:T(8,128)(2,1)}, bf16[3,360,227]{1,2,0:T(8,128)(2,1)S(1)}, u32[]{:S(2)}, u32[]{:S(2)}) collective-permute-start(bf16[3,360,227]{1,2,0:T(8,128)(2,1)} %param.16), channel_id=1, source_target_pairs={{0,4},{4,0},{8,12},{12,8},{1,5},{5,1},{9,13},{13,9},{2,6},{6,2},{1... | collective-permute-start | bytes 1470968 | tf_op jit(solution)/shard_map/ppermute | solution.py:269
  3.7 1.7 %collective-permute-start.1 = (bf16[3,360,227]{1,2,0:T(8,128)(2,1)}, bf16[3,360,227]{1,2,0:T(8,128)(2,1)S(1)}, u32[]{:S(2)}, u32[]{:S(2)}) collective-permute-start(bf16[3,360,227]{1,2,0:T(8,128)(2,1)} %param.16), channel_id=1, source_target_pairs={{0,0},{4,8},{8,4},{12,12},{1,1},{5,9},{9,5},{13,13},{2,2},{6,10},{... | collective-permute-start | bytes 1470968 | tf_op jit(solution)/shard_map/ppermute | solution.py:270
  5.4 1.6 %collective-permute-start.3 = (bf16[32,512]{1,0:T(8,128)(2,1)}, bf16[32,512]{1,0:T(8,128)(2,1)S(1)}, u32[]{:S(2)}, u32[]{:S(2)}) collective-permute-start(bf16[32,512]{1,0:T(8,128)(2,1)} %mesh_in.3), channel_id=1, source_target_pairs={{0,3},{1,2},{2,1},{3,0},{4,7},{5,6},{6,5},{7,4},{8,11},{9,10},{10,... | collective-permute-start | bytes 98312 | tf_op jit(solution)/shard_map/ppermute | solution.py:272
  7.0 1.3 %copy.22.grid = bf16[3,360,227]{2,1,0:T(8,128)(2,1)S(1)} copy(bf16[3,360,227]{1,2,0:T(8,128)(2,1)} %param.16) | data formatting | bytes 980640 | tf_op args[0]
  9.0 1.1 %shard_map.175 = (bf16[1024,227]{1,0:T(8,128)(2,1)S(1)}, bf16[128,512]{1,0:T(8,128)(2,1)S(1)}) custom-call(s32[1,1,1024]{2,1,0:T(1,128)S(1)} %copy-done.15, bf16[3,360,227]{2,1,0:T(8,128)(2,1)S(1)} %copy.22.grid, bf16[32,512]{1,0:T(8,128)(2,1)S(1)} %collective-permute-done.2.near.mesh_near, bf16[32,512]{1,0:T(8,128)(2,1)S(1)} %collective-permute-done.3.far.mesh_far, ...), custom_call_target="tpu_custom_call" | custom-call | tf_op jit(solution)/shard_map/pallas_call | solution.py:234
  10.1 0.8 copy-done.8
  10.9 0.6 copy-done.12
  11.5 4.5 %collective-permute-done = bf16[3,360,227]{1,2,0:T(8,128)(2,1)S(1)} collective-permute-done((bf16[3,360,227]{1,2,0:T(8,128)(2,1)}, bf16[3,360,227]{1,2,0:T(8,128)(2,1)S(1)}, u32[]{:S(2)}, u32[]{:S(2)}) %collective-permute-start) | collective-permute-done | bytes 490352 | tf_op jit(solution)/shard_map/ppermute | solution.py:269
  16.6 0.7 copy-done.10
  17.3 1.0 %copy-done.6 = bf16[512,512]{1,0:T(8,128)(2,1)S(1)} copy-done((bf16[512,512]{1,0:T(8,128)(2,1)S(1)}, bf16[512,512]{1,0:T(8,128)(2,1)}, u32[]{:S(2)}) %copy-start.6) | copy-done | bytes 524312
  18.3 1.0 %copy-done.9 = bf16[1024,227]{1,0:T(8,128)(2,1)S(1)} copy-done((bf16[1024,227]{1,0:T(8,128)(2,1)S(1)}, bf16[1024,227]{1,0:T(8,128)(2,1)}, u32[]{:S(2)}) %copy-start.9) | copy-done | bytes 464920
  19.4 0.9 %copy-done.13 = bf16[128,512]{1,0:T(8,128)(2,1)S(1)} copy-done((bf16[128,512]{1,0:T(8,128)(2,1)S(1)}, bf16[128,512]{1,0:T(8,128)(2,1)}, u32[]{:S(2)}) %copy-start.13) | copy-done | bytes 131096
  20.3 6.3 %shard_map.176 = (bf16[1024,512]{1,0:T(8,128)(2,1)S(1)}, bf16[1024,512]{1,0:T(8,128)(2,1)S(1)}, f32[64,512]{1,0:T(8,128)S(1)}, bf16[32,512]{1,0:T(8,128)(2,1)S(1)}, bf16[32,512]{1,0:T(8,128)(2,1)S(1)}) custom-call(s32[1,1,1024]{2,1,0:T(1,128)S(1)} %copy-done.15, s32[1,1,1024]{2,1,0:T(1,128)S(1)} %copy-done.16, s32[1,1]{1,0:T(1,128)S(6)} %copy.25.count, ...), custom_call_target="tpu_custom_call" | custom-call | tf_op jit(solution)/shard_map/pallas_call | solution.py:234
  26.6 1.0 %copy-done.3 = bf16[1024,512]{1,0:T(8,128)(2,1)} copy-done((bf16[1024,512]{1,0:T(8,128)(2,1)}, bf16[1024,512]{1,0:T(8,128)(2,1)S(1)}, u32[]{:S(2)}) %copy-start.3) | copy-done | bytes 1048600
  27.6 1.8 %collective-permute-start.5 = (bf16[32,512]{1,0:T(8,128)(2,1)S(1)}, bf16[32,512]{1,0:T(8,128)(2,1)S(1)}, u32[]{:S(2)}, u32[]{:S(2)}) collective-permute-start(bf16[32,512]{1,0:T(8,128)(2,1)S(1)} %get-tuple-element.26), channel_id=1, source_target_pairs={{0,3},{1,2},{2,1},{3,0},{4,7},{5,6},{6,5},{7,4},{8,11},{9,10},{10,... | collective-permute-start | bytes 98312 | tf_op jit(solution)/shard_map/ppermute | solution.py:291
  29.4 1.6 %collective-permute-done.5.far = bf16[32,512]{1,0:T(8,128)(2,1)S(1)} collective-permute-done((bf16[32,512]{1,0:T(8,128)(2,1)S(1)}, bf16[32,512]{1,0:T(8,128)(2,1)S(1)}, u32[]{:S(2)}, u32[]{:S(2)}) %collective-permute-start.5) | collective-permute-done | bytes 32800 | tf_op jit(solution)/shard_map/ppermute | solution.py:291
  31.3 4.3 %collective-permute-start.6 = (bf16[64,512]{1,0:T(8,128)(2,1)S(1)}, bf16[64,512]{1,0:T(8,128)(2,1)S(1)}, u32[]{:S(2)}, u32[]{:S(2)}) collective-permute-start(bf16[64,512]{1,0:T(8,128)(2,1)S(1)} %get-tuple-element.27.own), channel_id=1, source_target_pairs={{0,4},{4,0},{8,12},{12,8},{1,5},{5,1},{9,13},{13,9},{2,6},{6,2},{1... | collective-permute-start | bytes 196616 | tf_op jit(solution)/shard_map/ppermute | solution.py:297
  35.6 0.7 collective-permute-start.7
  36.9 1.5 %collective-permute-done.6.near = bf16[64,512]{1,0:T(8,128)(2,1)S(1)} collective-permute-done((bf16[64,512]{1,0:T(8,128)(2,1)S(1)}, bf16[64,512]{1,0:T(8,128)(2,1)S(1)}, u32[]{:S(2)}, u32[]{:S(2)}) %collective-permute-start.6) | collective-permute-done | bytes 65568 | tf_op jit(solution)/shard_map/ppermute | solution.py:297
  38.4 2.1 %shard_map.178 = (bf16[32,512]{1,0:T(8,128)(2,1)}, f32[192,512]{1,0:T(8,128)S(1)}, bf16[32,512]{1,0:T(8,128)(2,1)S(1)}, bf16[64,512]{1,0:T(8,128)(2,1)S(1)}, bf16[64,512]{1,0:T(8,128)(2,1)S(1)}) custom-call(s32[1,1,512]{2,1,0:T(1,128)S(1)} %copy-done.17, s32[1,1,512]{2,1,0:T(1,128)S(1)} %copy-done.18, s32[1,1]{1,0:T(1,128)S(6)} %copy.26.count, ...), custom_call_target="tpu_custom_call" | custom-call | tf_op jit(solution)/shard_map/pallas_call | solution.py:234
  40.5 1.1 %shard_map.179 = (bf16[16,128,128]{2,1,0:T(8,128)(2,1)}, f32[32,512]{1,0:T(8,128)S(1)}) custom-call(bf16[64,512]{1,0:T(8,128)(2,1)S(1)} %collective-permute-done.6.near, bf16[64,512]{1,0:T(8,128)(2,1)S(1)} %get-tuple-element.27.own, bf16[64,512]{1,0:T(8,128)(2,1)S(1)} %collective-permute-done.7.far, f32[192,512]{1,0:T(8,128)S(1)} %get-tuple-element.29.sums, ...), custom_call_target="tpu_custom_call" | custom-call | tf_op jit(solution)/shard_map/pallas_call | solution.py:234
  41.6 7.2 %all-to-all-start.1 = ((bf16[16,128,128]{2,1,0:T(8,128)(2,1)}), bf16[16,128,128]{2,1,0:T(8,128)(2,1)}, u32[]{:S(2)}, u32[]{:S(2)}) async-start(bf16[16,128,128]{2,1,0:T(8,128)(2,1)} %get-tuple-element.40), calls=%async_computation.1 | async-start | bytes 1048576 | tf_op jit(solution)/shard_map/all_to_all | solution.py:338
  48.8 1.9 %collective-permute-start.8 = (bf16[64,512]{1,0:T(8,128)(2,1)S(1)}, bf16[64,512]{1,0:T(8,128)(2,1)S(1)}, u32[]{:S(2)}, u32[]{:S(2)}) collective-permute-start(bf16[64,512]{1,0:T(8,128)(2,1)S(1)} %get-tuple-element.30), channel_id=1, source_target_pairs={{0,4},{4,0},{8,12},{12,8},{1,5},{5,1},{9,13},{13,9},{2,6},{6,2},{1... | collective-permute-start | bytes 196616 | tf_op jit(solution)/shard_map/ppermute | solution.py:311
  50.7 0.7 collective-permute-start.9
  51.4 9.0 %collective-permute-done.8.near = bf16[64,512]{1,0:T(8,128)(2,1)S(1)} collective-permute-done((bf16[64,512]{1,0:T(8,128)(2,1)S(1)}, bf16[64,512]{1,0:T(8,128)(2,1)S(1)}, u32[]{:S(2)}, u32[]{:S(2)}) %collective-permute-start.8) | collective-permute-done | bytes 65568 | tf_op jit(solution)/shard_map/ppermute | solution.py:311
  60.7 1.0 %collective-permute-start.11 = (bf16[32,512]{1,0:T(8,128)(2,1)S(1)}, bf16[32,512]{1,0:T(8,128)(2,1)S(1)}, u32[]{:S(2)}, u32[]{:S(2)}) collective-permute-start(bf16[32,512]{1,0:T(8,128)(2,1)S(1)} %get-tuple-element.36), channel_id=1, source_target_pairs={{0,3},{1,2},{2,1},{3,0},{4,7},{5,6},{6,5},{7,4},{8,11},{9,10},{10,... | collective-permute-start | bytes 98312 | tf_op jit(solution)/shard_map/ppermute | solution.py:329
  61.9 2.2 %collective-permute-done.11.far = bf16[32,512]{1,0:T(8,128)(2,1)S(1)} collective-permute-done((bf16[32,512]{1,0:T(8,128)(2,1)S(1)}, bf16[32,512]{1,0:T(8,128)(2,1)S(1)}, u32[]{:S(2)}, u32[]{:S(2)}) %collective-permute-start.11) | collective-permute-done | bytes 32800 | tf_op jit(solution)/shard_map/ppermute | solution.py:329
  64.1 2.0 %shard_map.181 = bf16[16,128,128]{2,1,0:T(8,128)(2,1)} custom-call(s32[1,1,1024]{2,1,0:T(1,128)S(1)} %copy-done.16, s32[1,1]{1,0:T(1,128)S(6)} %copy.25.count, f32[64,512]{1,0:T(8,128)S(1)} %get-tuple-element.34.part, bf16[32,512]{1,0:T(8,128)(2,1)S(1)} %collective-permute-done.10.near, bf16[32,512]{1,0:T(8,128)(2,1)S(1)} %collective-permute-done.11.far, ...), custom_call_target="tpu_custom_call" | custom-call | tf_op jit(solution)/shard_map/pallas_call | solution.py:234
  66.1 8.0 %all-to-all-start = ((bf16[16,128,128]{2,1,0:T(8,128)(2,1)}), bf16[16,128,128]{2,1,0:T(8,128)(2,1)S(1)}, u32[]{:S(2)}, u32[]{:S(2)}) async-start(bf16[16,128,128]{2,1,0:T(8,128)(2,1)} %shard_map.181), calls=%async_computation | async-start | bytes 1048576 | tf_op jit(solution)/shard_map/all_to_all | solution.py:338
  74.1 1.8 %convert_reduce_fusion = f32[128,128]{1,0:T(8,128)} fusion(bf16[16,128,128]{2,1,0:T(8,128)(2,1)} %all-to-all-done.1), kind=kLoop, calls=%fused_computation | loop fusion | flops 507904 | bytes 589824 | tf_op jit(solution)/shard_map/reduce_sum | solution.py:339
  75.9 12.7 %all-to-all-done = bf16[16,128,128]{2,1,0:T(8,128)(2,1)S(1)} async-done(((bf16[16,128,128]{2,1,0:T(8,128)(2,1)}), bf16[16,128,128]{2,1,0:T(8,128)(2,1)S(1)}, u32[]{:S(2)}, u32[]{:S(2)}) %all-to-all-start) | async-done | bytes 524320 | tf_op jit(solution)/shard_map/all_to_all | solution.py:338
  88.6 0.7 convert_reduce_fusion.1
  (46 shorter events, 1.3 us)
Async XLA Ops:
  0.6 8.4 %copy-start.14 = (bf16[32,512]{1,0:T(8,128)(2,1)S(1)}, bf16[32,512]{1,0:T(8,128)(2,1)}, u32[]{:S(2)}) copy-start(bf16[32,512]{1,0:T(8,128)(2,1)} %mesh_in.3) | copy-start | bytes 98308
  0.6 8.4 %copy-start.5 = (bf16[512,512]{1,0:T(8,128)(2,1)S(1)}, bf16[512,512]{1,0:T(8,128)(2,1)}, u32[]{:S(2)}) copy-start(bf16[512,512]{1,0:T(8,128)(2,1)} %w_gr.1) | copy-start | bytes 1572868
  0.7 15.4 %collective-permute-start = (bf16[3,360,227]{1,2,0:T(8,128)(2,1)}, bf16[3,360,227]{1,2,0:T(8,128)(2,1)S(1)}, u32[]{:S(2)}, u32[]{:S(2)}) collective-permute-start(bf16[3,360,227]{1,2,0:T(8,128)(2,1)} %param.16), channel_id=1, source_target_pairs={{0,4},{4,0},{8,12},{12,8},{1,5},{5,1},{9,13},{13,9},{2,6},{6,2},{1... | collective-permute-start | bytes 1470968 | tf_op jit(solution)/shard_map/ppermute | solution.py:269
  3.7 12.6 %collective-permute-start.1 = (bf16[3,360,227]{1,2,0:T(8,128)(2,1)}, bf16[3,360,227]{1,2,0:T(8,128)(2,1)S(1)}, u32[]{:S(2)}, u32[]{:S(2)}) collective-permute-start(bf16[3,360,227]{1,2,0:T(8,128)(2,1)} %param.16), channel_id=1, source_target_pairs={{0,0},{4,8},{8,4},{12,12},{1,1},{5,9},{9,5},{13,13},{2,2},{6,10},{... | collective-permute-start | bytes 1470968 | tf_op jit(solution)/shard_map/ppermute | solution.py:270
  5.4 3.6 %collective-permute-start.2 = (bf16[32,512]{1,0:T(8,128)(2,1)}, bf16[32,512]{1,0:T(8,128)(2,1)S(1)}, u32[]{:S(2)}, u32[]{:S(2)}) collective-permute-start(bf16[32,512]{1,0:T(8,128)(2,1)} %mesh_in.3), channel_id=1, source_target_pairs={{0,1},{1,0},{2,3},{3,2},{4,5},{5,4},{6,7},{7,6},{8,9},{9,8},{10,11... | collective-permute-start | bytes 98312 | tf_op jit(solution)/shard_map/ppermute | solution.py:271
  5.4 3.6 %collective-permute-start.3 = (bf16[32,512]{1,0:T(8,128)(2,1)}, bf16[32,512]{1,0:T(8,128)(2,1)S(1)}, u32[]{:S(2)}, u32[]{:S(2)}) collective-permute-start(bf16[32,512]{1,0:T(8,128)(2,1)} %mesh_in.3), channel_id=1, source_target_pairs={{0,3},{1,2},{2,1},{3,0},{4,7},{5,6},{6,5},{7,4},{8,11},{9,10},{10,... | collective-permute-start | bytes 98312 | tf_op jit(solution)/shard_map/ppermute | solution.py:272
  7.0 2.0 %copy-start.15 = (s32[1,1,1024]{2,1,0:T(1,128)S(1)}, s32[1,1,1024]{2,1,0:T(1,128)}, u32[]{:S(2)}) copy-start(s32[1,1,1024]{2,1,0:T(1,128)} %send.4) | copy-start | bytes 12292
  10.1 0.8 copy-start.8
  16.3 0.9 %copy-start.10 = (bf16[227,512]{1,0:T(8,128)(2,1)S(1)}, bf16[227,512]{1,0:T(8,128)(2,1)}, u32[]{:S(2)}) copy-start(bf16[227,512]{1,0:T(8,128)(2,1)} %w_grid.1) | copy-start | bytes 697348
  16.4 0.9 %copy-start.16 = (s32[1,1,1024]{2,1,0:T(1,128)S(1)}, s32[1,1,1024]{2,1,0:T(1,128)}, u32[]{:S(2)}) copy-start(s32[1,1,1024]{2,1,0:T(1,128)} %recv.5) | copy-start | bytes 12292
  17.3 1.0 %copy-start.6 = (bf16[512,512]{1,0:T(8,128)(2,1)S(1)}, bf16[512,512]{1,0:T(8,128)(2,1)}, u32[]{:S(2)}) copy-start(bf16[512,512]{1,0:T(8,128)(2,1)} %w_gs.1) | copy-start | bytes 1572868
  18.3 1.0 %copy-start.9 = (bf16[1024,227]{1,0:T(8,128)(2,1)S(1)}, bf16[1024,227]{1,0:T(8,128)(2,1)}, u32[]{:S(2)}) copy-start(bf16[1024,227]{1,0:T(8,128)(2,1)} %copy-done.8) | copy-start | bytes 1394692
  19.4 0.9 %copy-start.13 = (bf16[128,512]{1,0:T(8,128)(2,1)S(1)}, bf16[128,512]{1,0:T(8,128)(2,1)}, u32[]{:S(2)}) copy-start(bf16[128,512]{1,0:T(8,128)(2,1)} %copy-done.12) | copy-start | bytes 393220
  20.3 10.7 %copy-start.2 = (bf16[512,512]{1,0:T(8,128)(2,1)S(1)}, bf16[512,512]{1,0:T(8,128)(2,1)}, u32[]{:S(2)}) copy-start(bf16[512,512]{1,0:T(8,128)(2,1)} %w_gn.3) | copy-start | bytes 1572868
  20.3 18.0 %copy-start.1 = (bf16[512,512]{1,0:T(8,128)(2,1)S(1)}, bf16[512,512]{1,0:T(8,128)(2,1)}, u32[]{:S(2)}) copy-start(bf16[512,512]{1,0:T(8,128)(2,1)} %w_ms.3) | copy-start | bytes 1572868
  20.3 18.0 %copy-start.7 = (bf16[512,512]{1,0:T(8,128)(2,1)S(1)}, bf16[512,512]{1,0:T(8,128)(2,1)}, u32[]{:S(2)}) copy-start(bf16[512,512]{1,0:T(8,128)(2,1)} %w_mn.1) | copy-start | bytes 1572868
  26.6 1.0 %copy-start.3 = (bf16[1024,512]{1,0:T(8,128)(2,1)}, bf16[1024,512]{1,0:T(8,128)(2,1)S(1)}, u32[]{:S(2)}) copy-start(bf16[1024,512]{1,0:T(8,128)(2,1)S(1)} %get-tuple-element.39.edge_slope) | copy-start | bytes 3145732
  27.6 10.7 %copy-start = (bf16[512,512]{1,0:T(8,128)(2,1)S(1)}, bf16[512,512]{1,0:T(8,128)(2,1)}, u32[]{:S(2)}) copy-start(bf16[512,512]{1,0:T(8,128)(2,1)} %w_mr.3) | copy-start | bytes 1572868
  27.6 1.8 %collective-permute-start.4 = (bf16[32,512]{1,0:T(8,128)(2,1)S(1)}, bf16[32,512]{1,0:T(8,128)(2,1)S(1)}, u32[]{:S(2)}, u32[]{:S(2)}) collective-permute-start(bf16[32,512]{1,0:T(8,128)(2,1)S(1)} %get-tuple-element.25), channel_id=1, source_target_pairs={{0,1},{1,0},{2,3},{3,2},{4,5},{5,4},{6,7},{7,6},{8,9},{9,8},{10,11... | collective-permute-start | bytes 98312 | tf_op jit(solution)/shard_map/ppermute | solution.py:290
  27.6 3.4 %collective-permute-start.5 = (bf16[32,512]{1,0:T(8,128)(2,1)S(1)}, bf16[32,512]{1,0:T(8,128)(2,1)S(1)}, u32[]{:S(2)}, u32[]{:S(2)}) collective-permute-start(bf16[32,512]{1,0:T(8,128)(2,1)S(1)} %get-tuple-element.26), channel_id=1, source_target_pairs={{0,3},{1,2},{2,1},{3,0},{4,7},{5,6},{6,5},{7,4},{8,11},{9,10},{10,... | collective-permute-start | bytes 98312 | tf_op jit(solution)/shard_map/ppermute | solution.py:291
  31.0 7.4 %copy-start.11 = (bf16[32,512]{1,0:T(8,128)(2,1)S(1)}, bf16[32,512]{1,0:T(8,128)(2,1)}, u32[]{:S(2)}) copy-start(bf16[32,512]{1,0:T(8,128)(2,1)} %d_out.3) | copy-start | bytes 98308
  31.0 7.4 %copy-start.18 = (s32[1,1,512]{2,1,0:T(1,128)S(1)}, s32[1,1,512]{2,1,0:T(1,128)}, u32[]{:S(2)}) copy-start(s32[1,1,512]{2,1,0:T(1,128)} %recv.4) | copy-start | bytes 6148
  31.3 7.1 %copy-start.17 = (s32[1,1,512]{2,1,0:T(1,128)S(1)}, s32[1,1,512]{2,1,0:T(1,128)}, u32[]{:S(2)}) copy-start(s32[1,1,512]{2,1,0:T(1,128)} %send.5) | copy-start | bytes 6148
  31.3 7.1 %collective-permute-start.6 = (bf16[64,512]{1,0:T(8,128)(2,1)S(1)}, bf16[64,512]{1,0:T(8,128)(2,1)S(1)}, u32[]{:S(2)}, u32[]{:S(2)}) collective-permute-start(bf16[64,512]{1,0:T(8,128)(2,1)S(1)} %get-tuple-element.27.own), channel_id=1, source_target_pairs={{0,4},{4,0},{8,12},{12,8},{1,5},{5,1},{9,13},{13,9},{2,6},{6,2},{1... | collective-permute-start | bytes 196616 | tf_op jit(solution)/shard_map/ppermute | solution.py:297
  35.6 2.8 %collective-permute-start.7 = (bf16[64,512]{1,0:T(8,128)(2,1)S(1)}, bf16[64,512]{1,0:T(8,128)(2,1)S(1)}, u32[]{:S(2)}, u32[]{:S(2)}) collective-permute-start(bf16[64,512]{1,0:T(8,128)(2,1)S(1)} %get-tuple-element.27.own), channel_id=1, source_target_pairs={{0,0},{4,8},{8,4},{12,12},{1,1},{5,9},{9,5},{13,13},{2,2},{6,10},{... | collective-permute-start | bytes 196616 | tf_op jit(solution)/shard_map/ppermute | solution.py:298
  41.6 24.6 %all-to-all-start.1 = ((bf16[16,128,128]{2,1,0:T(8,128)(2,1)}), bf16[16,128,128]{2,1,0:T(8,128)(2,1)}, u32[]{:S(2)}, u32[]{:S(2)}) async-start(bf16[16,128,128]{2,1,0:T(8,128)(2,1)} %get-tuple-element.40), calls=%async_computation.1 | async-start | bytes 1048576 | tf_op jit(solution)/shard_map/all_to_all | solution.py:338
  48.8 15.3 %copy-start.4 = (bf16[1024,512]{1,0:T(8,128)(2,1)S(1)}, bf16[1024,512]{1,0:T(8,128)(2,1)}, u32[]{:S(2)}) copy-start(bf16[1024,512]{1,0:T(8,128)(2,1)} %copy-done.3) | copy-start | bytes 3145732
  48.8 11.6 %collective-permute-start.8 = (bf16[64,512]{1,0:T(8,128)(2,1)S(1)}, bf16[64,512]{1,0:T(8,128)(2,1)S(1)}, u32[]{:S(2)}, u32[]{:S(2)}) collective-permute-start(bf16[64,512]{1,0:T(8,128)(2,1)S(1)} %get-tuple-element.30), channel_id=1, source_target_pairs={{0,4},{4,0},{8,12},{12,8},{1,5},{5,1},{9,13},{13,9},{2,6},{6,2},{1... | collective-permute-start | bytes 196616 | tf_op jit(solution)/shard_map/ppermute | solution.py:311
  50.7 9.6 %collective-permute-start.9 = (bf16[64,512]{1,0:T(8,128)(2,1)S(1)}, bf16[64,512]{1,0:T(8,128)(2,1)S(1)}, u32[]{:S(2)}, u32[]{:S(2)}) collective-permute-start(bf16[64,512]{1,0:T(8,128)(2,1)S(1)} %get-tuple-element.31), channel_id=1, source_target_pairs={{0,0},{4,8},{8,4},{12,12},{1,1},{5,9},{9,5},{13,13},{2,2},{6,10},{... | collective-permute-start | bytes 196616 | tf_op jit(solution)/shard_map/ppermute | solution.py:312
  60.6 1.3 %collective-permute-start.10 = (bf16[32,512]{1,0:T(8,128)(2,1)S(1)}, bf16[32,512]{1,0:T(8,128)(2,1)S(1)}, u32[]{:S(2)}, u32[]{:S(2)}) collective-permute-start(bf16[32,512]{1,0:T(8,128)(2,1)S(1)} %get-tuple-element.35), channel_id=1, source_target_pairs={{0,1},{1,0},{2,3},{3,2},{4,5},{5,4},{6,7},{7,6},{8,9},{9,8},{10,11... | collective-permute-start | bytes 98312 | tf_op jit(solution)/shard_map/ppermute | solution.py:328
  60.7 3.4 %collective-permute-start.11 = (bf16[32,512]{1,0:T(8,128)(2,1)S(1)}, bf16[32,512]{1,0:T(8,128)(2,1)S(1)}, u32[]{:S(2)}, u32[]{:S(2)}) collective-permute-start(bf16[32,512]{1,0:T(8,128)(2,1)S(1)} %get-tuple-element.36), channel_id=1, source_target_pairs={{0,3},{1,2},{2,1},{3,0},{4,7},{5,6},{6,5},{7,4},{8,11},{9,10},{10,... | collective-permute-start | bytes 98312 | tf_op jit(solution)/shard_map/ppermute | solution.py:329
  66.1 22.4 %all-to-all-start = ((bf16[16,128,128]{2,1,0:T(8,128)(2,1)}), bf16[16,128,128]{2,1,0:T(8,128)(2,1)S(1)}, u32[]{:S(2)}, u32[]{:S(2)}) async-start(bf16[16,128,128]{2,1,0:T(8,128)(2,1)} %shard_map.181), calls=%async_computation | async-start | bytes 1048576 | tf_op jit(solution)/shard_map/all_to_all | solution.py:338
  (1 other events, 0.6 us)

commit v3 on v2

--- a/solution.py
+++ b/solution.py
@@ -1,5 +1,3 @@
-import functools
-
 import jax
 import jax.numpy as jnp
 from jax import lax
@@ -30,8 +28,9 @@
 
 
 def silu_parts(x):
-    g = 1.0 / (1.0 + jnp.exp(-x))
-    return x * g, g * (1.0 + x * (1.0 - g))
+    g = 0.5 * jnp.tanh(0.5 * x) + 0.5
+    value = x * g
+    return value, g + value * (1.0 - g)
 
 
 def ones_at(mask):
@@ -71,8 +70,29 @@
     return lax.rem(lax.axis_index(axis), 2) == 0
 
 
-def own_gather_kernel(send, grid, near, far, mesh_in, w_gr, rows_out, table_out):
-    band_rows, cols, _ = grid.shape
+def spread(index, cols, pitch):
+    extra = jnp.zeros_like(index)
+    block = 1
+    while block * cols < 9 * cols:
+        extra = extra + jnp.where(index >= block * cols, pitch - cols, 0)
+        block += 1
+    return index + extra
+
+
+def fill(wide, blocks, pitch, first):
+    for k in range(blocks.shape[0]):
+        at = first + k * pitch
+        cols = blocks.shape[2]
+        wide[:, at : at + cols] = blocks[k]
+        if cols < pitch:
+            wide[:, at + cols : at + pitch] = jnp.zeros(
+                (wide.shape[0], pitch - cols), wide.dtype
+            )
+
+
+def own_gather_kernel(send, grid, near, far, mesh_in, w_gr, rows_out, table_out, wide):
+    band_rows, _, cols = grid.shape
+    pitch = wide.shape[1] // band_rows
     node_count = mesh_in.shape[0]
     rim = node_count // 2
     even = even_on("lat")
@@ -82,37 +102,40 @@
     high, low = halves(mm(cycle, w_gr[...]))
     table_out[: 2 * node_count] = high
     table_out[2 * node_count :] = low
+    fill(wide, grid, pitch, 0)
     block = 256
+    width = band_rows * pitch
     for first in range(0, send.shape[2], block):
-        index = columns(send[0, :, first : first + block])
-        total = None
-        for k in range(band_rows):
-            hit = hits_from(index, cols, cols, (band_rows + k) * cols)
-            part = mm(hit, grid[k])
-            total = part if total is None else total + part
-        rows_out[first : first + block] = total.astype(BF16)
+        lane = spread(send[0, :, first : first + block], cols, pitch)
+        hit = hits_from(columns(lane), width, width, width)
+        rows_out[first : first + block] = mm_nt(hit, wide[...]).astype(BF16)
 
 
 def encode_kernel(
     send, recv, count, near, far, own, table, w_grid, w_gs,
-    senders_out, slope_out, part_out, near_out, far_out,
+    senders_out, slope_out, part_out, near_out, far_out, wide,
 ):
-    band_rows, cols, _ = near.shape
+    band_rows, _, cols = near.shape
+    pitch = wide.shape[1] // (2 * band_rows)
     cycle = table.shape[0] // 2
     half = cycle // 2
+    width = band_rows * pitch
+    fill(wide, near, pitch, 0)
+    fill(wide, far, pitch, width)
     even_band = even_on("band")
-    near_base = jnp.where(even_band, 2 * band_rows * cols, 0)
-    far_base = jnp.where(even_band, 0, 2 * band_rows * cols)
+    below = jnp.where(even_band, width, 0)
+    above = jnp.where(even_band, -2 * width, -width)
     block = 256
     sums = None
     for first in range(0, send.shape[2], block):
         part_of = slice(first, first + block)
-        index = columns(send[0, :, part_of])
-        total = own[part_of].astype(F32)
-        for base, halo in ((near_base, near), (far_base, far)):
-            for k in range(band_rows):
-                total = total + mm(hits_from(index, cols, cols, base + k * cols), halo[k])
-        latent, _ = silu_parts(mm(total.astype(BF16), w_grid[...]))
+        lane = spread(send[0, :, part_of], cols, pitch)
+        lane = jnp.where(
+            lane < width, lane + below, jnp.where(lane < 2 * width, -1, lane + above)
+        )
+        hit = hits_from(columns(lane), 2 * width, 2 * width)
+        raw = own[part_of] + mm_nt(hit, wide[...]).astype(BF16)
+        latent, _ = silu_parts(mm(raw, w_grid[...]))
         latent = latent.astype(BF16)
         senders_out[part_of] = latent
         target = live_only(recv[0, :, part_of], count[0, 0], first)
@@ -181,26 +204,41 @@
     far_out[...] = sums[2 * cycle :].astype(BF16)
 
 
-def store_tiles(out, gradient):
-    tiles, rows, cols = out.shape
-    across = gradient.shape[1] // cols
-    for i in range(tiles):
-        r, c = (i // across) * rows, (i % across) * cols
-        out[i] = gradient[r : r + rows, c : c + cols].astype(out.dtype)
-
-
-def process_grad_kernel(near, own, far, sums, recv_sum, d_out, w_mr, tiles_out, home_out):
-    block = jnp.concatenate([near[...], own[...], far[...]], axis=0)
-    store_tiles(tiles_out, mm_tn(block, sums[...].astype(BF16)))
+def split_store(gradient, keep, sends):
+    doms, _, cols = keep.shape
+    lats = sends.shape[0] // doms + 1
+    me = lax.axis_index("lat")
+    for dom in range(doms):
+        block = [
+            gradient[:, (dom * lats + i) * cols : (dom * lats + i + 1) * cols]
+            for i in range(lats)
+        ]
+        for shift in range(lats):
+            pick = block[shift]
+            for i in range(1, lats):
+                pick = jnp.where(me == i, block[(shift + i) % lats], pick)
+            if shift == 0:
+                keep[dom] = pick
+            else:
+                sends[(shift - 1) * doms + dom] = pick.astype(BF16)
+
+
+def home_kernel(recv_sum, d_out, w_mr, home_out):
     home_out[...] = mm_nt(recv_sum[...], w_mr[...]) + d_out[...].astype(F32)
 
 
-def cotangent_kernel(sums, near, far, home, w_ms, part_out, near_out, far_out):
+def process_grad_kernel(own, total, keep, sends):
+    split_store(mm_tn(own[...], total[...]), keep, sends)
+
+
+def cotangent_kernel(sums, near, far, home, w_ms, total_out, part_out, near_out, far_out):
     cycle = near.shape[0]
     half = cycle // 2
     rim = half // 2
     total = sums[cycle : 2 * cycle] + near[...].astype(F32) + far[...].astype(F32)
-    back = mm_nt(total.astype(BF16), w_ms[...])
+    total = total.astype(BF16)
+    total_out[...] = total
+    back = mm_nt(total, w_ms[...])
     back = jnp.concatenate(
         [back[:rim], back[rim : rim + half] + home[...], back[rim + half :]], axis=0
     )
@@ -211,7 +249,7 @@
 
 
 def encode_grad_kernel(
-    recv, count, part, near, far, node_slope, w_gn, senders, edge_slope, tiles_out
+    recv, count, part, near, far, node_slope, w_gn, senders, edge_slope, keep, sends
 ):
     cycle = part.shape[0]
     even = even_on("lat")
@@ -223,10 +261,46 @@
     target = live_only(recv[0], count[0, 0])
     hits = hits_from(columns(target), 2 * cycle, cycle)
     slope = (mm(hits, back) * edge_slope[...].astype(F32)).astype(BF16)
-    store_tiles(tiles_out, mm_tn(senders[...], slope))
-
-
-def call(kernel, outs, *args, scalars=()):
+    split_store(mm_tn(senders[...], slope), keep, sends)
+
+
+def over_lat_kernel(*refs):
+    keep, *came, keep_out, sends_out = refs
+    doms = keep.shape[0]
+    me = lax.axis_index("dom")
+    for shift in range(doms):
+        at = lax.rem(me + shift, doms)
+        total = keep[at]
+        for part in came:
+            total = total + part[at].astype(F32)
+        if shift == 0:
+            keep_out[...] = total
+        else:
+            sends_out[shift - 1] = total.astype(BF16)
+
+
+def over_dom_kernel(*refs):
+    *ins, out = refs
+    half = len(ins) // 2
+    bands, _, rows, _ = out.shape
+    for k in range(2):
+        keep, *came = ins[k * half : (k + 1) * half]
+        total = keep[...]
+        for part in came:
+            total = total + part[...].astype(F32)
+        for band in range(bands):
+            out[band, k] = total[band * rows : (band + 1) * rows].astype(BF16)
+
+
+def over_band_kernel(shares, first_out, second_out):
+    for k, out in enumerate((first_out, second_out)):
+        total = shares[0, k].astype(F32)
+        for band in range(1, shares.shape[0]):
+            total = total + shares[band, k].astype(F32)
+        out[...] = total
+
+
+def call(kernel, outs, *args, scalars=(), scratch=()):
     in_specs = [
         pl.BlockSpec(memory_space=pltpu.SMEM if i in scalars else pltpu.VMEM)
         for i in range(len(args))
@@ -236,7 +310,8 @@
         out_shape=[jax.ShapeDtypeStruct(shape, dtype) for shape, dtype in outs],
         in_specs=in_specs,
         out_specs=[pl.BlockSpec(memory_space=pltpu.VMEM)] * len(outs),
-        compiler_params=pltpu.CompilerParams(vmem_limit_bytes=48 << 20),
+        scratch_shapes=[pltpu.VMEM(shape, dtype) for shape, dtype in scratch],
+        compiler_params=pltpu.CompilerParams(vmem_limit_bytes=16 << 20),
     )(*args)
 
 
@@ -249,6 +324,11 @@
             j %= count
         far.append((i, j if 0 <= j < count else i))
     return near, far
+
+
+def shifted(x, axis, shift):
+    count = lax.axis_size(axis)
+    return lax.ppermute(x, axis, [(i, (i + shift) % count) for i in range(count)])
 
 
 def on_device(
@@ -266,14 +346,18 @@
     band_near, band_far = pairings(bands, False)
     ring_near, ring_far = pairings(sectors, True)
 
-    raw_near = lax.ppermute(grid_in, "band", band_near)
-    raw_far = lax.ppermute(grid_in, "band", band_far)
+    grid = jnp.transpose(grid_in, (0, 2, 1))
+    pitch = -(-grid.shape[2] // LANES) * LANES
+    wide = (variables, grid.shape[0] * pitch)
+    raw_near = lax.ppermute(grid, "band", band_near)
+    raw_far = lax.ppermute(grid, "band", band_far)
     mesh_near = lax.ppermute(mesh_in, around, ring_near)
     mesh_far = lax.ppermute(mesh_in, around, ring_far)
     own_rows, table = call(
         own_gather_kernel,
         [((edges, variables), BF16), ((2 * cycle, latent), BF16)],
-        g2m_send, grid_in, mesh_near, mesh_far, mesh_in, w_gr,
+        g2m_send, grid, mesh_near, mesh_far, mesh_in, w_gr,
+        scratch=[(wide, BF16)],
     )
     senders, edge_slope, part, to_near, to_far = call(
         encode_kernel,
@@ -286,6 +370,7 @@
         ],
         g2m_send, g2m_recv, g2m_count, raw_near, raw_far, own_rows, table, w_grid, w_gs,
         scalars=(2,),
+        scratch=[((variables, 2 * wide[1]), BF16)],
     )
     from_near = lax.ppermute(to_near, around, ring_near)
     from_far = lax.ppermute(to_far, around, ring_far)
@@ -310,15 +395,11 @@
     )
     from_near = lax.ppermute(to_near, "band", band_near)
     from_far = lax.ppermute(to_far, "band", band_far)
-    tile_shape = (bands * sectors, latent // bands, latent // sectors)
-    tiles_ms, home = call(
-        process_grad_kernel,
-        [(tile_shape, BF16), ((node_count, latent), F32)],
-        one_near, mesh_one, one_far, sums, recv_sum, d_out, w_mr,
-    )
-    part, to_near, to_far = call(
+    (home,) = call(home_kernel, [((node_count, latent), F32)], recv_sum, d_out, w_mr)
+    total, part, to_near, to_far = call(
         cotangent_kernel,
         [
+            ((cycle, latent), BF16),
             ((cycle, latent), F32),
             ((node_count, latent), BF16),
             ((node_count, latent), BF16),
@@ -327,18 +408,45 @@
     )
     from_near = lax.ppermute(to_near, around, ring_near)
     from_far = lax.ppermute(to_far, around, ring_far)
-    (tiles_gs,) = call(
-        encode_grad_kernel,
-        [(tile_shape, BF16)],
-        g2m_recv, g2m_count, part, from_near, from_far, node_slope, w_gn, senders, edge_slope,
-        scalars=(1,),
-    )
-
-    def summed(tiles):
-        shares = lax.all_to_all(tiles, ("band", "dom", "lat"), 0, 0, tiled=True)
-        return jnp.sum(shares.astype(F32), axis=0)
-
-    return mesh_out, summed(tiles_gs), summed(tiles_ms)
+
+    doms = lax.axis_size("dom")
+    lats = lax.axis_size("lat")
+    cols = latent // sectors
+    halves_shape = [
+        ((doms, latent, cols), F32),
+        (((lats - 1) * doms, latent, cols), BF16),
+    ]
+
+    def over_lat(keep, sends):
+        came = [
+            shifted(sends[i * doms : (i + 1) * doms], "lat", i + 1) for i in range(lats - 1)
+        ]
+        keep, sends = call(
+            over_lat_kernel,
+            [((latent, cols), F32), ((doms - 1, latent, cols), BF16)],
+            keep, *came,
+        )
+        return [keep] + [shifted(sends[i], "dom", i + 1) for i in range(doms - 1)]
+
+    ms_parts = over_lat(*call(process_grad_kernel, halves_shape, mesh_one, total))
+    gs_parts = over_lat(
+        *call(
+            encode_grad_kernel,
+            halves_shape,
+            g2m_recv, g2m_count, part, from_near, from_far, node_slope, w_gn, senders,
+            edge_slope,
+            scalars=(1,),
+        )
+    )
+    (shares,) = call(
+        over_dom_kernel,
+        [((bands, 2, latent // bands, cols), BF16)],
+        *gs_parts, *ms_parts,
+    )
+    shares = lax.all_to_all(shares, "band", 0, 0, tiled=True)
+    tile = ((latent // bands, cols), F32)
+    grad_gs, grad_ms = call(over_band_kernel, [tile, tile], shares)
+    return mesh_out, grad_gs, grad_ms
 
 
 def solution(mesh):

time: 89.9 us -> 70.5 us (0.78)
  waiting for transfers between devices: 31.7 us -> 15.2 us
  blocking collectives: 0 us -> 14.4 us
  starting transfers between devices: 31.9 us -> 23.1 us
  local copies, waits for them, and re-layouts: 7.88 us -> 3.59 us
  other arithmetic: 2.45 us -> 0 us
  Pallas kernels: 13.2 us -> 11.7 us
    all_to_all x2 -> x0, starting transfers between devices: 15.1 us -> none  [summed(): shares = lax.all_to_all(tiles, ('band', 'dom', 'lat'), 0, 0, tiled=True)]
    all_to_all x0 -> x1, blocking collectives: none -> 14.4 us  [on_device(): shares = lax.all_to_all(shares, 'band', 0, 0, tiled=True)]
    all_to_all x2 -> x0, waiting for transfers between devices: 12.7 us -> none  [summed(): shares = lax.all_to_all(tiles, ('band', 'dom', 'lat'), 0, 0, tiled=True)]
    ppermute x1, waiting for transfers between devices: 8.96 us -> 1.34 us  [on_device(): from_near = lax.ppermute(to_near, 'band', band_near)]
    unnamed x39 -> x30, local copies, waits for them, and re-layouts: 7.38 us -> 3.59 us
    ppermute x2 -> x6, waiting for transfers between devices: 4.55 us -> 8.17 us  [the longest x4 5.61 us: shifted(): lax.ppermute(x, axis, [(i, (i + shift) % count) for i in range(count)])]
    ppermute x2 -> x6, starting transfers between devices: 4.78 us -> 8.1 us  [the longest x4 3.32 us: shifted(): lax.ppermute(x, axis, [(i, (i + shift) % count) for i in range(count)])]
    reduce_sum x2 -> x0, other arithmetic: 2.45 us -> none  [summed(): return jnp.sum(shares.astype(F32), axis=0)]
  transfers between devices with their start and end apart: 14 -> 16, of which waited for: 7 -> 8; matrix products, arithmetic and copies ran while one was open for 4% -> 0% of each run, Pallas kernels for 4% -> 4%
where the time goes in v3:
time: 70.5 us; the launch traced here: 70.1 us
  starting transfers between devices  23.1 us (33%)
  waiting for transfers between devices  15.2 us (22%)
  blocking collectives  14.4 us (20%)
  Pallas kernels  11.7 us (17%)
  local copies, waits for them, and re-layouts  3.59 us (5%)
  between operations  2.15 us (3%)
    all_to_all x1, blocking collectives, on_device(): shares = lax.all_to_all(shares, 'band', 0, 0, tiled=True)  14.4 us
    pallas_call x12, Pallas kernels, call(): pl.pallas_call(kernel, out_shape=[jax.ShapeDtypeStruct(shape, dtype) for...  11.7 us
    ppermute x4, waiting for transfers between devices, shifted(): lax.ppermute(x, axis, [(i, (i + shift) % count) for i in range(count)])  5.61 us
    ppermute x1, starting transfers between devices, on_device(): one_near = lax.ppermute(mesh_one, 'band', band_near)  4.82 us
    ppermute x1, starting transfers between devices, on_device(): from_near = lax.ppermute(to_near, 'band', band_near)  3.7 us
    unnamed x30, local copies, waits for them, and re-layouts  3.59 us
    ppermute x2, starting transfers between devices, on_device(): from_far = lax.ppermute(to_far, around, ring_far)  3.38 us
    ppermute x4, starting transfers between devices, shifted(): lax.ppermute(x, axis, [(i, (i + shift) % count) for i in range(count)])  3.32 us
  transfers between devices with their start and end apart: 16, of which 8 were waited for; matrix products, arithmetic and copies ran while one was open for 0% of the time, Pallas kernels for 4%

profile of v3, /device:TPU:0, one launch (start us, length us, event | category | flops | bytes accessed | tf_op | source)
XLA Modules:
  0.0 70.1 jit_solution(6043370524518132399)
XLA Ops:
  0.6 3.1 %collective-permute-start = (bf16[3,227,360]{2,1,0:T(8,128)(2,1)}, bf16[3,227,360]{2,1,0:T(8,128)(2,1)S(1)}, u32[]{:S(2)}, u32[]{:S(2)}) collective-permute-start(bf16[3,227,360]{2,1,0:T(8,128)(2,1)} %bitcast.3), channel_id=1, source_target_pairs={{0,4},{4,0},{8,12},{12,8},{1,5},{5,1},{9,13},{13,9},{2,6},{6,2},{1... | collective-permute-start | bytes 1470968 | tf_op jit(solution)/shard_map/ppermute | solution.py:352
  3.7 1.7 %collective-permute-start.1 = (bf16[3,227,360]{2,1,0:T(8,128)(2,1)}, bf16[3,227,360]{2,1,0:T(8,128)(2,1)S(1)}, u32[]{:S(2)}, u32[]{:S(2)}) collective-permute-start(bf16[3,227,360]{2,1,0:T(8,128)(2,1)} %bitcast.4), channel_id=1, source_target_pairs={{0,0},{4,8},{8,4},{12,12},{1,1},{5,9},{9,5},{13,13},{2,2},{6,10},{... | collective-permute-start | bytes 1470968 | tf_op jit(solution)/shard_map/ppermute | solution.py:353
  5.4 1.6 %collective-permute-start.3 = (bf16[32,512]{1,0:T(8,128)(2,1)}, bf16[32,512]{1,0:T(8,128)(2,1)S(1)}, u32[]{:S(2)}, u32[]{:S(2)}) collective-permute-start(bf16[32,512]{1,0:T(8,128)(2,1)} %mesh_in.3), channel_id=1, source_target_pairs={{0,3},{1,2},{2,1},{3,0},{4,7},{5,6},{6,5},{7,4},{8,11},{9,10},{10,... | collective-permute-start | bytes 98312 | tf_op jit(solution)/shard_map/ppermute | solution.py:355
  7.7 1.3 %collective-permute-done.3.far.mesh_far = bf16[32,512]{1,0:T(8,128)(2,1)S(1)} collective-permute-done((bf16[32,512]{1,0:T(8,128)(2,1)}, bf16[32,512]{1,0:T(8,128)(2,1)S(1)}, u32[]{:S(2)}, u32[]{:S(2)}) %collective-permute-start.3) | collective-permute-done | bytes 32800 | tf_op jit(solution)/shard_map/ppermute | solution.py:355
  9.0 1.0 %copy-done.3 = bf16[3,360,227]{1,2,0:T(8,128)(2,1)S(1)} copy-done((bf16[3,360,227]{1,2,0:T(8,128)(2,1)S(1)}, bf16[3,360,227]{1,2,0:T(8,128)(2,1)}, u32[]{:S(2)}) %copy-start.3) | copy-done | bytes 490344
  10.0 1.0 %copy-done.4 = bf16[512,512]{1,0:T(8,128)(2,1)S(1)} copy-done((bf16[512,512]{1,0:T(8,128)(2,1)S(1)}, bf16[512,512]{1,0:T(8,128)(2,1)}, u32[]{:S(2)}) %copy-start.4) | copy-done | bytes 524312
  11.1 0.8 %copy-done.9 = bf16[32,512]{1,0:T(8,128)(2,1)S(1)} copy-done((bf16[32,512]{1,0:T(8,128)(2,1)S(1)}, bf16[32,512]{1,0:T(8,128)(2,1)}, u32[]{:S(2)}) %copy-start.9) | copy-done | bytes 32792
  11.8 0.7 copy-done.11
  12.5 1.0 %shard_map.175 = (bf16[1024,227]{1,0:T(8,128)(2,1)S(1)}, bf16[128,512]{1,0:T(8,128)(2,1)S(1)}) custom-call(s32[1,1,1024]{2,1,0:T(1,128)S(1)} %copy-done.11, bf16[3,227,360]{2,1,0:T(8,128)(2,1)S(1)} %bitcast.5, bf16[32,512]{1,0:T(8,128)(2,1)S(1)} %collective-permute-done.2.near.mesh_near, bf16[32,512]{1,0:T(8,128)(2,1)S(1)} %collective-permute-done.3.far.mesh_far, ...), custom_call_target="tpu_custom_call" | custom-call | tf_op jit(solution)/shard_map/pallas_call | solution.py:308
  13.5 2.6 %collective-permute-done.near = bf16[3,227,360]{2,1,0:T(8,128)(2,1)S(1)} collective-permute-done((bf16[3,227,360]{2,1,0:T(8,128)(2,1)}, bf16[3,227,360]{2,1,0:T(8,128)(2,1)S(1)}, u32[]{:S(2)}, u32[]{:S(2)}) %collective-permute-start) | collective-permute-done | bytes 490352 | tf_op jit(solution)/shard_map/ppermute | solution.py:352
  16.1 5.5 %shard_map.176 = (bf16[1024,512]{1,0:T(8,128)(2,1)S(1)}, bf16[1024,512]{1,0:T(8,128)(2,1)S(1)}, f32[64,512]{1,0:T(8,128)S(1)}, bf16[32,512]{1,0:T(8,128)(2,1)S(1)}, bf16[32,512]{1,0:T(8,128)(2,1)S(1)}) custom-call(s32[1,1,1024]{2,1,0:T(1,128)S(1)} %copy-done.11, s32[1,1,1024]{2,1,0:T(1,128)S(1)} %copy-done.12, s32[1,1]{1,0:T(1,128)S(6)} %copy.19.count, ...), custom_call_target="tpu_custom_call" | custom-call | tf_op jit(solution)/shard_map/pallas_call | solution.py:308
  21.8 1.8 %collective-permute-start.5 = (bf16[32,512]{1,0:T(8,128)(2,1)S(1)}, bf16[32,512]{1,0:T(8,128)(2,1)S(1)}, u32[]{:S(2)}, u32[]{:S(2)}) collective-permute-start(bf16[32,512]{1,0:T(8,128)(2,1)S(1)} %get-tuple-element.35), channel_id=1, source_target_pairs={{0,3},{1,2},{2,1},{3,0},{4,7},{5,6},{6,5},{7,4},{8,11},{9,10},{10,... | collective-permute-start | bytes 98312 | tf_op jit(solution)/shard_map/ppermute | solution.py:376
  23.5 1.6 %collective-permute-done.5.far = bf16[32,512]{1,0:T(8,128)(2,1)S(1)} collective-permute-done((bf16[32,512]{1,0:T(8,128)(2,1)S(1)}, bf16[32,512]{1,0:T(8,128)(2,1)S(1)}, u32[]{:S(2)}, u32[]{:S(2)}) %collective-permute-start.5) | collective-permute-done | bytes 32800 | tf_op jit(solution)/shard_map/ppermute | solution.py:376
  25.5 4.8 %collective-permute-start.6 = (bf16[64,512]{1,0:T(8,128)(2,1)S(1)}, bf16[64,512]{1,0:T(8,128)(2,1)S(1)}, u32[]{:S(2)}, u32[]{:S(2)}) collective-permute-start(bf16[64,512]{1,0:T(8,128)(2,1)S(1)} %get-tuple-element.36.own), channel_id=1, source_target_pairs={{0,4},{4,0},{8,12},{12,8},{1,5},{5,1},{9,13},{13,9},{2,6},{6,2},{1... | collective-permute-start | bytes 196616 | tf_op jit(solution)/shard_map/ppermute | solution.py:382
  30.3 0.7 collective-permute-start.7
  31.6 1.4 %collective-permute-done.6.near = bf16[64,512]{1,0:T(8,128)(2,1)S(1)} collective-permute-done((bf16[64,512]{1,0:T(8,128)(2,1)S(1)}, bf16[64,512]{1,0:T(8,128)(2,1)S(1)}, u32[]{:S(2)}, u32[]{:S(2)}) %collective-permute-start.6) | collective-permute-done | bytes 65568 | tf_op jit(solution)/shard_map/ppermute | solution.py:382
  33.0 2.0 %shard_map.178 = (bf16[32,512]{1,0:T(8,128)(2,1)}, f32[192,512]{1,0:T(8,128)S(1)}, bf16[32,512]{1,0:T(8,128)(2,1)S(1)}, bf16[64,512]{1,0:T(8,128)(2,1)S(1)}, bf16[64,512]{1,0:T(8,128)(2,1)S(1)}) custom-call(s32[1,1,512]{2,1,0:T(1,128)S(1)} %copy-done.13, s32[1,1,512]{2,1,0:T(1,128)S(1)} %copy-done.14, s32[1,1]{1,0:T(1,128)S(6)} %copy.20.count, ...), custom_call_target="tpu_custom_call" | custom-call | tf_op jit(solution)/shard_map/pallas_call | solution.py:308
  35.0 3.7 %collective-permute-start.8 = (bf16[64,512]{1,0:T(8,128)(2,1)S(1)}, bf16[64,512]{1,0:T(8,128)(2,1)S(1)}, u32[]{:S(2)}, u32[]{:S(2)}) collective-permute-start(bf16[64,512]{1,0:T(8,128)(2,1)S(1)} %get-tuple-element.39), channel_id=1, source_target_pairs={{0,4},{4,0},{8,12},{12,8},{1,5},{5,1},{9,13},{13,9},{2,6},{6,2},{1... | collective-permute-start | bytes 196616 | tf_op jit(solution)/shard_map/ppermute | solution.py:396
  38.7 0.7 collective-permute-start.9
  39.6 1.3 %collective-permute-done.8.near = bf16[64,512]{1,0:T(8,128)(2,1)S(1)} collective-permute-done((bf16[64,512]{1,0:T(8,128)(2,1)S(1)}, bf16[64,512]{1,0:T(8,128)(2,1)S(1)}, u32[]{:S(2)}, u32[]{:S(2)}) %collective-permute-start.8) | collective-permute-done | bytes 65568 | tf_op jit(solution)/shard_map/ppermute | solution.py:396
  41.0 0.3 shard_map.180
  41.3 1.6 %collective-permute-start.11 = (bf16[32,512]{1,0:T(8,128)(2,1)S(1)}, bf16[32,512]{1,0:T(8,128)(2,1)S(1)}, u32[]{:S(2)}, u32[]{:S(2)}) collective-permute-start(bf16[32,512]{1,0:T(8,128)(2,1)S(1)} %get-tuple-element.44), channel_id=1, source_target_pairs={{0,3},{1,2},{2,1},{3,0},{4,7},{5,6},{6,5},{7,4},{8,11},{9,10},{10,... | collective-permute-start | bytes 98312 | tf_op jit(solution)/shard_map/ppermute | solution.py:410
  43.0 0.3 shard_map.183
  43.4 1.3 %collective-permute-done.11.far = bf16[32,512]{1,0:T(8,128)(2,1)S(1)} collective-permute-done((bf16[32,512]{1,0:T(8,128)(2,1)S(1)}, bf16[32,512]{1,0:T(8,128)(2,1)S(1)}, u32[]{:S(2)}, u32[]{:S(2)}) %collective-permute-start.11) | collective-permute-done | bytes 32800 | tf_op jit(solution)/shard_map/ppermute | solution.py:410
  44.8 1.2 %shard_map.181 = (f32[2,512,128]{2,1,0:T(8,128)S(1)}, bf16[2,512,128]{2,1,0:T(8,128)(2,1)S(1)}) custom-call(s32[1,1,1024]{2,1,0:T(1,128)S(1)} %copy-done.12, s32[1,1]{1,0:T(1,128)S(6)} %copy.19.count, f32[64,512]{1,0:T(8,128)S(1)} %get-tuple-element.42.part, bf16[32,512]{1,0:T(8,128)(2,1)S(1)} %collective-permute-done.10.near, ...), custom_call_target="tpu_custom_call" | custom-call | tf_op jit(solution)/shard_map/pallas_call | solution.py:308
  46.0 0.5 collective-permute-start.12
  46.6 1.6 %collective-permute-start.15 = (bf16[512,128]{1,0:T(8,128)(2,1)S(1)}, bf16[512,128]{1,0:T(8,128)(2,1)S(1)}, u32[]{:S(2)}, u32[]{:S(2)}) collective-permute-start(bf16[512,128]{1,0:T(8,128)(2,1)S(1)} %bitcast.6), channel_id=1, source_target_pairs={{0,2},{2,0},{1,3},{3,1},{4,6},{6,4},{5,7},{7,5},{8,10},{10,8},{9,1... | collective-permute-start | bytes 393224 | tf_op jit(solution)/shard_map/ppermute | solution.py:331
  48.2 1.1 %collective-permute-start.13 = (bf16[512,128]{1,0:T(8,128)(2,1)S(1)}, bf16[512,128]{1,0:T(8,128)(2,1)S(1)}, u32[]{:S(2)}, u32[]{:S(2)}) collective-permute-start(bf16[512,128]{1,0:T(8,128)(2,1)S(1)} %bitcast.7), channel_id=1, source_target_pairs={{0,2},{2,0},{1,3},{3,1},{4,6},{6,4},{5,7},{7,5},{8,10},{10,8},{9,1... | collective-permute-start | bytes 393224 | tf_op jit(solution)/shard_map/ppermute | solution.py:331
  49.3 3.7 %collective-permute-done.15.refs_3_ = bf16[512,128]{1,0:T(8,128)(2,1)S(1)} collective-permute-done((bf16[512,128]{1,0:T(8,128)(2,1)S(1)}, bf16[512,128]{1,0:T(8,128)(2,1)S(1)}, u32[]{:S(2)}, u32[]{:S(2)}) %collective-permute-start.15) | collective-permute-done | bytes 131104 | tf_op jit(solution)/shard_map/ppermute | solution.py:331
  53.0 1.9 %collective-permute-done.13.refs_1_ = bf16[512,128]{1,0:T(8,128)(2,1)S(1)} collective-permute-done((bf16[512,128]{1,0:T(8,128)(2,1)S(1)}, bf16[512,128]{1,0:T(8,128)(2,1)S(1)}, u32[]{:S(2)}, u32[]{:S(2)}) %collective-permute-start.13) | collective-permute-done | bytes 131104 | tf_op jit(solution)/shard_map/ppermute | solution.py:331
  55.0 14.4 %all_to_all.5.shares = bf16[4,2,128,128]{3,2,1,0:T(8,128)(2,1)S(1)} all-to-all(bf16[4,2,128,128]{3,2,1,0:T(8,128)(2,1)S(1)} %shard_map.185), channel_id=1, replica_groups=mesh['groups'=2,'band'=4,'dom'=2,'lat'=2] {'band'}, dimensions={0} | all-to-all | bytes 524288 | tf_op jit(solution)/shard_map/all_to_all | solution.py:446
  69.4 0.7 shard_map.186
  (43 shorter events, 1.0 us)
Async XLA Ops:
  0.6 15.4 %collective-permute-start = (bf16[3,227,360]{2,1,0:T(8,128)(2,1)}, bf16[3,227,360]{2,1,0:T(8,128)(2,1)S(1)}, u32[]{:S(2)}, u32[]{:S(2)}) collective-permute-start(bf16[3,227,360]{2,1,0:T(8,128)(2,1)} %bitcast.3), channel_id=1, source_target_pairs={{0,4},{4,0},{8,12},{12,8},{1,5},{5,1},{9,13},{13,9},{2,6},{6,2},{1... | collective-permute-start | bytes 1470968 | tf_op jit(solution)/shard_map/ppermute | solution.py:352
  3.7 12.4 %collective-permute-start.1 = (bf16[3,227,360]{2,1,0:T(8,128)(2,1)}, bf16[3,227,360]{2,1,0:T(8,128)(2,1)S(1)}, u32[]{:S(2)}, u32[]{:S(2)}) collective-permute-start(bf16[3,227,360]{2,1,0:T(8,128)(2,1)} %bitcast.4), channel_id=1, source_target_pairs={{0,0},{4,8},{8,4},{12,12},{1,1},{5,9},{9,5},{13,13},{2,2},{6,10},{... | collective-permute-start | bytes 1470968 | tf_op jit(solution)/shard_map/ppermute | solution.py:353
  5.4 2.3 %collective-permute-start.2 = (bf16[32,512]{1,0:T(8,128)(2,1)}, bf16[32,512]{1,0:T(8,128)(2,1)S(1)}, u32[]{:S(2)}, u32[]{:S(2)}) collective-permute-start(bf16[32,512]{1,0:T(8,128)(2,1)} %mesh_in.3), channel_id=1, source_target_pairs={{0,1},{1,0},{2,3},{3,2},{4,5},{5,4},{6,7},{7,6},{8,9},{9,8},{10,11... | collective-permute-start | bytes 98312 | tf_op jit(solution)/shard_map/ppermute | solution.py:354
  5.4 3.6 %collective-permute-start.3 = (bf16[32,512]{1,0:T(8,128)(2,1)}, bf16[32,512]{1,0:T(8,128)(2,1)S(1)}, u32[]{:S(2)}, u32[]{:S(2)}) collective-permute-start(bf16[32,512]{1,0:T(8,128)(2,1)} %mesh_in.3), channel_id=1, source_target_pairs={{0,3},{1,2},{2,1},{3,0},{4,7},{5,6},{6,5},{7,4},{8,11},{9,10},{10,... | collective-permute-start | bytes 98312 | tf_op jit(solution)/shard_map/ppermute | solution.py:355
  9.0 1.0 %copy-start.3 = (bf16[3,360,227]{1,2,0:T(8,128)(2,1)S(1)}, bf16[3,360,227]{1,2,0:T(8,128)(2,1)}, u32[]{:S(2)}) copy-start(bf16[3,360,227]{1,2,0:T(8,128)(2,1)} %param.16) | copy-start | bytes 1470964
  10.0 1.0 %copy-start.4 = (bf16[512,512]{1,0:T(8,128)(2,1)S(1)}, bf16[512,512]{1,0:T(8,128)(2,1)}, u32[]{:S(2)}) copy-start(bf16[512,512]{1,0:T(8,128)(2,1)} %w_gr.1) | copy-start | bytes 1572868
  11.1 0.8 %copy-start.9 = (bf16[32,512]{1,0:T(8,128)(2,1)S(1)}, bf16[32,512]{1,0:T(8,128)(2,1)}, u32[]{:S(2)}) copy-start(bf16[32,512]{1,0:T(8,128)(2,1)} %mesh_in.3) | copy-start | bytes 98308
  11.8 0.7 copy-start.11
  12.5 3.6 %copy-start.5 = (bf16[512,512]{1,0:T(8,128)(2,1)S(1)}, bf16[512,512]{1,0:T(8,128)(2,1)}, u32[]{:S(2)}) copy-start(bf16[512,512]{1,0:T(8,128)(2,1)} %w_gs.1) | copy-start | bytes 1572868
  12.5 3.6 %copy-start.7 = (bf16[227,512]{1,0:T(8,128)(2,1)S(1)}, bf16[227,512]{1,0:T(8,128)(2,1)}, u32[]{:S(2)}) copy-start(bf16[227,512]{1,0:T(8,128)(2,1)} %w_grid.1) | copy-start | bytes 697348
  12.5 3.6 %copy-start.12 = (s32[1,1,1024]{2,1,0:T(1,128)S(1)}, s32[1,1,1024]{2,1,0:T(1,128)}, u32[]{:S(2)}) copy-start(s32[1,1,1024]{2,1,0:T(1,128)} %recv.5) | copy-start | bytes 12292
  16.1 9.1 %copy-start = (bf16[512,512]{1,0:T(8,128)(2,1)S(1)}, bf16[512,512]{1,0:T(8,128)(2,1)}, u32[]{:S(2)}) copy-start(bf16[512,512]{1,0:T(8,128)(2,1)} %w_gn.3) | copy-start | bytes 1572868
  16.1 9.1 %copy-start.10 = (bf16[32,512]{1,0:T(8,128)(2,1)S(1)}, bf16[32,512]{1,0:T(8,128)(2,1)}, u32[]{:S(2)}) copy-start(bf16[32,512]{1,0:T(8,128)(2,1)} %mesh_in.3) | copy-start | bytes 98308
  16.1 16.9 %copy-start.2 = (bf16[512,512]{1,0:T(8,128)(2,1)S(1)}, bf16[512,512]{1,0:T(8,128)(2,1)}, u32[]{:S(2)}) copy-start(bf16[512,512]{1,0:T(8,128)(2,1)} %w_ms.3) | copy-start | bytes 1572868
  16.1 16.9 %copy-start.6 = (bf16[512,512]{1,0:T(8,128)(2,1)S(1)}, bf16[512,512]{1,0:T(8,128)(2,1)}, u32[]{:S(2)}) copy-start(bf16[512,512]{1,0:T(8,128)(2,1)} %w_mn.1) | copy-start | bytes 1572868
  21.7 11.3 %copy-start.1 = (bf16[512,512]{1,0:T(8,128)(2,1)S(1)}, bf16[512,512]{1,0:T(8,128)(2,1)}, u32[]{:S(2)}) copy-start(bf16[512,512]{1,0:T(8,128)(2,1)} %w_mr.3) | copy-start | bytes 1572868
  21.7 1.9 %collective-permute-start.4 = (bf16[32,512]{1,0:T(8,128)(2,1)S(1)}, bf16[32,512]{1,0:T(8,128)(2,1)S(1)}, u32[]{:S(2)}, u32[]{:S(2)}) collective-permute-start(bf16[32,512]{1,0:T(8,128)(2,1)S(1)} %get-tuple-element.34), channel_id=1, source_target_pairs={{0,1},{1,0},{2,3},{3,2},{4,5},{5,4},{6,7},{7,6},{8,9},{9,8},{10,11... | collective-permute-start | bytes 98312 | tf_op jit(solution)/shard_map/ppermute | solution.py:375
  21.8 3.4 %collective-permute-start.5 = (bf16[32,512]{1,0:T(8,128)(2,1)S(1)}, bf16[32,512]{1,0:T(8,128)(2,1)S(1)}, u32[]{:S(2)}, u32[]{:S(2)}) collective-permute-start(bf16[32,512]{1,0:T(8,128)(2,1)S(1)} %get-tuple-element.35), channel_id=1, source_target_pairs={{0,3},{1,2},{2,1},{3,0},{4,7},{5,6},{6,5},{7,4},{8,11},{9,10},{10,... | collective-permute-start | bytes 98312 | tf_op jit(solution)/shard_map/ppermute | solution.py:376
  25.2 7.8 %copy-start.8 = (bf16[32,512]{1,0:T(8,128)(2,1)S(1)}, bf16[32,512]{1,0:T(8,128)(2,1)}, u32[]{:S(2)}) copy-start(bf16[32,512]{1,0:T(8,128)(2,1)} %d_out.3) | copy-start | bytes 98308
  25.2 7.8 %copy-start.14 = (s32[1,1,512]{2,1,0:T(1,128)S(1)}, s32[1,1,512]{2,1,0:T(1,128)}, u32[]{:S(2)}) copy-start(s32[1,1,512]{2,1,0:T(1,128)} %recv.4) | copy-start | bytes 6148
  25.4 7.6 %copy-start.13 = (s32[1,1,512]{2,1,0:T(1,128)S(1)}, s32[1,1,512]{2,1,0:T(1,128)}, u32[]{:S(2)}) copy-start(s32[1,1,512]{2,1,0:T(1,128)} %send.5) | copy-start | bytes 6148
  25.5 7.5 %collective-permute-start.6 = (bf16[64,512]{1,0:T(8,128)(2,1)S(1)}, bf16[64,512]{1,0:T(8,128)(2,1)S(1)}, u32[]{:S(2)}, u32[]{:S(2)}) collective-permute-start(bf16[64,512]{1,0:T(8,128)(2,1)S(1)} %get-tuple-element.36.own), channel_id=1, source_target_pairs={{0,4},{4,0},{8,12},{12,8},{1,5},{5,1},{9,13},{13,9},{2,6},{6,2},{1... | collective-permute-start | bytes 196616 | tf_op jit(solution)/shard_map/ppermute | solution.py:382
  30.3 2.7 %collective-permute-start.7 = (bf16[64,512]{1,0:T(8,128)(2,1)S(1)}, bf16[64,512]{1,0:T(8,128)(2,1)S(1)}, u32[]{:S(2)}, u32[]{:S(2)}) collective-permute-start(bf16[64,512]{1,0:T(8,128)(2,1)S(1)} %get-tuple-element.36.own), channel_id=1, source_target_pairs={{0,0},{4,8},{8,4},{12,12},{1,1},{5,9},{9,5},{13,13},{2,2},{6,10},{... | collective-permute-start | bytes 196616 | tf_op jit(solution)/shard_map/ppermute | solution.py:383
  35.0 5.9 %collective-permute-start.8 = (bf16[64,512]{1,0:T(8,128)(2,1)S(1)}, bf16[64,512]{1,0:T(8,128)(2,1)S(1)}, u32[]{:S(2)}, u32[]{:S(2)}) collective-permute-start(bf16[64,512]{1,0:T(8,128)(2,1)S(1)} %get-tuple-element.39), channel_id=1, source_target_pairs={{0,4},{4,0},{8,12},{12,8},{1,5},{5,1},{9,13},{13,9},{2,6},{6,2},{1... | collective-permute-start | bytes 196616 | tf_op jit(solution)/shard_map/ppermute | solution.py:396
  38.7 2.2 %collective-permute-start.9 = (bf16[64,512]{1,0:T(8,128)(2,1)S(1)}, bf16[64,512]{1,0:T(8,128)(2,1)S(1)}, u32[]{:S(2)}, u32[]{:S(2)}) collective-permute-start(bf16[64,512]{1,0:T(8,128)(2,1)S(1)} %get-tuple-element.40), channel_id=1, source_target_pairs={{0,0},{4,8},{8,4},{12,12},{1,1},{5,9},{9,5},{13,13},{2,2},{6,10},{... | collective-permute-start | bytes 196616 | tf_op jit(solution)/shard_map/ppermute | solution.py:397
  41.3 2.2 %collective-permute-start.10 = (bf16[32,512]{1,0:T(8,128)(2,1)S(1)}, bf16[32,512]{1,0:T(8,128)(2,1)S(1)}, u32[]{:S(2)}, u32[]{:S(2)}) collective-permute-start(bf16[32,512]{1,0:T(8,128)(2,1)S(1)} %get-tuple-element.43), channel_id=1, source_target_pairs={{0,1},{1,0},{2,3},{3,2},{4,5},{5,4},{6,7},{7,6},{8,9},{9,8},{10,11... | collective-permute-start | bytes 98312 | tf_op jit(solution)/shard_map/ppermute | solution.py:409
  41.3 3.4 %collective-permute-start.11 = (bf16[32,512]{1,0:T(8,128)(2,1)S(1)}, bf16[32,512]{1,0:T(8,128)(2,1)S(1)}, u32[]{:S(2)}, u32[]{:S(2)}) collective-permute-start(bf16[32,512]{1,0:T(8,128)(2,1)S(1)} %get-tuple-element.44), channel_id=1, source_target_pairs={{0,3},{1,2},{2,1},{3,0},{4,7},{5,6},{6,5},{7,4},{8,11},{9,10},{10,... | collective-permute-start | bytes 98312 | tf_op jit(solution)/shard_map/ppermute | solution.py:410
  43.3 3.2 %collective-permute-start.14 = (bf16[2,512,128]{2,1,0:T(8,128)(2,1)S(1)}, bf16[2,512,128]{2,1,0:T(8,128)(2,1)S(1)}, u32[]{:S(2)}, u32[]{:S(2)}) collective-permute-start(bf16[2,512,128]{2,1,0:T(8,128)(2,1)S(1)} %get-tuple-element.54), channel_id=1, source_target_pairs={{0,1},{1,0},{2,3},{3,2},{4,5},{5,4},{6,7},{7,6},{8,9},{9,8},{10,11... | collective-permute-start | bytes 786440 | tf_op jit(solution)/shard_map/ppermute | solution.py:331
  46.0 2.1 %collective-permute-start.12 = (bf16[2,512,128]{2,1,0:T(8,128)(2,1)S(1)}, bf16[2,512,128]{2,1,0:T(8,128)(2,1)S(1)}, u32[]{:S(2)}, u32[]{:S(2)}) collective-permute-start(bf16[2,512,128]{2,1,0:T(8,128)(2,1)S(1)} %get-tuple-element.49), channel_id=1, source_target_pairs={{0,1},{1,0},{2,3},{3,2},{4,5},{5,4},{6,7},{7,6},{8,9},{9,8},{10,11... | collective-permute-start | bytes 786440 | tf_op jit(solution)/shard_map/ppermute | solution.py:331
  46.6 6.4 %collective-permute-start.15 = (bf16[512,128]{1,0:T(8,128)(2,1)S(1)}, bf16[512,128]{1,0:T(8,128)(2,1)S(1)}, u32[]{:S(2)}, u32[]{:S(2)}) collective-permute-start(bf16[512,128]{1,0:T(8,128)(2,1)S(1)} %bitcast.6), channel_id=1, source_target_pairs={{0,2},{2,0},{1,3},{3,1},{4,6},{6,4},{5,7},{7,5},{8,10},{10,8},{9,1... | collective-permute-start | bytes 393224 | tf_op jit(solution)/shard_map/ppermute | solution.py:331
  48.2 6.7 %collective-permute-start.13 = (bf16[512,128]{1,0:T(8,128)(2,1)S(1)}, bf16[512,128]{1,0:T(8,128)(2,1)S(1)}, u32[]{:S(2)}, u32[]{:S(2)}) collective-permute-start(bf16[512,128]{1,0:T(8,128)(2,1)S(1)} %bitcast.7), channel_id=1, source_target_pairs={{0,2},{2,0},{1,3},{3,1},{4,6},{6,4},{5,7},{7,5},{8,10},{10,8},{9,1... | collective-permute-start | bytes 393224 | tf_op jit(solution)/shard_map/ppermute | solution.py:331

commit v4 on v3

--- a/solution.py
+++ b/solution.py
@@ -70,19 +70,17 @@
     return lax.rem(lax.axis_index(axis), 2) == 0
 
 
-def spread(index, cols, pitch):
+def spread(index, blocks, cols, pitch):
     extra = jnp.zeros_like(index)
-    block = 1
-    while block * cols < 9 * cols:
+    for block in range(1, blocks):
         extra = extra + jnp.where(index >= block * cols, pitch - cols, 0)
-        block += 1
     return index + extra
 
 
 def fill(wide, blocks, pitch, first):
+    cols = blocks.shape[2]
     for k in range(blocks.shape[0]):
         at = first + k * pitch
-        cols = blocks.shape[2]
         wide[:, at : at + cols] = blocks[k]
         if cols < pitch:
             wide[:, at + cols : at + pitch] = jnp.zeros(
@@ -90,9 +88,45 @@
             )
 
 
-def own_gather_kernel(send, grid, near, far, mesh_in, w_gr, rows_out, table_out, wide):
+def index_kernel(
+    send, recv, count, mesh_send, mesh_recv, mesh_count, grid,
+    own_out, halo_hits, recv_hits, recv_rows, from_hits, to_hits, from_rows, to_rows, wide,
+):
     band_rows, _, cols = grid.shape
     pitch = wide.shape[1] // band_rows
+    width = band_rows * pitch
+    cycle = recv_rows.shape[0]
+    node_count = to_rows.shape[0]
+    even_band = even_on("band")
+    fill(wide, grid, pitch, 0)
+    below = jnp.where(even_band, width, 0)
+    above = jnp.where(even_band, -2 * width, -width)
+    block = 256
+    for first in range(0, send.shape[2], block):
+        part_of = slice(first, first + block)
+        lane = spread(send[0, :, part_of], 3 * band_rows, cols, pitch)
+        inner = (lane >= width) & (lane < 2 * width)
+        index = columns(lane)
+        own_hit = hits_from(index, width, width, width)
+        own_out[part_of] = mm_nt(own_hit, wide[...]).astype(BF16)
+        lane = jnp.where(lane < width, lane + below, jnp.where(inner, -1, lane + above))
+        halo_hits[part_of] = hits_from(columns(lane), 2 * width, 2 * width)
+        target = live_only(recv[0, :, part_of], count[0, 0], first)
+        recv_hits[part_of] = hits_from(columns(target), 2 * cycle, cycle)
+        recv_rows[:, part_of] = hits_to(target, cycle)
+    raw = mesh_send[0]
+    flipped = jnp.where(
+        raw < cycle, raw + 2 * cycle, jnp.where(raw < 2 * cycle, raw, raw - 2 * cycle)
+    )
+    source = jnp.where(even_band, flipped, raw)
+    target = live_only(mesh_recv[0], mesh_count[0, 0])
+    from_hits[...] = hits_from(columns(source), 6 * cycle, 3 * cycle)
+    to_hits[...] = hits_from(columns(target), 2 * node_count, node_count)
+    from_rows[...] = hits_to(source, 3 * cycle)
+    to_rows[...] = hits_to(target, node_count)
+
+
+def table_kernel(near, far, mesh_in, w_gr, table_out):
     node_count = mesh_in.shape[0]
     rim = node_count // 2
     even = even_on("lat")
@@ -102,49 +136,29 @@
     high, low = halves(mm(cycle, w_gr[...]))
     table_out[: 2 * node_count] = high
     table_out[2 * node_count :] = low
-    fill(wide, grid, pitch, 0)
-    block = 256
-    width = band_rows * pitch
-    for first in range(0, send.shape[2], block):
-        lane = spread(send[0, :, first : first + block], cols, pitch)
-        hit = hits_from(columns(lane), width, width, width)
-        rows_out[first : first + block] = mm_nt(hit, wide[...]).astype(BF16)
 
 
 def encode_kernel(
-    send, recv, count, near, far, own, table, w_grid, w_gs,
+    near, far, halo_hits, recv_hits, recv_rows, own, table, w_grid, w_gs,
     senders_out, slope_out, part_out, near_out, far_out, wide,
 ):
-    band_rows, _, cols = near.shape
+    band_rows = near.shape[0]
     pitch = wide.shape[1] // (2 * band_rows)
-    cycle = table.shape[0] // 2
-    half = cycle // 2
-    width = band_rows * pitch
+    half = recv_rows.shape[0] // 2
     fill(wide, near, pitch, 0)
-    fill(wide, far, pitch, width)
-    even_band = even_on("band")
-    below = jnp.where(even_band, width, 0)
-    above = jnp.where(even_band, -2 * width, -width)
+    fill(wide, far, pitch, band_rows * pitch)
     block = 256
     sums = None
-    for first in range(0, send.shape[2], block):
+    for first in range(0, own.shape[0], block):
         part_of = slice(first, first + block)
-        lane = spread(send[0, :, part_of], cols, pitch)
-        lane = jnp.where(
-            lane < width, lane + below, jnp.where(lane < 2 * width, -1, lane + above)
-        )
-        hit = hits_from(columns(lane), 2 * width, 2 * width)
-        raw = own[part_of] + mm_nt(hit, wide[...]).astype(BF16)
+        raw = own[part_of] + mm_nt(halo_hits[part_of], wide[...]).astype(BF16)
         latent, _ = silu_parts(mm(raw, w_grid[...]))
         latent = latent.astype(BF16)
         senders_out[part_of] = latent
-        target = live_only(recv[0, :, part_of], count[0, 0], first)
-        pre = mm(latent, w_gs[...]) + mm(
-            hits_from(columns(target), 2 * cycle, cycle), table[...]
-        )
+        pre = mm(latent, w_gs[...]) + mm(recv_hits[part_of], table[...])
         value, slope = silu_parts(pre)
         slope_out[part_of] = slope.astype(BF16)
-        part = mm(hits_to(target, cycle), value.astype(BF16))
+        part = mm(recv_rows[:, part_of], value.astype(BF16))
         sums = part if sums is None else sums + part
     part_out[...] = sums
     even = even_on("lat")
@@ -168,37 +182,26 @@
 
 
 def process_kernel(
-    send, recv, count, near, own, far, d_out, w_ms, w_mr, w_mn,
+    from_hits, to_hits, from_rows, to_rows, near, own, far, d_out, w_ms, w_mr, w_mn,
     mesh_out, sums_out, recv_out, near_out, far_out,
 ):
     cycle = own.shape[0]
     node_count = cycle // 2
     rim = node_count // 2
-    even_band = even_on("band")
-    raw = send[0]
-    flipped = jnp.where(
-        raw < cycle, raw + 2 * cycle, jnp.where(raw < 2 * cycle, raw, raw - 2 * cycle)
-    )
-    source = jnp.where(even_band, flipped, raw)
-    target = live_only(recv[0], count[0, 0])
     home = own[rim : rim + node_count]
     block = jnp.concatenate([near[...], own[...], far[...]], axis=0)
-    table = jnp.concatenate(
-        [*halves(mm(block, w_ms[...])), *halves(mm(home, w_mr[...]))], axis=0
-    )
-    from_hits = hits_from(columns(source), 6 * cycle, 3 * cycle)
-    to_hits = hits_from(columns(target), 2 * node_count, node_count)
-    pre = mm(from_hits, table[: 6 * cycle]) + mm(to_hits, table[6 * cycle :])
+    table = jnp.concatenate(halves(mm(block, w_ms[...])), axis=0)
+    recv_table = jnp.concatenate(halves(mm(home, w_mr[...])), axis=0)
+    pre = mm(from_hits[...], table) + mm(to_hits[...], recv_table)
     value, slope = silu_parts(pre)
-    to_rows = hits_to(target, node_count)
-    gate = mm(mm(to_rows, value.astype(BF16)).astype(BF16), w_mn[...])
+    gate = mm(mm(to_rows[...], value.astype(BF16)).astype(BF16), w_mn[...])
     gate_value, gate_slope = silu_parts(gate)
     mesh_out[...] = (home.astype(F32) + gate_value).astype(BF16)
     gate_two = (d_out[...].astype(F32) * gate_slope).astype(BF16)
     back = jnp.concatenate(halves(mm_nt(gate_two, w_mn[...])), axis=0)
-    edge_slope = (mm(to_hits, back) * slope).astype(BF16)
-    sums = mm(hits_to(source, 3 * cycle), edge_slope)
-    recv_out[...] = mm(to_rows, edge_slope).astype(BF16)
+    edge_slope = (mm(to_hits[...], back) * slope).astype(BF16)
+    sums = mm(from_rows[...], edge_slope)
+    recv_out[...] = mm(to_rows[...], edge_slope).astype(BF16)
     sums_out[...] = sums
     near_out[...] = sums[:cycle].astype(BF16)
     far_out[...] = sums[2 * cycle :].astype(BF16)
@@ -227,18 +230,17 @@
     home_out[...] = mm_nt(recv_sum[...], w_mr[...]) + d_out[...].astype(F32)
 
 
-def process_grad_kernel(own, total, keep, sends):
-    split_store(mm_tn(own[...], total[...]), keep, sends)
-
-
-def cotangent_kernel(sums, near, far, home, w_ms, total_out, part_out, near_out, far_out):
+def process_grad_kernel(near, own, far, sums, after, keep, sends):
+    block = jnp.concatenate([near[...], own[...], far[...]], axis=0)
+    split_store(mm_tn(block, sums[...].astype(BF16)), keep, sends)
+
+
+def cotangent_kernel(sums, near, far, home, w_ms, part_out, near_out, far_out):
     cycle = near.shape[0]
     half = cycle // 2
     rim = half // 2
     total = sums[cycle : 2 * cycle] + near[...].astype(F32) + far[...].astype(F32)
-    total = total.astype(BF16)
-    total_out[...] = total
-    back = mm_nt(total, w_ms[...])
+    back = mm_nt(total.astype(BF16), w_ms[...])
     back = jnp.concatenate(
         [back[:rim], back[rim : rim + half] + home[...], back[rim + half :]], axis=0
     )
@@ -249,18 +251,15 @@
 
 
 def encode_grad_kernel(
-    recv, count, part, near, far, node_slope, w_gn, senders, edge_slope, keep, sends
+    recv_hits, part, near, far, node_slope, w_gn, senders, edge_slope, keep, sends
 ):
-    cycle = part.shape[0]
     even = even_on("lat")
     left = jnp.where(even, far[...], near[...]).astype(F32)
     right = jnp.where(even, near[...], far[...]).astype(F32)
     cot = part[...] + jnp.concatenate([left, right], axis=0)
     gate_one = (cot * node_slope[...]).astype(BF16)
     back = jnp.concatenate(halves(mm_nt(gate_one, w_gn[...])), axis=0)
-    target = live_only(recv[0], count[0, 0])
-    hits = hits_from(columns(target), 2 * cycle, cycle)
-    slope = (mm(hits, back) * edge_slope[...].astype(F32)).astype(BF16)
+    slope = (mm(recv_hits[...], back) * edge_slope[...].astype(F32)).astype(BF16)
     split_store(mm_tn(senders[...], slope), keep, sends)
 
 
@@ -349,15 +348,29 @@
     grid = jnp.transpose(grid_in, (0, 2, 1))
     pitch = -(-grid.shape[2] // LANES) * LANES
     wide = (variables, grid.shape[0] * pitch)
+    raw_far = lax.ppermute(grid, "band", band_far)
     raw_near = lax.ppermute(grid, "band", band_near)
-    raw_far = lax.ppermute(grid, "band", band_far)
+    mesh_far = lax.ppermute(mesh_in, around, ring_far)
     mesh_near = lax.ppermute(mesh_in, around, ring_near)
-    mesh_far = lax.ppermute(mesh_in, around, ring_far)
-    own_rows, table = call(
-        own_gather_kernel,
-        [((edges, variables), BF16), ((2 * cycle, latent), BF16)],
-        g2m_send, grid, mesh_near, mesh_far, mesh_in, w_gr,
+    mesh_edges = mesh_send.shape[2]
+    own_rows, halo_hits, recv_hits, recv_rows, from_hits, to_hits, from_rows, to_rows = call(
+        index_kernel,
+        [
+            ((edges, variables), BF16),
+            ((edges, 2 * wide[1]), BF16),
+            ((edges, 2 * cycle), BF16),
+            ((cycle, edges), BF16),
+            ((mesh_edges, 6 * cycle), BF16),
+            ((mesh_edges, 2 * node_count), BF16),
+            ((3 * cycle, mesh_edges), BF16),
+            ((node_count, mesh_edges), BF16),
+        ],
+        g2m_send, g2m_recv, g2m_count, mesh_send, mesh_recv, mesh_count, grid,
+        scalars=(2, 5),
         scratch=[(wide, BF16)],
+    )
+    (table,) = call(
+        table_kernel, [((2 * cycle, latent), BF16)], mesh_near, mesh_far, mesh_in, w_gr
     )
     senders, edge_slope, part, to_near, to_far = call(
         encode_kernel,
@@ -368,19 +381,18 @@
             ((node_count, latent), BF16),
             ((node_count, latent), BF16),
         ],
-        g2m_send, g2m_recv, g2m_count, raw_near, raw_far, own_rows, table, w_grid, w_gs,
-        scalars=(2,),
+        raw_near, raw_far, halo_hits, recv_hits, recv_rows, own_rows, table, w_grid, w_gs,
         scratch=[((variables, 2 * wide[1]), BF16)],
     )
+    from_far = lax.ppermute(to_far, around, ring_far)
     from_near = lax.ppermute(to_near, around, ring_near)
-    from_far = lax.ppermute(to_far, around, ring_far)
     mesh_one, node_slope = call(
         node_kernel,
         [((cycle, latent), BF16), ((cycle, latent), F32)],
         part, from_near, from_far, mesh_near, mesh_far, mesh_in, w_gn,
     )
+    one_far = lax.ppermute(mesh_one, "band", band_far)
     one_near = lax.ppermute(mesh_one, "band", band_near)
-    one_far = lax.ppermute(mesh_one, "band", band_far)
     mesh_out, sums, recv_sum, to_near, to_far = call(
         process_kernel,
         [
@@ -390,25 +402,11 @@
             ((cycle, latent), BF16),
             ((cycle, latent), BF16),
         ],
-        mesh_send, mesh_recv, mesh_count, one_near, mesh_one, one_far, d_out, w_ms, w_mr, w_mn,
-        scalars=(2,),
-    )
+        from_hits, to_hits, from_rows, to_rows, one_near, mesh_one, one_far, d_out,
+        w_ms, w_mr, w_mn,
+    )
+    from_far = lax.ppermute(to_far, "band", band_far)
     from_near = lax.ppermute(to_near, "band", band_near)
-    from_far = lax.ppermute(to_far, "band", band_far)
-    (home,) = call(home_kernel, [((node_count, latent), F32)], recv_sum, d_out, w_mr)
-    total, part, to_near, to_far = call(
-        cotangent_kernel,
-        [
-            ((cycle, latent), BF16),
-            ((cycle, latent), F32),
-            ((node_count, latent), BF16),
-            ((node_count, latent), BF16),
-        ],
-        sums, from_near, from_far, home, w_ms,
-    )
-    from_near = lax.ppermute(to_near, around, ring_near)
-    from_far = lax.ppermute(to_far, around, ring_far)
-
     doms = lax.axis_size("dom")
     lats = lax.axis_size("lat")
     cols = latent // sectors
@@ -416,6 +414,22 @@
         ((doms, latent, cols), F32),
         (((lats - 1) * doms, latent, cols), BF16),
     ]
+    ms_halves = call(
+        process_grad_kernel, halves_shape, one_near, mesh_one, one_far, sums, from_near
+    )
+    *ms_halves, from_far = lax.optimization_barrier((*ms_halves, from_far))
+    (home,) = call(home_kernel, [((node_count, latent), F32)], recv_sum, d_out, w_mr)
+    part, to_near, to_far = call(
+        cotangent_kernel,
+        [
+            ((cycle, latent), F32),
+            ((node_count, latent), BF16),
+            ((node_count, latent), BF16),
+        ],
+        sums, from_near, from_far, home, w_ms,
+    )
+    from_far = lax.ppermute(to_far, around, ring_far)
+    from_near = lax.ppermute(to_near, around, ring_near)
 
     def over_lat(keep, sends):
         came = [
@@ -428,14 +442,12 @@
         )
         return [keep] + [shifted(sends[i], "dom", i + 1) for i in range(doms - 1)]
 
-    ms_parts = over_lat(*call(process_grad_kernel, halves_shape, mesh_one, total))
+    ms_parts = over_lat(*ms_halves)
     gs_parts = over_lat(
         *call(
             encode_grad_kernel,
             halves_shape,
-            g2m_recv, g2m_count, part, from_near, from_far, node_slope, w_gn, senders,
-            edge_slope,
-            scalars=(1,),
+            recv_hits, part, from_near, from_far, node_slope, w_gn, senders, edge_slope,
         )
     )
     (shares,) = call(

time: 70.5 us -> 73 us (1.035)
  local copies, waits for them, and re-layouts: 3.59 us -> 7.65 us
  starting transfers between devices: 23.1 us -> 21.6 us
  Pallas kernels: 11.7 us -> 12.7 us
    unnamed x30 -> x28, local copies, waits for them, and re-layouts: 3.59 us -> 7.65 us
    ppermute x1, starting transfers between devices: 3.7 us -> 1.91 us  [on_device(): from_near = lax.ppermute(to_near, 'band', band_near)]
    ppermute x1, starting transfers between devices: 3.09 us -> 4.88 us  [on_device(): raw_near = lax.ppermute(grid, 'band', band_near)]
    ppermute x1, starting transfers between devices: 4.82 us -> 3.5 us  [on_device(): one_near = lax.ppermute(mesh_one, 'band', band_near)]
    ppermute x1, waiting for transfers between devices: 1.28 us -> 0.01 us  [on_device(): mesh_far = lax.ppermute(mesh_in, around, ring_far)]
    ppermute x1, starting transfers between devices: 0.01 us -> 1.24 us  [on_device(): mesh_near = lax.ppermute(mesh_in, around, ring_near)]
    ppermute x1, starting transfers between devices: 1.6 us -> 0.37 us  [on_device(): mesh_far = lax.ppermute(mesh_in, around, ring_far)]
    ppermute x1, waiting for transfers between devices: 2.56 us -> 1.36 us  [on_device(): raw_near = lax.ppermute(grid, 'band', band_near)]
  transfers between devices with their start and end apart: 16 -> 16, of which waited for: 8 -> 7; matrix products, arithmetic and copies ran while one was open for 0% -> 0% of each run, Pallas kernels for 4% -> 5%
where the time goes in v4:
time: 73 us; the launch traced here: 72.5 us
  starting transfers between devices  21.6 us (30%)
  waiting for transfers between devices  14.5 us (20%)
  blocking collectives  13.9 us (19%)
  Pallas kernels  12.7 us (17%)
  local copies, waits for them, and re-layouts  7.65 us (10%)
  between operations  2.13 us (3%)
    all_to_all x1, blocking collectives, on_device(): shares = lax.all_to_all(shares, 'band', 0, 0, tiled=True)  13.9 us
    pallas_call x13, Pallas kernels, call(): pl.pallas_call(kernel, out_shape=[jax.ShapeDtypeStruct(shape, dtype) for...  12.7 us
    unnamed x28, local copies, waits for them, and re-layouts  7.65 us
    ppermute x4, waiting for transfers between devices, shifted(): lax.ppermute(x, axis, [(i, (i + shift) % count) for i in range(count)])  5.62 us
    ppermute x1, starting transfers between devices, on_device(): raw_near = lax.ppermute(grid, 'band', band_near)  4.88 us
    ppermute x2, waiting for transfers between devices, on_device(): from_far = lax.ppermute(to_far, around, ring_far)  3.53 us
    ppermute x1, starting transfers between devices, on_device(): one_near = lax.ppermute(mesh_one, 'band', band_near)  3.5 us
    ppermute x4, starting transfers between devices, shifted(): lax.ppermute(x, axis, [(i, (i + shift) % count) for i in range(count)])  3.25 us
  transfers between devices with their start and end apart: 16, of which 7 were waited for; matrix products, arithmetic and copies ran while one was open for 0% of the time, Pallas kernels for 5%

profile of v4, /device:TPU:0, one launch (start us, length us, event | category | flops | bytes accessed | tf_op | source)
XLA Modules:
  0.0 72.5 jit_solution(3958417416427396699)
XLA Ops:
  0.6 1.8 %collective-permute-start.1 = (bf16[3,227,360]{2,1,0:T(8,128)(2,1)}, bf16[3,227,360]{2,1,0:T(8,128)(2,1)S(1)}, u32[]{:S(2)}, u32[]{:S(2)}) collective-permute-start(bf16[3,227,360]{2,1,0:T(8,128)(2,1)} %bitcast.3), channel_id=1, source_target_pairs={{0,0},{4,8},{8,4},{12,12},{1,1},{5,9},{9,5},{13,13},{2,2},{6,10},{... | collective-permute-start | bytes 1470968 | tf_op jit(solution)/shard_map/ppermute | solution.py:351
  2.5 4.9 %collective-permute-start = (bf16[3,227,360]{2,1,0:T(8,128)(2,1)}, bf16[3,227,360]{2,1,0:T(8,128)(2,1)S(1)}, u32[]{:S(2)}, u32[]{:S(2)}) collective-permute-start(bf16[3,227,360]{2,1,0:T(8,128)(2,1)} %bitcast.4), channel_id=1, source_target_pairs={{0,4},{4,0},{8,12},{12,8},{1,5},{5,1},{9,13},{13,9},{2,6},{6,2},{1... | collective-permute-start | bytes 1470968 | tf_op jit(solution)/shard_map/ppermute | solution.py:352
  7.7 1.2 %collective-permute-start.2 = (bf16[32,512]{1,0:T(8,128)(2,1)}, bf16[32,512]{1,0:T(8,128)(2,1)S(1)}, u32[]{:S(2)}, u32[]{:S(2)}) collective-permute-start(bf16[32,512]{1,0:T(8,128)(2,1)} %mesh_in.3), channel_id=1, source_target_pairs={{0,1},{1,0},{2,3},{3,2},{4,5},{5,4},{6,7},{7,6},{8,9},{9,8},{10,11... | collective-permute-start | bytes 98312 | tf_op jit(solution)/shard_map/ppermute | solution.py:354
  10.3 1.0 %copy-done.3 = bf16[3,360,227]{1,2,0:T(8,128)(2,1)S(1)} copy-done((bf16[3,360,227]{1,2,0:T(8,128)(2,1)S(1)}, bf16[3,360,227]{1,2,0:T(8,128)(2,1)}, u32[]{:S(2)}) %copy-start.3) | copy-done | bytes 490344
  11.3 0.7 copy-done.10
  12.0 0.7 copy-done.11
  12.7 0.7 copy-done.12
  13.4 0.7 copy-done.13
  14.0 1.9 %shard_map.175 = (bf16[1024,227]{1,0:T(8,128)(2,1)S(1)}, bf16[1024,2304]{1,0:T(8,128)(2,1)S(1)}, bf16[1024,128]{1,0:T(8,128)(2,1)S(1)}, bf16[64,1024]{1,0:T(8,12...) custom-call(s32[1,1,1024]{2,1,0:T(1,128)S(1)} %copy-done.10, ...), custom_call_target="tpu_custom_call" | custom-call | tf_op jit(solution)/shard_map/pallas_call | solution.py:307
  16.0 1.1 %copy-done.6 = bf16[512,512]{1,0:T(8,128)(2,1)S(1)} copy-done((bf16[512,512]{1,0:T(8,128)(2,1)S(1)}, bf16[512,512]{1,0:T(8,128)(2,1)}, u32[]{:S(2)}) %copy-start.6) | copy-done | bytes 524312
  17.1 0.8 %copy-done.9 = bf16[32,512]{1,0:T(8,128)(2,1)S(1)} copy-done((bf16[32,512]{1,0:T(8,128)(2,1)S(1)}, bf16[32,512]{1,0:T(8,128)(2,1)}, u32[]{:S(2)}) %copy-start.9) | copy-done | bytes 32792
  18.1 1.4 %collective-permute-done.near = bf16[3,227,360]{2,1,0:T(8,128)(2,1)S(1)} collective-permute-done((bf16[3,227,360]{2,1,0:T(8,128)(2,1)}, bf16[3,227,360]{2,1,0:T(8,128)(2,1)S(1)}, u32[]{:S(2)}, u32[]{:S(2)}) %collective-permute-start) | collective-permute-done | bytes 490352 | tf_op jit(solution)/shard_map/ppermute | solution.py:352
  19.4 1.0 %copy-done.4 = bf16[512,512]{1,0:T(8,128)(2,1)S(1)} copy-done((bf16[512,512]{1,0:T(8,128)(2,1)S(1)}, bf16[512,512]{1,0:T(8,128)(2,1)}, u32[]{:S(2)}) %copy-start.4) | copy-done | bytes 524312
  20.5 0.9 %copy-done.7 = bf16[227,512]{1,0:T(8,128)(2,1)S(1)} copy-done((bf16[227,512]{1,0:T(8,128)(2,1)S(1)}, bf16[227,512]{1,0:T(8,128)(2,1)}, u32[]{:S(2)}) %copy-start.7) | copy-done | bytes 232472
  21.4 5.5 %shard_map.177 = (bf16[1024,512]{1,0:T(8,128)(2,1)S(1)}, bf16[1024,512]{1,0:T(8,128)(2,1)S(1)}, f32[64,512]{1,0:T(8,128)S(1)}, bf16[32,512]{1,0:T(8,128)(2,1)S(1)}, bf16[32,512]{1,0:T(8,128)(2,1)S(1)}) custom-call(bf16[3,227,360]{2,1,0:T(8,128)(2,1)S(1)} %collective-permute-done.near, bf16[3,227,360]{2,1,0:T(8,128)(2,1)S(1)} %collective-permute-done.1.far, ...), custom_call_target="tpu_custom_call" | custom-call | tf_op jit(solution)/shard_map/pallas_call | solution.py:307
  27.0 1.6 %collective-permute-start.5 = (bf16[32,512]{1,0:T(8,128)(2,1)S(1)}, bf16[32,512]{1,0:T(8,128)(2,1)S(1)}, u32[]{:S(2)}, u32[]{:S(2)}) collective-permute-start(bf16[32,512]{1,0:T(8,128)(2,1)S(1)} %get-tuple-element.49), channel_id=1, source_target_pairs={{0,3},{1,2},{2,1},{3,0},{4,7},{5,6},{6,5},{7,4},{8,11},{9,10},{10,... | collective-permute-start | bytes 98312 | tf_op jit(solution)/shard_map/ppermute | solution.py:387
  28.6 1.8 %collective-permute-done.5.far = bf16[32,512]{1,0:T(8,128)(2,1)S(1)} collective-permute-done((bf16[32,512]{1,0:T(8,128)(2,1)S(1)}, bf16[32,512]{1,0:T(8,128)(2,1)S(1)}, u32[]{:S(2)}, u32[]{:S(2)}) %collective-permute-start.5) | collective-permute-done | bytes 32800 | tf_op jit(solution)/shard_map/ppermute | solution.py:387
  30.6 0.7 collective-permute-start.7
  31.3 3.5 %collective-permute-start.6 = (bf16[64,512]{1,0:T(8,128)(2,1)S(1)}, bf16[64,512]{1,0:T(8,128)(2,1)S(1)}, u32[]{:S(2)}, u32[]{:S(2)}) collective-permute-start(bf16[64,512]{1,0:T(8,128)(2,1)S(1)} %get-tuple-element.50.own), channel_id=1, source_target_pairs={{0,4},{4,0},{8,12},{12,8},{1,5},{5,1},{9,13},{13,9},{2,6},{6,2},{1... | collective-permute-start | bytes 196616 | tf_op jit(solution)/shard_map/ppermute | solution.py:395
  34.8 2.4 %collective-permute-done.6.near = bf16[64,512]{1,0:T(8,128)(2,1)S(1)} collective-permute-done((bf16[64,512]{1,0:T(8,128)(2,1)S(1)}, bf16[64,512]{1,0:T(8,128)(2,1)S(1)}, u32[]{:S(2)}, u32[]{:S(2)}) %collective-permute-start.6) | collective-permute-done | bytes 65568 | tf_op jit(solution)/shard_map/ppermute | solution.py:395
  37.3 2.0 %shard_map.179 = (bf16[32,512]{1,0:T(8,128)(2,1)}, f32[192,512]{1,0:T(8,128)S(1)}, bf16[32,512]{1,0:T(8,128)(2,1)S(1)}, bf16[64,512]{1,0:T(8,128)(2,1)S(1)}, bf16[64,512]{1,0:T(8,128)(2,1)S(1)}) custom-call(bf16[512,384]{1,0:T(8,128)(2,1)S(1)} %get-tuple-element.39.from_hits, bf16[512,64]{1,0:T(8,128)(2,1)S(1)} %get-tuple-element.40.to_hits, ...), custom_call_target="tpu_custom_call" | custom-call | tf_op jit(solution)/shard_map/pallas_call | solution.py:307
  39.3 1.9 %collective-permute-start.8 = (bf16[64,512]{1,0:T(8,128)(2,1)S(1)}, bf16[64,512]{1,0:T(8,128)(2,1)S(1)}, u32[]{:S(2)}, u32[]{:S(2)}) collective-permute-start(bf16[64,512]{1,0:T(8,128)(2,1)S(1)} %get-tuple-element.53), channel_id=1, source_target_pairs={{0,4},{4,0},{8,12},{12,8},{1,5},{5,1},{9,13},{13,9},{2,6},{6,2},{1... | collective-permute-start | bytes 196616 | tf_op jit(solution)/shard_map/ppermute | solution.py:409
  42.1 1.5 %collective-permute-done.8.after.near = bf16[64,512]{1,0:T(8,128)(2,1)S(1)} collective-permute-done((bf16[64,512]{1,0:T(8,128)(2,1)S(1)}, bf16[64,512]{1,0:T(8,128)(2,1)S(1)}, u32[]{:S(2)}, u32[]{:S(2)}) %collective-permute-start.8) | collective-permute-done | bytes 65568 | tf_op jit(solution)/shard_map/ppermute | solution.py:409
  44.3 1.6 %collective-permute-start.11 = (bf16[32,512]{1,0:T(8,128)(2,1)S(1)}, bf16[32,512]{1,0:T(8,128)(2,1)S(1)}, u32[]{:S(2)}, u32[]{:S(2)}) collective-permute-start(bf16[32,512]{1,0:T(8,128)(2,1)S(1)} %get-tuple-element.61), channel_id=1, source_target_pairs={{0,3},{1,2},{2,1},{3,0},{4,7},{5,6},{6,5},{7,4},{8,11},{9,10},{10,... | collective-permute-start | bytes 98312 | tf_op jit(solution)/shard_map/ppermute | solution.py:431
  46.0 1.7 %collective-permute-done.11.far = bf16[32,512]{1,0:T(8,128)(2,1)S(1)} collective-permute-done((bf16[32,512]{1,0:T(8,128)(2,1)S(1)}, bf16[32,512]{1,0:T(8,128)(2,1)S(1)}, u32[]{:S(2)}, u32[]{:S(2)}) %collective-permute-start.11) | collective-permute-done | bytes 32800 | tf_op jit(solution)/shard_map/ppermute | solution.py:431
  47.7 1.2 %shard_map.183 = (f32[2,512,128]{2,1,0:T(8,128)S(1)}, bf16[2,512,128]{2,1,0:T(8,128)(2,1)S(1)}) custom-call(bf16[1024,128]{1,0:T(8,128)(2,1)S(1)} %get-tuple-element.44.recv_hits, f32[64,512]{1,0:T(8,128)S(1)} %get-tuple-element.59.part, bf16[32,512]{1,0:T(8,128)(2,1)S(1)} %collective-permute-done.10.near, bf16[32,512]{1,0:T(8,128)(2,1)S(1)} %collective-permute-done.11.far, ...), custom_call_target="tpu_custom_call" | custom-call | tf_op jit(solution)/shard_map/pallas_call | solution.py:307
  49.5 1.6 %collective-permute-start.15 = (bf16[512,128]{1,0:T(8,128)(2,1)S(1)}, bf16[512,128]{1,0:T(8,128)(2,1)S(1)}, u32[]{:S(2)}, u32[]{:S(2)}) collective-permute-start(bf16[512,128]{1,0:T(8,128)(2,1)S(1)} %bitcast.6), channel_id=1, source_target_pairs={{0,2},{2,0},{1,3},{3,1},{4,6},{6,4},{5,7},{7,5},{8,10},{10,8},{9,1... | collective-permute-start | bytes 393224 | tf_op jit(solution)/shard_map/ppermute | solution.py:330
  51.1 1.1 %collective-permute-start.13 = (bf16[512,128]{1,0:T(8,128)(2,1)S(1)}, bf16[512,128]{1,0:T(8,128)(2,1)S(1)}, u32[]{:S(2)}, u32[]{:S(2)}) collective-permute-start(bf16[512,128]{1,0:T(8,128)(2,1)S(1)} %bitcast.7), channel_id=1, source_target_pairs={{0,2},{2,0},{1,3},{3,1},{4,6},{6,4},{5,7},{7,5},{8,10},{10,8},{9,1... | collective-permute-start | bytes 393224 | tf_op jit(solution)/shard_map/ppermute | solution.py:330
  52.3 3.7 %collective-permute-done.15.refs_3_ = bf16[512,128]{1,0:T(8,128)(2,1)S(1)} collective-permute-done((bf16[512,128]{1,0:T(8,128)(2,1)S(1)}, bf16[512,128]{1,0:T(8,128)(2,1)S(1)}, u32[]{:S(2)}, u32[]{:S(2)}) %collective-permute-start.15) | collective-permute-done | bytes 131104 | tf_op jit(solution)/shard_map/ppermute | solution.py:330
  56.0 1.9 %collective-permute-done.13.refs_1_ = bf16[512,128]{1,0:T(8,128)(2,1)S(1)} collective-permute-done((bf16[512,128]{1,0:T(8,128)(2,1)S(1)}, bf16[512,128]{1,0:T(8,128)(2,1)S(1)}, u32[]{:S(2)}, u32[]{:S(2)}) %collective-permute-start.13) | collective-permute-done | bytes 131104 | tf_op jit(solution)/shard_map/ppermute | solution.py:330
  57.9 13.9 %all_to_all.5.shares = bf16[4,2,128,128]{3,2,1,0:T(8,128)(2,1)S(1)} all-to-all(bf16[4,2,128,128]{3,2,1,0:T(8,128)(2,1)S(1)} %shard_map.186), channel_id=1, replica_groups=mesh['groups'=2,'band'=4,'dom'=2,'lat'=2] {'band'}, dimensions={0} | all-to-all | bytes 524288 | tf_op jit(solution)/shard_map/all_to_all | solution.py:458
  71.8 0.7 shard_map.187
  (42 shorter events, 3.3 us)
Async XLA Ops:
  0.6 29.8 %copy-start.2 = (bf16[512,512]{1,0:T(8,128)(2,1)S(1)}, bf16[512,512]{1,0:T(8,128)(2,1)}, u32[]{:S(2)}) copy-start(bf16[512,512]{1,0:T(8,128)(2,1)} %w_gn.3) | copy-start | bytes 1572868
  0.6 17.4 %collective-permute-start.1 = (bf16[3,227,360]{2,1,0:T(8,128)(2,1)}, bf16[3,227,360]{2,1,0:T(8,128)(2,1)S(1)}, u32[]{:S(2)}, u32[]{:S(2)}) collective-permute-start(bf16[3,227,360]{2,1,0:T(8,128)(2,1)} %bitcast.3), channel_id=1, source_target_pairs={{0,0},{4,8},{8,4},{12,12},{1,1},{5,9},{9,5},{13,13},{2,2},{6,10},{... | collective-permute-start | bytes 1470968 | tf_op jit(solution)/shard_map/ppermute | solution.py:351
  2.5 17.0 %collective-permute-start = (bf16[3,227,360]{2,1,0:T(8,128)(2,1)}, bf16[3,227,360]{2,1,0:T(8,128)(2,1)S(1)}, u32[]{:S(2)}, u32[]{:S(2)}) collective-permute-start(bf16[3,227,360]{2,1,0:T(8,128)(2,1)} %bitcast.4), channel_id=1, source_target_pairs={{0,4},{4,0},{8,12},{12,8},{1,5},{5,1},{9,13},{13,9},{2,6},{6,2},{1... | collective-permute-start | bytes 1470968 | tf_op jit(solution)/shard_map/ppermute | solution.py:352
  7.4 8.6 %collective-permute-start.3 = (bf16[32,512]{1,0:T(8,128)(2,1)}, bf16[32,512]{1,0:T(8,128)(2,1)S(1)}, u32[]{:S(2)}, u32[]{:S(2)}) collective-permute-start(bf16[32,512]{1,0:T(8,128)(2,1)} %mesh_in.3), channel_id=1, source_target_pairs={{0,3},{1,2},{2,1},{3,0},{4,7},{5,6},{6,5},{7,4},{8,11},{9,10},{10,... | collective-permute-start | bytes 98312 | tf_op jit(solution)/shard_map/ppermute | solution.py:353
  7.7 8.2 %collective-permute-start.2 = (bf16[32,512]{1,0:T(8,128)(2,1)}, bf16[32,512]{1,0:T(8,128)(2,1)S(1)}, u32[]{:S(2)}, u32[]{:S(2)}) collective-permute-start(bf16[32,512]{1,0:T(8,128)(2,1)} %mesh_in.3), channel_id=1, source_target_pairs={{0,1},{1,0},{2,3},{3,2},{4,5},{5,4},{6,7},{7,6},{8,9},{9,8},{10,11... | collective-permute-start | bytes 98312 | tf_op jit(solution)/shard_map/ppermute | solution.py:354
  10.3 1.0 %copy-start.3 = (bf16[3,360,227]{1,2,0:T(8,128)(2,1)S(1)}, bf16[3,360,227]{1,2,0:T(8,128)(2,1)}, u32[]{:S(2)}) copy-start(bf16[3,360,227]{1,2,0:T(8,128)(2,1)} %param.16) | copy-start | bytes 1470964
  11.3 0.7 copy-start.10
  12.0 0.7 copy-start.11
  12.7 0.7 copy-start.12
  13.4 0.7 copy-start.13
  15.9 21.3 %copy-start = (bf16[512,512]{1,0:T(8,128)(2,1)S(1)}, bf16[512,512]{1,0:T(8,128)(2,1)}, u32[]{:S(2)}) copy-start(bf16[512,512]{1,0:T(8,128)(2,1)} %w_mr.3) | copy-start | bytes 1572868
  15.9 21.3 %copy-start.1 = (bf16[512,512]{1,0:T(8,128)(2,1)S(1)}, bf16[512,512]{1,0:T(8,128)(2,1)}, u32[]{:S(2)}) copy-start(bf16[512,512]{1,0:T(8,128)(2,1)} %w_ms.3) | copy-start | bytes 1572868
  16.0 1.1 %copy-start.6 = (bf16[512,512]{1,0:T(8,128)(2,1)S(1)}, bf16[512,512]{1,0:T(8,128)(2,1)}, u32[]{:S(2)}) copy-start(bf16[512,512]{1,0:T(8,128)(2,1)} %w_gr.1) | copy-start | bytes 1572868
  17.1 0.8 %copy-start.9 = (bf16[32,512]{1,0:T(8,128)(2,1)S(1)}, bf16[32,512]{1,0:T(8,128)(2,1)}, u32[]{:S(2)}) copy-start(bf16[32,512]{1,0:T(8,128)(2,1)} %mesh_in.3) | copy-start | bytes 98308
  19.4 1.0 %copy-start.4 = (bf16[512,512]{1,0:T(8,128)(2,1)S(1)}, bf16[512,512]{1,0:T(8,128)(2,1)}, u32[]{:S(2)}) copy-start(bf16[512,512]{1,0:T(8,128)(2,1)} %w_gs.1) | copy-start | bytes 1572868
  20.5 0.9 %copy-start.7 = (bf16[227,512]{1,0:T(8,128)(2,1)S(1)}, bf16[227,512]{1,0:T(8,128)(2,1)}, u32[]{:S(2)}) copy-start(bf16[227,512]{1,0:T(8,128)(2,1)} %w_grid.1) | copy-start | bytes 697348
  21.4 15.8 %copy-start.5 = (bf16[512,512]{1,0:T(8,128)(2,1)S(1)}, bf16[512,512]{1,0:T(8,128)(2,1)}, u32[]{:S(2)}) copy-start(bf16[512,512]{1,0:T(8,128)(2,1)} %w_mn.1) | copy-start | bytes 1572868
  21.4 15.8 %copy-start.8 = (bf16[32,512]{1,0:T(8,128)(2,1)S(1)}, bf16[32,512]{1,0:T(8,128)(2,1)}, u32[]{:S(2)}) copy-start(bf16[32,512]{1,0:T(8,128)(2,1)} %d_out.3) | copy-start | bytes 98308
  26.9 1.7 %collective-permute-start.4 = (bf16[32,512]{1,0:T(8,128)(2,1)S(1)}, bf16[32,512]{1,0:T(8,128)(2,1)S(1)}, u32[]{:S(2)}, u32[]{:S(2)}) collective-permute-start(bf16[32,512]{1,0:T(8,128)(2,1)S(1)} %get-tuple-element.48), channel_id=1, source_target_pairs={{0,1},{1,0},{2,3},{3,2},{4,5},{5,4},{6,7},{7,6},{8,9},{9,8},{10,11... | collective-permute-start | bytes 98312 | tf_op jit(solution)/shard_map/ppermute | solution.py:388
  27.0 3.4 %collective-permute-start.5 = (bf16[32,512]{1,0:T(8,128)(2,1)S(1)}, bf16[32,512]{1,0:T(8,128)(2,1)S(1)}, u32[]{:S(2)}, u32[]{:S(2)}) collective-permute-start(bf16[32,512]{1,0:T(8,128)(2,1)S(1)} %get-tuple-element.49), channel_id=1, source_target_pairs={{0,3},{1,2},{2,1},{3,0},{4,7},{5,6},{6,5},{7,4},{8,11},{9,10},{10,... | collective-permute-start | bytes 98312 | tf_op jit(solution)/shard_map/ppermute | solution.py:387
  30.6 4.2 %collective-permute-start.7 = (bf16[64,512]{1,0:T(8,128)(2,1)S(1)}, bf16[64,512]{1,0:T(8,128)(2,1)S(1)}, u32[]{:S(2)}, u32[]{:S(2)}) collective-permute-start(bf16[64,512]{1,0:T(8,128)(2,1)S(1)} %get-tuple-element.50.own), channel_id=1, source_target_pairs={{0,0},{4,8},{8,4},{12,12},{1,1},{5,9},{9,5},{13,13},{2,2},{6,10},{... | collective-permute-start | bytes 196616 | tf_op jit(solution)/shard_map/ppermute | solution.py:394
  31.3 5.9 %collective-permute-start.6 = (bf16[64,512]{1,0:T(8,128)(2,1)S(1)}, bf16[64,512]{1,0:T(8,128)(2,1)S(1)}, u32[]{:S(2)}, u32[]{:S(2)}) collective-permute-start(bf16[64,512]{1,0:T(8,128)(2,1)S(1)} %get-tuple-element.50.own), channel_id=1, source_target_pairs={{0,4},{4,0},{8,12},{12,8},{1,5},{5,1},{9,13},{13,9},{2,6},{6,2},{1... | collective-permute-start | bytes 196616 | tf_op jit(solution)/shard_map/ppermute | solution.py:395
  39.3 4.3 %collective-permute-start.8 = (bf16[64,512]{1,0:T(8,128)(2,1)S(1)}, bf16[64,512]{1,0:T(8,128)(2,1)S(1)}, u32[]{:S(2)}, u32[]{:S(2)}) collective-permute-start(bf16[64,512]{1,0:T(8,128)(2,1)S(1)} %get-tuple-element.53), channel_id=1, source_target_pairs={{0,4},{4,0},{8,12},{12,8},{1,5},{5,1},{9,13},{13,9},{2,6},{6,2},{1... | collective-permute-start | bytes 196616 | tf_op jit(solution)/shard_map/ppermute | solution.py:409
  41.2 2.8 %collective-permute-start.9 = (bf16[64,512]{1,0:T(8,128)(2,1)S(1)}, bf16[64,512]{1,0:T(8,128)(2,1)S(1)}, u32[]{:S(2)}, u32[]{:S(2)}) collective-permute-start(bf16[64,512]{1,0:T(8,128)(2,1)S(1)} %get-tuple-element.56), channel_id=1, source_target_pairs={{0,0},{4,8},{8,4},{12,12},{1,1},{5,9},{9,5},{13,13},{2,2},{6,10},{... | collective-permute-start | bytes 196616 | tf_op jit(solution)/shard_map/ppermute | solution.py:408
  44.2 1.8 %collective-permute-start.10 = (bf16[32,512]{1,0:T(8,128)(2,1)S(1)}, bf16[32,512]{1,0:T(8,128)(2,1)S(1)}, u32[]{:S(2)}, u32[]{:S(2)}) collective-permute-start(bf16[32,512]{1,0:T(8,128)(2,1)S(1)} %get-tuple-element.60), channel_id=1, source_target_pairs={{0,1},{1,0},{2,3},{3,2},{4,5},{5,4},{6,7},{7,6},{8,9},{9,8},{10,11... | collective-permute-start | bytes 98312 | tf_op jit(solution)/shard_map/ppermute | solution.py:432
  44.3 3.4 %collective-permute-start.11 = (bf16[32,512]{1,0:T(8,128)(2,1)S(1)}, bf16[32,512]{1,0:T(8,128)(2,1)S(1)}, u32[]{:S(2)}, u32[]{:S(2)}) collective-permute-start(bf16[32,512]{1,0:T(8,128)(2,1)S(1)} %get-tuple-element.61), channel_id=1, source_target_pairs={{0,3},{1,2},{2,1},{3,0},{4,7},{5,6},{6,5},{7,4},{8,11},{9,10},{10,... | collective-permute-start | bytes 98312 | tf_op jit(solution)/shard_map/ppermute | solution.py:431
  45.9 3.6 %collective-permute-start.14 = (bf16[2,512,128]{2,1,0:T(8,128)(2,1)S(1)}, bf16[2,512,128]{2,1,0:T(8,128)(2,1)S(1)}, u32[]{:S(2)}, u32[]{:S(2)}) collective-permute-start(bf16[2,512,128]{2,1,0:T(8,128)(2,1)S(1)} %get-tuple-element.70), channel_id=1, source_target_pairs={{0,1},{1,0},{2,3},{3,2},{4,5},{5,4},{6,7},{7,6},{8,9},{9,8},{10,11... | collective-permute-start | bytes 786440 | tf_op jit(solution)/shard_map/ppermute | solution.py:330
  49.0 2.1 %collective-permute-start.12 = (bf16[2,512,128]{2,1,0:T(8,128)(2,1)S(1)}, bf16[2,512,128]{2,1,0:T(8,128)(2,1)S(1)}, u32[]{:S(2)}, u32[]{:S(2)}) collective-permute-start(bf16[2,512,128]{2,1,0:T(8,128)(2,1)S(1)} %get-tuple-element.66), channel_id=1, source_target_pairs={{0,1},{1,0},{2,3},{3,2},{4,5},{5,4},{6,7},{7,6},{8,9},{9,8},{10,11... | collective-permute-start | bytes 786440 | tf_op jit(solution)/shard_map/ppermute | solution.py:330
  49.5 6.4 %collective-permute-start.15 = (bf16[512,128]{1,0:T(8,128)(2,1)S(1)}, bf16[512,128]{1,0:T(8,128)(2,1)S(1)}, u32[]{:S(2)}, u32[]{:S(2)}) collective-permute-start(bf16[512,128]{1,0:T(8,128)(2,1)S(1)} %bitcast.6), channel_id=1, source_target_pairs={{0,2},{2,0},{1,3},{3,1},{4,6},{6,4},{5,7},{7,5},{8,10},{10,8},{9,1... | collective-permute-start | bytes 393224 | tf_op jit(solution)/shard_map/ppermute | solution.py:330
  51.1 6.7 %collective-permute-start.13 = (bf16[512,128]{1,0:T(8,128)(2,1)S(1)}, bf16[512,128]{1,0:T(8,128)(2,1)S(1)}, u32[]{:S(2)}, u32[]{:S(2)}) collective-permute-start(bf16[512,128]{1,0:T(8,128)(2,1)S(1)} %bitcast.7), channel_id=1, source_target_pairs={{0,2},{2,0},{1,3},{3,1},{4,6},{6,4},{5,7},{7,5},{8,10},{10,8},{9,1... | collective-permute-start | bytes 393224 | tf_op jit(solution)/shard_map/ppermute | solution.py:330

commit v5 on v4

--- a/solution.py
+++ b/solution.py
@@ -8,6 +8,7 @@
 F32 = jnp.float32
 BF16 = jnp.bfloat16
 LANES = 128
+FETCHED = 14
 
 
 def mm(a, b):
@@ -88,10 +89,23 @@
             )
 
 
-def index_kernel(
-    send, recv, count, mesh_send, mesh_recv, mesh_count, grid,
-    own_out, halo_hits, recv_hits, recv_rows, from_hits, to_hits, from_rows, to_rows, wide,
-):
+def index_kernel(count, mesh_count, *refs):
+    fetched, refs = refs[:FETCHED], refs[FETCHED:]
+    kept = refs[: FETCHED - 5]
+    (
+        own_out, recv_hits, recv_rows, from_hits, to_hits, from_rows, to_rows
+    ) = refs[FETCHED - 5 : FETCHED + 2]
+    halo_hits, wide, send, recv, mesh_send, mesh_recv, grid, sems = refs[FETCHED + 2 :]
+    copies = [
+        pltpu.make_async_copy(source, target, sems.at[i])
+        for i, (source, target) in enumerate(
+            zip(fetched, (send, recv, mesh_send, mesh_recv, grid) + tuple(kept))
+        )
+    ]
+    for copy in copies:
+        copy.start()
+    for copy in copies[:5]:
+        copy.wait()
     band_rows, _, cols = grid.shape
     pitch = wide.shape[1] // band_rows
     width = band_rows * pitch
@@ -99,18 +113,16 @@
     node_count = to_rows.shape[0]
     even_band = even_on("band")
     fill(wide, grid, pitch, 0)
-    below = jnp.where(even_band, width, 0)
-    above = jnp.where(even_band, -2 * width, -width)
+    near_base = jnp.where(even_band, 2 * width, 0)
+    far_base = jnp.where(even_band, 0, 2 * width)
     block = 256
     for first in range(0, send.shape[2], block):
         part_of = slice(first, first + block)
-        lane = spread(send[0, :, part_of], 3 * band_rows, cols, pitch)
-        inner = (lane >= width) & (lane < 2 * width)
-        index = columns(lane)
+        index = columns(spread(send[0, :, part_of], 3 * band_rows, cols, pitch))
         own_hit = hits_from(index, width, width, width)
         own_out[part_of] = mm_nt(own_hit, wide[...]).astype(BF16)
-        lane = jnp.where(lane < width, lane + below, jnp.where(inner, -1, lane + above))
-        halo_hits[part_of] = hits_from(columns(lane), 2 * width, 2 * width)
+        halo_hits[part_of, :width] = hits_from(index, width, width, near_base)
+        halo_hits[part_of, width:] = hits_from(index, width, width, far_base)
         target = live_only(recv[0, :, part_of], count[0, 0], first)
         recv_hits[part_of] = hits_from(columns(target), 2 * cycle, cycle)
         recv_rows[:, part_of] = hits_to(target, cycle)
@@ -124,6 +136,8 @@
     to_hits[...] = hits_from(columns(target), 2 * node_count, node_count)
     from_rows[...] = hits_to(source, 3 * cycle)
     to_rows[...] = hits_to(target, node_count)
+    for copy in copies[5:]:
+        copy.wait()
 
 
 def table_kernel(near, far, mesh_in, w_gr, table_out):
@@ -142,24 +156,19 @@
     near, far, halo_hits, recv_hits, recv_rows, own, table, w_grid, w_gs,
     senders_out, slope_out, part_out, near_out, far_out, wide,
 ):
-    band_rows = near.shape[0]
-    pitch = wide.shape[1] // (2 * band_rows)
     half = recv_rows.shape[0] // 2
+    width = wide.shape[1] // 2
+    pitch = width // near.shape[0]
     fill(wide, near, pitch, 0)
-    fill(wide, far, pitch, band_rows * pitch)
-    block = 256
-    sums = None
-    for first in range(0, own.shape[0], block):
-        part_of = slice(first, first + block)
-        raw = own[part_of] + mm_nt(halo_hits[part_of], wide[...]).astype(BF16)
-        latent, _ = silu_parts(mm(raw, w_grid[...]))
-        latent = latent.astype(BF16)
-        senders_out[part_of] = latent
-        pre = mm(latent, w_gs[...]) + mm(recv_hits[part_of], table[...])
-        value, slope = silu_parts(pre)
-        slope_out[part_of] = slope.astype(BF16)
-        part = mm(recv_rows[:, part_of], value.astype(BF16))
-        sums = part if sums is None else sums + part
+    fill(wide, far, pitch, width)
+    raw = own[...] + mm_nt(halo_hits[...], wide[...]).astype(BF16)
+    latent, _ = silu_parts(mm(raw, w_grid[...]))
+    latent = latent.astype(BF16)
+    senders_out[...] = latent
+    pre = mm(latent, w_gs[...]) + mm(recv_hits[...], table[...])
+    value, slope = silu_parts(pre)
+    slope_out[...] = slope.astype(BF16)
+    sums = mm(recv_rows[...], value.astype(BF16))
     part_out[...] = sums
     even = even_on("lat")
     near_out[...] = jnp.where(even, sums[half:], sums[:half]).astype(BF16)
@@ -278,30 +287,40 @@
             sends_out[shift - 1] = total.astype(BF16)
 
 
-def over_dom_kernel(*refs):
-    *ins, out = refs
-    half = len(ins) // 2
-    bands, _, rows, _ = out.shape
-    for k in range(2):
-        keep, *came = ins[k * half : (k + 1) * half]
-        total = keep[...]
+def over_dom_kernel(keep, *refs):
+    *came, out = refs
+    total = keep[...]
+    for part in came:
+        total = total + part[...].astype(F32)
+    rows = out.shape[1]
+    for band in range(out.shape[0]):
+        out[band] = total[band * rows : (band + 1) * rows].astype(BF16)
+
+
+def over_band_kernel(shares, out):
+    total = shares[0].astype(F32)
+    for band in range(1, shares.shape[0]):
+        total = total + shares[band].astype(F32)
+    out[...] = total
+
+
+def tiles_kernel(keep, *refs):
+    *came, out = refs
+    doms, _, _ = keep.shape
+    rows = out.shape[1]
+    for dom in range(doms):
+        total = keep[dom]
         for part in came:
-            total = total + part[...].astype(F32)
-        for band in range(bands):
-            out[band, k] = total[band * rows : (band + 1) * rows].astype(BF16)
-
-
-def over_band_kernel(shares, first_out, second_out):
-    for k, out in enumerate((first_out, second_out)):
-        total = shares[0, k].astype(F32)
-        for band in range(1, shares.shape[0]):
-            total = total + shares[band, k].astype(F32)
-        out[...] = total
-
-
-def call(kernel, outs, *args, scalars=(), scratch=()):
+            total = total + part[dom].astype(F32)
+        for band in range(out.shape[0] // doms):
+            out[band * doms + dom] = total[band * rows : (band + 1) * rows].astype(BF16)
+
+
+def call(kernel, outs, *args, scalars=(), fetched=(), scratch=()):
     in_specs = [
-        pl.BlockSpec(memory_space=pltpu.SMEM if i in scalars else pltpu.VMEM)
+        pl.BlockSpec(
+            memory_space=pltpu.SMEM if i in scalars else pltpu.HBM if i in fetched else pltpu.VMEM
+        )
         for i in range(len(args))
     ]
     return pl.pallas_call(
@@ -309,7 +328,7 @@
         out_shape=[jax.ShapeDtypeStruct(shape, dtype) for shape, dtype in outs],
         in_specs=in_specs,
         out_specs=[pl.BlockSpec(memory_space=pltpu.VMEM)] * len(outs),
-        scratch_shapes=[pltpu.VMEM(shape, dtype) for shape, dtype in scratch],
+        scratch_shapes=scratch,
         compiler_params=pltpu.CompilerParams(vmem_limit_bytes=16 << 20),
     )(*args)
 
@@ -347,28 +366,38 @@
 
     grid = jnp.transpose(grid_in, (0, 2, 1))
     pitch = -(-grid.shape[2] // LANES) * LANES
-    wide = (variables, grid.shape[0] * pitch)
+    band_rows = grid.shape[0]
+    width = band_rows * pitch
+    raw_near = lax.ppermute(grid, "band", band_near)
     raw_far = lax.ppermute(grid, "band", band_far)
-    raw_near = lax.ppermute(grid, "band", band_near)
-    mesh_far = lax.ppermute(mesh_in, around, ring_far)
-    mesh_near = lax.ppermute(mesh_in, around, ring_near)
     mesh_edges = mesh_send.shape[2]
-    own_rows, halo_hits, recv_hits, recv_rows, from_hits, to_hits, from_rows, to_rows = call(
+    weights = (w_grid, w_gs, w_gr, w_gn, w_ms, w_mr, w_mn, mesh_in, d_out)
+    inputs = (g2m_send, g2m_recv, mesh_send, mesh_recv, grid)
+    staged = call(
         index_kernel,
-        [
+        [(x.shape, x.dtype) for x in weights]
+        + [
             ((edges, variables), BF16),
-            ((edges, 2 * wide[1]), BF16),
             ((edges, 2 * cycle), BF16),
             ((cycle, edges), BF16),
             ((mesh_edges, 6 * cycle), BF16),
             ((mesh_edges, 2 * node_count), BF16),
             ((3 * cycle, mesh_edges), BF16),
             ((node_count, mesh_edges), BF16),
-        ],
-        g2m_send, g2m_recv, g2m_count, mesh_send, mesh_recv, mesh_count, grid,
-        scalars=(2, 5),
-        scratch=[(wide, BF16)],
-    )
+        ]
+        + [((edges, 2 * width), BF16)],
+        g2m_count, mesh_count, *inputs, *weights,
+        scalars=(0, 1),
+        fetched=range(2, 2 + FETCHED),
+        scratch=[pltpu.VMEM((variables, width), BF16)]
+        + [pltpu.VMEM(x.shape, x.dtype) for x in inputs]
+        + [pltpu.SemaphoreType.DMA((FETCHED,))],
+    )
+    w_grid, w_gs, w_gr, w_gn, w_ms, w_mr, w_mn, mesh_in, d_out = staged[:9]
+    rows, recv_hits, recv_rows, from_hits, to_hits, from_rows, to_rows = staged[9:16]
+    halo_hits = staged[16]
+    mesh_near = lax.ppermute(mesh_in, around, ring_near)
+    mesh_far = lax.ppermute(mesh_in, around, ring_far)
     (table,) = call(
         table_kernel, [((2 * cycle, latent), BF16)], mesh_near, mesh_far, mesh_in, w_gr
     )
@@ -381,18 +410,18 @@
             ((node_count, latent), BF16),
             ((node_count, latent), BF16),
         ],
-        raw_near, raw_far, halo_hits, recv_hits, recv_rows, own_rows, table, w_grid, w_gs,
-        scratch=[((variables, 2 * wide[1]), BF16)],
-    )
+        raw_near, raw_far, halo_hits, recv_hits, recv_rows, rows, table, w_grid, w_gs,
+        scratch=[pltpu.VMEM((variables, 2 * width), BF16)],
+    )
+    from_near = lax.ppermute(to_near, around, ring_near)
     from_far = lax.ppermute(to_far, around, ring_far)
-    from_near = lax.ppermute(to_near, around, ring_near)
     mesh_one, node_slope = call(
         node_kernel,
         [((cycle, latent), BF16), ((cycle, latent), F32)],
         part, from_near, from_far, mesh_near, mesh_far, mesh_in, w_gn,
     )
-    one_far = lax.ppermute(mesh_one, "band", band_far)
     one_near = lax.ppermute(mesh_one, "band", band_near)
+    one_far = lax.ppermute(mesh_one, "band", pairings(bands, True)[1])
     mesh_out, sums, recv_sum, to_near, to_far = call(
         process_kernel,
         [
@@ -405,8 +434,8 @@
         from_hits, to_hits, from_rows, to_rows, one_near, mesh_one, one_far, d_out,
         w_ms, w_mr, w_mn,
     )
+    from_near = lax.ppermute(to_near, "band", band_near)
     from_far = lax.ppermute(to_far, "band", band_far)
-    from_near = lax.ppermute(to_near, "band", band_near)
     doms = lax.axis_size("dom")
     lats = lax.axis_size("lat")
     cols = latent // sectors
@@ -428,37 +457,36 @@
         ],
         sums, from_near, from_far, home, w_ms,
     )
+    from_near = lax.ppermute(to_near, around, ring_near)
     from_far = lax.ppermute(to_far, around, ring_far)
-    from_near = lax.ppermute(to_near, around, ring_near)
-
-    def over_lat(keep, sends):
-        came = [
+
+    def over_lat(sends):
+        return [
             shifted(sends[i * doms : (i + 1) * doms], "lat", i + 1) for i in range(lats - 1)
         ]
-        keep, sends = call(
-            over_lat_kernel,
-            [((latent, cols), F32), ((doms - 1, latent, cols), BF16)],
-            keep, *came,
-        )
-        return [keep] + [shifted(sends[i], "dom", i + 1) for i in range(doms - 1)]
-
-    ms_parts = over_lat(*ms_halves)
-    gs_parts = over_lat(
-        *call(
-            encode_grad_kernel,
-            halves_shape,
-            recv_hits, part, from_near, from_far, node_slope, w_gn, senders, edge_slope,
-        )
-    )
-    (shares,) = call(
-        over_dom_kernel,
-        [((bands, 2, latent // bands, cols), BF16)],
-        *gs_parts, *ms_parts,
-    )
+
+    rows = latent // bands
+    ms_keep, ms_sends = ms_halves
+    (ms_tiles,) = call(
+        tiles_kernel, [((bands * doms, rows, cols), BF16)], ms_keep, *over_lat(ms_sends)
+    )
+    ms_tiles, from_near = lax.optimization_barrier((ms_tiles, from_near))
+    grad_ms = lax.psum_scatter(ms_tiles, ("band", "dom"), scatter_dimension=0, tiled=True)
+    gs_keep, gs_sends = call(
+        encode_grad_kernel,
+        halves_shape,
+        recv_hits, part, from_near, from_far, node_slope, w_gn, senders, edge_slope,
+    )
+    gs_keep, gs_sends = call(
+        over_lat_kernel,
+        [((latent, cols), F32), ((doms - 1, latent, cols), BF16)],
+        gs_keep, *over_lat(gs_sends),
+    )
+    gs_came = [shifted(gs_sends[i], "dom", i + 1) for i in range(doms - 1)]
+    (shares,) = call(over_dom_kernel, [((bands, rows, cols), BF16)], gs_keep, *gs_came)
     shares = lax.all_to_all(shares, "band", 0, 0, tiled=True)
-    tile = ((latent // bands, cols), F32)
-    grad_gs, grad_ms = call(over_band_kernel, [tile, tile], shares)
-    return mesh_out, grad_gs, grad_ms
+    (grad_gs,) = call(over_band_kernel, [((rows, cols), F32)], shares)
+    return mesh_out, grad_gs, grad_ms[0].astype(F32)
 
 
 def solution(mesh):

time: 73 us -> 132 us (1.81)
  waiting for transfers between devices: 14.5 us -> 66.7 us
  blocking collectives: 13.9 us -> 0 us
  between operations: 2.13 us -> 15.5 us
  local copies, waits for them, and re-layouts: 7.65 us -> 12.5 us
  Pallas kernels: 12.7 us -> 14.2 us
  other arithmetic: 0 us -> 1.39 us
    reduce_scatter x0 -> x1, waiting for transfers between devices: none -> 44.7 us  [on_device(): lax.psum_scatter(ms_tiles, ('band', 'dom'), scatter_dimension=0, tiled=True)]
    all_to_all x1 -> x0, blocking collectives: 13.9 us -> none  [on_device(): shares = lax.all_to_all(shares, 'band', 0, 0, tiled=True)]
    ppermute x1, waiting for transfers between devices: 0.01 us -> 5.36 us  [on_device(): one_far = lax.ppermute(mesh_one, 'band', pairings(bands, True)[1])]
    all_to_all x0 -> x1, starting transfers between devices: none -> 5.25 us  [on_device(): shares = lax.all_to_all(shares, 'band', 0, 0, tiled=True)]
    unnamed x28, local copies, waits for them, and re-layouts: 7.65 us -> 12.5 us
    ppermute x1, starting transfers between devices: 3.5 us -> 0.01 us  [on_device(): one_near = lax.ppermute(mesh_one, 'band', band_near)]
    ppermute x1, waiting for transfers between devices: 2.42 us -> 0.14 us  [on_device(): one_near = lax.ppermute(mesh_one, 'band', band_near)]
    ppermute x1, waiting for transfers between devices: 0.01 us -> 2.04 us  [on_device(): mesh_far = lax.ppermute(mesh_in, around, ring_far)]
  transfers between devices with their start and end apart: 16 -> 17, of which waited for: 7 -> 10; matrix products, arithmetic and copies ran while one was open for 0% -> 1% of each run, Pallas kernels for 5% -> 5%
where the time goes in v5:
time: 132 us; the launch traced here: 131 us
  waiting for transfers between devices  66.7 us (51%)
  starting transfers between devices  20.4 us (15%)
  between operations  15.5 us (12%)
  Pallas kernels  14.2 us (11%)
  local copies, waits for them, and re-layouts  12.5 us (9%)
  other arithmetic  1.39 us (1%)
    reduce_scatter x1, waiting for transfers between devices, on_device(): lax.psum_scatter(ms_tiles, ('band', 'dom'), scatter_dimension=0, tiled=True)  44.7 us
    pallas_call x13, Pallas kernels, call(): pl.pallas_call(kernel, out_shape=[jax.ShapeDtypeStruct(shape, dtype) for...  14.2 us
    unnamed x28, local copies, waits for them, and re-layouts  12.5 us
    ppermute x3, waiting for transfers between devices, shifted(): lax.ppermute(x, axis, [(i, (i + shift) % count) for i in range(count)])  6.5 us
    ppermute x1, waiting for transfers between devices, on_device(): one_far = lax.ppermute(mesh_one, 'band', pairings(bands, True)[1])  5.36 us
    all_to_all x1, starting transfers between devices, on_device(): shares = lax.all_to_all(shares, 'band', 0, 0, tiled=True)  5.25 us
    ppermute x1, starting transfers between devices, on_device(): raw_near = lax.ppermute(grid, 'band', band_near)  4.88 us
    ppermute x2, waiting for transfers between devices, on_device(): from_far = lax.ppermute(to_far, around, ring_far)  4.61 us
  transfers between devices with their start and end apart: 17, of which 10 were waited for; matrix products, arithmetic and copies ran while one was open for 1% of the time, Pallas kernels for 5%

profile of v5, /device:TPU:0, one launch (start us, length us, event | category | flops | bytes accessed | tf_op | source)
XLA Modules:
  0.0 130.7 jit_solution(12220637132860534060)
XLA Ops:
  7.2 1.7 %collective-permute-start.1 = (bf16[3,227,360]{2,1,0:T(8,128)(2,1)}, bf16[3,227,360]{2,1,0:T(8,128)(2,1)S(1)}, u32[]{:S(2)}, u32[]{:S(2)}) collective-permute-start(bf16[3,227,360]{2,1,0:T(8,128)(2,1)} %bitcast.5), channel_id=1, source_target_pairs={{0,0},{4,8},{8,4},{12,12},{1,1},{5,9},{9,5},{13,13},{2,2},{6,10},{... | collective-permute-start | bytes 1470968 | tf_op jit(solution)/shard_map/ppermute | solution.py:372
  8.9 4.9 %collective-permute-start = (bf16[3,227,360]{2,1,0:T(8,128)(2,1)}, bf16[3,227,360]{2,1,0:T(8,128)(2,1)S(1)}, u32[]{:S(2)}, u32[]{:S(2)}) collective-permute-start(bf16[3,227,360]{2,1,0:T(8,128)(2,1)} %bitcast.6), channel_id=1, source_target_pairs={{0,4},{4,0},{8,12},{12,8},{1,5},{5,1},{9,13},{13,9},{2,6},{6,2},{1... | collective-permute-start | bytes 1470968 | tf_op jit(solution)/shard_map/ppermute | solution.py:371
  15.1 1.0 copy-done
  16.1 1.0 copy-done.1
  17.2 1.0 copy-done.2
  18.2 1.0 copy-done.3
  19.3 1.0 copy-done.4
  20.3 1.0 copy-done.5
  21.3 1.0 copy-done.6
  22.4 0.9 copy-done.7
  23.3 0.8 copy-done.8
  24.1 0.8 copy-done.9
  27.6 2.5 %shard_map.175 = (bf16[227,512]{1,0:T(8,128)(2,1)S(1)}, bf16[512,512]{1,0:T(8,128)(2,1)S(1)}, bf16[512,512]{1,0:T(8,128)(2,1)S(1)}, bf16[512,512]{1,0:T(8,128)(2...) custom-call(s32[1,1]{1,0:T(1,128)S(6)} %copy.19.count, ...), custom_call_target="tpu_custom_call" | custom-call | tf_op jit(solution)/shard_map/pallas_call | solution.py:326
  30.5 1.2 collective-permute-start.2
  31.8 2.0 %collective-permute-done.3.far.mesh_far = bf16[32,512]{1,0:T(8,128)(2,1)S(1)} collective-permute-done((bf16[32,512]{1,0:T(8,128)(2,1)S(1)}, bf16[32,512]{1,0:T(8,128)(2,1)S(1)}, u32[]{:S(2)}, u32[]{:S(2)}) %collective-permute-start.3) | collective-permute-done | bytes 32800 | tf_op jit(solution)/shard_map/ppermute | solution.py:400
  34.1 5.1 %shard_map.177 = (bf16[1024,512]{1,0:T(8,128)(2,1)S(1)}, bf16[1024,512]{1,0:T(8,128)(2,1)S(1)}, f32[64,512]{1,0:T(8,128)S(1)}, bf16[32,512]{1,0:T(8,128)(2,1)S(1)}, bf16[32,512]{1,0:T(8,128)(2,1)S(1)}) custom-call(bf16[3,227,360]{2,1,0:T(8,128)(2,1)S(1)} %collective-permute-done.near, bf16[3,227,360]{2,1,0:T(8,128)(2,1)S(1)} %collective-permute-done.1.far, ...), custom_call_target="tpu_custom_call" | custom-call | tf_op jit(solution)/shard_map/pallas_call | solution.py:326
  39.3 1.2 collective-permute-start.5
  40.5 2.2 %collective-permute-done.5.far = bf16[32,512]{1,0:T(8,128)(2,1)S(1)} collective-permute-done((bf16[32,512]{1,0:T(8,128)(2,1)S(1)}, bf16[32,512]{1,0:T(8,128)(2,1)S(1)}, u32[]{:S(2)}, u32[]{:S(2)}) %collective-permute-start.5) | collective-permute-done | bytes 32800 | tf_op jit(solution)/shard_map/ppermute | solution.py:417
  42.9 1.4 %collective-permute-start.7 = (bf16[64,512]{1,0:T(8,128)(2,1)S(1)}, bf16[64,512]{1,0:T(8,128)(2,1)S(1)}, u32[]{:S(2)}, u32[]{:S(2)}) collective-permute-start(bf16[64,512]{1,0:T(8,128)(2,1)S(1)} %get-tuple-element.62.own), channel_id=1, source_target_pairs={{0,12},{4,8},{8,4},{12,0},{1,13},{5,9},{9,5},{13,1},{2,14},{6,10},... | collective-permute-start | bytes 196616 | tf_op jit(solution)/shard_map/ppermute | solution.py:424
  44.4 5.4 %collective-permute-done.7.far = bf16[64,512]{1,0:T(8,128)(2,1)S(1)} collective-permute-done((bf16[64,512]{1,0:T(8,128)(2,1)S(1)}, bf16[64,512]{1,0:T(8,128)(2,1)S(1)}, u32[]{:S(2)}, u32[]{:S(2)}) %collective-permute-start.7) | collective-permute-done | bytes 65568 | tf_op jit(solution)/shard_map/ppermute | solution.py:424
  49.8 2.0 %shard_map.179 = (bf16[32,512]{1,0:T(8,128)(2,1)}, f32[192,512]{1,0:T(8,128)S(1)}, bf16[32,512]{1,0:T(8,128)(2,1)S(1)}, bf16[64,512]{1,0:T(8,128)(2,1)S(1)}, bf16[64,512]{1,0:T(8,128)(2,1)S(1)}) custom-call(bf16[512,384]{1,0:T(8,128)(2,1)S(1)} %get-tuple-element.46.from_hits, bf16[512,64]{1,0:T(8,128)(2,1)S(1)} %get-tuple-element.47.to_hits, ...), custom_call_target="tpu_custom_call" | custom-call | tf_op jit(solution)/shard_map/pallas_call | solution.py:326
  52.8 3.4 %collective-permute-done.8.after.near = bf16[64,512]{1,0:T(8,128)(2,1)S(1)} collective-permute-done((bf16[64,512]{1,0:T(8,128)(2,1)S(1)}, bf16[64,512]{1,0:T(8,128)(2,1)S(1)}, u32[]{:S(2)}, u32[]{:S(2)}) %collective-permute-start.8) | collective-permute-done | bytes 65568 | tf_op jit(solution)/shard_map/ppermute | solution.py:437
  58.1 0.7 shard_map.183
  58.9 1.0 collective-permute-start.12
  59.9 2.4 %collective-permute-done.12.far = bf16[32,512]{1,0:T(8,128)(2,1)S(1)} collective-permute-done((bf16[32,512]{1,0:T(8,128)(2,1)S(1)}, bf16[32,512]{1,0:T(8,128)(2,1)S(1)}, u32[]{:S(2)}, u32[]{:S(2)}) %collective-permute-start.12) | collective-permute-done | bytes 32800 | tf_op jit(solution)/shard_map/ppermute | solution.py:461
  62.3 1.2 shard_map.184
  63.8 1.4 %collective-permute-done.13.refs_1_ = bf16[2,512,128]{2,1,0:T(8,128)(2,1)S(1)} collective-permute-done((bf16[2,512,128]{2,1,0:T(8,128)(2,1)S(1)}, bf16[2,512,128]{2,1,0:T(8,128)(2,1)S(1)}, u32[]{:S(2)}, u32[]{:S(2)}) %collective-permute-start.13) | collective-permute-done | bytes 262176 | tf_op jit(solution)/shard_map/ppermute | solution.py:349
  65.2 1.3 collective-permute-start.14
  66.5 4.7 %collective-permute-done.14.refs_0_ = bf16[512,128]{1,0:T(8,128)(2,1)S(1)} collective-permute-done((bf16[512,128]{1,0:T(8,128)(2,1)S(1)}, bf16[512,128]{1,0:T(8,128)(2,1)S(1)}, u32[]{:S(2)}, u32[]{:S(2)}) %collective-permute-start.14) | collective-permute-done | bytes 131104 | tf_op jit(solution)/shard_map/ppermute | solution.py:349
  71.9 5.3 %all-to-all-start = ((bf16[4,128,128]{2,1,0:T(8,128)(2,1)}), bf16[4,128,128]{2,1,0:T(8,128)(2,1)S(1)}, u32[]{:S(2)}, u32[]{:S(2)}) async-start(bf16[4,128,128]{2,1,0:T(8,128)(2,1)} %shard_map.186), calls=%async_computation | async-start | bytes 262144 | tf_op jit(solution)/shard_map/all_to_all | solution.py:487
  77.1 44.7 %reduce-scatter.2.cloned.1.call-done = bf16[1,128,128]{2,1,0:T(8,128)(2,1)} async-done(((bf16[8,128,128]{2,1,0:T(8,128)(2,1)}), bf16[1,128,128]{2,1,0:T(8,128)(2,1)}) %reduce-scatter.2.cloned.1.call-update) | async-done | bytes 32784 | tf_op jit(solution)/shard_map/reduce_scatter | solution.py:474
  121.8 1.4 %bitcast_convert_fusion = f32[128,128]{1,0:T(8,128)} fusion(bf16[1,128,128]{2,1,0:T(8,128)(2,1)} %reduce-scatter.2.cloned.1.call-done), kind=kLoop, calls=%fused_computation | loop fusion | flops 16384 | bytes 98304 | tf_op jit(solution)/shard_map/convert_element_type | solution.py:489
  (45 shorter events, 8.5 us)
Async XLA Ops:
  7.2 114.6 %reduce-scatter.2.cloned.1.call-start = ((), (), s32[]{:S(2)}) async-start(), calls=%async_computation.2 | async-start | bytes 294912 | tf_op jit(solution)/shard_map/reduce_scatter | solution.py:474
  7.2 26.8 %collective-permute-start.1 = (bf16[3,227,360]{2,1,0:T(8,128)(2,1)}, bf16[3,227,360]{2,1,0:T(8,128)(2,1)S(1)}, u32[]{:S(2)}, u32[]{:S(2)}) collective-permute-start(bf16[3,227,360]{2,1,0:T(8,128)(2,1)} %bitcast.5), channel_id=1, source_target_pairs={{0,0},{4,8},{8,4},{12,12},{1,1},{5,9},{9,5},{13,13},{2,2},{6,10},{... | collective-permute-start | bytes 1470968 | tf_op jit(solution)/shard_map/ppermute | solution.py:372
  8.9 25.1 %collective-permute-start = (bf16[3,227,360]{2,1,0:T(8,128)(2,1)}, bf16[3,227,360]{2,1,0:T(8,128)(2,1)S(1)}, u32[]{:S(2)}, u32[]{:S(2)}) collective-permute-start(bf16[3,227,360]{2,1,0:T(8,128)(2,1)} %bitcast.6), channel_id=1, source_target_pairs={{0,4},{4,0},{8,12},{12,8},{1,5},{5,1},{9,13},{13,9},{2,6},{6,2},{1... | collective-permute-start | bytes 1470968 | tf_op jit(solution)/shard_map/ppermute | solution.py:371
  15.1 1.0 copy-start
  16.1 1.0 copy-start.1
  17.2 1.0 copy-start.2
  18.2 1.0 copy-start.3
  19.3 1.0 copy-start.4
  20.3 1.0 copy-start.5
  21.3 1.0 copy-start.6
  22.4 0.9 copy-start.7
  23.3 0.8 copy-start.8
  24.1 0.8 copy-start.9
  24.8 0.7 copy-start.10
  25.5 0.7 copy-start.11
  26.2 0.7 copy-start.12
  26.9 0.7 copy-start.13
  30.1 3.7 %collective-permute-start.3 = (bf16[32,512]{1,0:T(8,128)(2,1)S(1)}, bf16[32,512]{1,0:T(8,128)(2,1)S(1)}, u32[]{:S(2)}, u32[]{:S(2)}) collective-permute-start(bf16[32,512]{1,0:T(8,128)(2,1)S(1)} %get-tuple-element.54.mesh_in), channel_id=1, source_target_pairs={{0,3},{1,2},{2,1},{3,0},{4,7},{5,6},{6,5},{7,4},{8,11},{9,10},{10,... | collective-permute-start | bytes 98312 | tf_op jit(solution)/shard_map/ppermute | solution.py:400
  30.5 3.3 %collective-permute-start.2 = (bf16[32,512]{1,0:T(8,128)(2,1)S(1)}, bf16[32,512]{1,0:T(8,128)(2,1)S(1)}, u32[]{:S(2)}, u32[]{:S(2)}) collective-permute-start(bf16[32,512]{1,0:T(8,128)(2,1)S(1)} %get-tuple-element.54.mesh_in), channel_id=1, source_target_pairs={{0,1},{1,0},{2,3},{3,2},{4,5},{5,4},{6,7},{7,6},{8,9},{9,8},{10,11... | collective-permute-start | bytes 98312 | tf_op jit(solution)/shard_map/ppermute | solution.py:399
  39.1 1.4 %collective-permute-start.4 = (bf16[32,512]{1,0:T(8,128)(2,1)S(1)}, bf16[32,512]{1,0:T(8,128)(2,1)S(1)}, u32[]{:S(2)}, u32[]{:S(2)}) collective-permute-start(bf16[32,512]{1,0:T(8,128)(2,1)S(1)} %get-tuple-element.59), channel_id=1, source_target_pairs={{0,1},{1,0},{2,3},{3,2},{4,5},{5,4},{6,7},{7,6},{8,9},{9,8},{10,11... | collective-permute-start | bytes 98312 | tf_op jit(solution)/shard_map/ppermute | solution.py:416
  39.3 3.4 %collective-permute-start.5 = (bf16[32,512]{1,0:T(8,128)(2,1)S(1)}, bf16[32,512]{1,0:T(8,128)(2,1)S(1)}, u32[]{:S(2)}, u32[]{:S(2)}) collective-permute-start(bf16[32,512]{1,0:T(8,128)(2,1)S(1)} %get-tuple-element.60), channel_id=1, source_target_pairs={{0,3},{1,2},{2,1},{3,0},{4,7},{5,6},{6,5},{7,4},{8,11},{9,10},{10,... | collective-permute-start | bytes 98312 | tf_op jit(solution)/shard_map/ppermute | solution.py:417
  42.9 6.8 %collective-permute-start.7 = (bf16[64,512]{1,0:T(8,128)(2,1)S(1)}, bf16[64,512]{1,0:T(8,128)(2,1)S(1)}, u32[]{:S(2)}, u32[]{:S(2)}) collective-permute-start(bf16[64,512]{1,0:T(8,128)(2,1)S(1)} %get-tuple-element.62.own), channel_id=1, source_target_pairs={{0,12},{4,8},{8,4},{12,0},{1,13},{5,9},{9,5},{13,1},{2,14},{6,10},... | collective-permute-start | bytes 196616 | tf_op jit(solution)/shard_map/ppermute | solution.py:424
  44.3 5.5 %collective-permute-start.6 = (bf16[64,512]{1,0:T(8,128)(2,1)S(1)}, bf16[64,512]{1,0:T(8,128)(2,1)S(1)}, u32[]{:S(2)}, u32[]{:S(2)}) collective-permute-start(bf16[64,512]{1,0:T(8,128)(2,1)S(1)} %get-tuple-element.62.own), channel_id=1, source_target_pairs={{0,4},{4,0},{8,12},{12,8},{1,5},{5,1},{9,13},{13,9},{2,6},{6,2},{1... | collective-permute-start | bytes 196616 | tf_op jit(solution)/shard_map/ppermute | solution.py:423
  51.8 4.3 %collective-permute-start.8 = (bf16[64,512]{1,0:T(8,128)(2,1)S(1)}, bf16[64,512]{1,0:T(8,128)(2,1)S(1)}, u32[]{:S(2)}, u32[]{:S(2)}) collective-permute-start(bf16[64,512]{1,0:T(8,128)(2,1)S(1)} %get-tuple-element.69), channel_id=1, source_target_pairs={{0,4},{4,0},{8,12},{12,8},{1,5},{5,1},{9,13},{13,9},{2,6},{6,2},{1... | collective-permute-start | bytes 196616 | tf_op jit(solution)/shard_map/ppermute | solution.py:437
  52.1 4.4 %collective-permute-start.9 = (bf16[64,512]{1,0:T(8,128)(2,1)S(1)}, bf16[64,512]{1,0:T(8,128)(2,1)S(1)}, u32[]{:S(2)}, u32[]{:S(2)}) collective-permute-start(bf16[64,512]{1,0:T(8,128)(2,1)S(1)} %get-tuple-element.72), channel_id=1, source_target_pairs={{0,0},{4,8},{8,4},{12,12},{1,1},{5,9},{9,5},{13,13},{2,2},{6,10},{... | collective-permute-start | bytes 196616 | tf_op jit(solution)/shard_map/ppermute | solution.py:438
  56.5 1.6 %collective-permute-start.10 = (bf16[2,512,128]{2,1,0:T(8,128)(2,1)S(1)}, bf16[2,512,128]{2,1,0:T(8,128)(2,1)S(1)}, u32[]{:S(2)}, u32[]{:S(2)}) collective-permute-start(bf16[2,512,128]{2,1,0:T(8,128)(2,1)S(1)} %get-tuple-element.77), channel_id=1, source_target_pairs={{0,1},{1,0},{2,3},{3,2},{4,5},{5,4},{6,7},{7,6},{8,9},{9,8},{10,11... | collective-permute-start | bytes 786440 | tf_op jit(solution)/shard_map/ppermute | solution.py:349
  57.1 1.7 %collective-permute-start.11 = (bf16[32,512]{1,0:T(8,128)(2,1)S(1)}, bf16[32,512]{1,0:T(8,128)(2,1)S(1)}, u32[]{:S(2)}, u32[]{:S(2)}) collective-permute-start(bf16[32,512]{1,0:T(8,128)(2,1)S(1)} %get-tuple-element.78), channel_id=1, source_target_pairs={{0,1},{1,0},{2,3},{3,2},{4,5},{5,4},{6,7},{7,6},{8,9},{9,8},{10,11... | collective-permute-start | bytes 98312 | tf_op jit(solution)/shard_map/ppermute | solution.py:460
  58.9 3.4 %collective-permute-start.12 = (bf16[32,512]{1,0:T(8,128)(2,1)S(1)}, bf16[32,512]{1,0:T(8,128)(2,1)S(1)}, u32[]{:S(2)}, u32[]{:S(2)}) collective-permute-start(bf16[32,512]{1,0:T(8,128)(2,1)S(1)} %get-tuple-element.80), channel_id=1, source_target_pairs={{0,3},{1,2},{2,1},{3,0},{4,7},{5,6},{6,5},{7,4},{8,11},{9,10},{10,... | collective-permute-start | bytes 98312 | tf_op jit(solution)/shard_map/ppermute | solution.py:461
  63.6 1.6 %collective-permute-start.13 = (bf16[2,512,128]{2,1,0:T(8,128)(2,1)S(1)}, bf16[2,512,128]{2,1,0:T(8,128)(2,1)S(1)}, u32[]{:S(2)}, u32[]{:S(2)}) collective-permute-start(bf16[2,512,128]{2,1,0:T(8,128)(2,1)S(1)} %get-tuple-element.85), channel_id=1, source_target_pairs={{0,1},{1,0},{2,3},{3,2},{4,5},{5,4},{6,7},{7,6},{8,9},{9,8},{10,11... | collective-permute-start | bytes 786440 | tf_op jit(solution)/shard_map/ppermute | solution.py:349
  65.2 6.0 %collective-permute-start.14 = (bf16[512,128]{1,0:T(8,128)(2,1)S(1)}, bf16[512,128]{1,0:T(8,128)(2,1)S(1)}, u32[]{:S(2)}, u32[]{:S(2)}) collective-permute-start(bf16[512,128]{1,0:T(8,128)(2,1)S(1)} %bitcast.8), channel_id=1, source_target_pairs={{0,2},{2,0},{1,3},{3,1},{4,6},{6,4},{5,7},{7,5},{8,10},{10,8},{9,1... | collective-permute-start | bytes 393224 | tf_op jit(solution)/shard_map/ppermute | solution.py:349
  71.9 51.3 %all-to-all-start = ((bf16[4,128,128]{2,1,0:T(8,128)(2,1)}), bf16[4,128,128]{2,1,0:T(8,128)(2,1)S(1)}, u32[]{:S(2)}, u32[]{:S(2)}) async-start(bf16[4,128,128]{2,1,0:T(8,128)(2,1)} %shard_map.186), calls=%async_computation | async-start | bytes 262144 | tf_op jit(solution)/shard_map/all_to_all | solution.py:487
Sparse Core Ops, SparseCore 0:
  59.0 62.7 reduce-scatter.1

commit v6 on v5

--- a/solution.py
+++ b/solution.py
@@ -239,87 +239,89 @@
     home_out[...] = mm_nt(recv_sum[...], w_mr[...]) + d_out[...].astype(F32)
 
 
-def process_grad_kernel(near, own, far, sums, after, keep, sends):
-    block = jnp.concatenate([near[...], own[...], far[...]], axis=0)
-    split_store(mm_tn(block, sums[...].astype(BF16)), keep, sends)
-
-
-def cotangent_kernel(sums, near, far, home, w_ms, part_out, near_out, far_out):
+def cotangent_kernel(sums, near, far, home, part_out, near_out, far_out):
     cycle = near.shape[0]
     half = cycle // 2
     rim = half // 2
     total = sums[cycle : 2 * cycle] + near[...].astype(F32) + far[...].astype(F32)
-    back = mm_nt(total.astype(BF16), w_ms[...])
-    back = jnp.concatenate(
-        [back[:rim], back[rim : rim + half] + home[...], back[rim + half :]], axis=0
-    )
-    part_out[...] = back
+    part_out[...] = total
     even = even_on("lat")
-    near_out[...] = jnp.where(even, back[half:], back[:half]).astype(BF16)
-    far_out[...] = jnp.where(even, back[:half], back[half:]).astype(BF16)
+    near_out[:half] = jnp.where(even, total[half:], total[:half]).astype(BF16)
+    near_out[half:] = jnp.where(even, home[rim:], home[:rim]).astype(BF16)
+    far_out[:half] = jnp.where(even, total[:half], total[half:]).astype(BF16)
+    far_out[half:] = jnp.where(even, home[:rim], home[rim:]).astype(BF16)
 
 
 def encode_grad_kernel(
-    recv_hits, part, near, far, node_slope, w_gn, senders, edge_slope, keep, sends
+    recv_hits, part, near, far, home, node_slope, w_ms, w_gn, senders, edge_slope,
+    keep, sends, total_out,
 ):
+    half = part.shape[0] // 2
     even = even_on("lat")
     left = jnp.where(even, far[...], near[...]).astype(F32)
     right = jnp.where(even, near[...], far[...]).astype(F32)
-    cot = part[...] + jnp.concatenate([left, right], axis=0)
+    total = part[...] + jnp.concatenate([left[:half], right[:half]], axis=0)
+    total = total.astype(BF16)
+    rest = jnp.concatenate([left[half:], home[...], right[half:]], axis=0)
+    cot = rest + mm_nt(total, w_ms[...])
     gate_one = (cot * node_slope[...]).astype(BF16)
     back = jnp.concatenate(halves(mm_nt(gate_one, w_gn[...])), axis=0)
     slope = (mm(recv_hits[...], back) * edge_slope[...].astype(F32)).astype(BF16)
     split_store(mm_tn(senders[...], slope), keep, sends)
-
-
-def over_lat_kernel(*refs):
-    keep, *came, keep_out, sends_out = refs
-    doms = keep.shape[0]
+    doms, _, cols = total_out.shape
+    lats = total.shape[1] // cols // doms
+    me = lax.axis_index("lat")
+    for dom in range(doms):
+        pick = total[:, dom * lats * cols : (dom * lats + 1) * cols]
+        for i in range(1, lats):
+            at = (dom * lats + i) * cols
+            pick = jnp.where(me == i, total[:, at : at + cols], pick)
+        total_out[dom] = pick
+
+
+def over_lat_kernel(keep, total, *refs):
+    *came, keep_out, sends_out = refs
+    doms, rows, _ = keep.shape
     me = lax.axis_index("dom")
     for shift in range(doms):
         at = lax.rem(me + shift, doms)
-        total = keep[at]
+        block = keep[at]
         for part in came:
-            total = total + part[at].astype(F32)
+            block = block + part[at].astype(F32)
         if shift == 0:
-            keep_out[...] = total
+            keep_out[...] = block
         else:
-            sends_out[shift - 1] = total.astype(BF16)
-
-
-def over_dom_kernel(keep, *refs):
+            sends_out[shift - 1, :rows] = block.astype(BF16)
+            sends_out[shift - 1, rows:] = total[at]
+
+
+def over_dom_kernel(keep, total, nodes, *refs):
     *came, out = refs
-    total = keep[...]
-    for part in came:
-        total = total + part[...].astype(F32)
-    rows = out.shape[1]
-    for band in range(out.shape[0]):
-        out[band] = total[band * rows : (band + 1) * rows].astype(BF16)
-
-
-def over_band_kernel(shares, out):
-    total = shares[0].astype(F32)
-    for band in range(1, shares.shape[0]):
-        total = total + shares[band].astype(F32)
-    out[...] = total
-
-
-def tiles_kernel(keep, *refs):
-    *came, out = refs
-    doms, _, _ = keep.shape
-    rows = out.shape[1]
-    for dom in range(doms):
-        total = keep[dom]
-        for part in came:
-            total = total + part[dom].astype(F32)
-        for band in range(out.shape[0] // doms):
-            out[band * doms + dom] = total[band * rows : (band + 1) * rows].astype(BF16)
+    bands, _, rows, _ = out.shape
+    latent = keep.shape[0]
+    came, came_nodes = came[: len(came) // 2], came[len(came) // 2 :]
+    first = keep[...]
+    second = mm_tn(nodes[...], total[lax.axis_index("dom")])
+    for part, part_nodes in zip(came, came_nodes):
+        first = first + part[:latent].astype(F32)
+        second = second + mm_tn(part_nodes[...], part[latent:])
+    for k, block in enumerate((first, second)):
+        for band in range(bands):
+            out[band, k] = block[band * rows : (band + 1) * rows].astype(BF16)
+
+
+def over_band_kernel(shares, first_out, second_out):
+    for k, out in enumerate((first_out, second_out)):
+        total = shares[0, k].astype(F32)
+        for band in range(1, shares.shape[0]):
+            total = total + shares[band, k].astype(F32)
+        out[...] = total
 
 
 def call(kernel, outs, *args, scalars=(), fetched=(), scratch=()):
     in_specs = [
         pl.BlockSpec(
-            memory_space=pltpu.SMEM if i in scalars else pltpu.HBM if i in fetched else pltpu.VMEM
+            memory_space=pltpu.SMEM if i in scalars else pl.ANY if i in fetched else pltpu.VMEM
         )
         for i in range(len(args))
     ]
@@ -333,15 +335,24 @@
     )(*args)
 
 
-def pairings(count, closed):
-    near = [(i, i ^ 1) for i in range(count)]
+def ring_pairings(count):
+    far = [(i, (i + 1 if i % 2 else i - 1) % count) for i in range(count)]
+    return [(i, i ^ 1) for i in range(count)], far
+
+
+def line_pairings(bands, doms, lats):
     far = []
-    for i in range(count):
-        j = i + 1 if i % 2 else i - 1
-        if closed:
-            j %= count
-        far.append((i, j if 0 <= j < count else i))
-    return near, far
+    for band in range(bands):
+        other = band + 1 if band % 2 else band - 1
+        for dom in range(doms):
+            for lat in range(lats):
+                here = (band * doms + dom) * lats + lat
+                if 0 <= other < bands:
+                    there = (other * doms + dom) * lats + lat
+                else:
+                    there = (band * doms + dom) * lats + (lat ^ 1)
+                far.append((here, there))
+    return [(i, i ^ 1) for i in range(bands)], far
 
 
 def shifted(x, axis, shift):
@@ -361,15 +372,16 @@
     sectors = lax.axis_size(("dom", "lat"))
     edges = g2m_send.shape[2]
     around = ("dom", "lat")
-    band_near, band_far = pairings(bands, False)
-    ring_near, ring_far = pairings(sectors, True)
+    whole = ("band", "dom", "lat")
+    band_near, band_far = line_pairings(bands, lax.axis_size("dom"), lax.axis_size("lat"))
+    ring_near, ring_far = ring_pairings(sectors)
 
     grid = jnp.transpose(grid_in, (0, 2, 1))
     pitch = -(-grid.shape[2] // LANES) * LANES
     band_rows = grid.shape[0]
     width = band_rows * pitch
     raw_near = lax.ppermute(grid, "band", band_near)
-    raw_far = lax.ppermute(grid, "band", band_far)
+    raw_far = lax.ppermute(grid, whole, band_far)
     mesh_edges = mesh_send.shape[2]
     weights = (w_grid, w_gs, w_gr, w_gn, w_ms, w_mr, w_mn, mesh_in, d_out)
     inputs = (g2m_send, g2m_recv, mesh_send, mesh_recv, grid)
@@ -421,7 +433,10 @@
         part, from_near, from_far, mesh_near, mesh_far, mesh_in, w_gn,
     )
     one_near = lax.ppermute(mesh_one, "band", band_near)
-    one_far = lax.ppermute(mesh_one, "band", pairings(bands, True)[1])
+    one_far = lax.ppermute(mesh_one, whole, band_far)
+    doms = lax.axis_size("dom")
+    lats = lax.axis_size("lat")
+    dom_nodes = [shifted(mesh_one, "dom", i + 1) for i in range(doms - 1)]
     mesh_out, sums, recv_sum, to_near, to_far = call(
         process_kernel,
         [
@@ -435,58 +450,45 @@
         w_ms, w_mr, w_mn,
     )
     from_near = lax.ppermute(to_near, "band", band_near)
-    from_far = lax.ppermute(to_far, "band", band_far)
-    doms = lax.axis_size("dom")
-    lats = lax.axis_size("lat")
-    cols = latent // sectors
-    halves_shape = [
-        ((doms, latent, cols), F32),
-        (((lats - 1) * doms, latent, cols), BF16),
-    ]
-    ms_halves = call(
-        process_grad_kernel, halves_shape, one_near, mesh_one, one_far, sums, from_near
-    )
-    *ms_halves, from_far = lax.optimization_barrier((*ms_halves, from_far))
+    from_far = lax.ppermute(to_far, whole, band_far)
+    from_near, *dom_nodes = lax.optimization_barrier((from_near, *dom_nodes))
     (home,) = call(home_kernel, [((node_count, latent), F32)], recv_sum, d_out, w_mr)
+    message = (node_count + node_count // 2, latent)
     part, to_near, to_far = call(
         cotangent_kernel,
-        [
-            ((cycle, latent), F32),
-            ((node_count, latent), BF16),
-            ((node_count, latent), BF16),
-        ],
-        sums, from_near, from_far, home, w_ms,
+        [((cycle, latent), F32), (message, BF16), (message, BF16)],
+        sums, from_near, from_far, home,
     )
     from_near = lax.ppermute(to_near, around, ring_near)
     from_far = lax.ppermute(to_far, around, ring_far)
 
-    def over_lat(sends):
-        return [
-            shifted(sends[i * doms : (i + 1) * doms], "lat", i + 1) for i in range(lats - 1)
-        ]
-
+    cols = latent // sectors
     rows = latent // bands
-    ms_keep, ms_sends = ms_halves
-    (ms_tiles,) = call(
-        tiles_kernel, [((bands * doms, rows, cols), BF16)], ms_keep, *over_lat(ms_sends)
-    )
-    ms_tiles, from_near = lax.optimization_barrier((ms_tiles, from_near))
-    grad_ms = lax.psum_scatter(ms_tiles, ("band", "dom"), scatter_dimension=0, tiled=True)
-    gs_keep, gs_sends = call(
+    keep, sends, total = call(
         encode_grad_kernel,
-        halves_shape,
-        recv_hits, part, from_near, from_far, node_slope, w_gn, senders, edge_slope,
-    )
-    gs_keep, gs_sends = call(
+        [
+            ((doms, latent, cols), F32),
+            (((lats - 1) * doms, latent, cols), BF16),
+            ((doms, cycle, cols), BF16),
+        ],
+        recv_hits, part, from_near, from_far, home, node_slope, w_ms, w_gn, senders, edge_slope,
+    )
+    came = [shifted(sends[i * doms : (i + 1) * doms], "lat", i + 1) for i in range(lats - 1)]
+    keep, sends = call(
         over_lat_kernel,
-        [((latent, cols), F32), ((doms - 1, latent, cols), BF16)],
-        gs_keep, *over_lat(gs_sends),
-    )
-    gs_came = [shifted(gs_sends[i], "dom", i + 1) for i in range(doms - 1)]
-    (shares,) = call(over_dom_kernel, [((bands, rows, cols), BF16)], gs_keep, *gs_came)
+        [((latent, cols), F32), ((doms - 1, latent + cycle, cols), BF16)],
+        keep, total, *came,
+    )
+    came = [shifted(sends[i], "dom", i + 1) for i in range(doms - 1)]
+    (shares,) = call(
+        over_dom_kernel,
+        [((bands, 2, rows, cols), BF16)],
+        keep, total, mesh_one, *came, *dom_nodes,
+    )
     shares = lax.all_to_all(shares, "band", 0, 0, tiled=True)
-    (grad_gs,) = call(over_band_kernel, [((rows, cols), F32)], shares)
-    return mesh_out, grad_gs, grad_ms[0].astype(F32)
+    tile = ((rows, cols), F32)
+    grad_gs, grad_ms = call(over_band_kernel, [tile, tile], shares)
+    return mesh_out, grad_gs, grad_ms
 
 
 def solution(mesh):

time: 132 us -> 71.9 us (0.54)
  waiting for transfers between devices: 66.7 us -> 17.3 us
  between operations: 15.5 us -> 2.06 us
  blocking collectives: 0 us -> 11.7 us
  starting transfers between devices: 20.4 us -> 14.9 us
  Pallas kernels: 14.2 us -> 12.7 us
  other arithmetic: 1.39 us -> 0 us
    reduce_scatter x1 -> x0, waiting for transfers between devices: 44.7 us -> none  [on_device(): lax.psum_scatter(ms_tiles, ('band', 'dom'), scatter_dimension=0, tiled=True)]
    all_to_all x0 -> x1, blocking collectives: none -> 11.7 us  [on_device(): shares = lax.all_to_all(shares, 'band', 0, 0, tiled=True)]
    ppermute x3, waiting for transfers between devices: 5.36 us -> 0.01 us  [the longest x1 0.01 us: on_device(): one_far = lax.ppermute(mesh_one, whole, band_far)]
    all_to_all x1 -> x0, starting transfers between devices: 5.25 us -> none  [on_device(): shares = lax.all_to_all(shares, 'band', 0, 0, tiled=True)]
    ppermute x3, starting transfers between devices: 3.78 us -> 0.95 us  [the longest x1 0.52 us: on_device(): raw_far = lax.ppermute(grid, whole, band_far)]
    ppermute x3, starting transfers between devices: 1.54 us -> 3.29 us  [shifted(): lax.ppermute(x, axis, [(i, (i + shift) % count) for i in range(count)])]
    ppermute x1, waiting for transfers between devices: 0.14 us -> 1.76 us  [on_device(): one_near = lax.ppermute(mesh_one, 'band', band_near)]
    pallas_call x13 -> x11, Pallas kernels: 14.2 us -> 12.7 us  [call(): pl.pallas_call(kernel, out_shape=[jax.ShapeDtypeStruct(shape, dtype) for...]
  transfers between devices with their start and end apart: 17 -> 15, of which waited for: 10 -> 7; matrix products, arithmetic and copies ran while one was open for 1% -> 0% of each run, Pallas kernels for 5% -> 7%
where the time goes in v6:
time: 71.9 us; the launch traced here: 71.1 us
  waiting for transfers between devices  17.3 us (24%)
  starting transfers between devices  14.9 us (21%)
  Pallas kernels  12.7 us (18%)
  local copies, waits for them, and re-layouts  12.5 us (17%)
  blocking collectives  11.7 us (16%)
  between operations  2.06 us (3%)
    pallas_call x11, Pallas kernels, call(): pl.pallas_call(kernel, out_shape=[jax.ShapeDtypeStruct(shape, dtype) for...  12.7 us
    unnamed x28, local copies, waits for them, and re-layouts  12.5 us
    all_to_all x1, blocking collectives, on_device(): shares = lax.all_to_all(shares, 'band', 0, 0, tiled=True)  11.7 us
    ppermute x3, waiting for transfers between devices, shifted(): lax.ppermute(x, axis, [(i, (i + shift) % count) for i in range(count)])  6.08 us
    ppermute x2, waiting for transfers between devices, on_device(): from_far = lax.ppermute(to_far, around, ring_far)  4.42 us
    ppermute x1, starting transfers between devices, on_device(): raw_near = lax.ppermute(grid, 'band', band_near)  4.15 us
    ppermute x3, starting transfers between devices, shifted(): lax.ppermute(x, axis, [(i, (i + shift) % count) for i in range(count)])  3.29 us
    ppermute x1, waiting for transfers between devices, on_device(): from_near = lax.ppermute(to_near, 'band', band_near)  2.97 us
  transfers between devices with their start and end apart: 15, of which 7 were waited for; matrix products, arithmetic and copies ran while one was open for 0% of the time, Pallas kernels for 7%

profile of v6, /device:TPU:0, one launch (start us, length us, event | category | flops | bytes accessed | tf_op | source)
XLA Modules:
  0.0 71.1 jit_solution(16988262021865133510)
XLA Ops:
  1.2 4.1 %collective-permute-start = (bf16[3,227,360]{2,1,0:T(8,128)(2,1)}, bf16[3,227,360]{2,1,0:T(8,128)(2,1)S(1)}, u32[]{:S(2)}, u32[]{:S(2)}) collective-permute-start(bf16[3,227,360]{2,1,0:T(8,128)(2,1)} %bitcast.3), channel_id=1, source_target_pairs={{0,4},{4,0},{8,12},{12,8},{1,5},{5,1},{9,13},{13,9},{2,6},{6,2},{1... | collective-permute-start | bytes 1470968 | tf_op jit(solution)/shard_map/ppermute | solution.py:383
  6.6 1.0 %copy-done = bf16[3,360,227]{1,2,0:T(8,128)(2,1)S(1)} copy-done((bf16[3,360,227]{1,2,0:T(8,128)(2,1)S(1)}, bf16[3,360,227]{1,2,0:T(8,128)(2,1)}, u32[]{:S(2)}) %copy-start) | copy-done | bytes 490344
  7.6 1.0 %copy-done.1 = bf16[512,512]{1,0:T(8,128)(2,1)S(1)} copy-done((bf16[512,512]{1,0:T(8,128)(2,1)S(1)}, bf16[512,512]{1,0:T(8,128)(2,1)}, u32[]{:S(2)}) %copy-start.1) | copy-done | bytes 524312
  8.7 1.0 %copy-done.2 = bf16[512,512]{1,0:T(8,128)(2,1)S(1)} copy-done((bf16[512,512]{1,0:T(8,128)(2,1)S(1)}, bf16[512,512]{1,0:T(8,128)(2,1)}, u32[]{:S(2)}) %copy-start.2) | copy-done | bytes 524312
  9.7 1.0 %copy-done.3 = bf16[512,512]{1,0:T(8,128)(2,1)S(1)} copy-done((bf16[512,512]{1,0:T(8,128)(2,1)S(1)}, bf16[512,512]{1,0:T(8,128)(2,1)}, u32[]{:S(2)}) %copy-start.3) | copy-done | bytes 524312
  10.8 1.0 %copy-done.4 = bf16[512,512]{1,0:T(8,128)(2,1)S(1)} copy-done((bf16[512,512]{1,0:T(8,128)(2,1)S(1)}, bf16[512,512]{1,0:T(8,128)(2,1)}, u32[]{:S(2)}) %copy-start.4) | copy-done | bytes 524312
  11.8 1.0 %copy-done.5 = bf16[512,512]{1,0:T(8,128)(2,1)S(1)} copy-done((bf16[512,512]{1,0:T(8,128)(2,1)S(1)}, bf16[512,512]{1,0:T(8,128)(2,1)}, u32[]{:S(2)}) %copy-start.5) | copy-done | bytes 524312
  12.9 1.0 %copy-done.6 = bf16[512,512]{1,0:T(8,128)(2,1)S(1)} copy-done((bf16[512,512]{1,0:T(8,128)(2,1)S(1)}, bf16[512,512]{1,0:T(8,128)(2,1)}, u32[]{:S(2)}) %copy-start.6) | copy-done | bytes 524312
  13.9 0.9 %copy-done.7 = bf16[227,512]{1,0:T(8,128)(2,1)S(1)} copy-done((bf16[227,512]{1,0:T(8,128)(2,1)S(1)}, bf16[227,512]{1,0:T(8,128)(2,1)}, u32[]{:S(2)}) %copy-start.7) | copy-done | bytes 232472
  14.8 0.8 %copy-done.8 = bf16[32,512]{1,0:T(8,128)(2,1)S(1)} copy-done((bf16[32,512]{1,0:T(8,128)(2,1)S(1)}, bf16[32,512]{1,0:T(8,128)(2,1)}, u32[]{:S(2)}) %copy-start.8) | copy-done | bytes 32792
  15.6 0.8 %copy-done.9 = bf16[32,512]{1,0:T(8,128)(2,1)S(1)} copy-done((bf16[32,512]{1,0:T(8,128)(2,1)S(1)}, bf16[32,512]{1,0:T(8,128)(2,1)}, u32[]{:S(2)}) %copy-start.9) | copy-done | bytes 32792
  16.4 0.7 copy-done.10
  17.0 0.7 copy-done.11
  19.1 2.5 %shard_map.175 = (bf16[227,512]{1,0:T(8,128)(2,1)S(1)}, bf16[512,512]{1,0:T(8,128)(2,1)S(1)}, bf16[512,512]{1,0:T(8,128)(2,1)S(1)}, bf16[512,512]{1,0:T(8,128)(2...) custom-call(s32[1,1]{1,0:T(1,128)S(6)} %copy.19.count, ...), custom_call_target="tpu_custom_call" | custom-call | tf_op jit(solution)/shard_map/pallas_call | solution.py:328
  22.0 1.2 %collective-permute-start.2 = (bf16[32,512]{1,0:T(8,128)(2,1)S(1)}, bf16[32,512]{1,0:T(8,128)(2,1)S(1)}, u32[]{:S(2)}, u32[]{:S(2)}) collective-permute-start(bf16[32,512]{1,0:T(8,128)(2,1)S(1)} %get-tuple-element.52.mesh_in), channel_id=1, source_target_pairs={{0,1},{1,0},{2,3},{3,2},{4,5},{5,4},{6,7},{7,6},{8,9},{9,8},{10,11... | collective-permute-start | bytes 98312 | tf_op jit(solution)/shard_map/ppermute | solution.py:411
  23.3 2.0 %collective-permute-done.3.far.mesh_far = bf16[32,512]{1,0:T(8,128)(2,1)S(1)} collective-permute-done((bf16[32,512]{1,0:T(8,128)(2,1)S(1)}, bf16[32,512]{1,0:T(8,128)(2,1)S(1)}, u32[]{:S(2)}, u32[]{:S(2)}) %collective-permute-start.3) | collective-permute-done | bytes 32800 | tf_op jit(solution)/shard_map/ppermute | solution.py:412
  25.6 5.1 %shard_map.177 = (bf16[1024,512]{1,0:T(8,128)(2,1)S(1)}, bf16[1024,512]{1,0:T(8,128)(2,1)S(1)}, f32[64,512]{1,0:T(8,128)S(1)}, bf16[32,512]{1,0:T(8,128)(2,1)S(1)}, bf16[32,512]{1,0:T(8,128)(2,1)S(1)}) custom-call(bf16[3,227,360]{2,1,0:T(8,128)(2,1)S(1)} %collective-permute-done.near, bf16[3,227,360]{2,1,0:T(8,128)(2,1)S(1)} %collective-permute-done.1.far, ...), custom_call_target="tpu_custom_call" | custom-call | tf_op jit(solution)/shard_map/pallas_call | solution.py:328
  30.8 1.2 %collective-permute-start.5 = (bf16[32,512]{1,0:T(8,128)(2,1)S(1)}, bf16[32,512]{1,0:T(8,128)(2,1)S(1)}, u32[]{:S(2)}, u32[]{:S(2)}) collective-permute-start(bf16[32,512]{1,0:T(8,128)(2,1)S(1)} %get-tuple-element.58), channel_id=1, source_target_pairs={{0,3},{1,2},{2,1},{3,0},{4,7},{5,6},{6,5},{7,4},{8,11},{9,10},{10,... | collective-permute-start | bytes 98312 | tf_op jit(solution)/shard_map/ppermute | solution.py:429
  32.0 2.2 %collective-permute-done.5.far = bf16[32,512]{1,0:T(8,128)(2,1)S(1)} collective-permute-done((bf16[32,512]{1,0:T(8,128)(2,1)S(1)}, bf16[32,512]{1,0:T(8,128)(2,1)S(1)}, u32[]{:S(2)}, u32[]{:S(2)}) %collective-permute-start.5) | collective-permute-done | bytes 32800 | tf_op jit(solution)/shard_map/ppermute | solution.py:429
  34.9 1.0 %collective-permute-start.6 = (bf16[64,512]{1,0:T(8,128)(2,1)S(1)}, bf16[64,512]{1,0:T(8,128)(2,1)S(1)}, u32[]{:S(2)}, u32[]{:S(2)}) collective-permute-start(bf16[64,512]{1,0:T(8,128)(2,1)S(1)} %get-tuple-element.60.own.nodes), channel_id=1, source_target_pairs={{0,4},{4,0},{8,12},{12,8},{1,5},{5,1},{9,13},{13,9},{2,6},{6,2},{1... | collective-permute-start | bytes 196616 | tf_op jit(solution)/shard_map/ppermute | solution.py:435
  35.9 1.5 %collective-permute-start.9 = (bf16[64,512]{1,0:T(8,128)(2,1)S(1)}, bf16[64,512]{1,0:T(8,128)(2,1)S(1)}, u32[]{:S(2)}, u32[]{:S(2)}) collective-permute-start(bf16[64,512]{1,0:T(8,128)(2,1)S(1)} %get-tuple-element.60.own.nodes), channel_id=1, source_target_pairs={{0,2},{2,0},{1,3},{3,1},{4,6},{6,4},{5,7},{7,5},{8,10},{10,8},{9,1... | collective-permute-start | bytes 196616 | tf_op jit(solution)/shard_map/ppermute | solution.py:360
  37.4 1.8 %collective-permute-done.6.near = bf16[64,512]{1,0:T(8,128)(2,1)S(1)} collective-permute-done((bf16[64,512]{1,0:T(8,128)(2,1)S(1)}, bf16[64,512]{1,0:T(8,128)(2,1)S(1)}, u32[]{:S(2)}, u32[]{:S(2)}) %collective-permute-start.6) | collective-permute-done | bytes 65568 | tf_op jit(solution)/shard_map/ppermute | solution.py:435
  39.1 2.0 %shard_map.179 = (bf16[32,512]{1,0:T(8,128)(2,1)}, f32[192,512]{1,0:T(8,128)S(1)}, bf16[32,512]{1,0:T(8,128)(2,1)S(1)}, bf16[64,512]{1,0:T(8,128)(2,1)S(1)}, bf16[64,512]{1,0:T(8,128)(2,1)S(1)}) custom-call(bf16[512,384]{1,0:T(8,128)(2,1)S(1)} %get-tuple-element.44.from_hits, bf16[512,64]{1,0:T(8,128)(2,1)S(1)} %get-tuple-element.45.to_hits, ...), custom_call_target="tpu_custom_call" | custom-call | tf_op jit(solution)/shard_map/pallas_call | solution.py:328
  41.1 1.1 %collective-permute-start.8 = (bf16[64,512]{1,0:T(8,128)(2,1)S(1)}, bf16[64,512]{1,0:T(8,128)(2,1)S(1)}, u32[]{:S(2)}, u32[]{:S(2)}) collective-permute-start(bf16[64,512]{1,0:T(8,128)(2,1)S(1)} %get-tuple-element.67), channel_id=1, source_target_pairs={{0,4},{4,0},{8,12},{12,8},{1,5},{5,1},{9,13},{13,9},{2,6},{6,2},{1... | collective-permute-start | bytes 196616 | tf_op jit(solution)/shard_map/ppermute | solution.py:452
  42.5 3.0 %collective-permute-done.8.near = bf16[64,512]{1,0:T(8,128)(2,1)S(1)} collective-permute-done((bf16[64,512]{1,0:T(8,128)(2,1)S(1)}, bf16[64,512]{1,0:T(8,128)(2,1)S(1)}, u32[]{:S(2)}, u32[]{:S(2)}) %collective-permute-start.8) | collective-permute-done | bytes 65568 | tf_op jit(solution)/shard_map/ppermute | solution.py:452
  45.6 1.3 %collective-permute-start.12 = (bf16[48,512]{1,0:T(8,128)(2,1)S(1)}, bf16[48,512]{1,0:T(8,128)(2,1)S(1)}, u32[]{:S(2)}, u32[]{:S(2)}) collective-permute-start(bf16[48,512]{1,0:T(8,128)(2,1)S(1)} %get-tuple-element.73), channel_id=1, source_target_pairs={{0,3},{1,2},{2,1},{3,0},{4,7},{5,6},{6,5},{7,4},{8,11},{9,10},{10,... | collective-permute-start | bytes 147464 | tf_op jit(solution)/shard_map/ppermute | solution.py:463
  46.9 2.3 %collective-permute-done.12.far = bf16[48,512]{1,0:T(8,128)(2,1)S(1)} collective-permute-done((bf16[48,512]{1,0:T(8,128)(2,1)S(1)}, bf16[48,512]{1,0:T(8,128)(2,1)S(1)}, u32[]{:S(2)}, u32[]{:S(2)}) %collective-permute-start.12) | collective-permute-done | bytes 49184 | tf_op jit(solution)/shard_map/ppermute | solution.py:463
  49.2 1.4 %shard_map.182 = (f32[2,512,128]{2,1,0:T(8,128)S(1)}, bf16[2,512,128]{2,1,0:T(8,128)(2,1)S(1)}, bf16[2,64,128]{2,1,0:T(8,128)(2,1)S(1)}) custom-call(bf16[1024,128]{1,0:T(8,128)(2,1)S(1)} %get-tuple-element.49.recv_hits, f32[64,512]{1,0:T(8,128)S(1)} %get-tuple-element.71.part, bf16[48,512]{1,0:T(8,128)(2,1)S(1)} %collective-permute-done.11.near, ...), custom_call_target="tpu_custom_call" | custom-call | tf_op jit(solution)/shard_map/pallas_call | solution.py:328
  51.1 1.2 %collective-permute-done.13.refs_0_ = bf16[2,512,128]{2,1,0:T(8,128)(2,1)S(1)} collective-permute-done((bf16[2,512,128]{2,1,0:T(8,128)(2,1)S(1)}, bf16[2,512,128]{2,1,0:T(8,128)(2,1)S(1)}, u32[]{:S(2)}, u32[]{:S(2)}) %collective-permute-start.13) | collective-permute-done | bytes 262176 | tf_op jit(solution)/shard_map/ppermute | solution.py:360
  52.3 1.3 %collective-permute-start.14 = (bf16[576,128]{1,0:T(8,128)(2,1)S(1)}, bf16[576,128]{1,0:T(8,128)(2,1)S(1)}, u32[]{:S(2)}, u32[]{:S(2)}) collective-permute-start(bf16[576,128]{1,0:T(8,128)(2,1)S(1)} %bitcast.5), channel_id=1, source_target_pairs={{0,2},{2,0},{1,3},{3,1},{4,6},{6,4},{5,7},{7,5},{8,10},{10,8},{9,1... | collective-permute-start | bytes 442376 | tf_op jit(solution)/shard_map/ppermute | solution.py:360
  53.6 4.9 %collective-permute-done.14.refs_0_ = bf16[576,128]{1,0:T(8,128)(2,1)S(1)} collective-permute-done((bf16[576,128]{1,0:T(8,128)(2,1)S(1)}, bf16[576,128]{1,0:T(8,128)(2,1)S(1)}, u32[]{:S(2)}, u32[]{:S(2)}) %collective-permute-start.14) | collective-permute-done | bytes 147488 | tf_op jit(solution)/shard_map/ppermute | solution.py:360
  58.8 11.7 %all_to_all.5.shares = bf16[4,2,128,128]{3,2,1,0:T(8,128)(2,1)S(1)} all-to-all(bf16[4,2,128,128]{3,2,1,0:T(8,128)(2,1)S(1)} %shard_map.184), channel_id=1, replica_groups=mesh['groups'=2,'band'=4,'dom'=2,'lat'=2] {'band'}, dimensions={0} | all-to-all | bytes 524288 | tf_op jit(solution)/shard_map/all_to_all | solution.py:488
  (38 shorter events, 5.3 us)
Async XLA Ops:
  0.6 24.9 %collective-permute-start.1 = (bf16[3,227,360]{2,1,0:T(8,128)(2,1)}, bf16[3,227,360]{2,1,0:T(8,128)(2,1)S(1)}, u32[]{:S(2)}, u32[]{:S(2)}) collective-permute-start(bf16[3,227,360]{2,1,0:T(8,128)(2,1)} %bitcast.2), channel_id=1, source_target_pairs={{0,1},{1,0},{2,3},{3,2},{4,8},{5,9},{6,10},{7,11},{8,4},{9,5},{10,... | collective-permute-start | bytes 1470968 | tf_op jit(solution)/shard_map/ppermute | solution.py:384
  1.2 24.4 %collective-permute-start = (bf16[3,227,360]{2,1,0:T(8,128)(2,1)}, bf16[3,227,360]{2,1,0:T(8,128)(2,1)S(1)}, u32[]{:S(2)}, u32[]{:S(2)}) collective-permute-start(bf16[3,227,360]{2,1,0:T(8,128)(2,1)} %bitcast.3), channel_id=1, source_target_pairs={{0,4},{4,0},{8,12},{12,8},{1,5},{5,1},{9,13},{13,9},{2,6},{6,2},{1... | collective-permute-start | bytes 1470968 | tf_op jit(solution)/shard_map/ppermute | solution.py:383
  6.6 1.0 %copy-start = (bf16[3,360,227]{1,2,0:T(8,128)(2,1)S(1)}, bf16[3,360,227]{1,2,0:T(8,128)(2,1)}, u32[]{:S(2)}) copy-start(bf16[3,360,227]{1,2,0:T(8,128)(2,1)} %param.16) | copy-start | bytes 1470964
  7.6 1.0 %copy-start.1 = (bf16[512,512]{1,0:T(8,128)(2,1)S(1)}, bf16[512,512]{1,0:T(8,128)(2,1)}, u32[]{:S(2)}) copy-start(bf16[512,512]{1,0:T(8,128)(2,1)} %refs_6_.1) | copy-start | bytes 1572868
  8.7 1.0 %copy-start.2 = (bf16[512,512]{1,0:T(8,128)(2,1)S(1)}, bf16[512,512]{1,0:T(8,128)(2,1)}, u32[]{:S(2)}) copy-start(bf16[512,512]{1,0:T(8,128)(2,1)} %refs_7_.1) | copy-start | bytes 1572868
  9.7 1.0 %copy-start.3 = (bf16[512,512]{1,0:T(8,128)(2,1)S(1)}, bf16[512,512]{1,0:T(8,128)(2,1)}, u32[]{:S(2)}) copy-start(bf16[512,512]{1,0:T(8,128)(2,1)} %refs_8_.1) | copy-start | bytes 1572868
  10.8 1.0 %copy-start.4 = (bf16[512,512]{1,0:T(8,128)(2,1)S(1)}, bf16[512,512]{1,0:T(8,128)(2,1)}, u32[]{:S(2)}) copy-start(bf16[512,512]{1,0:T(8,128)(2,1)} %refs_9_.1) | copy-start | bytes 1572868
  11.8 1.0 %copy-start.5 = (bf16[512,512]{1,0:T(8,128)(2,1)S(1)}, bf16[512,512]{1,0:T(8,128)(2,1)}, u32[]{:S(2)}) copy-start(bf16[512,512]{1,0:T(8,128)(2,1)} %refs_10_.1) | copy-start | bytes 1572868
  12.9 1.0 %copy-start.6 = (bf16[512,512]{1,0:T(8,128)(2,1)S(1)}, bf16[512,512]{1,0:T(8,128)(2,1)}, u32[]{:S(2)}) copy-start(bf16[512,512]{1,0:T(8,128)(2,1)} %refs_11_.1) | copy-start | bytes 1572868
  13.9 0.9 %copy-start.7 = (bf16[227,512]{1,0:T(8,128)(2,1)S(1)}, bf16[227,512]{1,0:T(8,128)(2,1)}, u32[]{:S(2)}) copy-start(bf16[227,512]{1,0:T(8,128)(2,1)} %refs_5_.1) | copy-start | bytes 697348
  14.8 0.8 %copy-start.8 = (bf16[32,512]{1,0:T(8,128)(2,1)S(1)}, bf16[32,512]{1,0:T(8,128)(2,1)}, u32[]{:S(2)}) copy-start(bf16[32,512]{1,0:T(8,128)(2,1)} %refs_12_.1) | copy-start | bytes 98308
  15.6 0.8 %copy-start.9 = (bf16[32,512]{1,0:T(8,128)(2,1)S(1)}, bf16[32,512]{1,0:T(8,128)(2,1)}, u32[]{:S(2)}) copy-start(bf16[32,512]{1,0:T(8,128)(2,1)} %refs_13_.1) | copy-start | bytes 98308
  16.4 0.7 copy-start.10
  17.0 0.7 copy-start.11
  17.7 0.7 copy-start.12
  18.4 0.7 copy-start.13
  21.6 3.7 %collective-permute-start.3 = (bf16[32,512]{1,0:T(8,128)(2,1)S(1)}, bf16[32,512]{1,0:T(8,128)(2,1)S(1)}, u32[]{:S(2)}, u32[]{:S(2)}) collective-permute-start(bf16[32,512]{1,0:T(8,128)(2,1)S(1)} %get-tuple-element.52.mesh_in), channel_id=1, source_target_pairs={{0,3},{1,2},{2,1},{3,0},{4,7},{5,6},{6,5},{7,4},{8,11},{9,10},{10,... | collective-permute-start | bytes 98312 | tf_op jit(solution)/shard_map/ppermute | solution.py:412
  22.0 3.3 %collective-permute-start.2 = (bf16[32,512]{1,0:T(8,128)(2,1)S(1)}, bf16[32,512]{1,0:T(8,128)(2,1)S(1)}, u32[]{:S(2)}, u32[]{:S(2)}) collective-permute-start(bf16[32,512]{1,0:T(8,128)(2,1)S(1)} %get-tuple-element.52.mesh_in), channel_id=1, source_target_pairs={{0,1},{1,0},{2,3},{3,2},{4,5},{5,4},{6,7},{7,6},{8,9},{9,8},{10,11... | collective-permute-start | bytes 98312 | tf_op jit(solution)/shard_map/ppermute | solution.py:411
  30.6 1.4 %collective-permute-start.4 = (bf16[32,512]{1,0:T(8,128)(2,1)S(1)}, bf16[32,512]{1,0:T(8,128)(2,1)S(1)}, u32[]{:S(2)}, u32[]{:S(2)}) collective-permute-start(bf16[32,512]{1,0:T(8,128)(2,1)S(1)} %get-tuple-element.57), channel_id=1, source_target_pairs={{0,1},{1,0},{2,3},{3,2},{4,5},{5,4},{6,7},{7,6},{8,9},{9,8},{10,11... | collective-permute-start | bytes 98312 | tf_op jit(solution)/shard_map/ppermute | solution.py:428
  30.8 3.4 %collective-permute-start.5 = (bf16[32,512]{1,0:T(8,128)(2,1)S(1)}, bf16[32,512]{1,0:T(8,128)(2,1)S(1)}, u32[]{:S(2)}, u32[]{:S(2)}) collective-permute-start(bf16[32,512]{1,0:T(8,128)(2,1)S(1)} %get-tuple-element.58), channel_id=1, source_target_pairs={{0,3},{1,2},{2,1},{3,0},{4,7},{5,6},{6,5},{7,4},{8,11},{9,10},{10,... | collective-permute-start | bytes 98312 | tf_op jit(solution)/shard_map/ppermute | solution.py:429
  34.4 2.9 %collective-permute-start.7 = (bf16[64,512]{1,0:T(8,128)(2,1)S(1)}, bf16[64,512]{1,0:T(8,128)(2,1)S(1)}, u32[]{:S(2)}, u32[]{:S(2)}) collective-permute-start(bf16[64,512]{1,0:T(8,128)(2,1)S(1)} %get-tuple-element.60.own.nodes), channel_id=1, source_target_pairs={{0,1},{1,0},{2,3},{3,2},{4,8},{5,9},{6,10},{7,11},{8,4},{9,5},{10,... | collective-permute-start | bytes 196616 | tf_op jit(solution)/shard_map/ppermute | solution.py:436
  34.9 4.3 %collective-permute-start.6 = (bf16[64,512]{1,0:T(8,128)(2,1)S(1)}, bf16[64,512]{1,0:T(8,128)(2,1)S(1)}, u32[]{:S(2)}, u32[]{:S(2)}) collective-permute-start(bf16[64,512]{1,0:T(8,128)(2,1)S(1)} %get-tuple-element.60.own.nodes), channel_id=1, source_target_pairs={{0,4},{4,0},{8,12},{12,8},{1,5},{5,1},{9,13},{13,9},{2,6},{6,2},{1... | collective-permute-start | bytes 196616 | tf_op jit(solution)/shard_map/ppermute | solution.py:435
  35.9 6.6 %collective-permute-start.9 = (bf16[64,512]{1,0:T(8,128)(2,1)S(1)}, bf16[64,512]{1,0:T(8,128)(2,1)S(1)}, u32[]{:S(2)}, u32[]{:S(2)}) collective-permute-start(bf16[64,512]{1,0:T(8,128)(2,1)S(1)} %get-tuple-element.60.own.nodes), channel_id=1, source_target_pairs={{0,2},{2,0},{1,3},{3,1},{4,6},{6,4},{5,7},{7,5},{8,10},{10,8},{9,1... | collective-permute-start | bytes 196616 | tf_op jit(solution)/shard_map/ppermute | solution.py:360
  41.1 4.3 %collective-permute-start.8 = (bf16[64,512]{1,0:T(8,128)(2,1)S(1)}, bf16[64,512]{1,0:T(8,128)(2,1)S(1)}, u32[]{:S(2)}, u32[]{:S(2)}) collective-permute-start(bf16[64,512]{1,0:T(8,128)(2,1)S(1)} %get-tuple-element.67), channel_id=1, source_target_pairs={{0,4},{4,0},{8,12},{12,8},{1,5},{5,1},{9,13},{13,9},{2,6},{6,2},{1... | collective-permute-start | bytes 196616 | tf_op jit(solution)/shard_map/ppermute | solution.py:452
  42.2 3.3 %collective-permute-start.10 = (bf16[64,512]{1,0:T(8,128)(2,1)S(1)}, bf16[64,512]{1,0:T(8,128)(2,1)S(1)}, u32[]{:S(2)}, u32[]{:S(2)}) collective-permute-start(bf16[64,512]{1,0:T(8,128)(2,1)S(1)} %get-tuple-element.69), channel_id=1, source_target_pairs={{0,1},{1,0},{2,3},{3,2},{4,8},{5,9},{6,10},{7,11},{8,4},{9,5},{10,... | collective-permute-start | bytes 196616 | tf_op jit(solution)/shard_map/ppermute | solution.py:453
  45.5 1.4 %collective-permute-start.11 = (bf16[48,512]{1,0:T(8,128)(2,1)S(1)}, bf16[48,512]{1,0:T(8,128)(2,1)S(1)}, u32[]{:S(2)}, u32[]{:S(2)}) collective-permute-start(bf16[48,512]{1,0:T(8,128)(2,1)S(1)} %get-tuple-element.72), channel_id=1, source_target_pairs={{0,1},{1,0},{2,3},{3,2},{4,5},{5,4},{6,7},{7,6},{8,9},{9,8},{10,11... | collective-permute-start | bytes 147464 | tf_op jit(solution)/shard_map/ppermute | solution.py:462
  45.6 3.6 %collective-permute-start.12 = (bf16[48,512]{1,0:T(8,128)(2,1)S(1)}, bf16[48,512]{1,0:T(8,128)(2,1)S(1)}, u32[]{:S(2)}, u32[]{:S(2)}) collective-permute-start(bf16[48,512]{1,0:T(8,128)(2,1)S(1)} %get-tuple-element.73), channel_id=1, source_target_pairs={{0,3},{1,2},{2,1},{3,0},{4,7},{5,6},{6,5},{7,4},{8,11},{9,10},{10,... | collective-permute-start | bytes 147464 | tf_op jit(solution)/shard_map/ppermute | solution.py:463
  50.6 1.7 %collective-permute-start.13 = (bf16[2,512,128]{2,1,0:T(8,128)(2,1)S(1)}, bf16[2,512,128]{2,1,0:T(8,128)(2,1)S(1)}, u32[]{:S(2)}, u32[]{:S(2)}) collective-permute-start(bf16[2,512,128]{2,1,0:T(8,128)(2,1)S(1)} %get-tuple-element.79), channel_id=1, source_target_pairs={{0,1},{1,0},{2,3},{3,2},{4,5},{5,4},{6,7},{7,6},{8,9},{9,8},{10,11... | collective-permute-start | bytes 786440 | tf_op jit(solution)/shard_map/ppermute | solution.py:360
  52.3 6.2 %collective-permute-start.14 = (bf16[576,128]{1,0:T(8,128)(2,1)S(1)}, bf16[576,128]{1,0:T(8,128)(2,1)S(1)}, u32[]{:S(2)}, u32[]{:S(2)}) collective-permute-start(bf16[576,128]{1,0:T(8,128)(2,1)S(1)} %bitcast.5), channel_id=1, source_target_pairs={{0,2},{2,0},{1,3},{3,1},{4,6},{6,4},{5,7},{7,5},{8,10},{10,8},{9,1... | collective-permute-start | bytes 442376 | tf_op jit(solution)/shard_map/ppermute | solution.py:360

commit v7 on v6

--- a/solution.py
+++ b/solution.py
@@ -8,7 +8,7 @@
 F32 = jnp.float32
 BF16 = jnp.bfloat16
 LANES = 128
-FETCHED = 14
+GS, GR, GN, MS, MR, MN = range(6)
 
 
 def mm(a, b):
@@ -67,6 +67,11 @@
     return jnp.where(slot < count, row, -1)
 
 
+def weight(stack, index):
+    latent = stack.shape[1]
+    return stack[index * latent : (index + 1) * latent]
+
+
 def even_on(axis):
     return lax.rem(lax.axis_index(axis), 2) == 0
 
@@ -89,23 +94,21 @@
             )
 
 
-def index_kernel(count, mesh_count, *refs):
-    fetched, refs = refs[:FETCHED], refs[FETCHED:]
-    kept = refs[: FETCHED - 5]
-    (
-        own_out, recv_hits, recv_rows, from_hits, to_hits, from_rows, to_rows
-    ) = refs[FETCHED - 5 : FETCHED + 2]
-    halo_hits, wide, send, recv, mesh_send, mesh_recv, grid, sems = refs[FETCHED + 2 :]
-    copies = [
-        pltpu.make_async_copy(source, target, sems.at[i])
-        for i, (source, target) in enumerate(
-            zip(fetched, (send, recv, mesh_send, mesh_recv, grid) + tuple(kept))
+def index_kernel(
+    count, mesh_count, indices, grid,
+    own_out, recv_hits, recv_rows, from_hits, to_hits, from_rows, to_rows, halo_hits, wide,
+):
+    edges = recv_hits.shape[0]
+    mesh_edges = to_hits.shape[0]
+    send, recv, mesh_send, mesh_recv = (
+        indices[0, :, first : first + size]
+        for first, size in (
+            (0, edges),
+            (edges, edges),
+            (2 * edges, mesh_edges),
+            (2 * edges + mesh_edges, mesh_edges),
         )
-    ]
-    for copy in copies:
-        copy.start()
-    for copy in copies[:5]:
-        copy.wait()
+    )
     band_rows, _, cols = grid.shape
     pitch = wide.shape[1] // band_rows
     width = band_rows * pitch
@@ -116,44 +119,42 @@
     near_base = jnp.where(even_band, 2 * width, 0)
     far_base = jnp.where(even_band, 0, 2 * width)
     block = 256
-    for first in range(0, send.shape[2], block):
+    for first in range(0, edges, block):
         part_of = slice(first, first + block)
-        index = columns(spread(send[0, :, part_of], 3 * band_rows, cols, pitch))
+        index = columns(spread(send[:, part_of], 3 * band_rows, cols, pitch))
         own_hit = hits_from(index, width, width, width)
         own_out[part_of] = mm_nt(own_hit, wide[...]).astype(BF16)
         halo_hits[part_of, :width] = hits_from(index, width, width, near_base)
         halo_hits[part_of, width:] = hits_from(index, width, width, far_base)
-        target = live_only(recv[0, :, part_of], count[0, 0], first)
+        target = live_only(recv[:, part_of], count[0, 0], first)
         recv_hits[part_of] = hits_from(columns(target), 2 * cycle, cycle)
         recv_rows[:, part_of] = hits_to(target, cycle)
-    raw = mesh_send[0]
+    raw = mesh_send
     flipped = jnp.where(
         raw < cycle, raw + 2 * cycle, jnp.where(raw < 2 * cycle, raw, raw - 2 * cycle)
     )
     source = jnp.where(even_band, flipped, raw)
-    target = live_only(mesh_recv[0], mesh_count[0, 0])
+    target = live_only(mesh_recv, mesh_count[0, 0])
     from_hits[...] = hits_from(columns(source), 6 * cycle, 3 * cycle)
     to_hits[...] = hits_from(columns(target), 2 * node_count, node_count)
     from_rows[...] = hits_to(source, 3 * cycle)
     to_rows[...] = hits_to(target, node_count)
-    for copy in copies[5:]:
-        copy.wait()
-
-
-def table_kernel(near, far, mesh_in, w_gr, table_out):
+
+
+def table_kernel(near, far, mesh_in, stack, table_out):
     node_count = mesh_in.shape[0]
     rim = node_count // 2
     even = even_on("lat")
     left = jnp.where(even, far[...], near[...])[rim:]
     right = jnp.where(even, near[...], far[...])[:rim]
     cycle = jnp.concatenate([left, mesh_in[...], right], axis=0)
-    high, low = halves(mm(cycle, w_gr[...]))
+    high, low = halves(mm(cycle, weight(stack, GR)))
     table_out[: 2 * node_count] = high
     table_out[2 * node_count :] = low
 
 
 def encode_kernel(
-    near, far, halo_hits, recv_hits, recv_rows, own, table, w_grid, w_gs,
+    near, far, halo_hits, recv_hits, recv_rows, own, table, stack,
     senders_out, slope_out, part_out, near_out, far_out, wide,
 ):
     half = recv_rows.shape[0] // 2
@@ -162,10 +163,10 @@
     fill(wide, near, pitch, 0)
     fill(wide, far, pitch, width)
     raw = own[...] + mm_nt(halo_hits[...], wide[...]).astype(BF16)
-    latent, _ = silu_parts(mm(raw, w_grid[...]))
+    latent, _ = silu_parts(mm(raw, stack[stack.shape[0] - raw.shape[1] :]))
     latent = latent.astype(BF16)
     senders_out[...] = latent
-    pre = mm(latent, w_gs[...]) + mm(recv_hits[...], table[...])
+    pre = mm(latent, weight(stack, GS)) + mm(recv_hits[...], table[...])
     value, slope = silu_parts(pre)
     slope_out[...] = slope.astype(BF16)
     sums = mm(recv_rows[...], value.astype(BF16))
@@ -175,7 +176,7 @@
     far_out[...] = jnp.where(even, sums[:half], sums[half:]).astype(BF16)
 
 
-def node_kernel(part, near, far, mesh_near, mesh_far, mesh_in, w_gn, mesh_out, slope_out):
+def node_kernel(part, near, far, mesh_near, mesh_far, mesh_in, stack, mesh_out, slope_out):
     node_count = mesh_in.shape[0]
     rim = node_count // 2
     even = even_on("lat")
@@ -185,13 +186,13 @@
     mesh_left = jnp.where(even, mesh_far[...], mesh_near[...])[rim:]
     mesh_right = jnp.where(even, mesh_near[...], mesh_far[...])[:rim]
     cycle = jnp.concatenate([mesh_left, mesh_in[...], mesh_right], axis=0)
-    value, slope = silu_parts(mm(total.astype(BF16), w_gn[...]))
+    value, slope = silu_parts(mm(total.astype(BF16), weight(stack, GN)))
     mesh_out[...] = (cycle.astype(F32) + value).astype(BF16)
     slope_out[...] = slope
 
 
 def process_kernel(
-    from_hits, to_hits, from_rows, to_rows, near, own, far, d_out, w_ms, w_mr, w_mn,
+    from_hits, to_hits, from_rows, to_rows, near, own, far, d_out, stack,
     mesh_out, sums_out, recv_out, near_out, far_out,
 ):
     cycle = own.shape[0]
@@ -199,15 +200,15 @@
     rim = node_count // 2
     home = own[rim : rim + node_count]
     block = jnp.concatenate([near[...], own[...], far[...]], axis=0)
-    table = jnp.concatenate(halves(mm(block, w_ms[...])), axis=0)
-    recv_table = jnp.concatenate(halves(mm(home, w_mr[...])), axis=0)
+    table = jnp.concatenate(halves(mm(block, weight(stack, MS))), axis=0)
+    recv_table = jnp.concatenate(halves(mm(home, weight(stack, MR))), axis=0)
     pre = mm(from_hits[...], table) + mm(to_hits[...], recv_table)
     value, slope = silu_parts(pre)
-    gate = mm(mm(to_rows[...], value.astype(BF16)).astype(BF16), w_mn[...])
+    gate = mm(mm(to_rows[...], value.astype(BF16)).astype(BF16), weight(stack, MN))
     gate_value, gate_slope = silu_parts(gate)
     mesh_out[...] = (home.astype(F32) + gate_value).astype(BF16)
     gate_two = (d_out[...].astype(F32) * gate_slope).astype(BF16)
-    back = jnp.concatenate(halves(mm_nt(gate_two, w_mn[...])), axis=0)
+    back = jnp.concatenate(halves(mm_nt(gate_two, weight(stack, MN))), axis=0)
     edge_slope = (mm(to_hits[...], back) * slope).astype(BF16)
     sums = mm(from_rows[...], edge_slope)
     recv_out[...] = mm(to_rows[...], edge_slope).astype(BF16)
@@ -235,8 +236,8 @@
                 sends[(shift - 1) * doms + dom] = pick.astype(BF16)
 
 
-def home_kernel(recv_sum, d_out, w_mr, home_out):
-    home_out[...] = mm_nt(recv_sum[...], w_mr[...]) + d_out[...].astype(F32)
+def home_kernel(recv_sum, d_out, stack, home_out):
+    home_out[...] = mm_nt(recv_sum[...], weight(stack, MR)) + d_out[...].astype(F32)
 
 
 def cotangent_kernel(sums, near, far, home, part_out, near_out, far_out):
@@ -253,7 +254,7 @@
 
 
 def encode_grad_kernel(
-    recv_hits, part, near, far, home, node_slope, w_ms, w_gn, senders, edge_slope,
+    recv_hits, part, near, far, home, node_slope, stack, senders, edge_slope,
     keep, sends, total_out,
 ):
     half = part.shape[0] // 2
@@ -263,9 +264,9 @@
     total = part[...] + jnp.concatenate([left[:half], right[:half]], axis=0)
     total = total.astype(BF16)
     rest = jnp.concatenate([left[half:], home[...], right[half:]], axis=0)
-    cot = rest + mm_nt(total, w_ms[...])
+    cot = rest + mm_nt(total, weight(stack, MS))
     gate_one = (cot * node_slope[...]).astype(BF16)
-    back = jnp.concatenate(halves(mm_nt(gate_one, w_gn[...])), axis=0)
+    back = jnp.concatenate(halves(mm_nt(gate_one, weight(stack, GN))), axis=0)
     slope = (mm(recv_hits[...], back) * edge_slope[...].astype(F32)).astype(BF16)
     split_store(mm_tn(senders[...], slope), keep, sends)
     doms, _, cols = total_out.shape
@@ -318,11 +319,9 @@
         out[...] = total
 
 
-def call(kernel, outs, *args, scalars=(), fetched=(), scratch=()):
+def call(kernel, outs, *args, scalars=(), scratch=()):
     in_specs = [
-        pl.BlockSpec(
-            memory_space=pltpu.SMEM if i in scalars else pl.ANY if i in fetched else pltpu.VMEM
-        )
+        pl.BlockSpec(memory_space=pltpu.SMEM if i in scalars else pltpu.VMEM)
         for i in range(len(args))
     ]
     return pl.pallas_call(
@@ -383,12 +382,11 @@
     raw_near = lax.ppermute(grid, "band", band_near)
     raw_far = lax.ppermute(grid, whole, band_far)
     mesh_edges = mesh_send.shape[2]
-    weights = (w_grid, w_gs, w_gr, w_gn, w_ms, w_mr, w_mn, mesh_in, d_out)
-    inputs = (g2m_send, g2m_recv, mesh_send, mesh_recv, grid)
-    staged = call(
+    stack = jnp.concatenate([w_gs, w_gr, w_gn, w_ms, w_mr, w_mn, w_grid], axis=0)
+    indices = jnp.concatenate([g2m_send, g2m_recv, mesh_send, mesh_recv], axis=2)
+    rows, recv_hits, recv_rows, from_hits, to_hits, from_rows, to_rows, halo_hits = call(
         index_kernel,
-        [(x.shape, x.dtype) for x in weights]
-        + [
+        [
             ((edges, variables), BF16),
             ((edges, 2 * cycle), BF16),
             ((cycle, edges), BF16),
@@ -396,22 +394,17 @@
             ((mesh_edges, 2 * node_count), BF16),
             ((3 * cycle, mesh_edges), BF16),
             ((node_count, mesh_edges), BF16),
-        ]
-        + [((edges, 2 * width), BF16)],
-        g2m_count, mesh_count, *inputs, *weights,
+            ((edges, 2 * width), BF16),
+        ],
+        g2m_count, mesh_count, indices, grid,
         scalars=(0, 1),
-        fetched=range(2, 2 + FETCHED),
-        scratch=[pltpu.VMEM((variables, width), BF16)]
-        + [pltpu.VMEM(x.shape, x.dtype) for x in inputs]
-        + [pltpu.SemaphoreType.DMA((FETCHED,))],
-    )
-    w_grid, w_gs, w_gr, w_gn, w_ms, w_mr, w_mn, mesh_in, d_out = staged[:9]
-    rows, recv_hits, recv_rows, from_hits, to_hits, from_rows, to_rows = staged[9:16]
-    halo_hits = staged[16]
-    mesh_near = lax.ppermute(mesh_in, around, ring_near)
-    mesh_far = lax.ppermute(mesh_in, around, ring_far)
+        scratch=[pltpu.VMEM((variables, width), BF16)],
+    )
+    late_mesh, rows = lax.optimization_barrier((mesh_in, rows))
+    mesh_near = lax.ppermute(late_mesh, around, ring_near)
+    mesh_far = lax.ppermute(late_mesh, around, ring_far)
     (table,) = call(
-        table_kernel, [((2 * cycle, latent), BF16)], mesh_near, mesh_far, mesh_in, w_gr
+        table_kernel, [((2 * cycle, latent), BF16)], mesh_near, mesh_far, mesh_in, stack
     )
     senders, edge_slope, part, to_near, to_far = call(
         encode_kernel,
@@ -422,7 +415,7 @@
             ((node_count, latent), BF16),
             ((node_count, latent), BF16),
         ],
-        raw_near, raw_far, halo_hits, recv_hits, recv_rows, rows, table, w_grid, w_gs,
+        raw_near, raw_far, halo_hits, recv_hits, recv_rows, rows, table, stack,
         scratch=[pltpu.VMEM((variables, 2 * width), BF16)],
     )
     from_near = lax.ppermute(to_near, around, ring_near)
@@ -430,7 +423,7 @@
     mesh_one, node_slope = call(
         node_kernel,
         [((cycle, latent), BF16), ((cycle, latent), F32)],
-        part, from_near, from_far, mesh_near, mesh_far, mesh_in, w_gn,
+        part, from_near, from_far, mesh_near, mesh_far, mesh_in, stack,
     )
     one_near = lax.ppermute(mesh_one, "band", band_near)
     one_far = lax.ppermute(mesh_one, whole, band_far)
@@ -447,12 +440,12 @@
             ((cycle, latent), BF16),
         ],
         from_hits, to_hits, from_rows, to_rows, one_near, mesh_one, one_far, d_out,
-        w_ms, w_mr, w_mn,
+        stack,
     )
     from_near = lax.ppermute(to_near, "band", band_near)
     from_far = lax.ppermute(to_far, whole, band_far)
     from_near, *dom_nodes = lax.optimization_barrier((from_near, *dom_nodes))
-    (home,) = call(home_kernel, [((node_count, latent), F32)], recv_sum, d_out, w_mr)
+    (home,) = call(home_kernel, [((node_count, latent), F32)], recv_sum, d_out, stack)
     message = (node_count + node_count // 2, latent)
     part, to_near, to_far = call(
         cotangent_kernel,
@@ -471,7 +464,7 @@
             (((lats - 1) * doms, latent, cols), BF16),
             ((doms, cycle, cols), BF16),
         ],
-        recv_hits, part, from_near, from_far, home, node_slope, w_ms, w_gn, senders, edge_slope,
+        recv_hits, part, from_near, from_far, home, node_slope, stack, senders, edge_slope,
     )
     came = [shifted(sends[i * doms : (i + 1) * doms], "lat", i + 1) for i in range(lats - 1)]
     keep, sends = call(

time: 71.9 us -> 65.1 us (0.905)
  local copies, waits for them, and re-layouts: 12.5 us -> 4.43 us
  starting transfers between devices: 14.9 us -> 17.8 us
  waiting for transfers between devices: 17.3 us -> 14.6 us
  blocking collectives: 11.7 us -> 13.1 us
  Pallas kernels: 12.7 us -> 11.9 us
  other arithmetic: 0 us -> 0.74 us
    unnamed x28 -> x20, local copies, waits for them, and re-layouts: 12.5 us -> 4.41 us
    ppermute x2, waiting for transfers between devices: 2.04 us -> 0.01 us  [the longest x1 0.01 us: on_device(): mesh_near = lax.ppermute(late_mesh, around, ring_near)]
    ppermute x1, waiting for transfers between devices: 0.01 us -> 1.93 us  [on_device(): raw_near = lax.ppermute(grid, 'band', band_near)]
    all_to_all x1, blocking collectives: 11.7 us -> 13.1 us  [on_device(): shares = lax.all_to_all(shares, 'band', 0, 0, tiled=True)]
    ppermute x1, starting transfers between devices: 1.01 us -> 2.05 us  [on_device(): one_near = lax.ppermute(mesh_one, 'band', band_near)]
    ppermute x1, waiting for transfers between devices: 1.76 us -> 0.93 us  [on_device(): one_near = lax.ppermute(mesh_one, 'band', band_near)]
    ppermute x1, starting transfers between devices: 1.08 us -> 1.91 us  [on_device(): from_near = lax.ppermute(to_near, 'band', band_near)]
    ppermute x1, waiting for transfers between devices: 2.97 us -> 2.14 us  [on_device(): from_near = lax.ppermute(to_near, 'band', band_near)]
  transfers between devices with their start and end apart: 15 -> 15, of which waited for: 7 -> 7; matrix products, arithmetic and copies ran while one was open for 0% -> 6% of each run, Pallas kernels for 7% -> 6%
where the time goes in v7:
time: 65.1 us; the launch traced here: 64.7 us
  starting transfers between devices  17.8 us (27%)
  waiting for transfers between devices  14.6 us (22%)
  blocking collectives  13.1 us (20%)
  Pallas kernels  11.9 us (18%)
  local copies, waits for them, and re-layouts  4.43 us (7%)
  between operations  2.15 us (3%)
  other arithmetic  0.74 us (1%)
    all_to_all x1, blocking collectives, on_device(): shares = lax.all_to_all(shares, 'band', 0, 0, tiled=True)  13.1 us
    pallas_call x11, Pallas kernels, call(): pl.pallas_call(kernel, out_shape=[jax.ShapeDtypeStruct(shape, dtype) for...  11.9 us
    ppermute x3, waiting for transfers between devices, shifted(): lax.ppermute(x, axis, [(i, (i + shift) % count) for i in range(count)])  5.8 us
    unnamed x20, local copies, waits for them, and re-layouts  4.41 us
    ppermute x1, starting transfers between devices, on_device(): raw_near = lax.ppermute(grid, 'band', band_near)  4.15 us
    ppermute x2, waiting for transfers between devices, on_device(): from_far = lax.ppermute(to_far, around, ring_far)  3.76 us
    ppermute x3, starting transfers between devices, shifted(): lax.ppermute(x, axis, [(i, (i + shift) % count) for i in range(count)])  3.57 us
    ppermute x2, starting transfers between devices, on_device(): from_far = lax.ppermute(to_far, around, ring_far)  3.22 us
  transfers between devices with their start and end apart: 15, of which 7 were waited for; matrix products, arithmetic and copies ran while one was open for 6% of the time, Pallas kernels for 6%

profile of v7, /device:TPU:0, one launch (start us, length us, event | category | flops | bytes accessed | tf_op | source)
XLA Modules:
  0.0 64.7 jit_solution(8946068038420668192)
XLA Ops:
  0.6 0.5 collective-permute-start.1
  1.2 4.1 %collective-permute-start = (bf16[3,227,360]{2,1,0:T(8,128)(2,1)}, bf16[3,227,360]{2,1,0:T(8,128)(2,1)S(1)}, u32[]{:S(2)}, u32[]{:S(2)}) collective-permute-start(bf16[3,227,360]{2,1,0:T(8,128)(2,1)} %bitcast.3), channel_id=1, source_target_pairs={{0,4},{4,0},{8,12},{12,8},{1,5},{5,1},{9,13},{13,9},{2,6},{6,2},{1... | collective-permute-start | bytes 1470968 | tf_op jit(solution)/shard_map/ppermute | solution.py:382
  6.6 0.7 %pad_add_fusion.indices = s32[1,1,3072]{2,1,0:T(1,128)S(1)} fusion(s32[1,1,512]{2,1,0:T(1,128)} %param.30, s32[1,1,512]{2,1,0:T(1,128)} %param.29, s32[1,1,1024]{2,1,0:T(1,128)} %param.27, s32[1,1,1024]{2,1,0:T(1,128)} %param.26), kind=kLoop, calls=%fused_computation.7 | loop fusion | flops 9216 | bytes 24576 | tf_op jit(solution)/shard_map/concatenate | solution.py:386
  7.3 1.0 %copy-done = bf16[3,360,227]{1,2,0:T(8,128)(2,1)S(1)} copy-done((bf16[3,360,227]{1,2,0:T(8,128)(2,1)S(1)}, bf16[3,360,227]{1,2,0:T(8,128)(2,1)}, u32[]{:S(2)}) %copy-start) | copy-done | bytes 490344
  8.4 1.7 %shard_map.175 = (bf16[1024,227]{1,0:T(8,128)(2,1)S(1)}, bf16[1024,128]{1,0:T(8,128)(2,1)S(1)}, bf16[64,1024]{1,0:T(8,128)(2,1)S(1)}, bf16[512,384]{1,0:T(8,128)...) custom-call(s32[1,1]{1,0:T(1,128)S(6)} %copy.25.count, ...), custom_call_target="tpu_custom_call" | custom-call | tf_op jit(solution)/shard_map/pallas_call | solution.py:327
  10.1 0.4 collective-permute-start.3
  10.5 1.2 %collective-permute-start.2 = (bf16[32,512]{1,0:T(8,128)(2,1)}, bf16[32,512]{1,0:T(8,128)(2,1)S(1)}, u32[]{:S(2)}, u32[]{:S(2)}) collective-permute-start(bf16[32,512]{1,0:T(8,128)(2,1)} %mesh_in.3), channel_id=1, source_target_pairs={{0,1},{1,0},{2,3},{3,2},{4,5},{5,4},{6,7},{7,6},{8,9},{9,8},{10,11... | collective-permute-start | bytes 98312 | tf_op jit(solution)/shard_map/ppermute | solution.py:404
  11.8 1.1 %constant_dynamic-update-slice_fusion.6 = bf16[3299,512]{1,0:T(8,128)(2,1)S(1)} fusion(bf16[512,512]{1,0:T(8,128)(2,1)} %param.18), kind=kLoop, calls=%fused_computation.6 | loop fusion | bytes 1048576
  12.8 1.1 %constant_dynamic-update-slice_fusion.5 = bf16[3299,512]{1,0:T(8,128)(2,1)S(1)} fusion(bf16[3299,512]{1,0:T(8,128)(2,1)S(1)} %constant_dynamic-update-slice_fusion.6, bf16[512,512]{1,0:T(8,128)(2,1)} %param.19), kind=kLoop, calls=%fused_computation.5 | loop fusion | bytes 1048576
  13.9 1.1 %constant_dynamic-update-slice_fusion.4 = bf16[3299,512]{1,0:T(8,128)(2,1)S(1)} fusion(bf16[3299,512]{1,0:T(8,128)(2,1)S(1)} %constant_dynamic-update-slice_fusion.5, bf16[512,512]{1,0:T(8,128)(2,1)} %param.20), kind=kLoop, calls=%fused_computation.4 | loop fusion | bytes 1048576
  15.5 1.9 %collective-permute-done.near = bf16[3,227,360]{2,1,0:T(8,128)(2,1)S(1)} collective-permute-done((bf16[3,227,360]{2,1,0:T(8,128)(2,1)}, bf16[3,227,360]{2,1,0:T(8,128)(2,1)S(1)}, u32[]{:S(2)}, u32[]{:S(2)}) %collective-permute-start) | collective-permute-done | bytes 490352 | tf_op jit(solution)/shard_map/ppermute | solution.py:382
  17.4 5.1 %shard_map.177 = (bf16[1024,512]{1,0:T(8,128)(2,1)S(1)}, bf16[1024,512]{1,0:T(8,128)(2,1)S(1)}, f32[64,512]{1,0:T(8,128)S(1)}, bf16[32,512]{1,0:T(8,128)(2,1)S(1)}, bf16[32,512]{1,0:T(8,128)(2,1)S(1)}) custom-call(bf16[3,227,360]{2,1,0:T(8,128)(2,1)S(1)} %collective-permute-done.near, bf16[3,227,360]{2,1,0:T(8,128)(2,1)S(1)} %collective-permute-done.1.far, ...), custom_call_target="tpu_custom_call" | custom-call | tf_op jit(solution)/shard_map/pallas_call | solution.py:327
  22.6 1.6 %collective-permute-start.5 = (bf16[32,512]{1,0:T(8,128)(2,1)S(1)}, bf16[32,512]{1,0:T(8,128)(2,1)S(1)}, u32[]{:S(2)}, u32[]{:S(2)}) collective-permute-start(bf16[32,512]{1,0:T(8,128)(2,1)S(1)} %get-tuple-element.49), channel_id=1, source_target_pairs={{0,3},{1,2},{2,1},{3,0},{4,7},{5,6},{6,5},{7,4},{8,11},{9,10},{10,... | collective-permute-start | bytes 98312 | tf_op jit(solution)/shard_map/ppermute | solution.py:422
  24.2 1.8 %collective-permute-done.5.far = bf16[32,512]{1,0:T(8,128)(2,1)S(1)} collective-permute-done((bf16[32,512]{1,0:T(8,128)(2,1)S(1)}, bf16[32,512]{1,0:T(8,128)(2,1)S(1)}, u32[]{:S(2)}, u32[]{:S(2)}) %collective-permute-start.5) | collective-permute-done | bytes 32800 | tf_op jit(solution)/shard_map/ppermute | solution.py:422
  26.0 0.2 shard_map.178
  26.2 0.5 collective-permute-start.7
  26.7 2.1 %collective-permute-start.6 = (bf16[64,512]{1,0:T(8,128)(2,1)S(1)}, bf16[64,512]{1,0:T(8,128)(2,1)S(1)}, u32[]{:S(2)}, u32[]{:S(2)}) collective-permute-start(bf16[64,512]{1,0:T(8,128)(2,1)S(1)} %get-tuple-element.50.own.nodes), channel_id=1, source_target_pairs={{0,4},{4,0},{8,12},{12,8},{1,5},{5,1},{9,13},{13,9},{2,6},{6,2},{1... | collective-permute-start | bytes 196616 | tf_op jit(solution)/shard_map/ppermute | solution.py:428
  28.8 1.5 %collective-permute-start.9 = (bf16[64,512]{1,0:T(8,128)(2,1)S(1)}, bf16[64,512]{1,0:T(8,128)(2,1)S(1)}, u32[]{:S(2)}, u32[]{:S(2)}) collective-permute-start(bf16[64,512]{1,0:T(8,128)(2,1)S(1)} %get-tuple-element.50.own.nodes), channel_id=1, source_target_pairs={{0,2},{2,0},{1,3},{3,1},{4,6},{6,4},{5,7},{7,5},{8,10},{10,8},{9,1... | collective-permute-start | bytes 196616 | tf_op jit(solution)/shard_map/ppermute | solution.py:359
  30.3 0.9 %collective-permute-done.6.near = bf16[64,512]{1,0:T(8,128)(2,1)S(1)} collective-permute-done((bf16[64,512]{1,0:T(8,128)(2,1)S(1)}, bf16[64,512]{1,0:T(8,128)(2,1)S(1)}, u32[]{:S(2)}, u32[]{:S(2)}) %collective-permute-start.6) | collective-permute-done | bytes 65568 | tf_op jit(solution)/shard_map/ppermute | solution.py:428
  31.2 2.0 %shard_map.179 = (bf16[32,512]{1,0:T(8,128)(2,1)}, f32[192,512]{1,0:T(8,128)S(1)}, bf16[32,512]{1,0:T(8,128)(2,1)S(1)}, bf16[64,512]{1,0:T(8,128)(2,1)S(1)}, bf16[64,512]{1,0:T(8,128)(2,1)S(1)}) custom-call(bf16[512,384]{1,0:T(8,128)(2,1)S(1)} %get-tuple-element.37.from_hits, bf16[512,64]{1,0:T(8,128)(2,1)S(1)} %get-tuple-element.38.to_hits, ...), custom_call_target="tpu_custom_call" | custom-call | tf_op jit(solution)/shard_map/pallas_call | solution.py:327
  33.2 1.9 %collective-permute-start.8 = (bf16[64,512]{1,0:T(8,128)(2,1)S(1)}, bf16[64,512]{1,0:T(8,128)(2,1)S(1)}, u32[]{:S(2)}, u32[]{:S(2)}) collective-permute-start(bf16[64,512]{1,0:T(8,128)(2,1)S(1)} %get-tuple-element.53), channel_id=1, source_target_pairs={{0,4},{4,0},{8,12},{12,8},{1,5},{5,1},{9,13},{13,9},{2,6},{6,2},{1... | collective-permute-start | bytes 196616 | tf_op jit(solution)/shard_map/ppermute | solution.py:445
  35.4 2.1 %collective-permute-done.8.near = bf16[64,512]{1,0:T(8,128)(2,1)S(1)} collective-permute-done((bf16[64,512]{1,0:T(8,128)(2,1)S(1)}, bf16[64,512]{1,0:T(8,128)(2,1)S(1)}, u32[]{:S(2)}, u32[]{:S(2)}) %collective-permute-start.8) | collective-permute-done | bytes 65568 | tf_op jit(solution)/shard_map/ppermute | solution.py:445
  37.6 1.6 %collective-permute-start.12 = (bf16[48,512]{1,0:T(8,128)(2,1)S(1)}, bf16[48,512]{1,0:T(8,128)(2,1)S(1)}, u32[]{:S(2)}, u32[]{:S(2)}) collective-permute-start(bf16[48,512]{1,0:T(8,128)(2,1)S(1)} %get-tuple-element.59), channel_id=1, source_target_pairs={{0,3},{1,2},{2,1},{3,0},{4,7},{5,6},{6,5},{7,4},{8,11},{9,10},{10,... | collective-permute-start | bytes 147464 | tf_op jit(solution)/shard_map/ppermute | solution.py:456
  39.2 2.0 %collective-permute-done.12.far = bf16[48,512]{1,0:T(8,128)(2,1)S(1)} collective-permute-done((bf16[48,512]{1,0:T(8,128)(2,1)S(1)}, bf16[48,512]{1,0:T(8,128)(2,1)S(1)}, u32[]{:S(2)}, u32[]{:S(2)}) %collective-permute-start.12) | collective-permute-done | bytes 49184 | tf_op jit(solution)/shard_map/ppermute | solution.py:456
  41.2 1.4 %shard_map.182 = (f32[2,512,128]{2,1,0:T(8,128)S(1)}, bf16[2,512,128]{2,1,0:T(8,128)(2,1)S(1)}, bf16[2,64,128]{2,1,0:T(8,128)(2,1)S(1)}) custom-call(bf16[1024,128]{1,0:T(8,128)(2,1)S(1)} %get-tuple-element.42.recv_hits, f32[64,512]{1,0:T(8,128)S(1)} %get-tuple-element.57.part, bf16[48,512]{1,0:T(8,128)(2,1)S(1)} %collective-permute-done.11.near, ...), custom_call_target="tpu_custom_call" | custom-call | tf_op jit(solution)/shard_map/pallas_call | solution.py:327
  42.7 0.5 collective-permute-start.13
  43.2 1.2 %collective-permute-done.13.refs_0_ = bf16[2,512,128]{2,1,0:T(8,128)(2,1)S(1)} collective-permute-done((bf16[2,512,128]{2,1,0:T(8,128)(2,1)S(1)}, bf16[2,512,128]{2,1,0:T(8,128)(2,1)S(1)}, u32[]{:S(2)}, u32[]{:S(2)}) %collective-permute-start.13) | collective-permute-done | bytes 262176 | tf_op jit(solution)/shard_map/ppermute | solution.py:359
  44.4 1.6 %collective-permute-start.14 = (bf16[576,128]{1,0:T(8,128)(2,1)S(1)}, bf16[576,128]{1,0:T(8,128)(2,1)S(1)}, u32[]{:S(2)}, u32[]{:S(2)}) collective-permute-start(bf16[576,128]{1,0:T(8,128)(2,1)S(1)} %bitcast.5), channel_id=1, source_target_pairs={{0,2},{2,0},{1,3},{3,1},{4,6},{6,4},{5,7},{7,5},{8,10},{10,8},{9,1... | collective-permute-start | bytes 442376 | tf_op jit(solution)/shard_map/ppermute | solution.py:359
  46.0 4.6 %collective-permute-done.14.refs_0_ = bf16[576,128]{1,0:T(8,128)(2,1)S(1)} collective-permute-done((bf16[576,128]{1,0:T(8,128)(2,1)S(1)}, bf16[576,128]{1,0:T(8,128)(2,1)S(1)}, u32[]{:S(2)}, u32[]{:S(2)}) %collective-permute-start.14) | collective-permute-done | bytes 147488 | tf_op jit(solution)/shard_map/ppermute | solution.py:359
  50.6 0.3 shard_map.184
  50.9 13.1 %all_to_all.5.shares = bf16[4,2,128,128]{3,2,1,0:T(8,128)(2,1)S(1)} all-to-all(bf16[4,2,128,128]{3,2,1,0:T(8,128)(2,1)S(1)} %shard_map.184), channel_id=1, replica_groups=mesh['groups'=2,'band'=4,'dom'=2,'lat'=2] {'band'}, dimensions={0} | all-to-all | bytes 524288 | tf_op jit(solution)/shard_map/all_to_all | solution.py:481
  64.0 0.7 %shard_map.185 = (f32[128,128]{1,0:T(8,128)}, f32[128,128]{1,0:T(8,128)}) custom-call(bf16[4,2,128,128]{3,2,1,0:T(8,128)(2,1)S(1)} %all_to_all.5.shares), custom_call_target="tpu_custom_call" | custom-call | tf_op jit(solution)/shard_map/pallas_call | solution.py:327
  (32 shorter events, 0.9 us)
Async XLA Ops:
  0.6 14.8 %collective-permute-start.1 = (bf16[3,227,360]{2,1,0:T(8,128)(2,1)}, bf16[3,227,360]{2,1,0:T(8,128)(2,1)S(1)}, u32[]{:S(2)}, u32[]{:S(2)}) collective-permute-start(bf16[3,227,360]{2,1,0:T(8,128)(2,1)} %bitcast.2), channel_id=1, source_target_pairs={{0,1},{1,0},{2,3},{3,2},{4,8},{5,9},{6,10},{7,11},{8,4},{9,5},{10,... | collective-permute-start | bytes 1470968 | tf_op jit(solution)/shard_map/ppermute | solution.py:383
  1.2 16.3 %collective-permute-start = (bf16[3,227,360]{2,1,0:T(8,128)(2,1)}, bf16[3,227,360]{2,1,0:T(8,128)(2,1)S(1)}, u32[]{:S(2)}, u32[]{:S(2)}) collective-permute-start(bf16[3,227,360]{2,1,0:T(8,128)(2,1)} %bitcast.3), channel_id=1, source_target_pairs={{0,4},{4,0},{8,12},{12,8},{1,5},{5,1},{9,13},{13,9},{2,6},{6,2},{1... | collective-permute-start | bytes 1470968 | tf_op jit(solution)/shard_map/ppermute | solution.py:382
  7.3 1.0 %copy-start = (bf16[3,360,227]{1,2,0:T(8,128)(2,1)S(1)}, bf16[3,360,227]{1,2,0:T(8,128)(2,1)}, u32[]{:S(2)}) copy-start(bf16[3,360,227]{1,2,0:T(8,128)(2,1)} %param.16) | copy-start | bytes 1470964
  8.4 6.6 %copy-start.3 = (bf16[512,512]{1,0:T(8,128)(2,1)S(1)}, bf16[512,512]{1,0:T(8,128)(2,1)}, u32[]{:S(2)}) copy-start(bf16[512,512]{1,0:T(8,128)(2,1)} %param.21) | copy-start | bytes 1572868
  8.4 6.7 %copy-start.4 = (bf16[512,512]{1,0:T(8,128)(2,1)S(1)}, bf16[512,512]{1,0:T(8,128)(2,1)}, u32[]{:S(2)}) copy-start(bf16[512,512]{1,0:T(8,128)(2,1)} %param.22) | copy-start | bytes 1572868
  8.4 6.7 %copy-start.5 = (bf16[512,512]{1,0:T(8,128)(2,1)S(1)}, bf16[512,512]{1,0:T(8,128)(2,1)}, u32[]{:S(2)}) copy-start(bf16[512,512]{1,0:T(8,128)(2,1)} %param.23) | copy-start | bytes 1572868
  8.4 6.8 %copy-start.6 = (bf16[227,512]{1,0:T(8,128)(2,1)S(1)}, bf16[227,512]{1,0:T(8,128)(2,1)}, u32[]{:S(2)}) copy-start(bf16[227,512]{1,0:T(8,128)(2,1)} %param.17) | copy-start | bytes 697348
  10.1 5.2 %copy-start.1 = (bf16[32,512]{1,0:T(8,128)(2,1)S(1)}, bf16[32,512]{1,0:T(8,128)(2,1)}, u32[]{:S(2)}) copy-start(bf16[32,512]{1,0:T(8,128)(2,1)} %mesh_in.3) | copy-start | bytes 98308
  10.1 5.1 %collective-permute-start.3 = (bf16[32,512]{1,0:T(8,128)(2,1)}, bf16[32,512]{1,0:T(8,128)(2,1)S(1)}, u32[]{:S(2)}, u32[]{:S(2)}) collective-permute-start(bf16[32,512]{1,0:T(8,128)(2,1)} %mesh_in.3), channel_id=1, source_target_pairs={{0,3},{1,2},{2,1},{3,0},{4,7},{5,6},{6,5},{7,4},{8,11},{9,10},{10,... | collective-permute-start | bytes 98312 | tf_op jit(solution)/shard_map/ppermute | solution.py:405
  10.5 4.7 %collective-permute-start.2 = (bf16[32,512]{1,0:T(8,128)(2,1)}, bf16[32,512]{1,0:T(8,128)(2,1)S(1)}, u32[]{:S(2)}, u32[]{:S(2)}) collective-permute-start(bf16[32,512]{1,0:T(8,128)(2,1)} %mesh_in.3), channel_id=1, source_target_pairs={{0,1},{1,0},{2,3},{3,2},{4,5},{5,4},{6,7},{7,6},{8,9},{9,8},{10,11... | collective-permute-start | bytes 98312 | tf_op jit(solution)/shard_map/ppermute | solution.py:404
  22.5 8.7 %copy-start.2 = (bf16[32,512]{1,0:T(8,128)(2,1)S(1)}, bf16[32,512]{1,0:T(8,128)(2,1)}, u32[]{:S(2)}) copy-start(bf16[32,512]{1,0:T(8,128)(2,1)} %d_out.3) | copy-start | bytes 98308
  22.5 1.7 %collective-permute-start.4 = (bf16[32,512]{1,0:T(8,128)(2,1)S(1)}, bf16[32,512]{1,0:T(8,128)(2,1)S(1)}, u32[]{:S(2)}, u32[]{:S(2)}) collective-permute-start(bf16[32,512]{1,0:T(8,128)(2,1)S(1)} %get-tuple-element.48), channel_id=1, source_target_pairs={{0,1},{1,0},{2,3},{3,2},{4,5},{5,4},{6,7},{7,6},{8,9},{9,8},{10,11... | collective-permute-start | bytes 98312 | tf_op jit(solution)/shard_map/ppermute | solution.py:421
  22.6 3.4 %collective-permute-start.5 = (bf16[32,512]{1,0:T(8,128)(2,1)S(1)}, bf16[32,512]{1,0:T(8,128)(2,1)S(1)}, u32[]{:S(2)}, u32[]{:S(2)}) collective-permute-start(bf16[32,512]{1,0:T(8,128)(2,1)S(1)} %get-tuple-element.49), channel_id=1, source_target_pairs={{0,3},{1,2},{2,1},{3,0},{4,7},{5,6},{6,5},{7,4},{8,11},{9,10},{10,... | collective-permute-start | bytes 98312 | tf_op jit(solution)/shard_map/ppermute | solution.py:422
  26.2 4.1 %collective-permute-start.7 = (bf16[64,512]{1,0:T(8,128)(2,1)S(1)}, bf16[64,512]{1,0:T(8,128)(2,1)S(1)}, u32[]{:S(2)}, u32[]{:S(2)}) collective-permute-start(bf16[64,512]{1,0:T(8,128)(2,1)S(1)} %get-tuple-element.50.own.nodes), channel_id=1, source_target_pairs={{0,1},{1,0},{2,3},{3,2},{4,8},{5,9},{6,10},{7,11},{8,4},{9,5},{10,... | collective-permute-start | bytes 196616 | tf_op jit(solution)/shard_map/ppermute | solution.py:429
  26.7 4.5 %collective-permute-start.6 = (bf16[64,512]{1,0:T(8,128)(2,1)S(1)}, bf16[64,512]{1,0:T(8,128)(2,1)S(1)}, u32[]{:S(2)}, u32[]{:S(2)}) collective-permute-start(bf16[64,512]{1,0:T(8,128)(2,1)S(1)} %get-tuple-element.50.own.nodes), channel_id=1, source_target_pairs={{0,4},{4,0},{8,12},{12,8},{1,5},{5,1},{9,13},{13,9},{2,6},{6,2},{1... | collective-permute-start | bytes 196616 | tf_op jit(solution)/shard_map/ppermute | solution.py:428
  28.8 6.6 %collective-permute-start.9 = (bf16[64,512]{1,0:T(8,128)(2,1)S(1)}, bf16[64,512]{1,0:T(8,128)(2,1)S(1)}, u32[]{:S(2)}, u32[]{:S(2)}) collective-permute-start(bf16[64,512]{1,0:T(8,128)(2,1)S(1)} %get-tuple-element.50.own.nodes), channel_id=1, source_target_pairs={{0,2},{2,0},{1,3},{3,1},{4,6},{6,4},{5,7},{7,5},{8,10},{10,8},{9,1... | collective-permute-start | bytes 196616 | tf_op jit(solution)/shard_map/ppermute | solution.py:359
  33.2 4.3 %collective-permute-start.8 = (bf16[64,512]{1,0:T(8,128)(2,1)S(1)}, bf16[64,512]{1,0:T(8,128)(2,1)S(1)}, u32[]{:S(2)}, u32[]{:S(2)}) collective-permute-start(bf16[64,512]{1,0:T(8,128)(2,1)S(1)} %get-tuple-element.53), channel_id=1, source_target_pairs={{0,4},{4,0},{8,12},{12,8},{1,5},{5,1},{9,13},{13,9},{2,6},{6,2},{1... | collective-permute-start | bytes 196616 | tf_op jit(solution)/shard_map/ppermute | solution.py:445
  35.1 2.4 %collective-permute-start.10 = (bf16[64,512]{1,0:T(8,128)(2,1)S(1)}, bf16[64,512]{1,0:T(8,128)(2,1)S(1)}, u32[]{:S(2)}, u32[]{:S(2)}) collective-permute-start(bf16[64,512]{1,0:T(8,128)(2,1)S(1)} %get-tuple-element.55), channel_id=1, source_target_pairs={{0,1},{1,0},{2,3},{3,2},{4,8},{5,9},{6,10},{7,11},{8,4},{9,5},{10,... | collective-permute-start | bytes 196616 | tf_op jit(solution)/shard_map/ppermute | solution.py:446
  37.6 1.7 %collective-permute-start.11 = (bf16[48,512]{1,0:T(8,128)(2,1)S(1)}, bf16[48,512]{1,0:T(8,128)(2,1)S(1)}, u32[]{:S(2)}, u32[]{:S(2)}) collective-permute-start(bf16[48,512]{1,0:T(8,128)(2,1)S(1)} %get-tuple-element.58), channel_id=1, source_target_pairs={{0,1},{1,0},{2,3},{3,2},{4,5},{5,4},{6,7},{7,6},{8,9},{9,8},{10,11... | collective-permute-start | bytes 147464 | tf_op jit(solution)/shard_map/ppermute | solution.py:455
  37.6 3.6 %collective-permute-start.12 = (bf16[48,512]{1,0:T(8,128)(2,1)S(1)}, bf16[48,512]{1,0:T(8,128)(2,1)S(1)}, u32[]{:S(2)}, u32[]{:S(2)}) collective-permute-start(bf16[48,512]{1,0:T(8,128)(2,1)S(1)} %get-tuple-element.59), channel_id=1, source_target_pairs={{0,3},{1,2},{2,1},{3,0},{4,7},{5,6},{6,5},{7,4},{8,11},{9,10},{10,... | collective-permute-start | bytes 147464 | tf_op jit(solution)/shard_map/ppermute | solution.py:456
  42.7 1.7 %collective-permute-start.13 = (bf16[2,512,128]{2,1,0:T(8,128)(2,1)S(1)}, bf16[2,512,128]{2,1,0:T(8,128)(2,1)S(1)}, u32[]{:S(2)}, u32[]{:S(2)}) collective-permute-start(bf16[2,512,128]{2,1,0:T(8,128)(2,1)S(1)} %get-tuple-element.65), channel_id=1, source_target_pairs={{0,1},{1,0},{2,3},{3,2},{4,5},{5,4},{6,7},{7,6},{8,9},{9,8},{10,11... | collective-permute-start | bytes 786440 | tf_op jit(solution)/shard_map/ppermute | solution.py:359
  44.4 6.2 %collective-permute-start.14 = (bf16[576,128]{1,0:T(8,128)(2,1)S(1)}, bf16[576,128]{1,0:T(8,128)(2,1)S(1)}, u32[]{:S(2)}, u32[]{:S(2)}) collective-permute-start(bf16[576,128]{1,0:T(8,128)(2,1)S(1)} %bitcast.5), channel_id=1, source_target_pairs={{0,2},{2,0},{1,3},{3,1},{4,6},{6,4},{5,7},{7,5},{8,10},{10,8},{9,1... | collective-permute-start | bytes 442376 | tf_op jit(solution)/shard_map/ppermute | solution.py:359

commit v8 on v7

--- a/solution.py
+++ b/solution.py
@@ -217,23 +217,19 @@
     far_out[...] = sums[2 * cycle :].astype(BF16)
 
 
-def split_store(gradient, keep, sends):
-    doms, _, cols = keep.shape
-    lats = sends.shape[0] // doms + 1
+def columns_of(x, shift, doms, lats):
+    cols = x.shape[1] // (doms * lats)
     me = lax.axis_index("lat")
+    picked = []
     for dom in range(doms):
         block = [
-            gradient[:, (dom * lats + i) * cols : (dom * lats + i + 1) * cols]
-            for i in range(lats)
+            x[:, (dom * lats + i) * cols : (dom * lats + i + 1) * cols] for i in range(lats)
         ]
-        for shift in range(lats):
-            pick = block[shift]
-            for i in range(1, lats):
-                pick = jnp.where(me == i, block[(shift + i) % lats], pick)
-            if shift == 0:
-                keep[dom] = pick
-            else:
-                sends[(shift - 1) * doms + dom] = pick.astype(BF16)
+        pick = block[shift]
+        for i in range(1, lats):
+            pick = jnp.where(me == i, block[(shift + i) % lats], pick)
+        picked.append(pick)
+    return jnp.concatenate(picked, axis=1)
 
 
 def home_kernel(recv_sum, d_out, stack, home_out):
@@ -255,7 +251,7 @@
 
 def encode_grad_kernel(
     recv_hits, part, near, far, home, node_slope, stack, senders, edge_slope,
-    keep, sends, total_out,
+    sends, kept_slope, total_out,
 ):
     half = part.shape[0] // 2
     even = even_on("lat")
@@ -268,16 +264,23 @@
     gate_one = (cot * node_slope[...]).astype(BF16)
     back = jnp.concatenate(halves(mm_nt(gate_one, weight(stack, GN))), axis=0)
     slope = (mm(recv_hits[...], back) * edge_slope[...].astype(F32)).astype(BF16)
-    split_store(mm_tn(senders[...], slope), keep, sends)
     doms, _, cols = total_out.shape
-    lats = total.shape[1] // cols // doms
-    me = lax.axis_index("lat")
+    lats = slope.shape[1] // cols // doms
+    for shift in range(1, lats):
+        gradient = mm_tn(senders[...], columns_of(slope, shift, doms, lats)).astype(BF16)
+        for dom in range(doms):
+            sends[(shift - 1) * doms + dom] = gradient[:, dom * cols : (dom + 1) * cols]
+    kept_slope[...] = columns_of(slope, 0, doms, lats)
+    kept_total = columns_of(total, 0, doms, lats)
     for dom in range(doms):
-        pick = total[:, dom * lats * cols : (dom * lats + 1) * cols]
-        for i in range(1, lats):
-            at = (dom * lats + i) * cols
-            pick = jnp.where(me == i, total[:, at : at + cols], pick)
-        total_out[dom] = pick
+        total_out[dom] = kept_total[:, dom * cols : (dom + 1) * cols]
+
+
+def kept_grad_kernel(senders, kept_slope, keep):
+    gradient = mm_tn(senders[...], kept_slope[...])
+    cols = keep.shape[2]
+    for dom in range(keep.shape[0]):
+        keep[dom] = gradient[:, dom * cols : (dom + 1) * cols]
 
 
 def over_lat_kernel(keep, total, *refs):
@@ -297,8 +300,9 @@
 
 
 def over_dom_kernel(keep, total, nodes, *refs):
-    *came, out = refs
-    bands, _, rows, _ = out.shape
+    rows = keep.shape[0] // lax.axis_size("band")
+    doms = lax.axis_size("dom")
+    came, (own_out, *sends_out, sums) = refs[: 2 * (doms - 1)], refs[2 * (doms - 1) :]
     latent = keep.shape[0]
     came, came_nodes = came[: len(came) // 2], came[len(came) // 2 :]
     first = keep[...]
@@ -306,16 +310,22 @@
     for part, part_nodes in zip(came, came_nodes):
         first = first + part[:latent].astype(F32)
         second = second + mm_tn(part_nodes[...], part[latent:])
-    for k, block in enumerate((first, second)):
-        for band in range(bands):
-            out[band, k] = block[band * rows : (band + 1) * rows].astype(BF16)
-
-
-def over_band_kernel(shares, first_out, second_out):
+    sums[0] = first
+    sums[1] = second
+    me = lax.axis_index("band")
+    for k in range(2):
+        own_out[k] = sums[k, pl.ds(pl.multiple_of(me * rows, rows), rows)]
+        for i, out in enumerate(sends_out):
+            at = pl.multiple_of(lax.bitwise_xor(me, i + 1) * rows, rows)
+            out[k] = sums[k, pl.ds(at, rows)].astype(BF16)
+
+
+def over_band_kernel(own, *refs):
+    *came, first_out, second_out = refs
     for k, out in enumerate((first_out, second_out)):
-        total = shares[0, k].astype(F32)
-        for band in range(1, shares.shape[0]):
-            total = total + shares[band, k].astype(F32)
+        total = own[k]
+        for part in came:
+            total = total + part[k].astype(F32)
         out[...] = total
 
 
@@ -457,30 +467,35 @@
 
     cols = latent // sectors
     rows = latent // bands
-    keep, sends, total = call(
+    sends, kept_slope, total = call(
         encode_grad_kernel,
         [
-            ((doms, latent, cols), F32),
             (((lats - 1) * doms, latent, cols), BF16),
+            ((edges, doms * cols), BF16),
             ((doms, cycle, cols), BF16),
         ],
         recv_hits, part, from_near, from_far, home, node_slope, stack, senders, edge_slope,
     )
     came = [shifted(sends[i * doms : (i + 1) * doms], "lat", i + 1) for i in range(lats - 1)]
+    (keep,) = call(kept_grad_kernel, [((doms, latent, cols), F32)], senders, kept_slope)
     keep, sends = call(
         over_lat_kernel,
         [((latent, cols), F32), ((doms - 1, latent + cycle, cols), BF16)],
         keep, total, *came,
     )
     came = [shifted(sends[i], "dom", i + 1) for i in range(doms - 1)]
-    (shares,) = call(
+    own, *sends = call(
         over_dom_kernel,
-        [((bands, 2, rows, cols), BF16)],
+        [((2, rows, cols), F32)] + [((2, rows, cols), BF16)] * (bands - 1),
         keep, total, mesh_one, *came, *dom_nodes,
-    )
-    shares = lax.all_to_all(shares, "band", 0, 0, tiled=True)
+        scratch=[pltpu.VMEM((2, latent, cols), F32)],
+    )
+    came = [
+        lax.ppermute(sends[i], "band", [(b, b ^ (i + 1)) for b in range(bands)])
+        for i in reversed(range(bands - 1))
+    ]
     tile = ((rows, cols), F32)
-    grad_gs, grad_ms = call(over_band_kernel, [tile, tile], shares)
+    grad_gs, grad_ms = call(over_band_kernel, [tile, tile], own, *came)
     return mesh_out, grad_gs, grad_ms
 
 

time: 65.1 us -> 61.6 us (0.946)
  blocking collectives: 13.1 us -> 0 us
  waiting for transfers between devices: 14.6 us -> 19.2 us
  starting transfers between devices: 17.8 us -> 22.2 us
    all_to_all x1 -> x0, blocking collectives: 13.1 us -> none  [on_device(): shares = lax.all_to_all(shares, 'band', 0, 0, tiled=True)]
    ppermute x0 -> x3, waiting for transfers between devices: none -> 5.11 us  [on_device(): lax.ppermute(sends[i], 'band', [(b, b ^ i + 1) for b in range(bands)])]
    ppermute x0 -> x3, starting transfers between devices: none -> 4.45 us  [on_device(): lax.ppermute(sends[i], 'band', [(b, b ^ i + 1) for b in range(bands)])]
    pallas_call x11 -> x12, Pallas kernels: 11.9 us -> 12.5 us  [call(): pl.pallas_call(kernel, out_shape=[jax.ShapeDtypeStruct(shape, dtype) for...]
  transfers between devices with their start and end apart: 15 -> 18, of which waited for: 7 -> 9; matrix products, arithmetic and copies ran while one was open for 6% -> 7% of each run, Pallas kernels for 6% -> 7%
where the time goes in v8:
time: 61.6 us; the launch traced here: 61.3 us
  starting transfers between devices  22.2 us (36%)
  waiting for transfers between devices  19.2 us (31%)
  Pallas kernels  12.5 us (20%)
  local copies, waits for them, and re-layouts  4.43 us (7%)
  between operations  2.17 us (4%)
  other arithmetic  0.74 us (1%)
    pallas_call x12, Pallas kernels, call(): pl.pallas_call(kernel, out_shape=[jax.ShapeDtypeStruct(shape, dtype) for...  12.5 us
    ppermute x3, waiting for transfers between devices, shifted(): lax.ppermute(x, axis, [(i, (i + shift) % count) for i in range(count)])  5.32 us
    ppermute x3, waiting for transfers between devices, on_device(): lax.ppermute(sends[i], 'band', [(b, b ^ i + 1) for b in range(bands)])  5.11 us
    ppermute x3, starting transfers between devices, on_device(): lax.ppermute(sends[i], 'band', [(b, b ^ i + 1) for b in range(bands)])  4.45 us
    unnamed x20, local copies, waits for them, and re-layouts  4.41 us
    ppermute x1, starting transfers between devices, on_device(): raw_near = lax.ppermute(grid, 'band', band_near)  4.15 us
    ppermute x2, waiting for transfers between devices, on_device(): from_far = lax.ppermute(to_far, around, ring_far)  3.76 us
    ppermute x3, starting transfers between devices, shifted(): lax.ppermute(x, axis, [(i, (i + shift) % count) for i in range(count)])  3.57 us
  transfers between devices with their start and end apart: 18, of which 9 were waited for; matrix products, arithmetic and copies ran while one was open for 7% of the time, Pallas kernels for 7%

profile of v8, /device:TPU:0, one launch (start us, length us, event | category | flops | bytes accessed | tf_op | source)
XLA Modules:
  0.0 61.3 jit_solution(7568613638885101304)
XLA Ops:
  0.6 0.5 collective-permute-start.1
  1.2 4.1 %collective-permute-start = (bf16[3,227,360]{2,1,0:T(8,128)(2,1)}, bf16[3,227,360]{2,1,0:T(8,128)(2,1)S(1)}, u32[]{:S(2)}, u32[]{:S(2)}) collective-permute-start(bf16[3,227,360]{2,1,0:T(8,128)(2,1)} %bitcast.3), channel_id=1, source_target_pairs={{0,4},{4,0},{8,12},{12,8},{1,5},{5,1},{9,13},{13,9},{2,6},{6,2},{1... | collective-permute-start | bytes 1470968 | tf_op jit(solution)/shard_map/ppermute | solution.py:392
  6.6 0.7 %pad_add_fusion.indices = s32[1,1,3072]{2,1,0:T(1,128)S(1)} fusion(s32[1,1,512]{2,1,0:T(1,128)} %param.30, s32[1,1,512]{2,1,0:T(1,128)} %param.29, s32[1,1,1024]{2,1,0:T(1,128)} %param.27, s32[1,1,1024]{2,1,0:T(1,128)} %param.26), kind=kLoop, calls=%fused_computation.7 | loop fusion | flops 9216 | bytes 24576 | tf_op jit(solution)/shard_map/concatenate | solution.py:396
  7.3 1.0 %copy-done = bf16[3,360,227]{1,2,0:T(8,128)(2,1)S(1)} copy-done((bf16[3,360,227]{1,2,0:T(8,128)(2,1)S(1)}, bf16[3,360,227]{1,2,0:T(8,128)(2,1)}, u32[]{:S(2)}) %copy-start) | copy-done | bytes 490344
  8.4 1.7 %shard_map.175 = (bf16[1024,227]{1,0:T(8,128)(2,1)S(1)}, bf16[1024,128]{1,0:T(8,128)(2,1)S(1)}, bf16[64,1024]{1,0:T(8,128)(2,1)S(1)}, bf16[512,384]{1,0:T(8,128)...) custom-call(s32[1,1]{1,0:T(1,128)S(6)} %copy.25.count, ...), custom_call_target="tpu_custom_call" | custom-call | tf_op jit(solution)/shard_map/pallas_call | solution.py:337
  10.5 1.2 %collective-permute-start.2 = (bf16[32,512]{1,0:T(8,128)(2,1)}, bf16[32,512]{1,0:T(8,128)(2,1)S(1)}, u32[]{:S(2)}, u32[]{:S(2)}) collective-permute-start(bf16[32,512]{1,0:T(8,128)(2,1)} %mesh_in.3), channel_id=1, source_target_pairs={{0,1},{1,0},{2,3},{3,2},{4,5},{5,4},{6,7},{7,6},{8,9},{9,8},{10,11... | collective-permute-start | bytes 98312 | tf_op jit(solution)/shard_map/ppermute | solution.py:414
  11.8 1.1 %constant_dynamic-update-slice_fusion.6 = bf16[3299,512]{1,0:T(8,128)(2,1)S(1)} fusion(bf16[512,512]{1,0:T(8,128)(2,1)} %param.18), kind=kLoop, calls=%fused_computation.6 | loop fusion | bytes 1048576
  12.8 1.1 %constant_dynamic-update-slice_fusion.5 = bf16[3299,512]{1,0:T(8,128)(2,1)S(1)} fusion(bf16[3299,512]{1,0:T(8,128)(2,1)S(1)} %constant_dynamic-update-slice_fusion.6, bf16[512,512]{1,0:T(8,128)(2,1)} %param.19), kind=kLoop, calls=%fused_computation.5 | loop fusion | bytes 1048576
  13.9 1.1 %constant_dynamic-update-slice_fusion.4 = bf16[3299,512]{1,0:T(8,128)(2,1)S(1)} fusion(bf16[3299,512]{1,0:T(8,128)(2,1)S(1)} %constant_dynamic-update-slice_fusion.5, bf16[512,512]{1,0:T(8,128)(2,1)} %param.20), kind=kLoop, calls=%fused_computation.4 | loop fusion | bytes 1048576
  15.5 1.9 %collective-permute-done.near = bf16[3,227,360]{2,1,0:T(8,128)(2,1)S(1)} collective-permute-done((bf16[3,227,360]{2,1,0:T(8,128)(2,1)}, bf16[3,227,360]{2,1,0:T(8,128)(2,1)S(1)}, u32[]{:S(2)}, u32[]{:S(2)}) %collective-permute-start) | collective-permute-done | bytes 490352 | tf_op jit(solution)/shard_map/ppermute | solution.py:392
  17.4 5.1 %shard_map.177 = (bf16[1024,512]{1,0:T(8,128)(2,1)S(1)}, bf16[1024,512]{1,0:T(8,128)(2,1)S(1)}, f32[64,512]{1,0:T(8,128)S(1)}, bf16[32,512]{1,0:T(8,128)(2,1)S(1)}, bf16[32,512]{1,0:T(8,128)(2,1)S(1)}) custom-call(bf16[3,227,360]{2,1,0:T(8,128)(2,1)S(1)} %collective-permute-done.near, bf16[3,227,360]{2,1,0:T(8,128)(2,1)S(1)} %collective-permute-done.1.far, ...), custom_call_target="tpu_custom_call" | custom-call | tf_op jit(solution)/shard_map/pallas_call | solution.py:337
  22.6 1.6 %collective-permute-start.5 = (bf16[32,512]{1,0:T(8,128)(2,1)S(1)}, bf16[32,512]{1,0:T(8,128)(2,1)S(1)}, u32[]{:S(2)}, u32[]{:S(2)}) collective-permute-start(bf16[32,512]{1,0:T(8,128)(2,1)S(1)} %get-tuple-element.53), channel_id=1, source_target_pairs={{0,3},{1,2},{2,1},{3,0},{4,7},{5,6},{6,5},{7,4},{8,11},{9,10},{10,... | collective-permute-start | bytes 98312 | tf_op jit(solution)/shard_map/ppermute | solution.py:432
  24.2 1.8 %collective-permute-done.5.far = bf16[32,512]{1,0:T(8,128)(2,1)S(1)} collective-permute-done((bf16[32,512]{1,0:T(8,128)(2,1)S(1)}, bf16[32,512]{1,0:T(8,128)(2,1)S(1)}, u32[]{:S(2)}, u32[]{:S(2)}) %collective-permute-start.5) | collective-permute-done | bytes 32800 | tf_op jit(solution)/shard_map/ppermute | solution.py:432
  26.7 2.1 %collective-permute-start.6 = (bf16[64,512]{1,0:T(8,128)(2,1)S(1)}, bf16[64,512]{1,0:T(8,128)(2,1)S(1)}, u32[]{:S(2)}, u32[]{:S(2)}) collective-permute-start(bf16[64,512]{1,0:T(8,128)(2,1)S(1)} %get-tuple-element.54.own.nodes), channel_id=1, source_target_pairs={{0,4},{4,0},{8,12},{12,8},{1,5},{5,1},{9,13},{13,9},{2,6},{6,2},{1... | collective-permute-start | bytes 196616 | tf_op jit(solution)/shard_map/ppermute | solution.py:438
  28.8 1.5 %collective-permute-start.9 = (bf16[64,512]{1,0:T(8,128)(2,1)S(1)}, bf16[64,512]{1,0:T(8,128)(2,1)S(1)}, u32[]{:S(2)}, u32[]{:S(2)}) collective-permute-start(bf16[64,512]{1,0:T(8,128)(2,1)S(1)} %get-tuple-element.54.own.nodes), channel_id=1, source_target_pairs={{0,2},{2,0},{1,3},{3,1},{4,6},{6,4},{5,7},{7,5},{8,10},{10,8},{9,1... | collective-permute-start | bytes 196616 | tf_op jit(solution)/shard_map/ppermute | solution.py:369
  30.3 0.9 %collective-permute-done.6.near = bf16[64,512]{1,0:T(8,128)(2,1)S(1)} collective-permute-done((bf16[64,512]{1,0:T(8,128)(2,1)S(1)}, bf16[64,512]{1,0:T(8,128)(2,1)S(1)}, u32[]{:S(2)}, u32[]{:S(2)}) %collective-permute-start.6) | collective-permute-done | bytes 65568 | tf_op jit(solution)/shard_map/ppermute | solution.py:438
  31.2 2.0 %shard_map.179 = (bf16[32,512]{1,0:T(8,128)(2,1)}, f32[192,512]{1,0:T(8,128)S(1)}, bf16[32,512]{1,0:T(8,128)(2,1)S(1)}, bf16[64,512]{1,0:T(8,128)(2,1)S(1)}, bf16[64,512]{1,0:T(8,128)(2,1)S(1)}) custom-call(bf16[512,384]{1,0:T(8,128)(2,1)S(1)} %get-tuple-element.41.from_hits, bf16[512,64]{1,0:T(8,128)(2,1)S(1)} %get-tuple-element.42.to_hits, ...), custom_call_target="tpu_custom_call" | custom-call | tf_op jit(solution)/shard_map/pallas_call | solution.py:337
  33.2 1.9 %collective-permute-start.8 = (bf16[64,512]{1,0:T(8,128)(2,1)S(1)}, bf16[64,512]{1,0:T(8,128)(2,1)S(1)}, u32[]{:S(2)}, u32[]{:S(2)}) collective-permute-start(bf16[64,512]{1,0:T(8,128)(2,1)S(1)} %get-tuple-element.58), channel_id=1, source_target_pairs={{0,4},{4,0},{8,12},{12,8},{1,5},{5,1},{9,13},{13,9},{2,6},{6,2},{1... | collective-permute-start | bytes 196616 | tf_op jit(solution)/shard_map/ppermute | solution.py:455
  35.4 2.1 %collective-permute-done.8.near = bf16[64,512]{1,0:T(8,128)(2,1)S(1)} collective-permute-done((bf16[64,512]{1,0:T(8,128)(2,1)S(1)}, bf16[64,512]{1,0:T(8,128)(2,1)S(1)}, u32[]{:S(2)}, u32[]{:S(2)}) %collective-permute-start.8) | collective-permute-done | bytes 65568 | tf_op jit(solution)/shard_map/ppermute | solution.py:455
  37.6 1.6 %collective-permute-start.12 = (bf16[48,512]{1,0:T(8,128)(2,1)S(1)}, bf16[48,512]{1,0:T(8,128)(2,1)S(1)}, u32[]{:S(2)}, u32[]{:S(2)}) collective-permute-start(bf16[48,512]{1,0:T(8,128)(2,1)S(1)} %get-tuple-element.64), channel_id=1, source_target_pairs={{0,3},{1,2},{2,1},{3,0},{4,7},{5,6},{6,5},{7,4},{8,11},{9,10},{10,... | collective-permute-start | bytes 147464 | tf_op jit(solution)/shard_map/ppermute | solution.py:466
  39.2 2.0 %collective-permute-done.12.far = bf16[48,512]{1,0:T(8,128)(2,1)S(1)} collective-permute-done((bf16[48,512]{1,0:T(8,128)(2,1)S(1)}, bf16[48,512]{1,0:T(8,128)(2,1)S(1)}, u32[]{:S(2)}, u32[]{:S(2)}) %collective-permute-start.12) | collective-permute-done | bytes 49184 | tf_op jit(solution)/shard_map/ppermute | solution.py:466
  41.2 1.6 %shard_map.182 = (bf16[2,512,128]{2,1,0:T(8,128)(2,1)S(1)}, bf16[1024,256]{1,0:T(8,128)(2,1)S(1)}, bf16[2,64,128]{2,1,0:T(8,128)(2,1)S(1)}) custom-call(bf16[1024,128]{1,0:T(8,128)(2,1)S(1)} %get-tuple-element.46.recv_hits, f32[64,512]{1,0:T(8,128)S(1)} %get-tuple-element.62.part, bf16[48,512]{1,0:T(8,128)(2,1)S(1)} %collective-permute-done.11.near, ...), custom_call_target="tpu_custom_call" | custom-call | tf_op jit(solution)/shard_map/pallas_call | solution.py:337
  42.8 0.5 collective-permute-start.13
  43.8 0.7 %collective-permute-done.13.refs_0_ = bf16[2,512,128]{2,1,0:T(8,128)(2,1)S(1)} collective-permute-done((bf16[2,512,128]{2,1,0:T(8,128)(2,1)S(1)}, bf16[2,512,128]{2,1,0:T(8,128)(2,1)S(1)}, u32[]{:S(2)}, u32[]{:S(2)}) %collective-permute-start.13) | collective-permute-done | bytes 262176 | tf_op jit(solution)/shard_map/ppermute | solution.py:369
  44.6 1.6 %collective-permute-start.14 = (bf16[576,128]{1,0:T(8,128)(2,1)S(1)}, bf16[576,128]{1,0:T(8,128)(2,1)S(1)}, u32[]{:S(2)}, u32[]{:S(2)}) collective-permute-start(bf16[576,128]{1,0:T(8,128)(2,1)S(1)} %bitcast.5), channel_id=1, source_target_pairs={{0,2},{2,0},{1,3},{3,1},{4,6},{6,4},{5,7},{7,5},{8,10},{10,8},{9,1... | collective-permute-start | bytes 442376 | tf_op jit(solution)/shard_map/ppermute | solution.py:369
  46.1 4.6 %collective-permute-done.14.refs_0_ = bf16[576,128]{1,0:T(8,128)(2,1)S(1)} collective-permute-done((bf16[576,128]{1,0:T(8,128)(2,1)S(1)}, bf16[576,128]{1,0:T(8,128)(2,1)S(1)}, u32[]{:S(2)}, u32[]{:S(2)}) %collective-permute-start.14) | collective-permute-done | bytes 147488 | tf_op jit(solution)/shard_map/ppermute | solution.py:369
  51.0 3.0 %collective-permute-start.15 = (bf16[2,128,128]{2,1,0:T(8,128)(2,1)S(1)}, bf16[2,128,128]{2,1,0:T(8,128)(2,1)S(1)}, u32[]{:S(2)}, u32[]{:S(2)}) collective-permute-start(bf16[2,128,128]{2,1,0:T(8,128)(2,1)S(1)} %get-tuple-element.74), channel_id=1, source_target_pairs={{0,12},{4,8},{8,4},{12,0},{1,13},{5,9},{9,5},{13,1},{2,14},{6,10},... | collective-permute-start | bytes 196616 | tf_op jit(solution)/shard_map/ppermute | solution.py:494
  54.0 0.6 %collective-permute-start.16 = (bf16[2,128,128]{2,1,0:T(8,128)(2,1)S(1)}, bf16[2,128,128]{2,1,0:T(8,128)(2,1)S(1)}, u32[]{:S(2)}, u32[]{:S(2)}) collective-permute-start(bf16[2,128,128]{2,1,0:T(8,128)(2,1)S(1)} %get-tuple-element.75), channel_id=1, source_target_pairs={{0,8},{4,12},{8,0},{12,4},{1,9},{5,13},{9,1},{13,5},{2,10},{6,14},... | collective-permute-start | bytes 196616 | tf_op jit(solution)/shard_map/ppermute | solution.py:494
  54.7 0.8 %collective-permute-start.17 = (bf16[2,128,128]{2,1,0:T(8,128)(2,1)S(1)}, bf16[2,128,128]{2,1,0:T(8,128)(2,1)S(1)}, u32[]{:S(2)}, u32[]{:S(2)}) collective-permute-start(bf16[2,128,128]{2,1,0:T(8,128)(2,1)S(1)} %get-tuple-element.76), channel_id=1, source_target_pairs={{0,4},{4,0},{8,12},{12,8},{1,5},{5,1},{9,13},{13,9},{2,6},{6,2},{1... | collective-permute-start | bytes 196616 | tf_op jit(solution)/shard_map/ppermute | solution.py:494
  55.5 1.9 %collective-permute-done.15.refs_0_ = bf16[2,128,128]{2,1,0:T(8,128)(2,1)S(1)} collective-permute-done((bf16[2,128,128]{2,1,0:T(8,128)(2,1)S(1)}, bf16[2,128,128]{2,1,0:T(8,128)(2,1)S(1)}, u32[]{:S(2)}, u32[]{:S(2)}) %collective-permute-start.15) | collective-permute-done | bytes 65568 | tf_op jit(solution)/shard_map/ppermute | solution.py:494
  57.4 3.2 %collective-permute-done.16.refs_1_ = bf16[2,128,128]{2,1,0:T(8,128)(2,1)S(1)} collective-permute-done((bf16[2,128,128]{2,1,0:T(8,128)(2,1)S(1)}, bf16[2,128,128]{2,1,0:T(8,128)(2,1)S(1)}, u32[]{:S(2)}, u32[]{:S(2)}) %collective-permute-start.16) | collective-permute-done | bytes 65568 | tf_op jit(solution)/shard_map/ppermute | solution.py:494
  60.6 0.7 %shard_map.186 = (f32[128,128]{1,0:T(8,128)}, f32[128,128]{1,0:T(8,128)}) custom-call(f32[2,128,128]{2,1,0:T(8,128)S(1)} %get-tuple-element.73.own, bf16[2,128,128]{2,1,0:T(8,128)(2,1)S(1)} %collective-permute-done.15.refs_0_, bf16[2,128,128]{2,1,0:T(8,128)(2,1)S(1)} %collective-permute-done.16.refs_1_, bf16[2,128,128]{2,1,0:T(8,128)(2,1)S(1)} %collective-permute-done.17.refs_2_), custom_call_target="tpu_custom_call" | custom-call | tf_op jit(solution)/shard_map/pallas_call | solution.py:337
  (38 shorter events, 2.8 us)
Async XLA Ops:
  0.6 14.8 %collective-permute-start.1 = (bf16[3,227,360]{2,1,0:T(8,128)(2,1)}, bf16[3,227,360]{2,1,0:T(8,128)(2,1)S(1)}, u32[]{:S(2)}, u32[]{:S(2)}) collective-permute-start(bf16[3,227,360]{2,1,0:T(8,128)(2,1)} %bitcast.2), channel_id=1, source_target_pairs={{0,1},{1,0},{2,3},{3,2},{4,8},{5,9},{6,10},{7,11},{8,4},{9,5},{10,... | collective-permute-start | bytes 1470968 | tf_op jit(solution)/shard_map/ppermute | solution.py:393
  1.2 16.3 %collective-permute-start = (bf16[3,227,360]{2,1,0:T(8,128)(2,1)}, bf16[3,227,360]{2,1,0:T(8,128)(2,1)S(1)}, u32[]{:S(2)}, u32[]{:S(2)}) collective-permute-start(bf16[3,227,360]{2,1,0:T(8,128)(2,1)} %bitcast.3), channel_id=1, source_target_pairs={{0,4},{4,0},{8,12},{12,8},{1,5},{5,1},{9,13},{13,9},{2,6},{6,2},{1... | collective-permute-start | bytes 1470968 | tf_op jit(solution)/shard_map/ppermute | solution.py:392
  7.3 1.0 %copy-start = (bf16[3,360,227]{1,2,0:T(8,128)(2,1)S(1)}, bf16[3,360,227]{1,2,0:T(8,128)(2,1)}, u32[]{:S(2)}) copy-start(bf16[3,360,227]{1,2,0:T(8,128)(2,1)} %param.16) | copy-start | bytes 1470964
  8.4 6.6 %copy-start.3 = (bf16[512,512]{1,0:T(8,128)(2,1)S(1)}, bf16[512,512]{1,0:T(8,128)(2,1)}, u32[]{:S(2)}) copy-start(bf16[512,512]{1,0:T(8,128)(2,1)} %param.21) | copy-start | bytes 1572868
  8.4 6.7 %copy-start.4 = (bf16[512,512]{1,0:T(8,128)(2,1)S(1)}, bf16[512,512]{1,0:T(8,128)(2,1)}, u32[]{:S(2)}) copy-start(bf16[512,512]{1,0:T(8,128)(2,1)} %param.22) | copy-start | bytes 1572868
  8.4 6.7 %copy-start.5 = (bf16[512,512]{1,0:T(8,128)(2,1)S(1)}, bf16[512,512]{1,0:T(8,128)(2,1)}, u32[]{:S(2)}) copy-start(bf16[512,512]{1,0:T(8,128)(2,1)} %param.23) | copy-start | bytes 1572868
  8.4 6.8 %copy-start.6 = (bf16[227,512]{1,0:T(8,128)(2,1)S(1)}, bf16[227,512]{1,0:T(8,128)(2,1)}, u32[]{:S(2)}) copy-start(bf16[227,512]{1,0:T(8,128)(2,1)} %param.17) | copy-start | bytes 697348
  10.1 5.2 %copy-start.1 = (bf16[32,512]{1,0:T(8,128)(2,1)S(1)}, bf16[32,512]{1,0:T(8,128)(2,1)}, u32[]{:S(2)}) copy-start(bf16[32,512]{1,0:T(8,128)(2,1)} %mesh_in.3) | copy-start | bytes 98308
  10.1 5.1 %collective-permute-start.3 = (bf16[32,512]{1,0:T(8,128)(2,1)}, bf16[32,512]{1,0:T(8,128)(2,1)S(1)}, u32[]{:S(2)}, u32[]{:S(2)}) collective-permute-start(bf16[32,512]{1,0:T(8,128)(2,1)} %mesh_in.3), channel_id=1, source_target_pairs={{0,3},{1,2},{2,1},{3,0},{4,7},{5,6},{6,5},{7,4},{8,11},{9,10},{10,... | collective-permute-start | bytes 98312 | tf_op jit(solution)/shard_map/ppermute | solution.py:415
  10.5 4.7 %collective-permute-start.2 = (bf16[32,512]{1,0:T(8,128)(2,1)}, bf16[32,512]{1,0:T(8,128)(2,1)S(1)}, u32[]{:S(2)}, u32[]{:S(2)}) collective-permute-start(bf16[32,512]{1,0:T(8,128)(2,1)} %mesh_in.3), channel_id=1, source_target_pairs={{0,1},{1,0},{2,3},{3,2},{4,5},{5,4},{6,7},{7,6},{8,9},{9,8},{10,11... | collective-permute-start | bytes 98312 | tf_op jit(solution)/shard_map/ppermute | solution.py:414
  22.5 8.7 %copy-start.2 = (bf16[32,512]{1,0:T(8,128)(2,1)S(1)}, bf16[32,512]{1,0:T(8,128)(2,1)}, u32[]{:S(2)}) copy-start(bf16[32,512]{1,0:T(8,128)(2,1)} %d_out.3) | copy-start | bytes 98308
  22.5 1.7 %collective-permute-start.4 = (bf16[32,512]{1,0:T(8,128)(2,1)S(1)}, bf16[32,512]{1,0:T(8,128)(2,1)S(1)}, u32[]{:S(2)}, u32[]{:S(2)}) collective-permute-start(bf16[32,512]{1,0:T(8,128)(2,1)S(1)} %get-tuple-element.52), channel_id=1, source_target_pairs={{0,1},{1,0},{2,3},{3,2},{4,5},{5,4},{6,7},{7,6},{8,9},{9,8},{10,11... | collective-permute-start | bytes 98312 | tf_op jit(solution)/shard_map/ppermute | solution.py:431
  22.6 3.4 %collective-permute-start.5 = (bf16[32,512]{1,0:T(8,128)(2,1)S(1)}, bf16[32,512]{1,0:T(8,128)(2,1)S(1)}, u32[]{:S(2)}, u32[]{:S(2)}) collective-permute-start(bf16[32,512]{1,0:T(8,128)(2,1)S(1)} %get-tuple-element.53), channel_id=1, source_target_pairs={{0,3},{1,2},{2,1},{3,0},{4,7},{5,6},{6,5},{7,4},{8,11},{9,10},{10,... | collective-permute-start | bytes 98312 | tf_op jit(solution)/shard_map/ppermute | solution.py:432
  26.2 4.1 %collective-permute-start.7 = (bf16[64,512]{1,0:T(8,128)(2,1)S(1)}, bf16[64,512]{1,0:T(8,128)(2,1)S(1)}, u32[]{:S(2)}, u32[]{:S(2)}) collective-permute-start(bf16[64,512]{1,0:T(8,128)(2,1)S(1)} %get-tuple-element.54.own.nodes), channel_id=1, source_target_pairs={{0,1},{1,0},{2,3},{3,2},{4,8},{5,9},{6,10},{7,11},{8,4},{9,5},{10,... | collective-permute-start | bytes 196616 | tf_op jit(solution)/shard_map/ppermute | solution.py:439
  26.7 4.5 %collective-permute-start.6 = (bf16[64,512]{1,0:T(8,128)(2,1)S(1)}, bf16[64,512]{1,0:T(8,128)(2,1)S(1)}, u32[]{:S(2)}, u32[]{:S(2)}) collective-permute-start(bf16[64,512]{1,0:T(8,128)(2,1)S(1)} %get-tuple-element.54.own.nodes), channel_id=1, source_target_pairs={{0,4},{4,0},{8,12},{12,8},{1,5},{5,1},{9,13},{13,9},{2,6},{6,2},{1... | collective-permute-start | bytes 196616 | tf_op jit(solution)/shard_map/ppermute | solution.py:438
  28.8 6.6 %collective-permute-start.9 = (bf16[64,512]{1,0:T(8,128)(2,1)S(1)}, bf16[64,512]{1,0:T(8,128)(2,1)S(1)}, u32[]{:S(2)}, u32[]{:S(2)}) collective-permute-start(bf16[64,512]{1,0:T(8,128)(2,1)S(1)} %get-tuple-element.54.own.nodes), channel_id=1, source_target_pairs={{0,2},{2,0},{1,3},{3,1},{4,6},{6,4},{5,7},{7,5},{8,10},{10,8},{9,1... | collective-permute-start | bytes 196616 | tf_op jit(solution)/shard_map/ppermute | solution.py:369
  33.2 4.3 %collective-permute-start.8 = (bf16[64,512]{1,0:T(8,128)(2,1)S(1)}, bf16[64,512]{1,0:T(8,128)(2,1)S(1)}, u32[]{:S(2)}, u32[]{:S(2)}) collective-permute-start(bf16[64,512]{1,0:T(8,128)(2,1)S(1)} %get-tuple-element.58), channel_id=1, source_target_pairs={{0,4},{4,0},{8,12},{12,8},{1,5},{5,1},{9,13},{13,9},{2,6},{6,2},{1... | collective-permute-start | bytes 196616 | tf_op jit(solution)/shard_map/ppermute | solution.py:455
  35.1 2.4 %collective-permute-start.10 = (bf16[64,512]{1,0:T(8,128)(2,1)S(1)}, bf16[64,512]{1,0:T(8,128)(2,1)S(1)}, u32[]{:S(2)}, u32[]{:S(2)}) collective-permute-start(bf16[64,512]{1,0:T(8,128)(2,1)S(1)} %get-tuple-element.60), channel_id=1, source_target_pairs={{0,1},{1,0},{2,3},{3,2},{4,8},{5,9},{6,10},{7,11},{8,4},{9,5},{10,... | collective-permute-start | bytes 196616 | tf_op jit(solution)/shard_map/ppermute | solution.py:456
  37.6 1.7 %collective-permute-start.11 = (bf16[48,512]{1,0:T(8,128)(2,1)S(1)}, bf16[48,512]{1,0:T(8,128)(2,1)S(1)}, u32[]{:S(2)}, u32[]{:S(2)}) collective-permute-start(bf16[48,512]{1,0:T(8,128)(2,1)S(1)} %get-tuple-element.63), channel_id=1, source_target_pairs={{0,1},{1,0},{2,3},{3,2},{4,5},{5,4},{6,7},{7,6},{8,9},{9,8},{10,11... | collective-permute-start | bytes 147464 | tf_op jit(solution)/shard_map/ppermute | solution.py:465
  37.6 3.6 %collective-permute-start.12 = (bf16[48,512]{1,0:T(8,128)(2,1)S(1)}, bf16[48,512]{1,0:T(8,128)(2,1)S(1)}, u32[]{:S(2)}, u32[]{:S(2)}) collective-permute-start(bf16[48,512]{1,0:T(8,128)(2,1)S(1)} %get-tuple-element.64), channel_id=1, source_target_pairs={{0,3},{1,2},{2,1},{3,0},{4,7},{5,6},{6,5},{7,4},{8,11},{9,10},{10,... | collective-permute-start | bytes 147464 | tf_op jit(solution)/shard_map/ppermute | solution.py:466
  42.8 1.7 %collective-permute-start.13 = (bf16[2,512,128]{2,1,0:T(8,128)(2,1)S(1)}, bf16[2,512,128]{2,1,0:T(8,128)(2,1)S(1)}, u32[]{:S(2)}, u32[]{:S(2)}) collective-permute-start(bf16[2,512,128]{2,1,0:T(8,128)(2,1)S(1)} %get-tuple-element.69), channel_id=1, source_target_pairs={{0,1},{1,0},{2,3},{3,2},{4,5},{5,4},{6,7},{7,6},{8,9},{9,8},{10,11... | collective-permute-start | bytes 786440 | tf_op jit(solution)/shard_map/ppermute | solution.py:369
  44.6 6.2 %collective-permute-start.14 = (bf16[576,128]{1,0:T(8,128)(2,1)S(1)}, bf16[576,128]{1,0:T(8,128)(2,1)S(1)}, u32[]{:S(2)}, u32[]{:S(2)}) collective-permute-start(bf16[576,128]{1,0:T(8,128)(2,1)S(1)} %bitcast.5), channel_id=1, source_target_pairs={{0,2},{2,0},{1,3},{3,1},{4,6},{6,4},{5,7},{7,5},{8,10},{10,8},{9,1... | collective-permute-start | bytes 442376 | tf_op jit(solution)/shard_map/ppermute | solution.py:369
  51.0 6.3 %collective-permute-start.15 = (bf16[2,128,128]{2,1,0:T(8,128)(2,1)S(1)}, bf16[2,128,128]{2,1,0:T(8,128)(2,1)S(1)}, u32[]{:S(2)}, u32[]{:S(2)}) collective-permute-start(bf16[2,128,128]{2,1,0:T(8,128)(2,1)S(1)} %get-tuple-element.74), channel_id=1, source_target_pairs={{0,12},{4,8},{8,4},{12,0},{1,13},{5,9},{9,5},{13,1},{2,14},{6,10},... | collective-permute-start | bytes 196616 | tf_op jit(solution)/shard_map/ppermute | solution.py:494
  54.0 6.6 %collective-permute-start.16 = (bf16[2,128,128]{2,1,0:T(8,128)(2,1)S(1)}, bf16[2,128,128]{2,1,0:T(8,128)(2,1)S(1)}, u32[]{:S(2)}, u32[]{:S(2)}) collective-permute-start(bf16[2,128,128]{2,1,0:T(8,128)(2,1)S(1)} %get-tuple-element.75), channel_id=1, source_target_pairs={{0,8},{4,12},{8,0},{12,4},{1,9},{5,13},{9,1},{13,5},{2,10},{6,14},... | collective-permute-start | bytes 196616 | tf_op jit(solution)/shard_map/ppermute | solution.py:494
  54.7 6.0 %collective-permute-start.17 = (bf16[2,128,128]{2,1,0:T(8,128)(2,1)S(1)}, bf16[2,128,128]{2,1,0:T(8,128)(2,1)S(1)}, u32[]{:S(2)}, u32[]{:S(2)}) collective-permute-start(bf16[2,128,128]{2,1,0:T(8,128)(2,1)S(1)} %get-tuple-element.76), channel_id=1, source_target_pairs={{0,4},{4,0},{8,12},{12,8},{1,5},{5,1},{9,13},{13,9},{2,6},{6,2},{1... | collective-permute-start | bytes 196616 | tf_op jit(solution)/shard_map/ppermute | solution.py:494

commit v9 on v8

--- a/solution.py
+++ b/solution.py
@@ -155,7 +155,7 @@
 
 def encode_kernel(
     near, far, halo_hits, recv_hits, recv_rows, own, table, stack,
-    senders_out, slope_out, part_out, near_out, far_out, wide,
+    senders_out, slope_out, part_out, far_out, near_out, wide,
 ):
     half = recv_rows.shape[0] // 2
     width = wide.shape[1] // 2
@@ -176,7 +176,7 @@
     far_out[...] = jnp.where(even, sums[:half], sums[half:]).astype(BF16)
 
 
-def node_kernel(part, near, far, mesh_near, mesh_far, mesh_in, stack, mesh_out, slope_out):
+def node_kernel(part, far, near, mesh_near, mesh_far, mesh_in, stack, mesh_out, slope_out):
     node_count = mesh_in.shape[0]
     rim = node_count // 2
     even = even_on("lat")
@@ -217,26 +217,22 @@
     far_out[...] = sums[2 * cycle :].astype(BF16)
 
 
-def columns_of(x, shift, doms, lats):
+def block_of(x, dom_shift, lat_shift, doms, lats):
     cols = x.shape[1] // (doms * lats)
-    me = lax.axis_index("lat")
-    picked = []
-    for dom in range(doms):
-        block = [
-            x[:, (dom * lats + i) * cols : (dom * lats + i + 1) * cols] for i in range(lats)
-        ]
-        pick = block[shift]
-        for i in range(1, lats):
-            pick = jnp.where(me == i, block[(shift + i) % lats], pick)
-        picked.append(pick)
-    return jnp.concatenate(picked, axis=1)
-
-
-def home_kernel(recv_sum, d_out, stack, home_out):
+    dom = lax.rem(lax.axis_index("dom") + dom_shift, doms)
+    index = dom * lats + lax.rem(lax.axis_index("lat") + lat_shift, lats)
+    pick = x[:, :cols]
+    for i in range(1, doms * lats):
+        pick = jnp.where(index == i, x[:, i * cols : (i + 1) * cols], pick)
+    return pick
+
+
+def home_kernel(recv_sum, d_out, stack, senders, home_out, turned_out):
     home_out[...] = mm_nt(recv_sum[...], weight(stack, MR)) + d_out[...].astype(F32)
-
-
-def cotangent_kernel(sums, near, far, home, part_out, near_out, far_out):
+    turned_out[...] = senders[...].T
+
+
+def cotangent_kernel(sums, near, far, home, part_out, far_out, near_out):
     cycle = near.shape[0]
     half = cycle // 2
     rim = half // 2
@@ -250,8 +246,8 @@
 
 
 def encode_grad_kernel(
-    recv_hits, part, near, far, home, node_slope, stack, senders, edge_slope,
-    sends, kept_slope, total_out,
+    recv_hits, part, far, near, home, node_slope, stack, senders, edge_slope,
+    sends, slope_out, total_out,
 ):
     half = part.shape[0] // 2
     even = even_on("lat")
@@ -264,49 +260,56 @@
     gate_one = (cot * node_slope[...]).astype(BF16)
     back = jnp.concatenate(halves(mm_nt(gate_one, weight(stack, GN))), axis=0)
     slope = (mm(recv_hits[...], back) * edge_slope[...].astype(F32)).astype(BF16)
-    doms, _, cols = total_out.shape
-    lats = slope.shape[1] // cols // doms
-    for shift in range(1, lats):
-        gradient = mm_tn(senders[...], columns_of(slope, shift, doms, lats)).astype(BF16)
-        for dom in range(doms):
-            sends[(shift - 1) * doms + dom] = gradient[:, dom * cols : (dom + 1) * cols]
-    kept_slope[...] = columns_of(slope, 0, doms, lats)
-    kept_total = columns_of(total, 0, doms, lats)
-    for dom in range(doms):
-        total_out[dom] = kept_total[:, dom * cols : (dom + 1) * cols]
-
-
-def kept_grad_kernel(senders, kept_slope, keep):
-    gradient = mm_tn(senders[...], kept_slope[...])
-    cols = keep.shape[2]
-    for dom in range(keep.shape[0]):
-        keep[dom] = gradient[:, dom * cols : (dom + 1) * cols]
-
-
-def over_lat_kernel(keep, total, *refs):
-    *came, keep_out, sends_out = refs
-    doms, rows, _ = keep.shape
-    me = lax.axis_index("dom")
-    for shift in range(doms):
-        at = lax.rem(me + shift, doms)
-        block = keep[at]
+    slope_out[...] = slope
+    lats = sends.shape[0] + 1
+    doms = sends.shape[1] + 1
+    for i in range(1, lats):
+        for j in range(1, doms):
+            block = mm(senders[...], block_of(slope, j, i, doms, lats))
+            sends[i - 1, j - 1] = block.astype(BF16)
+    for j in range(doms):
+        total_out[j] = block_of(total, j, 0, doms, lats)
+
+
+def other_doms_kernel(senders, slope, total, *refs):
+    *came, sends = refs
+    lats = len(came) + 1
+    doms = sends.shape[0] + 1
+    rows = senders.shape[0]
+    for j in range(1, doms):
+        block = mm(senders[...], block_of(slope[...], j, 0, doms, lats))
         for part in came:
-            block = block + part[at].astype(F32)
-        if shift == 0:
-            keep_out[...] = block
-        else:
-            sends_out[shift - 1, :rows] = block.astype(BF16)
-            sends_out[shift - 1, rows:] = total[at]
-
-
-def over_dom_kernel(keep, total, nodes, *refs):
-    rows = keep.shape[0] // lax.axis_size("band")
+            block = block + part[j - 1].astype(F32)
+        sends[j - 1, :rows] = block.astype(BF16)
+        sends[j - 1, rows:] = total[j]
+
+
+def other_lats_kernel(senders, slope, after, sends):
+    lats = sends.shape[0] + 1
+    doms = slope.shape[1] // sends.shape[2] // lats
+    for i in range(1, lats):
+        block = mm(senders[...], block_of(slope[...], 0, i, doms, lats))
+        sends[i - 1] = block.astype(BF16)
+
+
+def own_block_kernel(senders, slope, total, nodes, *refs):
+    *came, out = refs
+    lats = len(came) + 1
+    doms = slope.shape[1] // out.shape[2] // lats
+    block = mm(senders[...], block_of(slope[...], 0, 0, doms, lats))
+    for part in came:
+        block = block + part[...].astype(F32)
+    out[0] = block
+    out[1] = mm_tn(nodes[...], total[0])
+
+
+def over_dom_kernel(kept, *refs):
+    rows = kept.shape[1] // lax.axis_size("band")
     doms = lax.axis_size("dom")
     came, (own_out, *sends_out, sums) = refs[: 2 * (doms - 1)], refs[2 * (doms - 1) :]
-    latent = keep.shape[0]
+    latent = kept.shape[1]
     came, came_nodes = came[: len(came) // 2], came[len(came) // 2 :]
-    first = keep[...]
-    second = mm_tn(nodes[...], total[lax.axis_index("dom")])
+    first, second = kept[0], kept[1]
     for part, part_nodes in zip(came, came_nodes):
         first = first + part[:latent].astype(F32)
         second = second + mm_tn(part_nodes[...], part[latent:])
@@ -416,7 +419,7 @@
     (table,) = call(
         table_kernel, [((2 * cycle, latent), BF16)], mesh_near, mesh_far, mesh_in, stack
     )
-    senders, edge_slope, part, to_near, to_far = call(
+    senders, edge_slope, part, to_far, to_near = call(
         encode_kernel,
         [
             ((edges, latent), BF16),
@@ -428,12 +431,12 @@
         raw_near, raw_far, halo_hits, recv_hits, recv_rows, rows, table, stack,
         scratch=[pltpu.VMEM((variables, 2 * width), BF16)],
     )
+    from_far = lax.ppermute(to_far, around, ring_far)
     from_near = lax.ppermute(to_near, around, ring_near)
-    from_far = lax.ppermute(to_far, around, ring_far)
     mesh_one, node_slope = call(
         node_kernel,
         [((cycle, latent), BF16), ((cycle, latent), F32)],
-        part, from_near, from_far, mesh_near, mesh_far, mesh_in, stack,
+        part, from_far, from_near, mesh_near, mesh_far, mesh_in, stack,
     )
     one_near = lax.ppermute(mesh_one, "band", band_near)
     one_far = lax.ppermute(mesh_one, whole, band_far)
@@ -455,39 +458,51 @@
     from_near = lax.ppermute(to_near, "band", band_near)
     from_far = lax.ppermute(to_far, whole, band_far)
     from_near, *dom_nodes = lax.optimization_barrier((from_near, *dom_nodes))
-    (home,) = call(home_kernel, [((node_count, latent), F32)], recv_sum, d_out, stack)
+    home, senders = call(
+        home_kernel,
+        [((node_count, latent), F32), ((latent, edges), BF16)],
+        recv_sum, d_out, stack, senders,
+    )
     message = (node_count + node_count // 2, latent)
-    part, to_near, to_far = call(
+    part, to_far, to_near = call(
         cotangent_kernel,
         [((cycle, latent), F32), (message, BF16), (message, BF16)],
         sums, from_near, from_far, home,
     )
+    from_far = lax.ppermute(to_far, around, ring_far)
     from_near = lax.ppermute(to_near, around, ring_near)
-    from_far = lax.ppermute(to_far, around, ring_far)
 
     cols = latent // sectors
     rows = latent // bands
-    sends, kept_slope, total = call(
+    sends, slope, total = call(
         encode_grad_kernel,
         [
-            (((lats - 1) * doms, latent, cols), BF16),
-            ((edges, doms * cols), BF16),
+            ((lats - 1, doms - 1, latent, cols), BF16),
+            ((edges, latent), BF16),
             ((doms, cycle, cols), BF16),
         ],
-        recv_hits, part, from_near, from_far, home, node_slope, stack, senders, edge_slope,
-    )
-    came = [shifted(sends[i * doms : (i + 1) * doms], "lat", i + 1) for i in range(lats - 1)]
-    (keep,) = call(kept_grad_kernel, [((doms, latent, cols), F32)], senders, kept_slope)
-    keep, sends = call(
-        over_lat_kernel,
-        [((latent, cols), F32), ((doms - 1, latent + cycle, cols), BF16)],
-        keep, total, *came,
-    )
-    came = [shifted(sends[i], "dom", i + 1) for i in range(doms - 1)]
+        recv_hits, part, from_far, from_near, home, node_slope, stack, senders, edge_slope,
+    )
+    came = [shifted(sends[i], "lat", i + 1) for i in range(lats - 1)]
+    (sends,) = call(
+        other_doms_kernel,
+        [((doms - 1, latent + cycle, cols), BF16)],
+        senders, slope, total, *came,
+    )
+    other_doms = [shifted(sends[i], "dom", i + 1) for i in range(doms - 1)]
+    (sends,) = call(
+        other_lats_kernel, [((lats - 1, latent, cols), BF16)], senders, slope, sends
+    )
+    came = [shifted(sends[i], "lat", i + 1) for i in range(lats - 1)]
+    (kept,) = call(
+        own_block_kernel,
+        [((2, latent, cols), F32)],
+        senders, slope, total, mesh_one, *came,
+    )
     own, *sends = call(
         over_dom_kernel,
         [((2, rows, cols), F32)] + [((2, rows, cols), BF16)] * (bands - 1),
-        keep, total, mesh_one, *came, *dom_nodes,
+        kept, *other_doms, *dom_nodes,
         scratch=[pltpu.VMEM((2, latent, cols), F32)],
     )
     came = [

time: 61.6 us -> 61.7 us (level)
  starting transfers between devices: 22.2 us -> 20.8 us
  Pallas kernels: 12.5 us -> 13.5 us
    ppermute x2, starting transfers between devices: 3.22 us -> 0.19 us  [on_device(): from_far = lax.ppermute(to_far, around, ring_far)]
    ppermute x2, starting transfers between devices: 0.14 us -> 2.83 us  [on_device(): from_near = lax.ppermute(to_near, around, ring_near)]
    ppermute x3 -> x4, starting transfers between devices: 3.57 us -> 2.31 us  [shifted(): lax.ppermute(x, axis, [(i, (i + shift) % count) for i in range(count)])]
    pallas_call x12 -> x13, Pallas kernels: 12.5 us -> 13.5 us  [call(): pl.pallas_call(kernel, out_shape=[jax.ShapeDtypeStruct(shape, dtype) for...]
    ppermute x2, waiting for transfers between devices: 3.76 us -> 4.52 us  [on_device(): from_far = lax.ppermute(to_far, around, ring_far)]
    ppermute x3 -> x4, waiting for transfers between devices: 5.32 us -> 5.25 us  [shifted(): lax.ppermute(x, axis, [(i, (i + shift) % count) for i in range(count)])]
  transfers between devices with their start and end apart: 18 -> 19, of which waited for: 9 -> 10; matrix products, arithmetic and copies ran while one was open for 7% -> 7% of each run, Pallas kernels for 7% -> 9%
where the time goes in v9:
time: 61.7 us; the launch traced here: 61.3 us
  starting transfers between devices  20.8 us (34%)
  waiting for transfers between devices  19.7 us (32%)
  Pallas kernels  13.5 us (22%)
  local copies, waits for them, and re-layouts  4.43 us (7%)
  between operations  2.19 us (4%)
  other arithmetic  0.74 us (1%)
    pallas_call x13, Pallas kernels, call(): pl.pallas_call(kernel, out_shape=[jax.ShapeDtypeStruct(shape, dtype) for...  13.5 us
    ppermute x4, waiting for transfers between devices, shifted(): lax.ppermute(x, axis, [(i, (i + shift) % count) for i in range(count)])  5.25 us
    ppermute x3, waiting for transfers between devices, on_device(): lax.ppermute(sends[i], 'band', [(b, b ^ i + 1) for b in range(bands)])  5.04 us
    ppermute x2, waiting for transfers between devices, on_device(): from_far = lax.ppermute(to_far, around, ring_far)  4.52 us
    ppermute x3, starting transfers between devices, on_device(): lax.ppermute(sends[i], 'band', [(b, b ^ i + 1) for b in range(bands)])  4.45 us
    unnamed x20, local copies, waits for them, and re-layouts  4.41 us
    ppermute x1, starting transfers between devices, on_device(): raw_near = lax.ppermute(grid, 'band', band_near)  4.15 us
    ppermute x2, starting transfers between devices, on_device(): from_near = lax.ppermute(to_near, around, ring_near)  2.83 us
  transfers between devices with their start and end apart: 19, of which 10 were waited for; matrix products, arithmetic and copies ran while one was open for 7% of the time, Pallas kernels for 9%

profile of v9, /device:TPU:0, one launch (start us, length us, event | category | flops | bytes accessed | tf_op | source)
XLA Modules:
  0.0 61.3 jit_solution(7095448777299881736)
XLA Ops:
  0.6 0.5 collective-permute-start.1
  1.2 4.1 %collective-permute-start = (bf16[3,227,360]{2,1,0:T(8,128)(2,1)}, bf16[3,227,360]{2,1,0:T(8,128)(2,1)S(1)}, u32[]{:S(2)}, u32[]{:S(2)}) collective-permute-start(bf16[3,227,360]{2,1,0:T(8,128)(2,1)} %bitcast.6), channel_id=1, source_target_pairs={{0,4},{4,0},{8,12},{12,8},{1,5},{5,1},{9,13},{13,9},{2,6},{6,2},{1... | collective-permute-start | bytes 1470968 | tf_op jit(solution)/shard_map/ppermute | solution.py:395
  6.6 0.7 %pad_add_fusion.indices = s32[1,1,3072]{2,1,0:T(1,128)S(1)} fusion(s32[1,1,512]{2,1,0:T(1,128)} %param.30, s32[1,1,512]{2,1,0:T(1,128)} %param.29, s32[1,1,1024]{2,1,0:T(1,128)} %param.27, s32[1,1,1024]{2,1,0:T(1,128)} %param.26), kind=kLoop, calls=%fused_computation.7 | loop fusion | flops 9216 | bytes 24576 | tf_op jit(solution)/shard_map/concatenate | solution.py:399
  7.3 1.0 %copy-done = bf16[3,360,227]{1,2,0:T(8,128)(2,1)S(1)} copy-done((bf16[3,360,227]{1,2,0:T(8,128)(2,1)S(1)}, bf16[3,360,227]{1,2,0:T(8,128)(2,1)}, u32[]{:S(2)}) %copy-start) | copy-done | bytes 490344
  8.4 1.7 %shard_map.175 = (bf16[1024,227]{1,0:T(8,128)(2,1)S(1)}, bf16[1024,128]{1,0:T(8,128)(2,1)S(1)}, bf16[64,1024]{1,0:T(8,128)(2,1)S(1)}, bf16[512,384]{1,0:T(8,128)...) custom-call(s32[1,1]{1,0:T(1,128)S(6)} %copy.25.count, ...), custom_call_target="tpu_custom_call" | custom-call | tf_op jit(solution)/shard_map/pallas_call | solution.py:340
  10.5 1.2 %collective-permute-start.2 = (bf16[32,512]{1,0:T(8,128)(2,1)}, bf16[32,512]{1,0:T(8,128)(2,1)S(1)}, u32[]{:S(2)}, u32[]{:S(2)}) collective-permute-start(bf16[32,512]{1,0:T(8,128)(2,1)} %mesh_in.3), channel_id=1, source_target_pairs={{0,1},{1,0},{2,3},{3,2},{4,5},{5,4},{6,7},{7,6},{8,9},{9,8},{10,11... | collective-permute-start | bytes 98312 | tf_op jit(solution)/shard_map/ppermute | solution.py:417
  11.8 1.1 %constant_dynamic-update-slice_fusion.6 = bf16[3299,512]{1,0:T(8,128)(2,1)S(1)} fusion(bf16[512,512]{1,0:T(8,128)(2,1)} %param.18), kind=kLoop, calls=%fused_computation.6 | loop fusion | bytes 1048576
  12.8 1.1 %constant_dynamic-update-slice_fusion.5 = bf16[3299,512]{1,0:T(8,128)(2,1)S(1)} fusion(bf16[3299,512]{1,0:T(8,128)(2,1)S(1)} %constant_dynamic-update-slice_fusion.6, bf16[512,512]{1,0:T(8,128)(2,1)} %param.19), kind=kLoop, calls=%fused_computation.5 | loop fusion | bytes 1048576
  13.9 1.1 %constant_dynamic-update-slice_fusion.4 = bf16[3299,512]{1,0:T(8,128)(2,1)S(1)} fusion(bf16[3299,512]{1,0:T(8,128)(2,1)S(1)} %constant_dynamic-update-slice_fusion.5, bf16[512,512]{1,0:T(8,128)(2,1)} %param.20), kind=kLoop, calls=%fused_computation.4 | loop fusion | bytes 1048576
  15.5 1.9 %collective-permute-done.near = bf16[3,227,360]{2,1,0:T(8,128)(2,1)S(1)} collective-permute-done((bf16[3,227,360]{2,1,0:T(8,128)(2,1)}, bf16[3,227,360]{2,1,0:T(8,128)(2,1)S(1)}, u32[]{:S(2)}, u32[]{:S(2)}) %collective-permute-start) | collective-permute-done | bytes 490352 | tf_op jit(solution)/shard_map/ppermute | solution.py:395
  17.4 5.1 %shard_map.177 = (bf16[1024,512]{1,0:T(8,128)(2,1)S(1)}, bf16[1024,512]{1,0:T(8,128)(2,1)S(1)}, f32[64,512]{1,0:T(8,128)S(1)}, bf16[32,512]{1,0:T(8,128)(2,1)S(1)}, bf16[32,512]{1,0:T(8,128)(2,1)S(1)}) custom-call(bf16[3,227,360]{2,1,0:T(8,128)(2,1)S(1)} %collective-permute-done.near, bf16[3,227,360]{2,1,0:T(8,128)(2,1)S(1)} %collective-permute-done.1.far, ...), custom_call_target="tpu_custom_call" | custom-call | tf_op jit(solution)/shard_map/pallas_call | solution.py:340
  22.6 1.5 %collective-permute-start.5 = (bf16[32,512]{1,0:T(8,128)(2,1)S(1)}, bf16[32,512]{1,0:T(8,128)(2,1)S(1)}, u32[]{:S(2)}, u32[]{:S(2)}) collective-permute-start(bf16[32,512]{1,0:T(8,128)(2,1)S(1)} %get-tuple-element.53), channel_id=1, source_target_pairs={{0,1},{1,0},{2,3},{3,2},{4,5},{5,4},{6,7},{7,6},{8,9},{9,8},{10,11... | collective-permute-start | bytes 98312 | tf_op jit(solution)/shard_map/ppermute | solution.py:435
  24.1 2.0 %collective-permute-done.4.far = bf16[32,512]{1,0:T(8,128)(2,1)S(1)} collective-permute-done((bf16[32,512]{1,0:T(8,128)(2,1)S(1)}, bf16[32,512]{1,0:T(8,128)(2,1)S(1)}, u32[]{:S(2)}, u32[]{:S(2)}) %collective-permute-start.4) | collective-permute-done | bytes 32800 | tf_op jit(solution)/shard_map/ppermute | solution.py:434
  26.6 2.4 %collective-permute-start.6 = (bf16[64,512]{1,0:T(8,128)(2,1)S(1)}, bf16[64,512]{1,0:T(8,128)(2,1)S(1)}, u32[]{:S(2)}, u32[]{:S(2)}) collective-permute-start(bf16[64,512]{1,0:T(8,128)(2,1)S(1)} %get-tuple-element.54.own.nodes), channel_id=1, source_target_pairs={{0,4},{4,0},{8,12},{12,8},{1,5},{5,1},{9,13},{13,9},{2,6},{6,2},{1... | collective-permute-start | bytes 196616 | tf_op jit(solution)/shard_map/ppermute | solution.py:441
  29.0 1.2 %collective-permute-start.9 = (bf16[64,512]{1,0:T(8,128)(2,1)S(1)}, bf16[64,512]{1,0:T(8,128)(2,1)S(1)}, u32[]{:S(2)}, u32[]{:S(2)}) collective-permute-start(bf16[64,512]{1,0:T(8,128)(2,1)S(1)} %get-tuple-element.54.own.nodes), channel_id=1, source_target_pairs={{0,2},{2,0},{1,3},{3,1},{4,6},{6,4},{5,7},{7,5},{8,10},{10,8},{9,1... | collective-permute-start | bytes 196616 | tf_op jit(solution)/shard_map/ppermute | solution.py:372
  30.2 1.1 %collective-permute-done.6.near = bf16[64,512]{1,0:T(8,128)(2,1)S(1)} collective-permute-done((bf16[64,512]{1,0:T(8,128)(2,1)S(1)}, bf16[64,512]{1,0:T(8,128)(2,1)S(1)}, u32[]{:S(2)}, u32[]{:S(2)}) %collective-permute-start.6) | collective-permute-done | bytes 65568 | tf_op jit(solution)/shard_map/ppermute | solution.py:441
  31.2 2.0 %shard_map.179 = (bf16[32,512]{1,0:T(8,128)(2,1)}, f32[192,512]{1,0:T(8,128)S(1)}, bf16[32,512]{1,0:T(8,128)(2,1)S(1)}, bf16[64,512]{1,0:T(8,128)(2,1)S(1)}, bf16[64,512]{1,0:T(8,128)(2,1)S(1)}) custom-call(bf16[512,384]{1,0:T(8,128)(2,1)S(1)} %get-tuple-element.41.from_hits, bf16[512,64]{1,0:T(8,128)(2,1)S(1)} %get-tuple-element.42.to_hits, ...), custom_call_target="tpu_custom_call" | custom-call | tf_op jit(solution)/shard_map/pallas_call | solution.py:340
  33.2 2.1 %collective-permute-start.8 = (bf16[64,512]{1,0:T(8,128)(2,1)S(1)}, bf16[64,512]{1,0:T(8,128)(2,1)S(1)}, u32[]{:S(2)}, u32[]{:S(2)}) collective-permute-start(bf16[64,512]{1,0:T(8,128)(2,1)S(1)} %get-tuple-element.60), channel_id=1, source_target_pairs={{0,4},{4,0},{8,12},{12,8},{1,5},{5,1},{9,13},{13,9},{2,6},{6,2},{1... | collective-permute-start | bytes 196616 | tf_op jit(solution)/shard_map/ppermute | solution.py:458
  35.7 1.9 %collective-permute-done.8.near = bf16[64,512]{1,0:T(8,128)(2,1)S(1)} collective-permute-done((bf16[64,512]{1,0:T(8,128)(2,1)S(1)}, bf16[64,512]{1,0:T(8,128)(2,1)S(1)}, u32[]{:S(2)}, u32[]{:S(2)}) %collective-permute-start.8) | collective-permute-done | bytes 65568 | tf_op jit(solution)/shard_map/ppermute | solution.py:458
  37.7 1.3 %collective-permute-start.12 = (bf16[48,512]{1,0:T(8,128)(2,1)S(1)}, bf16[48,512]{1,0:T(8,128)(2,1)S(1)}, u32[]{:S(2)}, u32[]{:S(2)}) collective-permute-start(bf16[48,512]{1,0:T(8,128)(2,1)S(1)} %get-tuple-element.66), channel_id=1, source_target_pairs={{0,1},{1,0},{2,3},{3,2},{4,5},{5,4},{6,7},{7,6},{8,9},{9,8},{10,11... | collective-permute-start | bytes 147464 | tf_op jit(solution)/shard_map/ppermute | solution.py:473
  39.0 2.5 %collective-permute-done.11.far = bf16[48,512]{1,0:T(8,128)(2,1)S(1)} collective-permute-done((bf16[48,512]{1,0:T(8,128)(2,1)S(1)}, bf16[48,512]{1,0:T(8,128)(2,1)S(1)}, u32[]{:S(2)}, u32[]{:S(2)}) %collective-permute-start.11) | collective-permute-done | bytes 49184 | tf_op jit(solution)/shard_map/ppermute | solution.py:472
  41.5 1.6 %shard_map.182 = (bf16[1,1,512,128]{3,2,1,0:T(8,128)(2,1)S(1)}, bf16[1024,512]{1,0:T(8,128)(2,1)S(1)}, bf16[2,64,128]{2,1,0:T(8,128)(2,1)S(1)}) custom-call(bf16[1024,128]{1,0:T(8,128)(2,1)S(1)} %get-tuple-element.46.recv_hits, f32[64,512]{1,0:T(8,128)S(1)} %get-tuple-element.64.part, bf16[48,512]{1,0:T(8,128)(2,1)S(1)} %collective-permute-done.11.far, ...), custom_call_target="tpu_custom_call" | custom-call | tf_op jit(solution)/shard_map/pallas_call | solution.py:340
  43.1 1.3 %collective-permute-done.13.refs_0_ = bf16[1,512,128]{2,1,0:T(8,128)(2,1)S(1)} collective-permute-done((bf16[1,512,128]{2,1,0:T(8,128)(2,1)S(1)}, bf16[1,512,128]{2,1,0:T(8,128)(2,1)S(1)}, u32[]{:S(2)}, u32[]{:S(2)}) %collective-permute-start.13) | collective-permute-done | bytes 131104 | tf_op jit(solution)/shard_map/ppermute | solution.py:372
  45.0 1.0 %collective-permute-start.15 = (bf16[576,128]{1,0:T(8,128)(2,1)S(1)}, bf16[576,128]{1,0:T(8,128)(2,1)S(1)}, u32[]{:S(2)}, u32[]{:S(2)}) collective-permute-start(bf16[576,128]{1,0:T(8,128)(2,1)S(1)} %bitcast.4), channel_id=1, source_target_pairs={{0,2},{2,0},{1,3},{3,1},{4,6},{6,4},{5,7},{7,5},{8,10},{10,8},{9,1... | collective-permute-start | bytes 442376 | tf_op jit(solution)/shard_map/ppermute | solution.py:372
  46.5 1.3 %collective-permute-done.14.refs_0_ = bf16[512,128]{1,0:T(8,128)(2,1)S(1)} collective-permute-done((bf16[512,128]{1,0:T(8,128)(2,1)S(1)}, bf16[512,128]{1,0:T(8,128)(2,1)S(1)}, u32[]{:S(2)}, u32[]{:S(2)}) %collective-permute-start.14) | collective-permute-done | bytes 131104 | tf_op jit(solution)/shard_map/ppermute | solution.py:372
  48.3 2.6 %collective-permute-done.15.refs_0_ = bf16[576,128]{1,0:T(8,128)(2,1)S(1)} collective-permute-done((bf16[576,128]{1,0:T(8,128)(2,1)S(1)}, bf16[576,128]{1,0:T(8,128)(2,1)S(1)}, u32[]{:S(2)}, u32[]{:S(2)}) %collective-permute-start.15) | collective-permute-done | bytes 147488 | tf_op jit(solution)/shard_map/ppermute | solution.py:372
  51.2 3.2 %collective-permute-start.16 = (bf16[2,128,128]{2,1,0:T(8,128)(2,1)S(1)}, bf16[2,128,128]{2,1,0:T(8,128)(2,1)S(1)}, u32[]{:S(2)}, u32[]{:S(2)}) collective-permute-start(bf16[2,128,128]{2,1,0:T(8,128)(2,1)S(1)} %get-tuple-element.74), channel_id=1, source_target_pairs={{0,12},{4,8},{8,4},{12,0},{1,13},{5,9},{9,5},{13,1},{2,14},{6,10},... | collective-permute-start | bytes 196616 | tf_op jit(solution)/shard_map/ppermute | solution.py:509
  54.4 0.6 %collective-permute-start.17 = (bf16[2,128,128]{2,1,0:T(8,128)(2,1)S(1)}, bf16[2,128,128]{2,1,0:T(8,128)(2,1)S(1)}, u32[]{:S(2)}, u32[]{:S(2)}) collective-permute-start(bf16[2,128,128]{2,1,0:T(8,128)(2,1)S(1)} %get-tuple-element.75), channel_id=1, source_target_pairs={{0,8},{4,12},{8,0},{12,4},{1,9},{5,13},{9,1},{13,5},{2,10},{6,14},... | collective-permute-start | bytes 196616 | tf_op jit(solution)/shard_map/ppermute | solution.py:509
  55.0 0.6 %collective-permute-start.18 = (bf16[2,128,128]{2,1,0:T(8,128)(2,1)S(1)}, bf16[2,128,128]{2,1,0:T(8,128)(2,1)S(1)}, u32[]{:S(2)}, u32[]{:S(2)}) collective-permute-start(bf16[2,128,128]{2,1,0:T(8,128)(2,1)S(1)} %get-tuple-element.76), channel_id=1, source_target_pairs={{0,4},{4,0},{8,12},{12,8},{1,5},{5,1},{9,13},{13,9},{2,6},{6,2},{1... | collective-permute-start | bytes 196616 | tf_op jit(solution)/shard_map/ppermute | solution.py:509
  55.6 1.9 %collective-permute-done.16.refs_0_ = bf16[2,128,128]{2,1,0:T(8,128)(2,1)S(1)} collective-permute-done((bf16[2,128,128]{2,1,0:T(8,128)(2,1)S(1)}, bf16[2,128,128]{2,1,0:T(8,128)(2,1)S(1)}, u32[]{:S(2)}, u32[]{:S(2)}) %collective-permute-start.16) | collective-permute-done | bytes 65568 | tf_op jit(solution)/shard_map/ppermute | solution.py:509
  57.5 3.2 %collective-permute-done.17.refs_1_ = bf16[2,128,128]{2,1,0:T(8,128)(2,1)S(1)} collective-permute-done((bf16[2,128,128]{2,1,0:T(8,128)(2,1)S(1)}, bf16[2,128,128]{2,1,0:T(8,128)(2,1)S(1)}, u32[]{:S(2)}, u32[]{:S(2)}) %collective-permute-start.17) | collective-permute-done | bytes 65568 | tf_op jit(solution)/shard_map/ppermute | solution.py:509
  60.7 0.7 %shard_map.187 = (f32[128,128]{1,0:T(8,128)}, f32[128,128]{1,0:T(8,128)}) custom-call(f32[2,128,128]{2,1,0:T(8,128)S(1)} %get-tuple-element.73.own, bf16[2,128,128]{2,1,0:T(8,128)(2,1)S(1)} %collective-permute-done.16.refs_0_, bf16[2,128,128]{2,1,0:T(8,128)(2,1)S(1)} %collective-permute-done.17.refs_1_, bf16[2,128,128]{2,1,0:T(8,128)(2,1)S(1)} %collective-permute-done.18.refs_2_), custom_call_target="tpu_custom_call" | custom-call | tf_op jit(solution)/shard_map/pallas_call | solution.py:340
  (41 shorter events, 3.7 us)
Async XLA Ops:
  0.6 14.8 %collective-permute-start.1 = (bf16[3,227,360]{2,1,0:T(8,128)(2,1)}, bf16[3,227,360]{2,1,0:T(8,128)(2,1)S(1)}, u32[]{:S(2)}, u32[]{:S(2)}) collective-permute-start(bf16[3,227,360]{2,1,0:T(8,128)(2,1)} %bitcast.5), channel_id=1, source_target_pairs={{0,1},{1,0},{2,3},{3,2},{4,8},{5,9},{6,10},{7,11},{8,4},{9,5},{10,... | collective-permute-start | bytes 1470968 | tf_op jit(solution)/shard_map/ppermute | solution.py:396
  1.2 16.3 %collective-permute-start = (bf16[3,227,360]{2,1,0:T(8,128)(2,1)}, bf16[3,227,360]{2,1,0:T(8,128)(2,1)S(1)}, u32[]{:S(2)}, u32[]{:S(2)}) collective-permute-start(bf16[3,227,360]{2,1,0:T(8,128)(2,1)} %bitcast.6), channel_id=1, source_target_pairs={{0,4},{4,0},{8,12},{12,8},{1,5},{5,1},{9,13},{13,9},{2,6},{6,2},{1... | collective-permute-start | bytes 1470968 | tf_op jit(solution)/shard_map/ppermute | solution.py:395
  7.3 1.0 %copy-start = (bf16[3,360,227]{1,2,0:T(8,128)(2,1)S(1)}, bf16[3,360,227]{1,2,0:T(8,128)(2,1)}, u32[]{:S(2)}) copy-start(bf16[3,360,227]{1,2,0:T(8,128)(2,1)} %param.16) | copy-start | bytes 1470964
  8.4 6.6 %copy-start.3 = (bf16[512,512]{1,0:T(8,128)(2,1)S(1)}, bf16[512,512]{1,0:T(8,128)(2,1)}, u32[]{:S(2)}) copy-start(bf16[512,512]{1,0:T(8,128)(2,1)} %param.21) | copy-start | bytes 1572868
  8.4 6.7 %copy-start.4 = (bf16[512,512]{1,0:T(8,128)(2,1)S(1)}, bf16[512,512]{1,0:T(8,128)(2,1)}, u32[]{:S(2)}) copy-start(bf16[512,512]{1,0:T(8,128)(2,1)} %param.22) | copy-start | bytes 1572868
  8.4 6.7 %copy-start.5 = (bf16[512,512]{1,0:T(8,128)(2,1)S(1)}, bf16[512,512]{1,0:T(8,128)(2,1)}, u32[]{:S(2)}) copy-start(bf16[512,512]{1,0:T(8,128)(2,1)} %param.23) | copy-start | bytes 1572868
  8.4 6.8 %copy-start.6 = (bf16[227,512]{1,0:T(8,128)(2,1)S(1)}, bf16[227,512]{1,0:T(8,128)(2,1)}, u32[]{:S(2)}) copy-start(bf16[227,512]{1,0:T(8,128)(2,1)} %param.17) | copy-start | bytes 697348
  10.1 5.2 %copy-start.1 = (bf16[32,512]{1,0:T(8,128)(2,1)S(1)}, bf16[32,512]{1,0:T(8,128)(2,1)}, u32[]{:S(2)}) copy-start(bf16[32,512]{1,0:T(8,128)(2,1)} %mesh_in.3) | copy-start | bytes 98308
  10.1 5.1 %collective-permute-start.3 = (bf16[32,512]{1,0:T(8,128)(2,1)}, bf16[32,512]{1,0:T(8,128)(2,1)S(1)}, u32[]{:S(2)}, u32[]{:S(2)}) collective-permute-start(bf16[32,512]{1,0:T(8,128)(2,1)} %mesh_in.3), channel_id=1, source_target_pairs={{0,3},{1,2},{2,1},{3,0},{4,7},{5,6},{6,5},{7,4},{8,11},{9,10},{10,... | collective-permute-start | bytes 98312 | tf_op jit(solution)/shard_map/ppermute | solution.py:418
  10.5 4.7 %collective-permute-start.2 = (bf16[32,512]{1,0:T(8,128)(2,1)}, bf16[32,512]{1,0:T(8,128)(2,1)S(1)}, u32[]{:S(2)}, u32[]{:S(2)}) collective-permute-start(bf16[32,512]{1,0:T(8,128)(2,1)} %mesh_in.3), channel_id=1, source_target_pairs={{0,1},{1,0},{2,3},{3,2},{4,5},{5,4},{6,7},{7,6},{8,9},{9,8},{10,11... | collective-permute-start | bytes 98312 | tf_op jit(solution)/shard_map/ppermute | solution.py:417
  22.5 8.8 %copy-start.2 = (bf16[32,512]{1,0:T(8,128)(2,1)S(1)}, bf16[32,512]{1,0:T(8,128)(2,1)}, u32[]{:S(2)}) copy-start(bf16[32,512]{1,0:T(8,128)(2,1)} %d_out.3) | copy-start | bytes 98308
  22.5 3.7 %collective-permute-start.4 = (bf16[32,512]{1,0:T(8,128)(2,1)S(1)}, bf16[32,512]{1,0:T(8,128)(2,1)S(1)}, u32[]{:S(2)}, u32[]{:S(2)}) collective-permute-start(bf16[32,512]{1,0:T(8,128)(2,1)S(1)} %get-tuple-element.52), channel_id=1, source_target_pairs={{0,3},{1,2},{2,1},{3,0},{4,7},{5,6},{6,5},{7,4},{8,11},{9,10},{10,... | collective-permute-start | bytes 98312 | tf_op jit(solution)/shard_map/ppermute | solution.py:434
  22.6 3.6 %collective-permute-start.5 = (bf16[32,512]{1,0:T(8,128)(2,1)S(1)}, bf16[32,512]{1,0:T(8,128)(2,1)S(1)}, u32[]{:S(2)}, u32[]{:S(2)}) collective-permute-start(bf16[32,512]{1,0:T(8,128)(2,1)S(1)} %get-tuple-element.53), channel_id=1, source_target_pairs={{0,1},{1,0},{2,3},{3,2},{4,5},{5,4},{6,7},{7,6},{8,9},{9,8},{10,11... | collective-permute-start | bytes 98312 | tf_op jit(solution)/shard_map/ppermute | solution.py:435
  26.4 3.8 %collective-permute-start.7 = (bf16[64,512]{1,0:T(8,128)(2,1)S(1)}, bf16[64,512]{1,0:T(8,128)(2,1)S(1)}, u32[]{:S(2)}, u32[]{:S(2)}) collective-permute-start(bf16[64,512]{1,0:T(8,128)(2,1)S(1)} %get-tuple-element.54.own.nodes), channel_id=1, source_target_pairs={{0,1},{1,0},{2,3},{3,2},{4,8},{5,9},{6,10},{7,11},{8,4},{9,5},{10,... | collective-permute-start | bytes 196616 | tf_op jit(solution)/shard_map/ppermute | solution.py:442
  26.6 4.6 %collective-permute-start.6 = (bf16[64,512]{1,0:T(8,128)(2,1)S(1)}, bf16[64,512]{1,0:T(8,128)(2,1)S(1)}, u32[]{:S(2)}, u32[]{:S(2)}) collective-permute-start(bf16[64,512]{1,0:T(8,128)(2,1)S(1)} %get-tuple-element.54.own.nodes), channel_id=1, source_target_pairs={{0,4},{4,0},{8,12},{12,8},{1,5},{5,1},{9,13},{13,9},{2,6},{6,2},{1... | collective-permute-start | bytes 196616 | tf_op jit(solution)/shard_map/ppermute | solution.py:441
  29.0 6.7 %collective-permute-start.9 = (bf16[64,512]{1,0:T(8,128)(2,1)S(1)}, bf16[64,512]{1,0:T(8,128)(2,1)S(1)}, u32[]{:S(2)}, u32[]{:S(2)}) collective-permute-start(bf16[64,512]{1,0:T(8,128)(2,1)S(1)} %get-tuple-element.54.own.nodes), channel_id=1, source_target_pairs={{0,2},{2,0},{1,3},{3,1},{4,6},{6,4},{5,7},{7,5},{8,10},{10,8},{9,1... | collective-permute-start | bytes 196616 | tf_op jit(solution)/shard_map/ppermute | solution.py:372
  33.2 4.3 %collective-permute-start.8 = (bf16[64,512]{1,0:T(8,128)(2,1)S(1)}, bf16[64,512]{1,0:T(8,128)(2,1)S(1)}, u32[]{:S(2)}, u32[]{:S(2)}) collective-permute-start(bf16[64,512]{1,0:T(8,128)(2,1)S(1)} %get-tuple-element.60), channel_id=1, source_target_pairs={{0,4},{4,0},{8,12},{12,8},{1,5},{5,1},{9,13},{13,9},{2,6},{6,2},{1... | collective-permute-start | bytes 196616 | tf_op jit(solution)/shard_map/ppermute | solution.py:458
  35.3 2.2 %collective-permute-start.10 = (bf16[64,512]{1,0:T(8,128)(2,1)S(1)}, bf16[64,512]{1,0:T(8,128)(2,1)S(1)}, u32[]{:S(2)}, u32[]{:S(2)}) collective-permute-start(bf16[64,512]{1,0:T(8,128)(2,1)S(1)} %get-tuple-element.62), channel_id=1, source_target_pairs={{0,1},{1,0},{2,3},{3,2},{4,8},{5,9},{6,10},{7,11},{8,4},{9,5},{10,... | collective-permute-start | bytes 196616 | tf_op jit(solution)/shard_map/ppermute | solution.py:459
  37.6 3.8 %collective-permute-start.11 = (bf16[48,512]{1,0:T(8,128)(2,1)S(1)}, bf16[48,512]{1,0:T(8,128)(2,1)S(1)}, u32[]{:S(2)}, u32[]{:S(2)}) collective-permute-start(bf16[48,512]{1,0:T(8,128)(2,1)S(1)} %get-tuple-element.65), channel_id=1, source_target_pairs={{0,3},{1,2},{2,1},{3,0},{4,7},{5,6},{6,5},{7,4},{8,11},{9,10},{10,... | collective-permute-start | bytes 147464 | tf_op jit(solution)/shard_map/ppermute | solution.py:472
  37.7 3.8 %collective-permute-start.12 = (bf16[48,512]{1,0:T(8,128)(2,1)S(1)}, bf16[48,512]{1,0:T(8,128)(2,1)S(1)}, u32[]{:S(2)}, u32[]{:S(2)}) collective-permute-start(bf16[48,512]{1,0:T(8,128)(2,1)S(1)} %get-tuple-element.66), channel_id=1, source_target_pairs={{0,1},{1,0},{2,3},{3,2},{4,5},{5,4},{6,7},{7,6},{8,9},{9,8},{10,11... | collective-permute-start | bytes 147464 | tf_op jit(solution)/shard_map/ppermute | solution.py:473
  43.1 1.4 %collective-permute-start.13 = (bf16[1,512,128]{2,1,0:T(8,128)(2,1)S(1)}, bf16[1,512,128]{2,1,0:T(8,128)(2,1)S(1)}, u32[]{:S(2)}, u32[]{:S(2)}) collective-permute-start(bf16[1,512,128]{2,1,0:T(8,128)(2,1)S(1)} %bitcast.9), channel_id=1, source_target_pairs={{0,1},{1,0},{2,3},{3,2},{4,5},{5,4},{6,7},{7,6},{8,9},{9,8},{10,11... | collective-permute-start | bytes 393224 | tf_op jit(solution)/shard_map/ppermute | solution.py:372
  45.0 6.0 %collective-permute-start.15 = (bf16[576,128]{1,0:T(8,128)(2,1)S(1)}, bf16[576,128]{1,0:T(8,128)(2,1)S(1)}, u32[]{:S(2)}, u32[]{:S(2)}) collective-permute-start(bf16[576,128]{1,0:T(8,128)(2,1)S(1)} %bitcast.4), channel_id=1, source_target_pairs={{0,2},{2,0},{1,3},{3,1},{4,6},{6,4},{5,7},{7,5},{8,10},{10,8},{9,1... | collective-permute-start | bytes 442376 | tf_op jit(solution)/shard_map/ppermute | solution.py:372
  46.4 1.4 %collective-permute-start.14 = (bf16[512,128]{1,0:T(8,128)(2,1)S(1)}, bf16[512,128]{1,0:T(8,128)(2,1)S(1)}, u32[]{:S(2)}, u32[]{:S(2)}) collective-permute-start(bf16[512,128]{1,0:T(8,128)(2,1)S(1)} %bitcast.8), channel_id=1, source_target_pairs={{0,1},{1,0},{2,3},{3,2},{4,5},{5,4},{6,7},{7,6},{8,9},{9,8},{10,11... | collective-permute-start | bytes 393224 | tf_op jit(solution)/shard_map/ppermute | solution.py:372
  51.2 6.3 %collective-permute-start.16 = (bf16[2,128,128]{2,1,0:T(8,128)(2,1)S(1)}, bf16[2,128,128]{2,1,0:T(8,128)(2,1)S(1)}, u32[]{:S(2)}, u32[]{:S(2)}) collective-permute-start(bf16[2,128,128]{2,1,0:T(8,128)(2,1)S(1)} %get-tuple-element.74), channel_id=1, source_target_pairs={{0,12},{4,8},{8,4},{12,0},{1,13},{5,9},{9,5},{13,1},{2,14},{6,10},... | collective-permute-start | bytes 196616 | tf_op jit(solution)/shard_map/ppermute | solution.py:509
  54.4 6.3 %collective-permute-start.17 = (bf16[2,128,128]{2,1,0:T(8,128)(2,1)S(1)}, bf16[2,128,128]{2,1,0:T(8,128)(2,1)S(1)}, u32[]{:S(2)}, u32[]{:S(2)}) collective-permute-start(bf16[2,128,128]{2,1,0:T(8,128)(2,1)S(1)} %get-tuple-element.75), channel_id=1, source_target_pairs={{0,8},{4,12},{8,0},{12,4},{1,9},{5,13},{9,1},{13,5},{2,10},{6,14},... | collective-permute-start | bytes 196616 | tf_op jit(solution)/shard_map/ppermute | solution.py:509
  55.0 5.7 %collective-permute-start.18 = (bf16[2,128,128]{2,1,0:T(8,128)(2,1)S(1)}, bf16[2,128,128]{2,1,0:T(8,128)(2,1)S(1)}, u32[]{:S(2)}, u32[]{:S(2)}) collective-permute-start(bf16[2,128,128]{2,1,0:T(8,128)(2,1)S(1)} %get-tuple-element.76), channel_id=1, source_target_pairs={{0,4},{4,0},{8,12},{12,8},{1,5},{5,1},{9,13},{13,9},{2,6},{6,2},{1... | collective-permute-start | bytes 196616 | tf_op jit(solution)/shard_map/ppermute | solution.py:509

commit v10 on v9

--- a/solution.py
+++ b/solution.py
@@ -154,7 +154,7 @@
 
 
 def encode_kernel(
-    near, far, halo_hits, recv_hits, recv_rows, own, table, stack,
+    far, near, halo_hits, recv_hits, recv_rows, own, table, stack,
     senders_out, slope_out, part_out, far_out, near_out, wide,
 ):
     half = recv_rows.shape[0] // 2
@@ -245,9 +245,16 @@
     far_out[half:] = jnp.where(even, home[:rim], home[rim:]).astype(BF16)
 
 
+def gradient_block(recv_hits, back, edge_slope, senders, dom_shift, lat_shift, doms, lats):
+    place = (dom_shift, lat_shift, doms, lats)
+    slope = mm(recv_hits[...], block_of(back, *place))
+    slope = slope * block_of(edge_slope, *place).astype(F32)
+    return mm(senders[...], slope.astype(BF16))
+
+
 def encode_grad_kernel(
     recv_hits, part, far, near, home, node_slope, stack, senders, edge_slope,
-    sends, slope_out, total_out,
+    sends, back_out, total_out,
 ):
     half = part.shape[0] // 2
     even = even_on("lat")
@@ -259,58 +266,61 @@
     cot = rest + mm_nt(total, weight(stack, MS))
     gate_one = (cot * node_slope[...]).astype(BF16)
     back = jnp.concatenate(halves(mm_nt(gate_one, weight(stack, GN))), axis=0)
-    slope = (mm(recv_hits[...], back) * edge_slope[...].astype(F32)).astype(BF16)
-    slope_out[...] = slope
+    back_out[...] = back
     lats = sends.shape[0] + 1
     doms = sends.shape[1] + 1
     for i in range(1, lats):
         for j in range(1, doms):
-            block = mm(senders[...], block_of(slope, j, i, doms, lats))
+            block = gradient_block(recv_hits, back, edge_slope, senders, j, i, doms, lats)
             sends[i - 1, j - 1] = block.astype(BF16)
     for j in range(doms):
         total_out[j] = block_of(total, j, 0, doms, lats)
 
 
-def other_doms_kernel(senders, slope, total, *refs):
-    *came, sends = refs
-    lats = len(came) + 1
-    doms = sends.shape[0] + 1
-    rows = senders.shape[0]
+def kept_blocks_kernel(recv_hits, back, edge_slope, senders, after, kept):
+    doms = kept.shape[0] + 1
+    lats = back.shape[1] // kept.shape[2] // doms
     for j in range(1, doms):
-        block = mm(senders[...], block_of(slope[...], j, 0, doms, lats))
+        kept[j - 1] = gradient_block(recv_hits, back, edge_slope, senders, j, 0, doms, lats)
+
+
+def add_kernel(kept, total, *refs):
+    *came, out = refs
+    rows = kept.shape[1]
+    for j in range(kept.shape[0]):
+        block = kept[j]
         for part in came:
-            block = block + part[j - 1].astype(F32)
-        sends[j - 1, :rows] = block.astype(BF16)
-        sends[j - 1, rows:] = total[j]
-
-
-def other_lats_kernel(senders, slope, after, sends):
+            block = block + part[j].astype(F32)
+        out[j, :rows] = block.astype(BF16)
+        out[j, rows:] = total[j + 1]
+
+
+def other_lats_kernel(recv_hits, back, edge_slope, senders, after, sends):
     lats = sends.shape[0] + 1
-    doms = slope.shape[1] // sends.shape[2] // lats
+    doms = back.shape[1] // sends.shape[2] // lats
     for i in range(1, lats):
-        block = mm(senders[...], block_of(slope[...], 0, i, doms, lats))
+        block = gradient_block(recv_hits, back, edge_slope, senders, 0, i, doms, lats)
         sends[i - 1] = block.astype(BF16)
 
 
-def own_block_kernel(senders, slope, total, nodes, *refs):
+def own_block_kernel(recv_hits, back, edge_slope, senders, *refs):
     *came, out = refs
     lats = len(came) + 1
-    doms = slope.shape[1] // out.shape[2] // lats
-    block = mm(senders[...], block_of(slope[...], 0, 0, doms, lats))
+    doms = back.shape[1] // out.shape[1] // lats
+    block = gradient_block(recv_hits, back, edge_slope, senders, 0, 0, doms, lats)
     for part in came:
         block = block + part[...].astype(F32)
-    out[0] = block
-    out[1] = mm_tn(nodes[...], total[0])
-
-
-def over_dom_kernel(kept, *refs):
-    rows = kept.shape[1] // lax.axis_size("band")
-    doms = lax.axis_size("dom")
+    out[...] = block
+
+
+def over_dom_kernel(kept, total, nodes, *refs):
+    latent = kept.shape[0]
+    rows = latent // lax.axis_size("band")
+    doms = total.shape[0]
     came, (own_out, *sends_out, sums) = refs[: 2 * (doms - 1)], refs[2 * (doms - 1) :]
-    latent = kept.shape[1]
-    came, came_nodes = came[: len(came) // 2], came[len(came) // 2 :]
-    first, second = kept[0], kept[1]
-    for part, part_nodes in zip(came, came_nodes):
+    first = kept[...]
+    second = mm_tn(nodes[...], total[0])
+    for part, part_nodes in zip(came[: doms - 1], came[doms - 1 :]):
         first = first + part[:latent].astype(F32)
         second = second + mm_tn(part_nodes[...], part[latent:])
     sums[0] = first
@@ -428,7 +438,7 @@
             ((node_count, latent), BF16),
             ((node_count, latent), BF16),
         ],
-        raw_near, raw_far, halo_hits, recv_hits, recv_rows, rows, table, stack,
+        raw_far, raw_near, halo_hits, recv_hits, recv_rows, rows, table, stack,
         scratch=[pltpu.VMEM((variables, 2 * width), BF16)],
     )
     from_far = lax.ppermute(to_far, around, ring_far)
@@ -474,40 +484,37 @@
 
     cols = latent // sectors
     rows = latent // bands
-    sends, slope, total = call(
+    sends, back, total = call(
         encode_grad_kernel,
         [
             ((lats - 1, doms - 1, latent, cols), BF16),
-            ((edges, latent), BF16),
+            ((2 * cycle, latent), BF16),
             ((doms, cycle, cols), BF16),
         ],
         recv_hits, part, from_far, from_near, home, node_slope, stack, senders, edge_slope,
     )
+    edge = (recv_hits, back, edge_slope, senders)
     came = [shifted(sends[i], "lat", i + 1) for i in range(lats - 1)]
+    block = (latent, cols)
+    (kept,) = call(kept_blocks_kernel, [((doms - 1,) + block, F32)], *edge, sends)
+    (own_sends,) = call(other_lats_kernel, [((lats - 1,) + block, BF16)], *edge, sends)
+    own_came = [shifted(own_sends[i], "lat", i + 1) for i in range(lats - 1)]
+    kept, own_sends = lax.optimization_barrier((kept, own_sends))
     (sends,) = call(
-        other_doms_kernel,
-        [((doms - 1, latent + cycle, cols), BF16)],
-        senders, slope, total, *came,
+        add_kernel, [((doms - 1, latent + cycle, cols), BF16)], kept, total, *came
     )
     other_doms = [shifted(sends[i], "dom", i + 1) for i in range(doms - 1)]
-    (sends,) = call(
-        other_lats_kernel, [((lats - 1, latent, cols), BF16)], senders, slope, sends
-    )
-    came = [shifted(sends[i], "lat", i + 1) for i in range(lats - 1)]
-    (kept,) = call(
-        own_block_kernel,
-        [((2, latent, cols), F32)],
-        senders, slope, total, mesh_one, *came,
-    )
+    (kept,) = call(own_block_kernel, [(block, F32)], *edge, *own_came)
     own, *sends = call(
         over_dom_kernel,
         [((2, rows, cols), F32)] + [((2, rows, cols), BF16)] * (bands - 1),
-        kept, *other_doms, *dom_nodes,
-        scratch=[pltpu.VMEM((2, latent, cols), F32)],
-    )
+        kept, total, mesh_one, *other_doms, *dom_nodes,
+        scratch=[pltpu.VMEM((2,) + block, F32)],
+    )
+    count = lax.axis_size("band")
     came = [
-        lax.ppermute(sends[i], "band", [(b, b ^ (i + 1)) for b in range(bands)])
-        for i in reversed(range(bands - 1))
+        lax.ppermute(x, "band", [(b, b ^ (i + 1)) for b in range(count)])
+        for i, x in enumerate(sends)
     ]
     tile = ((rows, cols), F32)
     grad_gs, grad_ms = call(over_band_kernel, [tile, tile], own, *came)

time: 61.7 us -> 62.4 us (1.011)
  starting transfers between devices: 20.8 us -> 21.9 us
  waiting for transfers between devices: 19.7 us -> 19 us
    ppermute x1, starting transfers between devices: 2.38 us -> 4.65 us  [on_device(): one_near = lax.ppermute(mesh_one, 'band', band_near)]
    ppermute x1, starting transfers between devices: 1.24 us -> 0.01 us  [on_device(): mesh_near = lax.ppermute(late_mesh, around, ring_near)]
    ppermute x1, starting transfers between devices: 0.44 us -> 1.67 us  [on_device(): mesh_far = lax.ppermute(late_mesh, around, ring_far)]
    ppermute x1, starting transfers between devices: 4.15 us -> 3.09 us  [on_device(): raw_near = lax.ppermute(grid, 'band', band_near)]
    ppermute x4, waiting for transfers between devices: 5.25 us -> 4.43 us  [shifted(): lax.ppermute(x, axis, [(i, (i + shift) % count) for i in range(count)])]
    pallas_call x13 -> x14, Pallas kernels: 13.5 us -> 13.7 us  [call(): pl.pallas_call(kernel, out_shape=[jax.ShapeDtypeStruct(shape, dtype) for...]
  transfers between devices with their start and end apart: 19 -> 19, of which waited for: 10 -> 8; matrix products, arithmetic and copies ran while one was open for 7% -> 7% of each run, Pallas kernels for 9% -> 10%
where the time goes in v10:
time: 62.4 us; the launch traced here: 62 us
  starting transfers between devices  21.9 us (35%)
  waiting for transfers between devices  19 us (30%)
  Pallas kernels  13.7 us (22%)
  local copies, waits for them, and re-layouts  4.43 us (7%)
  between operations  2.18 us (3%)
  other arithmetic  0.74 us (1%)
    pallas_call x14, Pallas kernels, call(): pl.pallas_call(kernel, out_shape=[jax.ShapeDtypeStruct(shape, dtype) for...  13.7 us
    ppermute x3, waiting for transfers between devices, on_device(): lax.ppermute(x, 'band', [(b, b ^ i + 1) for b in range(count)])  5.21 us
    ppermute x1, starting transfers between devices, on_device(): one_near = lax.ppermute(mesh_one, 'band', band_near)  4.65 us
    ppermute x3, starting transfers between devices, on_device(): lax.ppermute(x, 'band', [(b, b ^ i + 1) for b in range(count)])  4.6 us
    ppermute x4, waiting for transfers between devices, shifted(): lax.ppermute(x, axis, [(i, (i + shift) % count) for i in range(count)])  4.43 us
    unnamed x20, local copies, waits for them, and re-layouts  4.41 us
    ppermute x2, waiting for transfers between devices, on_device(): from_far = lax.ppermute(to_far, around, ring_far)  4.2 us
    ppermute x1, starting transfers between devices, on_device(): raw_near = lax.ppermute(grid, 'band', band_near)  3.09 us
  transfers between devices with their start and end apart: 19, of which 8 were waited for; matrix products, arithmetic and copies ran while one was open for 7% of the time, Pallas kernels for 10%

profile of v10, /device:TPU:0, one launch (start us, length us, event | category | flops | bytes accessed | tf_op | source)
XLA Modules:
  0.0 62.0 jit_solution(4746346372143687901)
XLA Ops:
  0.6 3.1 %collective-permute-start.1 = (bf16[3,227,360]{2,1,0:T(8,128)(2,1)}, bf16[3,227,360]{2,1,0:T(8,128)(2,1)S(1)}, u32[]{:S(2)}, u32[]{:S(2)}) collective-permute-start(bf16[3,227,360]{2,1,0:T(8,128)(2,1)} %bitcast.4), channel_id=1, source_target_pairs={{0,4},{4,0},{8,12},{12,8},{1,5},{5,1},{9,13},{13,9},{2,6},{6,2},{1... | collective-permute-start | bytes 1470968 | tf_op jit(solution)/shard_map/ppermute | solution.py:405
  5.0 0.7 %pad_add_fusion.indices = s32[1,1,3072]{2,1,0:T(1,128)S(1)} fusion(s32[1,1,512]{2,1,0:T(1,128)} %param.30, s32[1,1,512]{2,1,0:T(1,128)} %param.29, s32[1,1,1024]{2,1,0:T(1,128)} %param.27, s32[1,1,1024]{2,1,0:T(1,128)} %param.26), kind=kLoop, calls=%fused_computation.7 | loop fusion | flops 9216 | bytes 24576 | tf_op jit(solution)/shard_map/concatenate | solution.py:409
  5.8 1.0 %copy-done = bf16[3,360,227]{1,2,0:T(8,128)(2,1)S(1)} copy-done((bf16[3,360,227]{1,2,0:T(8,128)(2,1)S(1)}, bf16[3,360,227]{1,2,0:T(8,128)(2,1)}, u32[]{:S(2)}) %copy-start) | copy-done | bytes 490344
  6.8 1.7 %shard_map.175 = (bf16[1024,227]{1,0:T(8,128)(2,1)S(1)}, bf16[1024,128]{1,0:T(8,128)(2,1)S(1)}, bf16[64,1024]{1,0:T(8,128)(2,1)S(1)}, bf16[512,384]{1,0:T(8,128)...) custom-call(s32[1,1]{1,0:T(1,128)S(6)} %copy.25.count, ...), custom_call_target="tpu_custom_call" | custom-call | tf_op jit(solution)/shard_map/pallas_call | solution.py:350
  8.5 1.7 %collective-permute-start.3 = (bf16[32,512]{1,0:T(8,128)(2,1)}, bf16[32,512]{1,0:T(8,128)(2,1)S(1)}, u32[]{:S(2)}, u32[]{:S(2)}) collective-permute-start(bf16[32,512]{1,0:T(8,128)(2,1)} %mesh_in.3), channel_id=1, source_target_pairs={{0,3},{1,2},{2,1},{3,0},{4,7},{5,6},{6,5},{7,4},{8,11},{9,10},{10,... | collective-permute-start | bytes 98312 | tf_op jit(solution)/shard_map/ppermute | solution.py:428
  10.2 1.1 %constant_dynamic-update-slice_fusion.6 = bf16[3299,512]{1,0:T(8,128)(2,1)S(1)} fusion(bf16[512,512]{1,0:T(8,128)(2,1)} %param.18), kind=kLoop, calls=%fused_computation.6 | loop fusion | bytes 1048576
  11.3 1.1 %constant_dynamic-update-slice_fusion.5 = bf16[3299,512]{1,0:T(8,128)(2,1)S(1)} fusion(bf16[3299,512]{1,0:T(8,128)(2,1)S(1)} %constant_dynamic-update-slice_fusion.6, bf16[512,512]{1,0:T(8,128)(2,1)} %param.19), kind=kLoop, calls=%fused_computation.5 | loop fusion | bytes 1048576
  12.4 1.1 %constant_dynamic-update-slice_fusion.4 = bf16[3299,512]{1,0:T(8,128)(2,1)S(1)} fusion(bf16[3299,512]{1,0:T(8,128)(2,1)S(1)} %constant_dynamic-update-slice_fusion.5, bf16[512,512]{1,0:T(8,128)(2,1)} %param.20), kind=kLoop, calls=%fused_computation.4 | loop fusion | bytes 1048576
  13.9 2.2 %collective-permute-done.1.near = bf16[3,227,360]{2,1,0:T(8,128)(2,1)S(1)} collective-permute-done((bf16[3,227,360]{2,1,0:T(8,128)(2,1)}, bf16[3,227,360]{2,1,0:T(8,128)(2,1)S(1)}, u32[]{:S(2)}, u32[]{:S(2)}) %collective-permute-start.1) | collective-permute-done | bytes 490352 | tf_op jit(solution)/shard_map/ppermute | solution.py:405
  16.1 5.0 %shard_map.177 = (bf16[1024,512]{1,0:T(8,128)(2,1)S(1)}, bf16[1024,512]{1,0:T(8,128)(2,1)S(1)}, f32[64,512]{1,0:T(8,128)S(1)}, bf16[32,512]{1,0:T(8,128)(2,1)S(1)}, bf16[32,512]{1,0:T(8,128)(2,1)S(1)}) custom-call(bf16[3,227,360]{2,1,0:T(8,128)(2,1)S(1)} %collective-permute-done.far, bf16[3,227,360]{2,1,0:T(8,128)(2,1)S(1)} %collective-permute-done.1.near, ...), custom_call_target="tpu_custom_call" | custom-call | tf_op jit(solution)/shard_map/pallas_call | solution.py:350
  21.4 1.5 %collective-permute-start.5 = (bf16[32,512]{1,0:T(8,128)(2,1)S(1)}, bf16[32,512]{1,0:T(8,128)(2,1)S(1)}, u32[]{:S(2)}, u32[]{:S(2)}) collective-permute-start(bf16[32,512]{1,0:T(8,128)(2,1)S(1)} %get-tuple-element.54), channel_id=1, source_target_pairs={{0,1},{1,0},{2,3},{3,2},{4,5},{5,4},{6,7},{7,6},{8,9},{9,8},{10,11... | collective-permute-start | bytes 98312 | tf_op jit(solution)/shard_map/ppermute | solution.py:445
  23.0 1.7 %collective-permute-done.4.far = bf16[32,512]{1,0:T(8,128)(2,1)S(1)} collective-permute-done((bf16[32,512]{1,0:T(8,128)(2,1)S(1)}, bf16[32,512]{1,0:T(8,128)(2,1)S(1)}, u32[]{:S(2)}, u32[]{:S(2)}) %collective-permute-start.4) | collective-permute-done | bytes 32800 | tf_op jit(solution)/shard_map/ppermute | solution.py:444
  25.1 4.6 %collective-permute-start.6 = (bf16[64,512]{1,0:T(8,128)(2,1)S(1)}, bf16[64,512]{1,0:T(8,128)(2,1)S(1)}, u32[]{:S(2)}, u32[]{:S(2)}) collective-permute-start(bf16[64,512]{1,0:T(8,128)(2,1)S(1)} %get-tuple-element.55.own.nodes), channel_id=1, source_target_pairs={{0,4},{4,0},{8,12},{12,8},{1,5},{5,1},{9,13},{13,9},{2,6},{6,2},{1... | collective-permute-start | bytes 196616 | tf_op jit(solution)/shard_map/ppermute | solution.py:451
  29.8 1.2 %collective-permute-start.9 = (bf16[64,512]{1,0:T(8,128)(2,1)S(1)}, bf16[64,512]{1,0:T(8,128)(2,1)S(1)}, u32[]{:S(2)}, u32[]{:S(2)}) collective-permute-start(bf16[64,512]{1,0:T(8,128)(2,1)S(1)} %get-tuple-element.55.own.nodes), channel_id=1, source_target_pairs={{0,2},{2,0},{1,3},{3,1},{4,6},{6,4},{5,7},{7,5},{8,10},{10,8},{9,1... | collective-permute-start | bytes 196616 | tf_op jit(solution)/shard_map/ppermute | solution.py:382
  31.0 1.0 %collective-permute-done.6.near = bf16[64,512]{1,0:T(8,128)(2,1)S(1)} collective-permute-done((bf16[64,512]{1,0:T(8,128)(2,1)S(1)}, bf16[64,512]{1,0:T(8,128)(2,1)S(1)}, u32[]{:S(2)}, u32[]{:S(2)}) %collective-permute-start.6) | collective-permute-done | bytes 65568 | tf_op jit(solution)/shard_map/ppermute | solution.py:451
  32.0 2.0 %shard_map.179 = (bf16[32,512]{1,0:T(8,128)(2,1)}, f32[192,512]{1,0:T(8,128)S(1)}, bf16[32,512]{1,0:T(8,128)(2,1)S(1)}, bf16[64,512]{1,0:T(8,128)(2,1)S(1)}, bf16[64,512]{1,0:T(8,128)(2,1)S(1)}) custom-call(bf16[512,384]{1,0:T(8,128)(2,1)S(1)} %get-tuple-element.42.from_hits, bf16[512,64]{1,0:T(8,128)(2,1)S(1)} %get-tuple-element.43.to_hits, ...), custom_call_target="tpu_custom_call" | custom-call | tf_op jit(solution)/shard_map/pallas_call | solution.py:350
  34.0 2.1 %collective-permute-start.8 = (bf16[64,512]{1,0:T(8,128)(2,1)S(1)}, bf16[64,512]{1,0:T(8,128)(2,1)S(1)}, u32[]{:S(2)}, u32[]{:S(2)}) collective-permute-start(bf16[64,512]{1,0:T(8,128)(2,1)S(1)} %get-tuple-element.58), channel_id=1, source_target_pairs={{0,4},{4,0},{8,12},{12,8},{1,5},{5,1},{9,13},{13,9},{2,6},{6,2},{1... | collective-permute-start | bytes 196616 | tf_op jit(solution)/shard_map/ppermute | solution.py:468
  36.1 0.4 shard_map.180
  36.5 1.9 %collective-permute-done.8.near = bf16[64,512]{1,0:T(8,128)(2,1)S(1)} collective-permute-done((bf16[64,512]{1,0:T(8,128)(2,1)S(1)}, bf16[64,512]{1,0:T(8,128)(2,1)S(1)}, u32[]{:S(2)}, u32[]{:S(2)}) %collective-permute-start.8) | collective-permute-done | bytes 65568 | tf_op jit(solution)/shard_map/ppermute | solution.py:468
  38.5 1.3 %collective-permute-start.12 = (bf16[48,512]{1,0:T(8,128)(2,1)S(1)}, bf16[48,512]{1,0:T(8,128)(2,1)S(1)}, u32[]{:S(2)}, u32[]{:S(2)}) collective-permute-start(bf16[48,512]{1,0:T(8,128)(2,1)S(1)} %get-tuple-element.66), channel_id=1, source_target_pairs={{0,1},{1,0},{2,3},{3,2},{4,5},{5,4},{6,7},{7,6},{8,9},{9,8},{10,11... | collective-permute-start | bytes 147464 | tf_op jit(solution)/shard_map/ppermute | solution.py:483
  39.8 2.5 %collective-permute-done.11.far = bf16[48,512]{1,0:T(8,128)(2,1)S(1)} collective-permute-done((bf16[48,512]{1,0:T(8,128)(2,1)S(1)}, bf16[48,512]{1,0:T(8,128)(2,1)S(1)}, u32[]{:S(2)}, u32[]{:S(2)}) %collective-permute-start.11) | collective-permute-done | bytes 49184 | tf_op jit(solution)/shard_map/ppermute | solution.py:482
  42.2 1.1 %shard_map.182 = (bf16[1,1,512,128]{3,2,1,0:T(8,128)(2,1)S(1)}, bf16[128,512]{1,0:T(8,128)(2,1)S(1)}, bf16[2,64,128]{2,1,0:T(8,128)(2,1)S(1)}) custom-call(bf16[1024,128]{1,0:T(8,128)(2,1)S(1)} %get-tuple-element.47.recv_hits, f32[64,512]{1,0:T(8,128)S(1)} %get-tuple-element.64.part, bf16[48,512]{1,0:T(8,128)(2,1)S(1)} %collective-permute-done.11.far, ...), custom_call_target="tpu_custom_call" | custom-call | tf_op jit(solution)/shard_map/pallas_call | solution.py:350
  43.5 0.7 %shard_map.183 = bf16[1,512,128]{2,1,0:T(8,128)(2,1)S(1)} custom-call(bf16[1024,128]{1,0:T(8,128)(2,1)S(1)} %get-tuple-element.47.recv_hits, bf16[128,512]{1,0:T(8,128)(2,1)S(1)} %get-tuple-element.70.back, bf16[1024,512]{1,0:T(8,128)(2,1)S(1)} %get-tuple-element.69.edge_slope, bf16[512,1024]{1,0:T(8,128)(2,1)S(1)} %get-tuple-element.68.senders, ...), custom_call_target="tpu_custom_call" | custom-call | tf_op jit(solution)/shard_map/pallas_call | solution.py:350
  44.2 0.7 %shard_map.185.kept = f32[1,512,128]{2,1,0:T(8,128)S(1)} custom-call(bf16[1024,128]{1,0:T(8,128)(2,1)S(1)} %get-tuple-element.47.recv_hits, bf16[128,512]{1,0:T(8,128)(2,1)S(1)} %get-tuple-element.70.back, bf16[1024,512]{1,0:T(8,128)(2,1)S(1)} %get-tuple-element.69.edge_slope, bf16[512,1024]{1,0:T(8,128)(2,1)S(1)} %get-tuple-element.68.senders, ...), custom_call_target="tpu_custom_call" | custom-call | tf_op jit(solution)/shard_map/pallas_call | solution.py:350
  44.9 1.0 %collective-permute-start.15 = (bf16[576,128]{1,0:T(8,128)(2,1)S(1)}, bf16[576,128]{1,0:T(8,128)(2,1)S(1)}, u32[]{:S(2)}, u32[]{:S(2)}) collective-permute-start(bf16[576,128]{1,0:T(8,128)(2,1)S(1)} %bitcast.8), channel_id=1, source_target_pairs={{0,2},{2,0},{1,3},{3,1},{4,6},{6,4},{5,7},{7,5},{8,10},{10,8},{9,1... | collective-permute-start | bytes 442376 | tf_op jit(solution)/shard_map/ppermute | solution.py:382
  46.1 1.1 %collective-permute-done.13.refs_0_ = bf16[512,128]{1,0:T(8,128)(2,1)S(1)} collective-permute-done((bf16[512,128]{1,0:T(8,128)(2,1)S(1)}, bf16[512,128]{1,0:T(8,128)(2,1)S(1)}, u32[]{:S(2)}, u32[]{:S(2)}) %collective-permute-start.13) | collective-permute-done | bytes 131104 | tf_op jit(solution)/shard_map/ppermute | solution.py:382
  47.2 0.7 %shard_map.184.kept = f32[512,128]{1,0:T(8,128)S(1)} custom-call(bf16[1024,128]{1,0:T(8,128)(2,1)S(1)} %get-tuple-element.47.recv_hits, bf16[128,512]{1,0:T(8,128)(2,1)S(1)} %get-tuple-element.70.back, bf16[1024,512]{1,0:T(8,128)(2,1)S(1)} %get-tuple-element.69.edge_slope, bf16[512,1024]{1,0:T(8,128)(2,1)S(1)} %get-tuple-element.68.senders, ...), custom_call_target="tpu_custom_call" | custom-call | tf_op jit(solution)/shard_map/pallas_call | solution.py:350
  47.9 3.3 %collective-permute-done.15.refs_0_ = bf16[576,128]{1,0:T(8,128)(2,1)S(1)} collective-permute-done((bf16[576,128]{1,0:T(8,128)(2,1)S(1)}, bf16[576,128]{1,0:T(8,128)(2,1)S(1)}, u32[]{:S(2)}, u32[]{:S(2)}) %collective-permute-start.15) | collective-permute-done | bytes 147488 | tf_op jit(solution)/shard_map/ppermute | solution.py:382
  51.5 2.2 %collective-permute-start.16 = (bf16[2,128,128]{2,1,0:T(8,128)(2,1)S(1)}, bf16[2,128,128]{2,1,0:T(8,128)(2,1)S(1)}, u32[]{:S(2)}, u32[]{:S(2)}) collective-permute-start(bf16[2,128,128]{2,1,0:T(8,128)(2,1)S(1)} %get-tuple-element.76), channel_id=1, source_target_pairs={{0,4},{4,0},{8,12},{12,8},{1,5},{5,1},{9,13},{13,9},{2,6},{6,2},{1... | collective-permute-start | bytes 196616 | tf_op jit(solution)/shard_map/ppermute | solution.py:516
  53.7 2.4 %collective-permute-start.18 = (bf16[2,128,128]{2,1,0:T(8,128)(2,1)S(1)}, bf16[2,128,128]{2,1,0:T(8,128)(2,1)S(1)}, u32[]{:S(2)}, u32[]{:S(2)}) collective-permute-start(bf16[2,128,128]{2,1,0:T(8,128)(2,1)S(1)} %get-tuple-element.78), channel_id=1, source_target_pairs={{0,12},{4,8},{8,4},{12,0},{1,13},{5,9},{9,5},{13,1},{2,14},{6,10},... | collective-permute-start | bytes 196616 | tf_op jit(solution)/shard_map/ppermute | solution.py:516
  56.1 5.2 %collective-permute-done.17.refs_1_ = bf16[2,128,128]{2,1,0:T(8,128)(2,1)S(1)} collective-permute-done((bf16[2,128,128]{2,1,0:T(8,128)(2,1)S(1)}, bf16[2,128,128]{2,1,0:T(8,128)(2,1)S(1)}, u32[]{:S(2)}, u32[]{:S(2)}) %collective-permute-start.17) | collective-permute-done | bytes 65568 | tf_op jit(solution)/shard_map/ppermute | solution.py:516
  61.3 0.7 %shard_map.188 = (f32[128,128]{1,0:T(8,128)}, f32[128,128]{1,0:T(8,128)}) custom-call(f32[2,128,128]{2,1,0:T(8,128)S(1)} %get-tuple-element.75.own, bf16[2,128,128]{2,1,0:T(8,128)(2,1)S(1)} %collective-permute-done.16.refs_0_, bf16[2,128,128]{2,1,0:T(8,128)(2,1)S(1)} %collective-permute-done.17.refs_1_, bf16[2,128,128]{2,1,0:T(8,128)(2,1)S(1)} %collective-permute-done.18.refs_2_), custom_call_target="tpu_custom_call" | custom-call | tf_op jit(solution)/shard_map/pallas_call | solution.py:350
  (42 shorter events, 1.8 us)
Async XLA Ops:
  0.6 15.4 %collective-permute-start.1 = (bf16[3,227,360]{2,1,0:T(8,128)(2,1)}, bf16[3,227,360]{2,1,0:T(8,128)(2,1)S(1)}, u32[]{:S(2)}, u32[]{:S(2)}) collective-permute-start(bf16[3,227,360]{2,1,0:T(8,128)(2,1)} %bitcast.4), channel_id=1, source_target_pairs={{0,4},{4,0},{8,12},{12,8},{1,5},{5,1},{9,13},{13,9},{2,6},{6,2},{1... | collective-permute-start | bytes 1470968 | tf_op jit(solution)/shard_map/ppermute | solution.py:405
  3.7 12.4 %collective-permute-start = (bf16[3,227,360]{2,1,0:T(8,128)(2,1)}, bf16[3,227,360]{2,1,0:T(8,128)(2,1)S(1)}, u32[]{:S(2)}, u32[]{:S(2)}) collective-permute-start(bf16[3,227,360]{2,1,0:T(8,128)(2,1)} %bitcast.5), channel_id=1, source_target_pairs={{0,1},{1,0},{2,3},{3,2},{4,8},{5,9},{6,10},{7,11},{8,4},{9,5},{10,... | collective-permute-start | bytes 1470968 | tf_op jit(solution)/shard_map/ppermute | solution.py:406
  5.8 1.0 %copy-start = (bf16[3,360,227]{1,2,0:T(8,128)(2,1)S(1)}, bf16[3,360,227]{1,2,0:T(8,128)(2,1)}, u32[]{:S(2)}) copy-start(bf16[3,360,227]{1,2,0:T(8,128)(2,1)} %param.16) | copy-start | bytes 1470964
  6.8 6.6 %copy-start.3 = (bf16[512,512]{1,0:T(8,128)(2,1)S(1)}, bf16[512,512]{1,0:T(8,128)(2,1)}, u32[]{:S(2)}) copy-start(bf16[512,512]{1,0:T(8,128)(2,1)} %param.21) | copy-start | bytes 1572868
  6.8 6.7 %copy-start.4 = (bf16[512,512]{1,0:T(8,128)(2,1)S(1)}, bf16[512,512]{1,0:T(8,128)(2,1)}, u32[]{:S(2)}) copy-start(bf16[512,512]{1,0:T(8,128)(2,1)} %param.22) | copy-start | bytes 1572868
  6.8 6.7 %copy-start.5 = (bf16[512,512]{1,0:T(8,128)(2,1)S(1)}, bf16[512,512]{1,0:T(8,128)(2,1)}, u32[]{:S(2)}) copy-start(bf16[512,512]{1,0:T(8,128)(2,1)} %param.23) | copy-start | bytes 1572868
  6.8 6.8 %copy-start.6 = (bf16[227,512]{1,0:T(8,128)(2,1)S(1)}, bf16[227,512]{1,0:T(8,128)(2,1)}, u32[]{:S(2)}) copy-start(bf16[227,512]{1,0:T(8,128)(2,1)} %param.17) | copy-start | bytes 697348
  8.5 5.1 %copy-start.1 = (bf16[32,512]{1,0:T(8,128)(2,1)S(1)}, bf16[32,512]{1,0:T(8,128)(2,1)}, u32[]{:S(2)}) copy-start(bf16[32,512]{1,0:T(8,128)(2,1)} %mesh_in.3) | copy-start | bytes 98308
  8.5 5.1 %collective-permute-start.3 = (bf16[32,512]{1,0:T(8,128)(2,1)}, bf16[32,512]{1,0:T(8,128)(2,1)S(1)}, u32[]{:S(2)}, u32[]{:S(2)}) collective-permute-start(bf16[32,512]{1,0:T(8,128)(2,1)} %mesh_in.3), channel_id=1, source_target_pairs={{0,3},{1,2},{2,1},{3,0},{4,7},{5,6},{6,5},{7,4},{8,11},{9,10},{10,... | collective-permute-start | bytes 98312 | tf_op jit(solution)/shard_map/ppermute | solution.py:428
  10.2 3.5 %collective-permute-start.2 = (bf16[32,512]{1,0:T(8,128)(2,1)}, bf16[32,512]{1,0:T(8,128)(2,1)S(1)}, u32[]{:S(2)}, u32[]{:S(2)}) collective-permute-start(bf16[32,512]{1,0:T(8,128)(2,1)} %mesh_in.3), channel_id=1, source_target_pairs={{0,1},{1,0},{2,3},{3,2},{4,5},{5,4},{6,7},{7,6},{8,9},{9,8},{10,11... | collective-permute-start | bytes 98312 | tf_op jit(solution)/shard_map/ppermute | solution.py:427
  21.1 10.9 %copy-start.2 = (bf16[32,512]{1,0:T(8,128)(2,1)S(1)}, bf16[32,512]{1,0:T(8,128)(2,1)}, u32[]{:S(2)}) copy-start(bf16[32,512]{1,0:T(8,128)(2,1)} %d_out.3) | copy-start | bytes 98308
  21.1 3.5 %collective-permute-start.4 = (bf16[32,512]{1,0:T(8,128)(2,1)S(1)}, bf16[32,512]{1,0:T(8,128)(2,1)S(1)}, u32[]{:S(2)}, u32[]{:S(2)}) collective-permute-start(bf16[32,512]{1,0:T(8,128)(2,1)S(1)} %get-tuple-element.53), channel_id=1, source_target_pairs={{0,3},{1,2},{2,1},{3,0},{4,7},{5,6},{6,5},{7,4},{8,11},{9,10},{10,... | collective-permute-start | bytes 98312 | tf_op jit(solution)/shard_map/ppermute | solution.py:444
  21.4 3.3 %collective-permute-start.5 = (bf16[32,512]{1,0:T(8,128)(2,1)S(1)}, bf16[32,512]{1,0:T(8,128)(2,1)S(1)}, u32[]{:S(2)}, u32[]{:S(2)}) collective-permute-start(bf16[32,512]{1,0:T(8,128)(2,1)S(1)} %get-tuple-element.54), channel_id=1, source_target_pairs={{0,1},{1,0},{2,3},{3,2},{4,5},{5,4},{6,7},{7,6},{8,9},{9,8},{10,11... | collective-permute-start | bytes 98312 | tf_op jit(solution)/shard_map/ppermute | solution.py:445
  24.9 6.0 %collective-permute-start.7 = (bf16[64,512]{1,0:T(8,128)(2,1)S(1)}, bf16[64,512]{1,0:T(8,128)(2,1)S(1)}, u32[]{:S(2)}, u32[]{:S(2)}) collective-permute-start(bf16[64,512]{1,0:T(8,128)(2,1)S(1)} %get-tuple-element.55.own.nodes), channel_id=1, source_target_pairs={{0,1},{1,0},{2,3},{3,2},{4,8},{5,9},{6,10},{7,11},{8,4},{9,5},{10,... | collective-permute-start | bytes 196616 | tf_op jit(solution)/shard_map/ppermute | solution.py:452
  25.1 6.9 %collective-permute-start.6 = (bf16[64,512]{1,0:T(8,128)(2,1)S(1)}, bf16[64,512]{1,0:T(8,128)(2,1)S(1)}, u32[]{:S(2)}, u32[]{:S(2)}) collective-permute-start(bf16[64,512]{1,0:T(8,128)(2,1)S(1)} %get-tuple-element.55.own.nodes), channel_id=1, source_target_pairs={{0,4},{4,0},{8,12},{12,8},{1,5},{5,1},{9,13},{13,9},{2,6},{6,2},{1... | collective-permute-start | bytes 196616 | tf_op jit(solution)/shard_map/ppermute | solution.py:451
  29.8 6.7 %collective-permute-start.9 = (bf16[64,512]{1,0:T(8,128)(2,1)S(1)}, bf16[64,512]{1,0:T(8,128)(2,1)S(1)}, u32[]{:S(2)}, u32[]{:S(2)}) collective-permute-start(bf16[64,512]{1,0:T(8,128)(2,1)S(1)} %get-tuple-element.55.own.nodes), channel_id=1, source_target_pairs={{0,2},{2,0},{1,3},{3,1},{4,6},{6,4},{5,7},{7,5},{8,10},{10,8},{9,1... | collective-permute-start | bytes 196616 | tf_op jit(solution)/shard_map/ppermute | solution.py:382
  34.0 4.3 %collective-permute-start.8 = (bf16[64,512]{1,0:T(8,128)(2,1)S(1)}, bf16[64,512]{1,0:T(8,128)(2,1)S(1)}, u32[]{:S(2)}, u32[]{:S(2)}) collective-permute-start(bf16[64,512]{1,0:T(8,128)(2,1)S(1)} %get-tuple-element.58), channel_id=1, source_target_pairs={{0,4},{4,0},{8,12},{12,8},{1,5},{5,1},{9,13},{13,9},{2,6},{6,2},{1... | collective-permute-start | bytes 196616 | tf_op jit(solution)/shard_map/ppermute | solution.py:468
  36.1 2.2 %collective-permute-start.10 = (bf16[64,512]{1,0:T(8,128)(2,1)S(1)}, bf16[64,512]{1,0:T(8,128)(2,1)S(1)}, u32[]{:S(2)}, u32[]{:S(2)}) collective-permute-start(bf16[64,512]{1,0:T(8,128)(2,1)S(1)} %get-tuple-element.60), channel_id=1, source_target_pairs={{0,1},{1,0},{2,3},{3,2},{4,8},{5,9},{6,10},{7,11},{8,4},{9,5},{10,... | collective-permute-start | bytes 196616 | tf_op jit(solution)/shard_map/ppermute | solution.py:469
  38.4 3.9 %collective-permute-start.11 = (bf16[48,512]{1,0:T(8,128)(2,1)S(1)}, bf16[48,512]{1,0:T(8,128)(2,1)S(1)}, u32[]{:S(2)}, u32[]{:S(2)}) collective-permute-start(bf16[48,512]{1,0:T(8,128)(2,1)S(1)} %get-tuple-element.65), channel_id=1, source_target_pairs={{0,3},{1,2},{2,1},{3,0},{4,7},{5,6},{6,5},{7,4},{8,11},{9,10},{10,... | collective-permute-start | bytes 147464 | tf_op jit(solution)/shard_map/ppermute | solution.py:482
  38.5 3.8 %collective-permute-start.12 = (bf16[48,512]{1,0:T(8,128)(2,1)S(1)}, bf16[48,512]{1,0:T(8,128)(2,1)S(1)}, u32[]{:S(2)}, u32[]{:S(2)}) collective-permute-start(bf16[48,512]{1,0:T(8,128)(2,1)S(1)} %get-tuple-element.66), channel_id=1, source_target_pairs={{0,1},{1,0},{2,3},{3,2},{4,5},{5,4},{6,7},{7,6},{8,9},{9,8},{10,11... | collective-permute-start | bytes 147464 | tf_op jit(solution)/shard_map/ppermute | solution.py:483
  43.4 1.5 %collective-permute-start.14 = (bf16[1,512,128]{2,1,0:T(8,128)(2,1)S(1)}, bf16[1,512,128]{2,1,0:T(8,128)(2,1)S(1)}, u32[]{:S(2)}, u32[]{:S(2)}) collective-permute-start(bf16[1,512,128]{2,1,0:T(8,128)(2,1)S(1)} %bitcast.7), channel_id=1, source_target_pairs={{0,1},{1,0},{2,3},{3,2},{4,5},{5,4},{6,7},{7,6},{8,9},{9,8},{10,11... | collective-permute-start | bytes 393224 | tf_op jit(solution)/shard_map/ppermute | solution.py:382
  44.9 6.3 %collective-permute-start.15 = (bf16[576,128]{1,0:T(8,128)(2,1)S(1)}, bf16[576,128]{1,0:T(8,128)(2,1)S(1)}, u32[]{:S(2)}, u32[]{:S(2)}) collective-permute-start(bf16[576,128]{1,0:T(8,128)(2,1)S(1)} %bitcast.8), channel_id=1, source_target_pairs={{0,2},{2,0},{1,3},{3,1},{4,6},{6,4},{5,7},{7,5},{8,10},{10,8},{9,1... | collective-permute-start | bytes 442376 | tf_op jit(solution)/shard_map/ppermute | solution.py:382
  45.9 1.3 %collective-permute-start.13 = (bf16[512,128]{1,0:T(8,128)(2,1)S(1)}, bf16[512,128]{1,0:T(8,128)(2,1)S(1)}, u32[]{:S(2)}, u32[]{:S(2)}) collective-permute-start(bf16[512,128]{1,0:T(8,128)(2,1)S(1)} %bitcast.9), channel_id=1, source_target_pairs={{0,1},{1,0},{2,3},{3,2},{4,5},{5,4},{6,7},{7,6},{8,9},{9,8},{10,11... | collective-permute-start | bytes 393224 | tf_op jit(solution)/shard_map/ppermute | solution.py:382
  51.5 4.6 %collective-permute-start.16 = (bf16[2,128,128]{2,1,0:T(8,128)(2,1)S(1)}, bf16[2,128,128]{2,1,0:T(8,128)(2,1)S(1)}, u32[]{:S(2)}, u32[]{:S(2)}) collective-permute-start(bf16[2,128,128]{2,1,0:T(8,128)(2,1)S(1)} %get-tuple-element.76), channel_id=1, source_target_pairs={{0,4},{4,0},{8,12},{12,8},{1,5},{5,1},{9,13},{13,9},{2,6},{6,2},{1... | collective-permute-start | bytes 196616 | tf_op jit(solution)/shard_map/ppermute | solution.py:516
  53.7 7.6 %collective-permute-start.17 = (bf16[2,128,128]{2,1,0:T(8,128)(2,1)S(1)}, bf16[2,128,128]{2,1,0:T(8,128)(2,1)S(1)}, u32[]{:S(2)}, u32[]{:S(2)}) collective-permute-start(bf16[2,128,128]{2,1,0:T(8,128)(2,1)S(1)} %get-tuple-element.77), channel_id=1, source_target_pairs={{0,8},{4,12},{8,0},{12,4},{1,9},{5,13},{9,1},{13,5},{2,10},{6,14},... | collective-permute-start | bytes 196616 | tf_op jit(solution)/shard_map/ppermute | solution.py:516
  53.7 7.6 %collective-permute-start.18 = (bf16[2,128,128]{2,1,0:T(8,128)(2,1)S(1)}, bf16[2,128,128]{2,1,0:T(8,128)(2,1)S(1)}, u32[]{:S(2)}, u32[]{:S(2)}) collective-permute-start(bf16[2,128,128]{2,1,0:T(8,128)(2,1)S(1)} %get-tuple-element.78), channel_id=1, source_target_pairs={{0,12},{4,8},{8,4},{12,0},{1,13},{5,9},{9,5},{13,1},{2,14},{6,10},... | collective-permute-start | bytes 196616 | tf_op jit(solution)/shard_map/ppermute | solution.py:516

commit v11 on v10

--- a/solution.py
+++ b/solution.py
@@ -96,7 +96,7 @@
 
 def index_kernel(
     count, mesh_count, indices, grid,
-    own_out, recv_hits, recv_rows, from_hits, to_hits, from_rows, to_rows, halo_hits, wide,
+    own_out, recv_hits, recv_rows, own_hits, outer_hits, to_hits, from_rows, to_rows, halo_hits, wide,
 ):
     edges = recv_hits.shape[0]
     mesh_edges = to_hits.shape[0]
@@ -130,32 +130,33 @@
         recv_hits[part_of] = hits_from(columns(target), 2 * cycle, cycle)
         recv_rows[:, part_of] = hits_to(target, cycle)
     raw = mesh_send
-    flipped = jnp.where(
-        raw < cycle, raw + 2 * cycle, jnp.where(raw < 2 * cycle, raw, raw - 2 * cycle)
-    )
-    source = jnp.where(even_band, flipped, raw)
+    inner = (raw >= cycle) & (raw < 2 * cycle)
+    above_near = jnp.where(raw < cycle, raw + cycle, raw - 2 * cycle)
+    below_near = jnp.where(raw < cycle, raw, raw - cycle)
+    outer = jnp.where(inner, -1, jnp.where(even_band, above_near, below_near))
     target = live_only(mesh_recv, mesh_count[0, 0])
-    from_hits[...] = hits_from(columns(source), 6 * cycle, 3 * cycle)
+    own_hits[...] = hits_from(columns(jnp.where(inner, raw - cycle, -1)), 2 * cycle, cycle)
+    outer_hits[...] = hits_from(columns(outer), 4 * cycle, 2 * cycle)
     to_hits[...] = hits_from(columns(target), 2 * node_count, node_count)
+    source = jnp.where(inner, raw, jnp.where(outer < cycle, outer, outer + cycle))
     from_rows[...] = hits_to(source, 3 * cycle)
     to_rows[...] = hits_to(target, node_count)
 
 
-def table_kernel(near, far, mesh_in, stack, table_out):
+def receiver_kernel(near, far, mesh_in, recv_hits, stack, pre_out):
     node_count = mesh_in.shape[0]
     rim = node_count // 2
     even = even_on("lat")
     left = jnp.where(even, far[...], near[...])[rim:]
     right = jnp.where(even, near[...], far[...])[:rim]
     cycle = jnp.concatenate([left, mesh_in[...], right], axis=0)
-    high, low = halves(mm(cycle, weight(stack, GR)))
-    table_out[: 2 * node_count] = high
-    table_out[2 * node_count :] = low
+    table = jnp.concatenate(halves(mm(cycle, weight(stack, GR))), axis=0)
+    pre_out[...] = mm(recv_hits[...], table)
 
 
 def encode_kernel(
-    far, near, halo_hits, recv_hits, recv_rows, own, table, stack,
-    senders_out, slope_out, part_out, far_out, near_out, wide,
+    near, far, halo_hits, recv_rows, own, recv_pre, stack,
+    senders_out, slope_out, part_out, near_out, far_out, wide,
 ):
     half = recv_rows.shape[0] // 2
     width = wide.shape[1] // 2
@@ -166,7 +167,7 @@
     latent, _ = silu_parts(mm(raw, stack[stack.shape[0] - raw.shape[1] :]))
     latent = latent.astype(BF16)
     senders_out[...] = latent
-    pre = mm(latent, weight(stack, GS)) + mm(recv_hits[...], table[...])
+    pre = mm(latent, weight(stack, GS)) + recv_pre[...]
     value, slope = silu_parts(pre)
     slope_out[...] = slope.astype(BF16)
     sums = mm(recv_rows[...], value.astype(BF16))
@@ -176,7 +177,7 @@
     far_out[...] = jnp.where(even, sums[:half], sums[half:]).astype(BF16)
 
 
-def node_kernel(part, far, near, mesh_near, mesh_far, mesh_in, stack, mesh_out, slope_out):
+def node_kernel(part, near, far, mesh_near, mesh_far, mesh_in, stack, mesh_out, slope_out):
     node_count = mesh_in.shape[0]
     rim = node_count // 2
     even = even_on("lat")
@@ -191,18 +192,25 @@
     slope_out[...] = slope
 
 
+def process_own_kernel(own_hits, to_hits, own, stack, pre_out):
+    rim = own.shape[0] // 4
+    home = own[rim : own.shape[0] - rim]
+    table = jnp.concatenate(halves(mm(own[...], weight(stack, MS))), axis=0)
+    recv_table = jnp.concatenate(halves(mm(home, weight(stack, MR))), axis=0)
+    pre_out[...] = mm(own_hits[...], table) + mm(to_hits[...], recv_table)
+
+
 def process_kernel(
-    from_hits, to_hits, from_rows, to_rows, near, own, far, d_out, stack,
+    own_pre, outer_hits, to_hits, from_rows, to_rows, near, own, far, d_out, stack,
     mesh_out, sums_out, recv_out, near_out, far_out,
 ):
     cycle = own.shape[0]
     node_count = cycle // 2
     rim = node_count // 2
     home = own[rim : rim + node_count]
-    block = jnp.concatenate([near[...], own[...], far[...]], axis=0)
+    block = jnp.concatenate([near[...], far[...]], axis=0)
     table = jnp.concatenate(halves(mm(block, weight(stack, MS))), axis=0)
-    recv_table = jnp.concatenate(halves(mm(home, weight(stack, MR))), axis=0)
-    pre = mm(from_hits[...], table) + mm(to_hits[...], recv_table)
+    pre = own_pre[...] + mm(outer_hits[...], table)
     value, slope = silu_parts(pre)
     gate = mm(mm(to_rows[...], value.astype(BF16)).astype(BF16), weight(stack, MN))
     gate_value, gate_slope = silu_parts(gate)
@@ -232,7 +240,7 @@
     turned_out[...] = senders[...].T
 
 
-def cotangent_kernel(sums, near, far, home, part_out, far_out, near_out):
+def cotangent_kernel(sums, near, far, home, part_out, near_out, far_out):
     cycle = near.shape[0]
     half = cycle // 2
     rim = half // 2
@@ -253,7 +261,7 @@
 
 
 def encode_grad_kernel(
-    recv_hits, part, far, near, home, node_slope, stack, senders, edge_slope,
+    recv_hits, part, near, far, home, node_slope, stack, senders, edge_slope,
     sends, back_out, total_out,
 ):
     half = part.shape[0] // 2
@@ -284,15 +292,27 @@
         kept[j - 1] = gradient_block(recv_hits, back, edge_slope, senders, j, 0, doms, lats)
 
 
+def rows_at(ref, place, partner):
+    bands = lax.axis_size("band")
+    rows = ref.shape[-2] // bands
+    at = pl.multiple_of(lax.bitwise_xor(lax.axis_index("band"), partner) * rows, rows)
+    return ref[(*place, pl.ds(at, rows))]
+
+
 def add_kernel(kept, total, *refs):
-    *came, out = refs
-    rows = kept.shape[1]
+    *came, first_out, second_out = refs
+    bands = lax.axis_size("band")
+    half = bands // 2
+    rows = kept.shape[1] // bands
     for j in range(kept.shape[0]):
-        block = kept[j]
-        for part in came:
-            block = block + part[j].astype(F32)
-        out[j, :rows] = block.astype(BF16)
-        out[j, rows:] = total[j + 1]
+        for k in range(bands):
+            block = rows_at(kept, (j,), k)
+            for part in came:
+                block = block + rows_at(part, (j,), k).astype(F32)
+            out = first_out if k >= half else second_out
+            at = (k % half) * rows
+            out[j, at : at + rows] = block.astype(BF16)
+        first_out[j, half * rows :] = total[j + 1]
 
 
 def other_lats_kernel(recv_hits, back, edge_slope, senders, after, sends):
@@ -313,28 +333,38 @@
     out[...] = block
 
 
-def over_dom_kernel(kept, total, nodes, *refs):
-    latent = kept.shape[0]
-    rows = latent // lax.axis_size("band")
+def first_kernel(kept, total, nodes, *refs):
     doms = total.shape[0]
-    came, (own_out, *sends_out, sums) = refs[: 2 * (doms - 1)], refs[2 * (doms - 1) :]
-    first = kept[...]
+    came, (*sends_out, sums) = refs[: 2 * (doms - 1)], refs[2 * (doms - 1) :]
+    came, came_nodes = came[: doms - 1], came[doms - 1 :]
+    half = len(sends_out)
+    rows = sends_out[0].shape[1]
     second = mm_tn(nodes[...], total[0])
-    for part, part_nodes in zip(came[: doms - 1], came[doms - 1 :]):
-        first = first + part[:latent].astype(F32)
-        second = second + mm_tn(part_nodes[...], part[latent:])
-    sums[0] = first
-    sums[1] = second
-    me = lax.axis_index("band")
-    for k in range(2):
-        own_out[k] = sums[k, pl.ds(pl.multiple_of(me * rows, rows), rows)]
-        for i, out in enumerate(sends_out):
-            at = pl.multiple_of(lax.bitwise_xor(me, i + 1) * rows, rows)
-            out[k] = sums[k, pl.ds(at, rows)].astype(BF16)
-
-
-def over_band_kernel(own, *refs):
-    *came, first_out, second_out = refs
+    for part, part_nodes in zip(came, came_nodes):
+        second = second + mm_tn(part_nodes[...], part[half * rows :])
+    sums[...] = second
+    for i, out in enumerate(sends_out):
+        block = rows_at(kept, (), half + i)
+        for part in came:
+            block = block + part[i * rows : (i + 1) * rows].astype(F32)
+        out[0] = block.astype(BF16)
+        out[1] = rows_at(sums, (), half + i).astype(BF16)
+
+
+def second_kernel(kept, sums, *refs):
+    half = lax.axis_size("band") // 2
+    came, outs = refs[:-half], refs[-half:]
+    rows = outs[0].shape[1]
+    for i, out in enumerate(outs):
+        block = rows_at(kept, (), i)
+        for part in came:
+            block = block + part[i * rows : (i + 1) * rows].astype(F32)
+        out[0] = block.astype(out.dtype)
+        out[1] = rows_at(sums, (), i).astype(out.dtype)
+
+
+def over_band_kernel(*refs):
+    *came, own, first_out, second_out = refs
     for k, out in enumerate((first_out, second_out)):
         total = own[k]
         for part in came:
@@ -380,6 +410,11 @@
 def shifted(x, axis, shift):
     count = lax.axis_size(axis)
     return lax.ppermute(x, axis, [(i, (i + shift) % count) for i in range(count)])
+
+
+def over_band(x, partner):
+    count = lax.axis_size("band")
+    return lax.ppermute(x, "band", [(b, b ^ partner) for b in range(count)])
 
 
 def on_device(
@@ -407,13 +442,16 @@
     mesh_edges = mesh_send.shape[2]
     stack = jnp.concatenate([w_gs, w_gr, w_gn, w_ms, w_mr, w_mn, w_grid], axis=0)
     indices = jnp.concatenate([g2m_send, g2m_recv, mesh_send, mesh_recv], axis=2)
-    rows, recv_hits, recv_rows, from_hits, to_hits, from_rows, to_rows, halo_hits = call(
+    (
+        rows, recv_hits, recv_rows, own_hits, outer_hits, to_hits, from_rows, to_rows, halo_hits
+    ) = call(
         index_kernel,
         [
             ((edges, variables), BF16),
             ((edges, 2 * cycle), BF16),
             ((cycle, edges), BF16),
-            ((mesh_edges, 6 * cycle), BF16),
+            ((mesh_edges, 2 * cycle), BF16),
+            ((mesh_edges, 4 * cycle), BF16),
             ((mesh_edges, 2 * node_count), BF16),
             ((3 * cycle, mesh_edges), BF16),
             ((node_count, mesh_edges), BF16),
@@ -426,10 +464,12 @@
     late_mesh, rows = lax.optimization_barrier((mesh_in, rows))
     mesh_near = lax.ppermute(late_mesh, around, ring_near)
     mesh_far = lax.ppermute(late_mesh, around, ring_far)
-    (table,) = call(
-        table_kernel, [((2 * cycle, latent), BF16)], mesh_near, mesh_far, mesh_in, stack
-    )
-    senders, edge_slope, part, to_far, to_near = call(
+    (recv_pre,) = call(
+        receiver_kernel,
+        [((edges, latent), F32)],
+        mesh_near, mesh_far, mesh_in, recv_hits, stack,
+    )
+    senders, edge_slope, part, to_near, to_far = call(
         encode_kernel,
         [
             ((edges, latent), BF16),
@@ -438,7 +478,7 @@
             ((node_count, latent), BF16),
             ((node_count, latent), BF16),
         ],
-        raw_far, raw_near, halo_hits, recv_hits, recv_rows, rows, table, stack,
+        raw_near, raw_far, halo_hits, recv_rows, rows, recv_pre, stack,
         scratch=[pltpu.VMEM((variables, 2 * width), BF16)],
     )
     from_far = lax.ppermute(to_far, around, ring_far)
@@ -446,13 +486,16 @@
     mesh_one, node_slope = call(
         node_kernel,
         [((cycle, latent), BF16), ((cycle, latent), F32)],
-        part, from_far, from_near, mesh_near, mesh_far, mesh_in, stack,
+        part, from_near, from_far, mesh_near, mesh_far, mesh_in, stack,
     )
     one_near = lax.ppermute(mesh_one, "band", band_near)
     one_far = lax.ppermute(mesh_one, whole, band_far)
     doms = lax.axis_size("dom")
     lats = lax.axis_size("lat")
     dom_nodes = [shifted(mesh_one, "dom", i + 1) for i in range(doms - 1)]
+    (own_pre,) = call(
+        process_own_kernel, [((mesh_edges, latent), F32)], own_hits, to_hits, mesh_one, stack
+    )
     mesh_out, sums, recv_sum, to_near, to_far = call(
         process_kernel,
         [
@@ -462,7 +505,7 @@
             ((cycle, latent), BF16),
             ((cycle, latent), BF16),
         ],
-        from_hits, to_hits, from_rows, to_rows, one_near, mesh_one, one_far, d_out,
+        own_pre, outer_hits, to_hits, from_rows, to_rows, one_near, mesh_one, one_far, d_out,
         stack,
     )
     from_near = lax.ppermute(to_near, "band", band_near)
@@ -474,7 +517,7 @@
         recv_sum, d_out, stack, senders,
     )
     message = (node_count + node_count // 2, latent)
-    part, to_far, to_near = call(
+    part, to_near, to_far = call(
         cotangent_kernel,
         [((cycle, latent), F32), (message, BF16), (message, BF16)],
         sums, from_near, from_far, home,
@@ -491,7 +534,7 @@
             ((2 * cycle, latent), BF16),
             ((doms, cycle, cols), BF16),
         ],
-        recv_hits, part, from_far, from_near, home, node_slope, stack, senders, edge_slope,
+        recv_hits, part, from_near, from_far, home, node_slope, stack, senders, edge_slope,
     )
     edge = (recv_hits, back, edge_slope, senders)
     came = [shifted(sends[i], "lat", i + 1) for i in range(lats - 1)]
@@ -500,24 +543,33 @@
     (own_sends,) = call(other_lats_kernel, [((lats - 1,) + block, BF16)], *edge, sends)
     own_came = [shifted(own_sends[i], "lat", i + 1) for i in range(lats - 1)]
     kept, own_sends = lax.optimization_barrier((kept, own_sends))
-    (sends,) = call(
-        add_kernel, [((doms - 1, latent + cycle, cols), BF16)], kept, total, *came
-    )
-    other_doms = [shifted(sends[i], "dom", i + 1) for i in range(doms - 1)]
+    half = bands // 2
+    first, second = call(
+        add_kernel,
+        [
+            ((doms - 1, half * rows + cycle, cols), BF16),
+            ((doms - 1, half * rows, cols), BF16),
+        ],
+        kept, total, *came,
+    )
+    first = [shifted(first[i], "dom", i + 1) for i in range(doms - 1)]
+    second = [shifted(second[i], "dom", i + 1) for i in range(doms - 1)]
     (kept,) = call(own_block_kernel, [(block, F32)], *edge, *own_came)
-    own, *sends = call(
-        over_dom_kernel,
-        [((2, rows, cols), F32)] + [((2, rows, cols), BF16)] * (bands - 1),
-        kept, total, mesh_one, *other_doms, *dom_nodes,
-        scratch=[pltpu.VMEM((2,) + block, F32)],
-    )
-    count = lax.axis_size("band")
-    came = [
-        lax.ppermute(x, "band", [(b, b ^ (i + 1)) for b in range(count)])
-        for i, x in enumerate(sends)
-    ]
+    pair = (2, rows, cols)
+    *far_sends, sums = call(
+        first_kernel,
+        [(pair, BF16)] * half + [(block, F32)],
+        kept, total, mesh_one, *first, *dom_nodes,
+    )
+    came = [over_band(x, half + i) for i, x in reversed(list(enumerate(far_sends)))]
+    own, *near_sends = call(
+        second_kernel,
+        [(pair, F32)] + [(pair, BF16)] * (half - 1),
+        kept, sums, *second,
+    )
+    came += [over_band(x, i + 1) for i, x in reversed(list(enumerate(near_sends)))]
     tile = ((rows, cols), F32)
-    grad_gs, grad_ms = call(over_band_kernel, [tile, tile], own, *came)
+    grad_gs, grad_ms = call(over_band_kernel, [tile, tile], *came, own)
     return mesh_out, grad_gs, grad_ms
 
 

time: 62.4 us -> 59.2 us (0.949)
  waiting for transfers between devices: 19 us -> 14.7 us
  starting transfers between devices: 21.9 us -> 22.9 us
    ppermute x2, starting transfers between devices: 0.36 us -> 3.21 us  [on_device(): from_far = lax.ppermute(to_far, around, ring_far)]
    ppermute x2, starting transfers between devices: 2.84 us -> 0.14 us  [on_device(): from_near = lax.ppermute(to_near, around, ring_near)]
    ppermute x1, starting transfers between devices: 4.65 us -> 2.05 us  [on_device(): one_near = lax.ppermute(mesh_one, 'band', band_near)]
    ppermute x4 -> x5, waiting for transfers between devices: 4.43 us -> 2.55 us  [shifted(): lax.ppermute(x, axis, [(i, (i + shift) % count) for i in range(count)])]
    ppermute x4 -> x5, starting transfers between devices: 2.46 us -> 4.22 us  [shifted(): lax.ppermute(x, axis, [(i, (i + shift) % count) for i in range(count)])]
    ppermute x1, starting transfers between devices: 1.67 us -> 0.43 us  [on_device(): mesh_far = lax.ppermute(late_mesh, around, ring_far)]
    ppermute x1, starting transfers between devices: 0.01 us -> 1.24 us  [on_device(): mesh_near = lax.ppermute(late_mesh, around, ring_near)]
    ppermute x1, starting transfers between devices: 3.09 us -> 4.15 us  [on_device(): raw_near = lax.ppermute(grid, 'band', band_near)]
  transfers between devices with their start and end apart: 19 -> 20, of which waited for: 8 -> 8; matrix products, arithmetic and copies ran while one was open for 7% -> 7% of each run, Pallas kernels for 10% -> 13%
where the time goes in v11:
time: 59.2 us; the launch traced here: 58.9 us
  starting transfers between devices  22.9 us (39%)
  waiting for transfers between devices  14.7 us (25%)
  Pallas kernels  13.9 us (23%)
  local copies, waits for them, and re-layouts  4.43 us (7%)
  between operations  2.19 us (4%)
  other arithmetic  0.74 us (1%)
    pallas_call x16, Pallas kernels, call(): pl.pallas_call(kernel, out_shape=[jax.ShapeDtypeStruct(shape, dtype) for...  13.9 us
    ppermute x3, waiting for transfers between devices, over_band(): return lax.ppermute(x, 'band', [(b, b ^ partner) for b in range(count)])  4.76 us
    ppermute x3, starting transfers between devices, over_band(): return lax.ppermute(x, 'band', [(b, b ^ partner) for b in range(count)])  4.52 us
    unnamed x20, local copies, waits for them, and re-layouts  4.41 us
    ppermute x5, starting transfers between devices, shifted(): lax.ppermute(x, axis, [(i, (i + shift) % count) for i in range(count)])  4.22 us
    ppermute x1, starting transfers between devices, on_device(): raw_near = lax.ppermute(grid, 'band', band_near)  4.15 us
    ppermute x2, waiting for transfers between devices, on_device(): from_far = lax.ppermute(to_far, around, ring_far)  3.77 us
    ppermute x2, starting transfers between devices, on_device(): from_far = lax.ppermute(to_far, around, ring_far)  3.21 us
  transfers between devices with their start and end apart: 20, of which 8 were waited for; matrix products, arithmetic and copies ran while one was open for 7% of the time, Pallas kernels for 13%

profile of v11, /device:TPU:0, one launch (start us, length us, event | category | flops | bytes accessed | tf_op | source)
XLA Modules:
  0.0 58.9 jit_solution(4962182919478404498)
XLA Ops:
  1.2 4.1 %collective-permute-start = (bf16[3,227,360]{2,1,0:T(8,128)(2,1)}, bf16[3,227,360]{2,1,0:T(8,128)(2,1)S(1)}, u32[]{:S(2)}, u32[]{:S(2)}) collective-permute-start(bf16[3,227,360]{2,1,0:T(8,128)(2,1)} %bitcast.6), channel_id=1, source_target_pairs={{0,4},{4,0},{8,12},{12,8},{1,5},{5,1},{9,13},{13,9},{2,6},{6,2},{1... | collective-permute-start | bytes 1470968 | tf_op jit(solution)/shard_map/ppermute | solution.py:440
  6.6 0.7 %pad_add_fusion.indices = s32[1,1,3072]{2,1,0:T(1,128)S(1)} fusion(s32[1,1,512]{2,1,0:T(1,128)} %param.30, s32[1,1,512]{2,1,0:T(1,128)} %param.29, s32[1,1,1024]{2,1,0:T(1,128)} %param.27, s32[1,1,1024]{2,1,0:T(1,128)} %param.26), kind=kLoop, calls=%fused_computation.7 | loop fusion | flops 9216 | bytes 24576 | tf_op jit(solution)/shard_map/concatenate | solution.py:444
  7.3 1.0 %copy-done = bf16[3,360,227]{1,2,0:T(8,128)(2,1)S(1)} copy-done((bf16[3,360,227]{1,2,0:T(8,128)(2,1)S(1)}, bf16[3,360,227]{1,2,0:T(8,128)(2,1)}, u32[]{:S(2)}) %copy-start) | copy-done | bytes 490344
  8.4 1.9 %shard_map.175 = (bf16[1024,227]{1,0:T(8,128)(2,1)S(1)}, bf16[1024,128]{1,0:T(8,128)(2,1)S(1)}, bf16[64,1024]{1,0:T(8,128)(2,1)S(1)}, bf16[512,128]{1,0:T(8,128)...) custom-call(s32[1,1]{1,0:T(1,128)S(6)} %copy.25.count, ...), custom_call_target="tpu_custom_call" | custom-call | tf_op jit(solution)/shard_map/pallas_call | solution.py:380
  10.7 1.2 %collective-permute-start.2 = (bf16[32,512]{1,0:T(8,128)(2,1)}, bf16[32,512]{1,0:T(8,128)(2,1)S(1)}, u32[]{:S(2)}, u32[]{:S(2)}) collective-permute-start(bf16[32,512]{1,0:T(8,128)(2,1)} %mesh_in.3), channel_id=1, source_target_pairs={{0,1},{1,0},{2,3},{3,2},{4,5},{5,4},{6,7},{7,6},{8,9},{9,8},{10,11... | collective-permute-start | bytes 98312 | tf_op jit(solution)/shard_map/ppermute | solution.py:465
  12.0 1.1 %constant_dynamic-update-slice_fusion.6 = bf16[3299,512]{1,0:T(8,128)(2,1)S(1)} fusion(bf16[512,512]{1,0:T(8,128)(2,1)} %param.18), kind=kLoop, calls=%fused_computation.6 | loop fusion | bytes 1048576
  13.1 1.1 %constant_dynamic-update-slice_fusion.5 = bf16[3299,512]{1,0:T(8,128)(2,1)S(1)} fusion(bf16[3299,512]{1,0:T(8,128)(2,1)S(1)} %constant_dynamic-update-slice_fusion.6, bf16[512,512]{1,0:T(8,128)(2,1)} %param.19), kind=kLoop, calls=%fused_computation.5 | loop fusion | bytes 1048576
  14.1 1.1 %constant_dynamic-update-slice_fusion.4 = bf16[3299,512]{1,0:T(8,128)(2,1)S(1)} fusion(bf16[3299,512]{1,0:T(8,128)(2,1)S(1)} %constant_dynamic-update-slice_fusion.5, bf16[512,512]{1,0:T(8,128)(2,1)} %param.20), kind=kLoop, calls=%fused_computation.4 | loop fusion | bytes 1048576
  16.1 1.3 %collective-permute-done.near = bf16[3,227,360]{2,1,0:T(8,128)(2,1)S(1)} collective-permute-done((bf16[3,227,360]{2,1,0:T(8,128)(2,1)}, bf16[3,227,360]{2,1,0:T(8,128)(2,1)S(1)}, u32[]{:S(2)}, u32[]{:S(2)}) %collective-permute-start) | collective-permute-done | bytes 490352 | tf_op jit(solution)/shard_map/ppermute | solution.py:440
  17.4 4.3 %shard_map.177 = (bf16[1024,512]{1,0:T(8,128)(2,1)S(1)}, bf16[1024,512]{1,0:T(8,128)(2,1)S(1)}, f32[64,512]{1,0:T(8,128)S(1)}, bf16[32,512]{1,0:T(8,128)(2,1)S(1)}, bf16[32,512]{1,0:T(8,128)(2,1)S(1)}) custom-call(bf16[3,227,360]{2,1,0:T(8,128)(2,1)S(1)} %collective-permute-done.near, bf16[3,227,360]{2,1,0:T(8,128)(2,1)S(1)} %collective-permute-done.1.far, ...), custom_call_target="tpu_custom_call" | custom-call | tf_op jit(solution)/shard_map/pallas_call | solution.py:380
  21.7 1.6 %collective-permute-start.5 = (bf16[32,512]{1,0:T(8,128)(2,1)S(1)}, bf16[32,512]{1,0:T(8,128)(2,1)S(1)}, u32[]{:S(2)}, u32[]{:S(2)}) collective-permute-start(bf16[32,512]{1,0:T(8,128)(2,1)S(1)} %get-tuple-element.56), channel_id=1, source_target_pairs={{0,3},{1,2},{2,1},{3,0},{4,7},{5,6},{6,5},{7,4},{8,11},{9,10},{10,... | collective-permute-start | bytes 98312 | tf_op jit(solution)/shard_map/ppermute | solution.py:484
  23.4 1.8 %collective-permute-done.5.far = bf16[32,512]{1,0:T(8,128)(2,1)S(1)} collective-permute-done((bf16[32,512]{1,0:T(8,128)(2,1)S(1)}, bf16[32,512]{1,0:T(8,128)(2,1)S(1)}, u32[]{:S(2)}, u32[]{:S(2)}) %collective-permute-start.5) | collective-permute-done | bytes 32800 | tf_op jit(solution)/shard_map/ppermute | solution.py:484
  25.9 2.1 %collective-permute-start.6 = (bf16[64,512]{1,0:T(8,128)(2,1)S(1)}, bf16[64,512]{1,0:T(8,128)(2,1)S(1)}, u32[]{:S(2)}, u32[]{:S(2)}) collective-permute-start(bf16[64,512]{1,0:T(8,128)(2,1)S(1)} %get-tuple-element.57.own.nodes), channel_id=1, source_target_pairs={{0,4},{4,0},{8,12},{12,8},{1,5},{5,1},{9,13},{13,9},{2,6},{6,2},{1... | collective-permute-start | bytes 196616 | tf_op jit(solution)/shard_map/ppermute | solution.py:491
  28.0 1.5 %collective-permute-start.9 = (bf16[64,512]{1,0:T(8,128)(2,1)S(1)}, bf16[64,512]{1,0:T(8,128)(2,1)S(1)}, u32[]{:S(2)}, u32[]{:S(2)}) collective-permute-start(bf16[64,512]{1,0:T(8,128)(2,1)S(1)} %get-tuple-element.57.own.nodes), channel_id=1, source_target_pairs={{0,2},{2,0},{1,3},{3,1},{4,6},{6,4},{5,7},{7,5},{8,10},{10,8},{9,1... | collective-permute-start | bytes 196616 | tf_op jit(solution)/shard_map/ppermute | solution.py:412
  29.5 0.7 %shard_map.179.own_pre = f32[512,512]{1,0:T(8,128)S(1)} custom-call(bf16[512,128]{1,0:T(8,128)(2,1)S(1)} %get-tuple-element.46.own_hits, bf16[512,64]{1,0:T(8,128)(2,1)S(1)} %get-tuple-element.47.to_hits, bf16[64,512]{1,0:T(8,128)(2,1)S(1)} %get-tuple-element.57.own.nodes, bf16[3299,512]{1,0:T(8,128)(2,1)S(1)} %constant_dynamic-update-slice_fusion.stack), custom_call_target="tpu_custom_call" | custom-call | tf_op jit(solution)/shard_map/pallas_call | solution.py:380
  30.4 1.6 %shard_map.180 = (bf16[32,512]{1,0:T(8,128)(2,1)}, f32[192,512]{1,0:T(8,128)S(1)}, bf16[32,512]{1,0:T(8,128)(2,1)S(1)}, bf16[64,512]{1,0:T(8,128)(2,1)S(1)}, bf16[64,512]{1,0:T(8,128)(2,1)S(1)}) custom-call(f32[512,512]{1,0:T(8,128)S(1)} %shard_map.179.own_pre, bf16[512,256]{1,0:T(8,128)(2,1)S(1)} %get-tuple-element.58.outer_hits, ...), custom_call_target="tpu_custom_call" | custom-call | tf_op jit(solution)/shard_map/pallas_call | solution.py:380
  32.0 1.9 %collective-permute-start.8 = (bf16[64,512]{1,0:T(8,128)(2,1)S(1)}, bf16[64,512]{1,0:T(8,128)(2,1)S(1)}, u32[]{:S(2)}, u32[]{:S(2)}) collective-permute-start(bf16[64,512]{1,0:T(8,128)(2,1)S(1)} %get-tuple-element.63), channel_id=1, source_target_pairs={{0,4},{4,0},{8,12},{12,8},{1,5},{5,1},{9,13},{13,9},{2,6},{6,2},{1... | collective-permute-start | bytes 196616 | tf_op jit(solution)/shard_map/ppermute | solution.py:511
  34.3 2.0 %collective-permute-done.8.near = bf16[64,512]{1,0:T(8,128)(2,1)S(1)} collective-permute-done((bf16[64,512]{1,0:T(8,128)(2,1)S(1)}, bf16[64,512]{1,0:T(8,128)(2,1)S(1)}, u32[]{:S(2)}, u32[]{:S(2)}) %collective-permute-start.8) | collective-permute-done | bytes 65568 | tf_op jit(solution)/shard_map/ppermute | solution.py:511
  36.5 1.6 %collective-permute-start.12 = (bf16[48,512]{1,0:T(8,128)(2,1)S(1)}, bf16[48,512]{1,0:T(8,128)(2,1)S(1)}, u32[]{:S(2)}, u32[]{:S(2)}) collective-permute-start(bf16[48,512]{1,0:T(8,128)(2,1)S(1)} %get-tuple-element.71), channel_id=1, source_target_pairs={{0,3},{1,2},{2,1},{3,0},{4,7},{5,6},{6,5},{7,4},{8,11},{9,10},{10,... | collective-permute-start | bytes 147464 | tf_op jit(solution)/shard_map/ppermute | solution.py:525
  38.1 2.0 %collective-permute-done.12.far = bf16[48,512]{1,0:T(8,128)(2,1)S(1)} collective-permute-done((bf16[48,512]{1,0:T(8,128)(2,1)S(1)}, bf16[48,512]{1,0:T(8,128)(2,1)S(1)}, u32[]{:S(2)}, u32[]{:S(2)}) %collective-permute-start.12) | collective-permute-done | bytes 49184 | tf_op jit(solution)/shard_map/ppermute | solution.py:525
  40.1 1.1 %shard_map.183 = (bf16[1,1,512,128]{3,2,1,0:T(8,128)(2,1)S(1)}, bf16[128,512]{1,0:T(8,128)(2,1)S(1)}, bf16[2,64,128]{2,1,0:T(8,128)(2,1)S(1)}) custom-call(bf16[1024,128]{1,0:T(8,128)(2,1)S(1)} %get-tuple-element.53.recv_hits, f32[64,512]{1,0:T(8,128)S(1)} %get-tuple-element.69.part, bf16[48,512]{1,0:T(8,128)(2,1)S(1)} %collective-permute-done.11.near, ...), custom_call_target="tpu_custom_call" | custom-call | tf_op jit(solution)/shard_map/pallas_call | solution.py:380
  41.7 0.7 %shard_map.184 = bf16[1,512,128]{2,1,0:T(8,128)(2,1)S(1)} custom-call(bf16[1024,128]{1,0:T(8,128)(2,1)S(1)} %get-tuple-element.53.recv_hits, bf16[128,512]{1,0:T(8,128)(2,1)S(1)} %get-tuple-element.75.back, bf16[1024,512]{1,0:T(8,128)(2,1)S(1)} %get-tuple-element.74.edge_slope, bf16[512,1024]{1,0:T(8,128)(2,1)S(1)} %get-tuple-element.73.senders, ...), custom_call_target="tpu_custom_call" | custom-call | tf_op jit(solution)/shard_map/pallas_call | solution.py:380
  42.5 0.7 %shard_map.186.kept = f32[1,512,128]{2,1,0:T(8,128)S(1)} custom-call(bf16[1024,128]{1,0:T(8,128)(2,1)S(1)} %get-tuple-element.53.recv_hits, bf16[128,512]{1,0:T(8,128)(2,1)S(1)} %get-tuple-element.75.back, bf16[1024,512]{1,0:T(8,128)(2,1)S(1)} %get-tuple-element.74.edge_slope, bf16[512,1024]{1,0:T(8,128)(2,1)S(1)} %get-tuple-element.73.senders, ...), custom_call_target="tpu_custom_call" | custom-call | tf_op jit(solution)/shard_map/pallas_call | solution.py:380
  43.3 1.6 %collective-permute-start.15 = (bf16[320,128]{1,0:T(8,128)(2,1)S(1)}, bf16[320,128]{1,0:T(8,128)(2,1)S(1)}, u32[]{:S(2)}, u32[]{:S(2)}) collective-permute-start(bf16[320,128]{1,0:T(8,128)(2,1)S(1)} %bitcast.10), channel_id=1, source_target_pairs={{0,2},{2,0},{1,3},{3,1},{4,6},{6,4},{5,7},{7,5},{8,10},{10,8},{9,1... | collective-permute-start | bytes 245768 | tf_op jit(solution)/shard_map/ppermute | solution.py:412
  45.4 0.7 %shard_map.185.kept = f32[512,128]{1,0:T(8,128)S(1)} custom-call(bf16[1024,128]{1,0:T(8,128)(2,1)S(1)} %get-tuple-element.53.recv_hits, bf16[128,512]{1,0:T(8,128)(2,1)S(1)} %get-tuple-element.75.back, bf16[1024,512]{1,0:T(8,128)(2,1)S(1)} %get-tuple-element.74.edge_slope, bf16[512,1024]{1,0:T(8,128)(2,1)S(1)} %get-tuple-element.73.senders, ...), custom_call_target="tpu_custom_call" | custom-call | tf_op jit(solution)/shard_map/pallas_call | solution.py:380
  46.1 2.5 %collective-permute-done.15.refs_0_ = bf16[320,128]{1,0:T(8,128)(2,1)S(1)} collective-permute-done((bf16[320,128]{1,0:T(8,128)(2,1)S(1)}, bf16[320,128]{1,0:T(8,128)(2,1)S(1)}, u32[]{:S(2)}, u32[]{:S(2)}) %collective-permute-start.15) | collective-permute-done | bytes 81952 | tf_op jit(solution)/shard_map/ppermute | solution.py:412
  48.9 3.0 %collective-permute-start.16 = (bf16[2,128,128]{2,1,0:T(8,128)(2,1)S(1)}, bf16[2,128,128]{2,1,0:T(8,128)(2,1)S(1)}, u32[]{:S(2)}, u32[]{:S(2)}) collective-permute-start(bf16[2,128,128]{2,1,0:T(8,128)(2,1)S(1)} %get-tuple-element.81), channel_id=1, source_target_pairs={{0,12},{4,8},{8,4},{12,0},{1,13},{5,9},{9,5},{13,1},{2,14},{6,10},... | collective-permute-start | bytes 196616 | tf_op jit(solution)/shard_map/ppermute | solution.py:417
  51.9 0.6 %collective-permute-start.17 = (bf16[2,128,128]{2,1,0:T(8,128)(2,1)S(1)}, bf16[2,128,128]{2,1,0:T(8,128)(2,1)S(1)}, u32[]{:S(2)}, u32[]{:S(2)}) collective-permute-start(bf16[2,128,128]{2,1,0:T(8,128)(2,1)S(1)} %get-tuple-element.82), channel_id=1, source_target_pairs={{0,8},{4,12},{8,0},{12,4},{1,9},{5,13},{9,1},{13,5},{2,10},{6,14},... | collective-permute-start | bytes 196616 | tf_op jit(solution)/shard_map/ppermute | solution.py:417
  52.5 0.9 %collective-permute-start.19 = (bf16[2,128,128]{2,1,0:T(8,128)(2,1)S(1)}, bf16[2,128,128]{2,1,0:T(8,128)(2,1)S(1)}, u32[]{:S(2)}, u32[]{:S(2)}) collective-permute-start(bf16[2,128,128]{2,1,0:T(8,128)(2,1)S(1)} %get-tuple-element.85), channel_id=1, source_target_pairs={{0,4},{4,0},{8,12},{12,8},{1,5},{5,1},{9,13},{13,9},{2,6},{6,2},{1... | collective-permute-start | bytes 196616 | tf_op jit(solution)/shard_map/ppermute | solution.py:417
  53.4 1.9 %collective-permute-done.16.refs_0_ = bf16[2,128,128]{2,1,0:T(8,128)(2,1)S(1)} collective-permute-done((bf16[2,128,128]{2,1,0:T(8,128)(2,1)S(1)}, bf16[2,128,128]{2,1,0:T(8,128)(2,1)S(1)}, u32[]{:S(2)}, u32[]{:S(2)}) %collective-permute-start.16) | collective-permute-done | bytes 65568 | tf_op jit(solution)/shard_map/ppermute | solution.py:417
  55.4 2.8 %collective-permute-done.17.refs_1_ = bf16[2,128,128]{2,1,0:T(8,128)(2,1)S(1)} collective-permute-done((bf16[2,128,128]{2,1,0:T(8,128)(2,1)S(1)}, bf16[2,128,128]{2,1,0:T(8,128)(2,1)S(1)}, u32[]{:S(2)}, u32[]{:S(2)}) %collective-permute-start.17) | collective-permute-done | bytes 65568 | tf_op jit(solution)/shard_map/ppermute | solution.py:417
  58.2 0.7 %shard_map.190 = (f32[128,128]{1,0:T(8,128)}, f32[128,128]{1,0:T(8,128)}) custom-call(bf16[2,128,128]{2,1,0:T(8,128)(2,1)S(1)} %collective-permute-done.16.refs_0_, bf16[2,128,128]{2,1,0:T(8,128)(2,1)S(1)} %collective-permute-done.17.refs_1_, bf16[2,128,128]{2,1,0:T(8,128)(2,1)S(1)} %collective-permute-done.19.refs_2_, ...), custom_call_target="tpu_custom_call" | custom-call | tf_op jit(solution)/shard_map/pallas_call | solution.py:380
  (46 shorter events, 4.8 us)
Async XLA Ops:
  0.6 15.4 %collective-permute-start.1 = (bf16[3,227,360]{2,1,0:T(8,128)(2,1)}, bf16[3,227,360]{2,1,0:T(8,128)(2,1)S(1)}, u32[]{:S(2)}, u32[]{:S(2)}) collective-permute-start(bf16[3,227,360]{2,1,0:T(8,128)(2,1)} %bitcast.5), channel_id=1, source_target_pairs={{0,1},{1,0},{2,3},{3,2},{4,8},{5,9},{6,10},{7,11},{8,4},{9,5},{10,... | collective-permute-start | bytes 1470968 | tf_op jit(solution)/shard_map/ppermute | solution.py:441
  1.2 16.3 %collective-permute-start = (bf16[3,227,360]{2,1,0:T(8,128)(2,1)}, bf16[3,227,360]{2,1,0:T(8,128)(2,1)S(1)}, u32[]{:S(2)}, u32[]{:S(2)}) collective-permute-start(bf16[3,227,360]{2,1,0:T(8,128)(2,1)} %bitcast.6), channel_id=1, source_target_pairs={{0,4},{4,0},{8,12},{12,8},{1,5},{5,1},{9,13},{13,9},{2,6},{6,2},{1... | collective-permute-start | bytes 1470968 | tf_op jit(solution)/shard_map/ppermute | solution.py:440
  7.3 1.0 %copy-start = (bf16[3,360,227]{1,2,0:T(8,128)(2,1)S(1)}, bf16[3,360,227]{1,2,0:T(8,128)(2,1)}, u32[]{:S(2)}) copy-start(bf16[3,360,227]{1,2,0:T(8,128)(2,1)} %param.16) | copy-start | bytes 1470964
  8.4 6.8 %copy-start.3 = (bf16[512,512]{1,0:T(8,128)(2,1)S(1)}, bf16[512,512]{1,0:T(8,128)(2,1)}, u32[]{:S(2)}) copy-start(bf16[512,512]{1,0:T(8,128)(2,1)} %param.21) | copy-start | bytes 1572868
  8.4 6.9 %copy-start.4 = (bf16[512,512]{1,0:T(8,128)(2,1)S(1)}, bf16[512,512]{1,0:T(8,128)(2,1)}, u32[]{:S(2)}) copy-start(bf16[512,512]{1,0:T(8,128)(2,1)} %param.22) | copy-start | bytes 1572868
  8.4 6.9 %copy-start.5 = (bf16[512,512]{1,0:T(8,128)(2,1)S(1)}, bf16[512,512]{1,0:T(8,128)(2,1)}, u32[]{:S(2)}) copy-start(bf16[512,512]{1,0:T(8,128)(2,1)} %param.23) | copy-start | bytes 1572868
  8.4 7.0 %copy-start.6 = (bf16[227,512]{1,0:T(8,128)(2,1)S(1)}, bf16[227,512]{1,0:T(8,128)(2,1)}, u32[]{:S(2)}) copy-start(bf16[227,512]{1,0:T(8,128)(2,1)} %param.17) | copy-start | bytes 697348
  10.3 5.1 %copy-start.1 = (bf16[32,512]{1,0:T(8,128)(2,1)S(1)}, bf16[32,512]{1,0:T(8,128)(2,1)}, u32[]{:S(2)}) copy-start(bf16[32,512]{1,0:T(8,128)(2,1)} %mesh_in.3) | copy-start | bytes 98308
  10.3 5.1 %collective-permute-start.3 = (bf16[32,512]{1,0:T(8,128)(2,1)}, bf16[32,512]{1,0:T(8,128)(2,1)S(1)}, u32[]{:S(2)}, u32[]{:S(2)}) collective-permute-start(bf16[32,512]{1,0:T(8,128)(2,1)} %mesh_in.3), channel_id=1, source_target_pairs={{0,3},{1,2},{2,1},{3,0},{4,7},{5,6},{6,5},{7,4},{8,11},{9,10},{10,... | collective-permute-start | bytes 98312 | tf_op jit(solution)/shard_map/ppermute | solution.py:466
  10.7 4.7 %collective-permute-start.2 = (bf16[32,512]{1,0:T(8,128)(2,1)}, bf16[32,512]{1,0:T(8,128)(2,1)S(1)}, u32[]{:S(2)}, u32[]{:S(2)}) collective-permute-start(bf16[32,512]{1,0:T(8,128)(2,1)} %mesh_in.3), channel_id=1, source_target_pairs={{0,1},{1,0},{2,3},{3,2},{4,5},{5,4},{6,7},{7,6},{8,9},{9,8},{10,11... | collective-permute-start | bytes 98312 | tf_op jit(solution)/shard_map/ppermute | solution.py:465
  21.7 1.7 %collective-permute-start.4 = (bf16[32,512]{1,0:T(8,128)(2,1)S(1)}, bf16[32,512]{1,0:T(8,128)(2,1)S(1)}, u32[]{:S(2)}, u32[]{:S(2)}) collective-permute-start(bf16[32,512]{1,0:T(8,128)(2,1)S(1)} %get-tuple-element.55), channel_id=1, source_target_pairs={{0,1},{1,0},{2,3},{3,2},{4,5},{5,4},{6,7},{7,6},{8,9},{9,8},{10,11... | collective-permute-start | bytes 98312 | tf_op jit(solution)/shard_map/ppermute | solution.py:485
  21.7 3.4 %collective-permute-start.5 = (bf16[32,512]{1,0:T(8,128)(2,1)S(1)}, bf16[32,512]{1,0:T(8,128)(2,1)S(1)}, u32[]{:S(2)}, u32[]{:S(2)}) collective-permute-start(bf16[32,512]{1,0:T(8,128)(2,1)S(1)} %get-tuple-element.56), channel_id=1, source_target_pairs={{0,3},{1,2},{2,1},{3,0},{4,7},{5,6},{6,5},{7,4},{8,11},{9,10},{10,... | collective-permute-start | bytes 98312 | tf_op jit(solution)/shard_map/ppermute | solution.py:484
  25.2 5.2 %copy-start.2 = (bf16[32,512]{1,0:T(8,128)(2,1)S(1)}, bf16[32,512]{1,0:T(8,128)(2,1)}, u32[]{:S(2)}) copy-start(bf16[32,512]{1,0:T(8,128)(2,1)} %d_out.3) | copy-start | bytes 98308
  25.4 4.8 %collective-permute-start.7 = (bf16[64,512]{1,0:T(8,128)(2,1)S(1)}, bf16[64,512]{1,0:T(8,128)(2,1)S(1)}, u32[]{:S(2)}, u32[]{:S(2)}) collective-permute-start(bf16[64,512]{1,0:T(8,128)(2,1)S(1)} %get-tuple-element.57.own.nodes), channel_id=1, source_target_pairs={{0,1},{1,0},{2,3},{3,2},{4,8},{5,9},{6,10},{7,11},{8,4},{9,5},{10,... | collective-permute-start | bytes 196616 | tf_op jit(solution)/shard_map/ppermute | solution.py:492
  25.9 4.5 %collective-permute-start.6 = (bf16[64,512]{1,0:T(8,128)(2,1)S(1)}, bf16[64,512]{1,0:T(8,128)(2,1)S(1)}, u32[]{:S(2)}, u32[]{:S(2)}) collective-permute-start(bf16[64,512]{1,0:T(8,128)(2,1)S(1)} %get-tuple-element.57.own.nodes), channel_id=1, source_target_pairs={{0,4},{4,0},{8,12},{12,8},{1,5},{5,1},{9,13},{13,9},{2,6},{6,2},{1... | collective-permute-start | bytes 196616 | tf_op jit(solution)/shard_map/ppermute | solution.py:491
  28.0 6.4 %collective-permute-start.9 = (bf16[64,512]{1,0:T(8,128)(2,1)S(1)}, bf16[64,512]{1,0:T(8,128)(2,1)S(1)}, u32[]{:S(2)}, u32[]{:S(2)}) collective-permute-start(bf16[64,512]{1,0:T(8,128)(2,1)S(1)} %get-tuple-element.57.own.nodes), channel_id=1, source_target_pairs={{0,2},{2,0},{1,3},{3,1},{4,6},{6,4},{5,7},{7,5},{8,10},{10,8},{9,1... | collective-permute-start | bytes 196616 | tf_op jit(solution)/shard_map/ppermute | solution.py:412
  32.0 4.3 %collective-permute-start.8 = (bf16[64,512]{1,0:T(8,128)(2,1)S(1)}, bf16[64,512]{1,0:T(8,128)(2,1)S(1)}, u32[]{:S(2)}, u32[]{:S(2)}) collective-permute-start(bf16[64,512]{1,0:T(8,128)(2,1)S(1)} %get-tuple-element.63), channel_id=1, source_target_pairs={{0,4},{4,0},{8,12},{12,8},{1,5},{5,1},{9,13},{13,9},{2,6},{6,2},{1... | collective-permute-start | bytes 196616 | tf_op jit(solution)/shard_map/ppermute | solution.py:511
  34.0 2.4 %collective-permute-start.10 = (bf16[64,512]{1,0:T(8,128)(2,1)S(1)}, bf16[64,512]{1,0:T(8,128)(2,1)S(1)}, u32[]{:S(2)}, u32[]{:S(2)}) collective-permute-start(bf16[64,512]{1,0:T(8,128)(2,1)S(1)} %get-tuple-element.65), channel_id=1, source_target_pairs={{0,1},{1,0},{2,3},{3,2},{4,8},{5,9},{6,10},{7,11},{8,4},{9,5},{10,... | collective-permute-start | bytes 196616 | tf_op jit(solution)/shard_map/ppermute | solution.py:512
  36.4 1.7 %collective-permute-start.11 = (bf16[48,512]{1,0:T(8,128)(2,1)S(1)}, bf16[48,512]{1,0:T(8,128)(2,1)S(1)}, u32[]{:S(2)}, u32[]{:S(2)}) collective-permute-start(bf16[48,512]{1,0:T(8,128)(2,1)S(1)} %get-tuple-element.70), channel_id=1, source_target_pairs={{0,1},{1,0},{2,3},{3,2},{4,5},{5,4},{6,7},{7,6},{8,9},{9,8},{10,11... | collective-permute-start | bytes 147464 | tf_op jit(solution)/shard_map/ppermute | solution.py:526
  36.5 3.6 %collective-permute-start.12 = (bf16[48,512]{1,0:T(8,128)(2,1)S(1)}, bf16[48,512]{1,0:T(8,128)(2,1)S(1)}, u32[]{:S(2)}, u32[]{:S(2)}) collective-permute-start(bf16[48,512]{1,0:T(8,128)(2,1)S(1)} %get-tuple-element.71), channel_id=1, source_target_pairs={{0,3},{1,2},{2,1},{3,0},{4,7},{5,6},{6,5},{7,4},{8,11},{9,10},{10,... | collective-permute-start | bytes 147464 | tf_op jit(solution)/shard_map/ppermute | solution.py:525
  41.2 2.0 %collective-permute-start.14 = (bf16[1,512,128]{2,1,0:T(8,128)(2,1)S(1)}, bf16[1,512,128]{2,1,0:T(8,128)(2,1)S(1)}, u32[]{:S(2)}, u32[]{:S(2)}) collective-permute-start(bf16[1,512,128]{2,1,0:T(8,128)(2,1)S(1)} %bitcast.8), channel_id=1, source_target_pairs={{0,1},{1,0},{2,3},{3,2},{4,5},{5,4},{6,7},{7,6},{8,9},{9,8},{10,11... | collective-permute-start | bytes 393224 | tf_op jit(solution)/shard_map/ppermute | solution.py:412
  42.4 3.0 %collective-permute-start.13 = (bf16[512,128]{1,0:T(8,128)(2,1)S(1)}, bf16[512,128]{1,0:T(8,128)(2,1)S(1)}, u32[]{:S(2)}, u32[]{:S(2)}) collective-permute-start(bf16[512,128]{1,0:T(8,128)(2,1)S(1)} %bitcast.9), channel_id=1, source_target_pairs={{0,1},{1,0},{2,3},{3,2},{4,5},{5,4},{6,7},{7,6},{8,9},{9,8},{10,11... | collective-permute-start | bytes 393224 | tf_op jit(solution)/shard_map/ppermute | solution.py:412
  43.3 5.3 %collective-permute-start.15 = (bf16[320,128]{1,0:T(8,128)(2,1)S(1)}, bf16[320,128]{1,0:T(8,128)(2,1)S(1)}, u32[]{:S(2)}, u32[]{:S(2)}) collective-permute-start(bf16[320,128]{1,0:T(8,128)(2,1)S(1)} %bitcast.10), channel_id=1, source_target_pairs={{0,2},{2,0},{1,3},{3,1},{4,6},{6,4},{5,7},{7,5},{8,10},{10,8},{9,1... | collective-permute-start | bytes 245768 | tf_op jit(solution)/shard_map/ppermute | solution.py:412
  44.8 7.7 %collective-permute-start.18 = (bf16[256,128]{1,0:T(8,128)(2,1)S(1)}, bf16[256,128]{1,0:T(8,128)(2,1)S(1)}, u32[]{:S(2)}, u32[]{:S(2)}) collective-permute-start(bf16[256,128]{1,0:T(8,128)(2,1)S(1)} %bitcast.11), channel_id=1, source_target_pairs={{0,2},{2,0},{1,3},{3,1},{4,6},{6,4},{5,7},{7,5},{8,10},{10,8},{9,1... | collective-permute-start | bytes 196616 | tf_op jit(solution)/shard_map/ppermute | solution.py:412
  48.9 6.5 %collective-permute-start.16 = (bf16[2,128,128]{2,1,0:T(8,128)(2,1)S(1)}, bf16[2,128,128]{2,1,0:T(8,128)(2,1)S(1)}, u32[]{:S(2)}, u32[]{:S(2)}) collective-permute-start(bf16[2,128,128]{2,1,0:T(8,128)(2,1)S(1)} %get-tuple-element.81), channel_id=1, source_target_pairs={{0,12},{4,8},{8,4},{12,0},{1,13},{5,9},{9,5},{13,1},{2,14},{6,10},... | collective-permute-start | bytes 196616 | tf_op jit(solution)/shard_map/ppermute | solution.py:417
  51.9 6.3 %collective-permute-start.17 = (bf16[2,128,128]{2,1,0:T(8,128)(2,1)S(1)}, bf16[2,128,128]{2,1,0:T(8,128)(2,1)S(1)}, u32[]{:S(2)}, u32[]{:S(2)}) collective-permute-start(bf16[2,128,128]{2,1,0:T(8,128)(2,1)S(1)} %get-tuple-element.82), channel_id=1, source_target_pairs={{0,8},{4,12},{8,0},{12,4},{1,9},{5,13},{9,1},{13,5},{2,10},{6,14},... | collective-permute-start | bytes 196616 | tf_op jit(solution)/shard_map/ppermute | solution.py:417
  52.5 5.7 %collective-permute-start.19 = (bf16[2,128,128]{2,1,0:T(8,128)(2,1)S(1)}, bf16[2,128,128]{2,1,0:T(8,128)(2,1)S(1)}, u32[]{:S(2)}, u32[]{:S(2)}) collective-permute-start(bf16[2,128,128]{2,1,0:T(8,128)(2,1)S(1)} %get-tuple-element.85), channel_id=1, source_target_pairs={{0,4},{4,0},{8,12},{12,8},{1,5},{5,1},{9,13},{13,9},{2,6},{6,2},{1... | collective-permute-start | bytes 196616 | tf_op jit(solution)/shard_map/ppermute | solution.py:417

commit v12 on v11

--- a/solution.py
+++ b/solution.py
@@ -96,7 +96,7 @@
 
 def index_kernel(
     count, mesh_count, indices, grid,
-    own_out, recv_hits, recv_rows, own_hits, outer_hits, to_hits, from_rows, to_rows, halo_hits, wide,
+    own_out, recv_hits, recv_rows, own_hits, outer_hits, to_hits, from_rows, to_rows, near_hits, far_hits, wide,
 ):
     edges = recv_hits.shape[0]
     mesh_edges = to_hits.shape[0]
@@ -124,8 +124,8 @@
         index = columns(spread(send[:, part_of], 3 * band_rows, cols, pitch))
         own_hit = hits_from(index, width, width, width)
         own_out[part_of] = mm_nt(own_hit, wide[...]).astype(BF16)
-        halo_hits[part_of, :width] = hits_from(index, width, width, near_base)
-        halo_hits[part_of, width:] = hits_from(index, width, width, far_base)
+        near_hits[part_of] = hits_from(index, width, width, near_base)
+        far_hits[part_of] = hits_from(index, width, width, far_base)
         target = live_only(recv[:, part_of], count[0, 0], first)
         recv_hits[part_of] = hits_from(columns(target), 2 * cycle, cycle)
         recv_rows[:, part_of] = hits_to(target, cycle)
@@ -154,16 +154,18 @@
     pre_out[...] = mm(recv_hits[...], table)
 
 
+def gather_kernel(halo, hits, rows, rows_out, wide):
+    fill(wide, halo, wide.shape[1] // halo.shape[0], 0)
+    rows_out[...] = rows[...] + mm_nt(hits[...], wide[...]).astype(BF16)
+
+
 def encode_kernel(
-    near, far, halo_hits, recv_rows, own, recv_pre, stack,
+    near, near_hits, recv_rows, rows, recv_pre, stack,
     senders_out, slope_out, part_out, near_out, far_out, wide,
 ):
     half = recv_rows.shape[0] // 2
-    width = wide.shape[1] // 2
-    pitch = width // near.shape[0]
-    fill(wide, near, pitch, 0)
-    fill(wide, far, pitch, width)
-    raw = own[...] + mm_nt(halo_hits[...], wide[...]).astype(BF16)
+    fill(wide, near, wide.shape[1] // near.shape[0], 0)
+    raw = rows[...] + mm_nt(near_hits[...], wide[...]).astype(BF16)
     latent, _ = silu_parts(mm(raw, stack[stack.shape[0] - raw.shape[1] :]))
     latent = latent.astype(BF16)
     senders_out[...] = latent
@@ -443,7 +445,7 @@
     stack = jnp.concatenate([w_gs, w_gr, w_gn, w_ms, w_mr, w_mn, w_grid], axis=0)
     indices = jnp.concatenate([g2m_send, g2m_recv, mesh_send, mesh_recv], axis=2)
     (
-        rows, recv_hits, recv_rows, own_hits, outer_hits, to_hits, from_rows, to_rows, halo_hits
+        rows, recv_hits, recv_rows, own_hits, outer_hits, to_hits, from_rows, to_rows, *halo_hits
     ) = call(
         index_kernel,
         [
@@ -455,7 +457,8 @@
             ((mesh_edges, 2 * node_count), BF16),
             ((3 * cycle, mesh_edges), BF16),
             ((node_count, mesh_edges), BF16),
-            ((edges, 2 * width), BF16),
+            ((edges, width), BF16),
+            ((edges, width), BF16),
         ],
         g2m_count, mesh_count, indices, grid,
         scalars=(0, 1),
@@ -468,6 +471,13 @@
         receiver_kernel,
         [((edges, latent), F32)],
         mesh_near, mesh_far, mesh_in, recv_hits, stack,
+    )
+    near_hits, far_hits = halo_hits
+    (rows,) = call(
+        gather_kernel,
+        [((edges, variables), BF16)],
+        raw_far, far_hits, rows,
+        scratch=[pltpu.VMEM((variables, width), BF16)],
     )
     senders, edge_slope, part, to_near, to_far = call(
         encode_kernel,
@@ -478,8 +488,8 @@
             ((node_count, latent), BF16),
             ((node_count, latent), BF16),
         ],
-        raw_near, raw_far, halo_hits, recv_rows, rows, recv_pre, stack,
-        scratch=[pltpu.VMEM((variables, 2 * width), BF16)],
+        raw_near, near_hits, recv_rows, rows, recv_pre, stack,
+        scratch=[pltpu.VMEM((variables, width), BF16)],
     )
     from_far = lax.ppermute(to_far, around, ring_far)
     from_near = lax.ppermute(to_near, around, ring_near)

time: 59.2 us -> 58.6 us (0.990)
  waiting for transfers between devices: 14.7 us -> 13.6 us
    ppermute x1, waiting for transfers between devices: 1.33 us -> 0.39 us  [on_device(): raw_near = lax.ppermute(grid, 'band', band_near)]
    pallas_call x16 -> x17, Pallas kernels: 13.9 us -> 13.9 us  [call(): pl.pallas_call(kernel, out_shape=[jax.ShapeDtypeStruct(shape, dtype) for...]
  transfers between devices with their start and end apart: 20 -> 20, of which waited for: 8 -> 8; matrix products, arithmetic and copies ran while one was open for 7% -> 7% of each run, Pallas kernels for 13% -> 15%
where the time goes in v12:
time: 58.6 us; the launch traced here: 58.2 us
  starting transfers between devices  23.3 us (40%)
  Pallas kernels  13.9 us (24%)
  waiting for transfers between devices  13.6 us (23%)
  local copies, waits for them, and re-layouts  4.43 us (8%)
  between operations  2.19 us (4%)
  other arithmetic  0.74 us (1%)
    pallas_call x17, Pallas kernels, call(): pl.pallas_call(kernel, out_shape=[jax.ShapeDtypeStruct(shape, dtype) for...  13.9 us
    ppermute x3, waiting for transfers between devices, over_band(): return lax.ppermute(x, 'band', [(b, b ^ partner) for b in range(count)])  4.65 us
    ppermute x3, starting transfers between devices, over_band(): return lax.ppermute(x, 'band', [(b, b ^ partner) for b in range(count)])  4.52 us
    unnamed x20, local copies, waits for them, and re-layouts  4.41 us
    ppermute x5, starting transfers between devices, shifted(): lax.ppermute(x, axis, [(i, (i + shift) % count) for i in range(count)])  4.22 us
    ppermute x1, starting transfers between devices, on_device(): raw_near = lax.ppermute(grid, 'band', band_near)  4.15 us
    ppermute x2, waiting for transfers between devices, on_device(): from_far = lax.ppermute(to_far, around, ring_far)  3.77 us
    ppermute x2, starting transfers between devices, on_device(): from_far = lax.ppermute(to_far, around, ring_far)  3.21 us
  transfers between devices with their start and end apart: 20, of which 8 were waited for; matrix products, arithmetic and copies ran while one was open for 7% of the time, Pallas kernels for 15%

profile of v12, /device:TPU:0, one launch (start us, length us, event | category | flops | bytes accessed | tf_op | source)
XLA Modules:
  0.0 58.2 jit_solution(4512972003753464625)
XLA Ops:
  1.2 4.1 %collective-permute-start = (bf16[3,227,360]{2,1,0:T(8,128)(2,1)}, bf16[3,227,360]{2,1,0:T(8,128)(2,1)S(1)}, u32[]{:S(2)}, u32[]{:S(2)}) collective-permute-start(bf16[3,227,360]{2,1,0:T(8,128)(2,1)} %bitcast.6), channel_id=1, source_target_pairs={{0,4},{4,0},{8,12},{12,8},{1,5},{5,1},{9,13},{13,9},{2,6},{6,2},{1... | collective-permute-start | bytes 1470968 | tf_op jit(solution)/shard_map/ppermute | solution.py:442
  6.6 0.7 %pad_add_fusion.indices = s32[1,1,3072]{2,1,0:T(1,128)S(1)} fusion(s32[1,1,512]{2,1,0:T(1,128)} %param.30, s32[1,1,512]{2,1,0:T(1,128)} %param.29, s32[1,1,1024]{2,1,0:T(1,128)} %param.27, s32[1,1,1024]{2,1,0:T(1,128)} %param.26), kind=kLoop, calls=%fused_computation.7 | loop fusion | flops 9216 | bytes 24576 | tf_op jit(solution)/shard_map/concatenate | solution.py:446
  7.3 1.0 %copy-done = bf16[3,360,227]{1,2,0:T(8,128)(2,1)S(1)} copy-done((bf16[3,360,227]{1,2,0:T(8,128)(2,1)S(1)}, bf16[3,360,227]{1,2,0:T(8,128)(2,1)}, u32[]{:S(2)}) %copy-start) | copy-done | bytes 490344
  8.4 1.9 %shard_map.175 = (bf16[1024,227]{1,0:T(8,128)(2,1)S(1)}, bf16[1024,128]{1,0:T(8,128)(2,1)S(1)}, bf16[64,1024]{1,0:T(8,128)(2,1)S(1)}, bf16[512,128]{1,0:T(8,128)...) custom-call(s32[1,1]{1,0:T(1,128)S(6)} %copy.25.count, ...), custom_call_target="tpu_custom_call" | custom-call | tf_op jit(solution)/shard_map/pallas_call | solution.py:382
  10.7 1.2 %collective-permute-start.2 = (bf16[32,512]{1,0:T(8,128)(2,1)}, bf16[32,512]{1,0:T(8,128)(2,1)S(1)}, u32[]{:S(2)}, u32[]{:S(2)}) collective-permute-start(bf16[32,512]{1,0:T(8,128)(2,1)} %mesh_in.3), channel_id=1, source_target_pairs={{0,1},{1,0},{2,3},{3,2},{4,5},{5,4},{6,7},{7,6},{8,9},{9,8},{10,11... | collective-permute-start | bytes 98312 | tf_op jit(solution)/shard_map/ppermute | solution.py:468
  12.0 1.1 %constant_dynamic-update-slice_fusion.6 = bf16[3299,512]{1,0:T(8,128)(2,1)S(1)} fusion(bf16[512,512]{1,0:T(8,128)(2,1)} %param.18), kind=kLoop, calls=%fused_computation.6 | loop fusion | bytes 1048576
  13.1 1.1 %constant_dynamic-update-slice_fusion.5 = bf16[3299,512]{1,0:T(8,128)(2,1)S(1)} fusion(bf16[3299,512]{1,0:T(8,128)(2,1)S(1)} %constant_dynamic-update-slice_fusion.6, bf16[512,512]{1,0:T(8,128)(2,1)} %param.19), kind=kLoop, calls=%fused_computation.5 | loop fusion | bytes 1048576
  14.1 1.1 %constant_dynamic-update-slice_fusion.4 = bf16[3299,512]{1,0:T(8,128)(2,1)S(1)} fusion(bf16[3299,512]{1,0:T(8,128)(2,1)S(1)} %constant_dynamic-update-slice_fusion.5, bf16[512,512]{1,0:T(8,128)(2,1)} %param.20), kind=kLoop, calls=%fused_computation.4 | loop fusion | bytes 1048576
  16.1 0.9 %shard_map.176.rows = bf16[1024,227]{1,0:T(8,128)(2,1)S(1)} custom-call(bf16[3,227,360]{2,1,0:T(8,128)(2,1)S(1)} %collective-permute-done.1.halo, bf16[1024,1152]{1,0:T(8,128)(2,1)S(1)} %get-tuple-element.51.hits, bf16[1024,227]{1,0:T(8,128)(2,1)S(1)} %get-tuple-element.53.rows), custom_call_target="tpu_custom_call" | custom-call | tf_op jit(solution)/shard_map/pallas_call | solution.py:382
  17.4 3.3 %shard_map.178 = (bf16[1024,512]{1,0:T(8,128)(2,1)S(1)}, bf16[1024,512]{1,0:T(8,128)(2,1)S(1)}, f32[64,512]{1,0:T(8,128)S(1)}, bf16[32,512]{1,0:T(8,128)(2,1)S(1)}, bf16[32,512]{1,0:T(8,128)(2,1)S(1)}) custom-call(bf16[3,227,360]{2,1,0:T(8,128)(2,1)S(1)} %collective-permute-done.near, bf16[1024,1152]{1,0:T(8,128)(2,1)S(1)} %get-tuple-element.49.near_hits, ...), custom_call_target="tpu_custom_call" | custom-call | tf_op jit(solution)/shard_map/pallas_call | solution.py:382
  20.8 1.6 %collective-permute-start.5 = (bf16[32,512]{1,0:T(8,128)(2,1)S(1)}, bf16[32,512]{1,0:T(8,128)(2,1)S(1)}, u32[]{:S(2)}, u32[]{:S(2)}) collective-permute-start(bf16[32,512]{1,0:T(8,128)(2,1)S(1)} %get-tuple-element.58), channel_id=1, source_target_pairs={{0,3},{1,2},{2,1},{3,0},{4,7},{5,6},{6,5},{7,4},{8,11},{9,10},{10,... | collective-permute-start | bytes 98312 | tf_op jit(solution)/shard_map/ppermute | solution.py:494
  22.4 1.8 %collective-permute-done.5.far = bf16[32,512]{1,0:T(8,128)(2,1)S(1)} collective-permute-done((bf16[32,512]{1,0:T(8,128)(2,1)S(1)}, bf16[32,512]{1,0:T(8,128)(2,1)S(1)}, u32[]{:S(2)}, u32[]{:S(2)}) %collective-permute-start.5) | collective-permute-done | bytes 32800 | tf_op jit(solution)/shard_map/ppermute | solution.py:494
  24.9 2.5 %collective-permute-start.6 = (bf16[64,512]{1,0:T(8,128)(2,1)S(1)}, bf16[64,512]{1,0:T(8,128)(2,1)S(1)}, u32[]{:S(2)}, u32[]{:S(2)}) collective-permute-start(bf16[64,512]{1,0:T(8,128)(2,1)S(1)} %get-tuple-element.59.own.nodes), channel_id=1, source_target_pairs={{0,4},{4,0},{8,12},{12,8},{1,5},{5,1},{9,13},{13,9},{2,6},{6,2},{1... | collective-permute-start | bytes 196616 | tf_op jit(solution)/shard_map/ppermute | solution.py:501
  27.4 1.5 %collective-permute-start.9 = (bf16[64,512]{1,0:T(8,128)(2,1)S(1)}, bf16[64,512]{1,0:T(8,128)(2,1)S(1)}, u32[]{:S(2)}, u32[]{:S(2)}) collective-permute-start(bf16[64,512]{1,0:T(8,128)(2,1)S(1)} %get-tuple-element.59.own.nodes), channel_id=1, source_target_pairs={{0,2},{2,0},{1,3},{3,1},{4,6},{6,4},{5,7},{7,5},{8,10},{10,8},{9,1... | collective-permute-start | bytes 196616 | tf_op jit(solution)/shard_map/ppermute | solution.py:414
  28.9 0.7 %shard_map.180.own_pre = f32[512,512]{1,0:T(8,128)S(1)} custom-call(bf16[512,128]{1,0:T(8,128)(2,1)S(1)} %get-tuple-element.47.own_hits, bf16[512,64]{1,0:T(8,128)(2,1)S(1)} %get-tuple-element.48.to_hits, bf16[64,512]{1,0:T(8,128)(2,1)S(1)} %get-tuple-element.59.own.nodes, bf16[3299,512]{1,0:T(8,128)(2,1)S(1)} %constant_dynamic-update-slice_fusion.stack), custom_call_target="tpu_custom_call" | custom-call | tf_op jit(solution)/shard_map/pallas_call | solution.py:382
  29.9 1.7 %shard_map.181 = (bf16[32,512]{1,0:T(8,128)(2,1)}, f32[192,512]{1,0:T(8,128)S(1)}, bf16[32,512]{1,0:T(8,128)(2,1)S(1)}, bf16[64,512]{1,0:T(8,128)(2,1)S(1)}, bf16[64,512]{1,0:T(8,128)(2,1)S(1)}) custom-call(f32[512,512]{1,0:T(8,128)S(1)} %shard_map.180.own_pre, bf16[512,256]{1,0:T(8,128)(2,1)S(1)} %get-tuple-element.60.outer_hits, ...), custom_call_target="tpu_custom_call" | custom-call | tf_op jit(solution)/shard_map/pallas_call | solution.py:382
  31.5 1.9 %collective-permute-start.8 = (bf16[64,512]{1,0:T(8,128)(2,1)S(1)}, bf16[64,512]{1,0:T(8,128)(2,1)S(1)}, u32[]{:S(2)}, u32[]{:S(2)}) collective-permute-start(bf16[64,512]{1,0:T(8,128)(2,1)S(1)} %get-tuple-element.65), channel_id=1, source_target_pairs={{0,4},{4,0},{8,12},{12,8},{1,5},{5,1},{9,13},{13,9},{2,6},{6,2},{1... | collective-permute-start | bytes 196616 | tf_op jit(solution)/shard_map/ppermute | solution.py:521
  33.8 2.1 %collective-permute-done.8.near = bf16[64,512]{1,0:T(8,128)(2,1)S(1)} collective-permute-done((bf16[64,512]{1,0:T(8,128)(2,1)S(1)}, bf16[64,512]{1,0:T(8,128)(2,1)S(1)}, u32[]{:S(2)}, u32[]{:S(2)}) %collective-permute-start.8) | collective-permute-done | bytes 65568 | tf_op jit(solution)/shard_map/ppermute | solution.py:521
  36.0 1.6 %collective-permute-start.12 = (bf16[48,512]{1,0:T(8,128)(2,1)S(1)}, bf16[48,512]{1,0:T(8,128)(2,1)S(1)}, u32[]{:S(2)}, u32[]{:S(2)}) collective-permute-start(bf16[48,512]{1,0:T(8,128)(2,1)S(1)} %get-tuple-element.73), channel_id=1, source_target_pairs={{0,3},{1,2},{2,1},{3,0},{4,7},{5,6},{6,5},{7,4},{8,11},{9,10},{10,... | collective-permute-start | bytes 147464 | tf_op jit(solution)/shard_map/ppermute | solution.py:535
  37.6 2.0 %collective-permute-done.12.far = bf16[48,512]{1,0:T(8,128)(2,1)S(1)} collective-permute-done((bf16[48,512]{1,0:T(8,128)(2,1)S(1)}, bf16[48,512]{1,0:T(8,128)(2,1)S(1)}, u32[]{:S(2)}, u32[]{:S(2)}) %collective-permute-start.12) | collective-permute-done | bytes 49184 | tf_op jit(solution)/shard_map/ppermute | solution.py:535
  39.5 1.2 %shard_map.184 = (bf16[1,1,512,128]{3,2,1,0:T(8,128)(2,1)S(1)}, bf16[128,512]{1,0:T(8,128)(2,1)S(1)}, bf16[2,64,128]{2,1,0:T(8,128)(2,1)S(1)}) custom-call(bf16[1024,128]{1,0:T(8,128)(2,1)S(1)} %get-tuple-element.55.recv_hits, f32[64,512]{1,0:T(8,128)S(1)} %get-tuple-element.71.part, bf16[48,512]{1,0:T(8,128)(2,1)S(1)} %collective-permute-done.11.near, ...), custom_call_target="tpu_custom_call" | custom-call | tf_op jit(solution)/shard_map/pallas_call | solution.py:382
  41.2 0.7 %shard_map.185 = bf16[1,512,128]{2,1,0:T(8,128)(2,1)S(1)} custom-call(bf16[1024,128]{1,0:T(8,128)(2,1)S(1)} %get-tuple-element.55.recv_hits, bf16[128,512]{1,0:T(8,128)(2,1)S(1)} %get-tuple-element.77.back, bf16[1024,512]{1,0:T(8,128)(2,1)S(1)} %get-tuple-element.76.edge_slope, bf16[512,1024]{1,0:T(8,128)(2,1)S(1)} %get-tuple-element.75.senders, ...), custom_call_target="tpu_custom_call" | custom-call | tf_op jit(solution)/shard_map/pallas_call | solution.py:382
  42.0 0.7 %shard_map.187.kept = f32[1,512,128]{2,1,0:T(8,128)S(1)} custom-call(bf16[1024,128]{1,0:T(8,128)(2,1)S(1)} %get-tuple-element.55.recv_hits, bf16[128,512]{1,0:T(8,128)(2,1)S(1)} %get-tuple-element.77.back, bf16[1024,512]{1,0:T(8,128)(2,1)S(1)} %get-tuple-element.76.edge_slope, bf16[512,1024]{1,0:T(8,128)(2,1)S(1)} %get-tuple-element.75.senders, ...), custom_call_target="tpu_custom_call" | custom-call | tf_op jit(solution)/shard_map/pallas_call | solution.py:382
  42.8 1.6 %collective-permute-start.15 = (bf16[320,128]{1,0:T(8,128)(2,1)S(1)}, bf16[320,128]{1,0:T(8,128)(2,1)S(1)}, u32[]{:S(2)}, u32[]{:S(2)}) collective-permute-start(bf16[320,128]{1,0:T(8,128)(2,1)S(1)} %bitcast.10), channel_id=1, source_target_pairs={{0,2},{2,0},{1,3},{3,1},{4,6},{6,4},{5,7},{7,5},{8,10},{10,8},{9,1... | collective-permute-start | bytes 245768 | tf_op jit(solution)/shard_map/ppermute | solution.py:414
  44.9 0.7 %shard_map.186.kept = f32[512,128]{1,0:T(8,128)S(1)} custom-call(bf16[1024,128]{1,0:T(8,128)(2,1)S(1)} %get-tuple-element.55.recv_hits, bf16[128,512]{1,0:T(8,128)(2,1)S(1)} %get-tuple-element.77.back, bf16[1024,512]{1,0:T(8,128)(2,1)S(1)} %get-tuple-element.76.edge_slope, bf16[512,1024]{1,0:T(8,128)(2,1)S(1)} %get-tuple-element.75.senders, ...), custom_call_target="tpu_custom_call" | custom-call | tf_op jit(solution)/shard_map/pallas_call | solution.py:382
  45.6 2.5 %collective-permute-done.15.refs_0_ = bf16[320,128]{1,0:T(8,128)(2,1)S(1)} collective-permute-done((bf16[320,128]{1,0:T(8,128)(2,1)S(1)}, bf16[320,128]{1,0:T(8,128)(2,1)S(1)}, u32[]{:S(2)}, u32[]{:S(2)}) %collective-permute-start.15) | collective-permute-done | bytes 81952 | tf_op jit(solution)/shard_map/ppermute | solution.py:414
  48.4 2.5 %collective-permute-start.16 = (bf16[2,128,128]{2,1,0:T(8,128)(2,1)S(1)}, bf16[2,128,128]{2,1,0:T(8,128)(2,1)S(1)}, u32[]{:S(2)}, u32[]{:S(2)}) collective-permute-start(bf16[2,128,128]{2,1,0:T(8,128)(2,1)S(1)} %get-tuple-element.83), channel_id=1, source_target_pairs={{0,12},{4,8},{8,4},{12,0},{1,13},{5,9},{9,5},{13,1},{2,14},{6,10},... | collective-permute-start | bytes 196616 | tf_op jit(solution)/shard_map/ppermute | solution.py:419
  50.9 1.0 %collective-permute-start.17 = (bf16[2,128,128]{2,1,0:T(8,128)(2,1)S(1)}, bf16[2,128,128]{2,1,0:T(8,128)(2,1)S(1)}, u32[]{:S(2)}, u32[]{:S(2)}) collective-permute-start(bf16[2,128,128]{2,1,0:T(8,128)(2,1)S(1)} %get-tuple-element.84), channel_id=1, source_target_pairs={{0,8},{4,12},{8,0},{12,4},{1,9},{5,13},{9,1},{13,5},{2,10},{6,14},... | collective-permute-start | bytes 196616 | tf_op jit(solution)/shard_map/ppermute | solution.py:419
  52.0 1.0 %collective-permute-start.19 = (bf16[2,128,128]{2,1,0:T(8,128)(2,1)S(1)}, bf16[2,128,128]{2,1,0:T(8,128)(2,1)S(1)}, u32[]{:S(2)}, u32[]{:S(2)}) collective-permute-start(bf16[2,128,128]{2,1,0:T(8,128)(2,1)S(1)} %get-tuple-element.87), channel_id=1, source_target_pairs={{0,4},{4,0},{8,12},{12,8},{1,5},{5,1},{9,13},{13,9},{2,6},{6,2},{1... | collective-permute-start | bytes 196616 | tf_op jit(solution)/shard_map/ppermute | solution.py:419
  52.9 2.3 %collective-permute-done.16.refs_0_ = bf16[2,128,128]{2,1,0:T(8,128)(2,1)S(1)} collective-permute-done((bf16[2,128,128]{2,1,0:T(8,128)(2,1)S(1)}, bf16[2,128,128]{2,1,0:T(8,128)(2,1)S(1)}, u32[]{:S(2)}, u32[]{:S(2)}) %collective-permute-start.16) | collective-permute-done | bytes 65568 | tf_op jit(solution)/shard_map/ppermute | solution.py:419
  55.2 2.4 %collective-permute-done.17.refs_1_ = bf16[2,128,128]{2,1,0:T(8,128)(2,1)S(1)} collective-permute-done((bf16[2,128,128]{2,1,0:T(8,128)(2,1)S(1)}, bf16[2,128,128]{2,1,0:T(8,128)(2,1)S(1)}, u32[]{:S(2)}, u32[]{:S(2)}) %collective-permute-start.17) | collective-permute-done | bytes 65568 | tf_op jit(solution)/shard_map/ppermute | solution.py:419
  57.6 0.7 %shard_map.191 = (f32[128,128]{1,0:T(8,128)}, f32[128,128]{1,0:T(8,128)}) custom-call(bf16[2,128,128]{2,1,0:T(8,128)(2,1)S(1)} %collective-permute-done.16.refs_0_, bf16[2,128,128]{2,1,0:T(8,128)(2,1)S(1)} %collective-permute-done.17.refs_1_, bf16[2,128,128]{2,1,0:T(8,128)(2,1)S(1)} %collective-permute-done.19.refs_2_, ...), custom_call_target="tpu_custom_call" | custom-call | tf_op jit(solution)/shard_map/pallas_call | solution.py:382
  (47 shorter events, 5.2 us)
Async XLA Ops:
  0.6 15.4 %collective-permute-start.1 = (bf16[3,227,360]{2,1,0:T(8,128)(2,1)}, bf16[3,227,360]{2,1,0:T(8,128)(2,1)S(1)}, u32[]{:S(2)}, u32[]{:S(2)}) collective-permute-start(bf16[3,227,360]{2,1,0:T(8,128)(2,1)} %bitcast.5), channel_id=1, source_target_pairs={{0,1},{1,0},{2,3},{3,2},{4,8},{5,9},{6,10},{7,11},{8,4},{9,5},{10,... | collective-permute-start | bytes 1470968 | tf_op jit(solution)/shard_map/ppermute | solution.py:443
  1.2 16.3 %collective-permute-start = (bf16[3,227,360]{2,1,0:T(8,128)(2,1)}, bf16[3,227,360]{2,1,0:T(8,128)(2,1)S(1)}, u32[]{:S(2)}, u32[]{:S(2)}) collective-permute-start(bf16[3,227,360]{2,1,0:T(8,128)(2,1)} %bitcast.6), channel_id=1, source_target_pairs={{0,4},{4,0},{8,12},{12,8},{1,5},{5,1},{9,13},{13,9},{2,6},{6,2},{1... | collective-permute-start | bytes 1470968 | tf_op jit(solution)/shard_map/ppermute | solution.py:442
  7.3 1.0 %copy-start = (bf16[3,360,227]{1,2,0:T(8,128)(2,1)S(1)}, bf16[3,360,227]{1,2,0:T(8,128)(2,1)}, u32[]{:S(2)}) copy-start(bf16[3,360,227]{1,2,0:T(8,128)(2,1)} %param.16) | copy-start | bytes 1470964
  8.4 6.8 %copy-start.3 = (bf16[512,512]{1,0:T(8,128)(2,1)S(1)}, bf16[512,512]{1,0:T(8,128)(2,1)}, u32[]{:S(2)}) copy-start(bf16[512,512]{1,0:T(8,128)(2,1)} %param.21) | copy-start | bytes 1572868
  8.4 6.9 %copy-start.4 = (bf16[512,512]{1,0:T(8,128)(2,1)S(1)}, bf16[512,512]{1,0:T(8,128)(2,1)}, u32[]{:S(2)}) copy-start(bf16[512,512]{1,0:T(8,128)(2,1)} %param.22) | copy-start | bytes 1572868
  8.4 6.9 %copy-start.5 = (bf16[512,512]{1,0:T(8,128)(2,1)S(1)}, bf16[512,512]{1,0:T(8,128)(2,1)}, u32[]{:S(2)}) copy-start(bf16[512,512]{1,0:T(8,128)(2,1)} %param.23) | copy-start | bytes 1572868
  8.4 7.0 %copy-start.6 = (bf16[227,512]{1,0:T(8,128)(2,1)S(1)}, bf16[227,512]{1,0:T(8,128)(2,1)}, u32[]{:S(2)}) copy-start(bf16[227,512]{1,0:T(8,128)(2,1)} %param.17) | copy-start | bytes 697348
  10.3 5.1 %copy-start.1 = (bf16[32,512]{1,0:T(8,128)(2,1)S(1)}, bf16[32,512]{1,0:T(8,128)(2,1)}, u32[]{:S(2)}) copy-start(bf16[32,512]{1,0:T(8,128)(2,1)} %mesh_in.3) | copy-start | bytes 98308
  10.3 5.1 %collective-permute-start.3 = (bf16[32,512]{1,0:T(8,128)(2,1)}, bf16[32,512]{1,0:T(8,128)(2,1)S(1)}, u32[]{:S(2)}, u32[]{:S(2)}) collective-permute-start(bf16[32,512]{1,0:T(8,128)(2,1)} %mesh_in.3), channel_id=1, source_target_pairs={{0,3},{1,2},{2,1},{3,0},{4,7},{5,6},{6,5},{7,4},{8,11},{9,10},{10,... | collective-permute-start | bytes 98312 | tf_op jit(solution)/shard_map/ppermute | solution.py:469
  10.7 4.7 %collective-permute-start.2 = (bf16[32,512]{1,0:T(8,128)(2,1)}, bf16[32,512]{1,0:T(8,128)(2,1)S(1)}, u32[]{:S(2)}, u32[]{:S(2)}) collective-permute-start(bf16[32,512]{1,0:T(8,128)(2,1)} %mesh_in.3), channel_id=1, source_target_pairs={{0,1},{1,0},{2,3},{3,2},{4,5},{5,4},{6,7},{7,6},{8,9},{9,8},{10,11... | collective-permute-start | bytes 98312 | tf_op jit(solution)/shard_map/ppermute | solution.py:468
  20.7 1.7 %collective-permute-start.4 = (bf16[32,512]{1,0:T(8,128)(2,1)S(1)}, bf16[32,512]{1,0:T(8,128)(2,1)S(1)}, u32[]{:S(2)}, u32[]{:S(2)}) collective-permute-start(bf16[32,512]{1,0:T(8,128)(2,1)S(1)} %get-tuple-element.57), channel_id=1, source_target_pairs={{0,1},{1,0},{2,3},{3,2},{4,5},{5,4},{6,7},{7,6},{8,9},{9,8},{10,11... | collective-permute-start | bytes 98312 | tf_op jit(solution)/shard_map/ppermute | solution.py:495
  20.8 3.4 %collective-permute-start.5 = (bf16[32,512]{1,0:T(8,128)(2,1)S(1)}, bf16[32,512]{1,0:T(8,128)(2,1)S(1)}, u32[]{:S(2)}, u32[]{:S(2)}) collective-permute-start(bf16[32,512]{1,0:T(8,128)(2,1)S(1)} %get-tuple-element.58), channel_id=1, source_target_pairs={{0,3},{1,2},{2,1},{3,0},{4,7},{5,6},{6,5},{7,4},{8,11},{9,10},{10,... | collective-permute-start | bytes 98312 | tf_op jit(solution)/shard_map/ppermute | solution.py:494
  24.2 5.7 %copy-start.2 = (bf16[32,512]{1,0:T(8,128)(2,1)S(1)}, bf16[32,512]{1,0:T(8,128)(2,1)}, u32[]{:S(2)}) copy-start(bf16[32,512]{1,0:T(8,128)(2,1)} %d_out.3) | copy-start | bytes 98308
  24.4 5.2 %collective-permute-start.7 = (bf16[64,512]{1,0:T(8,128)(2,1)S(1)}, bf16[64,512]{1,0:T(8,128)(2,1)S(1)}, u32[]{:S(2)}, u32[]{:S(2)}) collective-permute-start(bf16[64,512]{1,0:T(8,128)(2,1)S(1)} %get-tuple-element.59.own.nodes), channel_id=1, source_target_pairs={{0,1},{1,0},{2,3},{3,2},{4,8},{5,9},{6,10},{7,11},{8,4},{9,5},{10,... | collective-permute-start | bytes 196616 | tf_op jit(solution)/shard_map/ppermute | solution.py:502
  24.9 4.9 %collective-permute-start.6 = (bf16[64,512]{1,0:T(8,128)(2,1)S(1)}, bf16[64,512]{1,0:T(8,128)(2,1)S(1)}, u32[]{:S(2)}, u32[]{:S(2)}) collective-permute-start(bf16[64,512]{1,0:T(8,128)(2,1)S(1)} %get-tuple-element.59.own.nodes), channel_id=1, source_target_pairs={{0,4},{4,0},{8,12},{12,8},{1,5},{5,1},{9,13},{13,9},{2,6},{6,2},{1... | collective-permute-start | bytes 196616 | tf_op jit(solution)/shard_map/ppermute | solution.py:501
  27.4 6.4 %collective-permute-start.9 = (bf16[64,512]{1,0:T(8,128)(2,1)S(1)}, bf16[64,512]{1,0:T(8,128)(2,1)S(1)}, u32[]{:S(2)}, u32[]{:S(2)}) collective-permute-start(bf16[64,512]{1,0:T(8,128)(2,1)S(1)} %get-tuple-element.59.own.nodes), channel_id=1, source_target_pairs={{0,2},{2,0},{1,3},{3,1},{4,6},{6,4},{5,7},{7,5},{8,10},{10,8},{9,1... | collective-permute-start | bytes 196616 | tf_op jit(solution)/shard_map/ppermute | solution.py:414
  31.5 4.3 %collective-permute-start.8 = (bf16[64,512]{1,0:T(8,128)(2,1)S(1)}, bf16[64,512]{1,0:T(8,128)(2,1)S(1)}, u32[]{:S(2)}, u32[]{:S(2)}) collective-permute-start(bf16[64,512]{1,0:T(8,128)(2,1)S(1)} %get-tuple-element.65), channel_id=1, source_target_pairs={{0,4},{4,0},{8,12},{12,8},{1,5},{5,1},{9,13},{13,9},{2,6},{6,2},{1... | collective-permute-start | bytes 196616 | tf_op jit(solution)/shard_map/ppermute | solution.py:521
  33.4 2.4 %collective-permute-start.10 = (bf16[64,512]{1,0:T(8,128)(2,1)S(1)}, bf16[64,512]{1,0:T(8,128)(2,1)S(1)}, u32[]{:S(2)}, u32[]{:S(2)}) collective-permute-start(bf16[64,512]{1,0:T(8,128)(2,1)S(1)} %get-tuple-element.67), channel_id=1, source_target_pairs={{0,1},{1,0},{2,3},{3,2},{4,8},{5,9},{6,10},{7,11},{8,4},{9,5},{10,... | collective-permute-start | bytes 196616 | tf_op jit(solution)/shard_map/ppermute | solution.py:522
  35.9 1.7 %collective-permute-start.11 = (bf16[48,512]{1,0:T(8,128)(2,1)S(1)}, bf16[48,512]{1,0:T(8,128)(2,1)S(1)}, u32[]{:S(2)}, u32[]{:S(2)}) collective-permute-start(bf16[48,512]{1,0:T(8,128)(2,1)S(1)} %get-tuple-element.72), channel_id=1, source_target_pairs={{0,1},{1,0},{2,3},{3,2},{4,5},{5,4},{6,7},{7,6},{8,9},{9,8},{10,11... | collective-permute-start | bytes 147464 | tf_op jit(solution)/shard_map/ppermute | solution.py:536
  36.0 3.6 %collective-permute-start.12 = (bf16[48,512]{1,0:T(8,128)(2,1)S(1)}, bf16[48,512]{1,0:T(8,128)(2,1)S(1)}, u32[]{:S(2)}, u32[]{:S(2)}) collective-permute-start(bf16[48,512]{1,0:T(8,128)(2,1)S(1)} %get-tuple-element.73), channel_id=1, source_target_pairs={{0,3},{1,2},{2,1},{3,0},{4,7},{5,6},{6,5},{7,4},{8,11},{9,10},{10,... | collective-permute-start | bytes 147464 | tf_op jit(solution)/shard_map/ppermute | solution.py:535
  40.7 2.0 %collective-permute-start.14 = (bf16[1,512,128]{2,1,0:T(8,128)(2,1)S(1)}, bf16[1,512,128]{2,1,0:T(8,128)(2,1)S(1)}, u32[]{:S(2)}, u32[]{:S(2)}) collective-permute-start(bf16[1,512,128]{2,1,0:T(8,128)(2,1)S(1)} %bitcast.8), channel_id=1, source_target_pairs={{0,1},{1,0},{2,3},{3,2},{4,5},{5,4},{6,7},{7,6},{8,9},{9,8},{10,11... | collective-permute-start | bytes 393224 | tf_op jit(solution)/shard_map/ppermute | solution.py:414
  41.9 3.0 %collective-permute-start.13 = (bf16[512,128]{1,0:T(8,128)(2,1)S(1)}, bf16[512,128]{1,0:T(8,128)(2,1)S(1)}, u32[]{:S(2)}, u32[]{:S(2)}) collective-permute-start(bf16[512,128]{1,0:T(8,128)(2,1)S(1)} %bitcast.9), channel_id=1, source_target_pairs={{0,1},{1,0},{2,3},{3,2},{4,5},{5,4},{6,7},{7,6},{8,9},{9,8},{10,11... | collective-permute-start | bytes 393224 | tf_op jit(solution)/shard_map/ppermute | solution.py:414
  42.8 5.3 %collective-permute-start.15 = (bf16[320,128]{1,0:T(8,128)(2,1)S(1)}, bf16[320,128]{1,0:T(8,128)(2,1)S(1)}, u32[]{:S(2)}, u32[]{:S(2)}) collective-permute-start(bf16[320,128]{1,0:T(8,128)(2,1)S(1)} %bitcast.10), channel_id=1, source_target_pairs={{0,2},{2,0},{1,3},{3,1},{4,6},{6,4},{5,7},{7,5},{8,10},{10,8},{9,1... | collective-permute-start | bytes 245768 | tf_op jit(solution)/shard_map/ppermute | solution.py:414
  44.3 7.6 %collective-permute-start.18 = (bf16[256,128]{1,0:T(8,128)(2,1)S(1)}, bf16[256,128]{1,0:T(8,128)(2,1)S(1)}, u32[]{:S(2)}, u32[]{:S(2)}) collective-permute-start(bf16[256,128]{1,0:T(8,128)(2,1)S(1)} %bitcast.11), channel_id=1, source_target_pairs={{0,2},{2,0},{1,3},{3,1},{4,6},{6,4},{5,7},{7,5},{8,10},{10,8},{9,1... | collective-permute-start | bytes 196616 | tf_op jit(solution)/shard_map/ppermute | solution.py:414
  48.4 6.8 %collective-permute-start.16 = (bf16[2,128,128]{2,1,0:T(8,128)(2,1)S(1)}, bf16[2,128,128]{2,1,0:T(8,128)(2,1)S(1)}, u32[]{:S(2)}, u32[]{:S(2)}) collective-permute-start(bf16[2,128,128]{2,1,0:T(8,128)(2,1)S(1)} %get-tuple-element.83), channel_id=1, source_target_pairs={{0,12},{4,8},{8,4},{12,0},{1,13},{5,9},{9,5},{13,1},{2,14},{6,10},... | collective-permute-start | bytes 196616 | tf_op jit(solution)/shard_map/ppermute | solution.py:419
  50.9 6.6 %collective-permute-start.17 = (bf16[2,128,128]{2,1,0:T(8,128)(2,1)S(1)}, bf16[2,128,128]{2,1,0:T(8,128)(2,1)S(1)}, u32[]{:S(2)}, u32[]{:S(2)}) collective-permute-start(bf16[2,128,128]{2,1,0:T(8,128)(2,1)S(1)} %get-tuple-element.84), channel_id=1, source_target_pairs={{0,8},{4,12},{8,0},{12,4},{1,9},{5,13},{9,1},{13,5},{2,10},{6,14},... | collective-permute-start | bytes 196616 | tf_op jit(solution)/shard_map/ppermute | solution.py:419
  52.0 5.6 %collective-permute-start.19 = (bf16[2,128,128]{2,1,0:T(8,128)(2,1)S(1)}, bf16[2,128,128]{2,1,0:T(8,128)(2,1)S(1)}, u32[]{:S(2)}, u32[]{:S(2)}) collective-permute-start(bf16[2,128,128]{2,1,0:T(8,128)(2,1)S(1)} %get-tuple-element.87), channel_id=1, source_target_pairs={{0,4},{4,0},{8,12},{12,8},{1,5},{5,1},{9,13},{13,9},{2,6},{6,2},{1... | collective-permute-start | bytes 196616 | tf_op jit(solution)/shard_map/ppermute | solution.py:419

commit v13 on v12

--- a/solution.py
+++ b/solution.py
@@ -165,14 +165,19 @@
 ):
     half = recv_rows.shape[0] // 2
     fill(wide, near, wide.shape[1] // near.shape[0], 0)
-    raw = rows[...] + mm_nt(near_hits[...], wide[...]).astype(BF16)
-    latent, _ = silu_parts(mm(raw, stack[stack.shape[0] - raw.shape[1] :]))
-    latent = latent.astype(BF16)
-    senders_out[...] = latent
-    pre = mm(latent, weight(stack, GS)) + recv_pre[...]
-    value, slope = silu_parts(pre)
-    slope_out[...] = slope.astype(BF16)
-    sums = mm(recv_rows[...], value.astype(BF16))
+    block = rows.shape[0] // 2
+    sums = None
+    for first in range(0, rows.shape[0], block):
+        part_of = slice(first, first + block)
+        raw = rows[part_of] + mm_nt(near_hits[part_of], wide[...]).astype(BF16)
+        latent, _ = silu_parts(mm(raw, stack[stack.shape[0] - raw.shape[1] :]))
+        latent = latent.astype(BF16)
+        senders_out[part_of] = latent
+        pre = mm(latent, weight(stack, GS)) + recv_pre[part_of]
+        value, slope = silu_parts(pre)
+        slope_out[part_of] = slope.astype(BF16)
+        part = mm(recv_rows[:, part_of], value.astype(BF16))
+        sums = part if sums is None else sums + part
     part_out[...] = sums
     even = even_on("lat")
     near_out[...] = jnp.where(even, sums[half:], sums[:half]).astype(BF16)
@@ -304,17 +309,17 @@
 def add_kernel(kept, total, *refs):
     *came, first_out, second_out = refs
     bands = lax.axis_size("band")
-    half = bands // 2
     rows = kept.shape[1] // bands
+    near = second_out.shape[1] // rows
     for j in range(kept.shape[0]):
         for k in range(bands):
             block = rows_at(kept, (j,), k)
             for part in came:
                 block = block + rows_at(part, (j,), k).astype(F32)
-            out = first_out if k >= half else second_out
-            at = (k % half) * rows
+            out, at = (first_out, k - near) if k >= near else (second_out, k)
+            at = at * rows
             out[j, at : at + rows] = block.astype(BF16)
-        first_out[j, half * rows :] = total[j + 1]
+        first_out[j, (bands - near) * rows :] = total[j + 1]
 
 
 def other_lats_kernel(recv_hits, back, edge_slope, senders, after, sends):
@@ -339,23 +344,24 @@
     doms = total.shape[0]
     came, (*sends_out, sums) = refs[: 2 * (doms - 1)], refs[2 * (doms - 1) :]
     came, came_nodes = came[: doms - 1], came[doms - 1 :]
-    half = len(sends_out)
+    far = len(sends_out)
+    near = lax.axis_size("band") - far
     rows = sends_out[0].shape[1]
     second = mm_tn(nodes[...], total[0])
     for part, part_nodes in zip(came, came_nodes):
-        second = second + mm_tn(part_nodes[...], part[half * rows :])
+        second = second + mm_tn(part_nodes[...], part[far * rows :])
     sums[...] = second
     for i, out in enumerate(sends_out):
-        block = rows_at(kept, (), half + i)
+        block = rows_at(kept, (), near + i)
         for part in came:
             block = block + part[i * rows : (i + 1) * rows].astype(F32)
         out[0] = block.astype(BF16)
-        out[1] = rows_at(sums, (), half + i).astype(BF16)
+        out[1] = rows_at(sums, (), near + i).astype(BF16)
 
 
 def second_kernel(kept, sums, *refs):
-    half = lax.axis_size("band") // 2
-    came, outs = refs[:-half], refs[-half:]
+    doms = lax.axis_size("dom")
+    came, outs = refs[: doms - 1], refs[doms - 1 :]
     rows = outs[0].shape[1]
     for i, out in enumerate(outs):
         block = rows_at(kept, (), i)
@@ -553,12 +559,12 @@
     (own_sends,) = call(other_lats_kernel, [((lats - 1,) + block, BF16)], *edge, sends)
     own_came = [shifted(own_sends[i], "lat", i + 1) for i in range(lats - 1)]
     kept, own_sends = lax.optimization_barrier((kept, own_sends))
-    half = bands // 2
+    far = bands // 2
     first, second = call(
         add_kernel,
         [
-            ((doms - 1, half * rows + cycle, cols), BF16),
-            ((doms - 1, half * rows, cols), BF16),
+            ((doms - 1, far * rows + cycle, cols), BF16),
+            ((doms - 1, (bands - far) * rows, cols), BF16),
         ],
         kept, total, *came,
     )
@@ -568,13 +574,13 @@
     pair = (2, rows, cols)
     *far_sends, sums = call(
         first_kernel,
-        [(pair, BF16)] * half + [(block, F32)],
+        [(pair, BF16)] * far + [(block, F32)],
         kept, total, mesh_one, *first, *dom_nodes,
     )
-    came = [over_band(x, half + i) for i, x in reversed(list(enumerate(far_sends)))]
+    came = [over_band(x, bands - far + i) for i, x in reversed(list(enumerate(far_sends)))]
     own, *near_sends = call(
         second_kernel,
-        [(pair, F32)] + [(pair, BF16)] * (half - 1),
+        [(pair, F32)] + [(pair, BF16)] * (bands - far - 1),
         kept, sums, *second,
     )
     came += [over_band(x, i + 1) for i, x in reversed(list(enumerate(near_sends)))]

time: 58.6 us -> 58.2 us (level)
  no operation moved by 1% of the time
where the time goes in v13:
time: 58.2 us; the launch traced here: 57.8 us
  starting transfers between devices  23.3 us (40%)
  waiting for transfers between devices  13.6 us (23%)
  Pallas kernels  13.5 us (23%)
  local copies, waits for them, and re-layouts  4.43 us (8%)
  between operations  2.19 us (4%)
  other arithmetic  0.74 us (1%)
    pallas_call x17, Pallas kernels, call(): pl.pallas_call(kernel, out_shape=[jax.ShapeDtypeStruct(shape, dtype) for...  13.5 us
    ppermute x3, waiting for transfers between devices, over_band(): return lax.ppermute(x, 'band', [(b, b ^ partner) for b in range(count)])  4.65 us
    ppermute x3, starting transfers between devices, over_band(): return lax.ppermute(x, 'band', [(b, b ^ partner) for b in range(count)])  4.52 us
    unnamed x20, local copies, waits for them, and re-layouts  4.41 us
    ppermute x5, starting transfers between devices, shifted(): lax.ppermute(x, axis, [(i, (i + shift) % count) for i in range(count)])  4.22 us
    ppermute x1, starting transfers between devices, on_device(): raw_near = lax.ppermute(grid, 'band', band_near)  4.15 us
    ppermute x2, waiting for transfers between devices, on_device(): from_far = lax.ppermute(to_far, around, ring_far)  3.77 us
    ppermute x2, starting transfers between devices, on_device(): from_far = lax.ppermute(to_far, around, ring_far)  3.21 us
  transfers between devices with their start and end apart: 20, of which 8 were waited for; matrix products, arithmetic and copies ran while one was open for 7% of the time, Pallas kernels for 15%

profile of v13, /device:TPU:0, one launch (start us, length us, event | category | flops | bytes accessed | tf_op | source)
XLA Modules:
  0.0 57.8 jit_solution(6282140275343818931)
XLA Ops:
  1.2 4.1 %collective-permute-start = (bf16[3,227,360]{2,1,0:T(8,128)(2,1)}, bf16[3,227,360]{2,1,0:T(8,128)(2,1)S(1)}, u32[]{:S(2)}, u32[]{:S(2)}) collective-permute-start(bf16[3,227,360]{2,1,0:T(8,128)(2,1)} %bitcast.6), channel_id=1, source_target_pairs={{0,4},{4,0},{8,12},{12,8},{1,5},{5,1},{9,13},{13,9},{2,6},{6,2},{1... | collective-permute-start | bytes 1470968 | tf_op jit(solution)/shard_map/ppermute | solution.py:448
  6.6 0.7 %pad_add_fusion.indices = s32[1,1,3072]{2,1,0:T(1,128)S(1)} fusion(s32[1,1,512]{2,1,0:T(1,128)} %param.30, s32[1,1,512]{2,1,0:T(1,128)} %param.29, s32[1,1,1024]{2,1,0:T(1,128)} %param.27, s32[1,1,1024]{2,1,0:T(1,128)} %param.26), kind=kLoop, calls=%fused_computation.7 | loop fusion | flops 9216 | bytes 24576 | tf_op jit(solution)/shard_map/concatenate | solution.py:452
  7.3 1.0 %copy-done = bf16[3,360,227]{1,2,0:T(8,128)(2,1)S(1)} copy-done((bf16[3,360,227]{1,2,0:T(8,128)(2,1)S(1)}, bf16[3,360,227]{1,2,0:T(8,128)(2,1)}, u32[]{:S(2)}) %copy-start) | copy-done | bytes 490344
  8.4 1.9 %shard_map.175 = (bf16[1024,227]{1,0:T(8,128)(2,1)S(1)}, bf16[1024,128]{1,0:T(8,128)(2,1)S(1)}, bf16[64,1024]{1,0:T(8,128)(2,1)S(1)}, bf16[512,128]{1,0:T(8,128)...) custom-call(s32[1,1]{1,0:T(1,128)S(6)} %copy.25.count, ...), custom_call_target="tpu_custom_call" | custom-call | tf_op jit(solution)/shard_map/pallas_call | solution.py:388
  10.7 1.2 %collective-permute-start.2 = (bf16[32,512]{1,0:T(8,128)(2,1)}, bf16[32,512]{1,0:T(8,128)(2,1)S(1)}, u32[]{:S(2)}, u32[]{:S(2)}) collective-permute-start(bf16[32,512]{1,0:T(8,128)(2,1)} %mesh_in.3), channel_id=1, source_target_pairs={{0,1},{1,0},{2,3},{3,2},{4,5},{5,4},{6,7},{7,6},{8,9},{9,8},{10,11... | collective-permute-start | bytes 98312 | tf_op jit(solution)/shard_map/ppermute | solution.py:474
  12.0 1.1 %constant_dynamic-update-slice_fusion.6 = bf16[3299,512]{1,0:T(8,128)(2,1)S(1)} fusion(bf16[512,512]{1,0:T(8,128)(2,1)} %param.18), kind=kLoop, calls=%fused_computation.6 | loop fusion | bytes 1048576
  13.1 1.1 %constant_dynamic-update-slice_fusion.5 = bf16[3299,512]{1,0:T(8,128)(2,1)S(1)} fusion(bf16[3299,512]{1,0:T(8,128)(2,1)S(1)} %constant_dynamic-update-slice_fusion.6, bf16[512,512]{1,0:T(8,128)(2,1)} %param.19), kind=kLoop, calls=%fused_computation.5 | loop fusion | bytes 1048576
  14.1 1.1 %constant_dynamic-update-slice_fusion.4 = bf16[3299,512]{1,0:T(8,128)(2,1)S(1)} fusion(bf16[3299,512]{1,0:T(8,128)(2,1)S(1)} %constant_dynamic-update-slice_fusion.5, bf16[512,512]{1,0:T(8,128)(2,1)} %param.20), kind=kLoop, calls=%fused_computation.4 | loop fusion | bytes 1048576
  16.1 0.9 %shard_map.176.rows = bf16[1024,227]{1,0:T(8,128)(2,1)S(1)} custom-call(bf16[3,227,360]{2,1,0:T(8,128)(2,1)S(1)} %collective-permute-done.1.halo, bf16[1024,1152]{1,0:T(8,128)(2,1)S(1)} %get-tuple-element.51.hits, bf16[1024,227]{1,0:T(8,128)(2,1)S(1)} %get-tuple-element.53.rows), custom_call_target="tpu_custom_call" | custom-call | tf_op jit(solution)/shard_map/pallas_call | solution.py:388
  17.4 2.9 %shard_map.178 = (bf16[1024,512]{1,0:T(8,128)(2,1)S(1)}, bf16[1024,512]{1,0:T(8,128)(2,1)S(1)}, f32[64,512]{1,0:T(8,128)S(1)}, bf16[32,512]{1,0:T(8,128)(2,1)S(1)}, bf16[32,512]{1,0:T(8,128)(2,1)S(1)}) custom-call(bf16[3,227,360]{2,1,0:T(8,128)(2,1)S(1)} %collective-permute-done.near, bf16[1024,1152]{1,0:T(8,128)(2,1)S(1)} %get-tuple-element.49.near_hits, ...), custom_call_target="tpu_custom_call" | custom-call | tf_op jit(solution)/shard_map/pallas_call | solution.py:388
  20.4 1.6 %collective-permute-start.5 = (bf16[32,512]{1,0:T(8,128)(2,1)S(1)}, bf16[32,512]{1,0:T(8,128)(2,1)S(1)}, u32[]{:S(2)}, u32[]{:S(2)}) collective-permute-start(bf16[32,512]{1,0:T(8,128)(2,1)S(1)} %get-tuple-element.58), channel_id=1, source_target_pairs={{0,3},{1,2},{2,1},{3,0},{4,7},{5,6},{6,5},{7,4},{8,11},{9,10},{10,... | collective-permute-start | bytes 98312 | tf_op jit(solution)/shard_map/ppermute | solution.py:500
  22.0 1.8 %collective-permute-done.5.far = bf16[32,512]{1,0:T(8,128)(2,1)S(1)} collective-permute-done((bf16[32,512]{1,0:T(8,128)(2,1)S(1)}, bf16[32,512]{1,0:T(8,128)(2,1)S(1)}, u32[]{:S(2)}, u32[]{:S(2)}) %collective-permute-start.5) | collective-permute-done | bytes 32800 | tf_op jit(solution)/shard_map/ppermute | solution.py:500
  24.5 2.5 %collective-permute-start.6 = (bf16[64,512]{1,0:T(8,128)(2,1)S(1)}, bf16[64,512]{1,0:T(8,128)(2,1)S(1)}, u32[]{:S(2)}, u32[]{:S(2)}) collective-permute-start(bf16[64,512]{1,0:T(8,128)(2,1)S(1)} %get-tuple-element.59.own.nodes), channel_id=1, source_target_pairs={{0,4},{4,0},{8,12},{12,8},{1,5},{5,1},{9,13},{13,9},{2,6},{6,2},{1... | collective-permute-start | bytes 196616 | tf_op jit(solution)/shard_map/ppermute | solution.py:507
  27.0 1.5 %collective-permute-start.9 = (bf16[64,512]{1,0:T(8,128)(2,1)S(1)}, bf16[64,512]{1,0:T(8,128)(2,1)S(1)}, u32[]{:S(2)}, u32[]{:S(2)}) collective-permute-start(bf16[64,512]{1,0:T(8,128)(2,1)S(1)} %get-tuple-element.59.own.nodes), channel_id=1, source_target_pairs={{0,2},{2,0},{1,3},{3,1},{4,6},{6,4},{5,7},{7,5},{8,10},{10,8},{9,1... | collective-permute-start | bytes 196616 | tf_op jit(solution)/shard_map/ppermute | solution.py:420
  28.5 0.7 %shard_map.180.own_pre = f32[512,512]{1,0:T(8,128)S(1)} custom-call(bf16[512,128]{1,0:T(8,128)(2,1)S(1)} %get-tuple-element.47.own_hits, bf16[512,64]{1,0:T(8,128)(2,1)S(1)} %get-tuple-element.48.to_hits, bf16[64,512]{1,0:T(8,128)(2,1)S(1)} %get-tuple-element.59.own.nodes, bf16[3299,512]{1,0:T(8,128)(2,1)S(1)} %constant_dynamic-update-slice_fusion.stack), custom_call_target="tpu_custom_call" | custom-call | tf_op jit(solution)/shard_map/pallas_call | solution.py:388
  29.5 1.7 %shard_map.181 = (bf16[32,512]{1,0:T(8,128)(2,1)}, f32[192,512]{1,0:T(8,128)S(1)}, bf16[32,512]{1,0:T(8,128)(2,1)S(1)}, bf16[64,512]{1,0:T(8,128)(2,1)S(1)}, bf16[64,512]{1,0:T(8,128)(2,1)S(1)}) custom-call(f32[512,512]{1,0:T(8,128)S(1)} %shard_map.180.own_pre, bf16[512,256]{1,0:T(8,128)(2,1)S(1)} %get-tuple-element.60.outer_hits, ...), custom_call_target="tpu_custom_call" | custom-call | tf_op jit(solution)/shard_map/pallas_call | solution.py:388
  31.1 1.9 %collective-permute-start.8 = (bf16[64,512]{1,0:T(8,128)(2,1)S(1)}, bf16[64,512]{1,0:T(8,128)(2,1)S(1)}, u32[]{:S(2)}, u32[]{:S(2)}) collective-permute-start(bf16[64,512]{1,0:T(8,128)(2,1)S(1)} %get-tuple-element.65), channel_id=1, source_target_pairs={{0,4},{4,0},{8,12},{12,8},{1,5},{5,1},{9,13},{13,9},{2,6},{6,2},{1... | collective-permute-start | bytes 196616 | tf_op jit(solution)/shard_map/ppermute | solution.py:527
  33.4 2.0 %collective-permute-done.8.near = bf16[64,512]{1,0:T(8,128)(2,1)S(1)} collective-permute-done((bf16[64,512]{1,0:T(8,128)(2,1)S(1)}, bf16[64,512]{1,0:T(8,128)(2,1)S(1)}, u32[]{:S(2)}, u32[]{:S(2)}) %collective-permute-start.8) | collective-permute-done | bytes 65568 | tf_op jit(solution)/shard_map/ppermute | solution.py:527
  35.6 1.6 %collective-permute-start.12 = (bf16[48,512]{1,0:T(8,128)(2,1)S(1)}, bf16[48,512]{1,0:T(8,128)(2,1)S(1)}, u32[]{:S(2)}, u32[]{:S(2)}) collective-permute-start(bf16[48,512]{1,0:T(8,128)(2,1)S(1)} %get-tuple-element.73), channel_id=1, source_target_pairs={{0,3},{1,2},{2,1},{3,0},{4,7},{5,6},{6,5},{7,4},{8,11},{9,10},{10,... | collective-permute-start | bytes 147464 | tf_op jit(solution)/shard_map/ppermute | solution.py:541
  37.2 2.0 %collective-permute-done.12.far = bf16[48,512]{1,0:T(8,128)(2,1)S(1)} collective-permute-done((bf16[48,512]{1,0:T(8,128)(2,1)S(1)}, bf16[48,512]{1,0:T(8,128)(2,1)S(1)}, u32[]{:S(2)}, u32[]{:S(2)}) %collective-permute-start.12) | collective-permute-done | bytes 49184 | tf_op jit(solution)/shard_map/ppermute | solution.py:541
  39.2 1.2 %shard_map.184 = (bf16[1,1,512,128]{3,2,1,0:T(8,128)(2,1)S(1)}, bf16[128,512]{1,0:T(8,128)(2,1)S(1)}, bf16[2,64,128]{2,1,0:T(8,128)(2,1)S(1)}) custom-call(bf16[1024,128]{1,0:T(8,128)(2,1)S(1)} %get-tuple-element.55.recv_hits, f32[64,512]{1,0:T(8,128)S(1)} %get-tuple-element.71.part, bf16[48,512]{1,0:T(8,128)(2,1)S(1)} %collective-permute-done.11.near, ...), custom_call_target="tpu_custom_call" | custom-call | tf_op jit(solution)/shard_map/pallas_call | solution.py:388
  40.8 0.7 %shard_map.185 = bf16[1,512,128]{2,1,0:T(8,128)(2,1)S(1)} custom-call(bf16[1024,128]{1,0:T(8,128)(2,1)S(1)} %get-tuple-element.55.recv_hits, bf16[128,512]{1,0:T(8,128)(2,1)S(1)} %get-tuple-element.77.back, bf16[1024,512]{1,0:T(8,128)(2,1)S(1)} %get-tuple-element.76.edge_slope, bf16[512,1024]{1,0:T(8,128)(2,1)S(1)} %get-tuple-element.75.senders, ...), custom_call_target="tpu_custom_call" | custom-call | tf_op jit(solution)/shard_map/pallas_call | solution.py:388
  41.6 0.7 %shard_map.187.kept = f32[1,512,128]{2,1,0:T(8,128)S(1)} custom-call(bf16[1024,128]{1,0:T(8,128)(2,1)S(1)} %get-tuple-element.55.recv_hits, bf16[128,512]{1,0:T(8,128)(2,1)S(1)} %get-tuple-element.77.back, bf16[1024,512]{1,0:T(8,128)(2,1)S(1)} %get-tuple-element.76.edge_slope, bf16[512,1024]{1,0:T(8,128)(2,1)S(1)} %get-tuple-element.75.senders, ...), custom_call_target="tpu_custom_call" | custom-call | tf_op jit(solution)/shard_map/pallas_call | solution.py:388
  42.4 1.6 %collective-permute-start.15 = (bf16[320,128]{1,0:T(8,128)(2,1)S(1)}, bf16[320,128]{1,0:T(8,128)(2,1)S(1)}, u32[]{:S(2)}, u32[]{:S(2)}) collective-permute-start(bf16[320,128]{1,0:T(8,128)(2,1)S(1)} %bitcast.10), channel_id=1, source_target_pairs={{0,2},{2,0},{1,3},{3,1},{4,6},{6,4},{5,7},{7,5},{8,10},{10,8},{9,1... | collective-permute-start | bytes 245768 | tf_op jit(solution)/shard_map/ppermute | solution.py:420
  44.5 0.7 %shard_map.186.kept = f32[512,128]{1,0:T(8,128)S(1)} custom-call(bf16[1024,128]{1,0:T(8,128)(2,1)S(1)} %get-tuple-element.55.recv_hits, bf16[128,512]{1,0:T(8,128)(2,1)S(1)} %get-tuple-element.77.back, bf16[1024,512]{1,0:T(8,128)(2,1)S(1)} %get-tuple-element.76.edge_slope, bf16[512,1024]{1,0:T(8,128)(2,1)S(1)} %get-tuple-element.75.senders, ...), custom_call_target="tpu_custom_call" | custom-call | tf_op jit(solution)/shard_map/pallas_call | solution.py:388
  45.2 2.5 %collective-permute-done.15.refs_0_ = bf16[320,128]{1,0:T(8,128)(2,1)S(1)} collective-permute-done((bf16[320,128]{1,0:T(8,128)(2,1)S(1)}, bf16[320,128]{1,0:T(8,128)(2,1)S(1)}, u32[]{:S(2)}, u32[]{:S(2)}) %collective-permute-start.15) | collective-permute-done | bytes 81952 | tf_op jit(solution)/shard_map/ppermute | solution.py:420
  48.0 2.5 %collective-permute-start.16 = (bf16[2,128,128]{2,1,0:T(8,128)(2,1)S(1)}, bf16[2,128,128]{2,1,0:T(8,128)(2,1)S(1)}, u32[]{:S(2)}, u32[]{:S(2)}) collective-permute-start(bf16[2,128,128]{2,1,0:T(8,128)(2,1)S(1)} %get-tuple-element.83), channel_id=1, source_target_pairs={{0,12},{4,8},{8,4},{12,0},{1,13},{5,9},{9,5},{13,1},{2,14},{6,10},... | collective-permute-start | bytes 196616 | tf_op jit(solution)/shard_map/ppermute | solution.py:425
  50.5 1.0 %collective-permute-start.17 = (bf16[2,128,128]{2,1,0:T(8,128)(2,1)S(1)}, bf16[2,128,128]{2,1,0:T(8,128)(2,1)S(1)}, u32[]{:S(2)}, u32[]{:S(2)}) collective-permute-start(bf16[2,128,128]{2,1,0:T(8,128)(2,1)S(1)} %get-tuple-element.84), channel_id=1, source_target_pairs={{0,8},{4,12},{8,0},{12,4},{1,9},{5,13},{9,1},{13,5},{2,10},{6,14},... | collective-permute-start | bytes 196616 | tf_op jit(solution)/shard_map/ppermute | solution.py:425
  51.6 1.0 %collective-permute-start.19 = (bf16[2,128,128]{2,1,0:T(8,128)(2,1)S(1)}, bf16[2,128,128]{2,1,0:T(8,128)(2,1)S(1)}, u32[]{:S(2)}, u32[]{:S(2)}) collective-permute-start(bf16[2,128,128]{2,1,0:T(8,128)(2,1)S(1)} %get-tuple-element.87), channel_id=1, source_target_pairs={{0,4},{4,0},{8,12},{12,8},{1,5},{5,1},{9,13},{13,9},{2,6},{6,2},{1... | collective-permute-start | bytes 196616 | tf_op jit(solution)/shard_map/ppermute | solution.py:425
  52.5 2.3 %collective-permute-done.16.refs_0_ = bf16[2,128,128]{2,1,0:T(8,128)(2,1)S(1)} collective-permute-done((bf16[2,128,128]{2,1,0:T(8,128)(2,1)S(1)}, bf16[2,128,128]{2,1,0:T(8,128)(2,1)S(1)}, u32[]{:S(2)}, u32[]{:S(2)}) %collective-permute-start.16) | collective-permute-done | bytes 65568 | tf_op jit(solution)/shard_map/ppermute | solution.py:425
  54.8 2.4 %collective-permute-done.17.refs_1_ = bf16[2,128,128]{2,1,0:T(8,128)(2,1)S(1)} collective-permute-done((bf16[2,128,128]{2,1,0:T(8,128)(2,1)S(1)}, bf16[2,128,128]{2,1,0:T(8,128)(2,1)S(1)}, u32[]{:S(2)}, u32[]{:S(2)}) %collective-permute-start.17) | collective-permute-done | bytes 65568 | tf_op jit(solution)/shard_map/ppermute | solution.py:425
  57.2 0.7 %shard_map.191 = (f32[128,128]{1,0:T(8,128)}, f32[128,128]{1,0:T(8,128)}) custom-call(bf16[2,128,128]{2,1,0:T(8,128)(2,1)S(1)} %collective-permute-done.16.refs_0_, bf16[2,128,128]{2,1,0:T(8,128)(2,1)S(1)} %collective-permute-done.17.refs_1_, bf16[2,128,128]{2,1,0:T(8,128)(2,1)S(1)} %collective-permute-done.19.refs_2_, ...), custom_call_target="tpu_custom_call" | custom-call | tf_op jit(solution)/shard_map/pallas_call | solution.py:388
  (47 shorter events, 5.2 us)
Async XLA Ops:
  0.6 15.4 %collective-permute-start.1 = (bf16[3,227,360]{2,1,0:T(8,128)(2,1)}, bf16[3,227,360]{2,1,0:T(8,128)(2,1)S(1)}, u32[]{:S(2)}, u32[]{:S(2)}) collective-permute-start(bf16[3,227,360]{2,1,0:T(8,128)(2,1)} %bitcast.5), channel_id=1, source_target_pairs={{0,1},{1,0},{2,3},{3,2},{4,8},{5,9},{6,10},{7,11},{8,4},{9,5},{10,... | collective-permute-start | bytes 1470968 | tf_op jit(solution)/shard_map/ppermute | solution.py:449
  1.2 16.3 %collective-permute-start = (bf16[3,227,360]{2,1,0:T(8,128)(2,1)}, bf16[3,227,360]{2,1,0:T(8,128)(2,1)S(1)}, u32[]{:S(2)}, u32[]{:S(2)}) collective-permute-start(bf16[3,227,360]{2,1,0:T(8,128)(2,1)} %bitcast.6), channel_id=1, source_target_pairs={{0,4},{4,0},{8,12},{12,8},{1,5},{5,1},{9,13},{13,9},{2,6},{6,2},{1... | collective-permute-start | bytes 1470968 | tf_op jit(solution)/shard_map/ppermute | solution.py:448
  7.3 1.0 %copy-start = (bf16[3,360,227]{1,2,0:T(8,128)(2,1)S(1)}, bf16[3,360,227]{1,2,0:T(8,128)(2,1)}, u32[]{:S(2)}) copy-start(bf16[3,360,227]{1,2,0:T(8,128)(2,1)} %param.16) | copy-start | bytes 1470964
  8.4 6.8 %copy-start.3 = (bf16[512,512]{1,0:T(8,128)(2,1)S(1)}, bf16[512,512]{1,0:T(8,128)(2,1)}, u32[]{:S(2)}) copy-start(bf16[512,512]{1,0:T(8,128)(2,1)} %param.21) | copy-start | bytes 1572868
  8.4 6.9 %copy-start.4 = (bf16[512,512]{1,0:T(8,128)(2,1)S(1)}, bf16[512,512]{1,0:T(8,128)(2,1)}, u32[]{:S(2)}) copy-start(bf16[512,512]{1,0:T(8,128)(2,1)} %param.22) | copy-start | bytes 1572868
  8.4 6.9 %copy-start.5 = (bf16[512,512]{1,0:T(8,128)(2,1)S(1)}, bf16[512,512]{1,0:T(8,128)(2,1)}, u32[]{:S(2)}) copy-start(bf16[512,512]{1,0:T(8,128)(2,1)} %param.23) | copy-start | bytes 1572868
  8.4 7.0 %copy-start.6 = (bf16[227,512]{1,0:T(8,128)(2,1)S(1)}, bf16[227,512]{1,0:T(8,128)(2,1)}, u32[]{:S(2)}) copy-start(bf16[227,512]{1,0:T(8,128)(2,1)} %param.17) | copy-start | bytes 697348
  10.3 5.1 %copy-start.1 = (bf16[32,512]{1,0:T(8,128)(2,1)S(1)}, bf16[32,512]{1,0:T(8,128)(2,1)}, u32[]{:S(2)}) copy-start(bf16[32,512]{1,0:T(8,128)(2,1)} %mesh_in.3) | copy-start | bytes 98308
  10.3 5.1 %collective-permute-start.3 = (bf16[32,512]{1,0:T(8,128)(2,1)}, bf16[32,512]{1,0:T(8,128)(2,1)S(1)}, u32[]{:S(2)}, u32[]{:S(2)}) collective-permute-start(bf16[32,512]{1,0:T(8,128)(2,1)} %mesh_in.3), channel_id=1, source_target_pairs={{0,3},{1,2},{2,1},{3,0},{4,7},{5,6},{6,5},{7,4},{8,11},{9,10},{10,... | collective-permute-start | bytes 98312 | tf_op jit(solution)/shard_map/ppermute | solution.py:475
  10.7 4.7 %collective-permute-start.2 = (bf16[32,512]{1,0:T(8,128)(2,1)}, bf16[32,512]{1,0:T(8,128)(2,1)S(1)}, u32[]{:S(2)}, u32[]{:S(2)}) collective-permute-start(bf16[32,512]{1,0:T(8,128)(2,1)} %mesh_in.3), channel_id=1, source_target_pairs={{0,1},{1,0},{2,3},{3,2},{4,5},{5,4},{6,7},{7,6},{8,9},{9,8},{10,11... | collective-permute-start | bytes 98312 | tf_op jit(solution)/shard_map/ppermute | solution.py:474
  20.3 1.7 %collective-permute-start.4 = (bf16[32,512]{1,0:T(8,128)(2,1)S(1)}, bf16[32,512]{1,0:T(8,128)(2,1)S(1)}, u32[]{:S(2)}, u32[]{:S(2)}) collective-permute-start(bf16[32,512]{1,0:T(8,128)(2,1)S(1)} %get-tuple-element.57), channel_id=1, source_target_pairs={{0,1},{1,0},{2,3},{3,2},{4,5},{5,4},{6,7},{7,6},{8,9},{9,8},{10,11... | collective-permute-start | bytes 98312 | tf_op jit(solution)/shard_map/ppermute | solution.py:501
  20.4 3.4 %collective-permute-start.5 = (bf16[32,512]{1,0:T(8,128)(2,1)S(1)}, bf16[32,512]{1,0:T(8,128)(2,1)S(1)}, u32[]{:S(2)}, u32[]{:S(2)}) collective-permute-start(bf16[32,512]{1,0:T(8,128)(2,1)S(1)} %get-tuple-element.58), channel_id=1, source_target_pairs={{0,3},{1,2},{2,1},{3,0},{4,7},{5,6},{6,5},{7,4},{8,11},{9,10},{10,... | collective-permute-start | bytes 98312 | tf_op jit(solution)/shard_map/ppermute | solution.py:500
  23.8 5.7 %copy-start.2 = (bf16[32,512]{1,0:T(8,128)(2,1)S(1)}, bf16[32,512]{1,0:T(8,128)(2,1)}, u32[]{:S(2)}) copy-start(bf16[32,512]{1,0:T(8,128)(2,1)} %d_out.3) | copy-start | bytes 98308
  24.0 5.2 %collective-permute-start.7 = (bf16[64,512]{1,0:T(8,128)(2,1)S(1)}, bf16[64,512]{1,0:T(8,128)(2,1)S(1)}, u32[]{:S(2)}, u32[]{:S(2)}) collective-permute-start(bf16[64,512]{1,0:T(8,128)(2,1)S(1)} %get-tuple-element.59.own.nodes), channel_id=1, source_target_pairs={{0,1},{1,0},{2,3},{3,2},{4,8},{5,9},{6,10},{7,11},{8,4},{9,5},{10,... | collective-permute-start | bytes 196616 | tf_op jit(solution)/shard_map/ppermute | solution.py:508
  24.5 4.9 %collective-permute-start.6 = (bf16[64,512]{1,0:T(8,128)(2,1)S(1)}, bf16[64,512]{1,0:T(8,128)(2,1)S(1)}, u32[]{:S(2)}, u32[]{:S(2)}) collective-permute-start(bf16[64,512]{1,0:T(8,128)(2,1)S(1)} %get-tuple-element.59.own.nodes), channel_id=1, source_target_pairs={{0,4},{4,0},{8,12},{12,8},{1,5},{5,1},{9,13},{13,9},{2,6},{6,2},{1... | collective-permute-start | bytes 196616 | tf_op jit(solution)/shard_map/ppermute | solution.py:507
  27.0 6.4 %collective-permute-start.9 = (bf16[64,512]{1,0:T(8,128)(2,1)S(1)}, bf16[64,512]{1,0:T(8,128)(2,1)S(1)}, u32[]{:S(2)}, u32[]{:S(2)}) collective-permute-start(bf16[64,512]{1,0:T(8,128)(2,1)S(1)} %get-tuple-element.59.own.nodes), channel_id=1, source_target_pairs={{0,2},{2,0},{1,3},{3,1},{4,6},{6,4},{5,7},{7,5},{8,10},{10,8},{9,1... | collective-permute-start | bytes 196616 | tf_op jit(solution)/shard_map/ppermute | solution.py:420
  31.1 4.3 %collective-permute-start.8 = (bf16[64,512]{1,0:T(8,128)(2,1)S(1)}, bf16[64,512]{1,0:T(8,128)(2,1)S(1)}, u32[]{:S(2)}, u32[]{:S(2)}) collective-permute-start(bf16[64,512]{1,0:T(8,128)(2,1)S(1)} %get-tuple-element.65), channel_id=1, source_target_pairs={{0,4},{4,0},{8,12},{12,8},{1,5},{5,1},{9,13},{13,9},{2,6},{6,2},{1... | collective-permute-start | bytes 196616 | tf_op jit(solution)/shard_map/ppermute | solution.py:527
  33.0 2.4 %collective-permute-start.10 = (bf16[64,512]{1,0:T(8,128)(2,1)S(1)}, bf16[64,512]{1,0:T(8,128)(2,1)S(1)}, u32[]{:S(2)}, u32[]{:S(2)}) collective-permute-start(bf16[64,512]{1,0:T(8,128)(2,1)S(1)} %get-tuple-element.67), channel_id=1, source_target_pairs={{0,1},{1,0},{2,3},{3,2},{4,8},{5,9},{6,10},{7,11},{8,4},{9,5},{10,... | collective-permute-start | bytes 196616 | tf_op jit(solution)/shard_map/ppermute | solution.py:528
  35.5 1.7 %collective-permute-start.11 = (bf16[48,512]{1,0:T(8,128)(2,1)S(1)}, bf16[48,512]{1,0:T(8,128)(2,1)S(1)}, u32[]{:S(2)}, u32[]{:S(2)}) collective-permute-start(bf16[48,512]{1,0:T(8,128)(2,1)S(1)} %get-tuple-element.72), channel_id=1, source_target_pairs={{0,1},{1,0},{2,3},{3,2},{4,5},{5,4},{6,7},{7,6},{8,9},{9,8},{10,11... | collective-permute-start | bytes 147464 | tf_op jit(solution)/shard_map/ppermute | solution.py:542
  35.6 3.6 %collective-permute-start.12 = (bf16[48,512]{1,0:T(8,128)(2,1)S(1)}, bf16[48,512]{1,0:T(8,128)(2,1)S(1)}, u32[]{:S(2)}, u32[]{:S(2)}) collective-permute-start(bf16[48,512]{1,0:T(8,128)(2,1)S(1)} %get-tuple-element.73), channel_id=1, source_target_pairs={{0,3},{1,2},{2,1},{3,0},{4,7},{5,6},{6,5},{7,4},{8,11},{9,10},{10,... | collective-permute-start | bytes 147464 | tf_op jit(solution)/shard_map/ppermute | solution.py:541
  40.3 2.0 %collective-permute-start.14 = (bf16[1,512,128]{2,1,0:T(8,128)(2,1)S(1)}, bf16[1,512,128]{2,1,0:T(8,128)(2,1)S(1)}, u32[]{:S(2)}, u32[]{:S(2)}) collective-permute-start(bf16[1,512,128]{2,1,0:T(8,128)(2,1)S(1)} %bitcast.8), channel_id=1, source_target_pairs={{0,1},{1,0},{2,3},{3,2},{4,5},{5,4},{6,7},{7,6},{8,9},{9,8},{10,11... | collective-permute-start | bytes 393224 | tf_op jit(solution)/shard_map/ppermute | solution.py:420
  41.5 3.0 %collective-permute-start.13 = (bf16[512,128]{1,0:T(8,128)(2,1)S(1)}, bf16[512,128]{1,0:T(8,128)(2,1)S(1)}, u32[]{:S(2)}, u32[]{:S(2)}) collective-permute-start(bf16[512,128]{1,0:T(8,128)(2,1)S(1)} %bitcast.9), channel_id=1, source_target_pairs={{0,1},{1,0},{2,3},{3,2},{4,5},{5,4},{6,7},{7,6},{8,9},{9,8},{10,11... | collective-permute-start | bytes 393224 | tf_op jit(solution)/shard_map/ppermute | solution.py:420
  42.4 5.3 %collective-permute-start.15 = (bf16[320,128]{1,0:T(8,128)(2,1)S(1)}, bf16[320,128]{1,0:T(8,128)(2,1)S(1)}, u32[]{:S(2)}, u32[]{:S(2)}) collective-permute-start(bf16[320,128]{1,0:T(8,128)(2,1)S(1)} %bitcast.10), channel_id=1, source_target_pairs={{0,2},{2,0},{1,3},{3,1},{4,6},{6,4},{5,7},{7,5},{8,10},{10,8},{9,1... | collective-permute-start | bytes 245768 | tf_op jit(solution)/shard_map/ppermute | solution.py:420
  43.9 7.6 %collective-permute-start.18 = (bf16[256,128]{1,0:T(8,128)(2,1)S(1)}, bf16[256,128]{1,0:T(8,128)(2,1)S(1)}, u32[]{:S(2)}, u32[]{:S(2)}) collective-permute-start(bf16[256,128]{1,0:T(8,128)(2,1)S(1)} %bitcast.11), channel_id=1, source_target_pairs={{0,2},{2,0},{1,3},{3,1},{4,6},{6,4},{5,7},{7,5},{8,10},{10,8},{9,1... | collective-permute-start | bytes 196616 | tf_op jit(solution)/shard_map/ppermute | solution.py:420
  48.0 6.8 %collective-permute-start.16 = (bf16[2,128,128]{2,1,0:T(8,128)(2,1)S(1)}, bf16[2,128,128]{2,1,0:T(8,128)(2,1)S(1)}, u32[]{:S(2)}, u32[]{:S(2)}) collective-permute-start(bf16[2,128,128]{2,1,0:T(8,128)(2,1)S(1)} %get-tuple-element.83), channel_id=1, source_target_pairs={{0,12},{4,8},{8,4},{12,0},{1,13},{5,9},{9,5},{13,1},{2,14},{6,10},... | collective-permute-start | bytes 196616 | tf_op jit(solution)/shard_map/ppermute | solution.py:425
  50.5 6.6 %collective-permute-start.17 = (bf16[2,128,128]{2,1,0:T(8,128)(2,1)S(1)}, bf16[2,128,128]{2,1,0:T(8,128)(2,1)S(1)}, u32[]{:S(2)}, u32[]{:S(2)}) collective-permute-start(bf16[2,128,128]{2,1,0:T(8,128)(2,1)S(1)} %get-tuple-element.84), channel_id=1, source_target_pairs={{0,8},{4,12},{8,0},{12,4},{1,9},{5,13},{9,1},{13,5},{2,10},{6,14},... | collective-permute-start | bytes 196616 | tf_op jit(solution)/shard_map/ppermute | solution.py:425
  51.6 5.6 %collective-permute-start.19 = (bf16[2,128,128]{2,1,0:T(8,128)(2,1)S(1)}, bf16[2,128,128]{2,1,0:T(8,128)(2,1)S(1)}, u32[]{:S(2)}, u32[]{:S(2)}) collective-permute-start(bf16[2,128,128]{2,1,0:T(8,128)(2,1)S(1)} %get-tuple-element.87), channel_id=1, source_target_pairs={{0,4},{4,0},{8,12},{12,8},{1,5},{5,1},{9,13},{13,9},{2,6},{6,2},{1... | collective-permute-start | bytes 196616 | tf_op jit(solution)/shard_map/ppermute | solution.py:425

commit v14 on v13

--- a/solution.py
+++ b/solution.py
@@ -217,16 +217,28 @@
     home = own[rim : rim + node_count]
     block = jnp.concatenate([near[...], far[...]], axis=0)
     table = jnp.concatenate(halves(mm(block, weight(stack, MS))), axis=0)
-    pre = own_pre[...] + mm(outer_hits[...], table)
-    value, slope = silu_parts(pre)
-    gate = mm(mm(to_rows[...], value.astype(BF16)).astype(BF16), weight(stack, MN))
+    halves_of = [slice(i, i + own_pre.shape[0] // 2) for i in (0, own_pre.shape[0] // 2)]
+    slopes = []
+    total = None
+    for part_of in halves_of:
+        pre = own_pre[part_of] + mm(outer_hits[part_of], table)
+        value, slope = silu_parts(pre)
+        slopes.append(slope)
+        part = mm(to_rows[:, part_of], value.astype(BF16))
+        total = part if total is None else total + part
+    gate = mm(total.astype(BF16), weight(stack, MN))
     gate_value, gate_slope = silu_parts(gate)
     mesh_out[...] = (home.astype(F32) + gate_value).astype(BF16)
     gate_two = (d_out[...].astype(F32) * gate_slope).astype(BF16)
     back = jnp.concatenate(halves(mm_nt(gate_two, weight(stack, MN))), axis=0)
-    edge_slope = (mm(to_hits[...], back) * slope).astype(BF16)
-    sums = mm(from_rows[...], edge_slope)
-    recv_out[...] = mm(to_rows[...], edge_slope).astype(BF16)
+    sums = received = None
+    for part_of, slope in zip(halves_of, slopes):
+        edge_slope = (mm(to_hits[part_of], back) * slope).astype(BF16)
+        part = mm(from_rows[:, part_of], edge_slope)
+        sums = part if sums is None else sums + part
+        part = mm(to_rows[:, part_of], edge_slope)
+        received = part if received is None else received + part
+    recv_out[...] = received.astype(BF16)
     sums_out[...] = sums
     near_out[...] = sums[:cycle].astype(BF16)
     far_out[...] = sums[2 * cycle :].astype(BF16)
@@ -260,11 +272,19 @@
     far_out[half:] = jnp.where(even, home[:rim], home[rim:]).astype(BF16)
 
 
-def gradient_block(recv_hits, back, edge_slope, senders, dom_shift, lat_shift, doms, lats):
-    place = (dom_shift, lat_shift, doms, lats)
-    slope = mm(recv_hits[...], block_of(back, *place))
-    slope = slope * block_of(edge_slope, *place).astype(F32)
-    return mm(senders[...], slope.astype(BF16))
+def gradient_block(recv_hits, back, edge_slope, senders, shifts, doms, lats):
+    edges = recv_hits.shape[0]
+    back = [block_of(back, *shift, doms, lats) for shift in shifts]
+    back = back[0] if len(back) == 1 else jnp.concatenate(back, axis=1)
+    total = None
+    for first in range(0, edges, edges // 2):
+        part_of = slice(first, first + edges // 2)
+        weights = [block_of(edge_slope[part_of], *shift, doms, lats) for shift in shifts]
+        weights = weights[0] if len(weights) == 1 else jnp.concatenate(weights, axis=1)
+        slope = mm(recv_hits[part_of], back) * weights.astype(F32)
+        part = mm(senders[:, part_of], slope.astype(BF16))
+        total = part if total is None else total + part
+    return total
 
 
 def encode_grad_kernel(
@@ -286,17 +306,26 @@
     doms = sends.shape[1] + 1
     for i in range(1, lats):
         for j in range(1, doms):
-            block = gradient_block(recv_hits, back, edge_slope, senders, j, i, doms, lats)
+            block = gradient_block(
+                recv_hits, back, edge_slope, senders, [(j, i)], doms, lats
+            )
             sends[i - 1, j - 1] = block.astype(BF16)
     for j in range(doms):
         total_out[j] = block_of(total, j, 0, doms, lats)
 
 
-def kept_blocks_kernel(recv_hits, back, edge_slope, senders, after, kept):
+def middle_blocks_kernel(recv_hits, back, edge_slope, senders, after, kept, sends):
     doms = kept.shape[0] + 1
-    lats = back.shape[1] // kept.shape[2] // doms
-    for j in range(1, doms):
-        kept[j - 1] = gradient_block(recv_hits, back, edge_slope, senders, j, 0, doms, lats)
+    lats = sends.shape[0] + 1
+    cols = kept.shape[2]
+    shifts = [(j, 0) for j in range(1, doms)] + [(0, i) for i in range(1, lats)]
+    blocks = gradient_block(recv_hits, back[...], edge_slope, senders, shifts, doms, lats)
+    for k in range(len(shifts)):
+        block = blocks[:, k * cols : (k + 1) * cols]
+        if k < doms - 1:
+            kept[k] = block
+        else:
+            sends[k - doms + 1] = block.astype(BF16)
 
 
 def rows_at(ref, place, partner):
@@ -322,19 +351,13 @@
         first_out[j, (bands - near) * rows :] = total[j + 1]
 
 
-def other_lats_kernel(recv_hits, back, edge_slope, senders, after, sends):
-    lats = sends.shape[0] + 1
-    doms = back.shape[1] // sends.shape[2] // lats
-    for i in range(1, lats):
-        block = gradient_block(recv_hits, back, edge_slope, senders, 0, i, doms, lats)
-        sends[i - 1] = block.astype(BF16)
-
-
 def own_block_kernel(recv_hits, back, edge_slope, senders, *refs):
     *came, out = refs
     lats = len(came) + 1
     doms = back.shape[1] // out.shape[1] // lats
-    block = gradient_block(recv_hits, back, edge_slope, senders, 0, 0, doms, lats)
+    block = gradient_block(
+        recv_hits, back[...], edge_slope, senders, [(0, 0)], doms, lats
+    )
     for part in came:
         block = block + part[...].astype(F32)
     out[...] = block
@@ -555,10 +578,12 @@
     edge = (recv_hits, back, edge_slope, senders)
     came = [shifted(sends[i], "lat", i + 1) for i in range(lats - 1)]
     block = (latent, cols)
-    (kept,) = call(kept_blocks_kernel, [((doms - 1,) + block, F32)], *edge, sends)
-    (own_sends,) = call(other_lats_kernel, [((lats - 1,) + block, BF16)], *edge, sends)
+    kept, own_sends = call(
+        middle_blocks_kernel,
+        [((doms - 1,) + block, F32), ((lats - 1,) + block, BF16)],
+        *edge, sends,
+    )
     own_came = [shifted(own_sends[i], "lat", i + 1) for i in range(lats - 1)]
-    kept, own_sends = lax.optimization_barrier((kept, own_sends))
     far = bands // 2
     first, second = call(
         add_kernel,

time: 58.2 us -> 57.4 us (0.986)
  Pallas kernels: 13.5 us -> 12.7 us
    pallas_call x17 -> x16, Pallas kernels: 13.5 us -> 12.7 us  [call(): pl.pallas_call(kernel, out_shape=[jax.ShapeDtypeStruct(shape, dtype) for...]
  transfers between devices with their start and end apart: 20 -> 20, of which waited for: 8 -> 9; matrix products, arithmetic and copies ran while one was open for 7% -> 7% of each run, Pallas kernels for 15% -> 14%
where the time goes in v14:
time: 57.4 us; the launch traced here: 57.1 us
  starting transfers between devices  23.4 us (41%)
  waiting for transfers between devices  13.6 us (24%)
  Pallas kernels  12.7 us (22%)
  local copies, waits for them, and re-layouts  4.43 us (8%)
  between operations  2.19 us (4%)
  other arithmetic  0.74 us (1%)
    pallas_call x16, Pallas kernels, call(): pl.pallas_call(kernel, out_shape=[jax.ShapeDtypeStruct(shape, dtype) for...  12.7 us
    ppermute x3, starting transfers between devices, over_band(): return lax.ppermute(x, 'band', [(b, b ^ partner) for b in range(count)])  4.52 us
    ppermute x3, waiting for transfers between devices, over_band(): return lax.ppermute(x, 'band', [(b, b ^ partner) for b in range(count)])  4.45 us
    unnamed x20, local copies, waits for them, and re-layouts  4.41 us
    ppermute x5, starting transfers between devices, shifted(): lax.ppermute(x, axis, [(i, (i + shift) % count) for i in range(count)])  4.23 us
    ppermute x1, starting transfers between devices, on_device(): raw_near = lax.ppermute(grid, 'band', band_near)  4.15 us
    ppermute x2, waiting for transfers between devices, on_device(): from_far = lax.ppermute(to_far, around, ring_far)  3.76 us
    ppermute x2, starting transfers between devices, on_device(): from_far = lax.ppermute(to_far, around, ring_far)  3.22 us
  transfers between devices with their start and end apart: 20, of which 9 were waited for; matrix products, arithmetic and copies ran while one was open for 7% of the time, Pallas kernels for 14%

profile of v14, /device:TPU:0, one launch (start us, length us, event | category | flops | bytes accessed | tf_op | source)
XLA Modules:
  0.0 57.1 jit_solution(12666486554479643744)
XLA Ops:
  1.2 4.1 %collective-permute-start = (bf16[3,227,360]{2,1,0:T(8,128)(2,1)}, bf16[3,227,360]{2,1,0:T(8,128)(2,1)S(1)}, u32[]{:S(2)}, u32[]{:S(2)}) collective-permute-start(bf16[3,227,360]{2,1,0:T(8,128)(2,1)} %bitcast.6), channel_id=1, source_target_pairs={{0,4},{4,0},{8,12},{12,8},{1,5},{5,1},{9,13},{13,9},{2,6},{6,2},{1... | collective-permute-start | bytes 1470968 | tf_op jit(solution)/shard_map/ppermute | solution.py:471
  6.6 0.7 %pad_add_fusion.indices = s32[1,1,3072]{2,1,0:T(1,128)S(1)} fusion(s32[1,1,512]{2,1,0:T(1,128)} %param.30, s32[1,1,512]{2,1,0:T(1,128)} %param.29, s32[1,1,1024]{2,1,0:T(1,128)} %param.27, s32[1,1,1024]{2,1,0:T(1,128)} %param.26), kind=kLoop, calls=%fused_computation.7 | loop fusion | flops 9216 | bytes 24576 | tf_op jit(solution)/shard_map/concatenate | solution.py:475
  7.3 1.0 %copy-done = bf16[3,360,227]{1,2,0:T(8,128)(2,1)S(1)} copy-done((bf16[3,360,227]{1,2,0:T(8,128)(2,1)S(1)}, bf16[3,360,227]{1,2,0:T(8,128)(2,1)}, u32[]{:S(2)}) %copy-start) | copy-done | bytes 490344
  8.4 1.9 %shard_map.175 = (bf16[1024,227]{1,0:T(8,128)(2,1)S(1)}, bf16[1024,128]{1,0:T(8,128)(2,1)S(1)}, bf16[64,1024]{1,0:T(8,128)(2,1)S(1)}, bf16[512,128]{1,0:T(8,128)...) custom-call(s32[1,1]{1,0:T(1,128)S(6)} %copy.25.count, ...), custom_call_target="tpu_custom_call" | custom-call | tf_op jit(solution)/shard_map/pallas_call | solution.py:411
  10.7 1.2 %collective-permute-start.2 = (bf16[32,512]{1,0:T(8,128)(2,1)}, bf16[32,512]{1,0:T(8,128)(2,1)S(1)}, u32[]{:S(2)}, u32[]{:S(2)}) collective-permute-start(bf16[32,512]{1,0:T(8,128)(2,1)} %mesh_in.3), channel_id=1, source_target_pairs={{0,1},{1,0},{2,3},{3,2},{4,5},{5,4},{6,7},{7,6},{8,9},{9,8},{10,11... | collective-permute-start | bytes 98312 | tf_op jit(solution)/shard_map/ppermute | solution.py:497
  12.0 1.1 %constant_dynamic-update-slice_fusion.6 = bf16[3299,512]{1,0:T(8,128)(2,1)S(1)} fusion(bf16[512,512]{1,0:T(8,128)(2,1)} %param.18), kind=kLoop, calls=%fused_computation.6 | loop fusion | bytes 1048576
  13.1 1.1 %constant_dynamic-update-slice_fusion.5 = bf16[3299,512]{1,0:T(8,128)(2,1)S(1)} fusion(bf16[3299,512]{1,0:T(8,128)(2,1)S(1)} %constant_dynamic-update-slice_fusion.6, bf16[512,512]{1,0:T(8,128)(2,1)} %param.19), kind=kLoop, calls=%fused_computation.5 | loop fusion | bytes 1048576
  14.1 1.1 %constant_dynamic-update-slice_fusion.4 = bf16[3299,512]{1,0:T(8,128)(2,1)S(1)} fusion(bf16[3299,512]{1,0:T(8,128)(2,1)S(1)} %constant_dynamic-update-slice_fusion.5, bf16[512,512]{1,0:T(8,128)(2,1)} %param.20), kind=kLoop, calls=%fused_computation.4 | loop fusion | bytes 1048576
  15.4 0.6 %shard_map.177.recv_pre = f32[1024,512]{1,0:T(8,128)S(1)} custom-call(bf16[32,512]{1,0:T(8,128)(2,1)S(1)} %collective-permute-done.2.near.mesh_near, bf16[32,512]{1,0:T(8,128)(2,1)S(1)} %collective-permute-done.3.far.mesh_far, bf16[32,512]{1,0:T(8,128)(2,1)S(1)} %copy-done.1, bf16[1024,128]{1,0:T(8,128)(2,1)S(1)} %get-tuple-element.56.recv_hits, ...), custom_call_target="tpu_custom_call" | custom-call | tf_op jit(solution)/shard_map/pallas_call | solution.py:411
  16.1 0.9 %shard_map.176.rows = bf16[1024,227]{1,0:T(8,128)(2,1)S(1)} custom-call(bf16[3,227,360]{2,1,0:T(8,128)(2,1)S(1)} %collective-permute-done.1.halo, bf16[1024,1152]{1,0:T(8,128)(2,1)S(1)} %get-tuple-element.52.hits, bf16[1024,227]{1,0:T(8,128)(2,1)S(1)} %get-tuple-element.54.rows), custom_call_target="tpu_custom_call" | custom-call | tf_op jit(solution)/shard_map/pallas_call | solution.py:411
  17.4 2.9 %shard_map.178 = (bf16[1024,512]{1,0:T(8,128)(2,1)S(1)}, bf16[1024,512]{1,0:T(8,128)(2,1)S(1)}, f32[64,512]{1,0:T(8,128)S(1)}, bf16[32,512]{1,0:T(8,128)(2,1)S(1)}, bf16[32,512]{1,0:T(8,128)(2,1)S(1)}) custom-call(bf16[3,227,360]{2,1,0:T(8,128)(2,1)S(1)} %collective-permute-done.near, bf16[1024,1152]{1,0:T(8,128)(2,1)S(1)} %get-tuple-element.50.near_hits, ...), custom_call_target="tpu_custom_call" | custom-call | tf_op jit(solution)/shard_map/pallas_call | solution.py:411
  20.4 1.6 %collective-permute-start.5 = (bf16[32,512]{1,0:T(8,128)(2,1)S(1)}, bf16[32,512]{1,0:T(8,128)(2,1)S(1)}, u32[]{:S(2)}, u32[]{:S(2)}) collective-permute-start(bf16[32,512]{1,0:T(8,128)(2,1)S(1)} %get-tuple-element.59), channel_id=1, source_target_pairs={{0,3},{1,2},{2,1},{3,0},{4,7},{5,6},{6,5},{7,4},{8,11},{9,10},{10,... | collective-permute-start | bytes 98312 | tf_op jit(solution)/shard_map/ppermute | solution.py:523
  22.0 1.8 %collective-permute-done.5.far = bf16[32,512]{1,0:T(8,128)(2,1)S(1)} collective-permute-done((bf16[32,512]{1,0:T(8,128)(2,1)S(1)}, bf16[32,512]{1,0:T(8,128)(2,1)S(1)}, u32[]{:S(2)}, u32[]{:S(2)}) %collective-permute-start.5) | collective-permute-done | bytes 32800 | tf_op jit(solution)/shard_map/ppermute | solution.py:523
  24.5 2.5 %collective-permute-start.6 = (bf16[64,512]{1,0:T(8,128)(2,1)S(1)}, bf16[64,512]{1,0:T(8,128)(2,1)S(1)}, u32[]{:S(2)}, u32[]{:S(2)}) collective-permute-start(bf16[64,512]{1,0:T(8,128)(2,1)S(1)} %get-tuple-element.60.own.nodes), channel_id=1, source_target_pairs={{0,4},{4,0},{8,12},{12,8},{1,5},{5,1},{9,13},{13,9},{2,6},{6,2},{1... | collective-permute-start | bytes 196616 | tf_op jit(solution)/shard_map/ppermute | solution.py:530
  27.0 1.5 %collective-permute-start.9 = (bf16[64,512]{1,0:T(8,128)(2,1)S(1)}, bf16[64,512]{1,0:T(8,128)(2,1)S(1)}, u32[]{:S(2)}, u32[]{:S(2)}) collective-permute-start(bf16[64,512]{1,0:T(8,128)(2,1)S(1)} %get-tuple-element.60.own.nodes), channel_id=1, source_target_pairs={{0,2},{2,0},{1,3},{3,1},{4,6},{6,4},{5,7},{7,5},{8,10},{10,8},{9,1... | collective-permute-start | bytes 196616 | tf_op jit(solution)/shard_map/ppermute | solution.py:443
  28.5 0.7 %shard_map.180.own_pre = f32[512,512]{1,0:T(8,128)S(1)} custom-call(bf16[512,128]{1,0:T(8,128)(2,1)S(1)} %get-tuple-element.48.own_hits, bf16[512,64]{1,0:T(8,128)(2,1)S(1)} %get-tuple-element.49.to_hits, bf16[64,512]{1,0:T(8,128)(2,1)S(1)} %get-tuple-element.60.own.nodes, bf16[3299,512]{1,0:T(8,128)(2,1)S(1)} %constant_dynamic-update-slice_fusion.stack), custom_call_target="tpu_custom_call" | custom-call | tf_op jit(solution)/shard_map/pallas_call | solution.py:411
  29.5 1.7 %shard_map.181 = (bf16[32,512]{1,0:T(8,128)(2,1)}, f32[192,512]{1,0:T(8,128)S(1)}, bf16[32,512]{1,0:T(8,128)(2,1)S(1)}, bf16[64,512]{1,0:T(8,128)(2,1)S(1)}, bf16[64,512]{1,0:T(8,128)(2,1)S(1)}) custom-call(f32[512,512]{1,0:T(8,128)S(1)} %shard_map.180.own_pre, bf16[512,256]{1,0:T(8,128)(2,1)S(1)} %get-tuple-element.61.outer_hits, ...), custom_call_target="tpu_custom_call" | custom-call | tf_op jit(solution)/shard_map/pallas_call | solution.py:411
  31.2 1.9 %collective-permute-start.8 = (bf16[64,512]{1,0:T(8,128)(2,1)S(1)}, bf16[64,512]{1,0:T(8,128)(2,1)S(1)}, u32[]{:S(2)}, u32[]{:S(2)}) collective-permute-start(bf16[64,512]{1,0:T(8,128)(2,1)S(1)} %get-tuple-element.66), channel_id=1, source_target_pairs={{0,4},{4,0},{8,12},{12,8},{1,5},{5,1},{9,13},{13,9},{2,6},{6,2},{1... | collective-permute-start | bytes 196616 | tf_op jit(solution)/shard_map/ppermute | solution.py:550
  33.5 2.0 %collective-permute-done.8.near = bf16[64,512]{1,0:T(8,128)(2,1)S(1)} collective-permute-done((bf16[64,512]{1,0:T(8,128)(2,1)S(1)}, bf16[64,512]{1,0:T(8,128)(2,1)S(1)}, u32[]{:S(2)}, u32[]{:S(2)}) %collective-permute-start.8) | collective-permute-done | bytes 65568 | tf_op jit(solution)/shard_map/ppermute | solution.py:550
  35.6 1.6 %collective-permute-start.12 = (bf16[48,512]{1,0:T(8,128)(2,1)S(1)}, bf16[48,512]{1,0:T(8,128)(2,1)S(1)}, u32[]{:S(2)}, u32[]{:S(2)}) collective-permute-start(bf16[48,512]{1,0:T(8,128)(2,1)S(1)} %get-tuple-element.74), channel_id=1, source_target_pairs={{0,3},{1,2},{2,1},{3,0},{4,7},{5,6},{6,5},{7,4},{8,11},{9,10},{10,... | collective-permute-start | bytes 147464 | tf_op jit(solution)/shard_map/ppermute | solution.py:564
  37.2 2.0 %collective-permute-done.12.far = bf16[48,512]{1,0:T(8,128)(2,1)S(1)} collective-permute-done((bf16[48,512]{1,0:T(8,128)(2,1)S(1)}, bf16[48,512]{1,0:T(8,128)(2,1)S(1)}, u32[]{:S(2)}, u32[]{:S(2)}) %collective-permute-start.12) | collective-permute-done | bytes 49184 | tf_op jit(solution)/shard_map/ppermute | solution.py:564
  39.2 1.1 %shard_map.184 = (bf16[1,1,512,128]{3,2,1,0:T(8,128)(2,1)S(1)}, bf16[128,512]{1,0:T(8,128)(2,1)S(1)}, bf16[2,64,128]{2,1,0:T(8,128)(2,1)S(1)}) custom-call(bf16[1024,128]{1,0:T(8,128)(2,1)S(1)} %get-tuple-element.56.recv_hits, f32[64,512]{1,0:T(8,128)S(1)} %get-tuple-element.72.part, bf16[48,512]{1,0:T(8,128)(2,1)S(1)} %collective-permute-done.11.near, ...), custom_call_target="tpu_custom_call" | custom-call | tf_op jit(solution)/shard_map/pallas_call | solution.py:411
  40.8 0.7 %shard_map.185 = (f32[1,512,128]{2,1,0:T(8,128)S(1)}, bf16[1,512,128]{2,1,0:T(8,128)(2,1)S(1)}) custom-call(bf16[1024,128]{1,0:T(8,128)(2,1)S(1)} %get-tuple-element.56.recv_hits, bf16[128,512]{1,0:T(8,128)(2,1)S(1)} %get-tuple-element.78.back, bf16[1024,512]{1,0:T(8,128)(2,1)S(1)} %get-tuple-element.77.edge_slope, ...), custom_call_target="tpu_custom_call" | custom-call | tf_op jit(solution)/shard_map/pallas_call | solution.py:411
  41.8 1.6 %collective-permute-start.15 = (bf16[320,128]{1,0:T(8,128)(2,1)S(1)}, bf16[320,128]{1,0:T(8,128)(2,1)S(1)}, u32[]{:S(2)}, u32[]{:S(2)}) collective-permute-start(bf16[320,128]{1,0:T(8,128)(2,1)S(1)} %bitcast.10), channel_id=1, source_target_pairs={{0,2},{2,0},{1,3},{3,1},{4,6},{6,4},{5,7},{7,5},{8,10},{10,8},{9,1... | collective-permute-start | bytes 245768 | tf_op jit(solution)/shard_map/ppermute | solution.py:443
  43.9 0.6 %shard_map.186.kept = f32[512,128]{1,0:T(8,128)S(1)} custom-call(bf16[1024,128]{1,0:T(8,128)(2,1)S(1)} %get-tuple-element.56.recv_hits, bf16[128,512]{1,0:T(8,128)(2,1)S(1)} %get-tuple-element.78.back, bf16[1024,512]{1,0:T(8,128)(2,1)S(1)} %get-tuple-element.77.edge_slope, bf16[512,1024]{1,0:T(8,128)(2,1)S(1)} %get-tuple-element.76.senders, ...), custom_call_target="tpu_custom_call" | custom-call | tf_op jit(solution)/shard_map/pallas_call | solution.py:411
  44.6 2.6 %collective-permute-done.15.refs_0_ = bf16[320,128]{1,0:T(8,128)(2,1)S(1)} collective-permute-done((bf16[320,128]{1,0:T(8,128)(2,1)S(1)}, bf16[320,128]{1,0:T(8,128)(2,1)S(1)}, u32[]{:S(2)}, u32[]{:S(2)}) %collective-permute-start.15) | collective-permute-done | bytes 81952 | tf_op jit(solution)/shard_map/ppermute | solution.py:443
  47.4 2.6 %collective-permute-start.16 = (bf16[2,128,128]{2,1,0:T(8,128)(2,1)S(1)}, bf16[2,128,128]{2,1,0:T(8,128)(2,1)S(1)}, u32[]{:S(2)}, u32[]{:S(2)}) collective-permute-start(bf16[2,128,128]{2,1,0:T(8,128)(2,1)S(1)} %get-tuple-element.85), channel_id=1, source_target_pairs={{0,12},{4,8},{8,4},{12,0},{1,13},{5,9},{9,5},{13,1},{2,14},{6,10},... | collective-permute-start | bytes 196616 | tf_op jit(solution)/shard_map/ppermute | solution.py:448
  50.0 1.0 %collective-permute-start.17 = (bf16[2,128,128]{2,1,0:T(8,128)(2,1)S(1)}, bf16[2,128,128]{2,1,0:T(8,128)(2,1)S(1)}, u32[]{:S(2)}, u32[]{:S(2)}) collective-permute-start(bf16[2,128,128]{2,1,0:T(8,128)(2,1)S(1)} %get-tuple-element.86), channel_id=1, source_target_pairs={{0,8},{4,12},{8,0},{12,4},{1,9},{5,13},{9,1},{13,5},{2,10},{6,14},... | collective-permute-start | bytes 196616 | tf_op jit(solution)/shard_map/ppermute | solution.py:448
  51.0 1.0 %collective-permute-start.19 = (bf16[2,128,128]{2,1,0:T(8,128)(2,1)S(1)}, bf16[2,128,128]{2,1,0:T(8,128)(2,1)S(1)}, u32[]{:S(2)}, u32[]{:S(2)}) collective-permute-start(bf16[2,128,128]{2,1,0:T(8,128)(2,1)S(1)} %get-tuple-element.89), channel_id=1, source_target_pairs={{0,4},{4,0},{8,12},{12,8},{1,5},{5,1},{9,13},{13,9},{2,6},{6,2},{1... | collective-permute-start | bytes 196616 | tf_op jit(solution)/shard_map/ppermute | solution.py:448
  52.0 2.3 %collective-permute-done.16.refs_0_ = bf16[2,128,128]{2,1,0:T(8,128)(2,1)S(1)} collective-permute-done((bf16[2,128,128]{2,1,0:T(8,128)(2,1)S(1)}, bf16[2,128,128]{2,1,0:T(8,128)(2,1)S(1)}, u32[]{:S(2)}, u32[]{:S(2)}) %collective-permute-start.16) | collective-permute-done | bytes 65568 | tf_op jit(solution)/shard_map/ppermute | solution.py:448
  54.3 2.1 %collective-permute-done.17.refs_1_ = bf16[2,128,128]{2,1,0:T(8,128)(2,1)S(1)} collective-permute-done((bf16[2,128,128]{2,1,0:T(8,128)(2,1)S(1)}, bf16[2,128,128]{2,1,0:T(8,128)(2,1)S(1)}, u32[]{:S(2)}, u32[]{:S(2)}) %collective-permute-start.17) | collective-permute-done | bytes 65568 | tf_op jit(solution)/shard_map/ppermute | solution.py:448
  56.4 0.7 %shard_map.190 = (f32[128,128]{1,0:T(8,128)}, f32[128,128]{1,0:T(8,128)}) custom-call(bf16[2,128,128]{2,1,0:T(8,128)(2,1)S(1)} %collective-permute-done.16.refs_0_, bf16[2,128,128]{2,1,0:T(8,128)(2,1)S(1)} %collective-permute-done.17.refs_1_, bf16[2,128,128]{2,1,0:T(8,128)(2,1)S(1)} %collective-permute-done.19.refs_2_, ...), custom_call_target="tpu_custom_call" | custom-call | tf_op jit(solution)/shard_map/pallas_call | solution.py:411
  (46 shorter events, 4.7 us)
Async XLA Ops:
  0.6 15.4 %collective-permute-start.1 = (bf16[3,227,360]{2,1,0:T(8,128)(2,1)}, bf16[3,227,360]{2,1,0:T(8,128)(2,1)S(1)}, u32[]{:S(2)}, u32[]{:S(2)}) collective-permute-start(bf16[3,227,360]{2,1,0:T(8,128)(2,1)} %bitcast.5), channel_id=1, source_target_pairs={{0,1},{1,0},{2,3},{3,2},{4,8},{5,9},{6,10},{7,11},{8,4},{9,5},{10,... | collective-permute-start | bytes 1470968 | tf_op jit(solution)/shard_map/ppermute | solution.py:472
  1.2 16.3 %collective-permute-start = (bf16[3,227,360]{2,1,0:T(8,128)(2,1)}, bf16[3,227,360]{2,1,0:T(8,128)(2,1)S(1)}, u32[]{:S(2)}, u32[]{:S(2)}) collective-permute-start(bf16[3,227,360]{2,1,0:T(8,128)(2,1)} %bitcast.6), channel_id=1, source_target_pairs={{0,4},{4,0},{8,12},{12,8},{1,5},{5,1},{9,13},{13,9},{2,6},{6,2},{1... | collective-permute-start | bytes 1470968 | tf_op jit(solution)/shard_map/ppermute | solution.py:471
  7.3 1.0 %copy-start = (bf16[3,360,227]{1,2,0:T(8,128)(2,1)S(1)}, bf16[3,360,227]{1,2,0:T(8,128)(2,1)}, u32[]{:S(2)}) copy-start(bf16[3,360,227]{1,2,0:T(8,128)(2,1)} %param.16) | copy-start | bytes 1470964
  8.4 6.8 %copy-start.3 = (bf16[512,512]{1,0:T(8,128)(2,1)S(1)}, bf16[512,512]{1,0:T(8,128)(2,1)}, u32[]{:S(2)}) copy-start(bf16[512,512]{1,0:T(8,128)(2,1)} %param.21) | copy-start | bytes 1572868
  8.4 6.9 %copy-start.4 = (bf16[512,512]{1,0:T(8,128)(2,1)S(1)}, bf16[512,512]{1,0:T(8,128)(2,1)}, u32[]{:S(2)}) copy-start(bf16[512,512]{1,0:T(8,128)(2,1)} %param.22) | copy-start | bytes 1572868
  8.4 6.9 %copy-start.5 = (bf16[512,512]{1,0:T(8,128)(2,1)S(1)}, bf16[512,512]{1,0:T(8,128)(2,1)}, u32[]{:S(2)}) copy-start(bf16[512,512]{1,0:T(8,128)(2,1)} %param.23) | copy-start | bytes 1572868
  8.4 7.0 %copy-start.6 = (bf16[227,512]{1,0:T(8,128)(2,1)S(1)}, bf16[227,512]{1,0:T(8,128)(2,1)}, u32[]{:S(2)}) copy-start(bf16[227,512]{1,0:T(8,128)(2,1)} %param.17) | copy-start | bytes 697348
  10.3 5.1 %copy-start.1 = (bf16[32,512]{1,0:T(8,128)(2,1)S(1)}, bf16[32,512]{1,0:T(8,128)(2,1)}, u32[]{:S(2)}) copy-start(bf16[32,512]{1,0:T(8,128)(2,1)} %mesh_in.3) | copy-start | bytes 98308
  10.3 5.1 %collective-permute-start.3 = (bf16[32,512]{1,0:T(8,128)(2,1)}, bf16[32,512]{1,0:T(8,128)(2,1)S(1)}, u32[]{:S(2)}, u32[]{:S(2)}) collective-permute-start(bf16[32,512]{1,0:T(8,128)(2,1)} %mesh_in.3), channel_id=1, source_target_pairs={{0,3},{1,2},{2,1},{3,0},{4,7},{5,6},{6,5},{7,4},{8,11},{9,10},{10,... | collective-permute-start | bytes 98312 | tf_op jit(solution)/shard_map/ppermute | solution.py:498
  10.7 4.7 %collective-permute-start.2 = (bf16[32,512]{1,0:T(8,128)(2,1)}, bf16[32,512]{1,0:T(8,128)(2,1)S(1)}, u32[]{:S(2)}, u32[]{:S(2)}) collective-permute-start(bf16[32,512]{1,0:T(8,128)(2,1)} %mesh_in.3), channel_id=1, source_target_pairs={{0,1},{1,0},{2,3},{3,2},{4,5},{5,4},{6,7},{7,6},{8,9},{9,8},{10,11... | collective-permute-start | bytes 98312 | tf_op jit(solution)/shard_map/ppermute | solution.py:497
  20.3 1.7 %collective-permute-start.4 = (bf16[32,512]{1,0:T(8,128)(2,1)S(1)}, bf16[32,512]{1,0:T(8,128)(2,1)S(1)}, u32[]{:S(2)}, u32[]{:S(2)}) collective-permute-start(bf16[32,512]{1,0:T(8,128)(2,1)S(1)} %get-tuple-element.58), channel_id=1, source_target_pairs={{0,1},{1,0},{2,3},{3,2},{4,5},{5,4},{6,7},{7,6},{8,9},{9,8},{10,11... | collective-permute-start | bytes 98312 | tf_op jit(solution)/shard_map/ppermute | solution.py:524
  20.4 3.4 %collective-permute-start.5 = (bf16[32,512]{1,0:T(8,128)(2,1)S(1)}, bf16[32,512]{1,0:T(8,128)(2,1)S(1)}, u32[]{:S(2)}, u32[]{:S(2)}) collective-permute-start(bf16[32,512]{1,0:T(8,128)(2,1)S(1)} %get-tuple-element.59), channel_id=1, source_target_pairs={{0,3},{1,2},{2,1},{3,0},{4,7},{5,6},{6,5},{7,4},{8,11},{9,10},{10,... | collective-permute-start | bytes 98312 | tf_op jit(solution)/shard_map/ppermute | solution.py:523
  23.8 5.7 %copy-start.2 = (bf16[32,512]{1,0:T(8,128)(2,1)S(1)}, bf16[32,512]{1,0:T(8,128)(2,1)}, u32[]{:S(2)}) copy-start(bf16[32,512]{1,0:T(8,128)(2,1)} %d_out.3) | copy-start | bytes 98308
  24.0 5.2 %collective-permute-start.7 = (bf16[64,512]{1,0:T(8,128)(2,1)S(1)}, bf16[64,512]{1,0:T(8,128)(2,1)S(1)}, u32[]{:S(2)}, u32[]{:S(2)}) collective-permute-start(bf16[64,512]{1,0:T(8,128)(2,1)S(1)} %get-tuple-element.60.own.nodes), channel_id=1, source_target_pairs={{0,1},{1,0},{2,3},{3,2},{4,8},{5,9},{6,10},{7,11},{8,4},{9,5},{10,... | collective-permute-start | bytes 196616 | tf_op jit(solution)/shard_map/ppermute | solution.py:531
  24.5 4.9 %collective-permute-start.6 = (bf16[64,512]{1,0:T(8,128)(2,1)S(1)}, bf16[64,512]{1,0:T(8,128)(2,1)S(1)}, u32[]{:S(2)}, u32[]{:S(2)}) collective-permute-start(bf16[64,512]{1,0:T(8,128)(2,1)S(1)} %get-tuple-element.60.own.nodes), channel_id=1, source_target_pairs={{0,4},{4,0},{8,12},{12,8},{1,5},{5,1},{9,13},{13,9},{2,6},{6,2},{1... | collective-permute-start | bytes 196616 | tf_op jit(solution)/shard_map/ppermute | solution.py:530
  27.0 6.4 %collective-permute-start.9 = (bf16[64,512]{1,0:T(8,128)(2,1)S(1)}, bf16[64,512]{1,0:T(8,128)(2,1)S(1)}, u32[]{:S(2)}, u32[]{:S(2)}) collective-permute-start(bf16[64,512]{1,0:T(8,128)(2,1)S(1)} %get-tuple-element.60.own.nodes), channel_id=1, source_target_pairs={{0,2},{2,0},{1,3},{3,1},{4,6},{6,4},{5,7},{7,5},{8,10},{10,8},{9,1... | collective-permute-start | bytes 196616 | tf_op jit(solution)/shard_map/ppermute | solution.py:443
  31.2 4.3 %collective-permute-start.8 = (bf16[64,512]{1,0:T(8,128)(2,1)S(1)}, bf16[64,512]{1,0:T(8,128)(2,1)S(1)}, u32[]{:S(2)}, u32[]{:S(2)}) collective-permute-start(bf16[64,512]{1,0:T(8,128)(2,1)S(1)} %get-tuple-element.66), channel_id=1, source_target_pairs={{0,4},{4,0},{8,12},{12,8},{1,5},{5,1},{9,13},{13,9},{2,6},{6,2},{1... | collective-permute-start | bytes 196616 | tf_op jit(solution)/shard_map/ppermute | solution.py:550
  33.1 2.4 %collective-permute-start.10 = (bf16[64,512]{1,0:T(8,128)(2,1)S(1)}, bf16[64,512]{1,0:T(8,128)(2,1)S(1)}, u32[]{:S(2)}, u32[]{:S(2)}) collective-permute-start(bf16[64,512]{1,0:T(8,128)(2,1)S(1)} %get-tuple-element.68), channel_id=1, source_target_pairs={{0,1},{1,0},{2,3},{3,2},{4,8},{5,9},{6,10},{7,11},{8,4},{9,5},{10,... | collective-permute-start | bytes 196616 | tf_op jit(solution)/shard_map/ppermute | solution.py:551
  35.6 1.7 %collective-permute-start.11 = (bf16[48,512]{1,0:T(8,128)(2,1)S(1)}, bf16[48,512]{1,0:T(8,128)(2,1)S(1)}, u32[]{:S(2)}, u32[]{:S(2)}) collective-permute-start(bf16[48,512]{1,0:T(8,128)(2,1)S(1)} %get-tuple-element.73), channel_id=1, source_target_pairs={{0,1},{1,0},{2,3},{3,2},{4,5},{5,4},{6,7},{7,6},{8,9},{9,8},{10,11... | collective-permute-start | bytes 147464 | tf_op jit(solution)/shard_map/ppermute | solution.py:565
  35.6 3.6 %collective-permute-start.12 = (bf16[48,512]{1,0:T(8,128)(2,1)S(1)}, bf16[48,512]{1,0:T(8,128)(2,1)S(1)}, u32[]{:S(2)}, u32[]{:S(2)}) collective-permute-start(bf16[48,512]{1,0:T(8,128)(2,1)S(1)} %get-tuple-element.74), channel_id=1, source_target_pairs={{0,3},{1,2},{2,1},{3,0},{4,7},{5,6},{6,5},{7,4},{8,11},{9,10},{10,... | collective-permute-start | bytes 147464 | tf_op jit(solution)/shard_map/ppermute | solution.py:564
  40.3 1.5 %collective-permute-start.14 = (bf16[1,512,128]{2,1,0:T(8,128)(2,1)S(1)}, bf16[1,512,128]{2,1,0:T(8,128)(2,1)S(1)}, u32[]{:S(2)}, u32[]{:S(2)}) collective-permute-start(bf16[1,512,128]{2,1,0:T(8,128)(2,1)S(1)} %bitcast.8), channel_id=1, source_target_pairs={{0,1},{1,0},{2,3},{3,2},{4,5},{5,4},{6,7},{7,6},{8,9},{9,8},{10,11... | collective-permute-start | bytes 393224 | tf_op jit(solution)/shard_map/ppermute | solution.py:443
  41.5 2.4 %collective-permute-start.13 = (bf16[512,128]{1,0:T(8,128)(2,1)S(1)}, bf16[512,128]{1,0:T(8,128)(2,1)S(1)}, u32[]{:S(2)}, u32[]{:S(2)}) collective-permute-start(bf16[512,128]{1,0:T(8,128)(2,1)S(1)} %bitcast.9), channel_id=1, source_target_pairs={{0,1},{1,0},{2,3},{3,2},{4,5},{5,4},{6,7},{7,6},{8,9},{9,8},{10,11... | collective-permute-start | bytes 393224 | tf_op jit(solution)/shard_map/ppermute | solution.py:443
  41.8 5.3 %collective-permute-start.15 = (bf16[320,128]{1,0:T(8,128)(2,1)S(1)}, bf16[320,128]{1,0:T(8,128)(2,1)S(1)}, u32[]{:S(2)}, u32[]{:S(2)}) collective-permute-start(bf16[320,128]{1,0:T(8,128)(2,1)S(1)} %bitcast.10), channel_id=1, source_target_pairs={{0,2},{2,0},{1,3},{3,1},{4,6},{6,4},{5,7},{7,5},{8,10},{10,8},{9,1... | collective-permute-start | bytes 245768 | tf_op jit(solution)/shard_map/ppermute | solution.py:443
  43.4 7.6 %collective-permute-start.18 = (bf16[256,128]{1,0:T(8,128)(2,1)S(1)}, bf16[256,128]{1,0:T(8,128)(2,1)S(1)}, u32[]{:S(2)}, u32[]{:S(2)}) collective-permute-start(bf16[256,128]{1,0:T(8,128)(2,1)S(1)} %bitcast.11), channel_id=1, source_target_pairs={{0,2},{2,0},{1,3},{3,1},{4,6},{6,4},{5,7},{7,5},{8,10},{10,8},{9,1... | collective-permute-start | bytes 196616 | tf_op jit(solution)/shard_map/ppermute | solution.py:443
  47.4 6.9 %collective-permute-start.16 = (bf16[2,128,128]{2,1,0:T(8,128)(2,1)S(1)}, bf16[2,128,128]{2,1,0:T(8,128)(2,1)S(1)}, u32[]{:S(2)}, u32[]{:S(2)}) collective-permute-start(bf16[2,128,128]{2,1,0:T(8,128)(2,1)S(1)} %get-tuple-element.85), channel_id=1, source_target_pairs={{0,12},{4,8},{8,4},{12,0},{1,13},{5,9},{9,5},{13,1},{2,14},{6,10},... | collective-permute-start | bytes 196616 | tf_op jit(solution)/shard_map/ppermute | solution.py:448
  50.0 6.4 %collective-permute-start.17 = (bf16[2,128,128]{2,1,0:T(8,128)(2,1)S(1)}, bf16[2,128,128]{2,1,0:T(8,128)(2,1)S(1)}, u32[]{:S(2)}, u32[]{:S(2)}) collective-permute-start(bf16[2,128,128]{2,1,0:T(8,128)(2,1)S(1)} %get-tuple-element.86), channel_id=1, source_target_pairs={{0,8},{4,12},{8,0},{12,4},{1,9},{5,13},{9,1},{13,5},{2,10},{6,14},... | collective-permute-start | bytes 196616 | tf_op jit(solution)/shard_map/ppermute | solution.py:448
  51.0 5.4 %collective-permute-start.19 = (bf16[2,128,128]{2,1,0:T(8,128)(2,1)S(1)}, bf16[2,128,128]{2,1,0:T(8,128)(2,1)S(1)}, u32[]{:S(2)}, u32[]{:S(2)}) collective-permute-start(bf16[2,128,128]{2,1,0:T(8,128)(2,1)S(1)} %get-tuple-element.89), channel_id=1, source_target_pairs={{0,4},{4,0},{8,12},{12,8},{1,5},{5,1},{9,13},{13,9},{2,6},{6,2},{1... | collective-permute-start | bytes 196616 | tf_op jit(solution)/shard_map/ppermute | solution.py:448

commit v15 on v14

--- a/solution.py
+++ b/solution.py
@@ -165,7 +165,7 @@
 ):
     half = recv_rows.shape[0] // 2
     fill(wide, near, wide.shape[1] // near.shape[0], 0)
-    block = rows.shape[0] // 2
+    block = rows.shape[0] // 4
     sums = None
     for first in range(0, rows.shape[0], block):
         part_of = slice(first, first + block)
@@ -208,7 +208,7 @@
 
 
 def process_kernel(
-    own_pre, outer_hits, to_hits, from_rows, to_rows, near, own, far, d_out, stack,
+    own_pre, outer_hits, to_hits, from_rows, to_rows, far, own, near, d_out, stack,
     mesh_out, sums_out, recv_out, near_out, far_out,
 ):
     cycle = own.shape[0]
@@ -217,28 +217,16 @@
     home = own[rim : rim + node_count]
     block = jnp.concatenate([near[...], far[...]], axis=0)
     table = jnp.concatenate(halves(mm(block, weight(stack, MS))), axis=0)
-    halves_of = [slice(i, i + own_pre.shape[0] // 2) for i in (0, own_pre.shape[0] // 2)]
-    slopes = []
-    total = None
-    for part_of in halves_of:
-        pre = own_pre[part_of] + mm(outer_hits[part_of], table)
-        value, slope = silu_parts(pre)
-        slopes.append(slope)
-        part = mm(to_rows[:, part_of], value.astype(BF16))
-        total = part if total is None else total + part
-    gate = mm(total.astype(BF16), weight(stack, MN))
+    pre = own_pre[...] + mm(outer_hits[...], table)
+    value, slope = silu_parts(pre)
+    gate = mm(mm(to_rows[...], value.astype(BF16)).astype(BF16), weight(stack, MN))
     gate_value, gate_slope = silu_parts(gate)
     mesh_out[...] = (home.astype(F32) + gate_value).astype(BF16)
     gate_two = (d_out[...].astype(F32) * gate_slope).astype(BF16)
     back = jnp.concatenate(halves(mm_nt(gate_two, weight(stack, MN))), axis=0)
-    sums = received = None
-    for part_of, slope in zip(halves_of, slopes):
-        edge_slope = (mm(to_hits[part_of], back) * slope).astype(BF16)
-        part = mm(from_rows[:, part_of], edge_slope)
-        sums = part if sums is None else sums + part
-        part = mm(to_rows[:, part_of], edge_slope)
-        received = part if received is None else received + part
-    recv_out[...] = received.astype(BF16)
+    edge_slope = (mm(to_hits[...], back) * slope).astype(BF16)
+    sums = mm(from_rows[...], edge_slope)
+    recv_out[...] = mm(to_rows[...], edge_slope).astype(BF16)
     sums_out[...] = sums
     near_out[...] = sums[:cycle].astype(BF16)
     far_out[...] = sums[2 * cycle :].astype(BF16)
@@ -544,7 +532,7 @@
             ((cycle, latent), BF16),
             ((cycle, latent), BF16),
         ],
-        own_pre, outer_hits, to_hits, from_rows, to_rows, one_near, mesh_one, one_far, d_out,
+        own_pre, outer_hits, to_hits, from_rows, to_rows, one_far, mesh_one, one_near, d_out,
         stack,
     )
     from_near = lax.ppermute(to_near, "band", band_near)

time: 57.4 us -> 57.1 us (level)
  starting transfers between devices: 23.4 us -> 22.7 us
    ppermute x1, starting transfers between devices: 2.49 us -> 1.78 us  [on_device(): one_near = lax.ppermute(mesh_one, 'band', band_near)]
where the time goes in v15:
time: 57.1 us; the launch traced here: 56.8 us
  starting transfers between devices  22.7 us (40%)
  waiting for transfers between devices  14 us (25%)
  Pallas kernels  12.7 us (22%)
  local copies, waits for them, and re-layouts  4.43 us (8%)
  between operations  2.18 us (4%)
  other arithmetic  0.74 us (1%)
    pallas_call x16, Pallas kernels, call(): pl.pallas_call(kernel, out_shape=[jax.ShapeDtypeStruct(shape, dtype) for...  12.7 us
    ppermute x3, waiting for transfers between devices, over_band(): return lax.ppermute(x, 'band', [(b, b ^ partner) for b in range(count)])  4.81 us
    ppermute x3, starting transfers between devices, over_band(): return lax.ppermute(x, 'band', [(b, b ^ partner) for b in range(count)])  4.52 us
    unnamed x20, local copies, waits for them, and re-layouts  4.41 us
    ppermute x5, starting transfers between devices, shifted(): lax.ppermute(x, axis, [(i, (i + shift) % count) for i in range(count)])  4.23 us
    ppermute x1, starting transfers between devices, on_device(): raw_near = lax.ppermute(grid, 'band', band_near)  4.15 us
    ppermute x2, waiting for transfers between devices, on_device(): from_far = lax.ppermute(to_far, around, ring_far)  3.77 us
    ppermute x2, starting transfers between devices, on_device(): from_far = lax.ppermute(to_far, around, ring_far)  3.21 us
  transfers between devices with their start and end apart: 20, of which 9 were waited for; matrix products, arithmetic and copies ran while one was open for 7% of the time, Pallas kernels for 14%

profile of v15, /device:TPU:0, one launch (start us, length us, event | category | flops | bytes accessed | tf_op | source)
XLA Modules:
  0.0 56.8 jit_solution(13009213707436239972)
XLA Ops:
  1.2 4.1 %collective-permute-start = (bf16[3,227,360]{2,1,0:T(8,128)(2,1)}, bf16[3,227,360]{2,1,0:T(8,128)(2,1)S(1)}, u32[]{:S(2)}, u32[]{:S(2)}) collective-permute-start(bf16[3,227,360]{2,1,0:T(8,128)(2,1)} %bitcast.6), channel_id=1, source_target_pairs={{0,4},{4,0},{8,12},{12,8},{1,5},{5,1},{9,13},{13,9},{2,6},{6,2},{1... | collective-permute-start | bytes 1470968 | tf_op jit(solution)/shard_map/ppermute | solution.py:459
  6.6 0.7 %pad_add_fusion.indices = s32[1,1,3072]{2,1,0:T(1,128)S(1)} fusion(s32[1,1,512]{2,1,0:T(1,128)} %param.30, s32[1,1,512]{2,1,0:T(1,128)} %param.29, s32[1,1,1024]{2,1,0:T(1,128)} %param.27, s32[1,1,1024]{2,1,0:T(1,128)} %param.26), kind=kLoop, calls=%fused_computation.7 | loop fusion | flops 9216 | bytes 24576 | tf_op jit(solution)/shard_map/concatenate | solution.py:463
  7.3 1.0 %copy-done = bf16[3,360,227]{1,2,0:T(8,128)(2,1)S(1)} copy-done((bf16[3,360,227]{1,2,0:T(8,128)(2,1)S(1)}, bf16[3,360,227]{1,2,0:T(8,128)(2,1)}, u32[]{:S(2)}) %copy-start) | copy-done | bytes 490344
  8.4 1.9 %shard_map.175 = (bf16[1024,227]{1,0:T(8,128)(2,1)S(1)}, bf16[1024,128]{1,0:T(8,128)(2,1)S(1)}, bf16[64,1024]{1,0:T(8,128)(2,1)S(1)}, bf16[512,128]{1,0:T(8,128)...) custom-call(s32[1,1]{1,0:T(1,128)S(6)} %copy.25.count, ...), custom_call_target="tpu_custom_call" | custom-call | tf_op jit(solution)/shard_map/pallas_call | solution.py:399
  10.7 1.2 %collective-permute-start.2 = (bf16[32,512]{1,0:T(8,128)(2,1)}, bf16[32,512]{1,0:T(8,128)(2,1)S(1)}, u32[]{:S(2)}, u32[]{:S(2)}) collective-permute-start(bf16[32,512]{1,0:T(8,128)(2,1)} %mesh_in.3), channel_id=1, source_target_pairs={{0,1},{1,0},{2,3},{3,2},{4,5},{5,4},{6,7},{7,6},{8,9},{9,8},{10,11... | collective-permute-start | bytes 98312 | tf_op jit(solution)/shard_map/ppermute | solution.py:485
  12.0 1.1 %constant_dynamic-update-slice_fusion.6 = bf16[3299,512]{1,0:T(8,128)(2,1)S(1)} fusion(bf16[512,512]{1,0:T(8,128)(2,1)} %param.18), kind=kLoop, calls=%fused_computation.6 | loop fusion | bytes 1048576
  13.1 1.1 %constant_dynamic-update-slice_fusion.5 = bf16[3299,512]{1,0:T(8,128)(2,1)S(1)} fusion(bf16[3299,512]{1,0:T(8,128)(2,1)S(1)} %constant_dynamic-update-slice_fusion.6, bf16[512,512]{1,0:T(8,128)(2,1)} %param.19), kind=kLoop, calls=%fused_computation.5 | loop fusion | bytes 1048576
  14.1 1.1 %constant_dynamic-update-slice_fusion.4 = bf16[3299,512]{1,0:T(8,128)(2,1)S(1)} fusion(bf16[3299,512]{1,0:T(8,128)(2,1)S(1)} %constant_dynamic-update-slice_fusion.5, bf16[512,512]{1,0:T(8,128)(2,1)} %param.20), kind=kLoop, calls=%fused_computation.4 | loop fusion | bytes 1048576
  15.4 0.6 %shard_map.177.recv_pre = f32[1024,512]{1,0:T(8,128)S(1)} custom-call(bf16[32,512]{1,0:T(8,128)(2,1)S(1)} %collective-permute-done.2.near.mesh_near, bf16[32,512]{1,0:T(8,128)(2,1)S(1)} %collective-permute-done.3.far.mesh_far, bf16[32,512]{1,0:T(8,128)(2,1)S(1)} %copy-done.1, bf16[1024,128]{1,0:T(8,128)(2,1)S(1)} %get-tuple-element.56.recv_hits, ...), custom_call_target="tpu_custom_call" | custom-call | tf_op jit(solution)/shard_map/pallas_call | solution.py:399
  16.1 0.9 %shard_map.176.rows = bf16[1024,227]{1,0:T(8,128)(2,1)S(1)} custom-call(bf16[3,227,360]{2,1,0:T(8,128)(2,1)S(1)} %collective-permute-done.1.halo, bf16[1024,1152]{1,0:T(8,128)(2,1)S(1)} %get-tuple-element.52.hits, bf16[1024,227]{1,0:T(8,128)(2,1)S(1)} %get-tuple-element.54.rows), custom_call_target="tpu_custom_call" | custom-call | tf_op jit(solution)/shard_map/pallas_call | solution.py:399
  17.4 3.0 %shard_map.178 = (bf16[1024,512]{1,0:T(8,128)(2,1)S(1)}, bf16[1024,512]{1,0:T(8,128)(2,1)S(1)}, f32[64,512]{1,0:T(8,128)S(1)}, bf16[32,512]{1,0:T(8,128)(2,1)S(1)}, bf16[32,512]{1,0:T(8,128)(2,1)S(1)}) custom-call(bf16[3,227,360]{2,1,0:T(8,128)(2,1)S(1)} %collective-permute-done.near, bf16[1024,1152]{1,0:T(8,128)(2,1)S(1)} %get-tuple-element.50.near_hits, ...), custom_call_target="tpu_custom_call" | custom-call | tf_op jit(solution)/shard_map/pallas_call | solution.py:399
  20.4 1.6 %collective-permute-start.5 = (bf16[32,512]{1,0:T(8,128)(2,1)S(1)}, bf16[32,512]{1,0:T(8,128)(2,1)S(1)}, u32[]{:S(2)}, u32[]{:S(2)}) collective-permute-start(bf16[32,512]{1,0:T(8,128)(2,1)S(1)} %get-tuple-element.59), channel_id=1, source_target_pairs={{0,3},{1,2},{2,1},{3,0},{4,7},{5,6},{6,5},{7,4},{8,11},{9,10},{10,... | collective-permute-start | bytes 98312 | tf_op jit(solution)/shard_map/ppermute | solution.py:511
  22.1 1.8 %collective-permute-done.5.far = bf16[32,512]{1,0:T(8,128)(2,1)S(1)} collective-permute-done((bf16[32,512]{1,0:T(8,128)(2,1)S(1)}, bf16[32,512]{1,0:T(8,128)(2,1)S(1)}, u32[]{:S(2)}, u32[]{:S(2)}) %collective-permute-start.5) | collective-permute-done | bytes 32800 | tf_op jit(solution)/shard_map/ppermute | solution.py:511
  24.1 1.8 %collective-permute-start.7 = (bf16[64,512]{1,0:T(8,128)(2,1)S(1)}, bf16[64,512]{1,0:T(8,128)(2,1)S(1)}, u32[]{:S(2)}, u32[]{:S(2)}) collective-permute-start(bf16[64,512]{1,0:T(8,128)(2,1)S(1)} %get-tuple-element.60.own.nodes), channel_id=1, source_target_pairs={{0,4},{4,0},{8,12},{12,8},{1,5},{5,1},{9,13},{13,9},{2,6},{6,2},{1... | collective-permute-start | bytes 196616 | tf_op jit(solution)/shard_map/ppermute | solution.py:518
  26.1 1.5 %collective-permute-start.9 = (bf16[64,512]{1,0:T(8,128)(2,1)S(1)}, bf16[64,512]{1,0:T(8,128)(2,1)S(1)}, u32[]{:S(2)}, u32[]{:S(2)}) collective-permute-start(bf16[64,512]{1,0:T(8,128)(2,1)S(1)} %get-tuple-element.60.own.nodes), channel_id=1, source_target_pairs={{0,2},{2,0},{1,3},{3,1},{4,6},{6,4},{5,7},{7,5},{8,10},{10,8},{9,1... | collective-permute-start | bytes 196616 | tf_op jit(solution)/shard_map/ppermute | solution.py:431
  27.5 0.7 %shard_map.180.own_pre = f32[512,512]{1,0:T(8,128)S(1)} custom-call(bf16[512,128]{1,0:T(8,128)(2,1)S(1)} %get-tuple-element.48.own_hits, bf16[512,64]{1,0:T(8,128)(2,1)S(1)} %get-tuple-element.49.to_hits, bf16[64,512]{1,0:T(8,128)(2,1)S(1)} %get-tuple-element.60.own.nodes, bf16[3299,512]{1,0:T(8,128)(2,1)S(1)} %constant_dynamic-update-slice_fusion.stack), custom_call_target="tpu_custom_call" | custom-call | tf_op jit(solution)/shard_map/pallas_call | solution.py:399
  28.6 1.6 %shard_map.181 = (bf16[32,512]{1,0:T(8,128)(2,1)}, f32[192,512]{1,0:T(8,128)S(1)}, bf16[32,512]{1,0:T(8,128)(2,1)S(1)}, bf16[64,512]{1,0:T(8,128)(2,1)S(1)}, bf16[64,512]{1,0:T(8,128)(2,1)S(1)}) custom-call(f32[512,512]{1,0:T(8,128)S(1)} %shard_map.180.own_pre, bf16[512,256]{1,0:T(8,128)(2,1)S(1)} %get-tuple-element.61.outer_hits, ...), custom_call_target="tpu_custom_call" | custom-call | tf_op jit(solution)/shard_map/pallas_call | solution.py:399
  30.3 2.3 %collective-permute-start.8 = (bf16[64,512]{1,0:T(8,128)(2,1)S(1)}, bf16[64,512]{1,0:T(8,128)(2,1)S(1)}, u32[]{:S(2)}, u32[]{:S(2)}) collective-permute-start(bf16[64,512]{1,0:T(8,128)(2,1)S(1)} %get-tuple-element.66), channel_id=1, source_target_pairs={{0,4},{4,0},{8,12},{12,8},{1,5},{5,1},{9,13},{13,9},{2,6},{6,2},{1... | collective-permute-start | bytes 196616 | tf_op jit(solution)/shard_map/ppermute | solution.py:538
  33.0 1.9 %collective-permute-done.8.near = bf16[64,512]{1,0:T(8,128)(2,1)S(1)} collective-permute-done((bf16[64,512]{1,0:T(8,128)(2,1)S(1)}, bf16[64,512]{1,0:T(8,128)(2,1)S(1)}, u32[]{:S(2)}, u32[]{:S(2)}) %collective-permute-start.8) | collective-permute-done | bytes 65568 | tf_op jit(solution)/shard_map/ppermute | solution.py:538
  34.9 1.6 %collective-permute-start.12 = (bf16[48,512]{1,0:T(8,128)(2,1)S(1)}, bf16[48,512]{1,0:T(8,128)(2,1)S(1)}, u32[]{:S(2)}, u32[]{:S(2)}) collective-permute-start(bf16[48,512]{1,0:T(8,128)(2,1)S(1)} %get-tuple-element.74), channel_id=1, source_target_pairs={{0,3},{1,2},{2,1},{3,0},{4,7},{5,6},{6,5},{7,4},{8,11},{9,10},{10,... | collective-permute-start | bytes 147464 | tf_op jit(solution)/shard_map/ppermute | solution.py:552
  36.5 2.0 %collective-permute-done.12.far = bf16[48,512]{1,0:T(8,128)(2,1)S(1)} collective-permute-done((bf16[48,512]{1,0:T(8,128)(2,1)S(1)}, bf16[48,512]{1,0:T(8,128)(2,1)S(1)}, u32[]{:S(2)}, u32[]{:S(2)}) %collective-permute-start.12) | collective-permute-done | bytes 49184 | tf_op jit(solution)/shard_map/ppermute | solution.py:552
  38.5 1.1 %shard_map.184 = (bf16[1,1,512,128]{3,2,1,0:T(8,128)(2,1)S(1)}, bf16[128,512]{1,0:T(8,128)(2,1)S(1)}, bf16[2,64,128]{2,1,0:T(8,128)(2,1)S(1)}) custom-call(bf16[1024,128]{1,0:T(8,128)(2,1)S(1)} %get-tuple-element.56.recv_hits, f32[64,512]{1,0:T(8,128)S(1)} %get-tuple-element.72.part, bf16[48,512]{1,0:T(8,128)(2,1)S(1)} %collective-permute-done.11.near, ...), custom_call_target="tpu_custom_call" | custom-call | tf_op jit(solution)/shard_map/pallas_call | solution.py:399
  40.1 0.7 %shard_map.185 = (f32[1,512,128]{2,1,0:T(8,128)S(1)}, bf16[1,512,128]{2,1,0:T(8,128)(2,1)S(1)}) custom-call(bf16[1024,128]{1,0:T(8,128)(2,1)S(1)} %get-tuple-element.56.recv_hits, bf16[128,512]{1,0:T(8,128)(2,1)S(1)} %get-tuple-element.78.back, bf16[1024,512]{1,0:T(8,128)(2,1)S(1)} %get-tuple-element.77.edge_slope, ...), custom_call_target="tpu_custom_call" | custom-call | tf_op jit(solution)/shard_map/pallas_call | solution.py:399
  41.1 1.6 %collective-permute-start.15 = (bf16[320,128]{1,0:T(8,128)(2,1)S(1)}, bf16[320,128]{1,0:T(8,128)(2,1)S(1)}, u32[]{:S(2)}, u32[]{:S(2)}) collective-permute-start(bf16[320,128]{1,0:T(8,128)(2,1)S(1)} %bitcast.10), channel_id=1, source_target_pairs={{0,2},{2,0},{1,3},{3,1},{4,6},{6,4},{5,7},{7,5},{8,10},{10,8},{9,1... | collective-permute-start | bytes 245768 | tf_op jit(solution)/shard_map/ppermute | solution.py:431
  43.2 0.6 %shard_map.186.kept = f32[512,128]{1,0:T(8,128)S(1)} custom-call(bf16[1024,128]{1,0:T(8,128)(2,1)S(1)} %get-tuple-element.56.recv_hits, bf16[128,512]{1,0:T(8,128)(2,1)S(1)} %get-tuple-element.78.back, bf16[1024,512]{1,0:T(8,128)(2,1)S(1)} %get-tuple-element.77.edge_slope, bf16[512,1024]{1,0:T(8,128)(2,1)S(1)} %get-tuple-element.76.senders, ...), custom_call_target="tpu_custom_call" | custom-call | tf_op jit(solution)/shard_map/pallas_call | solution.py:399
  43.9 2.6 %collective-permute-done.15.refs_0_ = bf16[320,128]{1,0:T(8,128)(2,1)S(1)} collective-permute-done((bf16[320,128]{1,0:T(8,128)(2,1)S(1)}, bf16[320,128]{1,0:T(8,128)(2,1)S(1)}, u32[]{:S(2)}, u32[]{:S(2)}) %collective-permute-start.15) | collective-permute-done | bytes 81952 | tf_op jit(solution)/shard_map/ppermute | solution.py:431
  46.7 3.0 %collective-permute-start.16 = (bf16[2,128,128]{2,1,0:T(8,128)(2,1)S(1)}, bf16[2,128,128]{2,1,0:T(8,128)(2,1)S(1)}, u32[]{:S(2)}, u32[]{:S(2)}) collective-permute-start(bf16[2,128,128]{2,1,0:T(8,128)(2,1)S(1)} %get-tuple-element.85), channel_id=1, source_target_pairs={{0,12},{4,8},{8,4},{12,0},{1,13},{5,9},{9,5},{13,1},{2,14},{6,10},... | collective-permute-start | bytes 196616 | tf_op jit(solution)/shard_map/ppermute | solution.py:436
  49.7 0.6 %collective-permute-start.17 = (bf16[2,128,128]{2,1,0:T(8,128)(2,1)S(1)}, bf16[2,128,128]{2,1,0:T(8,128)(2,1)S(1)}, u32[]{:S(2)}, u32[]{:S(2)}) collective-permute-start(bf16[2,128,128]{2,1,0:T(8,128)(2,1)S(1)} %get-tuple-element.86), channel_id=1, source_target_pairs={{0,8},{4,12},{8,0},{12,4},{1,9},{5,13},{9,1},{13,5},{2,10},{6,14},... | collective-permute-start | bytes 196616 | tf_op jit(solution)/shard_map/ppermute | solution.py:436
  50.4 0.9 %collective-permute-start.19 = (bf16[2,128,128]{2,1,0:T(8,128)(2,1)S(1)}, bf16[2,128,128]{2,1,0:T(8,128)(2,1)S(1)}, u32[]{:S(2)}, u32[]{:S(2)}) collective-permute-start(bf16[2,128,128]{2,1,0:T(8,128)(2,1)S(1)} %get-tuple-element.89), channel_id=1, source_target_pairs={{0,4},{4,0},{8,12},{12,8},{1,5},{5,1},{9,13},{13,9},{2,6},{6,2},{1... | collective-permute-start | bytes 196616 | tf_op jit(solution)/shard_map/ppermute | solution.py:436
  51.3 2.1 %collective-permute-done.16.refs_0_ = bf16[2,128,128]{2,1,0:T(8,128)(2,1)S(1)} collective-permute-done((bf16[2,128,128]{2,1,0:T(8,128)(2,1)S(1)}, bf16[2,128,128]{2,1,0:T(8,128)(2,1)S(1)}, u32[]{:S(2)}, u32[]{:S(2)}) %collective-permute-start.16) | collective-permute-done | bytes 65568 | tf_op jit(solution)/shard_map/ppermute | solution.py:436
  53.4 2.7 %collective-permute-done.17.refs_1_ = bf16[2,128,128]{2,1,0:T(8,128)(2,1)S(1)} collective-permute-done((bf16[2,128,128]{2,1,0:T(8,128)(2,1)S(1)}, bf16[2,128,128]{2,1,0:T(8,128)(2,1)S(1)}, u32[]{:S(2)}, u32[]{:S(2)}) %collective-permute-start.17) | collective-permute-done | bytes 65568 | tf_op jit(solution)/shard_map/ppermute | solution.py:436
  56.1 0.7 %shard_map.190 = (f32[128,128]{1,0:T(8,128)}, f32[128,128]{1,0:T(8,128)}) custom-call(bf16[2,128,128]{2,1,0:T(8,128)(2,1)S(1)} %collective-permute-done.16.refs_0_, bf16[2,128,128]{2,1,0:T(8,128)(2,1)S(1)} %collective-permute-done.17.refs_1_, bf16[2,128,128]{2,1,0:T(8,128)(2,1)S(1)} %collective-permute-done.19.refs_2_, ...), custom_call_target="tpu_custom_call" | custom-call | tf_op jit(solution)/shard_map/pallas_call | solution.py:399
  (46 shorter events, 4.5 us)
Async XLA Ops:
  0.6 15.4 %collective-permute-start.1 = (bf16[3,227,360]{2,1,0:T(8,128)(2,1)}, bf16[3,227,360]{2,1,0:T(8,128)(2,1)S(1)}, u32[]{:S(2)}, u32[]{:S(2)}) collective-permute-start(bf16[3,227,360]{2,1,0:T(8,128)(2,1)} %bitcast.5), channel_id=1, source_target_pairs={{0,1},{1,0},{2,3},{3,2},{4,8},{5,9},{6,10},{7,11},{8,4},{9,5},{10,... | collective-permute-start | bytes 1470968 | tf_op jit(solution)/shard_map/ppermute | solution.py:460
  1.2 16.3 %collective-permute-start = (bf16[3,227,360]{2,1,0:T(8,128)(2,1)}, bf16[3,227,360]{2,1,0:T(8,128)(2,1)S(1)}, u32[]{:S(2)}, u32[]{:S(2)}) collective-permute-start(bf16[3,227,360]{2,1,0:T(8,128)(2,1)} %bitcast.6), channel_id=1, source_target_pairs={{0,4},{4,0},{8,12},{12,8},{1,5},{5,1},{9,13},{13,9},{2,6},{6,2},{1... | collective-permute-start | bytes 1470968 | tf_op jit(solution)/shard_map/ppermute | solution.py:459
  7.3 1.0 %copy-start = (bf16[3,360,227]{1,2,0:T(8,128)(2,1)S(1)}, bf16[3,360,227]{1,2,0:T(8,128)(2,1)}, u32[]{:S(2)}) copy-start(bf16[3,360,227]{1,2,0:T(8,128)(2,1)} %param.16) | copy-start | bytes 1470964
  8.4 6.8 %copy-start.3 = (bf16[512,512]{1,0:T(8,128)(2,1)S(1)}, bf16[512,512]{1,0:T(8,128)(2,1)}, u32[]{:S(2)}) copy-start(bf16[512,512]{1,0:T(8,128)(2,1)} %param.21) | copy-start | bytes 1572868
  8.4 6.9 %copy-start.4 = (bf16[512,512]{1,0:T(8,128)(2,1)S(1)}, bf16[512,512]{1,0:T(8,128)(2,1)}, u32[]{:S(2)}) copy-start(bf16[512,512]{1,0:T(8,128)(2,1)} %param.22) | copy-start | bytes 1572868
  8.4 6.9 %copy-start.5 = (bf16[512,512]{1,0:T(8,128)(2,1)S(1)}, bf16[512,512]{1,0:T(8,128)(2,1)}, u32[]{:S(2)}) copy-start(bf16[512,512]{1,0:T(8,128)(2,1)} %param.23) | copy-start | bytes 1572868
  8.4 7.0 %copy-start.6 = (bf16[227,512]{1,0:T(8,128)(2,1)S(1)}, bf16[227,512]{1,0:T(8,128)(2,1)}, u32[]{:S(2)}) copy-start(bf16[227,512]{1,0:T(8,128)(2,1)} %param.17) | copy-start | bytes 697348
  10.3 5.1 %copy-start.1 = (bf16[32,512]{1,0:T(8,128)(2,1)S(1)}, bf16[32,512]{1,0:T(8,128)(2,1)}, u32[]{:S(2)}) copy-start(bf16[32,512]{1,0:T(8,128)(2,1)} %mesh_in.3) | copy-start | bytes 98308
  10.3 5.1 %collective-permute-start.3 = (bf16[32,512]{1,0:T(8,128)(2,1)}, bf16[32,512]{1,0:T(8,128)(2,1)S(1)}, u32[]{:S(2)}, u32[]{:S(2)}) collective-permute-start(bf16[32,512]{1,0:T(8,128)(2,1)} %mesh_in.3), channel_id=1, source_target_pairs={{0,3},{1,2},{2,1},{3,0},{4,7},{5,6},{6,5},{7,4},{8,11},{9,10},{10,... | collective-permute-start | bytes 98312 | tf_op jit(solution)/shard_map/ppermute | solution.py:486
  10.7 4.7 %collective-permute-start.2 = (bf16[32,512]{1,0:T(8,128)(2,1)}, bf16[32,512]{1,0:T(8,128)(2,1)S(1)}, u32[]{:S(2)}, u32[]{:S(2)}) collective-permute-start(bf16[32,512]{1,0:T(8,128)(2,1)} %mesh_in.3), channel_id=1, source_target_pairs={{0,1},{1,0},{2,3},{3,2},{4,5},{5,4},{6,7},{7,6},{8,9},{9,8},{10,11... | collective-permute-start | bytes 98312 | tf_op jit(solution)/shard_map/ppermute | solution.py:485
  20.4 1.7 %collective-permute-start.4 = (bf16[32,512]{1,0:T(8,128)(2,1)S(1)}, bf16[32,512]{1,0:T(8,128)(2,1)S(1)}, u32[]{:S(2)}, u32[]{:S(2)}) collective-permute-start(bf16[32,512]{1,0:T(8,128)(2,1)S(1)} %get-tuple-element.58), channel_id=1, source_target_pairs={{0,1},{1,0},{2,3},{3,2},{4,5},{5,4},{6,7},{7,6},{8,9},{9,8},{10,11... | collective-permute-start | bytes 98312 | tf_op jit(solution)/shard_map/ppermute | solution.py:512
  20.4 3.4 %collective-permute-start.5 = (bf16[32,512]{1,0:T(8,128)(2,1)S(1)}, bf16[32,512]{1,0:T(8,128)(2,1)S(1)}, u32[]{:S(2)}, u32[]{:S(2)}) collective-permute-start(bf16[32,512]{1,0:T(8,128)(2,1)S(1)} %get-tuple-element.59), channel_id=1, source_target_pairs={{0,3},{1,2},{2,1},{3,0},{4,7},{5,6},{6,5},{7,4},{8,11},{9,10},{10,... | collective-permute-start | bytes 98312 | tf_op jit(solution)/shard_map/ppermute | solution.py:511
  23.8 4.8 %copy-start.2 = (bf16[32,512]{1,0:T(8,128)(2,1)S(1)}, bf16[32,512]{1,0:T(8,128)(2,1)}, u32[]{:S(2)}) copy-start(bf16[32,512]{1,0:T(8,128)(2,1)} %d_out.3) | copy-start | bytes 98308
  24.1 4.5 %collective-permute-start.7 = (bf16[64,512]{1,0:T(8,128)(2,1)S(1)}, bf16[64,512]{1,0:T(8,128)(2,1)S(1)}, u32[]{:S(2)}, u32[]{:S(2)}) collective-permute-start(bf16[64,512]{1,0:T(8,128)(2,1)S(1)} %get-tuple-element.60.own.nodes), channel_id=1, source_target_pairs={{0,4},{4,0},{8,12},{12,8},{1,5},{5,1},{9,13},{13,9},{2,6},{6,2},{1... | collective-permute-start | bytes 196616 | tf_op jit(solution)/shard_map/ppermute | solution.py:518
  25.9 2.7 %collective-permute-start.6 = (bf16[64,512]{1,0:T(8,128)(2,1)S(1)}, bf16[64,512]{1,0:T(8,128)(2,1)S(1)}, u32[]{:S(2)}, u32[]{:S(2)}) collective-permute-start(bf16[64,512]{1,0:T(8,128)(2,1)S(1)} %get-tuple-element.60.own.nodes), channel_id=1, source_target_pairs={{0,1},{1,0},{2,3},{3,2},{4,8},{5,9},{6,10},{7,11},{8,4},{9,5},{10,... | collective-permute-start | bytes 196616 | tf_op jit(solution)/shard_map/ppermute | solution.py:519
  26.1 6.9 %collective-permute-start.9 = (bf16[64,512]{1,0:T(8,128)(2,1)S(1)}, bf16[64,512]{1,0:T(8,128)(2,1)S(1)}, u32[]{:S(2)}, u32[]{:S(2)}) collective-permute-start(bf16[64,512]{1,0:T(8,128)(2,1)S(1)} %get-tuple-element.60.own.nodes), channel_id=1, source_target_pairs={{0,2},{2,0},{1,3},{3,1},{4,6},{6,4},{5,7},{7,5},{8,10},{10,8},{9,1... | collective-permute-start | bytes 196616 | tf_op jit(solution)/shard_map/ppermute | solution.py:431
  30.3 4.6 %collective-permute-start.8 = (bf16[64,512]{1,0:T(8,128)(2,1)S(1)}, bf16[64,512]{1,0:T(8,128)(2,1)S(1)}, u32[]{:S(2)}, u32[]{:S(2)}) collective-permute-start(bf16[64,512]{1,0:T(8,128)(2,1)S(1)} %get-tuple-element.66), channel_id=1, source_target_pairs={{0,4},{4,0},{8,12},{12,8},{1,5},{5,1},{9,13},{13,9},{2,6},{6,2},{1... | collective-permute-start | bytes 196616 | tf_op jit(solution)/shard_map/ppermute | solution.py:538
  32.6 2.2 %collective-permute-start.10 = (bf16[64,512]{1,0:T(8,128)(2,1)S(1)}, bf16[64,512]{1,0:T(8,128)(2,1)S(1)}, u32[]{:S(2)}, u32[]{:S(2)}) collective-permute-start(bf16[64,512]{1,0:T(8,128)(2,1)S(1)} %get-tuple-element.68), channel_id=1, source_target_pairs={{0,1},{1,0},{2,3},{3,2},{4,8},{5,9},{6,10},{7,11},{8,4},{9,5},{10,... | collective-permute-start | bytes 196616 | tf_op jit(solution)/shard_map/ppermute | solution.py:539
  34.9 1.7 %collective-permute-start.11 = (bf16[48,512]{1,0:T(8,128)(2,1)S(1)}, bf16[48,512]{1,0:T(8,128)(2,1)S(1)}, u32[]{:S(2)}, u32[]{:S(2)}) collective-permute-start(bf16[48,512]{1,0:T(8,128)(2,1)S(1)} %get-tuple-element.73), channel_id=1, source_target_pairs={{0,1},{1,0},{2,3},{3,2},{4,5},{5,4},{6,7},{7,6},{8,9},{9,8},{10,11... | collective-permute-start | bytes 147464 | tf_op jit(solution)/shard_map/ppermute | solution.py:553
  34.9 3.6 %collective-permute-start.12 = (bf16[48,512]{1,0:T(8,128)(2,1)S(1)}, bf16[48,512]{1,0:T(8,128)(2,1)S(1)}, u32[]{:S(2)}, u32[]{:S(2)}) collective-permute-start(bf16[48,512]{1,0:T(8,128)(2,1)S(1)} %get-tuple-element.74), channel_id=1, source_target_pairs={{0,3},{1,2},{2,1},{3,0},{4,7},{5,6},{6,5},{7,4},{8,11},{9,10},{10,... | collective-permute-start | bytes 147464 | tf_op jit(solution)/shard_map/ppermute | solution.py:552
  39.6 1.5 %collective-permute-start.14 = (bf16[1,512,128]{2,1,0:T(8,128)(2,1)S(1)}, bf16[1,512,128]{2,1,0:T(8,128)(2,1)S(1)}, u32[]{:S(2)}, u32[]{:S(2)}) collective-permute-start(bf16[1,512,128]{2,1,0:T(8,128)(2,1)S(1)} %bitcast.8), channel_id=1, source_target_pairs={{0,1},{1,0},{2,3},{3,2},{4,5},{5,4},{6,7},{7,6},{8,9},{9,8},{10,11... | collective-permute-start | bytes 393224 | tf_op jit(solution)/shard_map/ppermute | solution.py:431
  40.8 2.4 %collective-permute-start.13 = (bf16[512,128]{1,0:T(8,128)(2,1)S(1)}, bf16[512,128]{1,0:T(8,128)(2,1)S(1)}, u32[]{:S(2)}, u32[]{:S(2)}) collective-permute-start(bf16[512,128]{1,0:T(8,128)(2,1)S(1)} %bitcast.9), channel_id=1, source_target_pairs={{0,1},{1,0},{2,3},{3,2},{4,5},{5,4},{6,7},{7,6},{8,9},{9,8},{10,11... | collective-permute-start | bytes 393224 | tf_op jit(solution)/shard_map/ppermute | solution.py:431
  41.1 5.3 %collective-permute-start.15 = (bf16[320,128]{1,0:T(8,128)(2,1)S(1)}, bf16[320,128]{1,0:T(8,128)(2,1)S(1)}, u32[]{:S(2)}, u32[]{:S(2)}) collective-permute-start(bf16[320,128]{1,0:T(8,128)(2,1)S(1)} %bitcast.10), channel_id=1, source_target_pairs={{0,2},{2,0},{1,3},{3,1},{4,6},{6,4},{5,7},{7,5},{8,10},{10,8},{9,1... | collective-permute-start | bytes 245768 | tf_op jit(solution)/shard_map/ppermute | solution.py:431
  42.7 7.7 %collective-permute-start.18 = (bf16[256,128]{1,0:T(8,128)(2,1)S(1)}, bf16[256,128]{1,0:T(8,128)(2,1)S(1)}, u32[]{:S(2)}, u32[]{:S(2)}) collective-permute-start(bf16[256,128]{1,0:T(8,128)(2,1)S(1)} %bitcast.11), channel_id=1, source_target_pairs={{0,2},{2,0},{1,3},{3,1},{4,6},{6,4},{5,7},{7,5},{8,10},{10,8},{9,1... | collective-permute-start | bytes 196616 | tf_op jit(solution)/shard_map/ppermute | solution.py:431
  46.7 6.6 %collective-permute-start.16 = (bf16[2,128,128]{2,1,0:T(8,128)(2,1)S(1)}, bf16[2,128,128]{2,1,0:T(8,128)(2,1)S(1)}, u32[]{:S(2)}, u32[]{:S(2)}) collective-permute-start(bf16[2,128,128]{2,1,0:T(8,128)(2,1)S(1)} %get-tuple-element.85), channel_id=1, source_target_pairs={{0,12},{4,8},{8,4},{12,0},{1,13},{5,9},{9,5},{13,1},{2,14},{6,10},... | collective-permute-start | bytes 196616 | tf_op jit(solution)/shard_map/ppermute | solution.py:436
  49.7 6.4 %collective-permute-start.17 = (bf16[2,128,128]{2,1,0:T(8,128)(2,1)S(1)}, bf16[2,128,128]{2,1,0:T(8,128)(2,1)S(1)}, u32[]{:S(2)}, u32[]{:S(2)}) collective-permute-start(bf16[2,128,128]{2,1,0:T(8,128)(2,1)S(1)} %get-tuple-element.86), channel_id=1, source_target_pairs={{0,8},{4,12},{8,0},{12,4},{1,9},{5,13},{9,1},{13,5},{2,10},{6,14},... | collective-permute-start | bytes 196616 | tf_op jit(solution)/shard_map/ppermute | solution.py:436
  50.4 5.7 %collective-permute-start.19 = (bf16[2,128,128]{2,1,0:T(8,128)(2,1)S(1)}, bf16[2,128,128]{2,1,0:T(8,128)(2,1)S(1)}, u32[]{:S(2)}, u32[]{:S(2)}) collective-permute-start(bf16[2,128,128]{2,1,0:T(8,128)(2,1)S(1)} %get-tuple-element.89), channel_id=1, source_target_pairs={{0,4},{4,0},{8,12},{12,8},{1,5},{5,1},{9,13},{13,9},{2,6},{6,2},{1... | collective-permute-start | bytes 196616 | tf_op jit(solution)/shard_map/ppermute | solution.py:436

commit v16 on v15

--- a/solution.py
+++ b/solution.py
@@ -165,7 +165,7 @@
 ):
     half = recv_rows.shape[0] // 2
     fill(wide, near, wide.shape[1] // near.shape[0], 0)
-    block = rows.shape[0] // 4
+    block = rows.shape[0] // 2
     sums = None
     for first in range(0, rows.shape[0], block):
         part_of = slice(first, first + block)
@@ -537,7 +537,6 @@
     )
     from_near = lax.ppermute(to_near, "band", band_near)
     from_far = lax.ppermute(to_far, whole, band_far)
-    from_near, *dom_nodes = lax.optimization_barrier((from_near, *dom_nodes))
     home, senders = call(
         home_kernel,
         [((node_count, latent), F32), ((latent, edges), BF16)],
@@ -552,6 +551,7 @@
     from_far = lax.ppermute(to_far, around, ring_far)
     from_near = lax.ppermute(to_near, around, ring_near)
 
+    from_near, *dom_nodes = lax.optimization_barrier((from_near, *dom_nodes))
     cols = latent // sectors
     rows = latent // bands
     sends, back, total = call(

time: 57.1 us -> 57.1 us (level)
    ppermute x1, waiting for transfers between devices: 0.38 us -> 1.86 us  [on_device(): one_near = lax.ppermute(mesh_one, 'band', band_near)]
    ppermute x1, waiting for transfers between devices: 1.87 us -> 0.39 us  [on_device(): from_near = lax.ppermute(to_near, 'band', band_near)]
  transfers between devices with their start and end apart: 20 -> 20, of which waited for: 9 -> 10; matrix products, arithmetic and copies ran while one was open for 7% -> 7% of each run, Pallas kernels for 14% -> 11%
where the time goes in v16:
time: 57.1 us; the launch traced here: 56.7 us
  starting transfers between devices  22.7 us (40%)
  waiting for transfers between devices  14 us (25%)
  Pallas kernels  12.7 us (22%)
  local copies, waits for them, and re-layouts  4.43 us (8%)
  between operations  2.17 us (4%)
  other arithmetic  0.74 us (1%)
    pallas_call x16, Pallas kernels, call(): pl.pallas_call(kernel, out_shape=[jax.ShapeDtypeStruct(shape, dtype) for...  12.7 us
    ppermute x3, waiting for transfers between devices, over_band(): return lax.ppermute(x, 'band', [(b, b ^ partner) for b in range(count)])  4.83 us
    ppermute x3, starting transfers between devices, over_band(): return lax.ppermute(x, 'band', [(b, b ^ partner) for b in range(count)])  4.52 us
    unnamed x20, local copies, waits for them, and re-layouts  4.41 us
    ppermute x5, starting transfers between devices, shifted(): lax.ppermute(x, axis, [(i, (i + shift) % count) for i in range(count)])  4.23 us
    ppermute x1, starting transfers between devices, on_device(): raw_near = lax.ppermute(grid, 'band', band_near)  4.15 us
    ppermute x5, waiting for transfers between devices, shifted(): lax.ppermute(x, axis, [(i, (i + shift) % count) for i in range(count)])  3.29 us
    ppermute x2, waiting for transfers between devices, on_device(): from_far = lax.ppermute(to_far, around, ring_far)  3.23 us
  transfers between devices with their start and end apart: 20, of which 10 were waited for; matrix products, arithmetic and copies ran while one was open for 7% of the time, Pallas kernels for 11%

profile of v16, /device:TPU:0, one launch (start us, length us, event | category | flops | bytes accessed | tf_op | source)
XLA Modules:
  0.0 56.7 jit_solution(4548628794593851561)
XLA Ops:
  1.2 4.1 %collective-permute-start = (bf16[3,227,360]{2,1,0:T(8,128)(2,1)}, bf16[3,227,360]{2,1,0:T(8,128)(2,1)S(1)}, u32[]{:S(2)}, u32[]{:S(2)}) collective-permute-start(bf16[3,227,360]{2,1,0:T(8,128)(2,1)} %bitcast.6), channel_id=1, source_target_pairs={{0,4},{4,0},{8,12},{12,8},{1,5},{5,1},{9,13},{13,9},{2,6},{6,2},{1... | collective-permute-start | bytes 1470968 | tf_op jit(solution)/shard_map/ppermute | solution.py:459
  6.6 0.7 %pad_add_fusion.indices = s32[1,1,3072]{2,1,0:T(1,128)S(1)} fusion(s32[1,1,512]{2,1,0:T(1,128)} %param.30, s32[1,1,512]{2,1,0:T(1,128)} %param.29, s32[1,1,1024]{2,1,0:T(1,128)} %param.27, s32[1,1,1024]{2,1,0:T(1,128)} %param.26), kind=kLoop, calls=%fused_computation.7 | loop fusion | flops 9216 | bytes 24576 | tf_op jit(solution)/shard_map/concatenate | solution.py:463
  7.3 1.0 %copy-done = bf16[3,360,227]{1,2,0:T(8,128)(2,1)S(1)} copy-done((bf16[3,360,227]{1,2,0:T(8,128)(2,1)S(1)}, bf16[3,360,227]{1,2,0:T(8,128)(2,1)}, u32[]{:S(2)}) %copy-start) | copy-done | bytes 490344
  8.4 1.9 %shard_map.175 = (bf16[1024,227]{1,0:T(8,128)(2,1)S(1)}, bf16[1024,128]{1,0:T(8,128)(2,1)S(1)}, bf16[64,1024]{1,0:T(8,128)(2,1)S(1)}, bf16[512,128]{1,0:T(8,128)...) custom-call(s32[1,1]{1,0:T(1,128)S(6)} %copy.25.count, ...), custom_call_target="tpu_custom_call" | custom-call | tf_op jit(solution)/shard_map/pallas_call | solution.py:399
  10.7 1.2 %collective-permute-start.2 = (bf16[32,512]{1,0:T(8,128)(2,1)}, bf16[32,512]{1,0:T(8,128)(2,1)S(1)}, u32[]{:S(2)}, u32[]{:S(2)}) collective-permute-start(bf16[32,512]{1,0:T(8,128)(2,1)} %mesh_in.3), channel_id=1, source_target_pairs={{0,1},{1,0},{2,3},{3,2},{4,5},{5,4},{6,7},{7,6},{8,9},{9,8},{10,11... | collective-permute-start | bytes 98312 | tf_op jit(solution)/shard_map/ppermute | solution.py:485
  12.0 1.1 %constant_dynamic-update-slice_fusion.6 = bf16[3299,512]{1,0:T(8,128)(2,1)S(1)} fusion(bf16[512,512]{1,0:T(8,128)(2,1)} %param.18), kind=kLoop, calls=%fused_computation.6 | loop fusion | bytes 1048576
  13.1 1.1 %constant_dynamic-update-slice_fusion.5 = bf16[3299,512]{1,0:T(8,128)(2,1)S(1)} fusion(bf16[3299,512]{1,0:T(8,128)(2,1)S(1)} %constant_dynamic-update-slice_fusion.6, bf16[512,512]{1,0:T(8,128)(2,1)} %param.19), kind=kLoop, calls=%fused_computation.5 | loop fusion | bytes 1048576
  14.1 1.1 %constant_dynamic-update-slice_fusion.4 = bf16[3299,512]{1,0:T(8,128)(2,1)S(1)} fusion(bf16[3299,512]{1,0:T(8,128)(2,1)S(1)} %constant_dynamic-update-slice_fusion.5, bf16[512,512]{1,0:T(8,128)(2,1)} %param.20), kind=kLoop, calls=%fused_computation.4 | loop fusion | bytes 1048576
  15.4 0.6 %shard_map.177.recv_pre = f32[1024,512]{1,0:T(8,128)S(1)} custom-call(bf16[32,512]{1,0:T(8,128)(2,1)S(1)} %collective-permute-done.2.near.mesh_near, bf16[32,512]{1,0:T(8,128)(2,1)S(1)} %collective-permute-done.3.far.mesh_far, bf16[32,512]{1,0:T(8,128)(2,1)S(1)} %copy-done.1, bf16[1024,128]{1,0:T(8,128)(2,1)S(1)} %get-tuple-element.56.recv_hits, ...), custom_call_target="tpu_custom_call" | custom-call | tf_op jit(solution)/shard_map/pallas_call | solution.py:399
  16.1 0.9 %shard_map.176.rows = bf16[1024,227]{1,0:T(8,128)(2,1)S(1)} custom-call(bf16[3,227,360]{2,1,0:T(8,128)(2,1)S(1)} %collective-permute-done.1.halo, bf16[1024,1152]{1,0:T(8,128)(2,1)S(1)} %get-tuple-element.52.hits, bf16[1024,227]{1,0:T(8,128)(2,1)S(1)} %get-tuple-element.54.rows), custom_call_target="tpu_custom_call" | custom-call | tf_op jit(solution)/shard_map/pallas_call | solution.py:399
  17.4 2.9 %shard_map.178 = (bf16[1024,512]{1,0:T(8,128)(2,1)S(1)}, bf16[1024,512]{1,0:T(8,128)(2,1)S(1)}, f32[64,512]{1,0:T(8,128)S(1)}, bf16[32,512]{1,0:T(8,128)(2,1)S(1)}, bf16[32,512]{1,0:T(8,128)(2,1)S(1)}) custom-call(bf16[3,227,360]{2,1,0:T(8,128)(2,1)S(1)} %collective-permute-done.near, bf16[1024,1152]{1,0:T(8,128)(2,1)S(1)} %get-tuple-element.50.near_hits, ...), custom_call_target="tpu_custom_call" | custom-call | tf_op jit(solution)/shard_map/pallas_call | solution.py:399
  20.4 1.6 %collective-permute-start.5 = (bf16[32,512]{1,0:T(8,128)(2,1)S(1)}, bf16[32,512]{1,0:T(8,128)(2,1)S(1)}, u32[]{:S(2)}, u32[]{:S(2)}) collective-permute-start(bf16[32,512]{1,0:T(8,128)(2,1)S(1)} %get-tuple-element.59), channel_id=1, source_target_pairs={{0,3},{1,2},{2,1},{3,0},{4,7},{5,6},{6,5},{7,4},{8,11},{9,10},{10,... | collective-permute-start | bytes 98312 | tf_op jit(solution)/shard_map/ppermute | solution.py:511
  22.0 1.8 %collective-permute-done.5.far = bf16[32,512]{1,0:T(8,128)(2,1)S(1)} collective-permute-done((bf16[32,512]{1,0:T(8,128)(2,1)S(1)}, bf16[32,512]{1,0:T(8,128)(2,1)S(1)}, u32[]{:S(2)}, u32[]{:S(2)}) %collective-permute-start.5) | collective-permute-done | bytes 32800 | tf_op jit(solution)/shard_map/ppermute | solution.py:511
  24.0 1.8 %collective-permute-start.7 = (bf16[64,512]{1,0:T(8,128)(2,1)S(1)}, bf16[64,512]{1,0:T(8,128)(2,1)S(1)}, u32[]{:S(2)}, u32[]{:S(2)}) collective-permute-start(bf16[64,512]{1,0:T(8,128)(2,1)S(1)} %get-tuple-element.60.own.nodes), channel_id=1, source_target_pairs={{0,4},{4,0},{8,12},{12,8},{1,5},{5,1},{9,13},{13,9},{2,6},{6,2},{1... | collective-permute-start | bytes 196616 | tf_op jit(solution)/shard_map/ppermute | solution.py:518
  26.0 0.7 %shard_map.180.own_pre = f32[512,512]{1,0:T(8,128)S(1)} custom-call(bf16[512,128]{1,0:T(8,128)(2,1)S(1)} %get-tuple-element.48.own_hits, bf16[512,64]{1,0:T(8,128)(2,1)S(1)} %get-tuple-element.49.to_hits, bf16[64,512]{1,0:T(8,128)(2,1)S(1)} %get-tuple-element.60.own.nodes, bf16[3299,512]{1,0:T(8,128)(2,1)S(1)} %constant_dynamic-update-slice_fusion.stack), custom_call_target="tpu_custom_call" | custom-call | tf_op jit(solution)/shard_map/pallas_call | solution.py:399
  26.7 1.9 %collective-permute-done.7.near = bf16[64,512]{1,0:T(8,128)(2,1)S(1)} collective-permute-done((bf16[64,512]{1,0:T(8,128)(2,1)S(1)}, bf16[64,512]{1,0:T(8,128)(2,1)S(1)}, u32[]{:S(2)}, u32[]{:S(2)}) %collective-permute-start.7) | collective-permute-done | bytes 65568 | tf_op jit(solution)/shard_map/ppermute | solution.py:518
  28.6 1.7 %shard_map.181 = (bf16[32,512]{1,0:T(8,128)(2,1)}, f32[192,512]{1,0:T(8,128)S(1)}, bf16[32,512]{1,0:T(8,128)(2,1)S(1)}, bf16[64,512]{1,0:T(8,128)(2,1)S(1)}, bf16[64,512]{1,0:T(8,128)(2,1)S(1)}) custom-call(f32[512,512]{1,0:T(8,128)S(1)} %shard_map.180.own_pre, bf16[512,256]{1,0:T(8,128)(2,1)S(1)} %get-tuple-element.61.outer_hits, ...), custom_call_target="tpu_custom_call" | custom-call | tf_op jit(solution)/shard_map/pallas_call | solution.py:399
  30.2 2.3 %collective-permute-start.8 = (bf16[64,512]{1,0:T(8,128)(2,1)S(1)}, bf16[64,512]{1,0:T(8,128)(2,1)S(1)}, u32[]{:S(2)}, u32[]{:S(2)}) collective-permute-start(bf16[64,512]{1,0:T(8,128)(2,1)S(1)} %get-tuple-element.66), channel_id=1, source_target_pairs={{0,4},{4,0},{8,12},{12,8},{1,5},{5,1},{9,13},{13,9},{2,6},{6,2},{1... | collective-permute-start | bytes 196616 | tf_op jit(solution)/shard_map/ppermute | solution.py:538
  32.5 1.5 %collective-permute-start.11 = (bf16[64,512]{1,0:T(8,128)(2,1)S(1)}, bf16[64,512]{1,0:T(8,128)(2,1)S(1)}, u32[]{:S(2)}, u32[]{:S(2)}) collective-permute-start(bf16[64,512]{1,0:T(8,128)(2,1)S(1)} %get-tuple-element.60.own.nodes), channel_id=1, source_target_pairs={{0,2},{2,0},{1,3},{3,1},{4,6},{6,4},{5,7},{7,5},{8,10},{10,8},{9,1... | collective-permute-start | bytes 196616 | tf_op jit(solution)/shard_map/ppermute | solution.py:431
  34.9 1.6 %collective-permute-start.12 = (bf16[48,512]{1,0:T(8,128)(2,1)S(1)}, bf16[48,512]{1,0:T(8,128)(2,1)S(1)}, u32[]{:S(2)}, u32[]{:S(2)}) collective-permute-start(bf16[48,512]{1,0:T(8,128)(2,1)S(1)} %get-tuple-element.74), channel_id=1, source_target_pairs={{0,3},{1,2},{2,1},{3,0},{4,7},{5,6},{6,5},{7,4},{8,11},{9,10},{10,... | collective-permute-start | bytes 147464 | tf_op jit(solution)/shard_map/ppermute | solution.py:551
  37.0 1.4 %collective-permute-done.12.far = bf16[48,512]{1,0:T(8,128)(2,1)S(1)} collective-permute-done((bf16[48,512]{1,0:T(8,128)(2,1)S(1)}, bf16[48,512]{1,0:T(8,128)(2,1)S(1)}, u32[]{:S(2)}, u32[]{:S(2)}) %collective-permute-start.12) | collective-permute-done | bytes 49184 | tf_op jit(solution)/shard_map/ppermute | solution.py:551
  38.5 1.1 %shard_map.184 = (bf16[1,1,512,128]{3,2,1,0:T(8,128)(2,1)S(1)}, bf16[128,512]{1,0:T(8,128)(2,1)S(1)}, bf16[2,64,128]{2,1,0:T(8,128)(2,1)S(1)}) custom-call(bf16[1024,128]{1,0:T(8,128)(2,1)S(1)} %get-tuple-element.56.recv_hits, f32[64,512]{1,0:T(8,128)S(1)} %get-tuple-element.71.part, bf16[48,512]{1,0:T(8,128)(2,1)S(1)} %collective-permute-done.10.near, ...), custom_call_target="tpu_custom_call" | custom-call | tf_op jit(solution)/shard_map/pallas_call | solution.py:399
  40.0 0.7 %shard_map.185 = (f32[1,512,128]{2,1,0:T(8,128)S(1)}, bf16[1,512,128]{2,1,0:T(8,128)(2,1)S(1)}) custom-call(bf16[1024,128]{1,0:T(8,128)(2,1)S(1)} %get-tuple-element.56.recv_hits, bf16[128,512]{1,0:T(8,128)(2,1)S(1)} %get-tuple-element.78.back, bf16[1024,512]{1,0:T(8,128)(2,1)S(1)} %get-tuple-element.77.edge_slope, ...), custom_call_target="tpu_custom_call" | custom-call | tf_op jit(solution)/shard_map/pallas_call | solution.py:399
  41.1 1.6 %collective-permute-start.15 = (bf16[320,128]{1,0:T(8,128)(2,1)S(1)}, bf16[320,128]{1,0:T(8,128)(2,1)S(1)}, u32[]{:S(2)}, u32[]{:S(2)}) collective-permute-start(bf16[320,128]{1,0:T(8,128)(2,1)S(1)} %bitcast.10), channel_id=1, source_target_pairs={{0,2},{2,0},{1,3},{3,1},{4,6},{6,4},{5,7},{7,5},{8,10},{10,8},{9,1... | collective-permute-start | bytes 245768 | tf_op jit(solution)/shard_map/ppermute | solution.py:431
  43.2 0.6 %shard_map.186.kept = f32[512,128]{1,0:T(8,128)S(1)} custom-call(bf16[1024,128]{1,0:T(8,128)(2,1)S(1)} %get-tuple-element.56.recv_hits, bf16[128,512]{1,0:T(8,128)(2,1)S(1)} %get-tuple-element.78.back, bf16[1024,512]{1,0:T(8,128)(2,1)S(1)} %get-tuple-element.77.edge_slope, bf16[512,1024]{1,0:T(8,128)(2,1)S(1)} %get-tuple-element.76.senders, ...), custom_call_target="tpu_custom_call" | custom-call | tf_op jit(solution)/shard_map/pallas_call | solution.py:399
  43.8 2.6 %collective-permute-done.15.refs_0_ = bf16[320,128]{1,0:T(8,128)(2,1)S(1)} collective-permute-done((bf16[320,128]{1,0:T(8,128)(2,1)S(1)}, bf16[320,128]{1,0:T(8,128)(2,1)S(1)}, u32[]{:S(2)}, u32[]{:S(2)}) %collective-permute-start.15) | collective-permute-done | bytes 81952 | tf_op jit(solution)/shard_map/ppermute | solution.py:431
  46.7 3.0 %collective-permute-start.16 = (bf16[2,128,128]{2,1,0:T(8,128)(2,1)S(1)}, bf16[2,128,128]{2,1,0:T(8,128)(2,1)S(1)}, u32[]{:S(2)}, u32[]{:S(2)}) collective-permute-start(bf16[2,128,128]{2,1,0:T(8,128)(2,1)S(1)} %get-tuple-element.85), channel_id=1, source_target_pairs={{0,12},{4,8},{8,4},{12,0},{1,13},{5,9},{9,5},{13,1},{2,14},{6,10},... | collective-permute-start | bytes 196616 | tf_op jit(solution)/shard_map/ppermute | solution.py:436
  49.7 0.6 %collective-permute-start.17 = (bf16[2,128,128]{2,1,0:T(8,128)(2,1)S(1)}, bf16[2,128,128]{2,1,0:T(8,128)(2,1)S(1)}, u32[]{:S(2)}, u32[]{:S(2)}) collective-permute-start(bf16[2,128,128]{2,1,0:T(8,128)(2,1)S(1)} %get-tuple-element.86), channel_id=1, source_target_pairs={{0,8},{4,12},{8,0},{12,4},{1,9},{5,13},{9,1},{13,5},{2,10},{6,14},... | collective-permute-start | bytes 196616 | tf_op jit(solution)/shard_map/ppermute | solution.py:436
  50.3 0.9 %collective-permute-start.19 = (bf16[2,128,128]{2,1,0:T(8,128)(2,1)S(1)}, bf16[2,128,128]{2,1,0:T(8,128)(2,1)S(1)}, u32[]{:S(2)}, u32[]{:S(2)}) collective-permute-start(bf16[2,128,128]{2,1,0:T(8,128)(2,1)S(1)} %get-tuple-element.89), channel_id=1, source_target_pairs={{0,4},{4,0},{8,12},{12,8},{1,5},{5,1},{9,13},{13,9},{2,6},{6,2},{1... | collective-permute-start | bytes 196616 | tf_op jit(solution)/shard_map/ppermute | solution.py:436
  51.2 2.0 %collective-permute-done.16.refs_0_ = bf16[2,128,128]{2,1,0:T(8,128)(2,1)S(1)} collective-permute-done((bf16[2,128,128]{2,1,0:T(8,128)(2,1)S(1)}, bf16[2,128,128]{2,1,0:T(8,128)(2,1)S(1)}, u32[]{:S(2)}, u32[]{:S(2)}) %collective-permute-start.16) | collective-permute-done | bytes 65568 | tf_op jit(solution)/shard_map/ppermute | solution.py:436
  53.3 2.8 %collective-permute-done.17.refs_1_ = bf16[2,128,128]{2,1,0:T(8,128)(2,1)S(1)} collective-permute-done((bf16[2,128,128]{2,1,0:T(8,128)(2,1)S(1)}, bf16[2,128,128]{2,1,0:T(8,128)(2,1)S(1)}, u32[]{:S(2)}, u32[]{:S(2)}) %collective-permute-start.17) | collective-permute-done | bytes 65568 | tf_op jit(solution)/shard_map/ppermute | solution.py:436
  56.0 0.7 %shard_map.190 = (f32[128,128]{1,0:T(8,128)}, f32[128,128]{1,0:T(8,128)}) custom-call(bf16[2,128,128]{2,1,0:T(8,128)(2,1)S(1)} %collective-permute-done.16.refs_0_, bf16[2,128,128]{2,1,0:T(8,128)(2,1)S(1)} %collective-permute-done.17.refs_1_, bf16[2,128,128]{2,1,0:T(8,128)(2,1)S(1)} %collective-permute-done.19.refs_2_, ...), custom_call_target="tpu_custom_call" | custom-call | tf_op jit(solution)/shard_map/pallas_call | solution.py:399
  (46 shorter events, 5.1 us)
Async XLA Ops:
  0.6 15.4 %collective-permute-start.1 = (bf16[3,227,360]{2,1,0:T(8,128)(2,1)}, bf16[3,227,360]{2,1,0:T(8,128)(2,1)S(1)}, u32[]{:S(2)}, u32[]{:S(2)}) collective-permute-start(bf16[3,227,360]{2,1,0:T(8,128)(2,1)} %bitcast.5), channel_id=1, source_target_pairs={{0,1},{1,0},{2,3},{3,2},{4,8},{5,9},{6,10},{7,11},{8,4},{9,5},{10,... | collective-permute-start | bytes 1470968 | tf_op jit(solution)/shard_map/ppermute | solution.py:460
  1.2 16.3 %collective-permute-start = (bf16[3,227,360]{2,1,0:T(8,128)(2,1)}, bf16[3,227,360]{2,1,0:T(8,128)(2,1)S(1)}, u32[]{:S(2)}, u32[]{:S(2)}) collective-permute-start(bf16[3,227,360]{2,1,0:T(8,128)(2,1)} %bitcast.6), channel_id=1, source_target_pairs={{0,4},{4,0},{8,12},{12,8},{1,5},{5,1},{9,13},{13,9},{2,6},{6,2},{1... | collective-permute-start | bytes 1470968 | tf_op jit(solution)/shard_map/ppermute | solution.py:459
  7.3 1.0 %copy-start = (bf16[3,360,227]{1,2,0:T(8,128)(2,1)S(1)}, bf16[3,360,227]{1,2,0:T(8,128)(2,1)}, u32[]{:S(2)}) copy-start(bf16[3,360,227]{1,2,0:T(8,128)(2,1)} %param.16) | copy-start | bytes 1470964
  8.4 6.8 %copy-start.3 = (bf16[512,512]{1,0:T(8,128)(2,1)S(1)}, bf16[512,512]{1,0:T(8,128)(2,1)}, u32[]{:S(2)}) copy-start(bf16[512,512]{1,0:T(8,128)(2,1)} %param.21) | copy-start | bytes 1572868
  8.4 6.9 %copy-start.4 = (bf16[512,512]{1,0:T(8,128)(2,1)S(1)}, bf16[512,512]{1,0:T(8,128)(2,1)}, u32[]{:S(2)}) copy-start(bf16[512,512]{1,0:T(8,128)(2,1)} %param.22) | copy-start | bytes 1572868
  8.4 6.9 %copy-start.5 = (bf16[512,512]{1,0:T(8,128)(2,1)S(1)}, bf16[512,512]{1,0:T(8,128)(2,1)}, u32[]{:S(2)}) copy-start(bf16[512,512]{1,0:T(8,128)(2,1)} %param.23) | copy-start | bytes 1572868
  8.4 7.0 %copy-start.6 = (bf16[227,512]{1,0:T(8,128)(2,1)S(1)}, bf16[227,512]{1,0:T(8,128)(2,1)}, u32[]{:S(2)}) copy-start(bf16[227,512]{1,0:T(8,128)(2,1)} %param.17) | copy-start | bytes 697348
  10.3 5.1 %copy-start.1 = (bf16[32,512]{1,0:T(8,128)(2,1)S(1)}, bf16[32,512]{1,0:T(8,128)(2,1)}, u32[]{:S(2)}) copy-start(bf16[32,512]{1,0:T(8,128)(2,1)} %mesh_in.3) | copy-start | bytes 98308
  10.3 5.1 %collective-permute-start.3 = (bf16[32,512]{1,0:T(8,128)(2,1)}, bf16[32,512]{1,0:T(8,128)(2,1)S(1)}, u32[]{:S(2)}, u32[]{:S(2)}) collective-permute-start(bf16[32,512]{1,0:T(8,128)(2,1)} %mesh_in.3), channel_id=1, source_target_pairs={{0,3},{1,2},{2,1},{3,0},{4,7},{5,6},{6,5},{7,4},{8,11},{9,10},{10,... | collective-permute-start | bytes 98312 | tf_op jit(solution)/shard_map/ppermute | solution.py:486
  10.7 4.7 %collective-permute-start.2 = (bf16[32,512]{1,0:T(8,128)(2,1)}, bf16[32,512]{1,0:T(8,128)(2,1)S(1)}, u32[]{:S(2)}, u32[]{:S(2)}) collective-permute-start(bf16[32,512]{1,0:T(8,128)(2,1)} %mesh_in.3), channel_id=1, source_target_pairs={{0,1},{1,0},{2,3},{3,2},{4,5},{5,4},{6,7},{7,6},{8,9},{9,8},{10,11... | collective-permute-start | bytes 98312 | tf_op jit(solution)/shard_map/ppermute | solution.py:485
  20.3 1.7 %collective-permute-start.4 = (bf16[32,512]{1,0:T(8,128)(2,1)S(1)}, bf16[32,512]{1,0:T(8,128)(2,1)S(1)}, u32[]{:S(2)}, u32[]{:S(2)}) collective-permute-start(bf16[32,512]{1,0:T(8,128)(2,1)S(1)} %get-tuple-element.58), channel_id=1, source_target_pairs={{0,1},{1,0},{2,3},{3,2},{4,5},{5,4},{6,7},{7,6},{8,9},{9,8},{10,11... | collective-permute-start | bytes 98312 | tf_op jit(solution)/shard_map/ppermute | solution.py:512
  20.4 3.4 %collective-permute-start.5 = (bf16[32,512]{1,0:T(8,128)(2,1)S(1)}, bf16[32,512]{1,0:T(8,128)(2,1)S(1)}, u32[]{:S(2)}, u32[]{:S(2)}) collective-permute-start(bf16[32,512]{1,0:T(8,128)(2,1)S(1)} %get-tuple-element.59), channel_id=1, source_target_pairs={{0,3},{1,2},{2,1},{3,0},{4,7},{5,6},{6,5},{7,4},{8,11},{9,10},{10,... | collective-permute-start | bytes 98312 | tf_op jit(solution)/shard_map/ppermute | solution.py:511
  23.8 4.8 %copy-start.2 = (bf16[32,512]{1,0:T(8,128)(2,1)S(1)}, bf16[32,512]{1,0:T(8,128)(2,1)}, u32[]{:S(2)}) copy-start(bf16[32,512]{1,0:T(8,128)(2,1)} %d_out.3) | copy-start | bytes 98308
  24.0 4.5 %collective-permute-start.7 = (bf16[64,512]{1,0:T(8,128)(2,1)S(1)}, bf16[64,512]{1,0:T(8,128)(2,1)S(1)}, u32[]{:S(2)}, u32[]{:S(2)}) collective-permute-start(bf16[64,512]{1,0:T(8,128)(2,1)S(1)} %get-tuple-element.60.own.nodes), channel_id=1, source_target_pairs={{0,4},{4,0},{8,12},{12,8},{1,5},{5,1},{9,13},{13,9},{2,6},{6,2},{1... | collective-permute-start | bytes 196616 | tf_op jit(solution)/shard_map/ppermute | solution.py:518
  25.8 2.7 %collective-permute-start.6 = (bf16[64,512]{1,0:T(8,128)(2,1)S(1)}, bf16[64,512]{1,0:T(8,128)(2,1)S(1)}, u32[]{:S(2)}, u32[]{:S(2)}) collective-permute-start(bf16[64,512]{1,0:T(8,128)(2,1)S(1)} %get-tuple-element.60.own.nodes), channel_id=1, source_target_pairs={{0,1},{1,0},{2,3},{3,2},{4,8},{5,9},{6,10},{7,11},{8,4},{9,5},{10,... | collective-permute-start | bytes 196616 | tf_op jit(solution)/shard_map/ppermute | solution.py:519
  30.2 4.5 %collective-permute-start.8 = (bf16[64,512]{1,0:T(8,128)(2,1)S(1)}, bf16[64,512]{1,0:T(8,128)(2,1)S(1)}, u32[]{:S(2)}, u32[]{:S(2)}) collective-permute-start(bf16[64,512]{1,0:T(8,128)(2,1)S(1)} %get-tuple-element.66), channel_id=1, source_target_pairs={{0,4},{4,0},{8,12},{12,8},{1,5},{5,1},{9,13},{13,9},{2,6},{6,2},{1... | collective-permute-start | bytes 196616 | tf_op jit(solution)/shard_map/ppermute | solution.py:538
  32.5 2.2 %collective-permute-start.9 = (bf16[64,512]{1,0:T(8,128)(2,1)S(1)}, bf16[64,512]{1,0:T(8,128)(2,1)S(1)}, u32[]{:S(2)}, u32[]{:S(2)}) collective-permute-start(bf16[64,512]{1,0:T(8,128)(2,1)S(1)} %get-tuple-element.67), channel_id=1, source_target_pairs={{0,1},{1,0},{2,3},{3,2},{4,8},{5,9},{6,10},{7,11},{8,4},{9,5},{10,... | collective-permute-start | bytes 196616 | tf_op jit(solution)/shard_map/ppermute | solution.py:539
  32.5 4.5 %collective-permute-start.11 = (bf16[64,512]{1,0:T(8,128)(2,1)S(1)}, bf16[64,512]{1,0:T(8,128)(2,1)S(1)}, u32[]{:S(2)}, u32[]{:S(2)}) collective-permute-start(bf16[64,512]{1,0:T(8,128)(2,1)S(1)} %get-tuple-element.60.own.nodes), channel_id=1, source_target_pairs={{0,2},{2,0},{1,3},{3,1},{4,6},{6,4},{5,7},{7,5},{8,10},{10,8},{9,1... | collective-permute-start | bytes 196616 | tf_op jit(solution)/shard_map/ppermute | solution.py:431
  34.8 2.2 %collective-permute-start.10 = (bf16[48,512]{1,0:T(8,128)(2,1)S(1)}, bf16[48,512]{1,0:T(8,128)(2,1)S(1)}, u32[]{:S(2)}, u32[]{:S(2)}) collective-permute-start(bf16[48,512]{1,0:T(8,128)(2,1)S(1)} %get-tuple-element.72), channel_id=1, source_target_pairs={{0,1},{1,0},{2,3},{3,2},{4,5},{5,4},{6,7},{7,6},{8,9},{9,8},{10,11... | collective-permute-start | bytes 147464 | tf_op jit(solution)/shard_map/ppermute | solution.py:552
  34.9 3.6 %collective-permute-start.12 = (bf16[48,512]{1,0:T(8,128)(2,1)S(1)}, bf16[48,512]{1,0:T(8,128)(2,1)S(1)}, u32[]{:S(2)}, u32[]{:S(2)}) collective-permute-start(bf16[48,512]{1,0:T(8,128)(2,1)S(1)} %get-tuple-element.74), channel_id=1, source_target_pairs={{0,3},{1,2},{2,1},{3,0},{4,7},{5,6},{6,5},{7,4},{8,11},{9,10},{10,... | collective-permute-start | bytes 147464 | tf_op jit(solution)/shard_map/ppermute | solution.py:551
  39.5 1.5 %collective-permute-start.14 = (bf16[1,512,128]{2,1,0:T(8,128)(2,1)S(1)}, bf16[1,512,128]{2,1,0:T(8,128)(2,1)S(1)}, u32[]{:S(2)}, u32[]{:S(2)}) collective-permute-start(bf16[1,512,128]{2,1,0:T(8,128)(2,1)S(1)} %bitcast.8), channel_id=1, source_target_pairs={{0,1},{1,0},{2,3},{3,2},{4,5},{5,4},{6,7},{7,6},{8,9},{9,8},{10,11... | collective-permute-start | bytes 393224 | tf_op jit(solution)/shard_map/ppermute | solution.py:431
  40.7 2.4 %collective-permute-start.13 = (bf16[512,128]{1,0:T(8,128)(2,1)S(1)}, bf16[512,128]{1,0:T(8,128)(2,1)S(1)}, u32[]{:S(2)}, u32[]{:S(2)}) collective-permute-start(bf16[512,128]{1,0:T(8,128)(2,1)S(1)} %bitcast.9), channel_id=1, source_target_pairs={{0,1},{1,0},{2,3},{3,2},{4,5},{5,4},{6,7},{7,6},{8,9},{9,8},{10,11... | collective-permute-start | bytes 393224 | tf_op jit(solution)/shard_map/ppermute | solution.py:431
  41.1 5.3 %collective-permute-start.15 = (bf16[320,128]{1,0:T(8,128)(2,1)S(1)}, bf16[320,128]{1,0:T(8,128)(2,1)S(1)}, u32[]{:S(2)}, u32[]{:S(2)}) collective-permute-start(bf16[320,128]{1,0:T(8,128)(2,1)S(1)} %bitcast.10), channel_id=1, source_target_pairs={{0,2},{2,0},{1,3},{3,1},{4,6},{6,4},{5,7},{7,5},{8,10},{10,8},{9,1... | collective-permute-start | bytes 245768 | tf_op jit(solution)/shard_map/ppermute | solution.py:431
  42.6 7.7 %collective-permute-start.18 = (bf16[256,128]{1,0:T(8,128)(2,1)S(1)}, bf16[256,128]{1,0:T(8,128)(2,1)S(1)}, u32[]{:S(2)}, u32[]{:S(2)}) collective-permute-start(bf16[256,128]{1,0:T(8,128)(2,1)S(1)} %bitcast.11), channel_id=1, source_target_pairs={{0,2},{2,0},{1,3},{3,1},{4,6},{6,4},{5,7},{7,5},{8,10},{10,8},{9,1... | collective-permute-start | bytes 196616 | tf_op jit(solution)/shard_map/ppermute | solution.py:431
  46.7 6.6 %collective-permute-start.16 = (bf16[2,128,128]{2,1,0:T(8,128)(2,1)S(1)}, bf16[2,128,128]{2,1,0:T(8,128)(2,1)S(1)}, u32[]{:S(2)}, u32[]{:S(2)}) collective-permute-start(bf16[2,128,128]{2,1,0:T(8,128)(2,1)S(1)} %get-tuple-element.85), channel_id=1, source_target_pairs={{0,12},{4,8},{8,4},{12,0},{1,13},{5,9},{9,5},{13,1},{2,14},{6,10},... | collective-permute-start | bytes 196616 | tf_op jit(solution)/shard_map/ppermute | solution.py:436
  49.7 6.4 %collective-permute-start.17 = (bf16[2,128,128]{2,1,0:T(8,128)(2,1)S(1)}, bf16[2,128,128]{2,1,0:T(8,128)(2,1)S(1)}, u32[]{:S(2)}, u32[]{:S(2)}) collective-permute-start(bf16[2,128,128]{2,1,0:T(8,128)(2,1)S(1)} %get-tuple-element.86), channel_id=1, source_target_pairs={{0,8},{4,12},{8,0},{12,4},{1,9},{5,13},{9,1},{13,5},{2,10},{6,14},... | collective-permute-start | bytes 196616 | tf_op jit(solution)/shard_map/ppermute | solution.py:436
  50.3 5.7 %collective-permute-start.19 = (bf16[2,128,128]{2,1,0:T(8,128)(2,1)S(1)}, bf16[2,128,128]{2,1,0:T(8,128)(2,1)S(1)}, u32[]{:S(2)}, u32[]{:S(2)}) collective-permute-start(bf16[2,128,128]{2,1,0:T(8,128)(2,1)S(1)} %get-tuple-element.89), channel_id=1, source_target_pairs={{0,4},{4,0},{8,12},{12,8},{1,5},{5,1},{9,13},{13,9},{2,6},{6,2},{1... | collective-permute-start | bytes 196616 | tf_op jit(solution)/shard_map/ppermute | solution.py:436

commit v17 on v16

--- a/solution.py
+++ b/solution.py
@@ -154,21 +154,36 @@
     pre_out[...] = mm(recv_hits[...], table)
 
 
-def gather_kernel(halo, hits, rows, rows_out, wide):
+def live_blocks(count, edges, work, rest):
+    work(slice(0, edges // 2))
+    for first in (edges // 2, 3 * edges // 4):
+        part_of = slice(first, first + edges // 4)
+        pl.when(count[0, 0] > first)(lambda part_of=part_of: work(part_of))
+        pl.when(count[0, 0] <= first)(lambda part_of=part_of: rest(part_of))
+
+
+def gather_kernel(count, halo, hits, rows, rows_out, wide):
     fill(wide, halo, wide.shape[1] // halo.shape[0], 0)
-    rows_out[...] = rows[...] + mm_nt(hits[...], wide[...]).astype(BF16)
+
+    def work(part_of):
+        gathered = mm_nt(hits[part_of], wide[...]).astype(BF16)
+        rows_out[part_of] = rows[part_of] + gathered
+
+    def rest(part_of):
+        rows_out[part_of] = jnp.zeros_like(rows_out[part_of])
+
+    live_blocks(count, rows.shape[0], work, rest)
 
 
 def encode_kernel(
-    near, near_hits, recv_rows, rows, recv_pre, stack,
+    count, near, near_hits, recv_rows, rows, recv_pre, stack,
     senders_out, slope_out, part_out, near_out, far_out, wide,
 ):
     half = recv_rows.shape[0] // 2
     fill(wide, near, wide.shape[1] // near.shape[0], 0)
-    block = rows.shape[0] // 2
-    sums = None
-    for first in range(0, rows.shape[0], block):
-        part_of = slice(first, first + block)
+    part_out[...] = jnp.zeros_like(part_out)
+
+    def work(part_of):
         raw = rows[part_of] + mm_nt(near_hits[part_of], wide[...]).astype(BF16)
         latent, _ = silu_parts(mm(raw, stack[stack.shape[0] - raw.shape[1] :]))
         latent = latent.astype(BF16)
@@ -176,9 +191,14 @@
         pre = mm(latent, weight(stack, GS)) + recv_pre[part_of]
         value, slope = silu_parts(pre)
         slope_out[part_of] = slope.astype(BF16)
-        part = mm(recv_rows[:, part_of], value.astype(BF16))
-        sums = part if sums is None else sums + part
-    part_out[...] = sums
+        part_out[...] += mm(recv_rows[:, part_of], value.astype(BF16))
+
+    def rest(part_of):
+        senders_out[part_of] = jnp.zeros_like(senders_out[part_of])
+        slope_out[part_of] = jnp.zeros_like(slope_out[part_of])
+
+    live_blocks(count, rows.shape[0], work, rest)
+    sums = part_out[...]
     even = even_on("lat")
     near_out[...] = jnp.where(even, sums[half:], sums[:half]).astype(BF16)
     far_out[...] = jnp.where(even, sums[:half], sums[half:]).astype(BF16)
@@ -493,7 +513,8 @@
     (rows,) = call(
         gather_kernel,
         [((edges, variables), BF16)],
-        raw_far, far_hits, rows,
+        g2m_count, raw_far, far_hits, rows,
+        scalars=(0,),
         scratch=[pltpu.VMEM((variables, width), BF16)],
     )
     senders, edge_slope, part, to_near, to_far = call(
@@ -505,7 +526,8 @@
             ((node_count, latent), BF16),
             ((node_count, latent), BF16),
         ],
-        raw_near, near_hits, recv_rows, rows, recv_pre, stack,
+        g2m_count, raw_near, near_hits, recv_rows, rows, recv_pre, stack,
+        scalars=(0,),
         scratch=[pltpu.VMEM((variables, width), BF16)],
     )
     from_far = lax.ppermute(to_far, around, ring_far)

time: 57.1 us -> 57.8 us (1.012)
  Pallas kernels: 12.7 us -> 14.4 us
    pallas_call x16, Pallas kernels: 12.7 us -> 14.4 us  [call(): pl.pallas_call(kernel, out_shape=[jax.ShapeDtypeStruct(shape, dtype) for...]
where the time goes in v17:
time: 57.8 us; the launch traced here: 57.5 us
  starting transfers between devices  22.3 us (39%)
  Pallas kernels  14.4 us (25%)
  waiting for transfers between devices  13.5 us (23%)
  local copies, waits for them, and re-layouts  4.43 us (8%)
  between operations  2.18 us (4%)
  other arithmetic  0.74 us (1%)
    pallas_call x16, Pallas kernels, call(): pl.pallas_call(kernel, out_shape=[jax.ShapeDtypeStruct(shape, dtype) for...  14.4 us
    ppermute x3, starting transfers between devices, over_band(): return lax.ppermute(x, 'band', [(b, b ^ partner) for b in range(count)])  4.52 us
    ppermute x3, waiting for transfers between devices, over_band(): return lax.ppermute(x, 'band', [(b, b ^ partner) for b in range(count)])  4.48 us
    unnamed x20, local copies, waits for them, and re-layouts  4.41 us
    ppermute x5, starting transfers between devices, shifted(): lax.ppermute(x, axis, [(i, (i + shift) % count) for i in range(count)])  4.22 us
    ppermute x1, starting transfers between devices, on_device(): raw_near = lax.ppermute(grid, 'band', band_near)  4.15 us
    ppermute x2, waiting for transfers between devices, on_device(): from_far = lax.ppermute(to_far, around, ring_far)  3.44 us
    ppermute x2, starting transfers between devices, on_device(): from_far = lax.ppermute(to_far, around, ring_far)  3.18 us
  transfers between devices with their start and end apart: 20, of which 10 were waited for; matrix products, arithmetic and copies ran while one was open for 7% of the time, Pallas kernels for 11%

profile of v17, /device:TPU:0, one launch (start us, length us, event | category | flops | bytes accessed | tf_op | source)
XLA Modules:
  0.0 57.5 jit_solution(11597728617633948754)
XLA Ops:
  1.2 4.1 %collective-permute-start = (bf16[3,227,360]{2,1,0:T(8,128)(2,1)}, bf16[3,227,360]{2,1,0:T(8,128)(2,1)S(1)}, u32[]{:S(2)}, u32[]{:S(2)}) collective-permute-start(bf16[3,227,360]{2,1,0:T(8,128)(2,1)} %bitcast.6), channel_id=1, source_target_pairs={{0,4},{4,0},{8,12},{12,8},{1,5},{5,1},{9,13},{13,9},{2,6},{6,2},{1... | collective-permute-start | bytes 1470968 | tf_op jit(solution)/shard_map/ppermute | solution.py:479
  6.6 0.7 %pad_add_fusion.indices = s32[1,1,3072]{2,1,0:T(1,128)S(1)} fusion(s32[1,1,512]{2,1,0:T(1,128)} %param.30, s32[1,1,512]{2,1,0:T(1,128)} %param.29, s32[1,1,1024]{2,1,0:T(1,128)} %param.27, s32[1,1,1024]{2,1,0:T(1,128)} %param.26), kind=kLoop, calls=%fused_computation.7 | loop fusion | flops 9216 | bytes 24576 | tf_op jit(solution)/shard_map/concatenate | solution.py:483
  7.3 1.0 %copy-done = bf16[3,360,227]{1,2,0:T(8,128)(2,1)S(1)} copy-done((bf16[3,360,227]{1,2,0:T(8,128)(2,1)S(1)}, bf16[3,360,227]{1,2,0:T(8,128)(2,1)}, u32[]{:S(2)}) %copy-start) | copy-done | bytes 490344
  8.4 1.9 %shard_map.175 = (bf16[1024,227]{1,0:T(8,128)(2,1)S(1)}, bf16[1024,128]{1,0:T(8,128)(2,1)S(1)}, bf16[64,1024]{1,0:T(8,128)(2,1)S(1)}, bf16[512,128]{1,0:T(8,128)...) custom-call(s32[1,1]{1,0:T(1,128)S(6)} %copy.25.count, ...), custom_call_target="tpu_custom_call" | custom-call | tf_op jit(solution)/shard_map/pallas_call | solution.py:419
  10.7 1.2 %collective-permute-start.2 = (bf16[32,512]{1,0:T(8,128)(2,1)}, bf16[32,512]{1,0:T(8,128)(2,1)S(1)}, u32[]{:S(2)}, u32[]{:S(2)}) collective-permute-start(bf16[32,512]{1,0:T(8,128)(2,1)} %mesh_in.3), channel_id=1, source_target_pairs={{0,1},{1,0},{2,3},{3,2},{4,5},{5,4},{6,7},{7,6},{8,9},{9,8},{10,11... | collective-permute-start | bytes 98312 | tf_op jit(solution)/shard_map/ppermute | solution.py:505
  12.0 1.1 %constant_dynamic-update-slice_fusion.6 = bf16[3299,512]{1,0:T(8,128)(2,1)S(1)} fusion(bf16[512,512]{1,0:T(8,128)(2,1)} %param.18), kind=kLoop, calls=%fused_computation.6 | loop fusion | bytes 1048576
  13.1 1.1 %constant_dynamic-update-slice_fusion.5 = bf16[3299,512]{1,0:T(8,128)(2,1)S(1)} fusion(bf16[3299,512]{1,0:T(8,128)(2,1)S(1)} %constant_dynamic-update-slice_fusion.6, bf16[512,512]{1,0:T(8,128)(2,1)} %param.19), kind=kLoop, calls=%fused_computation.5 | loop fusion | bytes 1048576
  14.1 1.1 %constant_dynamic-update-slice_fusion.4 = bf16[3299,512]{1,0:T(8,128)(2,1)S(1)} fusion(bf16[3299,512]{1,0:T(8,128)(2,1)S(1)} %constant_dynamic-update-slice_fusion.5, bf16[512,512]{1,0:T(8,128)(2,1)} %param.20), kind=kLoop, calls=%fused_computation.4 | loop fusion | bytes 1048576
  15.4 0.6 %shard_map.177.recv_pre = f32[1024,512]{1,0:T(8,128)S(1)} custom-call(bf16[32,512]{1,0:T(8,128)(2,1)S(1)} %collective-permute-done.2.near.mesh_near, bf16[32,512]{1,0:T(8,128)(2,1)S(1)} %collective-permute-done.3.far.mesh_far, bf16[32,512]{1,0:T(8,128)(2,1)S(1)} %copy-done.1, bf16[1024,128]{1,0:T(8,128)(2,1)S(1)} %get-tuple-element.56.recv_hits, ...), custom_call_target="tpu_custom_call" | custom-call | tf_op jit(solution)/shard_map/pallas_call | solution.py:419
  16.1 1.3 %shard_map.176.rows = bf16[1024,227]{1,0:T(8,128)(2,1)S(1)} custom-call(s32[1,1]{1,0:T(1,128)S(6)} %copy.25.count, bf16[3,227,360]{2,1,0:T(8,128)(2,1)S(1)} %collective-permute-done.1.halo, bf16[1024,1152]{1,0:T(8,128)(2,1)S(1)} %get-tuple-element.52.hits, bf16[1024,227]{1,0:T(8,128)(2,1)S(1)} %get-tuple-element.54.rows), custom_call_target="tpu_custom_call" | custom-call | tf_op jit(solution)/shard_map/pallas_call | solution.py:419
  17.4 4.2 %shard_map.178 = (bf16[1024,512]{1,0:T(8,128)(2,1)S(1)}, bf16[1024,512]{1,0:T(8,128)(2,1)S(1)}, f32[64,512]{1,0:T(8,128)S(1)}, bf16[32,512]{1,0:T(8,128)(2,1)S(1)}, bf16[32,512]{1,0:T(8,128)(2,1)S(1)}) custom-call(s32[1,1]{1,0:T(1,128)S(6)} %copy.25.count, bf16[3,227,360]{2,1,0:T(8,128)(2,1)S(1)} %collective-permute-done.near, ...), custom_call_target="tpu_custom_call" | custom-call | tf_op jit(solution)/shard_map/pallas_call | solution.py:419
  21.7 1.6 %collective-permute-start.5 = (bf16[32,512]{1,0:T(8,128)(2,1)S(1)}, bf16[32,512]{1,0:T(8,128)(2,1)S(1)}, u32[]{:S(2)}, u32[]{:S(2)}) collective-permute-start(bf16[32,512]{1,0:T(8,128)(2,1)S(1)} %get-tuple-element.59), channel_id=1, source_target_pairs={{0,3},{1,2},{2,1},{3,0},{4,7},{5,6},{6,5},{7,4},{8,11},{9,10},{10,... | collective-permute-start | bytes 98312 | tf_op jit(solution)/shard_map/ppermute | solution.py:533
  23.3 1.8 %collective-permute-done.5.far = bf16[32,512]{1,0:T(8,128)(2,1)S(1)} collective-permute-done((bf16[32,512]{1,0:T(8,128)(2,1)S(1)}, bf16[32,512]{1,0:T(8,128)(2,1)S(1)}, u32[]{:S(2)}, u32[]{:S(2)}) %collective-permute-start.5) | collective-permute-done | bytes 32800 | tf_op jit(solution)/shard_map/ppermute | solution.py:533
  25.3 1.8 %collective-permute-start.7 = (bf16[64,512]{1,0:T(8,128)(2,1)S(1)}, bf16[64,512]{1,0:T(8,128)(2,1)S(1)}, u32[]{:S(2)}, u32[]{:S(2)}) collective-permute-start(bf16[64,512]{1,0:T(8,128)(2,1)S(1)} %get-tuple-element.60.own.nodes), channel_id=1, source_target_pairs={{0,4},{4,0},{8,12},{12,8},{1,5},{5,1},{9,13},{13,9},{2,6},{6,2},{1... | collective-permute-start | bytes 196616 | tf_op jit(solution)/shard_map/ppermute | solution.py:540
  27.3 0.7 %shard_map.180.own_pre = f32[512,512]{1,0:T(8,128)S(1)} custom-call(bf16[512,128]{1,0:T(8,128)(2,1)S(1)} %get-tuple-element.48.own_hits, bf16[512,64]{1,0:T(8,128)(2,1)S(1)} %get-tuple-element.49.to_hits, bf16[64,512]{1,0:T(8,128)(2,1)S(1)} %get-tuple-element.60.own.nodes, bf16[3299,512]{1,0:T(8,128)(2,1)S(1)} %constant_dynamic-update-slice_fusion.stack), custom_call_target="tpu_custom_call" | custom-call | tf_op jit(solution)/shard_map/pallas_call | solution.py:419
  28.0 1.8 %collective-permute-done.7.near = bf16[64,512]{1,0:T(8,128)(2,1)S(1)} collective-permute-done((bf16[64,512]{1,0:T(8,128)(2,1)S(1)}, bf16[64,512]{1,0:T(8,128)(2,1)S(1)}, u32[]{:S(2)}, u32[]{:S(2)}) %collective-permute-start.7) | collective-permute-done | bytes 65568 | tf_op jit(solution)/shard_map/ppermute | solution.py:540
  29.9 1.7 %shard_map.181 = (bf16[32,512]{1,0:T(8,128)(2,1)}, f32[192,512]{1,0:T(8,128)S(1)}, bf16[32,512]{1,0:T(8,128)(2,1)S(1)}, bf16[64,512]{1,0:T(8,128)(2,1)S(1)}, bf16[64,512]{1,0:T(8,128)(2,1)S(1)}) custom-call(f32[512,512]{1,0:T(8,128)S(1)} %shard_map.180.own_pre, bf16[512,256]{1,0:T(8,128)(2,1)S(1)} %get-tuple-element.61.outer_hits, ...), custom_call_target="tpu_custom_call" | custom-call | tf_op jit(solution)/shard_map/pallas_call | solution.py:419
  31.5 1.9 %collective-permute-start.8 = (bf16[64,512]{1,0:T(8,128)(2,1)S(1)}, bf16[64,512]{1,0:T(8,128)(2,1)S(1)}, u32[]{:S(2)}, u32[]{:S(2)}) collective-permute-start(bf16[64,512]{1,0:T(8,128)(2,1)S(1)} %get-tuple-element.66), channel_id=1, source_target_pairs={{0,4},{4,0},{8,12},{12,8},{1,5},{5,1},{9,13},{13,9},{2,6},{6,2},{1... | collective-permute-start | bytes 196616 | tf_op jit(solution)/shard_map/ppermute | solution.py:560
  33.4 1.5 %collective-permute-start.11 = (bf16[64,512]{1,0:T(8,128)(2,1)S(1)}, bf16[64,512]{1,0:T(8,128)(2,1)S(1)}, u32[]{:S(2)}, u32[]{:S(2)}) collective-permute-start(bf16[64,512]{1,0:T(8,128)(2,1)S(1)} %get-tuple-element.60.own.nodes), channel_id=1, source_target_pairs={{0,2},{2,0},{1,3},{3,1},{4,6},{6,4},{5,7},{7,5},{8,10},{10,8},{9,1... | collective-permute-start | bytes 196616 | tf_op jit(solution)/shard_map/ppermute | solution.py:451
  36.0 1.6 %collective-permute-start.12 = (bf16[48,512]{1,0:T(8,128)(2,1)S(1)}, bf16[48,512]{1,0:T(8,128)(2,1)S(1)}, u32[]{:S(2)}, u32[]{:S(2)}) collective-permute-start(bf16[48,512]{1,0:T(8,128)(2,1)S(1)} %get-tuple-element.74), channel_id=1, source_target_pairs={{0,3},{1,2},{2,1},{3,0},{4,7},{5,6},{6,5},{7,4},{8,11},{9,10},{10,... | collective-permute-start | bytes 147464 | tf_op jit(solution)/shard_map/ppermute | solution.py:573
  37.9 1.6 %collective-permute-done.12.far = bf16[48,512]{1,0:T(8,128)(2,1)S(1)} collective-permute-done((bf16[48,512]{1,0:T(8,128)(2,1)S(1)}, bf16[48,512]{1,0:T(8,128)(2,1)S(1)}, u32[]{:S(2)}, u32[]{:S(2)}) %collective-permute-start.12) | collective-permute-done | bytes 49184 | tf_op jit(solution)/shard_map/ppermute | solution.py:573
  39.5 1.1 %shard_map.184 = (bf16[1,1,512,128]{3,2,1,0:T(8,128)(2,1)S(1)}, bf16[128,512]{1,0:T(8,128)(2,1)S(1)}, bf16[2,64,128]{2,1,0:T(8,128)(2,1)S(1)}) custom-call(bf16[1024,128]{1,0:T(8,128)(2,1)S(1)} %get-tuple-element.56.recv_hits, f32[64,512]{1,0:T(8,128)S(1)} %get-tuple-element.71.part, bf16[48,512]{1,0:T(8,128)(2,1)S(1)} %collective-permute-done.10.near, ...), custom_call_target="tpu_custom_call" | custom-call | tf_op jit(solution)/shard_map/pallas_call | solution.py:419
  41.1 0.7 %shard_map.185 = (f32[1,512,128]{2,1,0:T(8,128)S(1)}, bf16[1,512,128]{2,1,0:T(8,128)(2,1)S(1)}) custom-call(bf16[1024,128]{1,0:T(8,128)(2,1)S(1)} %get-tuple-element.56.recv_hits, bf16[128,512]{1,0:T(8,128)(2,1)S(1)} %get-tuple-element.78.back, bf16[1024,512]{1,0:T(8,128)(2,1)S(1)} %get-tuple-element.77.edge_slope, ...), custom_call_target="tpu_custom_call" | custom-call | tf_op jit(solution)/shard_map/pallas_call | solution.py:419
  42.2 1.5 %collective-permute-start.15 = (bf16[320,128]{1,0:T(8,128)(2,1)S(1)}, bf16[320,128]{1,0:T(8,128)(2,1)S(1)}, u32[]{:S(2)}, u32[]{:S(2)}) collective-permute-start(bf16[320,128]{1,0:T(8,128)(2,1)S(1)} %bitcast.10), channel_id=1, source_target_pairs={{0,2},{2,0},{1,3},{3,1},{4,6},{6,4},{5,7},{7,5},{8,10},{10,8},{9,1... | collective-permute-start | bytes 245768 | tf_op jit(solution)/shard_map/ppermute | solution.py:451
  44.3 0.6 %shard_map.186.kept = f32[512,128]{1,0:T(8,128)S(1)} custom-call(bf16[1024,128]{1,0:T(8,128)(2,1)S(1)} %get-tuple-element.56.recv_hits, bf16[128,512]{1,0:T(8,128)(2,1)S(1)} %get-tuple-element.78.back, bf16[1024,512]{1,0:T(8,128)(2,1)S(1)} %get-tuple-element.77.edge_slope, bf16[512,1024]{1,0:T(8,128)(2,1)S(1)} %get-tuple-element.76.senders, ...), custom_call_target="tpu_custom_call" | custom-call | tf_op jit(solution)/shard_map/pallas_call | solution.py:419
  44.9 2.6 %collective-permute-done.15.refs_0_ = bf16[320,128]{1,0:T(8,128)(2,1)S(1)} collective-permute-done((bf16[320,128]{1,0:T(8,128)(2,1)S(1)}, bf16[320,128]{1,0:T(8,128)(2,1)S(1)}, u32[]{:S(2)}, u32[]{:S(2)}) %collective-permute-start.15) | collective-permute-done | bytes 81952 | tf_op jit(solution)/shard_map/ppermute | solution.py:451
  47.8 1.1 %collective-permute-start.16 = (bf16[2,128,128]{2,1,0:T(8,128)(2,1)S(1)}, bf16[2,128,128]{2,1,0:T(8,128)(2,1)S(1)}, u32[]{:S(2)}, u32[]{:S(2)}) collective-permute-start(bf16[2,128,128]{2,1,0:T(8,128)(2,1)S(1)} %get-tuple-element.85), channel_id=1, source_target_pairs={{0,12},{4,8},{8,4},{12,0},{1,13},{5,9},{9,5},{13,1},{2,14},{6,10},... | collective-permute-start | bytes 196616 | tf_op jit(solution)/shard_map/ppermute | solution.py:456
  48.9 2.5 %collective-permute-start.17 = (bf16[2,128,128]{2,1,0:T(8,128)(2,1)S(1)}, bf16[2,128,128]{2,1,0:T(8,128)(2,1)S(1)}, u32[]{:S(2)}, u32[]{:S(2)}) collective-permute-start(bf16[2,128,128]{2,1,0:T(8,128)(2,1)S(1)} %get-tuple-element.86), channel_id=1, source_target_pairs={{0,8},{4,12},{8,0},{12,4},{1,9},{5,13},{9,1},{13,5},{2,10},{6,14},... | collective-permute-start | bytes 196616 | tf_op jit(solution)/shard_map/ppermute | solution.py:456
  51.4 1.0 %collective-permute-start.19 = (bf16[2,128,128]{2,1,0:T(8,128)(2,1)S(1)}, bf16[2,128,128]{2,1,0:T(8,128)(2,1)S(1)}, u32[]{:S(2)}, u32[]{:S(2)}) collective-permute-start(bf16[2,128,128]{2,1,0:T(8,128)(2,1)S(1)} %get-tuple-element.89), channel_id=1, source_target_pairs={{0,4},{4,0},{8,12},{12,8},{1,5},{5,1},{9,13},{13,9},{2,6},{6,2},{1... | collective-permute-start | bytes 196616 | tf_op jit(solution)/shard_map/ppermute | solution.py:456
  52.3 1.8 %collective-permute-done.16.refs_0_ = bf16[2,128,128]{2,1,0:T(8,128)(2,1)S(1)} collective-permute-done((bf16[2,128,128]{2,1,0:T(8,128)(2,1)S(1)}, bf16[2,128,128]{2,1,0:T(8,128)(2,1)S(1)}, u32[]{:S(2)}, u32[]{:S(2)}) %collective-permute-start.16) | collective-permute-done | bytes 65568 | tf_op jit(solution)/shard_map/ppermute | solution.py:456
  54.2 2.4 %collective-permute-done.17.refs_1_ = bf16[2,128,128]{2,1,0:T(8,128)(2,1)S(1)} collective-permute-done((bf16[2,128,128]{2,1,0:T(8,128)(2,1)S(1)}, bf16[2,128,128]{2,1,0:T(8,128)(2,1)S(1)}, u32[]{:S(2)}, u32[]{:S(2)}) %collective-permute-start.17) | collective-permute-done | bytes 65568 | tf_op jit(solution)/shard_map/ppermute | solution.py:456
  56.8 0.7 %shard_map.190 = (f32[128,128]{1,0:T(8,128)}, f32[128,128]{1,0:T(8,128)}) custom-call(bf16[2,128,128]{2,1,0:T(8,128)(2,1)S(1)} %collective-permute-done.16.refs_0_, bf16[2,128,128]{2,1,0:T(8,128)(2,1)S(1)} %collective-permute-done.17.refs_1_, bf16[2,128,128]{2,1,0:T(8,128)(2,1)S(1)} %collective-permute-done.19.refs_2_, ...), custom_call_target="tpu_custom_call" | custom-call | tf_op jit(solution)/shard_map/pallas_call | solution.py:419
  (46 shorter events, 5.0 us)
Async XLA Ops:
  0.6 15.4 %collective-permute-start.1 = (bf16[3,227,360]{2,1,0:T(8,128)(2,1)}, bf16[3,227,360]{2,1,0:T(8,128)(2,1)S(1)}, u32[]{:S(2)}, u32[]{:S(2)}) collective-permute-start(bf16[3,227,360]{2,1,0:T(8,128)(2,1)} %bitcast.5), channel_id=1, source_target_pairs={{0,1},{1,0},{2,3},{3,2},{4,8},{5,9},{6,10},{7,11},{8,4},{9,5},{10,... | collective-permute-start | bytes 1470968 | tf_op jit(solution)/shard_map/ppermute | solution.py:480
  1.2 16.3 %collective-permute-start = (bf16[3,227,360]{2,1,0:T(8,128)(2,1)}, bf16[3,227,360]{2,1,0:T(8,128)(2,1)S(1)}, u32[]{:S(2)}, u32[]{:S(2)}) collective-permute-start(bf16[3,227,360]{2,1,0:T(8,128)(2,1)} %bitcast.6), channel_id=1, source_target_pairs={{0,4},{4,0},{8,12},{12,8},{1,5},{5,1},{9,13},{13,9},{2,6},{6,2},{1... | collective-permute-start | bytes 1470968 | tf_op jit(solution)/shard_map/ppermute | solution.py:479
  7.3 1.0 %copy-start = (bf16[3,360,227]{1,2,0:T(8,128)(2,1)S(1)}, bf16[3,360,227]{1,2,0:T(8,128)(2,1)}, u32[]{:S(2)}) copy-start(bf16[3,360,227]{1,2,0:T(8,128)(2,1)} %param.16) | copy-start | bytes 1470964
  8.4 6.8 %copy-start.3 = (bf16[512,512]{1,0:T(8,128)(2,1)S(1)}, bf16[512,512]{1,0:T(8,128)(2,1)}, u32[]{:S(2)}) copy-start(bf16[512,512]{1,0:T(8,128)(2,1)} %param.21) | copy-start | bytes 1572868
  8.4 6.9 %copy-start.4 = (bf16[512,512]{1,0:T(8,128)(2,1)S(1)}, bf16[512,512]{1,0:T(8,128)(2,1)}, u32[]{:S(2)}) copy-start(bf16[512,512]{1,0:T(8,128)(2,1)} %param.22) | copy-start | bytes 1572868
  8.4 6.9 %copy-start.5 = (bf16[512,512]{1,0:T(8,128)(2,1)S(1)}, bf16[512,512]{1,0:T(8,128)(2,1)}, u32[]{:S(2)}) copy-start(bf16[512,512]{1,0:T(8,128)(2,1)} %param.23) | copy-start | bytes 1572868
  8.4 7.0 %copy-start.6 = (bf16[227,512]{1,0:T(8,128)(2,1)S(1)}, bf16[227,512]{1,0:T(8,128)(2,1)}, u32[]{:S(2)}) copy-start(bf16[227,512]{1,0:T(8,128)(2,1)} %param.17) | copy-start | bytes 697348
  10.3 5.1 %copy-start.1 = (bf16[32,512]{1,0:T(8,128)(2,1)S(1)}, bf16[32,512]{1,0:T(8,128)(2,1)}, u32[]{:S(2)}) copy-start(bf16[32,512]{1,0:T(8,128)(2,1)} %mesh_in.3) | copy-start | bytes 98308
  10.3 5.1 %collective-permute-start.3 = (bf16[32,512]{1,0:T(8,128)(2,1)}, bf16[32,512]{1,0:T(8,128)(2,1)S(1)}, u32[]{:S(2)}, u32[]{:S(2)}) collective-permute-start(bf16[32,512]{1,0:T(8,128)(2,1)} %mesh_in.3), channel_id=1, source_target_pairs={{0,3},{1,2},{2,1},{3,0},{4,7},{5,6},{6,5},{7,4},{8,11},{9,10},{10,... | collective-permute-start | bytes 98312 | tf_op jit(solution)/shard_map/ppermute | solution.py:506
  10.7 4.7 %collective-permute-start.2 = (bf16[32,512]{1,0:T(8,128)(2,1)}, bf16[32,512]{1,0:T(8,128)(2,1)S(1)}, u32[]{:S(2)}, u32[]{:S(2)}) collective-permute-start(bf16[32,512]{1,0:T(8,128)(2,1)} %mesh_in.3), channel_id=1, source_target_pairs={{0,1},{1,0},{2,3},{3,2},{4,5},{5,4},{6,7},{7,6},{8,9},{9,8},{10,11... | collective-permute-start | bytes 98312 | tf_op jit(solution)/shard_map/ppermute | solution.py:505
  21.6 1.7 %collective-permute-start.4 = (bf16[32,512]{1,0:T(8,128)(2,1)S(1)}, bf16[32,512]{1,0:T(8,128)(2,1)S(1)}, u32[]{:S(2)}, u32[]{:S(2)}) collective-permute-start(bf16[32,512]{1,0:T(8,128)(2,1)S(1)} %get-tuple-element.58), channel_id=1, source_target_pairs={{0,1},{1,0},{2,3},{3,2},{4,5},{5,4},{6,7},{7,6},{8,9},{9,8},{10,11... | collective-permute-start | bytes 98312 | tf_op jit(solution)/shard_map/ppermute | solution.py:534
  21.7 3.4 %collective-permute-start.5 = (bf16[32,512]{1,0:T(8,128)(2,1)S(1)}, bf16[32,512]{1,0:T(8,128)(2,1)S(1)}, u32[]{:S(2)}, u32[]{:S(2)}) collective-permute-start(bf16[32,512]{1,0:T(8,128)(2,1)S(1)} %get-tuple-element.59), channel_id=1, source_target_pairs={{0,3},{1,2},{2,1},{3,0},{4,7},{5,6},{6,5},{7,4},{8,11},{9,10},{10,... | collective-permute-start | bytes 98312 | tf_op jit(solution)/shard_map/ppermute | solution.py:533
  25.1 4.8 %copy-start.2 = (bf16[32,512]{1,0:T(8,128)(2,1)S(1)}, bf16[32,512]{1,0:T(8,128)(2,1)}, u32[]{:S(2)}) copy-start(bf16[32,512]{1,0:T(8,128)(2,1)} %d_out.3) | copy-start | bytes 98308
  25.3 4.5 %collective-permute-start.7 = (bf16[64,512]{1,0:T(8,128)(2,1)S(1)}, bf16[64,512]{1,0:T(8,128)(2,1)S(1)}, u32[]{:S(2)}, u32[]{:S(2)}) collective-permute-start(bf16[64,512]{1,0:T(8,128)(2,1)S(1)} %get-tuple-element.60.own.nodes), channel_id=1, source_target_pairs={{0,4},{4,0},{8,12},{12,8},{1,5},{5,1},{9,13},{13,9},{2,6},{6,2},{1... | collective-permute-start | bytes 196616 | tf_op jit(solution)/shard_map/ppermute | solution.py:540
  27.1 2.7 %collective-permute-start.6 = (bf16[64,512]{1,0:T(8,128)(2,1)S(1)}, bf16[64,512]{1,0:T(8,128)(2,1)S(1)}, u32[]{:S(2)}, u32[]{:S(2)}) collective-permute-start(bf16[64,512]{1,0:T(8,128)(2,1)S(1)} %get-tuple-element.60.own.nodes), channel_id=1, source_target_pairs={{0,1},{1,0},{2,3},{3,2},{4,8},{5,9},{6,10},{7,11},{8,4},{9,5},{10,... | collective-permute-start | bytes 196616 | tf_op jit(solution)/shard_map/ppermute | solution.py:541
  31.5 4.3 %collective-permute-start.8 = (bf16[64,512]{1,0:T(8,128)(2,1)S(1)}, bf16[64,512]{1,0:T(8,128)(2,1)S(1)}, u32[]{:S(2)}, u32[]{:S(2)}) collective-permute-start(bf16[64,512]{1,0:T(8,128)(2,1)S(1)} %get-tuple-element.66), channel_id=1, source_target_pairs={{0,4},{4,0},{8,12},{12,8},{1,5},{5,1},{9,13},{13,9},{2,6},{6,2},{1... | collective-permute-start | bytes 196616 | tf_op jit(solution)/shard_map/ppermute | solution.py:560
  33.4 2.4 %collective-permute-start.9 = (bf16[64,512]{1,0:T(8,128)(2,1)S(1)}, bf16[64,512]{1,0:T(8,128)(2,1)S(1)}, u32[]{:S(2)}, u32[]{:S(2)}) collective-permute-start(bf16[64,512]{1,0:T(8,128)(2,1)S(1)} %get-tuple-element.67), channel_id=1, source_target_pairs={{0,1},{1,0},{2,3},{3,2},{4,8},{5,9},{6,10},{7,11},{8,4},{9,5},{10,... | collective-permute-start | bytes 196616 | tf_op jit(solution)/shard_map/ppermute | solution.py:561
  33.4 4.5 %collective-permute-start.11 = (bf16[64,512]{1,0:T(8,128)(2,1)S(1)}, bf16[64,512]{1,0:T(8,128)(2,1)S(1)}, u32[]{:S(2)}, u32[]{:S(2)}) collective-permute-start(bf16[64,512]{1,0:T(8,128)(2,1)S(1)} %get-tuple-element.60.own.nodes), channel_id=1, source_target_pairs={{0,2},{2,0},{1,3},{3,1},{4,6},{6,4},{5,7},{7,5},{8,10},{10,8},{9,1... | collective-permute-start | bytes 196616 | tf_op jit(solution)/shard_map/ppermute | solution.py:451
  35.9 2.0 %collective-permute-start.10 = (bf16[48,512]{1,0:T(8,128)(2,1)S(1)}, bf16[48,512]{1,0:T(8,128)(2,1)S(1)}, u32[]{:S(2)}, u32[]{:S(2)}) collective-permute-start(bf16[48,512]{1,0:T(8,128)(2,1)S(1)} %get-tuple-element.72), channel_id=1, source_target_pairs={{0,1},{1,0},{2,3},{3,2},{4,5},{5,4},{6,7},{7,6},{8,9},{9,8},{10,11... | collective-permute-start | bytes 147464 | tf_op jit(solution)/shard_map/ppermute | solution.py:574
  36.0 3.6 %collective-permute-start.12 = (bf16[48,512]{1,0:T(8,128)(2,1)S(1)}, bf16[48,512]{1,0:T(8,128)(2,1)S(1)}, u32[]{:S(2)}, u32[]{:S(2)}) collective-permute-start(bf16[48,512]{1,0:T(8,128)(2,1)S(1)} %get-tuple-element.74), channel_id=1, source_target_pairs={{0,3},{1,2},{2,1},{3,0},{4,7},{5,6},{6,5},{7,4},{8,11},{9,10},{10,... | collective-permute-start | bytes 147464 | tf_op jit(solution)/shard_map/ppermute | solution.py:573
  40.6 1.5 %collective-permute-start.14 = (bf16[1,512,128]{2,1,0:T(8,128)(2,1)S(1)}, bf16[1,512,128]{2,1,0:T(8,128)(2,1)S(1)}, u32[]{:S(2)}, u32[]{:S(2)}) collective-permute-start(bf16[1,512,128]{2,1,0:T(8,128)(2,1)S(1)} %bitcast.8), channel_id=1, source_target_pairs={{0,1},{1,0},{2,3},{3,2},{4,5},{5,4},{6,7},{7,6},{8,9},{9,8},{10,11... | collective-permute-start | bytes 393224 | tf_op jit(solution)/shard_map/ppermute | solution.py:451
  41.8 2.4 %collective-permute-start.13 = (bf16[512,128]{1,0:T(8,128)(2,1)S(1)}, bf16[512,128]{1,0:T(8,128)(2,1)S(1)}, u32[]{:S(2)}, u32[]{:S(2)}) collective-permute-start(bf16[512,128]{1,0:T(8,128)(2,1)S(1)} %bitcast.9), channel_id=1, source_target_pairs={{0,1},{1,0},{2,3},{3,2},{4,5},{5,4},{6,7},{7,6},{8,9},{9,8},{10,11... | collective-permute-start | bytes 393224 | tf_op jit(solution)/shard_map/ppermute | solution.py:451
  42.2 5.3 %collective-permute-start.15 = (bf16[320,128]{1,0:T(8,128)(2,1)S(1)}, bf16[320,128]{1,0:T(8,128)(2,1)S(1)}, u32[]{:S(2)}, u32[]{:S(2)}) collective-permute-start(bf16[320,128]{1,0:T(8,128)(2,1)S(1)} %bitcast.10), channel_id=1, source_target_pairs={{0,2},{2,0},{1,3},{3,1},{4,6},{6,4},{5,7},{7,5},{8,10},{10,8},{9,1... | collective-permute-start | bytes 245768 | tf_op jit(solution)/shard_map/ppermute | solution.py:451
  43.7 7.6 %collective-permute-start.18 = (bf16[256,128]{1,0:T(8,128)(2,1)S(1)}, bf16[256,128]{1,0:T(8,128)(2,1)S(1)}, u32[]{:S(2)}, u32[]{:S(2)}) collective-permute-start(bf16[256,128]{1,0:T(8,128)(2,1)S(1)} %bitcast.11), channel_id=1, source_target_pairs={{0,2},{2,0},{1,3},{3,1},{4,6},{6,4},{5,7},{7,5},{8,10},{10,8},{9,1... | collective-permute-start | bytes 196616 | tf_op jit(solution)/shard_map/ppermute | solution.py:451
  47.8 6.4 %collective-permute-start.16 = (bf16[2,128,128]{2,1,0:T(8,128)(2,1)S(1)}, bf16[2,128,128]{2,1,0:T(8,128)(2,1)S(1)}, u32[]{:S(2)}, u32[]{:S(2)}) collective-permute-start(bf16[2,128,128]{2,1,0:T(8,128)(2,1)S(1)} %get-tuple-element.85), channel_id=1, source_target_pairs={{0,12},{4,8},{8,4},{12,0},{1,13},{5,9},{9,5},{13,1},{2,14},{6,10},... | collective-permute-start | bytes 196616 | tf_op jit(solution)/shard_map/ppermute | solution.py:456
  48.9 7.7 %collective-permute-start.17 = (bf16[2,128,128]{2,1,0:T(8,128)(2,1)S(1)}, bf16[2,128,128]{2,1,0:T(8,128)(2,1)S(1)}, u32[]{:S(2)}, u32[]{:S(2)}) collective-permute-start(bf16[2,128,128]{2,1,0:T(8,128)(2,1)S(1)} %get-tuple-element.86), channel_id=1, source_target_pairs={{0,8},{4,12},{8,0},{12,4},{1,9},{5,13},{9,1},{13,5},{2,10},{6,14},... | collective-permute-start | bytes 196616 | tf_op jit(solution)/shard_map/ppermute | solution.py:456
  51.4 5.5 %collective-permute-start.19 = (bf16[2,128,128]{2,1,0:T(8,128)(2,1)S(1)}, bf16[2,128,128]{2,1,0:T(8,128)(2,1)S(1)}, u32[]{:S(2)}, u32[]{:S(2)}) collective-permute-start(bf16[2,128,128]{2,1,0:T(8,128)(2,1)S(1)} %get-tuple-element.89), channel_id=1, source_target_pairs={{0,4},{4,0},{8,12},{12,8},{1,5},{5,1},{9,13},{13,9},{2,6},{6,2},{1... | collective-permute-start | bytes 196616 | tf_op jit(solution)/shard_map/ppermute | solution.py:456

commit v18 on v17

--- a/solution.py
+++ b/solution.py
@@ -154,25 +154,32 @@
     pre_out[...] = mm(recv_hits[...], table)
 
 
-def live_blocks(count, edges, work, rest):
-    work(slice(0, edges // 2))
-    for first in (edges // 2, 3 * edges // 4):
-        part_of = slice(first, first + edges // 4)
-        pl.when(count[0, 0] > first)(lambda part_of=part_of: work(part_of))
-        pl.when(count[0, 0] <= first)(lambda part_of=part_of: rest(part_of))
+def live_slots(count, edges, work, rest):
+    lower = 0
+    for size in (edges // 2, 3 * edges // 4, edges):
+
+        def case(size=size):
+            work([slice(0, size // 2), slice(size // 2, size)])
+            if size < edges:
+                rest(slice(size, edges))
+
+        live = count[0, 0]
+        pl.when((live > lower) & (live <= size) if size < edges else live > lower)(case)
+        lower = size
 
 
 def gather_kernel(count, halo, hits, rows, rows_out, wide):
     fill(wide, halo, wide.shape[1] // halo.shape[0], 0)
 
-    def work(part_of):
+    def work(parts):
+        part_of = slice(0, parts[-1].stop)
         gathered = mm_nt(hits[part_of], wide[...]).astype(BF16)
         rows_out[part_of] = rows[part_of] + gathered
 
     def rest(part_of):
         rows_out[part_of] = jnp.zeros_like(rows_out[part_of])
 
-    live_blocks(count, rows.shape[0], work, rest)
+    live_slots(count, rows.shape[0], work, rest)
 
 
 def encode_kernel(
@@ -181,27 +188,29 @@
 ):
     half = recv_rows.shape[0] // 2
     fill(wide, near, wide.shape[1] // near.shape[0], 0)
-    part_out[...] = jnp.zeros_like(part_out)
-
-    def work(part_of):
-        raw = rows[part_of] + mm_nt(near_hits[part_of], wide[...]).astype(BF16)
-        latent, _ = silu_parts(mm(raw, stack[stack.shape[0] - raw.shape[1] :]))
-        latent = latent.astype(BF16)
-        senders_out[part_of] = latent
-        pre = mm(latent, weight(stack, GS)) + recv_pre[part_of]
-        value, slope = silu_parts(pre)
-        slope_out[part_of] = slope.astype(BF16)
-        part_out[...] += mm(recv_rows[:, part_of], value.astype(BF16))
+
+    def work(parts):
+        sums = None
+        for part_of in parts:
+            raw = rows[part_of] + mm_nt(near_hits[part_of], wide[...]).astype(BF16)
+            latent, _ = silu_parts(mm(raw, stack[stack.shape[0] - raw.shape[1] :]))
+            latent = latent.astype(BF16)
+            senders_out[part_of] = latent
+            pre = mm(latent, weight(stack, GS)) + recv_pre[part_of]
+            value, slope = silu_parts(pre)
+            slope_out[part_of] = slope.astype(BF16)
+            part = mm(recv_rows[:, part_of], value.astype(BF16))
+            sums = part if sums is None else sums + part
+        part_out[...] = sums
+        even = even_on("lat")
+        near_out[...] = jnp.where(even, sums[half:], sums[:half]).astype(BF16)
+        far_out[...] = jnp.where(even, sums[:half], sums[half:]).astype(BF16)
 
     def rest(part_of):
         senders_out[part_of] = jnp.zeros_like(senders_out[part_of])
         slope_out[part_of] = jnp.zeros_like(slope_out[part_of])
 
-    live_blocks(count, rows.shape[0], work, rest)
-    sums = part_out[...]
-    even = even_on("lat")
-    near_out[...] = jnp.where(even, sums[half:], sums[:half]).astype(BF16)
-    far_out[...] = jnp.where(even, sums[:half], sums[half:]).astype(BF16)
+    live_slots(count, rows.shape[0], work, rest)
 
 
 def node_kernel(part, near, far, mesh_near, mesh_far, mesh_in, stack, mesh_out, slope_out):

time: 57.8 us -> 56.5 us (0.978)
  Pallas kernels: 14.4 us -> 13 us
    pallas_call x16, Pallas kernels: 14.4 us -> 13 us  [call(): pl.pallas_call(kernel, out_shape=[jax.ShapeDtypeStruct(shape, dtype) for...]
where the time goes in v18:
time: 56.5 us; the launch traced here: 56.1 us
  starting transfers between devices  22.3 us (39%)
  waiting for transfers between devices  13.5 us (24%)
  Pallas kernels  13 us (23%)
  local copies, waits for them, and re-layouts  4.43 us (8%)
  between operations  2.17 us (4%)
  other arithmetic  0.74 us (1%)
    pallas_call x16, Pallas kernels, call(): pl.pallas_call(kernel, out_shape=[jax.ShapeDtypeStruct(shape, dtype) for...  13 us
    ppermute x3, starting transfers between devices, over_band(): return lax.ppermute(x, 'band', [(b, b ^ partner) for b in range(count)])  4.52 us
    unnamed x20, local copies, waits for them, and re-layouts  4.41 us
    ppermute x5, starting transfers between devices, shifted(): lax.ppermute(x, axis, [(i, (i + shift) % count) for i in range(count)])  4.24 us
    ppermute x3, waiting for transfers between devices, over_band(): return lax.ppermute(x, 'band', [(b, b ^ partner) for b in range(count)])  4.18 us
    ppermute x1, starting transfers between devices, on_device(): raw_near = lax.ppermute(grid, 'band', band_near)  4.15 us
    ppermute x2, waiting for transfers between devices, on_device(): from_far = lax.ppermute(to_far, around, ring_far)  3.42 us
    ppermute x2, starting transfers between devices, on_device(): from_far = lax.ppermute(to_far, around, ring_far)  3.21 us
  transfers between devices with their start and end apart: 20, of which 10 were waited for; matrix products, arithmetic and copies ran while one was open for 7% of the time, Pallas kernels for 11%

profile of v18, /device:TPU:0, one launch (start us, length us, event | category | flops | bytes accessed | tf_op | source)
XLA Modules:
  0.0 56.1 jit_solution(17392051914042887592)
XLA Ops:
  1.2 4.1 %collective-permute-start = (bf16[3,227,360]{2,1,0:T(8,128)(2,1)}, bf16[3,227,360]{2,1,0:T(8,128)(2,1)S(1)}, u32[]{:S(2)}, u32[]{:S(2)}) collective-permute-start(bf16[3,227,360]{2,1,0:T(8,128)(2,1)} %bitcast.6), channel_id=1, source_target_pairs={{0,4},{4,0},{8,12},{12,8},{1,5},{5,1},{9,13},{13,9},{2,6},{6,2},{1... | collective-permute-start | bytes 1470968 | tf_op jit(solution)/shard_map/ppermute | solution.py:488
  6.6 0.7 %pad_add_fusion.indices = s32[1,1,3072]{2,1,0:T(1,128)S(1)} fusion(s32[1,1,512]{2,1,0:T(1,128)} %param.30, s32[1,1,512]{2,1,0:T(1,128)} %param.29, s32[1,1,1024]{2,1,0:T(1,128)} %param.27, s32[1,1,1024]{2,1,0:T(1,128)} %param.26), kind=kLoop, calls=%fused_computation.7 | loop fusion | flops 9216 | bytes 24576 | tf_op jit(solution)/shard_map/concatenate | solution.py:492
  7.3 1.0 %copy-done = bf16[3,360,227]{1,2,0:T(8,128)(2,1)S(1)} copy-done((bf16[3,360,227]{1,2,0:T(8,128)(2,1)S(1)}, bf16[3,360,227]{1,2,0:T(8,128)(2,1)}, u32[]{:S(2)}) %copy-start) | copy-done | bytes 490344
  8.4 1.9 %shard_map.175 = (bf16[1024,227]{1,0:T(8,128)(2,1)S(1)}, bf16[1024,128]{1,0:T(8,128)(2,1)S(1)}, bf16[64,1024]{1,0:T(8,128)(2,1)S(1)}, bf16[512,128]{1,0:T(8,128)...) custom-call(s32[1,1]{1,0:T(1,128)S(6)} %copy.25.count, ...), custom_call_target="tpu_custom_call" | custom-call | tf_op jit(solution)/shard_map/pallas_call | solution.py:428
  10.7 1.2 %collective-permute-start.2 = (bf16[32,512]{1,0:T(8,128)(2,1)}, bf16[32,512]{1,0:T(8,128)(2,1)S(1)}, u32[]{:S(2)}, u32[]{:S(2)}) collective-permute-start(bf16[32,512]{1,0:T(8,128)(2,1)} %mesh_in.3), channel_id=1, source_target_pairs={{0,1},{1,0},{2,3},{3,2},{4,5},{5,4},{6,7},{7,6},{8,9},{9,8},{10,11... | collective-permute-start | bytes 98312 | tf_op jit(solution)/shard_map/ppermute | solution.py:514
  12.0 1.1 %constant_dynamic-update-slice_fusion.6 = bf16[3299,512]{1,0:T(8,128)(2,1)S(1)} fusion(bf16[512,512]{1,0:T(8,128)(2,1)} %param.18), kind=kLoop, calls=%fused_computation.6 | loop fusion | bytes 1048576
  13.1 1.1 %constant_dynamic-update-slice_fusion.5 = bf16[3299,512]{1,0:T(8,128)(2,1)S(1)} fusion(bf16[3299,512]{1,0:T(8,128)(2,1)S(1)} %constant_dynamic-update-slice_fusion.6, bf16[512,512]{1,0:T(8,128)(2,1)} %param.19), kind=kLoop, calls=%fused_computation.5 | loop fusion | bytes 1048576
  14.1 1.1 %constant_dynamic-update-slice_fusion.4 = bf16[3299,512]{1,0:T(8,128)(2,1)S(1)} fusion(bf16[3299,512]{1,0:T(8,128)(2,1)S(1)} %constant_dynamic-update-slice_fusion.5, bf16[512,512]{1,0:T(8,128)(2,1)} %param.20), kind=kLoop, calls=%fused_computation.4 | loop fusion | bytes 1048576
  15.4 0.6 %shard_map.177.recv_pre = f32[1024,512]{1,0:T(8,128)S(1)} custom-call(bf16[32,512]{1,0:T(8,128)(2,1)S(1)} %collective-permute-done.2.near.mesh_near, bf16[32,512]{1,0:T(8,128)(2,1)S(1)} %collective-permute-done.3.far.mesh_far, bf16[32,512]{1,0:T(8,128)(2,1)S(1)} %copy-done.1, bf16[1024,128]{1,0:T(8,128)(2,1)S(1)} %get-tuple-element.56.recv_hits, ...), custom_call_target="tpu_custom_call" | custom-call | tf_op jit(solution)/shard_map/pallas_call | solution.py:428
  16.1 1.0 %shard_map.176.rows = bf16[1024,227]{1,0:T(8,128)(2,1)S(1)} custom-call(s32[1,1]{1,0:T(1,128)S(6)} %copy.25.count, bf16[3,227,360]{2,1,0:T(8,128)(2,1)S(1)} %collective-permute-done.1.halo, bf16[1024,1152]{1,0:T(8,128)(2,1)S(1)} %get-tuple-element.52.hits, bf16[1024,227]{1,0:T(8,128)(2,1)S(1)} %get-tuple-element.54.rows), custom_call_target="tpu_custom_call" | custom-call | tf_op jit(solution)/shard_map/pallas_call | solution.py:428
  17.4 3.1 %shard_map.178 = (bf16[1024,512]{1,0:T(8,128)(2,1)S(1)}, bf16[1024,512]{1,0:T(8,128)(2,1)S(1)}, f32[64,512]{1,0:T(8,128)S(1)}, bf16[32,512]{1,0:T(8,128)(2,1)S(1)}, bf16[32,512]{1,0:T(8,128)(2,1)S(1)}) custom-call(s32[1,1]{1,0:T(1,128)S(6)} %copy.25.count, bf16[3,227,360]{2,1,0:T(8,128)(2,1)S(1)} %collective-permute-done.near, ...), custom_call_target="tpu_custom_call" | custom-call | tf_op jit(solution)/shard_map/pallas_call | solution.py:428
  20.6 1.6 %collective-permute-start.5 = (bf16[32,512]{1,0:T(8,128)(2,1)S(1)}, bf16[32,512]{1,0:T(8,128)(2,1)S(1)}, u32[]{:S(2)}, u32[]{:S(2)}) collective-permute-start(bf16[32,512]{1,0:T(8,128)(2,1)S(1)} %get-tuple-element.59), channel_id=1, source_target_pairs={{0,3},{1,2},{2,1},{3,0},{4,7},{5,6},{6,5},{7,4},{8,11},{9,10},{10,... | collective-permute-start | bytes 98312 | tf_op jit(solution)/shard_map/ppermute | solution.py:542
  22.2 1.8 %collective-permute-done.5.far = bf16[32,512]{1,0:T(8,128)(2,1)S(1)} collective-permute-done((bf16[32,512]{1,0:T(8,128)(2,1)S(1)}, bf16[32,512]{1,0:T(8,128)(2,1)S(1)}, u32[]{:S(2)}, u32[]{:S(2)}) %collective-permute-start.5) | collective-permute-done | bytes 32800 | tf_op jit(solution)/shard_map/ppermute | solution.py:542
  24.3 1.8 %collective-permute-start.7 = (bf16[64,512]{1,0:T(8,128)(2,1)S(1)}, bf16[64,512]{1,0:T(8,128)(2,1)S(1)}, u32[]{:S(2)}, u32[]{:S(2)}) collective-permute-start(bf16[64,512]{1,0:T(8,128)(2,1)S(1)} %get-tuple-element.60.own.nodes), channel_id=1, source_target_pairs={{0,4},{4,0},{8,12},{12,8},{1,5},{5,1},{9,13},{13,9},{2,6},{6,2},{1... | collective-permute-start | bytes 196616 | tf_op jit(solution)/shard_map/ppermute | solution.py:549
  26.2 0.7 %shard_map.180.own_pre = f32[512,512]{1,0:T(8,128)S(1)} custom-call(bf16[512,128]{1,0:T(8,128)(2,1)S(1)} %get-tuple-element.48.own_hits, bf16[512,64]{1,0:T(8,128)(2,1)S(1)} %get-tuple-element.49.to_hits, bf16[64,512]{1,0:T(8,128)(2,1)S(1)} %get-tuple-element.60.own.nodes, bf16[3299,512]{1,0:T(8,128)(2,1)S(1)} %constant_dynamic-update-slice_fusion.stack), custom_call_target="tpu_custom_call" | custom-call | tf_op jit(solution)/shard_map/pallas_call | solution.py:428
  26.9 1.9 %collective-permute-done.7.near = bf16[64,512]{1,0:T(8,128)(2,1)S(1)} collective-permute-done((bf16[64,512]{1,0:T(8,128)(2,1)S(1)}, bf16[64,512]{1,0:T(8,128)(2,1)S(1)}, u32[]{:S(2)}, u32[]{:S(2)}) %collective-permute-start.7) | collective-permute-done | bytes 65568 | tf_op jit(solution)/shard_map/ppermute | solution.py:549
  28.8 1.7 %shard_map.181 = (bf16[32,512]{1,0:T(8,128)(2,1)}, f32[192,512]{1,0:T(8,128)S(1)}, bf16[32,512]{1,0:T(8,128)(2,1)S(1)}, bf16[64,512]{1,0:T(8,128)(2,1)S(1)}, bf16[64,512]{1,0:T(8,128)(2,1)S(1)}) custom-call(f32[512,512]{1,0:T(8,128)S(1)} %shard_map.180.own_pre, bf16[512,256]{1,0:T(8,128)(2,1)S(1)} %get-tuple-element.61.outer_hits, ...), custom_call_target="tpu_custom_call" | custom-call | tf_op jit(solution)/shard_map/pallas_call | solution.py:428
  30.5 1.9 %collective-permute-start.8 = (bf16[64,512]{1,0:T(8,128)(2,1)S(1)}, bf16[64,512]{1,0:T(8,128)(2,1)S(1)}, u32[]{:S(2)}, u32[]{:S(2)}) collective-permute-start(bf16[64,512]{1,0:T(8,128)(2,1)S(1)} %get-tuple-element.66), channel_id=1, source_target_pairs={{0,4},{4,0},{8,12},{12,8},{1,5},{5,1},{9,13},{13,9},{2,6},{6,2},{1... | collective-permute-start | bytes 196616 | tf_op jit(solution)/shard_map/ppermute | solution.py:569
  32.4 1.5 %collective-permute-start.11 = (bf16[64,512]{1,0:T(8,128)(2,1)S(1)}, bf16[64,512]{1,0:T(8,128)(2,1)S(1)}, u32[]{:S(2)}, u32[]{:S(2)}) collective-permute-start(bf16[64,512]{1,0:T(8,128)(2,1)S(1)} %get-tuple-element.60.own.nodes), channel_id=1, source_target_pairs={{0,2},{2,0},{1,3},{3,1},{4,6},{6,4},{5,7},{7,5},{8,10},{10,8},{9,1... | collective-permute-start | bytes 196616 | tf_op jit(solution)/shard_map/ppermute | solution.py:460
  34.9 1.6 %collective-permute-start.12 = (bf16[48,512]{1,0:T(8,128)(2,1)S(1)}, bf16[48,512]{1,0:T(8,128)(2,1)S(1)}, u32[]{:S(2)}, u32[]{:S(2)}) collective-permute-start(bf16[48,512]{1,0:T(8,128)(2,1)S(1)} %get-tuple-element.74), channel_id=1, source_target_pairs={{0,3},{1,2},{2,1},{3,0},{4,7},{5,6},{6,5},{7,4},{8,11},{9,10},{10,... | collective-permute-start | bytes 147464 | tf_op jit(solution)/shard_map/ppermute | solution.py:582
  36.9 1.6 %collective-permute-done.12.far = bf16[48,512]{1,0:T(8,128)(2,1)S(1)} collective-permute-done((bf16[48,512]{1,0:T(8,128)(2,1)S(1)}, bf16[48,512]{1,0:T(8,128)(2,1)S(1)}, u32[]{:S(2)}, u32[]{:S(2)}) %collective-permute-start.12) | collective-permute-done | bytes 49184 | tf_op jit(solution)/shard_map/ppermute | solution.py:582
  38.5 1.1 %shard_map.184 = (bf16[1,1,512,128]{3,2,1,0:T(8,128)(2,1)S(1)}, bf16[128,512]{1,0:T(8,128)(2,1)S(1)}, bf16[2,64,128]{2,1,0:T(8,128)(2,1)S(1)}) custom-call(bf16[1024,128]{1,0:T(8,128)(2,1)S(1)} %get-tuple-element.56.recv_hits, f32[64,512]{1,0:T(8,128)S(1)} %get-tuple-element.71.part, bf16[48,512]{1,0:T(8,128)(2,1)S(1)} %collective-permute-done.10.near, ...), custom_call_target="tpu_custom_call" | custom-call | tf_op jit(solution)/shard_map/pallas_call | solution.py:428
  40.1 0.7 %shard_map.185 = (f32[1,512,128]{2,1,0:T(8,128)S(1)}, bf16[1,512,128]{2,1,0:T(8,128)(2,1)S(1)}) custom-call(bf16[1024,128]{1,0:T(8,128)(2,1)S(1)} %get-tuple-element.56.recv_hits, bf16[128,512]{1,0:T(8,128)(2,1)S(1)} %get-tuple-element.78.back, bf16[1024,512]{1,0:T(8,128)(2,1)S(1)} %get-tuple-element.77.edge_slope, ...), custom_call_target="tpu_custom_call" | custom-call | tf_op jit(solution)/shard_map/pallas_call | solution.py:428
  41.1 1.6 %collective-permute-start.15 = (bf16[320,128]{1,0:T(8,128)(2,1)S(1)}, bf16[320,128]{1,0:T(8,128)(2,1)S(1)}, u32[]{:S(2)}, u32[]{:S(2)}) collective-permute-start(bf16[320,128]{1,0:T(8,128)(2,1)S(1)} %bitcast.10), channel_id=1, source_target_pairs={{0,2},{2,0},{1,3},{3,1},{4,6},{6,4},{5,7},{7,5},{8,10},{10,8},{9,1... | collective-permute-start | bytes 245768 | tf_op jit(solution)/shard_map/ppermute | solution.py:460
  43.2 0.6 %shard_map.186.kept = f32[512,128]{1,0:T(8,128)S(1)} custom-call(bf16[1024,128]{1,0:T(8,128)(2,1)S(1)} %get-tuple-element.56.recv_hits, bf16[128,512]{1,0:T(8,128)(2,1)S(1)} %get-tuple-element.78.back, bf16[1024,512]{1,0:T(8,128)(2,1)S(1)} %get-tuple-element.77.edge_slope, bf16[512,1024]{1,0:T(8,128)(2,1)S(1)} %get-tuple-element.76.senders, ...), custom_call_target="tpu_custom_call" | custom-call | tf_op jit(solution)/shard_map/pallas_call | solution.py:428
  43.9 2.6 %collective-permute-done.15.refs_0_ = bf16[320,128]{1,0:T(8,128)(2,1)S(1)} collective-permute-done((bf16[320,128]{1,0:T(8,128)(2,1)S(1)}, bf16[320,128]{1,0:T(8,128)(2,1)S(1)}, u32[]{:S(2)}, u32[]{:S(2)}) %collective-permute-start.15) | collective-permute-done | bytes 81952 | tf_op jit(solution)/shard_map/ppermute | solution.py:460
  46.7 2.0 %collective-permute-start.16 = (bf16[2,128,128]{2,1,0:T(8,128)(2,1)S(1)}, bf16[2,128,128]{2,1,0:T(8,128)(2,1)S(1)}, u32[]{:S(2)}, u32[]{:S(2)}) collective-permute-start(bf16[2,128,128]{2,1,0:T(8,128)(2,1)S(1)} %get-tuple-element.85), channel_id=1, source_target_pairs={{0,12},{4,8},{8,4},{12,0},{1,13},{5,9},{9,5},{13,1},{2,14},{6,10},... | collective-permute-start | bytes 196616 | tf_op jit(solution)/shard_map/ppermute | solution.py:465
  48.7 1.6 %collective-permute-start.17 = (bf16[2,128,128]{2,1,0:T(8,128)(2,1)S(1)}, bf16[2,128,128]{2,1,0:T(8,128)(2,1)S(1)}, u32[]{:S(2)}, u32[]{:S(2)}) collective-permute-start(bf16[2,128,128]{2,1,0:T(8,128)(2,1)S(1)} %get-tuple-element.86), channel_id=1, source_target_pairs={{0,8},{4,12},{8,0},{12,4},{1,9},{5,13},{9,1},{13,5},{2,10},{6,14},... | collective-permute-start | bytes 196616 | tf_op jit(solution)/shard_map/ppermute | solution.py:465
  50.3 1.0 %collective-permute-start.19 = (bf16[2,128,128]{2,1,0:T(8,128)(2,1)S(1)}, bf16[2,128,128]{2,1,0:T(8,128)(2,1)S(1)}, u32[]{:S(2)}, u32[]{:S(2)}) collective-permute-start(bf16[2,128,128]{2,1,0:T(8,128)(2,1)S(1)} %get-tuple-element.89), channel_id=1, source_target_pairs={{0,4},{4,0},{8,12},{12,8},{1,5},{5,1},{9,13},{13,9},{2,6},{6,2},{1... | collective-permute-start | bytes 196616 | tf_op jit(solution)/shard_map/ppermute | solution.py:465
  51.3 2.3 %collective-permute-done.16.refs_0_ = bf16[2,128,128]{2,1,0:T(8,128)(2,1)S(1)} collective-permute-done((bf16[2,128,128]{2,1,0:T(8,128)(2,1)S(1)}, bf16[2,128,128]{2,1,0:T(8,128)(2,1)S(1)}, u32[]{:S(2)}, u32[]{:S(2)}) %collective-permute-start.16) | collective-permute-done | bytes 65568 | tf_op jit(solution)/shard_map/ppermute | solution.py:465
  53.5 1.9 %collective-permute-done.17.refs_1_ = bf16[2,128,128]{2,1,0:T(8,128)(2,1)S(1)} collective-permute-done((bf16[2,128,128]{2,1,0:T(8,128)(2,1)S(1)}, bf16[2,128,128]{2,1,0:T(8,128)(2,1)S(1)}, u32[]{:S(2)}, u32[]{:S(2)}) %collective-permute-start.17) | collective-permute-done | bytes 65568 | tf_op jit(solution)/shard_map/ppermute | solution.py:465
  55.5 0.7 %shard_map.190 = (f32[128,128]{1,0:T(8,128)}, f32[128,128]{1,0:T(8,128)}) custom-call(bf16[2,128,128]{2,1,0:T(8,128)(2,1)S(1)} %collective-permute-done.16.refs_0_, bf16[2,128,128]{2,1,0:T(8,128)(2,1)S(1)} %collective-permute-done.17.refs_1_, bf16[2,128,128]{2,1,0:T(8,128)(2,1)S(1)} %collective-permute-done.19.refs_2_, ...), custom_call_target="tpu_custom_call" | custom-call | tf_op jit(solution)/shard_map/pallas_call | solution.py:428
  (46 shorter events, 5.0 us)
Async XLA Ops:
  0.6 15.4 %collective-permute-start.1 = (bf16[3,227,360]{2,1,0:T(8,128)(2,1)}, bf16[3,227,360]{2,1,0:T(8,128)(2,1)S(1)}, u32[]{:S(2)}, u32[]{:S(2)}) collective-permute-start(bf16[3,227,360]{2,1,0:T(8,128)(2,1)} %bitcast.5), channel_id=1, source_target_pairs={{0,1},{1,0},{2,3},{3,2},{4,8},{5,9},{6,10},{7,11},{8,4},{9,5},{10,... | collective-permute-start | bytes 1470968 | tf_op jit(solution)/shard_map/ppermute | solution.py:489
  1.2 16.3 %collective-permute-start = (bf16[3,227,360]{2,1,0:T(8,128)(2,1)}, bf16[3,227,360]{2,1,0:T(8,128)(2,1)S(1)}, u32[]{:S(2)}, u32[]{:S(2)}) collective-permute-start(bf16[3,227,360]{2,1,0:T(8,128)(2,1)} %bitcast.6), channel_id=1, source_target_pairs={{0,4},{4,0},{8,12},{12,8},{1,5},{5,1},{9,13},{13,9},{2,6},{6,2},{1... | collective-permute-start | bytes 1470968 | tf_op jit(solution)/shard_map/ppermute | solution.py:488
  7.3 1.0 %copy-start = (bf16[3,360,227]{1,2,0:T(8,128)(2,1)S(1)}, bf16[3,360,227]{1,2,0:T(8,128)(2,1)}, u32[]{:S(2)}) copy-start(bf16[3,360,227]{1,2,0:T(8,128)(2,1)} %param.16) | copy-start | bytes 1470964
  8.4 6.8 %copy-start.3 = (bf16[512,512]{1,0:T(8,128)(2,1)S(1)}, bf16[512,512]{1,0:T(8,128)(2,1)}, u32[]{:S(2)}) copy-start(bf16[512,512]{1,0:T(8,128)(2,1)} %param.21) | copy-start | bytes 1572868
  8.4 6.9 %copy-start.4 = (bf16[512,512]{1,0:T(8,128)(2,1)S(1)}, bf16[512,512]{1,0:T(8,128)(2,1)}, u32[]{:S(2)}) copy-start(bf16[512,512]{1,0:T(8,128)(2,1)} %param.22) | copy-start | bytes 1572868
  8.4 6.9 %copy-start.5 = (bf16[512,512]{1,0:T(8,128)(2,1)S(1)}, bf16[512,512]{1,0:T(8,128)(2,1)}, u32[]{:S(2)}) copy-start(bf16[512,512]{1,0:T(8,128)(2,1)} %param.23) | copy-start | bytes 1572868
  8.4 7.0 %copy-start.6 = (bf16[227,512]{1,0:T(8,128)(2,1)S(1)}, bf16[227,512]{1,0:T(8,128)(2,1)}, u32[]{:S(2)}) copy-start(bf16[227,512]{1,0:T(8,128)(2,1)} %param.17) | copy-start | bytes 697348
  10.3 5.1 %copy-start.1 = (bf16[32,512]{1,0:T(8,128)(2,1)S(1)}, bf16[32,512]{1,0:T(8,128)(2,1)}, u32[]{:S(2)}) copy-start(bf16[32,512]{1,0:T(8,128)(2,1)} %mesh_in.3) | copy-start | bytes 98308
  10.3 5.1 %collective-permute-start.3 = (bf16[32,512]{1,0:T(8,128)(2,1)}, bf16[32,512]{1,0:T(8,128)(2,1)S(1)}, u32[]{:S(2)}, u32[]{:S(2)}) collective-permute-start(bf16[32,512]{1,0:T(8,128)(2,1)} %mesh_in.3), channel_id=1, source_target_pairs={{0,3},{1,2},{2,1},{3,0},{4,7},{5,6},{6,5},{7,4},{8,11},{9,10},{10,... | collective-permute-start | bytes 98312 | tf_op jit(solution)/shard_map/ppermute | solution.py:515
  10.7 4.7 %collective-permute-start.2 = (bf16[32,512]{1,0:T(8,128)(2,1)}, bf16[32,512]{1,0:T(8,128)(2,1)S(1)}, u32[]{:S(2)}, u32[]{:S(2)}) collective-permute-start(bf16[32,512]{1,0:T(8,128)(2,1)} %mesh_in.3), channel_id=1, source_target_pairs={{0,1},{1,0},{2,3},{3,2},{4,5},{5,4},{6,7},{7,6},{8,9},{9,8},{10,11... | collective-permute-start | bytes 98312 | tf_op jit(solution)/shard_map/ppermute | solution.py:514
  20.5 1.7 %collective-permute-start.4 = (bf16[32,512]{1,0:T(8,128)(2,1)S(1)}, bf16[32,512]{1,0:T(8,128)(2,1)S(1)}, u32[]{:S(2)}, u32[]{:S(2)}) collective-permute-start(bf16[32,512]{1,0:T(8,128)(2,1)S(1)} %get-tuple-element.58), channel_id=1, source_target_pairs={{0,1},{1,0},{2,3},{3,2},{4,5},{5,4},{6,7},{7,6},{8,9},{9,8},{10,11... | collective-permute-start | bytes 98312 | tf_op jit(solution)/shard_map/ppermute | solution.py:543
  20.6 3.4 %collective-permute-start.5 = (bf16[32,512]{1,0:T(8,128)(2,1)S(1)}, bf16[32,512]{1,0:T(8,128)(2,1)S(1)}, u32[]{:S(2)}, u32[]{:S(2)}) collective-permute-start(bf16[32,512]{1,0:T(8,128)(2,1)S(1)} %get-tuple-element.59), channel_id=1, source_target_pairs={{0,3},{1,2},{2,1},{3,0},{4,7},{5,6},{6,5},{7,4},{8,11},{9,10},{10,... | collective-permute-start | bytes 98312 | tf_op jit(solution)/shard_map/ppermute | solution.py:542
  24.0 4.8 %copy-start.2 = (bf16[32,512]{1,0:T(8,128)(2,1)S(1)}, bf16[32,512]{1,0:T(8,128)(2,1)}, u32[]{:S(2)}) copy-start(bf16[32,512]{1,0:T(8,128)(2,1)} %d_out.3) | copy-start | bytes 98308
  24.3 4.5 %collective-permute-start.7 = (bf16[64,512]{1,0:T(8,128)(2,1)S(1)}, bf16[64,512]{1,0:T(8,128)(2,1)S(1)}, u32[]{:S(2)}, u32[]{:S(2)}) collective-permute-start(bf16[64,512]{1,0:T(8,128)(2,1)S(1)} %get-tuple-element.60.own.nodes), channel_id=1, source_target_pairs={{0,4},{4,0},{8,12},{12,8},{1,5},{5,1},{9,13},{13,9},{2,6},{6,2},{1... | collective-permute-start | bytes 196616 | tf_op jit(solution)/shard_map/ppermute | solution.py:549
  26.1 2.7 %collective-permute-start.6 = (bf16[64,512]{1,0:T(8,128)(2,1)S(1)}, bf16[64,512]{1,0:T(8,128)(2,1)S(1)}, u32[]{:S(2)}, u32[]{:S(2)}) collective-permute-start(bf16[64,512]{1,0:T(8,128)(2,1)S(1)} %get-tuple-element.60.own.nodes), channel_id=1, source_target_pairs={{0,1},{1,0},{2,3},{3,2},{4,8},{5,9},{6,10},{7,11},{8,4},{9,5},{10,... | collective-permute-start | bytes 196616 | tf_op jit(solution)/shard_map/ppermute | solution.py:550
  30.5 4.3 %collective-permute-start.8 = (bf16[64,512]{1,0:T(8,128)(2,1)S(1)}, bf16[64,512]{1,0:T(8,128)(2,1)S(1)}, u32[]{:S(2)}, u32[]{:S(2)}) collective-permute-start(bf16[64,512]{1,0:T(8,128)(2,1)S(1)} %get-tuple-element.66), channel_id=1, source_target_pairs={{0,4},{4,0},{8,12},{12,8},{1,5},{5,1},{9,13},{13,9},{2,6},{6,2},{1... | collective-permute-start | bytes 196616 | tf_op jit(solution)/shard_map/ppermute | solution.py:569
  32.4 2.4 %collective-permute-start.9 = (bf16[64,512]{1,0:T(8,128)(2,1)S(1)}, bf16[64,512]{1,0:T(8,128)(2,1)S(1)}, u32[]{:S(2)}, u32[]{:S(2)}) collective-permute-start(bf16[64,512]{1,0:T(8,128)(2,1)S(1)} %get-tuple-element.67), channel_id=1, source_target_pairs={{0,1},{1,0},{2,3},{3,2},{4,8},{5,9},{6,10},{7,11},{8,4},{9,5},{10,... | collective-permute-start | bytes 196616 | tf_op jit(solution)/shard_map/ppermute | solution.py:570
  32.4 4.5 %collective-permute-start.11 = (bf16[64,512]{1,0:T(8,128)(2,1)S(1)}, bf16[64,512]{1,0:T(8,128)(2,1)S(1)}, u32[]{:S(2)}, u32[]{:S(2)}) collective-permute-start(bf16[64,512]{1,0:T(8,128)(2,1)S(1)} %get-tuple-element.60.own.nodes), channel_id=1, source_target_pairs={{0,2},{2,0},{1,3},{3,1},{4,6},{6,4},{5,7},{7,5},{8,10},{10,8},{9,1... | collective-permute-start | bytes 196616 | tf_op jit(solution)/shard_map/ppermute | solution.py:460
  34.8 2.0 %collective-permute-start.10 = (bf16[48,512]{1,0:T(8,128)(2,1)S(1)}, bf16[48,512]{1,0:T(8,128)(2,1)S(1)}, u32[]{:S(2)}, u32[]{:S(2)}) collective-permute-start(bf16[48,512]{1,0:T(8,128)(2,1)S(1)} %get-tuple-element.72), channel_id=1, source_target_pairs={{0,1},{1,0},{2,3},{3,2},{4,5},{5,4},{6,7},{7,6},{8,9},{9,8},{10,11... | collective-permute-start | bytes 147464 | tf_op jit(solution)/shard_map/ppermute | solution.py:583
  34.9 3.6 %collective-permute-start.12 = (bf16[48,512]{1,0:T(8,128)(2,1)S(1)}, bf16[48,512]{1,0:T(8,128)(2,1)S(1)}, u32[]{:S(2)}, u32[]{:S(2)}) collective-permute-start(bf16[48,512]{1,0:T(8,128)(2,1)S(1)} %get-tuple-element.74), channel_id=1, source_target_pairs={{0,3},{1,2},{2,1},{3,0},{4,7},{5,6},{6,5},{7,4},{8,11},{9,10},{10,... | collective-permute-start | bytes 147464 | tf_op jit(solution)/shard_map/ppermute | solution.py:582
  39.6 1.5 %collective-permute-start.14 = (bf16[1,512,128]{2,1,0:T(8,128)(2,1)S(1)}, bf16[1,512,128]{2,1,0:T(8,128)(2,1)S(1)}, u32[]{:S(2)}, u32[]{:S(2)}) collective-permute-start(bf16[1,512,128]{2,1,0:T(8,128)(2,1)S(1)} %bitcast.8), channel_id=1, source_target_pairs={{0,1},{1,0},{2,3},{3,2},{4,5},{5,4},{6,7},{7,6},{8,9},{9,8},{10,11... | collective-permute-start | bytes 393224 | tf_op jit(solution)/shard_map/ppermute | solution.py:460
  40.8 2.4 %collective-permute-start.13 = (bf16[512,128]{1,0:T(8,128)(2,1)S(1)}, bf16[512,128]{1,0:T(8,128)(2,1)S(1)}, u32[]{:S(2)}, u32[]{:S(2)}) collective-permute-start(bf16[512,128]{1,0:T(8,128)(2,1)S(1)} %bitcast.9), channel_id=1, source_target_pairs={{0,1},{1,0},{2,3},{3,2},{4,5},{5,4},{6,7},{7,6},{8,9},{9,8},{10,11... | collective-permute-start | bytes 393224 | tf_op jit(solution)/shard_map/ppermute | solution.py:460
  41.1 5.3 %collective-permute-start.15 = (bf16[320,128]{1,0:T(8,128)(2,1)S(1)}, bf16[320,128]{1,0:T(8,128)(2,1)S(1)}, u32[]{:S(2)}, u32[]{:S(2)}) collective-permute-start(bf16[320,128]{1,0:T(8,128)(2,1)S(1)} %bitcast.10), channel_id=1, source_target_pairs={{0,2},{2,0},{1,3},{3,1},{4,6},{6,4},{5,7},{7,5},{8,10},{10,8},{9,1... | collective-permute-start | bytes 245768 | tf_op jit(solution)/shard_map/ppermute | solution.py:460
  42.7 7.6 %collective-permute-start.18 = (bf16[256,128]{1,0:T(8,128)(2,1)S(1)}, bf16[256,128]{1,0:T(8,128)(2,1)S(1)}, u32[]{:S(2)}, u32[]{:S(2)}) collective-permute-start(bf16[256,128]{1,0:T(8,128)(2,1)S(1)} %bitcast.11), channel_id=1, source_target_pairs={{0,2},{2,0},{1,3},{3,1},{4,6},{6,4},{5,7},{7,5},{8,10},{10,8},{9,1... | collective-permute-start | bytes 196616 | tf_op jit(solution)/shard_map/ppermute | solution.py:460
  46.7 6.8 %collective-permute-start.16 = (bf16[2,128,128]{2,1,0:T(8,128)(2,1)S(1)}, bf16[2,128,128]{2,1,0:T(8,128)(2,1)S(1)}, u32[]{:S(2)}, u32[]{:S(2)}) collective-permute-start(bf16[2,128,128]{2,1,0:T(8,128)(2,1)S(1)} %get-tuple-element.85), channel_id=1, source_target_pairs={{0,12},{4,8},{8,4},{12,0},{1,13},{5,9},{9,5},{13,1},{2,14},{6,10},... | collective-permute-start | bytes 196616 | tf_op jit(solution)/shard_map/ppermute | solution.py:465
  48.7 6.8 %collective-permute-start.17 = (bf16[2,128,128]{2,1,0:T(8,128)(2,1)S(1)}, bf16[2,128,128]{2,1,0:T(8,128)(2,1)S(1)}, u32[]{:S(2)}, u32[]{:S(2)}) collective-permute-start(bf16[2,128,128]{2,1,0:T(8,128)(2,1)S(1)} %get-tuple-element.86), channel_id=1, source_target_pairs={{0,8},{4,12},{8,0},{12,4},{1,9},{5,13},{9,1},{13,5},{2,10},{6,14},... | collective-permute-start | bytes 196616 | tf_op jit(solution)/shard_map/ppermute | solution.py:465
  50.3 5.2 %collective-permute-start.19 = (bf16[2,128,128]{2,1,0:T(8,128)(2,1)S(1)}, bf16[2,128,128]{2,1,0:T(8,128)(2,1)S(1)}, u32[]{:S(2)}, u32[]{:S(2)}) collective-permute-start(bf16[2,128,128]{2,1,0:T(8,128)(2,1)S(1)} %get-tuple-element.89), channel_id=1, source_target_pairs={{0,4},{4,0},{8,12},{12,8},{1,5},{5,1},{9,13},{13,9},{2,6},{6,2},{1... | collective-permute-start | bytes 196616 | tf_op jit(solution)/shard_map/ppermute | solution.py:465

commit v19 on v18

--- a/solution.py
+++ b/solution.py
@@ -156,10 +156,11 @@
 
 def live_slots(count, edges, work, rest):
     lower = 0
-    for size in (edges // 2, 3 * edges // 4, edges):
+    for size in range(edges // 2, edges + 1, edges // 8):
 
         def case(size=size):
-            work([slice(0, size // 2), slice(size // 2, size)])
+            middle = -(-size // 2 // LANES) * LANES
+            work([slice(0, middle), slice(middle, size)])
             if size < edges:
                 rest(slice(size, edges))
 
@@ -169,9 +170,8 @@
 
 
 def gather_kernel(count, halo, hits, rows, rows_out, wide):
-    fill(wide, halo, wide.shape[1] // halo.shape[0], 0)
-
     def work(parts):
+        fill(wide, halo, wide.shape[1] // halo.shape[0], 0)
         part_of = slice(0, parts[-1].stop)
         gathered = mm_nt(hits[part_of], wide[...]).astype(BF16)
         rows_out[part_of] = rows[part_of] + gathered
@@ -187,9 +187,9 @@
     senders_out, slope_out, part_out, near_out, far_out, wide,
 ):
     half = recv_rows.shape[0] // 2
-    fill(wide, near, wide.shape[1] // near.shape[0], 0)
 
     def work(parts):
+        fill(wide, near, wide.shape[1] // near.shape[0], 0)
         sums = None
         for part_of in parts:
             raw = rows[part_of] + mm_nt(near_hits[part_of], wide[...]).astype(BF16)

time: 56.5 us -> 56.2 us (level)
  no operation moved by 1% of the time
where the time goes in v19:
time: 56.2 us; the launch traced here: 55.9 us
  starting transfers between devices  21.9 us (39%)
  waiting for transfers between devices  13.9 us (25%)
  Pallas kernels  12.7 us (23%)
  local copies, waits for them, and re-layouts  4.43 us (8%)
  between operations  2.17 us (4%)
  other arithmetic  0.74 us (1%)
    pallas_call x16, Pallas kernels, call(): pl.pallas_call(kernel, out_shape=[jax.ShapeDtypeStruct(shape, dtype) for...  12.7 us
    ppermute x3, starting transfers between devices, over_band(): return lax.ppermute(x, 'band', [(b, b ^ partner) for b in range(count)])  4.52 us
    unnamed x20, local copies, waits for them, and re-layouts  4.41 us
    ppermute x5, starting transfers between devices, shifted(): lax.ppermute(x, axis, [(i, (i + shift) % count) for i in range(count)])  4.22 us
    ppermute x3, waiting for transfers between devices, over_band(): return lax.ppermute(x, 'band', [(b, b ^ partner) for b in range(count)])  4.19 us
    ppermute x1, starting transfers between devices, on_device(): raw_near = lax.ppermute(grid, 'band', band_near)  4.15 us
    ppermute x2, waiting for transfers between devices, on_device(): from_far = lax.ppermute(to_far, around, ring_far)  3.4 us
    ppermute x2, starting transfers between devices, on_device(): from_far = lax.ppermute(to_far, around, ring_far)  3.22 us
  transfers between devices with their start and end apart: 20, of which 10 were waited for; matrix products, arithmetic and copies ran while one was open for 7% of the time, Pallas kernels for 11%

profile of v19, /device:TPU:0, one launch (start us, length us, event | category | flops | bytes accessed | tf_op | source)
XLA Modules:
  0.0 55.9 jit_solution(6932567116893671516)
XLA Ops:
  1.2 4.1 %collective-permute-start = (bf16[3,227,360]{2,1,0:T(8,128)(2,1)}, bf16[3,227,360]{2,1,0:T(8,128)(2,1)S(1)}, u32[]{:S(2)}, u32[]{:S(2)}) collective-permute-start(bf16[3,227,360]{2,1,0:T(8,128)(2,1)} %bitcast.6), channel_id=1, source_target_pairs={{0,4},{4,0},{8,12},{12,8},{1,5},{5,1},{9,13},{13,9},{2,6},{6,2},{1... | collective-permute-start | bytes 1470968 | tf_op jit(solution)/shard_map/ppermute | solution.py:488
  6.6 0.7 %pad_add_fusion.indices = s32[1,1,3072]{2,1,0:T(1,128)S(1)} fusion(s32[1,1,512]{2,1,0:T(1,128)} %param.30, s32[1,1,512]{2,1,0:T(1,128)} %param.29, s32[1,1,1024]{2,1,0:T(1,128)} %param.27, s32[1,1,1024]{2,1,0:T(1,128)} %param.26), kind=kLoop, calls=%fused_computation.7 | loop fusion | flops 9216 | bytes 24576 | tf_op jit(solution)/shard_map/concatenate | solution.py:492
  7.3 1.0 %copy-done = bf16[3,360,227]{1,2,0:T(8,128)(2,1)S(1)} copy-done((bf16[3,360,227]{1,2,0:T(8,128)(2,1)S(1)}, bf16[3,360,227]{1,2,0:T(8,128)(2,1)}, u32[]{:S(2)}) %copy-start) | copy-done | bytes 490344
  8.4 1.9 %shard_map.175 = (bf16[1024,227]{1,0:T(8,128)(2,1)S(1)}, bf16[1024,128]{1,0:T(8,128)(2,1)S(1)}, bf16[64,1024]{1,0:T(8,128)(2,1)S(1)}, bf16[512,128]{1,0:T(8,128)...) custom-call(s32[1,1]{1,0:T(1,128)S(6)} %copy.25.count, ...), custom_call_target="tpu_custom_call" | custom-call | tf_op jit(solution)/shard_map/pallas_call | solution.py:428
  10.7 1.2 %collective-permute-start.2 = (bf16[32,512]{1,0:T(8,128)(2,1)}, bf16[32,512]{1,0:T(8,128)(2,1)S(1)}, u32[]{:S(2)}, u32[]{:S(2)}) collective-permute-start(bf16[32,512]{1,0:T(8,128)(2,1)} %mesh_in.3), channel_id=1, source_target_pairs={{0,1},{1,0},{2,3},{3,2},{4,5},{5,4},{6,7},{7,6},{8,9},{9,8},{10,11... | collective-permute-start | bytes 98312 | tf_op jit(solution)/shard_map/ppermute | solution.py:514
  12.0 1.1 %constant_dynamic-update-slice_fusion.6 = bf16[3299,512]{1,0:T(8,128)(2,1)S(1)} fusion(bf16[512,512]{1,0:T(8,128)(2,1)} %param.18), kind=kLoop, calls=%fused_computation.6 | loop fusion | bytes 1048576
  13.0 1.1 %constant_dynamic-update-slice_fusion.5 = bf16[3299,512]{1,0:T(8,128)(2,1)S(1)} fusion(bf16[3299,512]{1,0:T(8,128)(2,1)S(1)} %constant_dynamic-update-slice_fusion.6, bf16[512,512]{1,0:T(8,128)(2,1)} %param.19), kind=kLoop, calls=%fused_computation.5 | loop fusion | bytes 1048576
  14.1 1.1 %constant_dynamic-update-slice_fusion.4 = bf16[3299,512]{1,0:T(8,128)(2,1)S(1)} fusion(bf16[3299,512]{1,0:T(8,128)(2,1)S(1)} %constant_dynamic-update-slice_fusion.5, bf16[512,512]{1,0:T(8,128)(2,1)} %param.20), kind=kLoop, calls=%fused_computation.4 | loop fusion | bytes 1048576
  15.4 0.6 %shard_map.177.recv_pre = f32[1024,512]{1,0:T(8,128)S(1)} custom-call(bf16[32,512]{1,0:T(8,128)(2,1)S(1)} %collective-permute-done.2.near.mesh_near, bf16[32,512]{1,0:T(8,128)(2,1)S(1)} %collective-permute-done.3.far.mesh_far, bf16[32,512]{1,0:T(8,128)(2,1)S(1)} %copy-done.1, bf16[1024,128]{1,0:T(8,128)(2,1)S(1)} %get-tuple-element.56.recv_hits, ...), custom_call_target="tpu_custom_call" | custom-call | tf_op jit(solution)/shard_map/pallas_call | solution.py:428
  16.1 1.0 %shard_map.176.rows = bf16[1024,227]{1,0:T(8,128)(2,1)S(1)} custom-call(s32[1,1]{1,0:T(1,128)S(6)} %copy.25.count, bf16[3,227,360]{2,1,0:T(8,128)(2,1)S(1)} %collective-permute-done.1.halo, bf16[1024,1152]{1,0:T(8,128)(2,1)S(1)} %get-tuple-element.52.hits, bf16[1024,227]{1,0:T(8,128)(2,1)S(1)} %get-tuple-element.54.rows), custom_call_target="tpu_custom_call" | custom-call | tf_op jit(solution)/shard_map/pallas_call | solution.py:428
  17.4 2.9 %shard_map.178 = (bf16[1024,512]{1,0:T(8,128)(2,1)S(1)}, bf16[1024,512]{1,0:T(8,128)(2,1)S(1)}, f32[64,512]{1,0:T(8,128)S(1)}, bf16[32,512]{1,0:T(8,128)(2,1)S(1)}, bf16[32,512]{1,0:T(8,128)(2,1)S(1)}) custom-call(s32[1,1]{1,0:T(1,128)S(6)} %copy.25.count, bf16[3,227,360]{2,1,0:T(8,128)(2,1)S(1)} %collective-permute-done.near, ...), custom_call_target="tpu_custom_call" | custom-call | tf_op jit(solution)/shard_map/pallas_call | solution.py:428
  20.4 1.6 %collective-permute-start.5 = (bf16[32,512]{1,0:T(8,128)(2,1)S(1)}, bf16[32,512]{1,0:T(8,128)(2,1)S(1)}, u32[]{:S(2)}, u32[]{:S(2)}) collective-permute-start(bf16[32,512]{1,0:T(8,128)(2,1)S(1)} %get-tuple-element.59), channel_id=1, source_target_pairs={{0,3},{1,2},{2,1},{3,0},{4,7},{5,6},{6,5},{7,4},{8,11},{9,10},{10,... | collective-permute-start | bytes 98312 | tf_op jit(solution)/shard_map/ppermute | solution.py:542
  22.0 1.8 %collective-permute-done.5.far = bf16[32,512]{1,0:T(8,128)(2,1)S(1)} collective-permute-done((bf16[32,512]{1,0:T(8,128)(2,1)S(1)}, bf16[32,512]{1,0:T(8,128)(2,1)S(1)}, u32[]{:S(2)}, u32[]{:S(2)}) %collective-permute-start.5) | collective-permute-done | bytes 32800 | tf_op jit(solution)/shard_map/ppermute | solution.py:542
  24.0 1.4 %collective-permute-start.7 = (bf16[64,512]{1,0:T(8,128)(2,1)S(1)}, bf16[64,512]{1,0:T(8,128)(2,1)S(1)}, u32[]{:S(2)}, u32[]{:S(2)}) collective-permute-start(bf16[64,512]{1,0:T(8,128)(2,1)S(1)} %get-tuple-element.60.own.nodes), channel_id=1, source_target_pairs={{0,4},{4,0},{8,12},{12,8},{1,5},{5,1},{9,13},{13,9},{2,6},{6,2},{1... | collective-permute-start | bytes 196616 | tf_op jit(solution)/shard_map/ppermute | solution.py:549
  25.6 0.7 %shard_map.180.own_pre = f32[512,512]{1,0:T(8,128)S(1)} custom-call(bf16[512,128]{1,0:T(8,128)(2,1)S(1)} %get-tuple-element.48.own_hits, bf16[512,64]{1,0:T(8,128)(2,1)S(1)} %get-tuple-element.49.to_hits, bf16[64,512]{1,0:T(8,128)(2,1)S(1)} %get-tuple-element.60.own.nodes, bf16[3299,512]{1,0:T(8,128)(2,1)S(1)} %constant_dynamic-update-slice_fusion.stack), custom_call_target="tpu_custom_call" | custom-call | tf_op jit(solution)/shard_map/pallas_call | solution.py:428
  26.3 2.2 %collective-permute-done.7.near = bf16[64,512]{1,0:T(8,128)(2,1)S(1)} collective-permute-done((bf16[64,512]{1,0:T(8,128)(2,1)S(1)}, bf16[64,512]{1,0:T(8,128)(2,1)S(1)}, u32[]{:S(2)}, u32[]{:S(2)}) %collective-permute-start.7) | collective-permute-done | bytes 65568 | tf_op jit(solution)/shard_map/ppermute | solution.py:549
  28.6 1.7 %shard_map.181 = (bf16[32,512]{1,0:T(8,128)(2,1)}, f32[192,512]{1,0:T(8,128)S(1)}, bf16[32,512]{1,0:T(8,128)(2,1)S(1)}, bf16[64,512]{1,0:T(8,128)(2,1)S(1)}, bf16[64,512]{1,0:T(8,128)(2,1)S(1)}) custom-call(f32[512,512]{1,0:T(8,128)S(1)} %shard_map.180.own_pre, bf16[512,256]{1,0:T(8,128)(2,1)S(1)} %get-tuple-element.61.outer_hits, ...), custom_call_target="tpu_custom_call" | custom-call | tf_op jit(solution)/shard_map/pallas_call | solution.py:428
  30.2 1.9 %collective-permute-start.8 = (bf16[64,512]{1,0:T(8,128)(2,1)S(1)}, bf16[64,512]{1,0:T(8,128)(2,1)S(1)}, u32[]{:S(2)}, u32[]{:S(2)}) collective-permute-start(bf16[64,512]{1,0:T(8,128)(2,1)S(1)} %get-tuple-element.66), channel_id=1, source_target_pairs={{0,4},{4,0},{8,12},{12,8},{1,5},{5,1},{9,13},{13,9},{2,6},{6,2},{1... | collective-permute-start | bytes 196616 | tf_op jit(solution)/shard_map/ppermute | solution.py:569
  32.1 1.5 %collective-permute-start.11 = (bf16[64,512]{1,0:T(8,128)(2,1)S(1)}, bf16[64,512]{1,0:T(8,128)(2,1)S(1)}, u32[]{:S(2)}, u32[]{:S(2)}) collective-permute-start(bf16[64,512]{1,0:T(8,128)(2,1)S(1)} %get-tuple-element.60.own.nodes), channel_id=1, source_target_pairs={{0,2},{2,0},{1,3},{3,1},{4,6},{6,4},{5,7},{7,5},{8,10},{10,8},{9,1... | collective-permute-start | bytes 196616 | tf_op jit(solution)/shard_map/ppermute | solution.py:460
  34.7 1.6 %collective-permute-start.12 = (bf16[48,512]{1,0:T(8,128)(2,1)S(1)}, bf16[48,512]{1,0:T(8,128)(2,1)S(1)}, u32[]{:S(2)}, u32[]{:S(2)}) collective-permute-start(bf16[48,512]{1,0:T(8,128)(2,1)S(1)} %get-tuple-element.74), channel_id=1, source_target_pairs={{0,3},{1,2},{2,1},{3,0},{4,7},{5,6},{6,5},{7,4},{8,11},{9,10},{10,... | collective-permute-start | bytes 147464 | tf_op jit(solution)/shard_map/ppermute | solution.py:582
  36.6 1.6 %collective-permute-done.12.far = bf16[48,512]{1,0:T(8,128)(2,1)S(1)} collective-permute-done((bf16[48,512]{1,0:T(8,128)(2,1)S(1)}, bf16[48,512]{1,0:T(8,128)(2,1)S(1)}, u32[]{:S(2)}, u32[]{:S(2)}) %collective-permute-start.12) | collective-permute-done | bytes 49184 | tf_op jit(solution)/shard_map/ppermute | solution.py:582
  38.2 1.1 %shard_map.184 = (bf16[1,1,512,128]{3,2,1,0:T(8,128)(2,1)S(1)}, bf16[128,512]{1,0:T(8,128)(2,1)S(1)}, bf16[2,64,128]{2,1,0:T(8,128)(2,1)S(1)}) custom-call(bf16[1024,128]{1,0:T(8,128)(2,1)S(1)} %get-tuple-element.56.recv_hits, f32[64,512]{1,0:T(8,128)S(1)} %get-tuple-element.71.part, bf16[48,512]{1,0:T(8,128)(2,1)S(1)} %collective-permute-done.10.near, ...), custom_call_target="tpu_custom_call" | custom-call | tf_op jit(solution)/shard_map/pallas_call | solution.py:428
  39.8 0.7 %shard_map.185 = (f32[1,512,128]{2,1,0:T(8,128)S(1)}, bf16[1,512,128]{2,1,0:T(8,128)(2,1)S(1)}) custom-call(bf16[1024,128]{1,0:T(8,128)(2,1)S(1)} %get-tuple-element.56.recv_hits, bf16[128,512]{1,0:T(8,128)(2,1)S(1)} %get-tuple-element.78.back, bf16[1024,512]{1,0:T(8,128)(2,1)S(1)} %get-tuple-element.77.edge_slope, ...), custom_call_target="tpu_custom_call" | custom-call | tf_op jit(solution)/shard_map/pallas_call | solution.py:428
  40.9 1.6 %collective-permute-start.15 = (bf16[320,128]{1,0:T(8,128)(2,1)S(1)}, bf16[320,128]{1,0:T(8,128)(2,1)S(1)}, u32[]{:S(2)}, u32[]{:S(2)}) collective-permute-start(bf16[320,128]{1,0:T(8,128)(2,1)S(1)} %bitcast.10), channel_id=1, source_target_pairs={{0,2},{2,0},{1,3},{3,1},{4,6},{6,4},{5,7},{7,5},{8,10},{10,8},{9,1... | collective-permute-start | bytes 245768 | tf_op jit(solution)/shard_map/ppermute | solution.py:460
  43.0 0.6 %shard_map.186.kept = f32[512,128]{1,0:T(8,128)S(1)} custom-call(bf16[1024,128]{1,0:T(8,128)(2,1)S(1)} %get-tuple-element.56.recv_hits, bf16[128,512]{1,0:T(8,128)(2,1)S(1)} %get-tuple-element.78.back, bf16[1024,512]{1,0:T(8,128)(2,1)S(1)} %get-tuple-element.77.edge_slope, bf16[512,1024]{1,0:T(8,128)(2,1)S(1)} %get-tuple-element.76.senders, ...), custom_call_target="tpu_custom_call" | custom-call | tf_op jit(solution)/shard_map/pallas_call | solution.py:428
  43.6 2.6 %collective-permute-done.15.refs_0_ = bf16[320,128]{1,0:T(8,128)(2,1)S(1)} collective-permute-done((bf16[320,128]{1,0:T(8,128)(2,1)S(1)}, bf16[320,128]{1,0:T(8,128)(2,1)S(1)}, u32[]{:S(2)}, u32[]{:S(2)}) %collective-permute-start.15) | collective-permute-done | bytes 81952 | tf_op jit(solution)/shard_map/ppermute | solution.py:460
  46.4 2.2 %collective-permute-start.16 = (bf16[2,128,128]{2,1,0:T(8,128)(2,1)S(1)}, bf16[2,128,128]{2,1,0:T(8,128)(2,1)S(1)}, u32[]{:S(2)}, u32[]{:S(2)}) collective-permute-start(bf16[2,128,128]{2,1,0:T(8,128)(2,1)S(1)} %get-tuple-element.85), channel_id=1, source_target_pairs={{0,12},{4,8},{8,4},{12,0},{1,13},{5,9},{9,5},{13,1},{2,14},{6,10},... | collective-permute-start | bytes 196616 | tf_op jit(solution)/shard_map/ppermute | solution.py:465
  48.7 1.3 %collective-permute-start.17 = (bf16[2,128,128]{2,1,0:T(8,128)(2,1)S(1)}, bf16[2,128,128]{2,1,0:T(8,128)(2,1)S(1)}, u32[]{:S(2)}, u32[]{:S(2)}) collective-permute-start(bf16[2,128,128]{2,1,0:T(8,128)(2,1)S(1)} %get-tuple-element.86), channel_id=1, source_target_pairs={{0,8},{4,12},{8,0},{12,4},{1,9},{5,13},{9,1},{13,5},{2,10},{6,14},... | collective-permute-start | bytes 196616 | tf_op jit(solution)/shard_map/ppermute | solution.py:465
  50.0 1.0 %collective-permute-start.19 = (bf16[2,128,128]{2,1,0:T(8,128)(2,1)S(1)}, bf16[2,128,128]{2,1,0:T(8,128)(2,1)S(1)}, u32[]{:S(2)}, u32[]{:S(2)}) collective-permute-start(bf16[2,128,128]{2,1,0:T(8,128)(2,1)S(1)} %get-tuple-element.89), channel_id=1, source_target_pairs={{0,4},{4,0},{8,12},{12,8},{1,5},{5,1},{9,13},{13,9},{2,6},{6,2},{1... | collective-permute-start | bytes 196616 | tf_op jit(solution)/shard_map/ppermute | solution.py:465
  51.0 2.2 %collective-permute-done.16.refs_0_ = bf16[2,128,128]{2,1,0:T(8,128)(2,1)S(1)} collective-permute-done((bf16[2,128,128]{2,1,0:T(8,128)(2,1)S(1)}, bf16[2,128,128]{2,1,0:T(8,128)(2,1)S(1)}, u32[]{:S(2)}, u32[]{:S(2)}) %collective-permute-start.16) | collective-permute-done | bytes 65568 | tf_op jit(solution)/shard_map/ppermute | solution.py:465
  53.2 1.9 %collective-permute-done.17.refs_1_ = bf16[2,128,128]{2,1,0:T(8,128)(2,1)S(1)} collective-permute-done((bf16[2,128,128]{2,1,0:T(8,128)(2,1)S(1)}, bf16[2,128,128]{2,1,0:T(8,128)(2,1)S(1)}, u32[]{:S(2)}, u32[]{:S(2)}) %collective-permute-start.17) | collective-permute-done | bytes 65568 | tf_op jit(solution)/shard_map/ppermute | solution.py:465
  55.2 0.7 %shard_map.190 = (f32[128,128]{1,0:T(8,128)}, f32[128,128]{1,0:T(8,128)}) custom-call(bf16[2,128,128]{2,1,0:T(8,128)(2,1)S(1)} %collective-permute-done.16.refs_0_, bf16[2,128,128]{2,1,0:T(8,128)(2,1)S(1)} %collective-permute-done.17.refs_1_, bf16[2,128,128]{2,1,0:T(8,128)(2,1)S(1)} %collective-permute-done.19.refs_2_, ...), custom_call_target="tpu_custom_call" | custom-call | tf_op jit(solution)/shard_map/pallas_call | solution.py:428
  (46 shorter events, 5.0 us)
Async XLA Ops:
  0.6 15.4 %collective-permute-start.1 = (bf16[3,227,360]{2,1,0:T(8,128)(2,1)}, bf16[3,227,360]{2,1,0:T(8,128)(2,1)S(1)}, u32[]{:S(2)}, u32[]{:S(2)}) collective-permute-start(bf16[3,227,360]{2,1,0:T(8,128)(2,1)} %bitcast.5), channel_id=1, source_target_pairs={{0,1},{1,0},{2,3},{3,2},{4,8},{5,9},{6,10},{7,11},{8,4},{9,5},{10,... | collective-permute-start | bytes 1470968 | tf_op jit(solution)/shard_map/ppermute | solution.py:489
  1.2 16.3 %collective-permute-start = (bf16[3,227,360]{2,1,0:T(8,128)(2,1)}, bf16[3,227,360]{2,1,0:T(8,128)(2,1)S(1)}, u32[]{:S(2)}, u32[]{:S(2)}) collective-permute-start(bf16[3,227,360]{2,1,0:T(8,128)(2,1)} %bitcast.6), channel_id=1, source_target_pairs={{0,4},{4,0},{8,12},{12,8},{1,5},{5,1},{9,13},{13,9},{2,6},{6,2},{1... | collective-permute-start | bytes 1470968 | tf_op jit(solution)/shard_map/ppermute | solution.py:488
  7.3 1.0 %copy-start = (bf16[3,360,227]{1,2,0:T(8,128)(2,1)S(1)}, bf16[3,360,227]{1,2,0:T(8,128)(2,1)}, u32[]{:S(2)}) copy-start(bf16[3,360,227]{1,2,0:T(8,128)(2,1)} %param.16) | copy-start | bytes 1470964
  8.4 6.8 %copy-start.3 = (bf16[512,512]{1,0:T(8,128)(2,1)S(1)}, bf16[512,512]{1,0:T(8,128)(2,1)}, u32[]{:S(2)}) copy-start(bf16[512,512]{1,0:T(8,128)(2,1)} %param.21) | copy-start | bytes 1572868
  8.4 6.9 %copy-start.4 = (bf16[512,512]{1,0:T(8,128)(2,1)S(1)}, bf16[512,512]{1,0:T(8,128)(2,1)}, u32[]{:S(2)}) copy-start(bf16[512,512]{1,0:T(8,128)(2,1)} %param.22) | copy-start | bytes 1572868
  8.4 6.9 %copy-start.5 = (bf16[512,512]{1,0:T(8,128)(2,1)S(1)}, bf16[512,512]{1,0:T(8,128)(2,1)}, u32[]{:S(2)}) copy-start(bf16[512,512]{1,0:T(8,128)(2,1)} %param.23) | copy-start | bytes 1572868
  8.4 7.0 %copy-start.6 = (bf16[227,512]{1,0:T(8,128)(2,1)S(1)}, bf16[227,512]{1,0:T(8,128)(2,1)}, u32[]{:S(2)}) copy-start(bf16[227,512]{1,0:T(8,128)(2,1)} %param.17) | copy-start | bytes 697348
  10.3 5.1 %copy-start.1 = (bf16[32,512]{1,0:T(8,128)(2,1)S(1)}, bf16[32,512]{1,0:T(8,128)(2,1)}, u32[]{:S(2)}) copy-start(bf16[32,512]{1,0:T(8,128)(2,1)} %mesh_in.3) | copy-start | bytes 98308
  10.3 5.1 %collective-permute-start.3 = (bf16[32,512]{1,0:T(8,128)(2,1)}, bf16[32,512]{1,0:T(8,128)(2,1)S(1)}, u32[]{:S(2)}, u32[]{:S(2)}) collective-permute-start(bf16[32,512]{1,0:T(8,128)(2,1)} %mesh_in.3), channel_id=1, source_target_pairs={{0,3},{1,2},{2,1},{3,0},{4,7},{5,6},{6,5},{7,4},{8,11},{9,10},{10,... | collective-permute-start | bytes 98312 | tf_op jit(solution)/shard_map/ppermute | solution.py:515
  10.7 4.7 %collective-permute-start.2 = (bf16[32,512]{1,0:T(8,128)(2,1)}, bf16[32,512]{1,0:T(8,128)(2,1)S(1)}, u32[]{:S(2)}, u32[]{:S(2)}) collective-permute-start(bf16[32,512]{1,0:T(8,128)(2,1)} %mesh_in.3), channel_id=1, source_target_pairs={{0,1},{1,0},{2,3},{3,2},{4,5},{5,4},{6,7},{7,6},{8,9},{9,8},{10,11... | collective-permute-start | bytes 98312 | tf_op jit(solution)/shard_map/ppermute | solution.py:514
  20.3 1.7 %collective-permute-start.4 = (bf16[32,512]{1,0:T(8,128)(2,1)S(1)}, bf16[32,512]{1,0:T(8,128)(2,1)S(1)}, u32[]{:S(2)}, u32[]{:S(2)}) collective-permute-start(bf16[32,512]{1,0:T(8,128)(2,1)S(1)} %get-tuple-element.58), channel_id=1, source_target_pairs={{0,1},{1,0},{2,3},{3,2},{4,5},{5,4},{6,7},{7,6},{8,9},{9,8},{10,11... | collective-permute-start | bytes 98312 | tf_op jit(solution)/shard_map/ppermute | solution.py:543
  20.4 3.4 %collective-permute-start.5 = (bf16[32,512]{1,0:T(8,128)(2,1)S(1)}, bf16[32,512]{1,0:T(8,128)(2,1)S(1)}, u32[]{:S(2)}, u32[]{:S(2)}) collective-permute-start(bf16[32,512]{1,0:T(8,128)(2,1)S(1)} %get-tuple-element.59), channel_id=1, source_target_pairs={{0,3},{1,2},{2,1},{3,0},{4,7},{5,6},{6,5},{7,4},{8,11},{9,10},{10,... | collective-permute-start | bytes 98312 | tf_op jit(solution)/shard_map/ppermute | solution.py:542
  23.8 4.8 %copy-start.2 = (bf16[32,512]{1,0:T(8,128)(2,1)S(1)}, bf16[32,512]{1,0:T(8,128)(2,1)}, u32[]{:S(2)}) copy-start(bf16[32,512]{1,0:T(8,128)(2,1)} %d_out.3) | copy-start | bytes 98308
  24.0 4.5 %collective-permute-start.7 = (bf16[64,512]{1,0:T(8,128)(2,1)S(1)}, bf16[64,512]{1,0:T(8,128)(2,1)S(1)}, u32[]{:S(2)}, u32[]{:S(2)}) collective-permute-start(bf16[64,512]{1,0:T(8,128)(2,1)S(1)} %get-tuple-element.60.own.nodes), channel_id=1, source_target_pairs={{0,4},{4,0},{8,12},{12,8},{1,5},{5,1},{9,13},{13,9},{2,6},{6,2},{1... | collective-permute-start | bytes 196616 | tf_op jit(solution)/shard_map/ppermute | solution.py:549
  25.4 3.1 %collective-permute-start.6 = (bf16[64,512]{1,0:T(8,128)(2,1)S(1)}, bf16[64,512]{1,0:T(8,128)(2,1)S(1)}, u32[]{:S(2)}, u32[]{:S(2)}) collective-permute-start(bf16[64,512]{1,0:T(8,128)(2,1)S(1)} %get-tuple-element.60.own.nodes), channel_id=1, source_target_pairs={{0,1},{1,0},{2,3},{3,2},{4,8},{5,9},{6,10},{7,11},{8,4},{9,5},{10,... | collective-permute-start | bytes 196616 | tf_op jit(solution)/shard_map/ppermute | solution.py:550
  30.2 4.3 %collective-permute-start.8 = (bf16[64,512]{1,0:T(8,128)(2,1)S(1)}, bf16[64,512]{1,0:T(8,128)(2,1)S(1)}, u32[]{:S(2)}, u32[]{:S(2)}) collective-permute-start(bf16[64,512]{1,0:T(8,128)(2,1)S(1)} %get-tuple-element.66), channel_id=1, source_target_pairs={{0,4},{4,0},{8,12},{12,8},{1,5},{5,1},{9,13},{13,9},{2,6},{6,2},{1... | collective-permute-start | bytes 196616 | tf_op jit(solution)/shard_map/ppermute | solution.py:569
  32.1 2.4 %collective-permute-start.9 = (bf16[64,512]{1,0:T(8,128)(2,1)S(1)}, bf16[64,512]{1,0:T(8,128)(2,1)S(1)}, u32[]{:S(2)}, u32[]{:S(2)}) collective-permute-start(bf16[64,512]{1,0:T(8,128)(2,1)S(1)} %get-tuple-element.67), channel_id=1, source_target_pairs={{0,1},{1,0},{2,3},{3,2},{4,8},{5,9},{6,10},{7,11},{8,4},{9,5},{10,... | collective-permute-start | bytes 196616 | tf_op jit(solution)/shard_map/ppermute | solution.py:570
  32.1 4.5 %collective-permute-start.11 = (bf16[64,512]{1,0:T(8,128)(2,1)S(1)}, bf16[64,512]{1,0:T(8,128)(2,1)S(1)}, u32[]{:S(2)}, u32[]{:S(2)}) collective-permute-start(bf16[64,512]{1,0:T(8,128)(2,1)S(1)} %get-tuple-element.60.own.nodes), channel_id=1, source_target_pairs={{0,2},{2,0},{1,3},{3,1},{4,6},{6,4},{5,7},{7,5},{8,10},{10,8},{9,1... | collective-permute-start | bytes 196616 | tf_op jit(solution)/shard_map/ppermute | solution.py:460
  34.6 2.1 %collective-permute-start.10 = (bf16[48,512]{1,0:T(8,128)(2,1)S(1)}, bf16[48,512]{1,0:T(8,128)(2,1)S(1)}, u32[]{:S(2)}, u32[]{:S(2)}) collective-permute-start(bf16[48,512]{1,0:T(8,128)(2,1)S(1)} %get-tuple-element.72), channel_id=1, source_target_pairs={{0,1},{1,0},{2,3},{3,2},{4,5},{5,4},{6,7},{7,6},{8,9},{9,8},{10,11... | collective-permute-start | bytes 147464 | tf_op jit(solution)/shard_map/ppermute | solution.py:583
  34.7 3.6 %collective-permute-start.12 = (bf16[48,512]{1,0:T(8,128)(2,1)S(1)}, bf16[48,512]{1,0:T(8,128)(2,1)S(1)}, u32[]{:S(2)}, u32[]{:S(2)}) collective-permute-start(bf16[48,512]{1,0:T(8,128)(2,1)S(1)} %get-tuple-element.74), channel_id=1, source_target_pairs={{0,3},{1,2},{2,1},{3,0},{4,7},{5,6},{6,5},{7,4},{8,11},{9,10},{10,... | collective-permute-start | bytes 147464 | tf_op jit(solution)/shard_map/ppermute | solution.py:582
  39.3 1.5 %collective-permute-start.14 = (bf16[1,512,128]{2,1,0:T(8,128)(2,1)S(1)}, bf16[1,512,128]{2,1,0:T(8,128)(2,1)S(1)}, u32[]{:S(2)}, u32[]{:S(2)}) collective-permute-start(bf16[1,512,128]{2,1,0:T(8,128)(2,1)S(1)} %bitcast.8), channel_id=1, source_target_pairs={{0,1},{1,0},{2,3},{3,2},{4,5},{5,4},{6,7},{7,6},{8,9},{9,8},{10,11... | collective-permute-start | bytes 393224 | tf_op jit(solution)/shard_map/ppermute | solution.py:460
  40.5 2.4 %collective-permute-start.13 = (bf16[512,128]{1,0:T(8,128)(2,1)S(1)}, bf16[512,128]{1,0:T(8,128)(2,1)S(1)}, u32[]{:S(2)}, u32[]{:S(2)}) collective-permute-start(bf16[512,128]{1,0:T(8,128)(2,1)S(1)} %bitcast.9), channel_id=1, source_target_pairs={{0,1},{1,0},{2,3},{3,2},{4,5},{5,4},{6,7},{7,6},{8,9},{9,8},{10,11... | collective-permute-start | bytes 393224 | tf_op jit(solution)/shard_map/ppermute | solution.py:460
  40.9 5.3 %collective-permute-start.15 = (bf16[320,128]{1,0:T(8,128)(2,1)S(1)}, bf16[320,128]{1,0:T(8,128)(2,1)S(1)}, u32[]{:S(2)}, u32[]{:S(2)}) collective-permute-start(bf16[320,128]{1,0:T(8,128)(2,1)S(1)} %bitcast.10), channel_id=1, source_target_pairs={{0,2},{2,0},{1,3},{3,1},{4,6},{6,4},{5,7},{7,5},{8,10},{10,8},{9,1... | collective-permute-start | bytes 245768 | tf_op jit(solution)/shard_map/ppermute | solution.py:460
  42.4 7.6 %collective-permute-start.18 = (bf16[256,128]{1,0:T(8,128)(2,1)S(1)}, bf16[256,128]{1,0:T(8,128)(2,1)S(1)}, u32[]{:S(2)}, u32[]{:S(2)}) collective-permute-start(bf16[256,128]{1,0:T(8,128)(2,1)S(1)} %bitcast.11), channel_id=1, source_target_pairs={{0,2},{2,0},{1,3},{3,1},{4,6},{6,4},{5,7},{7,5},{8,10},{10,8},{9,1... | collective-permute-start | bytes 196616 | tf_op jit(solution)/shard_map/ppermute | solution.py:460
  46.4 6.8 %collective-permute-start.16 = (bf16[2,128,128]{2,1,0:T(8,128)(2,1)S(1)}, bf16[2,128,128]{2,1,0:T(8,128)(2,1)S(1)}, u32[]{:S(2)}, u32[]{:S(2)}) collective-permute-start(bf16[2,128,128]{2,1,0:T(8,128)(2,1)S(1)} %get-tuple-element.85), channel_id=1, source_target_pairs={{0,12},{4,8},{8,4},{12,0},{1,13},{5,9},{9,5},{13,1},{2,14},{6,10},... | collective-permute-start | bytes 196616 | tf_op jit(solution)/shard_map/ppermute | solution.py:465
  48.7 6.5 %collective-permute-start.17 = (bf16[2,128,128]{2,1,0:T(8,128)(2,1)S(1)}, bf16[2,128,128]{2,1,0:T(8,128)(2,1)S(1)}, u32[]{:S(2)}, u32[]{:S(2)}) collective-permute-start(bf16[2,128,128]{2,1,0:T(8,128)(2,1)S(1)} %get-tuple-element.86), channel_id=1, source_target_pairs={{0,8},{4,12},{8,0},{12,4},{1,9},{5,13},{9,1},{13,5},{2,10},{6,14},... | collective-permute-start | bytes 196616 | tf_op jit(solution)/shard_map/ppermute | solution.py:465
  50.0 5.2 %collective-permute-start.19 = (bf16[2,128,128]{2,1,0:T(8,128)(2,1)S(1)}, bf16[2,128,128]{2,1,0:T(8,128)(2,1)S(1)}, u32[]{:S(2)}, u32[]{:S(2)}) collective-permute-start(bf16[2,128,128]{2,1,0:T(8,128)(2,1)S(1)} %get-tuple-element.89), channel_id=1, source_target_pairs={{0,4},{4,0},{8,12},{12,8},{1,5},{5,1},{9,13},{13,9},{2,6},{6,2},{1... | collective-permute-start | bytes 196616 | tf_op jit(solution)/shard_map/ppermute | solution.py:465

commit v20 on v18

--- a/solution.py
+++ b/solution.py
@@ -154,24 +154,33 @@
     pre_out[...] = mm(recv_hits[...], table)
 
 
+def live_sizes(count, edges, steps, case):
+    lower = 0
+    for step in steps:
+        size = edges * step // 8
+        live = count[0, 0]
+        fits = (live > lower) & (live <= size) if size < edges else live > lower
+        pl.when(fits)(lambda size=size: case(size))
+        lower = size
+
+
+def in_two(size):
+    middle = -(-size // 2 // LANES) * LANES
+    return [slice(0, middle), slice(middle, size)]
+
+
 def live_slots(count, edges, work, rest):
-    lower = 0
-    for size in (edges // 2, 3 * edges // 4, edges):
-
-        def case(size=size):
-            work([slice(0, size // 2), slice(size // 2, size)])
-            if size < edges:
-                rest(slice(size, edges))
-
-        live = count[0, 0]
-        pl.when((live > lower) & (live <= size) if size < edges else live > lower)(case)
-        lower = size
+    def case(size):
+        work(in_two(size))
+        if size < edges:
+            rest(slice(size, edges))
+
+    live_sizes(count, edges, (4, 5, 6, 7, 8), case)
 
 
 def gather_kernel(count, halo, hits, rows, rows_out, wide):
-    fill(wide, halo, wide.shape[1] // halo.shape[0], 0)
-
     def work(parts):
+        fill(wide, halo, wide.shape[1] // halo.shape[0], 0)
         part_of = slice(0, parts[-1].stop)
         gathered = mm_nt(hits[part_of], wide[...]).astype(BF16)
         rows_out[part_of] = rows[part_of] + gathered
@@ -187,9 +196,9 @@
     senders_out, slope_out, part_out, near_out, far_out, wide,
 ):
     half = recv_rows.shape[0] // 2
-    fill(wide, near, wide.shape[1] // near.shape[0], 0)
 
     def work(parts):
+        fill(wide, near, wide.shape[1] // near.shape[0], 0)
         sums = None
         for part_of in parts:
             raw = rows[part_of] + mm_nt(near_hits[part_of], wide[...]).astype(BF16)
@@ -237,28 +246,34 @@
 
 
 def process_kernel(
-    own_pre, outer_hits, to_hits, from_rows, to_rows, far, own, near, d_out, stack,
+    count, own_pre, outer_hits, to_hits, from_rows, to_rows, far, own, near, d_out, stack,
     mesh_out, sums_out, recv_out, near_out, far_out,
 ):
     cycle = own.shape[0]
     node_count = cycle // 2
     rim = node_count // 2
-    home = own[rim : rim + node_count]
-    block = jnp.concatenate([near[...], far[...]], axis=0)
-    table = jnp.concatenate(halves(mm(block, weight(stack, MS))), axis=0)
-    pre = own_pre[...] + mm(outer_hits[...], table)
-    value, slope = silu_parts(pre)
-    gate = mm(mm(to_rows[...], value.astype(BF16)).astype(BF16), weight(stack, MN))
-    gate_value, gate_slope = silu_parts(gate)
-    mesh_out[...] = (home.astype(F32) + gate_value).astype(BF16)
-    gate_two = (d_out[...].astype(F32) * gate_slope).astype(BF16)
-    back = jnp.concatenate(halves(mm_nt(gate_two, weight(stack, MN))), axis=0)
-    edge_slope = (mm(to_hits[...], back) * slope).astype(BF16)
-    sums = mm(from_rows[...], edge_slope)
-    recv_out[...] = mm(to_rows[...], edge_slope).astype(BF16)
-    sums_out[...] = sums
-    near_out[...] = sums[:cycle].astype(BF16)
-    far_out[...] = sums[2 * cycle :].astype(BF16)
+
+    def case(size):
+        live = slice(0, size)
+        home = own[rim : rim + node_count]
+        block = jnp.concatenate([near[...], far[...]], axis=0)
+        table = jnp.concatenate(halves(mm(block, weight(stack, MS))), axis=0)
+        pre = own_pre[live] + mm(outer_hits[live], table)
+        value, slope = silu_parts(pre)
+        total = mm(to_rows[:, live], value.astype(BF16))
+        gate = mm(total.astype(BF16), weight(stack, MN))
+        gate_value, gate_slope = silu_parts(gate)
+        mesh_out[...] = (home.astype(F32) + gate_value).astype(BF16)
+        gate_two = (d_out[...].astype(F32) * gate_slope).astype(BF16)
+        back = jnp.concatenate(halves(mm_nt(gate_two, weight(stack, MN))), axis=0)
+        edge_slope = (mm(to_hits[live], back) * slope).astype(BF16)
+        sums = mm(from_rows[:, live], edge_slope)
+        recv_out[...] = mm(to_rows[:, live], edge_slope).astype(BF16)
+        sums_out[...] = sums
+        near_out[...] = sums[:cycle].astype(BF16)
+        far_out[...] = sums[2 * cycle :].astype(BF16)
+
+    live_sizes(count, own_pre.shape[0], (2, 4, 6, 8), case)
 
 
 def block_of(x, dom_shift, lat_shift, doms, lats):
@@ -289,13 +304,11 @@
     far_out[half:] = jnp.where(even, home[:rim], home[rim:]).astype(BF16)
 
 
-def gradient_block(recv_hits, back, edge_slope, senders, shifts, doms, lats):
-    edges = recv_hits.shape[0]
+def gradient_block(recv_hits, back, edge_slope, senders, shifts, doms, lats, size=None):
     back = [block_of(back, *shift, doms, lats) for shift in shifts]
     back = back[0] if len(back) == 1 else jnp.concatenate(back, axis=1)
     total = None
-    for first in range(0, edges, edges // 2):
-        part_of = slice(first, first + edges // 2)
+    for part_of in in_two(size or recv_hits.shape[0]):
         weights = [block_of(edge_slope[part_of], *shift, doms, lats) for shift in shifts]
         weights = weights[0] if len(weights) == 1 else jnp.concatenate(weights, axis=1)
         slope = mm(recv_hits[part_of], back) * weights.astype(F32)
@@ -305,7 +318,7 @@
 
 
 def encode_grad_kernel(
-    recv_hits, part, near, far, home, node_slope, stack, senders, edge_slope,
+    count, recv_hits, part, near, far, home, node_slope, stack, senders, edge_slope,
     sends, back_out, total_out,
 ):
     half = part.shape[0] // 2
@@ -321,12 +334,16 @@
     back_out[...] = back
     lats = sends.shape[0] + 1
     doms = sends.shape[1] + 1
-    for i in range(1, lats):
-        for j in range(1, doms):
-            block = gradient_block(
-                recv_hits, back, edge_slope, senders, [(j, i)], doms, lats
-            )
-            sends[i - 1, j - 1] = block.astype(BF16)
+
+    def case(size):
+        for i in range(1, lats):
+            for j in range(1, doms):
+                block = gradient_block(
+                    recv_hits, back, edge_slope, senders, [(j, i)], doms, lats, size
+                )
+                sends[i - 1, j - 1] = block.astype(BF16)
+
+    live_sizes(count, recv_hits.shape[0], (4, 5, 6, 7, 8), case)
     for j in range(doms):
         total_out[j] = block_of(total, j, 0, doms, lats)
 
@@ -563,8 +580,9 @@
             ((cycle, latent), BF16),
             ((cycle, latent), BF16),
         ],
-        own_pre, outer_hits, to_hits, from_rows, to_rows, one_far, mesh_one, one_near, d_out,
-        stack,
+        mesh_count, own_pre, outer_hits, to_hits, from_rows, to_rows, one_far, mesh_one,
+        one_near, d_out, stack,
+        scalars=(0,),
     )
     from_near = lax.ppermute(to_near, "band", band_near)
     from_far = lax.ppermute(to_far, whole, band_far)
@@ -592,7 +610,9 @@
             ((2 * cycle, latent), BF16),
             ((doms, cycle, cols), BF16),
         ],
-        recv_hits, part, from_near, from_far, home, node_slope, stack, senders, edge_slope,
+        g2m_count, recv_hits, part, from_near, from_far, home, node_slope, stack, senders,
+        edge_slope,
+        scalars=(0,),
     )
     edge = (recv_hits, back, edge_slope, senders)
     came = [shifted(sends[i], "lat", i + 1) for i in range(lats - 1)]

time: 56.5 us -> 56.8 us (level)
  starting transfers between devices: 22.3 us -> 21.7 us
  waiting for transfers between devices: 13.5 us -> 14.1 us
where the time goes in v20:
time: 56.8 us; the launch traced here: 56.5 us
  starting transfers between devices  21.7 us (38%)
  waiting for transfers between devices  14.1 us (25%)
  Pallas kernels  13.4 us (24%)
  local copies, waits for them, and re-layouts  4.43 us (8%)
  between operations  2.17 us (4%)
  other arithmetic  0.74 us (1%)
    pallas_call x16, Pallas kernels, call(): pl.pallas_call(kernel, out_shape=[jax.ShapeDtypeStruct(shape, dtype) for...  13.4 us
    ppermute x3, starting transfers between devices, over_band(): return lax.ppermute(x, 'band', [(b, b ^ partner) for b in range(count)])  4.52 us
    unnamed x20, local copies, waits for them, and re-layouts  4.41 us
    ppermute x5, starting transfers between devices, shifted(): lax.ppermute(x, axis, [(i, (i + shift) % count) for i in range(count)])  4.24 us
    ppermute x3, waiting for transfers between devices, over_band(): return lax.ppermute(x, 'band', [(b, b ^ partner) for b in range(count)])  4.22 us
    ppermute x1, starting transfers between devices, on_device(): raw_near = lax.ppermute(grid, 'band', band_near)  4.15 us
    ppermute x2, waiting for transfers between devices, on_device(): from_far = lax.ppermute(to_far, around, ring_far)  3.52 us
    ppermute x2, starting transfers between devices, on_device(): from_far = lax.ppermute(to_far, around, ring_far)  3.23 us
  transfers between devices with their start and end apart: 20, of which 10 were waited for; matrix products, arithmetic and copies ran while one was open for 7% of the time, Pallas kernels for 11%

profile of v20, /device:TPU:0, one launch (start us, length us, event | category | flops | bytes accessed | tf_op | source)
XLA Modules:
  0.0 56.5 jit_solution(267848070372536438)
XLA Ops:
  1.2 4.1 %collective-permute-start = (bf16[3,227,360]{2,1,0:T(8,128)(2,1)}, bf16[3,227,360]{2,1,0:T(8,128)(2,1)S(1)}, u32[]{:S(2)}, u32[]{:S(2)}) collective-permute-start(bf16[3,227,360]{2,1,0:T(8,128)(2,1)} %bitcast.6), channel_id=1, source_target_pairs={{0,4},{4,0},{8,12},{12,8},{1,5},{5,1},{9,13},{13,9},{2,6},{6,2},{1... | collective-permute-start | bytes 1470968 | tf_op jit(solution)/shard_map/ppermute | solution.py:505
  6.6 0.7 %pad_add_fusion.indices = s32[1,1,3072]{2,1,0:T(1,128)S(1)} fusion(s32[1,1,512]{2,1,0:T(1,128)} %param.30, s32[1,1,512]{2,1,0:T(1,128)} %param.29, s32[1,1,1024]{2,1,0:T(1,128)} %param.27, s32[1,1,1024]{2,1,0:T(1,128)} %param.26), kind=kLoop, calls=%fused_computation.7 | loop fusion | flops 9216 | bytes 24576 | tf_op jit(solution)/shard_map/concatenate | solution.py:509
  7.3 1.0 %copy-done = bf16[3,360,227]{1,2,0:T(8,128)(2,1)S(1)} copy-done((bf16[3,360,227]{1,2,0:T(8,128)(2,1)S(1)}, bf16[3,360,227]{1,2,0:T(8,128)(2,1)}, u32[]{:S(2)}) %copy-start) | copy-done | bytes 490344
  8.4 1.9 %shard_map.175 = (bf16[1024,227]{1,0:T(8,128)(2,1)S(1)}, bf16[1024,128]{1,0:T(8,128)(2,1)S(1)}, bf16[64,1024]{1,0:T(8,128)(2,1)S(1)}, bf16[512,128]{1,0:T(8,128)...) custom-call(s32[1,1]{1,0:T(1,128)S(6)} %copy.25.count, ...), custom_call_target="tpu_custom_call" | custom-call | tf_op jit(solution)/shard_map/pallas_call | solution.py:445
  10.7 1.2 %collective-permute-start.2 = (bf16[32,512]{1,0:T(8,128)(2,1)}, bf16[32,512]{1,0:T(8,128)(2,1)S(1)}, u32[]{:S(2)}, u32[]{:S(2)}) collective-permute-start(bf16[32,512]{1,0:T(8,128)(2,1)} %mesh_in.3), channel_id=1, source_target_pairs={{0,1},{1,0},{2,3},{3,2},{4,5},{5,4},{6,7},{7,6},{8,9},{9,8},{10,11... | collective-permute-start | bytes 98312 | tf_op jit(solution)/shard_map/ppermute | solution.py:531
  12.0 1.1 %constant_dynamic-update-slice_fusion.6 = bf16[3299,512]{1,0:T(8,128)(2,1)S(1)} fusion(bf16[512,512]{1,0:T(8,128)(2,1)} %param.18), kind=kLoop, calls=%fused_computation.6 | loop fusion | bytes 1048576
  13.0 1.1 %constant_dynamic-update-slice_fusion.5 = bf16[3299,512]{1,0:T(8,128)(2,1)S(1)} fusion(bf16[3299,512]{1,0:T(8,128)(2,1)S(1)} %constant_dynamic-update-slice_fusion.6, bf16[512,512]{1,0:T(8,128)(2,1)} %param.19), kind=kLoop, calls=%fused_computation.5 | loop fusion | bytes 1048576
  14.1 1.1 %constant_dynamic-update-slice_fusion.4 = bf16[3299,512]{1,0:T(8,128)(2,1)S(1)} fusion(bf16[3299,512]{1,0:T(8,128)(2,1)S(1)} %constant_dynamic-update-slice_fusion.5, bf16[512,512]{1,0:T(8,128)(2,1)} %param.20), kind=kLoop, calls=%fused_computation.4 | loop fusion | bytes 1048576
  16.1 1.0 %shard_map.176.rows = bf16[1024,227]{1,0:T(8,128)(2,1)S(1)} custom-call(s32[1,1]{1,0:T(1,128)S(6)} %copy.25.count, bf16[3,227,360]{2,1,0:T(8,128)(2,1)S(1)} %collective-permute-done.1.halo, bf16[1024,1152]{1,0:T(8,128)(2,1)S(1)} %get-tuple-element.52.hits, bf16[1024,227]{1,0:T(8,128)(2,1)S(1)} %get-tuple-element.54.rows), custom_call_target="tpu_custom_call" | custom-call | tf_op jit(solution)/shard_map/pallas_call | solution.py:445
  17.4 2.9 %shard_map.178 = (bf16[1024,512]{1,0:T(8,128)(2,1)S(1)}, bf16[1024,512]{1,0:T(8,128)(2,1)S(1)}, f32[64,512]{1,0:T(8,128)S(1)}, bf16[32,512]{1,0:T(8,128)(2,1)S(1)}, bf16[32,512]{1,0:T(8,128)(2,1)S(1)}) custom-call(s32[1,1]{1,0:T(1,128)S(6)} %copy.25.count, bf16[3,227,360]{2,1,0:T(8,128)(2,1)S(1)} %collective-permute-done.near, ...), custom_call_target="tpu_custom_call" | custom-call | tf_op jit(solution)/shard_map/pallas_call | solution.py:445
  20.4 1.6 %collective-permute-start.5 = (bf16[32,512]{1,0:T(8,128)(2,1)S(1)}, bf16[32,512]{1,0:T(8,128)(2,1)S(1)}, u32[]{:S(2)}, u32[]{:S(2)}) collective-permute-start(bf16[32,512]{1,0:T(8,128)(2,1)S(1)} %get-tuple-element.59), channel_id=1, source_target_pairs={{0,3},{1,2},{2,1},{3,0},{4,7},{5,6},{6,5},{7,4},{8,11},{9,10},{10,... | collective-permute-start | bytes 98312 | tf_op jit(solution)/shard_map/ppermute | solution.py:559
  22.0 1.8 %collective-permute-done.5.far = bf16[32,512]{1,0:T(8,128)(2,1)S(1)} collective-permute-done((bf16[32,512]{1,0:T(8,128)(2,1)S(1)}, bf16[32,512]{1,0:T(8,128)(2,1)S(1)}, u32[]{:S(2)}, u32[]{:S(2)}) %collective-permute-start.5) | collective-permute-done | bytes 32800 | tf_op jit(solution)/shard_map/ppermute | solution.py:559
  24.0 1.3 %collective-permute-start.7 = (bf16[64,512]{1,0:T(8,128)(2,1)S(1)}, bf16[64,512]{1,0:T(8,128)(2,1)S(1)}, u32[]{:S(2)}, u32[]{:S(2)}) collective-permute-start(bf16[64,512]{1,0:T(8,128)(2,1)S(1)} %get-tuple-element.60.own.nodes), channel_id=1, source_target_pairs={{0,4},{4,0},{8,12},{12,8},{1,5},{5,1},{9,13},{13,9},{2,6},{6,2},{1... | collective-permute-start | bytes 196616 | tf_op jit(solution)/shard_map/ppermute | solution.py:566
  25.5 0.7 %shard_map.180.own_pre = f32[512,512]{1,0:T(8,128)S(1)} custom-call(bf16[512,128]{1,0:T(8,128)(2,1)S(1)} %get-tuple-element.48.own_hits, bf16[512,64]{1,0:T(8,128)(2,1)S(1)} %get-tuple-element.49.to_hits, bf16[64,512]{1,0:T(8,128)(2,1)S(1)} %get-tuple-element.60.own.nodes, bf16[3299,512]{1,0:T(8,128)(2,1)S(1)} %constant_dynamic-update-slice_fusion.stack), custom_call_target="tpu_custom_call" | custom-call | tf_op jit(solution)/shard_map/pallas_call | solution.py:445
  26.2 2.3 %collective-permute-done.7.near = bf16[64,512]{1,0:T(8,128)(2,1)S(1)} collective-permute-done((bf16[64,512]{1,0:T(8,128)(2,1)S(1)}, bf16[64,512]{1,0:T(8,128)(2,1)S(1)}, u32[]{:S(2)}, u32[]{:S(2)}) %collective-permute-start.7) | collective-permute-done | bytes 65568 | tf_op jit(solution)/shard_map/ppermute | solution.py:566
  28.6 2.3 %shard_map.181 = (bf16[32,512]{1,0:T(8,128)(2,1)}, f32[192,512]{1,0:T(8,128)S(1)}, bf16[32,512]{1,0:T(8,128)(2,1)S(1)}, bf16[64,512]{1,0:T(8,128)(2,1)S(1)}, bf16[64,512]{1,0:T(8,128)(2,1)S(1)}) custom-call(s32[1,1]{1,0:T(1,128)S(6)} %copy.26.mesh_count.count, f32[512,512]{1,0:T(8,128)S(1)} %shard_map.180.own_pre, ...), custom_call_target="tpu_custom_call" | custom-call | tf_op jit(solution)/shard_map/pallas_call | solution.py:445
  30.8 1.7 %collective-permute-start.8 = (bf16[64,512]{1,0:T(8,128)(2,1)S(1)}, bf16[64,512]{1,0:T(8,128)(2,1)S(1)}, u32[]{:S(2)}, u32[]{:S(2)}) collective-permute-start(bf16[64,512]{1,0:T(8,128)(2,1)S(1)} %get-tuple-element.66), channel_id=1, source_target_pairs={{0,4},{4,0},{8,12},{12,8},{1,5},{5,1},{9,13},{13,9},{2,6},{6,2},{1... | collective-permute-start | bytes 196616 | tf_op jit(solution)/shard_map/ppermute | solution.py:587
  32.5 1.5 %collective-permute-start.11 = (bf16[64,512]{1,0:T(8,128)(2,1)S(1)}, bf16[64,512]{1,0:T(8,128)(2,1)S(1)}, u32[]{:S(2)}, u32[]{:S(2)}) collective-permute-start(bf16[64,512]{1,0:T(8,128)(2,1)S(1)} %get-tuple-element.60.own.nodes), channel_id=1, source_target_pairs={{0,2},{2,0},{1,3},{3,1},{4,6},{6,4},{5,7},{7,5},{8,10},{10,8},{9,1... | collective-permute-start | bytes 196616 | tf_op jit(solution)/shard_map/ppermute | solution.py:477
  34.4 0.7 %collective-permute-done.8.near = bf16[64,512]{1,0:T(8,128)(2,1)S(1)} collective-permute-done((bf16[64,512]{1,0:T(8,128)(2,1)S(1)}, bf16[64,512]{1,0:T(8,128)(2,1)S(1)}, u32[]{:S(2)}, u32[]{:S(2)}) %collective-permute-start.8) | collective-permute-done | bytes 65568 | tf_op jit(solution)/shard_map/ppermute | solution.py:587
  35.2 1.6 %collective-permute-start.12 = (bf16[48,512]{1,0:T(8,128)(2,1)S(1)}, bf16[48,512]{1,0:T(8,128)(2,1)S(1)}, u32[]{:S(2)}, u32[]{:S(2)}) collective-permute-start(bf16[48,512]{1,0:T(8,128)(2,1)S(1)} %get-tuple-element.74), channel_id=1, source_target_pairs={{0,3},{1,2},{2,1},{3,0},{4,7},{5,6},{6,5},{7,4},{8,11},{9,10},{10,... | collective-permute-start | bytes 147464 | tf_op jit(solution)/shard_map/ppermute | solution.py:600
  37.1 1.7 %collective-permute-done.12.far = bf16[48,512]{1,0:T(8,128)(2,1)S(1)} collective-permute-done((bf16[48,512]{1,0:T(8,128)(2,1)S(1)}, bf16[48,512]{1,0:T(8,128)(2,1)S(1)}, u32[]{:S(2)}, u32[]{:S(2)}) %collective-permute-start.12) | collective-permute-done | bytes 49184 | tf_op jit(solution)/shard_map/ppermute | solution.py:600
  38.8 1.1 %shard_map.184 = (bf16[1,1,512,128]{3,2,1,0:T(8,128)(2,1)S(1)}, bf16[128,512]{1,0:T(8,128)(2,1)S(1)}, bf16[2,64,128]{2,1,0:T(8,128)(2,1)S(1)}) custom-call(s32[1,1]{1,0:T(1,128)S(6)} %copy.25.count, bf16[1024,128]{1,0:T(8,128)(2,1)S(1)} %get-tuple-element.56.recv_hits, f32[64,512]{1,0:T(8,128)S(1)} %get-tuple-element.71.part, ...), custom_call_target="tpu_custom_call" | custom-call | tf_op jit(solution)/shard_map/pallas_call | solution.py:445
  40.4 0.7 %shard_map.185 = (f32[1,512,128]{2,1,0:T(8,128)S(1)}, bf16[1,512,128]{2,1,0:T(8,128)(2,1)S(1)}) custom-call(bf16[1024,128]{1,0:T(8,128)(2,1)S(1)} %get-tuple-element.56.recv_hits, bf16[128,512]{1,0:T(8,128)(2,1)S(1)} %get-tuple-element.78.back, bf16[1024,512]{1,0:T(8,128)(2,1)S(1)} %get-tuple-element.77.edge_slope, ...), custom_call_target="tpu_custom_call" | custom-call | tf_op jit(solution)/shard_map/pallas_call | solution.py:445
  41.5 1.6 %collective-permute-start.15 = (bf16[320,128]{1,0:T(8,128)(2,1)S(1)}, bf16[320,128]{1,0:T(8,128)(2,1)S(1)}, u32[]{:S(2)}, u32[]{:S(2)}) collective-permute-start(bf16[320,128]{1,0:T(8,128)(2,1)S(1)} %bitcast.10), channel_id=1, source_target_pairs={{0,2},{2,0},{1,3},{3,1},{4,6},{6,4},{5,7},{7,5},{8,10},{10,8},{9,1... | collective-permute-start | bytes 245768 | tf_op jit(solution)/shard_map/ppermute | solution.py:477
  43.6 0.6 %shard_map.186.kept = f32[512,128]{1,0:T(8,128)S(1)} custom-call(bf16[1024,128]{1,0:T(8,128)(2,1)S(1)} %get-tuple-element.56.recv_hits, bf16[128,512]{1,0:T(8,128)(2,1)S(1)} %get-tuple-element.78.back, bf16[1024,512]{1,0:T(8,128)(2,1)S(1)} %get-tuple-element.77.edge_slope, bf16[512,1024]{1,0:T(8,128)(2,1)S(1)} %get-tuple-element.76.senders, ...), custom_call_target="tpu_custom_call" | custom-call | tf_op jit(solution)/shard_map/pallas_call | solution.py:445
  44.2 2.6 %collective-permute-done.15.refs_0_ = bf16[320,128]{1,0:T(8,128)(2,1)S(1)} collective-permute-done((bf16[320,128]{1,0:T(8,128)(2,1)S(1)}, bf16[320,128]{1,0:T(8,128)(2,1)S(1)}, u32[]{:S(2)}, u32[]{:S(2)}) %collective-permute-start.15) | collective-permute-done | bytes 81952 | tf_op jit(solution)/shard_map/ppermute | solution.py:477
  47.1 1.7 %collective-permute-start.16 = (bf16[2,128,128]{2,1,0:T(8,128)(2,1)S(1)}, bf16[2,128,128]{2,1,0:T(8,128)(2,1)S(1)}, u32[]{:S(2)}, u32[]{:S(2)}) collective-permute-start(bf16[2,128,128]{2,1,0:T(8,128)(2,1)S(1)} %get-tuple-element.85), channel_id=1, source_target_pairs={{0,12},{4,8},{8,4},{12,0},{1,13},{5,9},{9,5},{13,1},{2,14},{6,10},... | collective-permute-start | bytes 196616 | tf_op jit(solution)/shard_map/ppermute | solution.py:482
  48.8 1.8 %collective-permute-start.17 = (bf16[2,128,128]{2,1,0:T(8,128)(2,1)S(1)}, bf16[2,128,128]{2,1,0:T(8,128)(2,1)S(1)}, u32[]{:S(2)}, u32[]{:S(2)}) collective-permute-start(bf16[2,128,128]{2,1,0:T(8,128)(2,1)S(1)} %get-tuple-element.86), channel_id=1, source_target_pairs={{0,8},{4,12},{8,0},{12,4},{1,9},{5,13},{9,1},{13,5},{2,10},{6,14},... | collective-permute-start | bytes 196616 | tf_op jit(solution)/shard_map/ppermute | solution.py:482
  50.6 1.0 %collective-permute-start.19 = (bf16[2,128,128]{2,1,0:T(8,128)(2,1)S(1)}, bf16[2,128,128]{2,1,0:T(8,128)(2,1)S(1)}, u32[]{:S(2)}, u32[]{:S(2)}) collective-permute-start(bf16[2,128,128]{2,1,0:T(8,128)(2,1)S(1)} %get-tuple-element.89), channel_id=1, source_target_pairs={{0,4},{4,0},{8,12},{12,8},{1,5},{5,1},{9,13},{13,9},{2,6},{6,2},{1... | collective-permute-start | bytes 196616 | tf_op jit(solution)/shard_map/ppermute | solution.py:482
  51.6 2.1 %collective-permute-done.16.refs_0_ = bf16[2,128,128]{2,1,0:T(8,128)(2,1)S(1)} collective-permute-done((bf16[2,128,128]{2,1,0:T(8,128)(2,1)S(1)}, bf16[2,128,128]{2,1,0:T(8,128)(2,1)S(1)}, u32[]{:S(2)}, u32[]{:S(2)}) %collective-permute-start.16) | collective-permute-done | bytes 65568 | tf_op jit(solution)/shard_map/ppermute | solution.py:482
  53.7 2.1 %collective-permute-done.17.refs_1_ = bf16[2,128,128]{2,1,0:T(8,128)(2,1)S(1)} collective-permute-done((bf16[2,128,128]{2,1,0:T(8,128)(2,1)S(1)}, bf16[2,128,128]{2,1,0:T(8,128)(2,1)S(1)}, u32[]{:S(2)}, u32[]{:S(2)}) %collective-permute-start.17) | collective-permute-done | bytes 65568 | tf_op jit(solution)/shard_map/ppermute | solution.py:482
  55.9 0.7 %shard_map.190 = (f32[128,128]{1,0:T(8,128)}, f32[128,128]{1,0:T(8,128)}) custom-call(bf16[2,128,128]{2,1,0:T(8,128)(2,1)S(1)} %collective-permute-done.16.refs_0_, bf16[2,128,128]{2,1,0:T(8,128)(2,1)S(1)} %collective-permute-done.17.refs_1_, bf16[2,128,128]{2,1,0:T(8,128)(2,1)S(1)} %collective-permute-done.19.refs_2_, ...), custom_call_target="tpu_custom_call" | custom-call | tf_op jit(solution)/shard_map/pallas_call | solution.py:445
  (46 shorter events, 4.9 us)
Async XLA Ops:
  0.6 15.4 %collective-permute-start.1 = (bf16[3,227,360]{2,1,0:T(8,128)(2,1)}, bf16[3,227,360]{2,1,0:T(8,128)(2,1)S(1)}, u32[]{:S(2)}, u32[]{:S(2)}) collective-permute-start(bf16[3,227,360]{2,1,0:T(8,128)(2,1)} %bitcast.5), channel_id=1, source_target_pairs={{0,1},{1,0},{2,3},{3,2},{4,8},{5,9},{6,10},{7,11},{8,4},{9,5},{10,... | collective-permute-start | bytes 1470968 | tf_op jit(solution)/shard_map/ppermute | solution.py:506
  1.2 16.3 %collective-permute-start = (bf16[3,227,360]{2,1,0:T(8,128)(2,1)}, bf16[3,227,360]{2,1,0:T(8,128)(2,1)S(1)}, u32[]{:S(2)}, u32[]{:S(2)}) collective-permute-start(bf16[3,227,360]{2,1,0:T(8,128)(2,1)} %bitcast.6), channel_id=1, source_target_pairs={{0,4},{4,0},{8,12},{12,8},{1,5},{5,1},{9,13},{13,9},{2,6},{6,2},{1... | collective-permute-start | bytes 1470968 | tf_op jit(solution)/shard_map/ppermute | solution.py:505
  7.3 1.0 %copy-start = (bf16[3,360,227]{1,2,0:T(8,128)(2,1)S(1)}, bf16[3,360,227]{1,2,0:T(8,128)(2,1)}, u32[]{:S(2)}) copy-start(bf16[3,360,227]{1,2,0:T(8,128)(2,1)} %param.16) | copy-start | bytes 1470964
  8.4 6.8 %copy-start.3 = (bf16[512,512]{1,0:T(8,128)(2,1)S(1)}, bf16[512,512]{1,0:T(8,128)(2,1)}, u32[]{:S(2)}) copy-start(bf16[512,512]{1,0:T(8,128)(2,1)} %param.21) | copy-start | bytes 1572868
  8.4 6.9 %copy-start.4 = (bf16[512,512]{1,0:T(8,128)(2,1)S(1)}, bf16[512,512]{1,0:T(8,128)(2,1)}, u32[]{:S(2)}) copy-start(bf16[512,512]{1,0:T(8,128)(2,1)} %param.22) | copy-start | bytes 1572868
  8.4 6.9 %copy-start.5 = (bf16[512,512]{1,0:T(8,128)(2,1)S(1)}, bf16[512,512]{1,0:T(8,128)(2,1)}, u32[]{:S(2)}) copy-start(bf16[512,512]{1,0:T(8,128)(2,1)} %param.23) | copy-start | bytes 1572868
  8.4 7.0 %copy-start.6 = (bf16[227,512]{1,0:T(8,128)(2,1)S(1)}, bf16[227,512]{1,0:T(8,128)(2,1)}, u32[]{:S(2)}) copy-start(bf16[227,512]{1,0:T(8,128)(2,1)} %param.17) | copy-start | bytes 697348
  10.3 5.1 %copy-start.1 = (bf16[32,512]{1,0:T(8,128)(2,1)S(1)}, bf16[32,512]{1,0:T(8,128)(2,1)}, u32[]{:S(2)}) copy-start(bf16[32,512]{1,0:T(8,128)(2,1)} %mesh_in.3) | copy-start | bytes 98308
  10.3 5.1 %collective-permute-start.3 = (bf16[32,512]{1,0:T(8,128)(2,1)}, bf16[32,512]{1,0:T(8,128)(2,1)S(1)}, u32[]{:S(2)}, u32[]{:S(2)}) collective-permute-start(bf16[32,512]{1,0:T(8,128)(2,1)} %mesh_in.3), channel_id=1, source_target_pairs={{0,3},{1,2},{2,1},{3,0},{4,7},{5,6},{6,5},{7,4},{8,11},{9,10},{10,... | collective-permute-start | bytes 98312 | tf_op jit(solution)/shard_map/ppermute | solution.py:532
  10.7 4.7 %collective-permute-start.2 = (bf16[32,512]{1,0:T(8,128)(2,1)}, bf16[32,512]{1,0:T(8,128)(2,1)S(1)}, u32[]{:S(2)}, u32[]{:S(2)}) collective-permute-start(bf16[32,512]{1,0:T(8,128)(2,1)} %mesh_in.3), channel_id=1, source_target_pairs={{0,1},{1,0},{2,3},{3,2},{4,5},{5,4},{6,7},{7,6},{8,9},{9,8},{10,11... | collective-permute-start | bytes 98312 | tf_op jit(solution)/shard_map/ppermute | solution.py:531
  20.3 1.7 %collective-permute-start.4 = (bf16[32,512]{1,0:T(8,128)(2,1)S(1)}, bf16[32,512]{1,0:T(8,128)(2,1)S(1)}, u32[]{:S(2)}, u32[]{:S(2)}) collective-permute-start(bf16[32,512]{1,0:T(8,128)(2,1)S(1)} %get-tuple-element.58), channel_id=1, source_target_pairs={{0,1},{1,0},{2,3},{3,2},{4,5},{5,4},{6,7},{7,6},{8,9},{9,8},{10,11... | collective-permute-start | bytes 98312 | tf_op jit(solution)/shard_map/ppermute | solution.py:560
  20.4 3.4 %collective-permute-start.5 = (bf16[32,512]{1,0:T(8,128)(2,1)S(1)}, bf16[32,512]{1,0:T(8,128)(2,1)S(1)}, u32[]{:S(2)}, u32[]{:S(2)}) collective-permute-start(bf16[32,512]{1,0:T(8,128)(2,1)S(1)} %get-tuple-element.59), channel_id=1, source_target_pairs={{0,3},{1,2},{2,1},{3,0},{4,7},{5,6},{6,5},{7,4},{8,11},{9,10},{10,... | collective-permute-start | bytes 98312 | tf_op jit(solution)/shard_map/ppermute | solution.py:559
  23.8 4.8 %copy-start.2 = (bf16[32,512]{1,0:T(8,128)(2,1)S(1)}, bf16[32,512]{1,0:T(8,128)(2,1)}, u32[]{:S(2)}) copy-start(bf16[32,512]{1,0:T(8,128)(2,1)} %d_out.3) | copy-start | bytes 98308
  24.0 4.5 %collective-permute-start.7 = (bf16[64,512]{1,0:T(8,128)(2,1)S(1)}, bf16[64,512]{1,0:T(8,128)(2,1)S(1)}, u32[]{:S(2)}, u32[]{:S(2)}) collective-permute-start(bf16[64,512]{1,0:T(8,128)(2,1)S(1)} %get-tuple-element.60.own.nodes), channel_id=1, source_target_pairs={{0,4},{4,0},{8,12},{12,8},{1,5},{5,1},{9,13},{13,9},{2,6},{6,2},{1... | collective-permute-start | bytes 196616 | tf_op jit(solution)/shard_map/ppermute | solution.py:566
  25.4 3.2 %collective-permute-start.6 = (bf16[64,512]{1,0:T(8,128)(2,1)S(1)}, bf16[64,512]{1,0:T(8,128)(2,1)S(1)}, u32[]{:S(2)}, u32[]{:S(2)}) collective-permute-start(bf16[64,512]{1,0:T(8,128)(2,1)S(1)} %get-tuple-element.60.own.nodes), channel_id=1, source_target_pairs={{0,1},{1,0},{2,3},{3,2},{4,8},{5,9},{6,10},{7,11},{8,4},{9,5},{10,... | collective-permute-start | bytes 196616 | tf_op jit(solution)/shard_map/ppermute | solution.py:567
  30.8 4.3 %collective-permute-start.8 = (bf16[64,512]{1,0:T(8,128)(2,1)S(1)}, bf16[64,512]{1,0:T(8,128)(2,1)S(1)}, u32[]{:S(2)}, u32[]{:S(2)}) collective-permute-start(bf16[64,512]{1,0:T(8,128)(2,1)S(1)} %get-tuple-element.66), channel_id=1, source_target_pairs={{0,4},{4,0},{8,12},{12,8},{1,5},{5,1},{9,13},{13,9},{2,6},{6,2},{1... | collective-permute-start | bytes 196616 | tf_op jit(solution)/shard_map/ppermute | solution.py:587
  32.5 2.5 %collective-permute-start.9 = (bf16[64,512]{1,0:T(8,128)(2,1)S(1)}, bf16[64,512]{1,0:T(8,128)(2,1)S(1)}, u32[]{:S(2)}, u32[]{:S(2)}) collective-permute-start(bf16[64,512]{1,0:T(8,128)(2,1)S(1)} %get-tuple-element.67), channel_id=1, source_target_pairs={{0,1},{1,0},{2,3},{3,2},{4,8},{5,9},{6,10},{7,11},{8,4},{9,5},{10,... | collective-permute-start | bytes 196616 | tf_op jit(solution)/shard_map/ppermute | solution.py:588
  32.5 4.5 %collective-permute-start.11 = (bf16[64,512]{1,0:T(8,128)(2,1)S(1)}, bf16[64,512]{1,0:T(8,128)(2,1)S(1)}, u32[]{:S(2)}, u32[]{:S(2)}) collective-permute-start(bf16[64,512]{1,0:T(8,128)(2,1)S(1)} %get-tuple-element.60.own.nodes), channel_id=1, source_target_pairs={{0,2},{2,0},{1,3},{3,1},{4,6},{6,4},{5,7},{7,5},{8,10},{10,8},{9,1... | collective-permute-start | bytes 196616 | tf_op jit(solution)/shard_map/ppermute | solution.py:477
  35.1 1.9 %collective-permute-start.10 = (bf16[48,512]{1,0:T(8,128)(2,1)S(1)}, bf16[48,512]{1,0:T(8,128)(2,1)S(1)}, u32[]{:S(2)}, u32[]{:S(2)}) collective-permute-start(bf16[48,512]{1,0:T(8,128)(2,1)S(1)} %get-tuple-element.72), channel_id=1, source_target_pairs={{0,1},{1,0},{2,3},{3,2},{4,5},{5,4},{6,7},{7,6},{8,9},{9,8},{10,11... | collective-permute-start | bytes 147464 | tf_op jit(solution)/shard_map/ppermute | solution.py:601
  35.2 3.6 %collective-permute-start.12 = (bf16[48,512]{1,0:T(8,128)(2,1)S(1)}, bf16[48,512]{1,0:T(8,128)(2,1)S(1)}, u32[]{:S(2)}, u32[]{:S(2)}) collective-permute-start(bf16[48,512]{1,0:T(8,128)(2,1)S(1)} %get-tuple-element.74), channel_id=1, source_target_pairs={{0,3},{1,2},{2,1},{3,0},{4,7},{5,6},{6,5},{7,4},{8,11},{9,10},{10,... | collective-permute-start | bytes 147464 | tf_op jit(solution)/shard_map/ppermute | solution.py:600
  39.9 1.5 %collective-permute-start.14 = (bf16[1,512,128]{2,1,0:T(8,128)(2,1)S(1)}, bf16[1,512,128]{2,1,0:T(8,128)(2,1)S(1)}, u32[]{:S(2)}, u32[]{:S(2)}) collective-permute-start(bf16[1,512,128]{2,1,0:T(8,128)(2,1)S(1)} %bitcast.8), channel_id=1, source_target_pairs={{0,1},{1,0},{2,3},{3,2},{4,5},{5,4},{6,7},{7,6},{8,9},{9,8},{10,11... | collective-permute-start | bytes 393224 | tf_op jit(solution)/shard_map/ppermute | solution.py:477
  41.1 2.4 %collective-permute-start.13 = (bf16[512,128]{1,0:T(8,128)(2,1)S(1)}, bf16[512,128]{1,0:T(8,128)(2,1)S(1)}, u32[]{:S(2)}, u32[]{:S(2)}) collective-permute-start(bf16[512,128]{1,0:T(8,128)(2,1)S(1)} %bitcast.9), channel_id=1, source_target_pairs={{0,1},{1,0},{2,3},{3,2},{4,5},{5,4},{6,7},{7,6},{8,9},{9,8},{10,11... | collective-permute-start | bytes 393224 | tf_op jit(solution)/shard_map/ppermute | solution.py:477
  41.5 5.4 %collective-permute-start.15 = (bf16[320,128]{1,0:T(8,128)(2,1)S(1)}, bf16[320,128]{1,0:T(8,128)(2,1)S(1)}, u32[]{:S(2)}, u32[]{:S(2)}) collective-permute-start(bf16[320,128]{1,0:T(8,128)(2,1)S(1)} %bitcast.10), channel_id=1, source_target_pairs={{0,2},{2,0},{1,3},{3,1},{4,6},{6,4},{5,7},{7,5},{8,10},{10,8},{9,1... | collective-permute-start | bytes 245768 | tf_op jit(solution)/shard_map/ppermute | solution.py:477
  43.0 7.6 %collective-permute-start.18 = (bf16[256,128]{1,0:T(8,128)(2,1)S(1)}, bf16[256,128]{1,0:T(8,128)(2,1)S(1)}, u32[]{:S(2)}, u32[]{:S(2)}) collective-permute-start(bf16[256,128]{1,0:T(8,128)(2,1)S(1)} %bitcast.11), channel_id=1, source_target_pairs={{0,2},{2,0},{1,3},{3,1},{4,6},{6,4},{5,7},{7,5},{8,10},{10,8},{9,1... | collective-permute-start | bytes 196616 | tf_op jit(solution)/shard_map/ppermute | solution.py:477
  47.1 6.6 %collective-permute-start.16 = (bf16[2,128,128]{2,1,0:T(8,128)(2,1)S(1)}, bf16[2,128,128]{2,1,0:T(8,128)(2,1)S(1)}, u32[]{:S(2)}, u32[]{:S(2)}) collective-permute-start(bf16[2,128,128]{2,1,0:T(8,128)(2,1)S(1)} %get-tuple-element.85), channel_id=1, source_target_pairs={{0,12},{4,8},{8,4},{12,0},{1,13},{5,9},{9,5},{13,1},{2,14},{6,10},... | collective-permute-start | bytes 196616 | tf_op jit(solution)/shard_map/ppermute | solution.py:482
  48.8 7.1 %collective-permute-start.17 = (bf16[2,128,128]{2,1,0:T(8,128)(2,1)S(1)}, bf16[2,128,128]{2,1,0:T(8,128)(2,1)S(1)}, u32[]{:S(2)}, u32[]{:S(2)}) collective-permute-start(bf16[2,128,128]{2,1,0:T(8,128)(2,1)S(1)} %get-tuple-element.86), channel_id=1, source_target_pairs={{0,8},{4,12},{8,0},{12,4},{1,9},{5,13},{9,1},{13,5},{2,10},{6,14},... | collective-permute-start | bytes 196616 | tf_op jit(solution)/shard_map/ppermute | solution.py:482
  50.6 5.2 %collective-permute-start.19 = (bf16[2,128,128]{2,1,0:T(8,128)(2,1)S(1)}, bf16[2,128,128]{2,1,0:T(8,128)(2,1)S(1)}, u32[]{:S(2)}, u32[]{:S(2)}) collective-permute-start(bf16[2,128,128]{2,1,0:T(8,128)(2,1)S(1)} %get-tuple-element.89), channel_id=1, source_target_pairs={{0,4},{4,0},{8,12},{12,8},{1,5},{5,1},{9,13},{13,9},{2,6},{6,2},{1... | collective-permute-start | bytes 196616 | tf_op jit(solution)/shard_map/ppermute | solution.py:482

commit v21 on v19

--- a/solution.py
+++ b/solution.py
@@ -368,8 +368,8 @@
         first_out[j, (bands - near) * rows :] = total[j + 1]
 
 
-def own_block_kernel(recv_hits, back, edge_slope, senders, *refs):
-    *came, out = refs
+def own_block_kernel(recv_hits, back, edge_slope, senders, total, nodes, *refs):
+    *came, out, sums_out = refs
     lats = len(came) + 1
     doms = back.shape[1] // out.shape[1] // lats
     block = gradient_block(
@@ -378,16 +378,17 @@
     for part in came:
         block = block + part[...].astype(F32)
     out[...] = block
-
-
-def first_kernel(kept, total, nodes, *refs):
-    doms = total.shape[0]
+    sums_out[...] = mm_tn(nodes[...], total[0])
+
+
+def first_kernel(kept, own_sums, *refs):
+    doms = lax.axis_size("dom")
     came, (*sends_out, sums) = refs[: 2 * (doms - 1)], refs[2 * (doms - 1) :]
     came, came_nodes = came[: doms - 1], came[doms - 1 :]
     far = len(sends_out)
     near = lax.axis_size("band") - far
     rows = sends_out[0].shape[1]
-    second = mm_tn(nodes[...], total[0])
+    second = own_sums[...]
     for part, part_nodes in zip(came, came_nodes):
         second = second + mm_tn(part_nodes[...], part[far * rows :])
     sums[...] = second
@@ -614,12 +615,14 @@
     )
     first = [shifted(first[i], "dom", i + 1) for i in range(doms - 1)]
     second = [shifted(second[i], "dom", i + 1) for i in range(doms - 1)]
-    (kept,) = call(own_block_kernel, [(block, F32)], *edge, *own_came)
+    kept, own_sums = call(
+        own_block_kernel, [(block, F32)] * 2, *edge, total, mesh_one, *own_came
+    )
     pair = (2, rows, cols)
     *far_sends, sums = call(
         first_kernel,
         [(pair, BF16)] * far + [(block, F32)],
-        kept, total, mesh_one, *first, *dom_nodes,
+        kept, own_sums, *first, *dom_nodes,
     )
     came = [over_band(x, bands - far + i) for i, x in reversed(list(enumerate(far_sends)))]
     own, *near_sends = call(

time: 56.2 us -> 56.2 us (level)
  no operation moved by 1% of the time
where the time goes in v21:
time: 56.2 us; the launch traced here: 55.8 us
  starting transfers between devices  21.9 us (39%)
  waiting for transfers between devices  13.9 us (25%)
  Pallas kernels  12.7 us (23%)
  local copies, waits for them, and re-layouts  4.43 us (8%)
  between operations  2.17 us (4%)
  other arithmetic  0.74 us (1%)
    pallas_call x16, Pallas kernels, call(): pl.pallas_call(kernel, out_shape=[jax.ShapeDtypeStruct(shape, dtype) for...  12.7 us
    ppermute x3, starting transfers between devices, over_band(): return lax.ppermute(x, 'band', [(b, b ^ partner) for b in range(count)])  4.52 us
    unnamed x20, local copies, waits for them, and re-layouts  4.41 us
    ppermute x5, starting transfers between devices, shifted(): lax.ppermute(x, axis, [(i, (i + shift) % count) for i in range(count)])  4.22 us
    ppermute x3, waiting for transfers between devices, over_band(): return lax.ppermute(x, 'band', [(b, b ^ partner) for b in range(count)])  4.19 us
    ppermute x1, starting transfers between devices, on_device(): raw_near = lax.ppermute(grid, 'band', band_near)  4.15 us
    ppermute x2, waiting for transfers between devices, on_device(): from_far = lax.ppermute(to_far, around, ring_far)  3.4 us
    ppermute x2, starting transfers between devices, on_device(): from_far = lax.ppermute(to_far, around, ring_far)  3.22 us
  transfers between devices with their start and end apart: 20, of which 10 were waited for; matrix products, arithmetic and copies ran while one was open for 7% of the time, Pallas kernels for 11%

profile of v21, /device:TPU:0, one launch (start us, length us, event | category | flops | bytes accessed | tf_op | source)
XLA Modules:
  0.0 55.8 jit_solution(16379160768488279774)
XLA Ops:
  1.2 4.1 %collective-permute-start = (bf16[3,227,360]{2,1,0:T(8,128)(2,1)}, bf16[3,227,360]{2,1,0:T(8,128)(2,1)S(1)}, u32[]{:S(2)}, u32[]{:S(2)}) collective-permute-start(bf16[3,227,360]{2,1,0:T(8,128)(2,1)} %bitcast.6), channel_id=1, source_target_pairs={{0,4},{4,0},{8,12},{12,8},{1,5},{5,1},{9,13},{13,9},{2,6},{6,2},{1... | collective-permute-start | bytes 1470968 | tf_op jit(solution)/shard_map/ppermute | solution.py:489
  6.6 0.7 %pad_add_fusion.indices = s32[1,1,3072]{2,1,0:T(1,128)S(1)} fusion(s32[1,1,512]{2,1,0:T(1,128)} %param.30, s32[1,1,512]{2,1,0:T(1,128)} %param.29, s32[1,1,1024]{2,1,0:T(1,128)} %param.27, s32[1,1,1024]{2,1,0:T(1,128)} %param.26), kind=kLoop, calls=%fused_computation.7 | loop fusion | flops 9216 | bytes 24576 | tf_op jit(solution)/shard_map/concatenate | solution.py:493
  7.3 1.0 %copy-done = bf16[3,360,227]{1,2,0:T(8,128)(2,1)S(1)} copy-done((bf16[3,360,227]{1,2,0:T(8,128)(2,1)S(1)}, bf16[3,360,227]{1,2,0:T(8,128)(2,1)}, u32[]{:S(2)}) %copy-start) | copy-done | bytes 490344
  8.4 1.9 %shard_map.175 = (bf16[1024,227]{1,0:T(8,128)(2,1)S(1)}, bf16[1024,128]{1,0:T(8,128)(2,1)S(1)}, bf16[64,1024]{1,0:T(8,128)(2,1)S(1)}, bf16[512,128]{1,0:T(8,128)...) custom-call(s32[1,1]{1,0:T(1,128)S(6)} %copy.25.count, ...), custom_call_target="tpu_custom_call" | custom-call | tf_op jit(solution)/shard_map/pallas_call | solution.py:429
  10.7 1.2 %collective-permute-start.2 = (bf16[32,512]{1,0:T(8,128)(2,1)}, bf16[32,512]{1,0:T(8,128)(2,1)S(1)}, u32[]{:S(2)}, u32[]{:S(2)}) collective-permute-start(bf16[32,512]{1,0:T(8,128)(2,1)} %mesh_in.3), channel_id=1, source_target_pairs={{0,1},{1,0},{2,3},{3,2},{4,5},{5,4},{6,7},{7,6},{8,9},{9,8},{10,11... | collective-permute-start | bytes 98312 | tf_op jit(solution)/shard_map/ppermute | solution.py:515
  12.0 1.1 %constant_dynamic-update-slice_fusion.6 = bf16[3299,512]{1,0:T(8,128)(2,1)S(1)} fusion(bf16[512,512]{1,0:T(8,128)(2,1)} %param.18), kind=kLoop, calls=%fused_computation.6 | loop fusion | bytes 1048576
  13.0 1.1 %constant_dynamic-update-slice_fusion.5 = bf16[3299,512]{1,0:T(8,128)(2,1)S(1)} fusion(bf16[3299,512]{1,0:T(8,128)(2,1)S(1)} %constant_dynamic-update-slice_fusion.6, bf16[512,512]{1,0:T(8,128)(2,1)} %param.19), kind=kLoop, calls=%fused_computation.5 | loop fusion | bytes 1048576
  14.1 1.1 %constant_dynamic-update-slice_fusion.4 = bf16[3299,512]{1,0:T(8,128)(2,1)S(1)} fusion(bf16[3299,512]{1,0:T(8,128)(2,1)S(1)} %constant_dynamic-update-slice_fusion.5, bf16[512,512]{1,0:T(8,128)(2,1)} %param.20), kind=kLoop, calls=%fused_computation.4 | loop fusion | bytes 1048576
  15.4 0.6 %shard_map.177.recv_pre = f32[1024,512]{1,0:T(8,128)S(1)} custom-call(bf16[32,512]{1,0:T(8,128)(2,1)S(1)} %collective-permute-done.2.near.mesh_near, bf16[32,512]{1,0:T(8,128)(2,1)S(1)} %collective-permute-done.3.far.mesh_far, bf16[32,512]{1,0:T(8,128)(2,1)S(1)} %copy-done.1, bf16[1024,128]{1,0:T(8,128)(2,1)S(1)} %get-tuple-element.58.recv_hits, ...), custom_call_target="tpu_custom_call" | custom-call | tf_op jit(solution)/shard_map/pallas_call | solution.py:429
  16.1 1.0 %shard_map.176.rows = bf16[1024,227]{1,0:T(8,128)(2,1)S(1)} custom-call(s32[1,1]{1,0:T(1,128)S(6)} %copy.25.count, bf16[3,227,360]{2,1,0:T(8,128)(2,1)S(1)} %collective-permute-done.1.halo, bf16[1024,1152]{1,0:T(8,128)(2,1)S(1)} %get-tuple-element.54.hits, bf16[1024,227]{1,0:T(8,128)(2,1)S(1)} %get-tuple-element.56.rows), custom_call_target="tpu_custom_call" | custom-call | tf_op jit(solution)/shard_map/pallas_call | solution.py:429
  17.4 2.9 %shard_map.178 = (bf16[1024,512]{1,0:T(8,128)(2,1)S(1)}, bf16[1024,512]{1,0:T(8,128)(2,1)S(1)}, f32[64,512]{1,0:T(8,128)S(1)}, bf16[32,512]{1,0:T(8,128)(2,1)S(1)}, bf16[32,512]{1,0:T(8,128)(2,1)S(1)}) custom-call(s32[1,1]{1,0:T(1,128)S(6)} %copy.25.count, bf16[3,227,360]{2,1,0:T(8,128)(2,1)S(1)} %collective-permute-done.near, ...), custom_call_target="tpu_custom_call" | custom-call | tf_op jit(solution)/shard_map/pallas_call | solution.py:429
  20.4 1.6 %collective-permute-start.5 = (bf16[32,512]{1,0:T(8,128)(2,1)S(1)}, bf16[32,512]{1,0:T(8,128)(2,1)S(1)}, u32[]{:S(2)}, u32[]{:S(2)}) collective-permute-start(bf16[32,512]{1,0:T(8,128)(2,1)S(1)} %get-tuple-element.61), channel_id=1, source_target_pairs={{0,3},{1,2},{2,1},{3,0},{4,7},{5,6},{6,5},{7,4},{8,11},{9,10},{10,... | collective-permute-start | bytes 98312 | tf_op jit(solution)/shard_map/ppermute | solution.py:543
  22.0 1.8 %collective-permute-done.5.far = bf16[32,512]{1,0:T(8,128)(2,1)S(1)} collective-permute-done((bf16[32,512]{1,0:T(8,128)(2,1)S(1)}, bf16[32,512]{1,0:T(8,128)(2,1)S(1)}, u32[]{:S(2)}, u32[]{:S(2)}) %collective-permute-start.5) | collective-permute-done | bytes 32800 | tf_op jit(solution)/shard_map/ppermute | solution.py:543
  24.0 1.3 %collective-permute-start.7 = (bf16[64,512]{1,0:T(8,128)(2,1)S(1)}, bf16[64,512]{1,0:T(8,128)(2,1)S(1)}, u32[]{:S(2)}, u32[]{:S(2)}) collective-permute-start(bf16[64,512]{1,0:T(8,128)(2,1)S(1)} %get-tuple-element.62.own.nodes), channel_id=1, source_target_pairs={{0,4},{4,0},{8,12},{12,8},{1,5},{5,1},{9,13},{13,9},{2,6},{6,2},{1... | collective-permute-start | bytes 196616 | tf_op jit(solution)/shard_map/ppermute | solution.py:550
  25.5 0.7 %shard_map.180.own_pre = f32[512,512]{1,0:T(8,128)S(1)} custom-call(bf16[512,128]{1,0:T(8,128)(2,1)S(1)} %get-tuple-element.50.own_hits, bf16[512,64]{1,0:T(8,128)(2,1)S(1)} %get-tuple-element.51.to_hits, bf16[64,512]{1,0:T(8,128)(2,1)S(1)} %get-tuple-element.62.own.nodes, bf16[3299,512]{1,0:T(8,128)(2,1)S(1)} %constant_dynamic-update-slice_fusion.stack), custom_call_target="tpu_custom_call" | custom-call | tf_op jit(solution)/shard_map/pallas_call | solution.py:429
  26.2 2.3 %collective-permute-done.7.near = bf16[64,512]{1,0:T(8,128)(2,1)S(1)} collective-permute-done((bf16[64,512]{1,0:T(8,128)(2,1)S(1)}, bf16[64,512]{1,0:T(8,128)(2,1)S(1)}, u32[]{:S(2)}, u32[]{:S(2)}) %collective-permute-start.7) | collective-permute-done | bytes 65568 | tf_op jit(solution)/shard_map/ppermute | solution.py:550
  28.6 1.7 %shard_map.181 = (bf16[32,512]{1,0:T(8,128)(2,1)}, f32[192,512]{1,0:T(8,128)S(1)}, bf16[32,512]{1,0:T(8,128)(2,1)S(1)}, bf16[64,512]{1,0:T(8,128)(2,1)S(1)}, bf16[64,512]{1,0:T(8,128)(2,1)S(1)}) custom-call(f32[512,512]{1,0:T(8,128)S(1)} %shard_map.180.own_pre, bf16[512,256]{1,0:T(8,128)(2,1)S(1)} %get-tuple-element.63.outer_hits, ...), custom_call_target="tpu_custom_call" | custom-call | tf_op jit(solution)/shard_map/pallas_call | solution.py:429
  30.2 1.9 %collective-permute-start.8 = (bf16[64,512]{1,0:T(8,128)(2,1)S(1)}, bf16[64,512]{1,0:T(8,128)(2,1)S(1)}, u32[]{:S(2)}, u32[]{:S(2)}) collective-permute-start(bf16[64,512]{1,0:T(8,128)(2,1)S(1)} %get-tuple-element.68), channel_id=1, source_target_pairs={{0,4},{4,0},{8,12},{12,8},{1,5},{5,1},{9,13},{13,9},{2,6},{6,2},{1... | collective-permute-start | bytes 196616 | tf_op jit(solution)/shard_map/ppermute | solution.py:570
  32.1 1.5 %collective-permute-start.11 = (bf16[64,512]{1,0:T(8,128)(2,1)S(1)}, bf16[64,512]{1,0:T(8,128)(2,1)S(1)}, u32[]{:S(2)}, u32[]{:S(2)}) collective-permute-start(bf16[64,512]{1,0:T(8,128)(2,1)S(1)} %get-tuple-element.62.own.nodes), channel_id=1, source_target_pairs={{0,2},{2,0},{1,3},{3,1},{4,6},{6,4},{5,7},{7,5},{8,10},{10,8},{9,1... | collective-permute-start | bytes 196616 | tf_op jit(solution)/shard_map/ppermute | solution.py:461
  34.7 1.6 %collective-permute-start.12 = (bf16[48,512]{1,0:T(8,128)(2,1)S(1)}, bf16[48,512]{1,0:T(8,128)(2,1)S(1)}, u32[]{:S(2)}, u32[]{:S(2)}) collective-permute-start(bf16[48,512]{1,0:T(8,128)(2,1)S(1)} %get-tuple-element.76), channel_id=1, source_target_pairs={{0,3},{1,2},{2,1},{3,0},{4,7},{5,6},{6,5},{7,4},{8,11},{9,10},{10,... | collective-permute-start | bytes 147464 | tf_op jit(solution)/shard_map/ppermute | solution.py:583
  36.6 1.6 %collective-permute-done.12.far = bf16[48,512]{1,0:T(8,128)(2,1)S(1)} collective-permute-done((bf16[48,512]{1,0:T(8,128)(2,1)S(1)}, bf16[48,512]{1,0:T(8,128)(2,1)S(1)}, u32[]{:S(2)}, u32[]{:S(2)}) %collective-permute-start.12) | collective-permute-done | bytes 49184 | tf_op jit(solution)/shard_map/ppermute | solution.py:583
  38.2 1.1 %shard_map.184 = (bf16[1,1,512,128]{3,2,1,0:T(8,128)(2,1)S(1)}, bf16[128,512]{1,0:T(8,128)(2,1)S(1)}, bf16[2,64,128]{2,1,0:T(8,128)(2,1)S(1)}) custom-call(bf16[1024,128]{1,0:T(8,128)(2,1)S(1)} %get-tuple-element.58.recv_hits, f32[64,512]{1,0:T(8,128)S(1)} %get-tuple-element.73.part, bf16[48,512]{1,0:T(8,128)(2,1)S(1)} %collective-permute-done.10.near, ...), custom_call_target="tpu_custom_call" | custom-call | tf_op jit(solution)/shard_map/pallas_call | solution.py:429
  39.8 0.7 %shard_map.185 = (f32[1,512,128]{2,1,0:T(8,128)S(1)}, bf16[1,512,128]{2,1,0:T(8,128)(2,1)S(1)}) custom-call(bf16[1024,128]{1,0:T(8,128)(2,1)S(1)} %get-tuple-element.58.recv_hits, bf16[128,512]{1,0:T(8,128)(2,1)S(1)} %get-tuple-element.80.back, bf16[1024,512]{1,0:T(8,128)(2,1)S(1)} %get-tuple-element.79.edge_slope, ...), custom_call_target="tpu_custom_call" | custom-call | tf_op jit(solution)/shard_map/pallas_call | solution.py:429
  40.9 1.6 %collective-permute-start.15 = (bf16[320,128]{1,0:T(8,128)(2,1)S(1)}, bf16[320,128]{1,0:T(8,128)(2,1)S(1)}, u32[]{:S(2)}, u32[]{:S(2)}) collective-permute-start(bf16[320,128]{1,0:T(8,128)(2,1)S(1)} %bitcast.10), channel_id=1, source_target_pairs={{0,2},{2,0},{1,3},{3,1},{4,6},{6,4},{5,7},{7,5},{8,10},{10,8},{9,1... | collective-permute-start | bytes 245768 | tf_op jit(solution)/shard_map/ppermute | solution.py:461
  43.0 0.7 %shard_map.186 = (f32[512,128]{1,0:T(8,128)S(1)}, f32[512,128]{1,0:T(8,128)S(1)}) custom-call(bf16[1024,128]{1,0:T(8,128)(2,1)S(1)} %get-tuple-element.58.recv_hits, bf16[128,512]{1,0:T(8,128)(2,1)S(1)} %get-tuple-element.80.back, bf16[1024,512]{1,0:T(8,128)(2,1)S(1)} %get-tuple-element.79.edge_slope, bf16[512,1024]{1,0:T(8,128)(2,1)S(1)} %get-tuple-element.78.senders, ...), custom_call_target="tpu_custom_call" | custom-call | tf_op jit(solution)/shard_map/pallas_call | solution.py:429
  43.7 2.5 %collective-permute-done.15.refs_0_ = bf16[320,128]{1,0:T(8,128)(2,1)S(1)} collective-permute-done((bf16[320,128]{1,0:T(8,128)(2,1)S(1)}, bf16[320,128]{1,0:T(8,128)(2,1)S(1)}, u32[]{:S(2)}, u32[]{:S(2)}) %collective-permute-start.15) | collective-permute-done | bytes 81952 | tf_op jit(solution)/shard_map/ppermute | solution.py:461
  46.4 2.2 %collective-permute-start.16 = (bf16[2,128,128]{2,1,0:T(8,128)(2,1)S(1)}, bf16[2,128,128]{2,1,0:T(8,128)(2,1)S(1)}, u32[]{:S(2)}, u32[]{:S(2)}) collective-permute-start(bf16[2,128,128]{2,1,0:T(8,128)(2,1)S(1)} %get-tuple-element.89), channel_id=1, source_target_pairs={{0,12},{4,8},{8,4},{12,0},{1,13},{5,9},{9,5},{13,1},{2,14},{6,10},... | collective-permute-start | bytes 196616 | tf_op jit(solution)/shard_map/ppermute | solution.py:466
  48.6 1.3 %collective-permute-start.17 = (bf16[2,128,128]{2,1,0:T(8,128)(2,1)S(1)}, bf16[2,128,128]{2,1,0:T(8,128)(2,1)S(1)}, u32[]{:S(2)}, u32[]{:S(2)}) collective-permute-start(bf16[2,128,128]{2,1,0:T(8,128)(2,1)S(1)} %get-tuple-element.90), channel_id=1, source_target_pairs={{0,8},{4,12},{8,0},{12,4},{1,9},{5,13},{9,1},{13,5},{2,10},{6,14},... | collective-permute-start | bytes 196616 | tf_op jit(solution)/shard_map/ppermute | solution.py:466
  50.0 1.0 %collective-permute-start.19 = (bf16[2,128,128]{2,1,0:T(8,128)(2,1)S(1)}, bf16[2,128,128]{2,1,0:T(8,128)(2,1)S(1)}, u32[]{:S(2)}, u32[]{:S(2)}) collective-permute-start(bf16[2,128,128]{2,1,0:T(8,128)(2,1)S(1)} %get-tuple-element.93), channel_id=1, source_target_pairs={{0,4},{4,0},{8,12},{12,8},{1,5},{5,1},{9,13},{13,9},{2,6},{6,2},{1... | collective-permute-start | bytes 196616 | tf_op jit(solution)/shard_map/ppermute | solution.py:466
  50.9 2.2 %collective-permute-done.16.refs_0_ = bf16[2,128,128]{2,1,0:T(8,128)(2,1)S(1)} collective-permute-done((bf16[2,128,128]{2,1,0:T(8,128)(2,1)S(1)}, bf16[2,128,128]{2,1,0:T(8,128)(2,1)S(1)}, u32[]{:S(2)}, u32[]{:S(2)}) %collective-permute-start.16) | collective-permute-done | bytes 65568 | tf_op jit(solution)/shard_map/ppermute | solution.py:466
  53.2 1.9 %collective-permute-done.17.refs_1_ = bf16[2,128,128]{2,1,0:T(8,128)(2,1)S(1)} collective-permute-done((bf16[2,128,128]{2,1,0:T(8,128)(2,1)S(1)}, bf16[2,128,128]{2,1,0:T(8,128)(2,1)S(1)}, u32[]{:S(2)}, u32[]{:S(2)}) %collective-permute-start.17) | collective-permute-done | bytes 65568 | tf_op jit(solution)/shard_map/ppermute | solution.py:466
  55.1 0.7 %shard_map.190 = (f32[128,128]{1,0:T(8,128)}, f32[128,128]{1,0:T(8,128)}) custom-call(bf16[2,128,128]{2,1,0:T(8,128)(2,1)S(1)} %collective-permute-done.16.refs_0_, bf16[2,128,128]{2,1,0:T(8,128)(2,1)S(1)} %collective-permute-done.17.refs_1_, bf16[2,128,128]{2,1,0:T(8,128)(2,1)S(1)} %collective-permute-done.19.refs_2_, ...), custom_call_target="tpu_custom_call" | custom-call | tf_op jit(solution)/shard_map/pallas_call | solution.py:429
  (46 shorter events, 5.0 us)
Async XLA Ops:
  0.6 15.4 %collective-permute-start.1 = (bf16[3,227,360]{2,1,0:T(8,128)(2,1)}, bf16[3,227,360]{2,1,0:T(8,128)(2,1)S(1)}, u32[]{:S(2)}, u32[]{:S(2)}) collective-permute-start(bf16[3,227,360]{2,1,0:T(8,128)(2,1)} %bitcast.5), channel_id=1, source_target_pairs={{0,1},{1,0},{2,3},{3,2},{4,8},{5,9},{6,10},{7,11},{8,4},{9,5},{10,... | collective-permute-start | bytes 1470968 | tf_op jit(solution)/shard_map/ppermute | solution.py:490
  1.2 16.3 %collective-permute-start = (bf16[3,227,360]{2,1,0:T(8,128)(2,1)}, bf16[3,227,360]{2,1,0:T(8,128)(2,1)S(1)}, u32[]{:S(2)}, u32[]{:S(2)}) collective-permute-start(bf16[3,227,360]{2,1,0:T(8,128)(2,1)} %bitcast.6), channel_id=1, source_target_pairs={{0,4},{4,0},{8,12},{12,8},{1,5},{5,1},{9,13},{13,9},{2,6},{6,2},{1... | collective-permute-start | bytes 1470968 | tf_op jit(solution)/shard_map/ppermute | solution.py:489
  7.3 1.0 %copy-start = (bf16[3,360,227]{1,2,0:T(8,128)(2,1)S(1)}, bf16[3,360,227]{1,2,0:T(8,128)(2,1)}, u32[]{:S(2)}) copy-start(bf16[3,360,227]{1,2,0:T(8,128)(2,1)} %param.16) | copy-start | bytes 1470964
  8.4 6.8 %copy-start.3 = (bf16[512,512]{1,0:T(8,128)(2,1)S(1)}, bf16[512,512]{1,0:T(8,128)(2,1)}, u32[]{:S(2)}) copy-start(bf16[512,512]{1,0:T(8,128)(2,1)} %param.21) | copy-start | bytes 1572868
  8.4 6.9 %copy-start.4 = (bf16[512,512]{1,0:T(8,128)(2,1)S(1)}, bf16[512,512]{1,0:T(8,128)(2,1)}, u32[]{:S(2)}) copy-start(bf16[512,512]{1,0:T(8,128)(2,1)} %param.22) | copy-start | bytes 1572868
  8.4 6.9 %copy-start.5 = (bf16[512,512]{1,0:T(8,128)(2,1)S(1)}, bf16[512,512]{1,0:T(8,128)(2,1)}, u32[]{:S(2)}) copy-start(bf16[512,512]{1,0:T(8,128)(2,1)} %param.23) | copy-start | bytes 1572868
  8.4 7.0 %copy-start.6 = (bf16[227,512]{1,0:T(8,128)(2,1)S(1)}, bf16[227,512]{1,0:T(8,128)(2,1)}, u32[]{:S(2)}) copy-start(bf16[227,512]{1,0:T(8,128)(2,1)} %param.17) | copy-start | bytes 697348
  10.3 5.1 %copy-start.1 = (bf16[32,512]{1,0:T(8,128)(2,1)S(1)}, bf16[32,512]{1,0:T(8,128)(2,1)}, u32[]{:S(2)}) copy-start(bf16[32,512]{1,0:T(8,128)(2,1)} %mesh_in.3) | copy-start | bytes 98308
  10.3 5.1 %collective-permute-start.3 = (bf16[32,512]{1,0:T(8,128)(2,1)}, bf16[32,512]{1,0:T(8,128)(2,1)S(1)}, u32[]{:S(2)}, u32[]{:S(2)}) collective-permute-start(bf16[32,512]{1,0:T(8,128)(2,1)} %mesh_in.3), channel_id=1, source_target_pairs={{0,3},{1,2},{2,1},{3,0},{4,7},{5,6},{6,5},{7,4},{8,11},{9,10},{10,... | collective-permute-start | bytes 98312 | tf_op jit(solution)/shard_map/ppermute | solution.py:516
  10.7 4.7 %collective-permute-start.2 = (bf16[32,512]{1,0:T(8,128)(2,1)}, bf16[32,512]{1,0:T(8,128)(2,1)S(1)}, u32[]{:S(2)}, u32[]{:S(2)}) collective-permute-start(bf16[32,512]{1,0:T(8,128)(2,1)} %mesh_in.3), channel_id=1, source_target_pairs={{0,1},{1,0},{2,3},{3,2},{4,5},{5,4},{6,7},{7,6},{8,9},{9,8},{10,11... | collective-permute-start | bytes 98312 | tf_op jit(solution)/shard_map/ppermute | solution.py:515
  20.3 1.7 %collective-permute-start.4 = (bf16[32,512]{1,0:T(8,128)(2,1)S(1)}, bf16[32,512]{1,0:T(8,128)(2,1)S(1)}, u32[]{:S(2)}, u32[]{:S(2)}) collective-permute-start(bf16[32,512]{1,0:T(8,128)(2,1)S(1)} %get-tuple-element.60), channel_id=1, source_target_pairs={{0,1},{1,0},{2,3},{3,2},{4,5},{5,4},{6,7},{7,6},{8,9},{9,8},{10,11... | collective-permute-start | bytes 98312 | tf_op jit(solution)/shard_map/ppermute | solution.py:544
  20.4 3.4 %collective-permute-start.5 = (bf16[32,512]{1,0:T(8,128)(2,1)S(1)}, bf16[32,512]{1,0:T(8,128)(2,1)S(1)}, u32[]{:S(2)}, u32[]{:S(2)}) collective-permute-start(bf16[32,512]{1,0:T(8,128)(2,1)S(1)} %get-tuple-element.61), channel_id=1, source_target_pairs={{0,3},{1,2},{2,1},{3,0},{4,7},{5,6},{6,5},{7,4},{8,11},{9,10},{10,... | collective-permute-start | bytes 98312 | tf_op jit(solution)/shard_map/ppermute | solution.py:543
  23.8 4.8 %copy-start.2 = (bf16[32,512]{1,0:T(8,128)(2,1)S(1)}, bf16[32,512]{1,0:T(8,128)(2,1)}, u32[]{:S(2)}) copy-start(bf16[32,512]{1,0:T(8,128)(2,1)} %d_out.3) | copy-start | bytes 98308
  24.0 4.5 %collective-permute-start.7 = (bf16[64,512]{1,0:T(8,128)(2,1)S(1)}, bf16[64,512]{1,0:T(8,128)(2,1)S(1)}, u32[]{:S(2)}, u32[]{:S(2)}) collective-permute-start(bf16[64,512]{1,0:T(8,128)(2,1)S(1)} %get-tuple-element.62.own.nodes), channel_id=1, source_target_pairs={{0,4},{4,0},{8,12},{12,8},{1,5},{5,1},{9,13},{13,9},{2,6},{6,2},{1... | collective-permute-start | bytes 196616 | tf_op jit(solution)/shard_map/ppermute | solution.py:550
  25.4 3.2 %collective-permute-start.6 = (bf16[64,512]{1,0:T(8,128)(2,1)S(1)}, bf16[64,512]{1,0:T(8,128)(2,1)S(1)}, u32[]{:S(2)}, u32[]{:S(2)}) collective-permute-start(bf16[64,512]{1,0:T(8,128)(2,1)S(1)} %get-tuple-element.62.own.nodes), channel_id=1, source_target_pairs={{0,1},{1,0},{2,3},{3,2},{4,8},{5,9},{6,10},{7,11},{8,4},{9,5},{10,... | collective-permute-start | bytes 196616 | tf_op jit(solution)/shard_map/ppermute | solution.py:551
  30.2 4.3 %collective-permute-start.8 = (bf16[64,512]{1,0:T(8,128)(2,1)S(1)}, bf16[64,512]{1,0:T(8,128)(2,1)S(1)}, u32[]{:S(2)}, u32[]{:S(2)}) collective-permute-start(bf16[64,512]{1,0:T(8,128)(2,1)S(1)} %get-tuple-element.68), channel_id=1, source_target_pairs={{0,4},{4,0},{8,12},{12,8},{1,5},{5,1},{9,13},{13,9},{2,6},{6,2},{1... | collective-permute-start | bytes 196616 | tf_op jit(solution)/shard_map/ppermute | solution.py:570
  32.1 2.4 %collective-permute-start.9 = (bf16[64,512]{1,0:T(8,128)(2,1)S(1)}, bf16[64,512]{1,0:T(8,128)(2,1)S(1)}, u32[]{:S(2)}, u32[]{:S(2)}) collective-permute-start(bf16[64,512]{1,0:T(8,128)(2,1)S(1)} %get-tuple-element.69), channel_id=1, source_target_pairs={{0,1},{1,0},{2,3},{3,2},{4,8},{5,9},{6,10},{7,11},{8,4},{9,5},{10,... | collective-permute-start | bytes 196616 | tf_op jit(solution)/shard_map/ppermute | solution.py:571
  32.1 4.5 %collective-permute-start.11 = (bf16[64,512]{1,0:T(8,128)(2,1)S(1)}, bf16[64,512]{1,0:T(8,128)(2,1)S(1)}, u32[]{:S(2)}, u32[]{:S(2)}) collective-permute-start(bf16[64,512]{1,0:T(8,128)(2,1)S(1)} %get-tuple-element.62.own.nodes), channel_id=1, source_target_pairs={{0,2},{2,0},{1,3},{3,1},{4,6},{6,4},{5,7},{7,5},{8,10},{10,8},{9,1... | collective-permute-start | bytes 196616 | tf_op jit(solution)/shard_map/ppermute | solution.py:461
  34.6 2.1 %collective-permute-start.10 = (bf16[48,512]{1,0:T(8,128)(2,1)S(1)}, bf16[48,512]{1,0:T(8,128)(2,1)S(1)}, u32[]{:S(2)}, u32[]{:S(2)}) collective-permute-start(bf16[48,512]{1,0:T(8,128)(2,1)S(1)} %get-tuple-element.74), channel_id=1, source_target_pairs={{0,1},{1,0},{2,3},{3,2},{4,5},{5,4},{6,7},{7,6},{8,9},{9,8},{10,11... | collective-permute-start | bytes 147464 | tf_op jit(solution)/shard_map/ppermute | solution.py:584
  34.7 3.6 %collective-permute-start.12 = (bf16[48,512]{1,0:T(8,128)(2,1)S(1)}, bf16[48,512]{1,0:T(8,128)(2,1)S(1)}, u32[]{:S(2)}, u32[]{:S(2)}) collective-permute-start(bf16[48,512]{1,0:T(8,128)(2,1)S(1)} %get-tuple-element.76), channel_id=1, source_target_pairs={{0,3},{1,2},{2,1},{3,0},{4,7},{5,6},{6,5},{7,4},{8,11},{9,10},{10,... | collective-permute-start | bytes 147464 | tf_op jit(solution)/shard_map/ppermute | solution.py:583
  39.3 1.5 %collective-permute-start.14 = (bf16[1,512,128]{2,1,0:T(8,128)(2,1)S(1)}, bf16[1,512,128]{2,1,0:T(8,128)(2,1)S(1)}, u32[]{:S(2)}, u32[]{:S(2)}) collective-permute-start(bf16[1,512,128]{2,1,0:T(8,128)(2,1)S(1)} %bitcast.8), channel_id=1, source_target_pairs={{0,1},{1,0},{2,3},{3,2},{4,5},{5,4},{6,7},{7,6},{8,9},{9,8},{10,11... | collective-permute-start | bytes 393224 | tf_op jit(solution)/shard_map/ppermute | solution.py:461
  40.5 2.4 %collective-permute-start.13 = (bf16[512,128]{1,0:T(8,128)(2,1)S(1)}, bf16[512,128]{1,0:T(8,128)(2,1)S(1)}, u32[]{:S(2)}, u32[]{:S(2)}) collective-permute-start(bf16[512,128]{1,0:T(8,128)(2,1)S(1)} %bitcast.9), channel_id=1, source_target_pairs={{0,1},{1,0},{2,3},{3,2},{4,5},{5,4},{6,7},{7,6},{8,9},{9,8},{10,11... | collective-permute-start | bytes 393224 | tf_op jit(solution)/shard_map/ppermute | solution.py:461
  40.9 5.3 %collective-permute-start.15 = (bf16[320,128]{1,0:T(8,128)(2,1)S(1)}, bf16[320,128]{1,0:T(8,128)(2,1)S(1)}, u32[]{:S(2)}, u32[]{:S(2)}) collective-permute-start(bf16[320,128]{1,0:T(8,128)(2,1)S(1)} %bitcast.10), channel_id=1, source_target_pairs={{0,2},{2,0},{1,3},{3,1},{4,6},{6,4},{5,7},{7,5},{8,10},{10,8},{9,1... | collective-permute-start | bytes 245768 | tf_op jit(solution)/shard_map/ppermute | solution.py:461
  42.4 7.5 %collective-permute-start.18 = (bf16[256,128]{1,0:T(8,128)(2,1)S(1)}, bf16[256,128]{1,0:T(8,128)(2,1)S(1)}, u32[]{:S(2)}, u32[]{:S(2)}) collective-permute-start(bf16[256,128]{1,0:T(8,128)(2,1)S(1)} %bitcast.11), channel_id=1, source_target_pairs={{0,2},{2,0},{1,3},{3,1},{4,6},{6,4},{5,7},{7,5},{8,10},{10,8},{9,1... | collective-permute-start | bytes 196616 | tf_op jit(solution)/shard_map/ppermute | solution.py:461
  46.4 6.8 %collective-permute-start.16 = (bf16[2,128,128]{2,1,0:T(8,128)(2,1)S(1)}, bf16[2,128,128]{2,1,0:T(8,128)(2,1)S(1)}, u32[]{:S(2)}, u32[]{:S(2)}) collective-permute-start(bf16[2,128,128]{2,1,0:T(8,128)(2,1)S(1)} %get-tuple-element.89), channel_id=1, source_target_pairs={{0,12},{4,8},{8,4},{12,0},{1,13},{5,9},{9,5},{13,1},{2,14},{6,10},... | collective-permute-start | bytes 196616 | tf_op jit(solution)/shard_map/ppermute | solution.py:466
  48.6 6.5 %collective-permute-start.17 = (bf16[2,128,128]{2,1,0:T(8,128)(2,1)S(1)}, bf16[2,128,128]{2,1,0:T(8,128)(2,1)S(1)}, u32[]{:S(2)}, u32[]{:S(2)}) collective-permute-start(bf16[2,128,128]{2,1,0:T(8,128)(2,1)S(1)} %get-tuple-element.90), channel_id=1, source_target_pairs={{0,8},{4,12},{8,0},{12,4},{1,9},{5,13},{9,1},{13,5},{2,10},{6,14},... | collective-permute-start | bytes 196616 | tf_op jit(solution)/shard_map/ppermute | solution.py:466
  50.0 5.2 %collective-permute-start.19 = (bf16[2,128,128]{2,1,0:T(8,128)(2,1)S(1)}, bf16[2,128,128]{2,1,0:T(8,128)(2,1)S(1)}, u32[]{:S(2)}, u32[]{:S(2)}) collective-permute-start(bf16[2,128,128]{2,1,0:T(8,128)(2,1)S(1)} %get-tuple-element.93), channel_id=1, source_target_pairs={{0,4},{4,0},{8,12},{12,8},{1,5},{5,1},{9,13},{13,9},{2,6},{6,2},{1... | collective-permute-start | bytes 196616 | tf_op jit(solution)/shard_map/ppermute | solution.py:466
